TPU v7x, 32 devices: a whole 2x2x4 slice. The times are simulated.
32 devices in a mesh: section: 4 (over y, core), dp: 8 (over z, x).
Axes of the slice: x: 2, y: 2, z: 4, core: 2. Of those that a mesh axis runs over, the one named last changes fastest.
Arguments:
- acts: bfloat16 [4, 2, 1024, 512], P('section', None, 'dp'), may hold values from -12 to 12
- weights: bfloat16 [4, 512, 512], P('section'), may hold values from -0.25 to 0.25
- cot_last: bfloat16 [2, 1024, 512], P(None, 'dp'), may hold values from -1.796875 to 1.796875
Outputs:
- input_cots: bfloat16 [4, 2, 1024, 512], P('section', None, 'dp')
- update: float32 [4, 512, 512], P('section')
All inputs are finite; a program needn't handle non-finite values.
Results may differ from a plain program's by a relative error of at most 0.025.
Values may be sent and summed in bfloat16 or wider, within the bound.
No kernel may reach another device: no remote copies, remote signals or barrier semaphores. Data moves between devices by JAX's collectives and lax.ppermute only.
A program may use at most 64 MiB of HBM per device.

v0:
```python
import jax
import jax.numpy as jnp
from jax import lax
from jax.sharding import PartitionSpec as P

NS_STEPS = 3


def shifted(block, axis, distance):
    devices = range(lax.axis_size(axis))
    route = [(i - distance, i) for i in devices if i - distance in devices]
    return lax.ppermute(block, axis, route)


def silu_slope(pre):
    sig = jax.nn.sigmoid(pre)
    return sig * (1.0 + pre * (1.0 - sig))


def moment(left, right):
    return lax.dot_general(
        left, right, (((0,), (0,)), ((), ())), preferred_element_type=jnp.float32
    )


def newton(matrix):
    eye = jnp.eye(matrix.shape[0], dtype=jnp.float32)
    approx = eye / jnp.sqrt(jnp.sum(matrix * matrix))
    for step in range(NS_STEPS):
        inner = jnp.dot(matrix, approx, precision=lax.Precision.HIGHEST)
        approx = 2.0 * approx - jnp.dot(approx, inner, precision=lax.Precision.HIGHEST)
    return approx


def body(acts, weights, cot_last):
    sections = lax.axis_size("section")
    here = lax.axis_index("section")
    weight = weights[0]
    local = acts[0]
    micro, rows, width = local.shape
    flat = local.reshape(micro * rows, width)
    count = micro * rows * lax.axis_size("dp")
    eye = jnp.eye(width, dtype=jnp.float32)

    def tick(turn, carry):
        incoming, dh_store, dx_store = carry
        slot = turn - (sections - 1 - here)
        active = jnp.logical_and(slot >= 0, slot < micro)
        index = jnp.clip(slot, 0, micro - 1)
        inputs = lax.dynamic_index_in_dim(local, index, 0, keepdims=False)
        arriving = lax.dynamic_index_in_dim(cot_last, index, 0, keepdims=False)
        upstream = jnp.where(here == sections - 1, arriving, incoming)
        pre = jnp.dot(inputs, weight, preferred_element_type=jnp.float32)
        slope_dh = (upstream.astype(jnp.float32) * silu_slope(pre)).astype(jnp.bfloat16)
        back = lax.dot_general(
            slope_dh, weight, (((1,), (1,)), ((), ())), preferred_element_type=jnp.float32
        )
        result = (upstream.astype(jnp.float32) + back).astype(jnp.bfloat16)
        old_dh = lax.dynamic_index_in_dim(dh_store, index, 0, keepdims=False)
        old_dx = lax.dynamic_index_in_dim(dx_store, index, 0, keepdims=False)
        dh_store = lax.dynamic_update_index_in_dim(
            dh_store, jnp.where(active, slope_dh, old_dh), index, 0
        )
        dx_store = lax.dynamic_update_index_in_dim(
            dx_store, jnp.where(active, result, old_dx), index, 0
        )
        incoming = shifted(result, "section", -1)
        return (incoming, dh_store, dx_store)

    start = (
        jnp.zeros((rows, width), jnp.bfloat16),
        jnp.zeros((micro, rows, width), jnp.bfloat16),
        jnp.zeros((micro, rows, width), jnp.bfloat16),
    )
    finished = lax.fori_loop(0, sections + micro - 1, tick, start)
    dh_flat = finished[1].reshape(micro * rows, width)
    act_sum, out_sum, grad_sum = lax.psum(
        (moment(flat, flat), moment(dh_flat, dh_flat), moment(flat, dh_flat)), "dp"
    )
    act_factor = act_sum / count + 0.01 * eye
    out_factor = out_sum / count + 0.01 * eye
    act_inv = newton(act_factor)
    out_inv = newton(out_factor)
    update = jnp.dot(
        jnp.dot(act_inv, grad_sum, precision=lax.Precision.HIGHEST),
        out_inv,
        precision=lax.Precision.HIGHEST,
    )
    return (finished[2][None], update[None])


def solution(mesh):
    placed = (P("section", None, "dp", None), P("section", None, None), P(None, "dp", None))
    return jax.shard_map(
        body,
        mesh=mesh,
        in_specs=placed,
        out_specs=(P("section", None, "dp", None), P("section", None, None)),
        check_vma=False,
    )
```

profile of v0, /device:TPU:0, one launch (start us, length us, event | category | flops | bytes accessed | tf_op | source)
XLA Modules:
  0.0 217.7 jit_solution(6684111621291629351)
XLA Ops:
  7.2 0.0 all-reduce.3.cloned.1.call-start
  7.2 0.0 copy-start.4
  7.2 0.0 copy-start.6
  7.2 2.4 %convolution_bitcast_fusion.2 = f32[512,512]{1,0:T(8,128)} fusion(bf16[1,2,128,512]{3,2,1,0:T(8,128)(2,1)} %param.5), kind=kOutput, calls=%fused_computation.31 | convolution fusion | flops 134217728 | bytes 1310720 | tf_op jit(solution)/shard_map/dot_general | solution.py:21
  9.6 0.0 copy-start
  9.7 0.0 copy-done.4
  9.7 0.0 copy-done.6
  9.7 0.9 copy-done
  10.7 32.7 %while.19 = (s32[]{:T(128)}, bf16[128,512]{1,0:T(8,128)(2,1)S(1)}, bf16[2,128,512]{2,1,0:T(8,128)(2,1)S(1)}, bf16[2,128,512]{2,1,0:T(8,128)(2,1)S(1)}, pred[]{:T...) while((s32[]{:T(128)}, bf16[128,512]{1,0:T(8,128)(2,1)S(1)}, ...), condition=%wide.region_1.2_spmd, body=%wide.region_0.1_spmd.sunk | while | flops 135331840 | bytes 3671777 | solution.py:75
  10.7 0.3 bitcast_dynamic-update-slice_fusion.4
  11.0 0.3 bitcast_dynamic-update-slice_fusion.5
  11.4 1.3 collective-permute-start
  12.7 1.9 collective-permute-done
  14.6 0.3 bitcast_dynamic-update-slice_fusion.4
  15.0 0.3 bitcast_dynamic-update-slice_fusion.5
  15.3 1.3 collective-permute-start
  16.6 5.8 %collective-permute-done = bf16[128,512]{1,0:T(8,128)(2,1)S(1)} collective-permute-done((bf16[128,512]{1,0:T(8,128)(2,1)S(1)}, bf16[128,512]{1,0:T(8,128)(2,1)S(1)}, u32[]{:S(2)}, u32[]{:S(2)}) %collective-permute-start) | collective-permute-done | bytes 131104 | tf_op jit(solution)/shard_map/while/body/eval_jaxpr/ppermute | solution.py:12
  22.4 0.3 bitcast_dynamic-update-slice_fusion.4
  22.8 0.3 bitcast_dynamic-update-slice_fusion.5
  23.1 1.3 collective-permute-start
  24.4 5.0 %collective-permute-done = bf16[128,512]{1,0:T(8,128)(2,1)S(1)} collective-permute-done((bf16[128,512]{1,0:T(8,128)(2,1)S(1)}, bf16[128,512]{1,0:T(8,128)(2,1)S(1)}, u32[]{:S(2)}, u32[]{:S(2)}) %collective-permute-start) | collective-permute-done | bytes 131104 | tf_op jit(solution)/shard_map/while/body/eval_jaxpr/ppermute | solution.py:12
  29.4 0.3 bitcast_dynamic-update-slice_fusion.4
  29.8 0.3 bitcast_dynamic-update-slice_fusion.5
  30.1 1.3 collective-permute-start
  31.4 5.0 %collective-permute-done = bf16[128,512]{1,0:T(8,128)(2,1)S(1)} collective-permute-done((bf16[128,512]{1,0:T(8,128)(2,1)S(1)}, bf16[128,512]{1,0:T(8,128)(2,1)S(1)}, u32[]{:S(2)}, u32[]{:S(2)}) %collective-permute-start) | collective-permute-done | bytes 131104 | tf_op jit(solution)/shard_map/while/body/eval_jaxpr/ppermute | solution.py:12
  36.4 0.3 bitcast_dynamic-update-slice_fusion.4
  36.8 0.3 bitcast_dynamic-update-slice_fusion.5
  37.1 1.3 collective-permute-start
  38.4 5.0 %collective-permute-done = bf16[128,512]{1,0:T(8,128)(2,1)S(1)} collective-permute-done((bf16[128,512]{1,0:T(8,128)(2,1)S(1)}, bf16[128,512]{1,0:T(8,128)(2,1)S(1)}, u32[]{:S(2)}, u32[]{:S(2)}) %collective-permute-start) | collective-permute-done | bytes 131104 | tf_op jit(solution)/shard_map/while/body/eval_jaxpr/ppermute | solution.py:12
  43.4 0.0 copy-start.3
  43.4 1.3 convolution_bitcast_fusion
  44.7 0.0 copy-done.3
  44.7 1.3 convolution_bitcast_fusion.1
  46.0 0.0 all-reduce.3.cloned.1.call-update
  46.0 133.6 %all-reduce.3.cloned.1.call-done = (f32[512,512]{1,0:T(8,128)}, f32[512,512]{0,1:T(8,128)}, f32[512,512]{1,0:T(8,128)}) async-done(((f32[512,512]{1,0:T(8,128)}, f32[512,512]{0,1:T(8,128)}, f32[512,512]{1,0:T(8,128)}), (f32[512,512]{1,0:T(8,128)}, f32[512,512]{0,1:T(8,128)}, f32[512,512]{1,0:T(8,128)})) %all-reduce.3.cloned.1.call-update) | async-done | bytes 3145744 | tf_op jit(solution)/shard_map/psum | solution.py:77
  179.6 0.0 copy-start.2
  179.6 2.6 %multiply_reduce_fusion = (f32[]{:T(128)}, f32[]{:T(128)}) fusion(f32[512,512]{1,0:T(8,128)} %get-tuple-element.221, f32[512,512]{1,0:T(8,128)} %get-tuple-element.219), kind=kLoop, calls=%fused_computation.37 | loop fusion | flops 2621438 | bytes 2097160 | tf_op jit(solution)/shard_map/reduce_sum | solution.py:28
  183.5 0.0 copy-done.2
  183.6 1.8 fusion.10
  185.4 1.8 fusion.19
  187.2 1.9 fusion.33
  189.1 1.8 convolution_subtract_fusion.1
  191.0 1.9 fusion.32
  192.9 0.0 copy-start.1
  192.9 1.9 convolution_subtract_fusion
  194.7 0.0 copy-done.1
  194.7 2.0 fusion.14
  196.8 1.8 fusion.16
  198.6 1.9 fusion.31
  200.5 1.8 convolution_subtract_fusion.3
  202.3 1.9 fusion.30
  204.2 0.0 copy-start.5
  204.3 1.9 convolution_subtract_fusion.2
  206.1 0.0 copy-done.5
  206.1 1.9 fusion.55
  208.0 2.8 %convolution_bitcast_fusion.3 = f32[1,512,512]{2,1,0:T(8,128)} fusion(f32[512,512]{1,0:T(8,128)S(1)} %fusion.55, f32[512,512]{1,0:T(8,128)S(1)} %convolution_subtract_fusion), kind=kOutput, calls=%fused_computation.32 | convolution fusion | flops 1610612736 | bytes 3145728 | tf_op jit(solution)/shard_map/dot_general | solution.py:84
  (8 shorter events, 0.1 us)
Async XLA Ops:
  7.2 172.5 %all-reduce.3.cloned.1.call-start = ((), (), s32[]{:S(2)}) async-start(), calls=%async_computation | async-start | bytes 6291456 | tf_op jit(solution)/shard_map/psum | solution.py:77
  7.2 2.5 %copy-start.4 = (bf16[2,128,512]{2,1,0:T(8,128)(2,1)S(1)}, bf16[2,128,512]{2,1,0:T(8,128)(2,1)}, u32[]{:S(2)}) copy-start(bf16[2,128,512]{2,1,0:T(8,128)(2,1)} %param.7) | copy-start | bytes 786436
  7.2 2.5 %copy-start.6 = (bf16[1,2,128,512]{3,2,1,0:T(8,128)(2,1)S(1)}, bf16[1,2,128,512]{3,2,1,0:T(8,128)(2,1)}, u32[]{:S(2)}) copy-start(bf16[1,2,128,512]{3,2,1,0:T(8,128)(2,1)} %param.5) | copy-start | bytes 786436
  9.6 1.0 copy-start
  11.4 3.2 %collective-permute-start = (bf16[128,512]{1,0:T(8,128)(2,1)S(1)}, bf16[128,512]{1,0:T(8,128)(2,1)S(1)}, u32[]{:S(2)}, u32[]{:S(2)}) collective-permute-start(bf16[128,512]{1,0:T(8,128)(2,1)S(1)} %get-tuple-element.294), channel_id=1, source_target_pairs={{8,0},{16,8},{24,16},{9,1},{17,9},{25,17},{10,2},{18,10},{26,18},{... | collective-permute-start | bytes 393224 | tf_op jit(solution)/shard_map/while/body/eval_jaxpr/ppermute | solution.py:12
  15.3 7.1 %collective-permute-start = (bf16[128,512]{1,0:T(8,128)(2,1)S(1)}, bf16[128,512]{1,0:T(8,128)(2,1)S(1)}, u32[]{:S(2)}, u32[]{:S(2)}) collective-permute-start(bf16[128,512]{1,0:T(8,128)(2,1)S(1)} %get-tuple-element.294), channel_id=1, source_target_pairs={{8,0},{16,8},{24,16},{9,1},{17,9},{25,17},{10,2},{18,10},{26,18},{... | collective-permute-start | bytes 393224 | tf_op jit(solution)/shard_map/while/body/eval_jaxpr/ppermute | solution.py:12
  23.1 6.3 %collective-permute-start = (bf16[128,512]{1,0:T(8,128)(2,1)S(1)}, bf16[128,512]{1,0:T(8,128)(2,1)S(1)}, u32[]{:S(2)}, u32[]{:S(2)}) collective-permute-start(bf16[128,512]{1,0:T(8,128)(2,1)S(1)} %get-tuple-element.294), channel_id=1, source_target_pairs={{8,0},{16,8},{24,16},{9,1},{17,9},{25,17},{10,2},{18,10},{26,18},{... | collective-permute-start | bytes 393224 | tf_op jit(solution)/shard_map/while/body/eval_jaxpr/ppermute | solution.py:12
  30.1 6.3 %collective-permute-start = (bf16[128,512]{1,0:T(8,128)(2,1)S(1)}, bf16[128,512]{1,0:T(8,128)(2,1)S(1)}, u32[]{:S(2)}, u32[]{:S(2)}) collective-permute-start(bf16[128,512]{1,0:T(8,128)(2,1)S(1)} %get-tuple-element.294), channel_id=1, source_target_pairs={{8,0},{16,8},{24,16},{9,1},{17,9},{25,17},{10,2},{18,10},{26,18},{... | collective-permute-start | bytes 393224 | tf_op jit(solution)/shard_map/while/body/eval_jaxpr/ppermute | solution.py:12
  37.1 6.3 %collective-permute-start = (bf16[128,512]{1,0:T(8,128)(2,1)S(1)}, bf16[128,512]{1,0:T(8,128)(2,1)S(1)}, u32[]{:S(2)}, u32[]{:S(2)}) collective-permute-start(bf16[128,512]{1,0:T(8,128)(2,1)S(1)} %get-tuple-element.294), channel_id=1, source_target_pairs={{8,0},{16,8},{24,16},{9,1},{17,9},{25,17},{10,2},{18,10},{26,18},{... | collective-permute-start | bytes 393224 | tf_op jit(solution)/shard_map/while/body/eval_jaxpr/ppermute | solution.py:12
  43.4 1.3 copy-start.3
  179.6 3.9 %copy-start.2 = (f32[512,512]{1,0:T(8,128)S(1)}, f32[512,512]{1,0:T(8,128)}, u32[]{:S(2)}) copy-start(f32[512,512]{1,0:T(8,128)} %get-tuple-element.221) | copy-start | bytes 3145732
  192.9 1.9 copy-start.1
  204.2 1.9 copy-start.5
Sparse Core Ops, SparseCore 0:
  46.1 133.4 all-reduce.2
where the time goes:
time: 218 us
  waiting for transfers between devices  156 us (72%)
  matrix products  35.4 us (16%)
  between operations  15.6 us (7%)
  starting transfers between devices  6.5 us (3%)
  other arithmetic  2.57 us (1%)
    psum x1, waiting for transfers between devices, body(): lax.psum((moment(flat, flat), moment(dh_flat, dh_flat), moment(flat, dh_f...  134 us
    ppermute x5, waiting for transfers between devices, shifted(): return lax.ppermute(block, axis, route)  22.7 us
    dot_general x6, matrix products, newton(): inner = jnp.dot(matrix, approx, precision=lax.Precision.HIGHEST)  11.4 us
    dot_general x6, matrix products, newton(): jnp.dot(approx, inner, precision=lax.Precision.HIGHEST)  11 us
    ppermute x5, starting transfers between devices, shifted(): return lax.ppermute(block, axis, route)  6.46 us
    dot_general x3, matrix products, moment(): lax.dot_general(left, right, (((0,), (0,)), ((), ())), preferred_element_...  4.98 us
  transfers between devices with their start and end apart: 6, of which 6 were waited for; matrix products, arithmetic and copies ran while one was open for 0% of the time, Pallas kernels for 0%

commit v1 on v0

v1 whole, which is shorter than its diff:
```python
import jax
import jax.numpy as jnp
from jax import lax
from jax.sharding import PartitionSpec as P


def silu_slope(pre):
    sig = jax.nn.sigmoid(pre)
    return sig * (1.0 + pre * (1.0 - sig))


def moment(left, right):
    return lax.dot_general(
        left, right, (((0,), (0,)), ((), ())), preferred_element_type=jnp.float32
    )


def mul(left, right):
    return jnp.dot(left, right, precision=lax.Precision.HIGH)


def inverse(matrix):
    eye = jnp.eye(matrix.shape[0], dtype=jnp.float32)
    scale = lax.rsqrt(jnp.sum(matrix * matrix))
    first = matrix * scale
    second = 2.0 * first - mul(first, first)
    square = mul(second, second)
    tail = mul(2.0 * eye - second, 2.0 * eye - 2.0 * second + square)
    return mul(2.0 * eye - first, tail) * scale


def body(acts, weights, cot_last):
    sections = lax.axis_size("section")
    here = lax.axis_index("section")
    pairs = sections // 2
    odd = (here % 2) == 1
    weight = weights[0]
    micro, rows, width = acts.shape[1:]
    tokens = micro * rows
    count = tokens * lax.axis_size("dp")
    eye = jnp.eye(width, dtype=jnp.float32)
    flat = acts[0].reshape(tokens, width)

    to_even = [(s, s - 1) for s in range(1, sections, 2)]
    odd_weight = jnp.where(odd, weight, lax.ppermute(weight, "section", to_even))
    odd_flat = jnp.where(odd, flat, lax.ppermute(flat, "section", to_even))

    every = lax.all_gather(flat, "dp", tiled=True)
    act_inv = inverse(moment(every, every) / count + 0.01 * eye)

    slope_odd = silu_slope(jnp.dot(odd_flat, odd_weight, preferred_element_type=jnp.float32))
    slope_own = silu_slope(jnp.dot(flat, weight, preferred_element_type=jnp.float32))

    def layer(upstream, slope, matrix):
        dh = (upstream.astype(jnp.float32) * slope).astype(jnp.bfloat16)
        back = lax.dot_general(dh, matrix, (((1,), (1,)), ((), ())), preferred_element_type=jnp.float32)
        return dh, (upstream.astype(jnp.float32) + back).astype(jnp.bfloat16)

    upstream = cot_last.reshape(tokens, width)
    for turn in range(pairs):
        dh_odd, cot_odd = layer(upstream, slope_odd, odd_weight)
        dh_even, cot_even = layer(cot_odd, slope_own, weight)
        mine_dh = jnp.where(odd, dh_odd, dh_even)
        mine_cot = jnp.where(odd, cot_odd, cot_even)
        if turn == 0:
            dh, cot = mine_dh, mine_cot
        else:
            now = (here // 2) == pairs - 1 - turn
            dh, cot = jnp.where(now, mine_dh, dh), jnp.where(now, mine_cot, cot)
        if turn < pairs - 1:
            low = lax.ppermute(cot_even, "section", [(s, s - 2) for s in range(2, sections, 2)])
            high = lax.ppermute(cot_even, "section", [(s, s - 1) for s in range(2, sections, 2)])
            upstream = jnp.where(odd, high, low)

    out_sum, grad = lax.psum(
        (moment(dh, dh).astype(jnp.bfloat16), moment(flat, dh).astype(jnp.bfloat16)), "dp"
    )
    out_inv = inverse(out_sum.astype(jnp.float32) / count + 0.01 * eye)
    update = mul(mul(act_inv, grad.astype(jnp.float32)), out_inv)
    return (cot.reshape(1, micro, rows, width), update[None])


def solution(mesh):
    placed = (P("section", None, "dp", None), P("section", None, None), P(None, "dp", None))
    return jax.shard_map(
        body,
        mesh=mesh,
        in_specs=placed,
        out_specs=(P("section", None, "dp", None), P("section", None, None)),
        check_vma=False,
    )
```

time: 218 us -> 180 us (0.83)
  waiting for transfers between devices: 156 us -> 132 us
  matrix products: 35.4 us -> 24.9 us
    psum x1, waiting for transfers between devices: 134 us -> 78.4 us  [body(): lax.psum((moment(dh, dh).astype(jnp.bfloat16), moment(flat, dh).astype(jn...]
    all_gather x0 -> x1, waiting for transfers between devices: none -> 42.7 us  [body(): every = lax.all_gather(flat, 'dp', tiled=True)]
    ppermute x5 -> x4, waiting for transfers between devices: 22.7 us -> 10.4 us  [the longest x1 9.63 us: body(): lax.ppermute(cot_even, 'section', [(s, s - 2) for s in range(2, sections,...]
    dot_general x24 -> x16, matrix products: 30.4 us -> 18.4 us  [the longest x10 12.5 us: mul(): return jnp.dot(left, right, precision=lax.Precision.HIGH)]
    ppermute x5 -> x4, starting transfers between devices: 6.46 us -> 4.69 us  [the longest x1 1.42 us: body(): lax.ppermute(weight, 'section', to_even)]
  transfers between devices with their start and end apart: 6 -> 6, of which waited for: 6 -> 4; matrix products, arithmetic and copies ran while one was open for 0% -> 6% of each run, Pallas kernels for 0% -> 0%
where the time goes in v1:
time: 180 us
  waiting for transfers between devices  132 us (73%)
  matrix products  24.9 us (14%)
  between operations  15.7 us (9%)
  starting transfers between devices  4.95 us (3%)
  other arithmetic  1.92 us (1%)
    psum x1, waiting for transfers between devices, body(): lax.psum((moment(dh, dh).astype(jnp.bfloat16), moment(flat, dh).astype(jn...  78.4 us
    all_gather x1, waiting for transfers between devices, body(): every = lax.all_gather(flat, 'dp', tiled=True)  42.7 us
    dot_general x10, matrix products, mul(): return jnp.dot(left, right, precision=lax.Precision.HIGH)  12.5 us
    ppermute x1, waiting for transfers between devices, body(): lax.ppermute(cot_even, 'section', [(s, s - 2) for s in range(2, sections,...  9.63 us
    dot_general x3, matrix products, moment(): lax.dot_general(left, right, (((0,), (0,)), ((), ())), preferred_element_...  6.51 us
    dot_general x4, matrix products, layer(): lax.dot_general(dh, matrix, (((1,), (1,)), ((), ())), preferred_element_t...  3.93 us
  transfers between devices with their start and end apart: 6, of which 4 were waited for; matrix products, arithmetic and copies ran while one was open for 6% of the time, Pallas kernels for 0%

profile of v1, /device:TPU:0, one launch (start us, length us, event | category | flops | bytes accessed | tf_op | source)
XLA Modules:
  0.0 179.6 jit_solution(11913840252441903065)
XLA Ops:
  7.2 0.0 copy-start
  7.2 0.0 copy-start.1
  7.2 0.0 all-reduce.3.cloned.1.call-start
  7.2 1.4 collective-permute-start.1
  8.7 1.3 collective-permute-start
  10.0 1.5 add_multiply_fusion
  11.5 0.0 copy-start.4
  11.5 0.8 collective-permute-done
  12.3 0.0 collective-permute-done.1
  12.3 0.0 copy-done
  12.3 0.0 copy-done.1
  12.3 0.4 add_multiply_fusion.1
  12.8 0.0 copy-done.4
  12.8 0.3 fusion.1
  13.1 0.3 fusion.2
  13.5 0.7 collective-permute-start.2
  14.2 1.3 collective-permute-start.3
  15.5 0.0 collective-permute-done.2
  15.5 9.6 %collective-permute-done.3 = bf16[256,512]{1,0:T(8,128)(2,1)} collective-permute-done((bf16[256,512]{1,0:T(8,128)(2,1)S(1)}, bf16[256,512]{1,0:T(8,128)(2,1)}, u32[]{:S(2)}, u32[]{:S(2)}) %collective-permute-start.3) | collective-permute-done | bytes 262176 | tf_op jit(solution)/shard_map/ppermute | solution.py:71
  25.1 2.2 %select_select_fusion = (bf16[256,512]{1,0:T(8,128)(2,1)S(1)}, bf16[256,512]{1,0:T(8,128)(2,1)}) fusion(pred[]{:T(512)S(6)} %eq.28, pred[]{:T(512)S(6)} %eq.27, f32[256,512]{1,0:T(8,128)S(1)} %add_multiply_fusion.1, f32[256,512]{1,0:T(8,128)S(1)} %add_multiply_fusion, bf16[256,512]{1,0:T(8,128)(2,1)S(1)} %collective-permute-done.2, ...), kind=kOutput, calls=%fused_computation.64 | convolution fusion | flops 137363456 | bytes 3670018 | tf_op jit(solution)/shard_map/dot_general | solution.py:56
  27.3 0.0 copy-start.5
  27.3 1.1 fusion
  28.4 1.1 convolution_convert_fusion
  29.6 0.0 all-reduce.3.cloned.1.call-update
  29.6 0.2 all-gather.2.cloned.1.call-start
  29.8 0.5 all-gather.2.cloned.1.call-update
  30.4 0.0 copy-done.5
  30.4 1.1 select_select_fusion.1
  31.4 78.4 %all-reduce.3.cloned.1.call-done = (bf16[512,512]{0,1:T(8,128)(2,1)}, bf16[512,512]{1,0:T(8,128)(2,1)}) async-done(((bf16[512,512]{0,1:T(8,128)(2,1)}, bf16[512,512]{1,0:T(8,128)(2,1)}), (bf16[512,512]{0,1:T(8,128)(2,1)}, bf16[512,512]{1,0:T(8,128)(2,1)})) %all-reduce.3.cloned.1.call-update) | async-done | bytes 1048592 | tf_op jit(solution)/shard_map/psum | solution.py:75
  109.9 1.9 %multiply_reduce_fusion = f32[]{:T(128)} fusion(bf16[512,512]{1,0:T(8,128)(2,1)} %get-tuple-element.3), kind=kLoop, calls=%fused_computation.30 | loop fusion | flops 1835007 | bytes 524292 | tf_op jit(solution)/shard_map/reduce_sum | solution.py:24
  112.5 2.6 %convolution_subtract_fusion = f32[512,512]{1,0:T(8,128)S(1)} fusion(bf16[512,512]{1,0:T(8,128)(2,1)} %get-tuple-element.3, f32[]{:T(128)S(6)} %rsqrt.7), kind=kOutput, calls=%fused_computation.11 | convolution fusion | flops 808976384 | bytes 1572868 | tf_op jit(solution)/shard_map/dot_general | solution.py:19
  115.1 1.0 convolution_add_fusion
  116.1 0.0 copy-start.3
  116.1 1.0 fusion.7
  117.2 0.0 copy-done.3
  117.2 1.0 convolution_multiply_fusion
  118.2 42.7 %all-gather.2.cloned.1.call-done = bf16[2048,512]{1,0:T(8,128)(2,1)} async-done(((bf16[256,512]{1,0:T(8,128)(2,1)}), bf16[2048,512]{1,0:T(8,128)(2,1)}) %all-gather.2.cloned.1.call-update) | async-done | bytes 2097168 | tf_op jit(solution)/shard_map/all_gather | solution.py:48
  160.9 4.2 %multiply_reduce_fusion.1 = (f32[]{:T(128)}, f32[512,512]{1,0:T(8,128)S(1)}) fusion(bf16[2048,512]{1,0:T(8,128)(2,1)} %all-gather.2.cloned.1.call-done), kind=kOutput, calls=%fused_computation.31 | convolution fusion | flops 1075314688 | bytes 3145732 | tf_op jit(solution)/shard_map/dot_general | solution.py:13
  165.9 1.0 convolution_subtract_fusion.1
  166.9 1.0 convolution_add_fusion.1
  167.9 1.0 fusion.6
  168.9 0.0 copy-start.2
  168.9 1.0 convolution_multiply_fusion.1
  170.0 0.0 copy-done.2
  170.0 0.8 fusion.62
  170.8 2.0 %convolution_bitcast_fusion = f32[1,512,512]{2,1,0:T(8,128)} fusion(f32[512,512]{1,0:T(8,128)S(1)} %fusion.62, f32[512,512]{1,0:T(8,128)S(1)} %convolution_multiply_fusion), kind=kOutput, calls=%fused_computation.8 | convolution fusion | flops 805306368 | bytes 3145728 | tf_op jit(solution)/shard_map/dot_general | solution.py:19
Async XLA Ops:
  7.2 5.2 %copy-start = (bf16[1,512,512]{2,1,0:T(8,128)(2,1)S(1)}, bf16[1,512,512]{2,1,0:T(8,128)(2,1)}, u32[]{:S(2)}) copy-start(bf16[1,512,512]{2,1,0:T(8,128)(2,1)} %param.4) | copy-start | bytes 1572868
  7.2 5.2 %copy-start.1 = (bf16[1,2,128,512]{3,2,1,0:T(8,128)(2,1)S(1)}, bf16[1,2,128,512]{3,2,1,0:T(8,128)(2,1)}, u32[]{:S(2)}) copy-start(bf16[1,2,128,512]{3,2,1,0:T(8,128)(2,1)} %param.3) | copy-start | bytes 786436
  7.2 102.7 %all-reduce.3.cloned.1.call-start = ((), (), s32[]{:S(2)}) async-start(), calls=%async_computation.1 | async-start | bytes 2097152 | tf_op jit(solution)/shard_map/psum | solution.py:75
  7.2 5.1 %collective-permute-start.1 = (bf16[512,512]{1,0:T(8,128)(2,1)}, bf16[512,512]{1,0:T(8,128)(2,1)S(1)}, u32[]{:S(2)}, u32[]{:S(2)}) collective-permute-start(bf16[512,512]{1,0:T(8,128)(2,1)} %bitcast.43), channel_id=1, source_target_pairs={{8,0},{24,16},{9,1},{25,17},{10,2},{26,18},{11,3},{27,19},{12,4},{... | collective-permute-start | bytes 1572872 | tf_op jit(solution)/shard_map/ppermute | solution.py:45
  8.7 3.7 %collective-permute-start = (bf16[256,512]{1,0:T(8,128)(2,1)}, bf16[256,512]{1,0:T(8,128)(2,1)S(1)}, u32[]{:S(2)}, u32[]{:S(2)}) collective-permute-start(bf16[256,512]{1,0:T(8,128)(2,1)} %bitcast.44), channel_id=1, source_target_pairs={{8,0},{24,16},{9,1},{25,17},{10,2},{26,18},{11,3},{27,19},{12,4},{... | collective-permute-start | bytes 786440 | tf_op jit(solution)/shard_map/ppermute | solution.py:46
  11.5 1.3 copy-start.4
  13.5 2.0 %collective-permute-start.2 = (bf16[256,512]{1,0:T(8,128)(2,1)S(1)}, bf16[256,512]{1,0:T(8,128)(2,1)S(1)}, u32[]{:S(2)}, u32[]{:S(2)}) collective-permute-start(bf16[256,512]{1,0:T(8,128)(2,1)S(1)} %fusion.2), channel_id=1, source_target_pairs={{16,8},{17,9},{18,10},{19,11},{20,12},{21,13},{22,14},{23,15}} | collective-permute-start | bytes 786440 | tf_op jit(solution)/shard_map/ppermute | solution.py:72
  14.2 11.0 %collective-permute-start.3 = (bf16[256,512]{1,0:T(8,128)(2,1)S(1)}, bf16[256,512]{1,0:T(8,128)(2,1)}, u32[]{:S(2)}, u32[]{:S(2)}) collective-permute-start(bf16[256,512]{1,0:T(8,128)(2,1)S(1)} %fusion.2), channel_id=1, source_target_pairs={{16,0},{17,1},{18,2},{19,3},{20,4},{21,5},{22,6},{23,7}} | collective-permute-start | bytes 786440 | tf_op jit(solution)/shard_map/ppermute | solution.py:71
  27.3 3.1 %copy-start.5 = (bf16[256,512]{1,0:T(8,128)(2,1)S(1)}, bf16[256,512]{1,0:T(8,128)(2,1)}, u32[]{:S(2)}) copy-start(bf16[256,512]{1,0:T(8,128)(2,1)} %get-tuple-element.7) | copy-start | bytes 786436
  29.6 131.3 %all-gather.2.cloned.1.call-start = ((), (), s32[]{:S(2)}) async-start(), calls=%async_computation | async-start | bytes 2359296 | tf_op jit(solution)/shard_map/all_gather | solution.py:48
  116.1 1.0 copy-start.3
  168.9 1.0 copy-start.2
Sparse Core Ops, SparseCore 0:
  29.7 80.0 all-reduce.2
  112.2 48.6 all-gather.1

commit v2 on v1

v2 whole, which is shorter than its diff:
```python
import jax
import jax.numpy as jnp
import numpy as np
from jax import lax
from jax.sharding import Mesh, PartitionSpec as P

BF16 = jnp.bfloat16


def silu_slope(pre):
    sig = jax.nn.sigmoid(pre)
    return sig * (1.0 + pre * (1.0 - sig))


def moment(left, right):
    return lax.dot_general(
        left, right, (((0,), (0,)), ((), ())), preferred_element_type=jnp.float32
    )


def mul(left, right):
    return jnp.dot(left, right, precision=lax.Precision.HIGH)


def inverse(matrix):
    eye = jnp.eye(matrix.shape[0], dtype=jnp.float32)
    scale = lax.rsqrt(jnp.sum(matrix * matrix))
    first = matrix * scale
    second = 2.0 * first - mul(first, first)
    square = mul(second, second)
    tail = mul(2.0 * eye - second, 2.0 * eye - 2.0 * second + square)
    return mul(2.0 * eye - first, tail) * scale


def packed(full):
    half = full.shape[1] // 2
    return jnp.concatenate([full[:, :half], full[:, half:]], axis=0)


def unpacked(rows):
    half = rows.shape[0] // 2
    return jnp.concatenate([rows[:half], rows[half:]], axis=1)


def packed_symmetric(full):
    half = full.shape[1] // 2
    return jnp.concatenate([full[:, :half], full[half:, half:]], axis=0)


def unpacked_symmetric(rows):
    half = rows.shape[1]
    low = rows[half:2 * half]
    return jnp.concatenate(
        [
            jnp.concatenate([rows[:half], low.T], axis=1),
            jnp.concatenate([low, rows[2 * half:]], axis=1),
        ],
        axis=0,
    )


def body(acts, weights, cot_last):
    pairs = lax.axis_size("row")
    line = lax.axis_size("line")
    row = lax.axis_index("row")
    core = lax.axis_index("core")
    side = lax.axis_index("side")
    weight = weights[0]
    local = acts[0]
    micro, rows, width = local.shape
    count = micro * rows * line * lax.axis_size("side")
    eye = jnp.eye(width, dtype=jnp.float32)
    odd = core == 1
    swap = [(0, 1), (1, 0)]

    partner_weight = lax.ppermute(weight, "core", swap)
    mine = jnp.where(odd, local[1], local[0])
    partner = lax.ppermute(jnp.where(odd, local[0], local[1]), "core", swap)
    weight_odd = jnp.where(odd, weight, partner_weight)
    weight_even = jnp.where(odd, partner_weight, weight)
    x_odd = jnp.where(odd, mine, partner)
    x_even = jnp.where(odd, partner, mine)
    slope_odd = silu_slope(jnp.dot(x_odd, weight_odd, preferred_element_type=jnp.float32))
    slope_even = silu_slope(jnp.dot(x_even, weight_even, preferred_element_type=jnp.float32))

    def layer(upstream, slope, matrix):
        dh = (upstream.astype(jnp.float32) * slope).astype(BF16)
        back = lax.dot_general(dh, matrix, (((1,), (1,)), ((), ())), preferred_element_type=jnp.float32)
        return dh, (upstream.astype(jnp.float32) + back).astype(BF16)

    upstream = jnp.where(odd, cot_last[1], cot_last[0])
    for turn in range(pairs):
        now = (layer(upstream, slope_odd, weight_odd),)
        now += (layer(now[0][1], slope_even, weight_even),)
        if turn == 0:
            kept = now
        else:
            here = row == pairs - 1 - turn
            kept = jax.tree.map(lambda new, old: jnp.where(here, new, old), now, kept)
        if turn < pairs - 1:
            upstream = lax.ppermute(now[1][1], "row", [(r, r - 1) for r in range(1, pairs)])
    (dh_odd, cot_odd), (dh_even, cot_even) = kept

    other_cot = lax.ppermute(jnp.where(odd, cot_even, cot_odd), "core", swap)
    own_cot = jnp.where(odd, cot_odd, cot_even)
    cot = jnp.stack([jnp.where(odd, other_cot, own_cot), jnp.where(odd, own_cot, other_cot)])

    dh = lax.all_to_all(
        jnp.concatenate([dh_even, dh_even, dh_odd, dh_odd]), ("core", "side"), 0, 0, tiled=True
    )
    far = lax.ppermute(local, "side", swap)
    first = jnp.where(side == 0, local, far)
    second = jnp.where(side == 0, far, local)
    x = jnp.stack([first, second], axis=1).reshape(-1, width)

    sums = jnp.concatenate(
        [
            packed_symmetric(moment(dh, dh).astype(BF16)),
            packed_symmetric(moment(x, x).astype(BF16)),
            packed(moment(x, dh).astype(BF16)),
        ]
    )
    height, across = sums.shape
    part = height // 2 // line
    half = lax.dynamic_slice_in_dim(sums, side * (height // 2), height // 2, 0)
    parts = lax.all_to_all(half, "line", 0, 0, tiled=True).reshape(line, part, across)
    total = jnp.sum(parts.astype(jnp.float32), axis=0).astype(BF16)
    copies = jnp.broadcast_to(total[None], (line * 2, part, across))
    every = lax.all_to_all(copies, ("line", "side"), 0, 0, tiled=True)
    every = every.reshape(line, 2, part, across).swapaxes(0, 1).reshape(height, across)
    every = every.astype(jnp.float32)
    cut = 3 * width // 2
    out_inv = inverse(unpacked_symmetric(every[:cut]) / count + 0.01 * eye)
    act_inv = inverse(unpacked_symmetric(every[cut:2 * cut]) / count + 0.01 * eye)
    update = mul(mul(act_inv, unpacked(every[2 * cut:])), out_inv)
    return (cot[None], update[None])


def solution(mesh):
    sections, shards = mesh.devices.shape
    finer = Mesh(
        np.reshape(mesh.devices, (sections // 2, 2, shards // 2, 2)),
        ("row", "core", "line", "side"),
    )
    section, dp = ("row", "core"), ("line", "side")
    placed = (P(section, None, dp, None), P(section, None, None), P(None, dp, None))
    return jax.shard_map(
        body,
        mesh=finer,
        in_specs=placed,
        out_specs=(P(section, None, dp, None), P(section, None, None)),
        check_vma=False,
    )
```

time: 180 us -> 104 us (0.58)
  waiting for transfers between devices: 132 us -> 41.9 us
  blocking collectives: 0 us -> 22.4 us
  between operations: 15.7 us -> 2.36 us
  matrix products: 24.9 us -> 14.8 us
  starting transfers between devices: 4.95 us -> 12.3 us
  local copies, waits for them, and re-layouts: 0.03 us -> 4.17 us
  other arithmetic: 1.92 us -> 5.16 us
    psum x1 -> x0, waiting for transfers between devices: 78.4 us -> none  [body(): lax.psum((moment(dh, dh).astype(jnp.bfloat16), moment(flat, dh).astype(jn...]
    all_gather x1 -> x0, waiting for transfers between devices: 42.7 us -> none  [body(): every = lax.all_gather(flat, 'dp', tiled=True)]
    all_to_all x0 -> x2, waiting for transfers between devices: none -> 36.3 us  [the longest x1 28 us: body(): every = lax.all_to_all(copies, ('line', 'side'), 0, 0, tiled=True)]
    all_to_all x0 -> x1, blocking collectives: none -> 22.4 us  [body(): lax.all_to_all(half, 'line', 0, 0, tiled=True).reshape(line, part, across)]
    all_to_all x0 -> x2, starting transfers between devices: none -> 7.35 us  [the longest x1 3.75 us: body(): every = lax.all_to_all(copies, ('line', 'side'), 0, 0, tiled=True)]
    dot_general x3, matrix products: 6.51 us -> 1.39 us  [moment(): lax.dot_general(left, right, (((0,), (0,)), ((), ())), preferred_element_...]
    ppermute x4 -> x5, waiting for transfers between devices: 10.4 us -> 5.64 us  [the longest x1 3.73 us: body(): lax.ppermute(now[1][1], 'row', [(r, r - 1) for r in range(1, pairs)])]
    dot_general x4, matrix products: 3.93 us -> 1.24 us  [layer(): lax.dot_general(dh, matrix, (((1,), (1,)), ((), ())), preferred_element_t...]
  transfers between devices with their start and end apart: 6 -> 7, of which waited for: 4 -> 5; matrix products, arithmetic and copies ran while one was open for 6% -> 5% of each run, Pallas kernels for 0% -> 0%
where the time goes in v2:
time: 104 us; the launch traced here: 103 us
  waiting for transfers between devices  41.9 us (40%)
  blocking collectives  22.4 us (22%)
  matrix products  14.8 us (14%)
  starting transfers between devices  12.3 us (12%)
  other arithmetic  5.16 us (5%)
  local copies, waits for them, and re-layouts  4.17 us (4%)
  between operations  2.36 us (2%)
    all_to_all x1, waiting for transfers between devices, body(): every = lax.all_to_all(copies, ('line', 'side'), 0, 0, tiled=True)  28 us
    all_to_all x1, blocking collectives, body(): lax.all_to_all(half, 'line', 0, 0, tiled=True).reshape(line, part, across)  22.4 us
    dot_general x10, matrix products, mul(): return jnp.dot(left, right, precision=lax.Precision.HIGH)  11.6 us
    all_to_all x1, waiting for transfers between devices, body(): lax.all_to_all(jnp.concatenate([dh_even, dh_even, dh_odd, dh_odd]), ('cor...  8.27 us
    all_to_all x1, starting transfers between devices, body(): every = lax.all_to_all(copies, ('line', 'side'), 0, 0, tiled=True)  3.75 us
    ppermute x1, waiting for transfers between devices, body(): lax.ppermute(now[1][1], 'row', [(r, r - 1) for r in range(1, pairs)])  3.73 us
    all_to_all x1, starting transfers between devices, body(): lax.all_to_all(jnp.concatenate([dh_even, dh_even, dh_odd, dh_odd]), ('cor...  3.6 us
    ppermute x1, starting transfers between devices, body(): far = lax.ppermute(local, 'side', swap)  2.92 us
  transfers between devices with their start and end apart: 7, of which 5 were waited for; matrix products, arithmetic and copies ran while one was open for 5% of the time, Pallas kernels for 0%

profile of v2, /device:TPU:0, one launch (start us, length us, event | category | flops | bytes accessed | tf_op | source)
XLA Modules:
  0.0 103.2 jit_solution(17776847783926786879)
XLA Ops:
  0.6 0.0 copy-start
  0.6 0.0 copy-start.1
  0.7 0.5 collective-permute-start.1
  1.2 1.0 select_bitcast_fusion.4
  2.2 0.2 collective-permute-start
  2.3 0.6 collective-permute-done.1
  2.9 1.1 %broadcast_select_fusion = bf16[512,512]{1,0:T(8,128)(2,1)S(1)} fusion(bf16[512,512]{1,0:T(8,128)(2,1)S(1)} %collective-permute-done.1, pred[]{:T(512)S(6)} %eq.29, bf16[1,512,512]{2,1,0:T(8,128)(2,1)} %param.4), kind=kLoop, calls=%fused_computation.60 | loop fusion | flops 262144 | bytes 1572865 | tf_op jit(solution)/shard_map/jit(_where)/select_n | solution.py:80
  4.0 0.0 collective-permute-done
  4.0 0.0 copy-done
  4.0 0.0 copy-done.1
  4.0 0.3 add_multiply_fusion.1
  4.4 0.0 copy-start.3
  4.4 0.3 add_multiply_fusion
  4.7 0.6 copy-done.3
  5.3 0.3 fusion.2
  5.6 0.3 fusion.3
  5.9 1.3 %collective-permute-start.2 = (bf16[128,512]{1,0:T(8,128)(2,1)S(1)}, bf16[128,512]{1,0:T(8,128)(2,1)S(1)}, u32[]{:S(2)}, u32[]{:S(2)}) collective-permute-start(bf16[128,512]{1,0:T(8,128)(2,1)S(1)} %fusion.3), channel_id=1, source_target_pairs={{16,0},{17,1},{18,2},{19,3},{20,4},{21,5},{22,6},{23,7},{24,8},{25... | collective-permute-start | bytes 393224 | tf_op jit(solution)/shard_map/ppermute | solution.py:101
  7.2 2.9 %collective-permute-start.4 = (bf16[2,128,512]{2,1,0:T(8,128)(2,1)S(1)}, bf16[2,128,512]{2,1,0:T(8,128)(2,1)S(1)}, u32[]{:S(2)}, u32[]{:S(2)}) collective-permute-start(bf16[2,128,512]{2,1,0:T(8,128)(2,1)S(1)} %bitcast.86), channel_id=1, source_target_pairs={{0,1},{1,0},{2,3},{3,2},{4,5},{5,4},{6,7},{7,6},{8,9},{9,8},{10,11... | collective-permute-start | bytes 786440 | tf_op jit(solution)/shard_map/ppermute | solution.py:111
  10.2 3.7 %collective-permute-done.2 = bf16[128,512]{1,0:T(8,128)(2,1)S(1)} collective-permute-done((bf16[128,512]{1,0:T(8,128)(2,1)S(1)}, bf16[128,512]{1,0:T(8,128)(2,1)S(1)}, u32[]{:S(2)}, u32[]{:S(2)}) %collective-permute-start.2) | collective-permute-done | bytes 131104 | tf_op jit(solution)/shard_map/ppermute | solution.py:101
  13.9 0.3 fusion.4
  14.2 0.3 broadcast_select_fusion.7
  14.5 0.1 broadcast_select_fusion.3
  14.6 0.8 pad_maximum_fusion
  15.4 3.6 %all-to-all-start = ((bf16[4,128,512]{2,1,0:T(8,128)(2,1)}), bf16[4,128,512]{2,1,0:T(8,128)(2,1)S(1)}, u32[]{:S(2)}, u32[]{:S(2)}) async-start(bf16[4,128,512]{2,1,0:T(8,128)(2,1)} %bitcast.8), calls=%async_computation | async-start | bytes 1048576 | tf_op jit(solution)/shard_map/all_to_all | solution.py:108
  19.0 0.0 collective-permute-done.4
  19.1 0.5 fusion.1
  19.6 0.1 pad_maximum_fusion.1
  19.6 8.3 %all-to-all-done = bf16[4,128,512]{2,1,0:T(8,128)(2,1)S(1)} async-done(((bf16[4,128,512]{2,1,0:T(8,128)(2,1)}), bf16[4,128,512]{2,1,0:T(8,128)(2,1)S(1)}, u32[]{:S(2)}, u32[]{:S(2)}) %all-to-all-start) | async-done | bytes 524320 | tf_op jit(solution)/shard_map/all_to_all | solution.py:108
  27.9 0.5 fusion
  28.5 0.5 convolution_convert_fusion
  29.0 0.1 constant_dynamic-slice_fusion
  29.0 22.4 %all_to_all.26 = bf16[4,320,256]{2,1,0:T(8,128)(2,1)S(1)} all-to-all(bf16[4,320,256]{2,1,0:T(8,128)(2,1)S(1)} %bitcast.84), channel_id=1, replica_groups=mesh['row'=2,'core'=2,'line'=4,'side'=2] {'line'}, dimensions={0} | all-to-all | bytes 1310720 | tf_op jit(solution)/shard_map/all_to_all | solution.py:126
  51.5 0.1 reduce_sum.30
  51.6 1.2 %broadcast_in_dim.13 = bf16[8,320,256]{2,1,0:T(8,128)(2,1)} broadcast(bf16[320,256]{1,0:T(8,128)(2,1)S(1)} %reduce_sum.30), dimensions={1,2} | broadcast | bytes 1474560 | tf_op jit(solution)/shard_map/broadcast_in_dim | solution.py:128
  52.8 3.7 %all-to-all-start.2 = ((bf16[8,320,256]{2,1,0:T(8,128)(2,1)}), bf16[8,320,256]{2,1,0:T(8,128)(2,1)S(1)}, u32[]{:S(2)}, u32[]{:S(2)}) async-start(bf16[8,320,256]{2,1,0:T(8,128)(2,1)} %broadcast_in_dim.13), calls=%async_computation.2 | async-start | bytes 2621440 | tf_op jit(solution)/shard_map/all_to_all | solution.py:129
  56.5 0.1 collective-permute-start.3
  56.6 1.3 %collective-permute-done.3 = bf16[128,512]{1,0:T(8,128)(2,1)S(1)} collective-permute-done((bf16[128,512]{1,0:T(8,128)(2,1)S(1)}, bf16[128,512]{1,0:T(8,128)(2,1)S(1)}, u32[]{:S(2)}, u32[]{:S(2)}) %collective-permute-start.3) | collective-permute-done | bytes 131104 | tf_op jit(solution)/shard_map/ppermute | solution.py:104
  58.0 0.7 maximum_bitcast_fusion
  58.7 28.0 %all-to-all-done.2 = bf16[8,320,256]{2,1,0:T(8,128)(2,1)S(1)} async-done(((bf16[8,320,256]{2,1,0:T(8,128)(2,1)}), bf16[8,320,256]{2,1,0:T(8,128)(2,1)S(1)}, u32[]{:S(2)}, u32[]{:S(2)}) %all-to-all-start.2) | async-done | bytes 1310752 | tf_op jit(solution)/shard_map/all_to_all | solution.py:129
  86.7 0.2 convert_bitcast_fusion
  87.0 0.2 copy.15
  87.2 0.1 fusion.51
  87.2 0.9 fusion.50
  88.1 0.1 copy.24
  88.3 0.0 copy-start.2
  88.3 0.2 copy.19
  88.5 0.1 copy.23
  88.6 0.6 copy-done.2
  89.2 1.0 multiply_reduce_fusion
  91.6 1.1 %convolution_subtract_fusion = f32[512,512]{1,0:T(8,128)S(1)} fusion(f32[]{:T(128)S(6)} %rsqrt.7, f32[256,256]{1,0:T(8,128)S(1)} %get-tuple-element.8, f32[256,256]{1,0:T(8,128)S(1)} %get-tuple-element.7, f32[256,512]{1,0:T(8,128)S(1)} %copy.19), kind=kOutput, calls=%fused_computation.12 | convolution fusion | flops 809500672 | bytes 2097156 | tf_op jit(solution)/shard_map/dot_general | solution.py:22
  92.7 1.1 %convolution_subtract_fusion.1 = f32[512,512]{1,0:T(8,128)S(1)} fusion(f32[]{:T(128)S(6)} %rsqrt.6, f32[256,256]{1,0:T(8,128)S(1)} %get-tuple-element.9, f32[256,256]{1,0:T(8,128)S(1)} %get-tuple-element.6, f32[256,256]{1,0:T(8,128)S(1)} %bitcast.88, f32[256,256]{1,0:T(8,128)S(1)} %copy-done.2), kind=kOutput, calls=%fused_computation.15 | convolution fusion | flops 810024960 | bytes 2097156 | tf_op jit(solution)/shard_map/dot_general | solution.py:22
  93.8 1.1 %convolution_add_fusion.1 = f32[512,512]{1,0:T(8,128)S(1)} fusion(f32[512,512]{1,0:T(8,128)S(1)} %convolution_subtract_fusion.1), kind=kOutput, calls=%fused_computation.14 | convolution fusion | flops 806617088 | bytes 2097152 | tf_op jit(solution)/shard_map/dot_general | solution.py:22
  94.9 1.0 fusion.7
  95.9 1.1 %convolution_multiply_fusion.1 = f32[512,512]{1,0:T(8,128)S(1)} fusion(f32[512,512]{1,0:T(8,128)S(1)} %fusion.7, f32[]{:T(128)S(6)} %rsqrt.6, f32[256,256]{1,0:T(8,128)S(1)} %get-tuple-element.9, f32[256,256]{1,0:T(8,128)S(1)} %get-tuple-element.6, f32[256,256]{1,0:T(8,128)S(1)} %bitcast.89, f32[256,256]{1,0:T(8,128)S(1)} %copy-done.2), kind=kOutput, calls=%fused_computation.13 | convolution fusion | flops 808189952 | bytes 3145732 | tf_op jit(solution)/shard_map/dot_general | solution.py:22
  97.0 1.1 %convolution_add_fusion = f32[512,512]{1,0:T(8,128)S(1)} fusion(f32[512,512]{1,0:T(8,128)S(1)} %convolution_subtract_fusion), kind=kOutput, calls=%fused_computation.11 | convolution fusion | flops 806617088 | bytes 2097152 | tf_op jit(solution)/shard_map/dot_general | solution.py:22
  98.1 1.0 fusion.8
  99.1 1.1 %convolution_multiply_fusion = f32[512,512]{1,0:T(8,128)S(1)} fusion(f32[512,512]{1,0:T(8,128)S(1)} %fusion.8, f32[]{:T(128)S(6)} %rsqrt.7, f32[256,256]{1,0:T(8,128)S(1)} %get-tuple-element.8, f32[256,256]{1,0:T(8,128)S(1)} %get-tuple-element.7, f32[256,512]{1,0:T(8,128)S(1)} %copy.19), kind=kOutput, calls=%fused_computation.10 | convolution fusion | flops 807927808 | bytes 3145732 | tf_op jit(solution)/shard_map/dot_general | solution.py:22
  100.2 1.0 fusion.9
  101.2 2.0 %convolution_bitcast_fusion = f32[1,512,512]{2,1,0:T(8,128)} fusion(f32[512,512]{1,0:T(8,128)S(1)} %fusion.9, f32[512,512]{1,0:T(8,128)S(1)} %convolution_multiply_fusion), kind=kOutput, calls=%fused_computation.9 | convolution fusion | flops 805306368 | bytes 3145728 | tf_op jit(solution)/shard_map/dot_general | solution.py:22
  (9 shorter events, 0.2 us)
Async XLA Ops:
  0.6 3.4 %copy-start = (bf16[1,512,512]{2,1,0:T(8,128)(2,1)S(1)}, bf16[1,512,512]{2,1,0:T(8,128)(2,1)}, u32[]{:S(2)}) copy-start(bf16[1,512,512]{2,1,0:T(8,128)(2,1)} %param.4) | copy-start | bytes 1572868
  0.6 3.4 %copy-start.1 = (bf16[1,2,128,512]{3,2,1,0:T(8,128)(2,1)S(1)}, bf16[1,2,128,512]{3,2,1,0:T(8,128)(2,1)}, u32[]{:S(2)}) copy-start(bf16[1,2,128,512]{3,2,1,0:T(8,128)(2,1)} %param.3) | copy-start | bytes 786436
  0.7 2.3 %collective-permute-start.1 = (bf16[512,512]{1,0:T(8,128)(2,1)}, bf16[512,512]{1,0:T(8,128)(2,1)S(1)}, u32[]{:S(2)}, u32[]{:S(2)}) collective-permute-start(bf16[512,512]{1,0:T(8,128)(2,1)} %bitcast.85), channel_id=1, source_target_pairs={{0,8},{8,0},{1,9},{9,1},{2,10},{10,2},{3,11},{11,3},{4,12},{12,4},... | collective-permute-start | bytes 1572872 | tf_op jit(solution)/shard_map/ppermute | solution.py:76
  2.2 1.9 %collective-permute-start = (bf16[128,512]{1,0:T(8,128)(2,1)S(1)}, bf16[128,512]{1,0:T(8,128)(2,1)S(1)}, u32[]{:S(2)}, u32[]{:S(2)}) collective-permute-start(bf16[128,512]{1,0:T(8,128)(2,1)S(1)} %select_bitcast_fusion.4), channel_id=1, source_target_pairs={{0,8},{8,0},{1,9},{9,1},{2,10},{10,2},{3,11},{11,3},{4,12},{12,4},... | collective-permute-start | bytes 393224 | tf_op jit(solution)/shard_map/ppermute | solution.py:78
  4.4 1.0 copy-start.3
  5.9 8.0 %collective-permute-start.2 = (bf16[128,512]{1,0:T(8,128)(2,1)S(1)}, bf16[128,512]{1,0:T(8,128)(2,1)S(1)}, u32[]{:S(2)}, u32[]{:S(2)}) collective-permute-start(bf16[128,512]{1,0:T(8,128)(2,1)S(1)} %fusion.3), channel_id=1, source_target_pairs={{16,0},{17,1},{18,2},{19,3},{20,4},{21,5},{22,6},{23,7},{24,8},{25... | collective-permute-start | bytes 393224 | tf_op jit(solution)/shard_map/ppermute | solution.py:101
  7.2 11.8 %collective-permute-start.4 = (bf16[2,128,512]{2,1,0:T(8,128)(2,1)S(1)}, bf16[2,128,512]{2,1,0:T(8,128)(2,1)S(1)}, u32[]{:S(2)}, u32[]{:S(2)}) collective-permute-start(bf16[2,128,512]{2,1,0:T(8,128)(2,1)S(1)} %bitcast.86), channel_id=1, source_target_pairs={{0,1},{1,0},{2,3},{3,2},{4,5},{5,4},{6,7},{7,6},{8,9},{9,8},{10,11... | collective-permute-start | bytes 786440 | tf_op jit(solution)/shard_map/ppermute | solution.py:111
  15.4 12.4 %all-to-all-start = ((bf16[4,128,512]{2,1,0:T(8,128)(2,1)}), bf16[4,128,512]{2,1,0:T(8,128)(2,1)S(1)}, u32[]{:S(2)}, u32[]{:S(2)}) async-start(bf16[4,128,512]{2,1,0:T(8,128)(2,1)} %bitcast.8), calls=%async_computation | async-start | bytes 1048576 | tf_op jit(solution)/shard_map/all_to_all | solution.py:108
  52.8 33.9 %all-to-all-start.2 = ((bf16[8,320,256]{2,1,0:T(8,128)(2,1)}), bf16[8,320,256]{2,1,0:T(8,128)(2,1)S(1)}, u32[]{:S(2)}, u32[]{:S(2)}) async-start(bf16[8,320,256]{2,1,0:T(8,128)(2,1)} %broadcast_in_dim.13), calls=%async_computation.2 | async-start | bytes 2621440 | tf_op jit(solution)/shard_map/all_to_all | solution.py:129
  56.5 1.4 %collective-permute-start.3 = (bf16[128,512]{1,0:T(8,128)(2,1)S(1)}, bf16[128,512]{1,0:T(8,128)(2,1)S(1)}, u32[]{:S(2)}, u32[]{:S(2)}) collective-permute-start(bf16[128,512]{1,0:T(8,128)(2,1)S(1)} %get-tuple-element.2), channel_id=1, source_target_pairs={{0,8},{8,0},{1,9},{9,1},{2,10},{10,2},{3,11},{11,3},{4,12},{12,4},... | collective-permute-start | bytes 393224 | tf_op jit(solution)/shard_map/ppermute | solution.py:104
  88.3 1.0 copy-start.2

commit v3 on v1

v3 whole, which is shorter than its diff:
```python
import jax
import jax.numpy as jnp
import numpy as np
from jax import lax
from jax.sharding import Mesh, PartitionSpec as P

BF16 = jnp.bfloat16
SWAP = [(0, 1), (1, 0)]


def silu_slope(pre):
    sig = jax.nn.sigmoid(pre)
    return sig * (1.0 + pre * (1.0 - sig))


def moment(left, right):
    return lax.dot_general(
        left, right, (((0,), (0,)), ((), ())), preferred_element_type=jnp.float32
    )


def mul(left, right):
    return jnp.dot(left, right, precision=lax.Precision.HIGH)


def inverse(matrix):
    eye = jnp.eye(matrix.shape[0], dtype=jnp.float32)
    scale = lax.rsqrt(jnp.sum(matrix * matrix))
    first = matrix * scale
    second = 2.0 * first - mul(first, first)
    square = mul(second, second)
    tail = mul(2.0 * eye - second, 2.0 * eye - 2.0 * second + square)
    return mul(2.0 * eye - first, tail) * scale


def rolled(full, side, axis):
    half = full.shape[axis] // 2
    low = lax.slice_in_dim(full, 0, half, axis=axis)
    high = lax.slice_in_dim(full, half, 2 * half, axis=axis)
    return jnp.where(side == 0, full, jnp.concatenate([high, low], axis=axis))


def half_factor(full, side):
    quarter = full.shape[0] // 4
    mine = lax.dynamic_slice_in_dim(full, side * 2 * quarter, 2 * quarter, 0)
    mine = rolled(mine, side, 1)
    top = (jnp.arange(2 * quarter) < quarter)[:, None]
    return jnp.where(top, mine[:, :3 * quarter], mine[:, quarter:])


def whole_factor(mine, other):
    quarter = mine.shape[0] // 2

    def block(source, row, column):
        return source[row * quarter:(row + 1) * quarter, column * quarter:(column + 1) * quarter]

    def across(row):
        return jnp.concatenate(row, axis=1)

    return jnp.concatenate(
        [
            across([mine[:quarter], block(other, 1, 1).T]),
            across([block(mine, 0, 1).T, mine[quarter:]]),
            across([block(other, 0, 2), block(mine, 1, 1).T, other[:quarter, :2 * quarter]]),
            across([other[quarter:, quarter:], block(other, 0, 1).T, block(other, 1, 0)]),
        ]
    )


def scatter_sum(parts):
    line = lax.axis_size("line")
    place = lax.axis_index("line")
    total = lax.dynamic_index_in_dim(parts, place, 0, keepdims=False).astype(jnp.float32)
    for step in sorted(range(1, line), key=lambda k: -min(k, line - k)):
        term = lax.dynamic_index_in_dim(parts, (place + step) % line, 0, keepdims=False)
        route = [(i, (i + step) % line) for i in range(line)]
        total += lax.ppermute(term, "line", route).astype(jnp.float32)
    return total


def gather(part):
    line = lax.axis_size("line")
    place = lax.axis_index("line")
    every = jnp.zeros((line,) + part.shape, part.dtype)
    every = lax.dynamic_update_index_in_dim(every, part, place, 0)
    for step in sorted(range(1, line), key=lambda k: -min(k, line - k)):
        route = [(i, (i + step) % line) for i in range(line)]
        got = lax.ppermute(part, "line", route)
        every = lax.dynamic_update_index_in_dim(every, got, (place - step) % line, 0)
    return every.reshape((line * part.shape[0],) + part.shape[1:])


def body(acts, weights, cot_last):
    pairs = lax.axis_size("row")
    line = lax.axis_size("line")
    row = lax.axis_index("row")
    core = lax.axis_index("core")
    side = lax.axis_index("side")
    weight = weights[0]
    local = acts[0]
    micro, rows, width = local.shape
    count = micro * rows * line * 2
    eye = jnp.eye(width, dtype=jnp.float32)
    odd = core == 1

    def mine_of(pair):
        return jnp.where(odd, pair[1], pair[0])

    def others_of(pair):
        return jnp.where(odd, pair[0], pair[1])

    partner_weight = lax.ppermute(weight, "core", SWAP)
    partner_x = lax.ppermute(others_of(local), "core", SWAP)
    weight_odd = jnp.where(odd, weight, partner_weight)
    weight_even = jnp.where(odd, partner_weight, weight)

    def slopes(own, partner):
        def slope(inputs, matrix):
            return silu_slope(jnp.dot(inputs, matrix, preferred_element_type=jnp.float32))

        return (
            slope(jnp.where(odd, own, partner), weight_odd),
            slope(jnp.where(odd, partner, own), weight_even),
        )

    def layer(upstream, slope, matrix):
        dh = (upstream.astype(jnp.float32) * slope).astype(BF16)
        back = lax.dot_general(dh, matrix, (((1,), (1,)), ((), ())), preferred_element_type=jnp.float32)
        return dh, (upstream.astype(jnp.float32) + back).astype(BF16)

    def layers(upstream, slope):
        dh_odd, cot_odd = layer(upstream, slope[0], weight_odd)
        return (dh_odd, cot_odd) + layer(cot_odd, slope[1], weight_even)

    slope_near = slopes(mine_of(local), partner_x)
    last = mine_of(cot_last)
    near = layers(last, slope_near)
    upstream_far = lax.ppermute(last, "side", SWAP)
    far = lax.ppermute(local, "side", SWAP)
    slope_far = slopes(mine_of(far), lax.ppermute(others_of(far), "core", SWAP))
    latest = near
    for turn in range(1, pairs):
        straight = [(r, r - 1) for r in range(1, pairs)]
        diagonal = [(2 * r + s, 2 * r - 1 - s) for r in range(1, pairs) for s in range(2)]
        upstream = lax.ppermute(latest[3], "row", straight)
        crossing = lax.ppermute(latest[3], ("row", "side"), diagonal)
        latest = layers(upstream, slope_near)
        here = row == pairs - 1 - turn
        near = jax.tree.map(lambda new, old: jnp.where(here, new, old), latest, near)
        upstream_far = jnp.where(here, crossing, upstream_far)

    x = jnp.concatenate([mine_of(local), mine_of(far), others_of(local), others_of(far)])
    act_half = half_factor(moment(x, x).astype(BF16), side)
    act_half = gather(scatter_sum(act_half.reshape(line, -1, act_half.shape[1])).astype(BF16))
    act_sum = whole_factor(act_half, lax.ppermute(act_half, "side", SWAP)).astype(jnp.float32)
    act_sum = rolled(rolled(act_sum, side, 0), side, 1)
    act_inv = inverse(act_sum / count + 0.01 * eye)

    away = layers(upstream_far, slope_far)
    other_cot = lax.ppermute(others_of((near[3], near[1])), "core", SWAP)
    own_cot = mine_of((near[3], near[1]))
    cot = jnp.stack([mine_of((own_cot, other_cot)), mine_of((other_cot, own_cot))])
    own_dh = jnp.concatenate([mine_of((near[2], near[0])), mine_of((away[2], away[0]))])
    give_dh = jnp.concatenate([others_of((near[2], near[0])), others_of((away[2], away[0]))])
    dh = jnp.concatenate([own_dh, lax.ppermute(give_dh, "core", SWAP)])

    out_half = half_factor(moment(dh, dh).astype(BF16), side)
    grad_half = lax.dynamic_slice_in_dim(moment(dh, x).astype(BF16), side * (width // 2), width // 2, 0)
    both = jnp.concatenate([out_half, grad_half], axis=1)
    total = scatter_sum(both.reshape(line, -1, both.shape[1]))
    cut = out_half.shape[1]
    out_half = gather(total[:, :cut].astype(BF16))
    out_other = lax.ppermute(out_half, "side", SWAP)
    half = gather(mul(total[:, cut:], act_inv).astype(BF16))
    other = lax.ppermute(half, "side", SWAP)
    out_inv = inverse(whole_factor(out_half, out_other).astype(jnp.float32) / count + 0.01 * eye)
    rows_of = jnp.concatenate([half, other]).astype(jnp.float32)
    update = lax.dot_general(rows_of, out_inv, (((0,), (0,)), ((), ())), precision=lax.Precision.HIGH)
    return (cot[None], rolled(update, side, 1)[None])


def solution(mesh):
    sections, shards = mesh.devices.shape
    finer = Mesh(
        np.reshape(mesh.devices, (sections // 2, 2, shards // 2, 2)),
        ("row", "core", "line", "side"),
    )
    section, dp = ("row", "core"), ("line", "side")
    placed = (P(section, None, dp, None), P(section, None, None), P(None, dp, None))
    return jax.shard_map(
        body,
        mesh=finer,
        in_specs=placed,
        out_specs=(P(section, None, dp, None), P(section, None, None)),
        check_vma=False,
    )
```

time: 180 us -> 93.1 us (0.52)
  waiting for transfers between devices: 132 us -> 28.4 us
  starting transfers between devices: 4.95 us -> 39.5 us
  between operations: 15.7 us -> 2.73 us
  matrix products: 24.9 us -> 13.7 us
  other arithmetic: 1.92 us -> 5.48 us
  local copies, waits for them, and re-layouts: 0.03 us -> 3.01 us
    psum x1 -> x0, waiting for transfers between devices: 78.4 us -> none  [body(): lax.psum((moment(dh, dh).astype(jnp.bfloat16), moment(flat, dh).astype(jn...]
    all_gather x1 -> x0, waiting for transfers between devices: 42.7 us -> none  [body(): every = lax.all_gather(flat, 'dp', tiled=True)]
    ppermute x4 -> x27, starting transfers between devices: 4.69 us -> 39.5 us  [the longest x9 16.7 us: gather(): got = lax.ppermute(part, 'line', route)]
    ppermute x4 -> x27, waiting for transfers between devices: 10.4 us -> 28.4 us  [the longest x9 11.3 us: gather(): got = lax.ppermute(part, 'line', route)]
    dot_general x3, matrix products: 6.51 us -> 1.45 us  [moment(): lax.dot_general(left, right, (((0,), (0,)), ((), ())), preferred_element_...]
    dot_general x10 -> x9, matrix products: 12.5 us -> 8.69 us  [mul(): return jnp.dot(left, right, precision=lax.Precision.HIGH)]
    dot_general x4 -> x5, matrix products: 3.93 us -> 1.67 us  [layer(): lax.dot_general(dh, matrix, (((1,), (1,)), ((), ())), preferred_element_t...]
    broadcast_in_dim x0 -> x2, other arithmetic: none -> 1.86 us  [body(): return (cot[None], rolled(update, side, 1)[None])]
  transfers between devices with their start and end apart: 6 -> 27, of which waited for: 4 -> 12; matrix products, arithmetic and copies ran while one was open for 6% -> 19% of each run, Pallas kernels for 0% -> 0%
where the time goes in v3:
time: 93.1 us; the launch traced here: 92.9 us
  starting transfers between devices  39.5 us (42%)
  waiting for transfers between devices  28.4 us (31%)
  matrix products  13.7 us (15%)
  other arithmetic  5.48 us (6%)
  local copies, waits for them, and re-layouts  3.01 us (3%)
  between operations  2.73 us (3%)
    ppermute x9, starting transfers between devices, gather(): got = lax.ppermute(part, 'line', route)  16.7 us
    ppermute x6, starting transfers between devices, scatter_sum(): total += lax.ppermute(term, 'line', route).astype(jnp.float32)  12.7 us
    ppermute x9, waiting for transfers between devices, gather(): got = lax.ppermute(part, 'line', route)  11.3 us
    dot_general x9, matrix products, mul(): return jnp.dot(left, right, precision=lax.Precision.HIGH)  8.69 us
    ppermute x1, waiting for transfers between devices, body(): far = lax.ppermute(local, 'side', SWAP)  6.87 us
    ppermute x1, waiting for transfers between devices, body(): upstream = lax.ppermute(latest[3], 'row', straight)  4.95 us
    ppermute x1, starting transfers between devices, body(): far = lax.ppermute(local, 'side', SWAP)  2.94 us
    ppermute x6, waiting for transfers between devices, scatter_sum(): total += lax.ppermute(term, 'line', route).astype(jnp.float32)  2.57 us
  transfers between devices with their start and end apart: 27, of which 12 were waited for; matrix products, arithmetic and copies ran while one was open for 19% of the time, Pallas kernels for 0%

profile of v3, /device:TPU:0, one launch (start us, length us, event | category | flops | bytes accessed | tf_op | source)
XLA Modules:
  0.0 92.9 jit_solution(3662866957308553097)
XLA Ops:
  0.6 0.5 collective-permute-start.1
  1.2 1.0 %select_bitcast_fusion.4 = (bf16[128,512]{1,0:T(8,128)(2,1)S(1)}, bf16[128,512]{1,0:T(8,128)(2,1)S(1)}) fusion(pred[]{:T(512)S(6)} %eq.48, bf16[1,2,128,512]{3,2,1,0:T(8,128)(2,1)} %param.3), kind=kLoop, calls=%fused_computation.109 | loop fusion | flops 131072 | bytes 524289 | tf_op jit(solution)/shard_map/jit(_where)/select_n | solution.py:110
  2.2 0.1 collective-permute-start
  2.3 2.9 %collective-permute-start.6 = (bf16[2,128,512]{2,1,0:T(8,128)(2,1)S(1)}, bf16[2,128,512]{2,1,0:T(8,128)(2,1)S(1)}, u32[]{:S(2)}, u32[]{:S(2)}) collective-permute-start(bf16[2,128,512]{2,1,0:T(8,128)(2,1)S(1)} %bitcast.127), channel_id=1, source_target_pairs={{0,1},{1,0},{2,3},{3,2},{4,5},{5,4},{6,7},{7,6},{8,9},{9,8},{10,11... | collective-permute-start | bytes 786440 | tf_op jit(solution)/shard_map/ppermute | solution.py:139
  5.5 6.9 %collective-permute-done.6 = bf16[2,128,512]{2,1,0:T(8,128)(2,1)S(1)} collective-permute-done((bf16[2,128,512]{2,1,0:T(8,128)(2,1)S(1)}, bf16[2,128,512]{2,1,0:T(8,128)(2,1)S(1)}, u32[]{:S(2)}, u32[]{:S(2)}) %collective-permute-start.6) | collective-permute-done | bytes 262176 | tf_op jit(solution)/shard_map/ppermute | solution.py:139
  12.5 0.5 fusion.70
  13.1 0.9 %copy-done = bf16[1,512,512]{2,1,0:T(8,128)(2,1)S(1)} copy-done((bf16[1,512,512]{2,1,0:T(8,128)(2,1)S(1)}, bf16[1,512,512]{2,1,0:T(8,128)(2,1)}, u32[]{:S(2)}) %copy-start) | copy-done | bytes 524312
  14.2 0.3 add_multiply_fusion.1
  14.5 0.3 fusion
  14.8 0.3 add_multiply_fusion
  15.1 0.3 fusion.1
  15.4 1.3 %collective-permute-start.2 = (bf16[128,512]{1,0:T(8,128)(2,1)S(1)}, bf16[128,512]{1,0:T(8,128)(2,1)S(1)}, u32[]{:S(2)}, u32[]{:S(2)}) collective-permute-start(bf16[128,512]{1,0:T(8,128)(2,1)S(1)} %fusion.1), channel_id=1, source_target_pairs={{16,0},{17,1},{18,2},{19,3},{20,4},{21,5},{22,6},{23,7},{24,8},{25... | collective-permute-start | bytes 393224 | tf_op jit(solution)/shard_map/ppermute | solution.py:145
  16.7 1.3 %collective-permute-start.4 = (bf16[128,512]{1,0:T(8,128)(2,1)S(1)}, bf16[128,512]{1,0:T(8,128)(2,1)S(1)}, u32[]{:S(2)}, u32[]{:S(2)}) collective-permute-start(bf16[128,512]{1,0:T(8,128)(2,1)S(1)} %fusion.1), channel_id=1, source_target_pairs={{16,1},{17,0},{18,3},{19,2},{20,5},{21,4},{22,7},{23,6},{24,9},{25... | collective-permute-start | bytes 393224 | tf_op jit(solution)/shard_map/ppermute | solution.py:146
  18.0 0.2 fusion.49
  18.2 4.9 %collective-permute-done.2 = bf16[128,512]{1,0:T(8,128)(2,1)S(1)} collective-permute-done((bf16[128,512]{1,0:T(8,128)(2,1)S(1)}, bf16[128,512]{1,0:T(8,128)(2,1)S(1)}, u32[]{:S(2)}, u32[]{:S(2)}) %collective-permute-start.2) | collective-permute-done | bytes 131104 | tf_op jit(solution)/shard_map/ppermute | solution.py:145
  23.2 0.3 fusion.2
  23.5 0.4 broadcast_select_fusion.9
  24.0 2.0 %collective-permute-done.4 = bf16[128,512]{1,0:T(8,128)(2,1)S(1)} collective-permute-done((bf16[128,512]{1,0:T(8,128)(2,1)S(1)}, bf16[128,512]{1,0:T(8,128)(2,1)S(1)}, u32[]{:S(2)}, u32[]{:S(2)}) %collective-permute-start.4) | collective-permute-done | bytes 131104 | tf_op jit(solution)/shard_map/ppermute | solution.py:146
  26.0 0.3 fusion.43
  26.3 0.4 broadcast_select_fusion.8
  26.9 0.7 maximum_bitcast_fusion
  27.6 0.7 collective-permute-done.8
  28.3 0.5 fusion.47
  28.8 0.5 fusion.46
  29.5 0.2 copy.29
  29.7 4.2 %collective-permute-start.12 = (bf16[64,384]{1,0:T(8,128)(2,1)S(1)}, bf16[64,384]{1,0:T(8,128)(2,1)S(1)}, u32[]{:S(2)}, u32[]{:S(2)}) collective-permute-start(bf16[64,384]{1,0:T(8,128)(2,1)S(1)} %get-tuple-element.50), channel_id=1, source_target_pairs={{0,4},{2,6},{4,0},{6,2},{1,5},{3,7},{5,1},{7,3},{8,12},{10,14},{12... | collective-permute-start | bytes 147464 | tf_op jit(solution)/shard_map/ppermute | solution.py:77
  33.9 1.6 %collective-permute-start.13 = (bf16[64,384]{1,0:T(8,128)(2,1)S(1)}, bf16[64,384]{1,0:T(8,128)(2,1)S(1)}, u32[]{:S(2)}, u32[]{:S(2)}) collective-permute-start(bf16[64,384]{1,0:T(8,128)(2,1)S(1)} %get-tuple-element.52), channel_id=1, source_target_pairs={{0,2},{2,4},{4,6},{6,0},{1,3},{3,5},{5,7},{7,1},{8,10},{10,12},{12... | collective-permute-start | bytes 147464 | tf_op jit(solution)/shard_map/ppermute | solution.py:77
  35.4 2.3 %collective-permute-start.14 = (bf16[64,384]{1,0:T(8,128)(2,1)S(1)}, bf16[64,384]{1,0:T(8,128)(2,1)S(1)}, u32[]{:S(2)}, u32[]{:S(2)}) collective-permute-start(bf16[64,384]{1,0:T(8,128)(2,1)S(1)} %get-tuple-element.51), channel_id=1, source_target_pairs={{0,6},{2,0},{4,2},{6,4},{1,7},{3,1},{5,3},{7,5},{8,14},{10,8},{12,... | collective-permute-start | bytes 147464 | tf_op jit(solution)/shard_map/ppermute | solution.py:77
  37.7 0.2 copy.27
  38.0 2.0 %collective-permute-done.13 = bf16[64,384]{1,0:T(8,128)(2,1)S(1)} collective-permute-done((bf16[64,384]{1,0:T(8,128)(2,1)S(1)}, bf16[64,384]{1,0:T(8,128)(2,1)S(1)}, u32[]{:S(2)}, u32[]{:S(2)}) %collective-permute-start.13) | collective-permute-done | bytes 49184 | tf_op jit(solution)/shard_map/ppermute | solution.py:77
  40.1 1.0 %collective-permute-start.15 = (bf16[64,384]{1,0:T(8,128)(2,1)S(1)}, bf16[64,384]{1,0:T(8,128)(2,1)S(1)}, u32[]{:S(2)}, u32[]{:S(2)}) collective-permute-start(bf16[64,384]{1,0:T(8,128)(2,1)S(1)} %get-tuple-element.5), channel_id=1, source_target_pairs={{0,4},{2,6},{4,0},{6,2},{1,5},{3,7},{5,1},{7,3},{8,12},{10,14},{12... | collective-permute-start | bytes 147464 | tf_op jit(solution)/shard_map/ppermute | solution.py:88
  41.2 3.2 %collective-permute-start.10 = (bf16[64,896]{1,0:T(8,128)(2,1)S(1)}, bf16[64,896]{1,0:T(8,128)(2,1)S(1)}, u32[]{:S(2)}, u32[]{:S(2)}) collective-permute-start(bf16[64,896]{1,0:T(8,128)(2,1)S(1)} %get-tuple-element.25), channel_id=1, source_target_pairs={{0,2},{2,4},{4,6},{6,0},{1,3},{3,5},{5,7},{7,1},{8,10},{10,12},{12... | collective-permute-start | bytes 344072 | tf_op jit(solution)/shard_map/ppermute | solution.py:77
  44.4 0.7 collective-permute-start.11
  45.1 0.8 collective-permute-start.9
  45.9 0.5 collective-permute-start.16
  46.4 1.5 %collective-permute-done.15 = bf16[64,384]{1,0:T(8,128)(2,1)S(1)} collective-permute-done((bf16[64,384]{1,0:T(8,128)(2,1)S(1)}, bf16[64,384]{1,0:T(8,128)(2,1)S(1)}, u32[]{:S(2)}, u32[]{:S(2)}) %collective-permute-start.15) | collective-permute-done | bytes 49184 | tf_op jit(solution)/shard_map/ppermute | solution.py:88
  47.9 2.9 %collective-permute-start.17 = (bf16[64,384]{1,0:T(8,128)(2,1)S(1)}, bf16[64,384]{1,0:T(8,128)(2,1)S(1)}, u32[]{:S(2)}, u32[]{:S(2)}) collective-permute-start(bf16[64,384]{1,0:T(8,128)(2,1)S(1)} %get-tuple-element.5), channel_id=1, source_target_pairs={{0,6},{2,0},{4,2},{6,4},{1,7},{3,1},{5,3},{7,5},{8,14},{10,8},{12,... | collective-permute-start | bytes 147464 | tf_op jit(solution)/shard_map/ppermute | solution.py:88
  50.8 4.0 %collective-permute-done.16 = bf16[64,384]{1,0:T(8,128)(2,1)S(1)} collective-permute-done((bf16[64,384]{1,0:T(8,128)(2,1)S(1)}, bf16[64,384]{1,0:T(8,128)(2,1)S(1)}, u32[]{:S(2)}, u32[]{:S(2)}) %collective-permute-start.16) | collective-permute-done | bytes 49184 | tf_op jit(solution)/shard_map/ppermute | solution.py:88
  54.9 1.5 %collective-permute-start.18 = (bf16[256,384]{1,0:T(8,128)(2,1)S(1)}, bf16[256,384]{1,0:T(8,128)(2,1)S(1)}, u32[]{:S(2)}, u32[]{:S(2)}) collective-permute-start(bf16[256,384]{1,0:T(8,128)(2,1)S(1)} %bitcast.108), channel_id=1, source_target_pairs={{0,1},{1,0},{2,3},{3,2},{4,5},{5,4},{6,7},{7,6},{8,9},{9,8},{10,11... | collective-permute-start | bytes 589832 | tf_op jit(solution)/shard_map/ppermute | solution.py:155
  56.4 0.5 collective-permute-done.9
  57.1 3.4 %collective-permute-start.23 = (bf16[64,384]{1,0:T(8,128)(2,1)S(1)}, bf16[64,384]{1,0:T(8,128)(2,1)S(1)}, u32[]{:S(2)}, u32[]{:S(2)}) collective-permute-start(bf16[64,384]{1,0:T(8,128)(2,1)S(1)} %get-tuple-element.9), channel_id=1, source_target_pairs={{0,4},{2,6},{4,0},{6,2},{1,5},{3,7},{5,1},{7,3},{8,12},{10,14},{12... | collective-permute-start | bytes 147464 | tf_op jit(solution)/shard_map/ppermute | solution.py:88
  60.8 3.8 %collective-permute-start.25 = (bf16[64,384]{1,0:T(8,128)(2,1)S(1)}, bf16[64,384]{1,0:T(8,128)(2,1)S(1)}, u32[]{:S(2)}, u32[]{:S(2)}) collective-permute-start(bf16[64,384]{1,0:T(8,128)(2,1)S(1)} %get-tuple-element.9), channel_id=1, source_target_pairs={{0,6},{2,0},{4,2},{6,4},{1,7},{3,1},{5,3},{7,5},{8,14},{10,8},{12,... | collective-permute-start | bytes 147464 | tf_op jit(solution)/shard_map/ppermute | solution.py:88
  64.6 2.0 %collective-permute-done.24 = bf16[64,384]{1,0:T(8,128)(2,1)S(1)} collective-permute-done((bf16[64,384]{1,0:T(8,128)(2,1)S(1)}, bf16[64,384]{1,0:T(8,128)(2,1)S(1)}, u32[]{:S(2)}, u32[]{:S(2)}) %collective-permute-start.24) | collective-permute-done | bytes 49184 | tf_op jit(solution)/shard_map/ppermute | solution.py:88
  66.7 0.6 collective-permute-start.26
  67.8 0.2 maximum_select_fusion
  68.1 0.9 %multiply_reduce_fusion.1 = (f32[]{:T(128)}, f32[512,512]{1,0:T(8,128)S(1)}) fusion(f32[512,512]{1,0:T(8,128)S(1)} %maximum_select_fusion, f32[512,256]{1,0:T(8,128)S(1)} %get-tuple-element.18, f32[512,256]{1,0:T(8,128)S(1)} %get-tuple-element.17, pred[]{:T(512)S(6)} %eq.50), kind=kLoop, calls=%fused_computation.37 | loop fusion | flops 2097151 | bytes 3145733 | tf_op jit(solution)/shard_map/reduce_sum | solution.py:28
  69.7 1.0 %convolution_subtract_fusion.1 = f32[512,512]{1,0:T(8,128)S(1)} fusion(f32[512,512]{1,0:T(8,128)S(1)} %get-tuple-element.3, f32[]{:T(128)S(6)} %rsqrt.6), kind=kOutput, calls=%fused_computation.13 | convolution fusion | flops 806354944 | bytes 2097156 | tf_op jit(solution)/shard_map/dot_general | solution.py:23
  70.7 1.0 %convolution_add_fusion.1 = f32[512,512]{1,0:T(8,128)S(1)} fusion(f32[512,512]{1,0:T(8,128)S(1)} %convolution_subtract_fusion.1), kind=kOutput, calls=%fused_computation.12 | convolution fusion | flops 806617088 | bytes 2097152 | tf_op jit(solution)/shard_map/dot_general | solution.py:23
  71.8 1.0 %fusion.9 = f32[512,512]{1,0:T(8,128)S(1)} fusion(f32[512,512]{1,0:T(8,128)S(1)} %convolution_add_fusion.1, f32[512,512]{1,0:T(8,128)S(1)} %convolution_subtract_fusion.1), kind=kOutput, calls=%fused_computation.29 | convolution fusion | flops 806092800 | bytes 3145728 | tf_op jit(solution)/shard_map/dot_general | solution.py:23
  72.8 1.0 %convolution_multiply_fusion.1 = f32[512,512]{1,0:T(8,128)S(1)} fusion(f32[512,512]{1,0:T(8,128)S(1)} %fusion.9, f32[512,512]{1,0:T(8,128)S(1)} %get-tuple-element.3, f32[]{:T(128)S(6)} %rsqrt.6), kind=kOutput, calls=%fused_computation.11 | convolution fusion | flops 806617088 | bytes 3145732 | tf_op jit(solution)/shard_map/dot_general | solution.py:23
  73.9 0.4 bitcast_dynamic-update-slice_fusion.3
  74.3 1.1 %collective-permute-start.19 = (bf16[64,512]{1,0:T(8,128)(2,1)S(1)}, bf16[64,512]{1,0:T(8,128)(2,1)S(1)}, u32[]{:S(2)}, u32[]{:S(2)}) collective-permute-start(bf16[64,512]{1,0:T(8,128)(2,1)S(1)} %get-tuple-element.67), channel_id=1, source_target_pairs={{0,4},{2,6},{4,0},{6,2},{1,5},{3,7},{5,1},{7,3},{8,12},{10,14},{12... | collective-permute-start | bytes 196616 | tf_op jit(solution)/shard_map/ppermute | solution.py:88
  75.6 3.4 %collective-permute-start.20 = (bf16[64,512]{1,0:T(8,128)(2,1)S(1)}, bf16[64,512]{1,0:T(8,128)(2,1)S(1)}, u32[]{:S(2)}, u32[]{:S(2)}) collective-permute-start(bf16[64,512]{1,0:T(8,128)(2,1)S(1)} %get-tuple-element.67), channel_id=1, source_target_pairs={{0,2},{2,4},{4,6},{6,0},{1,3},{3,5},{5,7},{7,1},{8,10},{10,12},{12... | collective-permute-start | bytes 196616 | tf_op jit(solution)/shard_map/ppermute | solution.py:88
  79.0 0.5 collective-permute-start.21
  79.5 2.2 %collective-permute-done.20 = bf16[64,512]{1,0:T(8,128)(2,1)S(1)} collective-permute-done((bf16[64,512]{1,0:T(8,128)(2,1)S(1)}, bf16[64,512]{1,0:T(8,128)(2,1)S(1)}, u32[]{:S(2)}, u32[]{:S(2)}) %collective-permute-start.20) | collective-permute-done | bytes 65568 | tf_op jit(solution)/shard_map/ppermute | solution.py:88
  81.8 1.5 %collective-permute-done.21 = bf16[64,512]{1,0:T(8,128)(2,1)S(1)} collective-permute-done((bf16[64,512]{1,0:T(8,128)(2,1)S(1)}, bf16[64,512]{1,0:T(8,128)(2,1)S(1)}, u32[]{:S(2)}, u32[]{:S(2)}) %collective-permute-start.21) | collective-permute-done | bytes 65568 | tf_op jit(solution)/shard_map/ppermute | solution.py:88
  83.3 1.6 %collective-permute-start.22 = (bf16[256,512]{1,0:T(8,128)(2,1)S(1)}, bf16[256,512]{1,0:T(8,128)(2,1)S(1)}, u32[]{:S(2)}, u32[]{:S(2)}) collective-permute-start(bf16[256,512]{1,0:T(8,128)(2,1)S(1)} %bitcast.112), channel_id=1, source_target_pairs={{0,1},{1,0},{2,3},{3,2},{4,5},{5,4},{6,7},{7,6},{8,9},{9,8},{10,11... | collective-permute-start | bytes 786440 | tf_op jit(solution)/shard_map/ppermute | solution.py:175
  85.1 0.9 multiply_reduce_fusion
  86.7 1.1 %convolution_subtract_fusion = f32[512,512]{1,0:T(8,128)S(1)} fusion(bf16[512,512]{1,0:T(8,128)(2,1)S(1)} %get-tuple-element.7, f32[]{:T(128)S(6)} %rsqrt.7), kind=kOutput, calls=%fused_computation.10 | convolution fusion | flops 808976384 | bytes 1572868 | tf_op jit(solution)/shard_map/dot_general | solution.py:23
  87.8 1.0 %convolution_add_fusion = f32[512,512]{1,0:T(8,128)S(1)} fusion(f32[512,512]{1,0:T(8,128)S(1)} %convolution_subtract_fusion), kind=kOutput, calls=%fused_computation.9 | convolution fusion | flops 806617088 | bytes 2097152 | tf_op jit(solution)/shard_map/dot_general | solution.py:23
  88.8 1.0 %fusion.10 = f32[512,512]{1,0:T(8,128)S(1)} fusion(f32[512,512]{1,0:T(8,128)S(1)} %convolution_add_fusion, f32[512,512]{1,0:T(8,128)S(1)} %convolution_subtract_fusion), kind=kOutput, calls=%fused_computation.30 | convolution fusion | flops 806092800 | bytes 3145728 | tf_op jit(solution)/shard_map/dot_general | solution.py:23
  89.9 1.0 %convolution_multiply_fusion = f32[512,512]{1,0:T(8,128)S(1)} fusion(f32[512,512]{1,0:T(8,128)S(1)} %fusion.10, bf16[512,512]{1,0:T(8,128)(2,1)S(1)} %get-tuple-element.7, f32[]{:T(128)S(6)} %rsqrt.7), kind=kOutput, calls=%fused_computation.8 | convolution fusion | flops 807665664 | bytes 2621444 | tf_op jit(solution)/shard_map/dot_general | solution.py:23
  90.9 0.8 fusion.18
  91.8 1.1 %fusion.12 = f32[1,512,512]{2,1,0:T(8,128)} fusion(f32[512,512]{1,0:T(8,128)S(1)} %fusion.18, f32[512,256]{1,0:T(8,128)S(1)} %get-tuple-element.16, f32[512,256]{1,0:T(8,128)S(1)} %get-tuple-element.15, pred[]{:T(512)S(6)} %eq.50), kind=kLoop, calls=%fused_computation.35 | loop fusion | flops 524288 | bytes 3145729 | tf_op jit(solution)/shard_map/broadcast_in_dim | solution.py:179
  (78 shorter events, 2.7 us)
Async XLA Ops:
  0.6 12.5 %collective-permute-start.1 = (bf16[512,512]{1,0:T(8,128)(2,1)}, bf16[512,512]{1,0:T(8,128)(2,1)S(1)}, u32[]{:S(2)}, u32[]{:S(2)}) collective-permute-start(bf16[512,512]{1,0:T(8,128)(2,1)} %bitcast.120), channel_id=1, source_target_pairs={{0,8},{8,0},{1,9},{9,1},{2,10},{10,2},{3,11},{11,3},{4,12},{12,4},... | collective-permute-start | bytes 1572872 | tf_op jit(solution)/shard_map/ppermute | solution.py:112
  1.1 1.2 %copy-start.1 = (bf16[1,2,128,512]{3,2,1,0:T(8,128)(2,1)S(1)}, bf16[1,2,128,512]{3,2,1,0:T(8,128)(2,1)}, u32[]{:S(2)}) copy-start(bf16[1,2,128,512]{3,2,1,0:T(8,128)(2,1)} %param.3) | copy-start | bytes 786436
  1.1 4.1 %copy-start.2 = (bf16[2,128,512]{2,1,0:T(8,128)(2,1)S(1)}, bf16[2,128,512]{2,1,0:T(8,128)(2,1)}, u32[]{:S(2)}) copy-start(bf16[2,128,512]{2,1,0:T(8,128)(2,1)} %param.5) | copy-start | bytes 786436
  2.2 11.9 %collective-permute-start = (bf16[128,512]{1,0:T(8,128)(2,1)S(1)}, bf16[128,512]{1,0:T(8,128)(2,1)S(1)}, u32[]{:S(2)}, u32[]{:S(2)}) collective-permute-start(bf16[128,512]{1,0:T(8,128)(2,1)S(1)} %get-tuple-element.38), channel_id=1, source_target_pairs={{0,8},{8,0},{1,9},{9,1},{2,10},{10,2},{3,11},{11,3},{4,12},{12,4},... | collective-permute-start | bytes 393224 | tf_op jit(solution)/shard_map/ppermute | solution.py:113
  2.3 10.0 %collective-permute-start.6 = (bf16[2,128,512]{2,1,0:T(8,128)(2,1)S(1)}, bf16[2,128,512]{2,1,0:T(8,128)(2,1)S(1)}, u32[]{:S(2)}, u32[]{:S(2)}) collective-permute-start(bf16[2,128,512]{2,1,0:T(8,128)(2,1)S(1)} %bitcast.127), channel_id=1, source_target_pairs={{0,1},{1,0},{2,3},{3,2},{4,5},{5,4},{6,7},{7,6},{8,9},{9,8},{10,11... | collective-permute-start | bytes 786440 | tf_op jit(solution)/shard_map/ppermute | solution.py:139
  5.3 18.7 %collective-permute-start.5 = (bf16[128,512]{1,0:T(8,128)(2,1)S(1)}, bf16[128,512]{1,0:T(8,128)(2,1)S(1)}, u32[]{:S(2)}, u32[]{:S(2)}) collective-permute-start(bf16[128,512]{1,0:T(8,128)(2,1)S(1)} %select_bitcast_fusion.6), channel_id=1, source_target_pairs={{0,1},{1,0},{2,3},{3,2},{4,5},{5,4},{6,7},{7,6},{8,9},{9,8},{10,11... | collective-permute-start | bytes 393224 | tf_op jit(solution)/shard_map/ppermute | solution.py:138
  12.4 5.6 %collective-permute-start.7 = (bf16[128,512]{1,0:T(8,128)(2,1)S(1)}, bf16[128,512]{1,0:T(8,128)(2,1)S(1)}, u32[]{:S(2)}, u32[]{:S(2)}) collective-permute-start(bf16[128,512]{1,0:T(8,128)(2,1)S(1)} %get-tuple-element.36), channel_id=1, source_target_pairs={{0,8},{8,0},{1,9},{9,1},{2,10},{10,2},{3,11},{11,3},{4,12},{12,4},... | collective-permute-start | bytes 393224 | tf_op jit(solution)/shard_map/ppermute | solution.py:140
  13.0 1.0 %copy-start = (bf16[1,512,512]{2,1,0:T(8,128)(2,1)S(1)}, bf16[1,512,512]{2,1,0:T(8,128)(2,1)}, u32[]{:S(2)}) copy-start(bf16[1,512,512]{2,1,0:T(8,128)(2,1)} %param.4) | copy-start | bytes 1572868
  15.4 7.8 %collective-permute-start.2 = (bf16[128,512]{1,0:T(8,128)(2,1)S(1)}, bf16[128,512]{1,0:T(8,128)(2,1)S(1)}, u32[]{:S(2)}, u32[]{:S(2)}) collective-permute-start(bf16[128,512]{1,0:T(8,128)(2,1)S(1)} %fusion.1), channel_id=1, source_target_pairs={{16,0},{17,1},{18,2},{19,3},{20,4},{21,5},{22,6},{23,7},{24,8},{25... | collective-permute-start | bytes 393224 | tf_op jit(solution)/shard_map/ppermute | solution.py:145
  16.7 9.3 %collective-permute-start.4 = (bf16[128,512]{1,0:T(8,128)(2,1)S(1)}, bf16[128,512]{1,0:T(8,128)(2,1)S(1)}, u32[]{:S(2)}, u32[]{:S(2)}) collective-permute-start(bf16[128,512]{1,0:T(8,128)(2,1)S(1)} %fusion.1), channel_id=1, source_target_pairs={{16,1},{17,0},{18,3},{19,2},{20,5},{21,4},{22,7},{23,6},{24,9},{25... | collective-permute-start | bytes 393224 | tf_op jit(solution)/shard_map/ppermute | solution.py:146
  23.9 2.9 %collective-permute-start.3 = (bf16[128,512]{1,0:T(8,128)(2,1)S(1)}, bf16[128,512]{1,0:T(8,128)(2,1)S(1)}, u32[]{:S(2)}, u32[]{:S(2)}) collective-permute-start(bf16[128,512]{1,0:T(8,128)(2,1)S(1)} %get-tuple-element.34), channel_id=1, source_target_pairs={{0,8},{8,0},{1,9},{9,1},{2,10},{10,2},{3,11},{11,3},{4,12},{12,4},... | collective-permute-start | bytes 393224 | tf_op jit(solution)/shard_map/ppermute | solution.py:160
  26.7 1.6 %collective-permute-start.8 = (bf16[256,512]{1,0:T(8,128)(2,1)S(1)}, bf16[256,512]{1,0:T(8,128)(2,1)S(1)}, u32[]{:S(2)}, u32[]{:S(2)}) collective-permute-start(bf16[256,512]{1,0:T(8,128)(2,1)S(1)} %pad_maximum_fusion.3), channel_id=1, source_target_pairs={{0,8},{8,0},{1,9},{9,1},{2,10},{10,2},{3,11},{11,3},{4,12},{12,4},... | collective-permute-start | bytes 786440 | tf_op jit(solution)/shard_map/ppermute | solution.py:165
  29.7 8.3 %collective-permute-start.12 = (bf16[64,384]{1,0:T(8,128)(2,1)S(1)}, bf16[64,384]{1,0:T(8,128)(2,1)S(1)}, u32[]{:S(2)}, u32[]{:S(2)}) collective-permute-start(bf16[64,384]{1,0:T(8,128)(2,1)S(1)} %get-tuple-element.50), channel_id=1, source_target_pairs={{0,4},{2,6},{4,0},{6,2},{1,5},{3,7},{5,1},{7,3},{8,12},{10,14},{12... | collective-permute-start | bytes 147464 | tf_op jit(solution)/shard_map/ppermute | solution.py:77
  33.9 6.1 %collective-permute-start.13 = (bf16[64,384]{1,0:T(8,128)(2,1)S(1)}, bf16[64,384]{1,0:T(8,128)(2,1)S(1)}, u32[]{:S(2)}, u32[]{:S(2)}) collective-permute-start(bf16[64,384]{1,0:T(8,128)(2,1)S(1)} %get-tuple-element.52), channel_id=1, source_target_pairs={{0,2},{2,4},{4,6},{6,0},{1,3},{3,5},{5,7},{7,1},{8,10},{10,12},{12... | collective-permute-start | bytes 147464 | tf_op jit(solution)/shard_map/ppermute | solution.py:77
  35.4 4.6 %collective-permute-start.14 = (bf16[64,384]{1,0:T(8,128)(2,1)S(1)}, bf16[64,384]{1,0:T(8,128)(2,1)S(1)}, u32[]{:S(2)}, u32[]{:S(2)}) collective-permute-start(bf16[64,384]{1,0:T(8,128)(2,1)S(1)} %get-tuple-element.51), channel_id=1, source_target_pairs={{0,6},{2,0},{4,2},{6,4},{1,7},{3,1},{5,3},{7,5},{8,14},{10,8},{12,... | collective-permute-start | bytes 147464 | tf_op jit(solution)/shard_map/ppermute | solution.py:77
  40.1 7.8 %collective-permute-start.15 = (bf16[64,384]{1,0:T(8,128)(2,1)S(1)}, bf16[64,384]{1,0:T(8,128)(2,1)S(1)}, u32[]{:S(2)}, u32[]{:S(2)}) collective-permute-start(bf16[64,384]{1,0:T(8,128)(2,1)S(1)} %get-tuple-element.5), channel_id=1, source_target_pairs={{0,4},{2,6},{4,0},{6,2},{1,5},{3,7},{5,1},{7,3},{8,12},{10,14},{12... | collective-permute-start | bytes 147464 | tf_op jit(solution)/shard_map/ppermute | solution.py:88
  41.2 15.3 %collective-permute-start.10 = (bf16[64,896]{1,0:T(8,128)(2,1)S(1)}, bf16[64,896]{1,0:T(8,128)(2,1)S(1)}, u32[]{:S(2)}, u32[]{:S(2)}) collective-permute-start(bf16[64,896]{1,0:T(8,128)(2,1)S(1)} %get-tuple-element.25), channel_id=1, source_target_pairs={{0,2},{2,4},{4,6},{6,0},{1,3},{3,5},{5,7},{7,1},{8,10},{10,12},{12... | collective-permute-start | bytes 344072 | tf_op jit(solution)/shard_map/ppermute | solution.py:77
  44.4 12.1 %collective-permute-start.11 = (bf16[64,896]{1,0:T(8,128)(2,1)S(1)}, bf16[64,896]{1,0:T(8,128)(2,1)S(1)}, u32[]{:S(2)}, u32[]{:S(2)}) collective-permute-start(bf16[64,896]{1,0:T(8,128)(2,1)S(1)} %get-tuple-element.24), channel_id=1, source_target_pairs={{0,6},{2,0},{4,2},{6,4},{1,7},{3,1},{5,3},{7,5},{8,14},{10,8},{12,... | collective-permute-start | bytes 344072 | tf_op jit(solution)/shard_map/ppermute | solution.py:77
  45.1 11.9 %collective-permute-start.9 = (bf16[64,896]{1,0:T(8,128)(2,1)S(1)}, bf16[64,896]{1,0:T(8,128)(2,1)S(1)}, u32[]{:S(2)}, u32[]{:S(2)}) collective-permute-start(bf16[64,896]{1,0:T(8,128)(2,1)S(1)} %get-tuple-element.23), channel_id=1, source_target_pairs={{0,4},{2,6},{4,0},{6,2},{1,5},{3,7},{5,1},{7,3},{8,12},{10,14},{12... | collective-permute-start | bytes 344072 | tf_op jit(solution)/shard_map/ppermute | solution.py:77
  45.9 8.9 %collective-permute-start.16 = (bf16[64,384]{1,0:T(8,128)(2,1)S(1)}, bf16[64,384]{1,0:T(8,128)(2,1)S(1)}, u32[]{:S(2)}, u32[]{:S(2)}) collective-permute-start(bf16[64,384]{1,0:T(8,128)(2,1)S(1)} %get-tuple-element.5), channel_id=1, source_target_pairs={{0,2},{2,4},{4,6},{6,0},{1,3},{3,5},{5,7},{7,1},{8,10},{10,12},{12... | collective-permute-start | bytes 147464 | tf_op jit(solution)/shard_map/ppermute | solution.py:88
  47.9 6.9 %collective-permute-start.17 = (bf16[64,384]{1,0:T(8,128)(2,1)S(1)}, bf16[64,384]{1,0:T(8,128)(2,1)S(1)}, u32[]{:S(2)}, u32[]{:S(2)}) collective-permute-start(bf16[64,384]{1,0:T(8,128)(2,1)S(1)} %get-tuple-element.5), channel_id=1, source_target_pairs={{0,6},{2,0},{4,2},{6,4},{1,7},{3,1},{5,3},{7,5},{8,14},{10,8},{12,... | collective-permute-start | bytes 147464 | tf_op jit(solution)/shard_map/ppermute | solution.py:88
  54.9 12.4 %collective-permute-start.18 = (bf16[256,384]{1,0:T(8,128)(2,1)S(1)}, bf16[256,384]{1,0:T(8,128)(2,1)S(1)}, u32[]{:S(2)}, u32[]{:S(2)}) collective-permute-start(bf16[256,384]{1,0:T(8,128)(2,1)S(1)} %bitcast.108), channel_id=1, source_target_pairs={{0,1},{1,0},{2,3},{3,2},{4,5},{5,4},{6,7},{7,6},{8,9},{9,8},{10,11... | collective-permute-start | bytes 589832 | tf_op jit(solution)/shard_map/ppermute | solution.py:155
  57.1 7.5 %collective-permute-start.23 = (bf16[64,384]{1,0:T(8,128)(2,1)S(1)}, bf16[64,384]{1,0:T(8,128)(2,1)S(1)}, u32[]{:S(2)}, u32[]{:S(2)}) collective-permute-start(bf16[64,384]{1,0:T(8,128)(2,1)S(1)} %get-tuple-element.9), channel_id=1, source_target_pairs={{0,4},{2,6},{4,0},{6,2},{1,5},{3,7},{5,1},{7,3},{8,12},{10,14},{12... | collective-permute-start | bytes 147464 | tf_op jit(solution)/shard_map/ppermute | solution.py:88
  60.7 5.9 %collective-permute-start.24 = (bf16[64,384]{1,0:T(8,128)(2,1)S(1)}, bf16[64,384]{1,0:T(8,128)(2,1)S(1)}, u32[]{:S(2)}, u32[]{:S(2)}) collective-permute-start(bf16[64,384]{1,0:T(8,128)(2,1)S(1)} %get-tuple-element.9), channel_id=1, source_target_pairs={{0,2},{2,4},{4,6},{6,0},{1,3},{3,5},{5,7},{7,1},{8,10},{10,12},{12... | collective-permute-start | bytes 147464 | tf_op jit(solution)/shard_map/ppermute | solution.py:88
  60.8 5.9 %collective-permute-start.25 = (bf16[64,384]{1,0:T(8,128)(2,1)S(1)}, bf16[64,384]{1,0:T(8,128)(2,1)S(1)}, u32[]{:S(2)}, u32[]{:S(2)}) collective-permute-start(bf16[64,384]{1,0:T(8,128)(2,1)S(1)} %get-tuple-element.9), channel_id=1, source_target_pairs={{0,6},{2,0},{4,2},{6,4},{1,7},{3,1},{5,3},{7,5},{8,14},{10,8},{12,... | collective-permute-start | bytes 147464 | tf_op jit(solution)/shard_map/ppermute | solution.py:88
  66.7 18.1 %collective-permute-start.26 = (bf16[256,384]{1,0:T(8,128)(2,1)S(1)}, bf16[256,384]{1,0:T(8,128)(2,1)S(1)}, u32[]{:S(2)}, u32[]{:S(2)}) collective-permute-start(bf16[256,384]{1,0:T(8,128)(2,1)S(1)} %bitcast.110), channel_id=1, source_target_pairs={{0,1},{1,0},{2,3},{3,2},{4,5},{5,4},{6,7},{7,6},{8,9},{9,8},{10,11... | collective-permute-start | bytes 589832 | tf_op jit(solution)/shard_map/ppermute | solution.py:173
  74.3 5.2 %collective-permute-start.19 = (bf16[64,512]{1,0:T(8,128)(2,1)S(1)}, bf16[64,512]{1,0:T(8,128)(2,1)S(1)}, u32[]{:S(2)}, u32[]{:S(2)}) collective-permute-start(bf16[64,512]{1,0:T(8,128)(2,1)S(1)} %get-tuple-element.67), channel_id=1, source_target_pairs={{0,4},{2,6},{4,0},{6,2},{1,5},{3,7},{5,1},{7,3},{8,12},{10,14},{12... | collective-permute-start | bytes 196616 | tf_op jit(solution)/shard_map/ppermute | solution.py:88
  75.6 6.1 %collective-permute-start.20 = (bf16[64,512]{1,0:T(8,128)(2,1)S(1)}, bf16[64,512]{1,0:T(8,128)(2,1)S(1)}, u32[]{:S(2)}, u32[]{:S(2)}) collective-permute-start(bf16[64,512]{1,0:T(8,128)(2,1)S(1)} %get-tuple-element.67), channel_id=1, source_target_pairs={{0,2},{2,4},{4,6},{6,0},{1,3},{3,5},{5,7},{7,1},{8,10},{10,12},{12... | collective-permute-start | bytes 196616 | tf_op jit(solution)/shard_map/ppermute | solution.py:88
  79.0 4.3 %collective-permute-start.21 = (bf16[64,512]{1,0:T(8,128)(2,1)S(1)}, bf16[64,512]{1,0:T(8,128)(2,1)S(1)}, u32[]{:S(2)}, u32[]{:S(2)}) collective-permute-start(bf16[64,512]{1,0:T(8,128)(2,1)S(1)} %get-tuple-element.67), channel_id=1, source_target_pairs={{0,6},{2,0},{4,2},{6,4},{1,7},{3,1},{5,3},{7,5},{8,14},{10,8},{12,... | collective-permute-start | bytes 196616 | tf_op jit(solution)/shard_map/ppermute | solution.py:88
  83.3 7.6 %collective-permute-start.22 = (bf16[256,512]{1,0:T(8,128)(2,1)S(1)}, bf16[256,512]{1,0:T(8,128)(2,1)S(1)}, u32[]{:S(2)}, u32[]{:S(2)}) collective-permute-start(bf16[256,512]{1,0:T(8,128)(2,1)S(1)} %bitcast.112), channel_id=1, source_target_pairs={{0,1},{1,0},{2,3},{3,2},{4,5},{5,4},{6,7},{7,6},{8,9},{9,8},{10,11... | collective-permute-start | bytes 786440 | tf_op jit(solution)/shard_map/ppermute | solution.py:175

commit v4 on v1

v4 whole, which is shorter than its diff:
```python
import functools

import jax
import jax.numpy as jnp
import numpy as np
from jax import lax
from jax.experimental import pallas as pl
from jax.experimental.pallas import tpu as pltpu
from jax.sharding import Mesh, PartitionSpec as P

BF16 = jnp.bfloat16
F32 = jnp.float32
SWAP = [(0, 1), (1, 0)]
SMEM = pl.BlockSpec(memory_space=pltpu.SMEM)
VMEM = pl.BlockSpec(memory_space=pltpu.VMEM)
ANY = pl.BlockSpec(memory_space=pl.ANY)


def silu_slope(pre):
    sig = jax.nn.sigmoid(pre)
    return sig * (1.0 + pre * (1.0 - sig))


def slope_of(inputs, matrix):
    return silu_slope(jnp.dot(inputs, matrix, preferred_element_type=F32))


def layer(upstream, slope, matrix):
    dh = (upstream.astype(F32) * slope).astype(BF16)
    back = lax.dot_general(dh, matrix, (((1,), (1,)), ((), ())), preferred_element_type=F32)
    return dh, (upstream.astype(F32) + back).astype(BF16)


def by_core(core, run, own, partner):
    @pl.when(core == 1)
    def _():
        run(own, partner)

    @pl.when(core == 0)
    def _():
        run(partner, own)


def first_kernel(where, own, partner, local, partner_x, cot_last, slope_odd, slope_even, down, cross):
    core = where[2]
    upstream = cot_last[core]

    def run(odd, even):
        slope_odd[...] = slope_of(odd[1], odd[0][...])
        slope_even[...] = slope_of(even[1], even[0][...])
        cot = layer(upstream, slope_odd[...], odd[0][...])[1]
        down[...] = layer(cot, slope_even[...], even[0][...])[1]

    by_core(core, run, (own, local[core]), (partner, partner_x[...]))
    cross[...] = jnp.where(where[3] == 0, upstream, down[...])


def far_kernel(where, own, partner, far, partner_far, slope_odd, slope_even):
    core = where[2]

    def run(odd, even):
        slope_odd[...] = slope_of(odd[1], odd[0][...])
        slope_even[...] = slope_of(even[1], even[0][...])

    by_core(core, run, (own, far[core]), (partner, partner_far[...]))


def layers_kernel(
    where, own, partner, near_odd, near_even, far_odd, far_even, near, far, cot_last,
    own_dh, give_dh, own_cot, give_cot, upstream,
):
    rows = near.shape[0]
    top = where[3] == where[4] - 1
    upstream[:rows] = jnp.where(top, cot_last[where[2]], near[...])
    upstream[rows:] = far[...]

    def run(odd, even):
        slope = jnp.concatenate([near_odd[...], far_odd[...]])
        dh, cot = layer(upstream[...], slope, odd[0][...])
        odd[1][...] = dh
        odd[2][...] = cot[:rows]
        slope = jnp.concatenate([near_even[...], far_even[...]])
        dh, cot = layer(cot, slope, even[0][...])
        even[1][...] = dh
        even[2][...] = cot[:rows]

    by_core(where[2], run, (own, own_dh, own_cot), (partner, give_dh, give_cot))


def moment(left, right):
    return lax.dot_general(left, right, (((0,), (0,)), ((), ())), preferred_element_type=F32)


def split(value):
    high = value.astype(BF16)
    return high, (value - high.astype(F32)).astype(BF16)


def product(left, right, dims=((1,), (0,))):
    def dot(a, b):
        return lax.dot_general(a, b, (dims, ((), ())), preferred_element_type=F32)

    total = dot(left[0], right[0])
    if len(right) > 1:
        total += dot(left[0], right[1])
    if len(left) > 1:
        total += dot(left[1], right[0])
    return total


def call(kernel, flops, out_shape, in_specs, scratch=()):
    return pl.pallas_call(
        kernel,
        out_shape=out_shape,
        in_specs=in_specs,
        out_specs=jax.tree.map(lambda _: VMEM, out_shape),
        scratch_shapes=list(scratch),
        cost_estimate=pl.CostEstimate(flops=flops, bytes_accessed=1 << 20, transcendentals=0),
        compiler_params=pltpu.CompilerParams(vmem_limit_bytes=40 << 20),
    )


def packed_moment(tokens, side, place_in):
    half = tokens.shape[1] // 2
    quarter = half // 2
    own = pl.multiple_of(side * half, half)
    other = pl.multiple_of(half - side * half, half)
    mine = tokens[:, pl.ds(own, half)]
    rest = tokens[:, pl.ds(other, half)]
    place_in[:quarter, :half] = moment(mine[:, :quarter], mine).astype(BF16)
    place_in[:quarter, half:3 * quarter] = moment(mine[:, :quarter], rest[:, :quarter]).astype(BF16)
    place_in[quarter:, :quarter] = moment(mine[:, quarter:], mine[:, quarter:]).astype(BF16)
    place_in[quarter:, quarter:3 * quarter] = moment(mine[:, quarter:], rest).astype(BF16)
    return mine


def act_kernel(where, local, far, after, *refs):
    parts, (tokens, whole) = refs[:-2], refs[-2:]
    micro, rows = local.shape[:2]
    for m in range(micro):
        tokens[m * rows:(m + 1) * rows] = local[m]
        tokens[(micro + m) * rows:(micro + m + 1) * rows] = far[m]
    packed_moment(tokens, where[1], whole)
    cut_parts(where[0], whole, parts)


def cut_parts(place, whole, parts):
    rows = parts[0].shape[0]
    for step, part in enumerate(parts):
        start = pl.multiple_of((place ^ step) * rows, rows)
        part[:, :whole.shape[1]] = whole[pl.ds(start, rows)]


def grad_kernel(where, local, far, dh_own, dh_got, act_part, *refs):
    parts, (inputs, tokens, whole) = refs[:-3], refs[-3:]
    rows, width = local.shape[1:]
    core = where[2]
    inputs[:rows] = local[core]
    inputs[rows:2 * rows] = far[core]
    inputs[2 * rows:3 * rows] = local[1 - core]
    inputs[3 * rows:] = far[1 - core]
    tokens[:2 * rows] = dh_own[...]
    tokens[2 * rows:] = dh_got[...]
    cut = 3 * width // 4
    mine = packed_moment(tokens, where[1], whole)
    whole[:, cut:] = moment(mine, inputs[...]).astype(BF16)
    cut_parts(where[0], whole, parts)
    for part in parts:
        part[:, whole.shape[1]:] = act_part[...]


def inverse_kernel(unroll, count, where, mine, other, result, ours, theirs, matrix):
    line, rows = mine.shape[:2]
    for step in range(line):
        start = pl.multiple_of((where[0] ^ step) * rows, rows)
        ours[pl.ds(start, rows)] = mine[step].astype(F32)
        theirs[pl.ds(start, rows)] = other[step].astype(F32)
    q = ours.shape[0] // 2
    matrix[:q, :3 * q] = ours[:q]
    matrix[:q, 3 * q:] = theirs[q:, q:2 * q].T
    matrix[q:2 * q, :q] = ours[:q, q:2 * q].T
    matrix[q:2 * q, q:] = ours[q:]
    matrix[2 * q:3 * q, :q] = theirs[:q, 2 * q:]
    matrix[2 * q:3 * q, q:2 * q] = ours[q:, q:2 * q].T
    matrix[2 * q:3 * q, 2 * q:] = theirs[:q, :2 * q]
    matrix[3 * q:, :2 * q] = theirs[q:, q:]
    matrix[3 * q:, 2 * q:3 * q] = theirs[:q, q:2 * q].T
    matrix[3 * q:, 3 * q:] = theirs[q:, :q]
    width = 4 * q
    row = lax.broadcasted_iota(jnp.int32, (width, width), 0)
    column = lax.broadcasted_iota(jnp.int32, (width, width), 1)
    eye = (row == column).astype(F32)
    full = matrix[...] * (1.0 / count) + 0.01 * eye
    scale = lax.rsqrt(jnp.sum(full * full, keepdims=True))
    first = full * scale
    first_terms = split(first)
    second = 2.0 * first - product(first_terms, first_terms)
    second_terms = split(second)
    square = product(second_terms, second_terms)
    last = 2.0 * (eye - second) + square
    tail = 2.0 * last - product(second_terms, split(last))
    inverse = (2.0 * tail - product(first_terms, split(tail))) * scale
    if unroll:
        half = 2 * q
        own = pl.multiple_of(where[1] * half, half)
        away = pl.multiple_of(half - where[1] * half, half)
        for i, a in enumerate((own, away)):
            for j, b in enumerate((own, away)):
                result[pl.ds(a, half), pl.ds(b, half)] = inverse[
                    i * half:(i + 1) * half, j * half:(j + 1) * half
                ]
    else:
        result[...] = inverse


def update_kernel(where, mine, other, act_inv, out_inv, result, rows_of):
    line, rows = mine.shape[:2]
    half = line * rows
    for step in range(line):
        start = pl.multiple_of((where[0] ^ step) * rows, rows)
        rows_of[pl.ds(start, rows)] = mine[step]
        rows_of[pl.ds(half + start, rows)] = other[step]
    left = product((rows_of[...],), split(act_inv[...]))
    update = product(split(left), split(out_inv[...]), ((0,), (0,)))
    own = pl.multiple_of(where[1] * half, half)
    away = pl.multiple_of(half - where[1] * half, half)
    result[:, pl.ds(own, half)] = update[:, :half]
    result[:, pl.ds(away, half)] = update[:, half:]


def send(parts):
    line = len(parts)
    got = {0: parts[0]}
    for step in sorted(range(1, line), key=lambda k: (-(k & (line // 2)), k)):
        got[step] = lax.ppermute(parts[step], "line", [(i, i ^ step) for i in range(line)])
    return [got[step] for step in range(line)]


def body(acts, weights, cot_last):
    pairs = lax.axis_size("row")
    line = lax.axis_size("line")
    row = lax.axis_index("row")
    core = lax.axis_index("core")
    side = lax.axis_index("side")
    weight = weights[0]
    local = acts[0]
    micro, rows, width = local.shape
    count = micro * rows * line * 2
    odd = core == 1
    where = jnp.stack([lax.axis_index("line"), side, core, row, pairs]).astype(jnp.int32)

    def mine_of(pair):
        return jnp.where(odd, pair[1], pair[0])

    def others_of(pair):
        return jnp.where(odd, pair[0], pair[1])

    partner = lax.ppermute(weight, "core", SWAP)
    partner_x = lax.ppermute(others_of(local), "core", SWAP)
    far = lax.ppermute(local, "side", SWAP)
    partner_far = lax.ppermute(partner_x, "side", SWAP)
    block = jax.ShapeDtypeStruct((rows, width), BF16)
    slope = jax.ShapeDtypeStruct((rows, width), F32)
    near_odd, near_even, down, cross = call(
        first_kernel, 8 * rows * width**2, [slope, slope, block, block], [SMEM] + [VMEM] * 5
    )(where, weight, partner, local, partner_x, cot_last)
    first = down
    for turn in range(1, pairs):
        straight = [(r, r - 1) for r in range(1, pairs)]
        diagonal = [(2 * r + s, 2 * ((r - 1) % pairs) + 1 - s) for r in range(pairs) for s in range(2)]
        upstream = lax.ppermute(down, "row", straight)
        crossing = lax.ppermute(cross, ("row", "side"), diagonal)
        here = row == pairs - 1 - turn
        if turn == 1:
            near_up, far_up = upstream, crossing
        else:
            near_up = jnp.where(here, upstream, near_up)
            far_up = jnp.where(here, crossing, far_up)
        if turn < pairs - 1:
            cot = layer(upstream, near_odd, jnp.where(odd, weight, partner))[1]
            down = layer(cot, near_even, jnp.where(odd, partner, weight))[1]
            cross = jnp.where(row == 0, mine_of(cot_last), down)

    tokens = 2 * micro * rows
    half, cut = width // 2, 3 * width // 4
    part = half // line
    act_parts = call(
        act_kernel,
        2 * tokens * half * cut,
        [jax.ShapeDtypeStruct((part, cut), BF16)] * line,
        [SMEM, VMEM, VMEM, ANY],
        [pltpu.VMEM((tokens, width), BF16), pltpu.VMEM((half, cut), BF16)],
    )(where, local, far, first)
    act_part = sum(piece.astype(F32) for piece in send(act_parts)).astype(BF16)

    far_odd, far_even = call(far_kernel, 4 * rows * width**2, [slope, slope], [SMEM] + [VMEM] * 4)(
        where, weight, partner, far, partner_far
    )
    pair = jax.ShapeDtypeStruct((2 * rows, width), BF16)
    own_dh, give_dh, own_cot, give_cot = call(
        layers_kernel,
        8 * rows * width**2,
        [pair, pair, block, block],
        [SMEM] + [VMEM] * 9,
        [pltpu.VMEM((2 * rows, width), BF16)],
    )(where, weight, partner, near_odd, near_even, far_odd, far_even, near_up, far_up, cot_last)
    got_dh = lax.ppermute(give_dh, "core", SWAP)
    other_cot = lax.ppermute(give_cot, "core", SWAP)
    cot = jnp.stack([mine_of((own_cot, other_cot)), mine_of((other_cot, own_cot))])

    parts = call(
        grad_kernel,
        2 * tokens * half * (cut + width),
        [jax.ShapeDtypeStruct((part, 2 * cut + width), BF16)] * line,
        [SMEM] + [VMEM] * 5,
        [pltpu.VMEM((tokens, width), BF16)] * 2 + [pltpu.VMEM((half, cut + width), BF16)],
    )(where, local, far, own_dh, got_dh, act_part)
    got = send(parts)
    act_mine = jnp.stack([piece[:, cut + width:] for piece in got])
    act_other = lax.ppermute(act_mine, "side", SWAP)
    total = sum(piece[:, :cut + width].astype(F32) for piece in got).astype(BF16)
    got = send([total] * line)
    out_mine = jnp.stack([piece[:, :cut] for piece in got])
    grad_mine = jnp.stack([piece[:, cut:] for piece in got])
    out_other = lax.ppermute(out_mine, "side", SWAP)
    grad_other = lax.ppermute(grad_mine, "side", SWAP)

    def inverse(unroll, ours, theirs):
        return call(
            functools.partial(inverse_kernel, unroll, count),
            8 * width**3,
            jax.ShapeDtypeStruct((width, width), F32),
            [SMEM, VMEM, VMEM],
            [pltpu.VMEM((half, cut), F32)] * 2 + [pltpu.VMEM((width, width), F32)],
        )(where, ours, theirs)

    act_inv = inverse(True, act_mine, act_other)
    out_inv = inverse(False, out_mine, out_other)
    update = call(
        update_kernel,
        4 * width**3,
        jax.ShapeDtypeStruct((width, width), F32),
        [SMEM] + [VMEM] * 4,
        [pltpu.VMEM((width, width), BF16)],
    )(where, grad_mine, grad_other, act_inv, out_inv)
    return (cot[None], update[None])


def solution(mesh):
    sections, shards = mesh.devices.shape
    finer = Mesh(
        np.reshape(mesh.devices, (sections // 2, 2, shards // 2, 2)),
        ("row", "core", "line", "side"),
    )
    section, dp = ("row", "core"), ("line", "side")
    placed = (P(section, None, dp, None), P(section, None, None), P(None, dp, None))
    return jax.shard_map(
        body,
        mesh=finer,
        in_specs=placed,
        out_specs=(P(section, None, dp, None), P(section, None, None)),
        check_vma=False,
    )
```

time: 180 us -> 70.9 us (0.39)
  waiting for transfers between devices: 132 us -> 21.5 us
  matrix products: 24.9 us -> 0 us
  starting transfers between devices: 4.95 us -> 25.6 us
  Pallas kernels: 0 us -> 18.6 us
  between operations: 15.7 us -> 0.87 us
  local copies, waits for them, and re-layouts: 0.03 us -> 2.16 us
    psum x1 -> x0, waiting for transfers between devices: 78.4 us -> none  [body(): lax.psum((moment(dh, dh).astype(jnp.bfloat16), moment(flat, dh).astype(jn...]
    all_gather x1 -> x0, waiting for transfers between devices: 42.7 us -> none  [body(): every = lax.all_gather(flat, 'dp', tiled=True)]
    dot_general x19 -> x0, matrix products: 24.9 us -> none  [the longest x10 12.5 us: mul(): return jnp.dot(left, right, precision=lax.Precision.HIGH)]
    ppermute x4 -> x20, starting transfers between devices: 4.69 us -> 25.6 us  [the longest x9 13.7 us: send(): lax.ppermute(parts[step], 'line', [(i, i ^ step) for i in range(line)])]
    pallas_call x0 -> x8, Pallas kernels: none -> 18.6 us  [the longest x2 9.85 us: inverse(): call(functools.partial(inverse_kernel, unroll, count), 8 * width ** 3, ja...]
    ppermute x4 -> x20, waiting for transfers between devices: 10.4 us -> 21.5 us  [the longest x9 19.9 us: send(): lax.ppermute(parts[step], 'line', [(i, i ^ step) for i in range(line)])]
    unnamed x12 -> x10, local copies, waits for them, and re-layouts: 0.03 us -> 2.01 us
    reduce_sum x1 -> x0, other arithmetic: 1.92 us -> none  [inverse(): scale = lax.rsqrt(jnp.sum(matrix * matrix))]
  transfers between devices with their start and end apart: 6 -> 20, of which waited for: 4 -> 7; matrix products, arithmetic and copies ran while one was open for 6% -> 3% of each run, Pallas kernels for 0% -> 20%
where the time goes in v4:
time: 70.9 us; the launch traced here: 70.7 us
  starting transfers between devices  25.6 us (36%)
  waiting for transfers between devices  21.5 us (30%)
  Pallas kernels  18.6 us (26%)
  local copies, waits for them, and re-layouts  2.16 us (3%)
  other arithmetic  1.94 us (3%)
  between operations  0.87 us (1%)
    ppermute x9, waiting for transfers between devices, send(): lax.ppermute(parts[step], 'line', [(i, i ^ step) for i in range(line)])  19.9 us
    ppermute x9, starting transfers between devices, send(): lax.ppermute(parts[step], 'line', [(i, i ^ step) for i in range(line)])  13.7 us
    pallas_call x2, Pallas kernels, inverse(): call(functools.partial(inverse_kernel, unroll, count), 8 * width ** 3, ja...  9.85 us
    pallas_call x1, Pallas kernels, body(): call(update_kernel, 4 * width ** 3, jax.ShapeDtypeStruct((width, width),...  3.23 us
    ppermute x1, starting transfers between devices, body(): crossing = lax.ppermute(cross, ('row', 'side'), diagonal)  2.96 us
    ppermute x1, starting transfers between devices, body(): far = lax.ppermute(local, 'side', SWAP)  2.57 us
    unnamed x10, local copies, waits for them, and re-layouts  2.01 us
    ppermute x1, starting transfers between devices, body(): act_other = lax.ppermute(act_mine, 'side', SWAP)  1.56 us
  transfers between devices with their start and end apart: 20, of which 7 were waited for; matrix products, arithmetic and copies ran while one was open for 3% of the time, Pallas kernels for 20%

profile of v4, /device:TPU:0, one launch (start us, length us, event | category | flops | bytes accessed | tf_op | source)
XLA Modules:
  0.0 70.7 jit_solution(3714482747187102465)
XLA Ops:
  0.6 0.0 copy-start.2
  0.6 0.5 collective-permute-start
  1.2 2.6 %collective-permute-start.2 = (bf16[2,128,512]{2,1,0:T(8,128)(2,1)}, bf16[2,128,512]{2,1,0:T(8,128)(2,1)S(1)}, u32[]{:S(2)}, u32[]{:S(2)}) collective-permute-start(bf16[2,128,512]{2,1,0:T(8,128)(2,1)} %bitcast.43), channel_id=1, source_target_pairs={{0,1},{1,0},{2,3},{3,2},{4,5},{5,4},{6,7},{7,6},{8,9},{9,8},{10,11... | collective-permute-start | bytes 786440 | tf_op jit(solution)/shard_map/ppermute | solution.py:260
  3.7 1.0 %select_bitcast_fusion.2 = bf16[128,512]{1,0:T(8,128)(2,1)S(1)} fusion(bf16[1,2,128,512]{3,2,1,0:T(8,128)(2,1)} %param.3, pred[]{:T(512)S(6)} %eq.3), kind=kLoop, calls=%fused_computation.7 | loop fusion | flops 65536 | bytes 393217 | tf_op jit(solution)/shard_map/jit(_where)/select_n | solution.py:256
  4.7 0.2 collective-permute-start.1
  4.9 0.1 stack.73.where
  5.0 1.1 %collective-permute-done.1.partner_x = bf16[128,512]{1,0:T(8,128)(2,1)S(1)} collective-permute-done((bf16[128,512]{1,0:T(8,128)(2,1)S(1)}, bf16[128,512]{1,0:T(8,128)(2,1)S(1)}, u32[]{:S(2)}, u32[]{:S(2)}) %collective-permute-start.1) | collective-permute-done | bytes 131104 | tf_op jit(solution)/shard_map/ppermute | solution.py:259
  6.1 0.1 collective-permute-start.3
  6.2 0.0 collective-permute-done.partner
  6.2 0.0 copy-done.2
  6.2 0.0 copy-start
  6.2 1.0 %copy-done = bf16[1,512,512]{2,1,0:T(8,128)(2,1)S(1)} copy-done((bf16[1,512,512]{2,1,0:T(8,128)(2,1)S(1)}, bf16[1,512,512]{2,1,0:T(8,128)(2,1)}, u32[]{:S(2)}) %copy-start) | copy-done | bytes 524312
  7.3 0.0 copy-start.3
  7.3 0.9 %copy-done.3 = bf16[2,128,512]{2,1,0:T(8,128)(2,1)S(1)} copy-done((bf16[2,128,512]{2,1,0:T(8,128)(2,1)S(1)}, bf16[2,128,512]{2,1,0:T(8,128)(2,1)}, u32[]{:S(2)}) %copy-start.3) | copy-done | bytes 262168
  8.2 1.3 %shard_map.50 = (f32[128,512]{1,0:T(8,128)S(1)}, f32[128,512]{1,0:T(8,128)S(1)}, bf16[128,512]{1,0:T(8,128)(2,1)S(1)}, bf16[128,512]{1,0:T(8,128)(2,1)S(1)}) custom-call(s32[5]{0:T(128)S(1)} %stack.73.where, bf16[512,512]{1,0:T(8,128)(2,1)S(1)} %bitcast.40, bf16[512,512]{1,0:T(8,128)(2,1)S(1)} %collective-permute-done.partner, ...), custom_call_target="tpu_custom_call" | custom-call | flops 268435456 | bytes 1048576 | tf_op jit(solution)/shard_map/pallas_call | solution.py:264
  9.5 0.0 copy-start.1
  9.5 3.0 %collective-permute-start.5 = (bf16[128,512]{1,0:T(8,128)(2,1)S(1)}, bf16[128,512]{1,0:T(8,128)(2,1)S(1)}, u32[]{:S(2)}, u32[]{:S(2)}) collective-permute-start(bf16[128,512]{1,0:T(8,128)(2,1)S(1)} %get-tuple-element.25), channel_id=1, source_target_pairs={{0,17},{1,16},{16,1},{17,0},{2,19},{3,18},{18,3},{19,2},{4,21},{5,... | collective-permute-start | bytes 393224 | tf_op jit(solution)/shard_map/ppermute | solution.py:272
  12.5 1.3 %collective-permute-start.4 = (bf16[128,512]{1,0:T(8,128)(2,1)S(1)}, bf16[128,512]{1,0:T(8,128)(2,1)S(1)}, u32[]{:S(2)}, u32[]{:S(2)}) collective-permute-start(bf16[128,512]{1,0:T(8,128)(2,1)S(1)} %get-tuple-element.24.after), channel_id=1, source_target_pairs={{16,0},{17,1},{18,2},{19,3},{20,4},{21,5},{22,6},{23,7},{24,8},{25... | collective-permute-start | bytes 393224 | tf_op jit(solution)/shard_map/ppermute | solution.py:271
  13.8 0.0 collective-permute-done.2.far
  13.8 0.9 %shard_map.53 = (bf16[64,384]{1,0:T(8,128)(2,1)S(1)}, bf16[64,384]{1,0:T(8,128)(2,1)S(1)}, bf16[64,384]{1,0:T(8,128)(2,1)S(1)}, bf16[64,384]{1,0:T(8,128)(2,1)S(1)}) custom-call(s32[5]{0:T(128)S(1)} %stack.73.where, bf16[2,128,512]{2,1,0:T(8,128)(2,1)S(1)} %bitcast.45, bf16[2,128,512]{2,1,0:T(8,128)(2,1)S(1)} %collective-permute-done.2.far, ...), custom_call_target="tpu_custom_call" | custom-call | flops 100663296 | bytes 1048576 | tf_op jit(solution)/shard_map/pallas_call | solution.py:287
  14.7 1.6 %collective-permute-start.8 = (bf16[64,384]{1,0:T(8,128)(2,1)S(1)}, bf16[64,384]{1,0:T(8,128)(2,1)S(1)}, u32[]{:S(2)}, u32[]{:S(2)}) collective-permute-start(bf16[64,384]{1,0:T(8,128)(2,1)S(1)} %get-tuple-element.31), channel_id=1, source_target_pairs={{0,2},{2,0},{4,6},{6,4},{1,3},{3,1},{5,7},{7,5},{8,10},{10,8},{12,... | collective-permute-start | bytes 147464 | tf_op jit(solution)/shard_map/ppermute | solution.py:235
  16.3 2.6 %collective-permute-start.9 = (bf16[64,384]{1,0:T(8,128)(2,1)S(1)}, bf16[64,384]{1,0:T(8,128)(2,1)S(1)}, u32[]{:S(2)}, u32[]{:S(2)}) collective-permute-start(bf16[64,384]{1,0:T(8,128)(2,1)S(1)} %get-tuple-element.32), channel_id=1, source_target_pairs={{0,4},{2,6},{4,0},{6,2},{1,5},{3,7},{5,1},{7,3},{8,12},{10,14},{12... | collective-permute-start | bytes 147464 | tf_op jit(solution)/shard_map/ppermute | solution.py:235
  18.9 0.0 collective-permute-done.3.partner_far
  18.9 0.0 copy-start.4
  18.9 0.2 collective-permute-start.10
  19.2 0.0 copy-done.1
  19.2 0.9 %shard_map.51 = (f32[128,512]{1,0:T(8,128)S(1)}, f32[128,512]{1,0:T(8,128)S(1)}) custom-call(s32[5]{0:T(128)S(1)} %stack.73.where, bf16[512,512]{1,0:T(8,128)(2,1)S(1)} %bitcast.41, bf16[512,512]{1,0:T(8,128)(2,1)S(1)} %collective-permute-done.partner, bf16[2,128,512]{2,1,0:T(8,128)(2,1)S(1)} %collective-permute-done.2.far, ...), custom_call_target="tpu_custom_call" | custom-call | flops 134217728 | bytes 1048576 | tf_op jit(solution)/shard_map/pallas_call | solution.py:296
  20.1 0.0 collective-permute-done.5.far
  20.1 0.4 collective-permute-done.4.near
  20.5 0.0 copy-done.4
  20.5 1.3 %shard_map.52 = (bf16[256,512]{1,0:T(8,128)(2,1)S(1)}, bf16[256,512]{1,0:T(8,128)(2,1)S(1)}, bf16[128,512]{1,0:T(8,128)(2,1)S(1)}, bf16[128,512]{1,0:T(8,128)(2,1)S(1)}) custom-call(s32[5]{0:T(128)S(1)} %stack.73.where, bf16[512,512]{1,0:T(8,128)(2,1)S(1)} %bitcast.42, bf16[512,512]{1,0:T(8,128)(2,1)S(1)} %collective-permute-done.partner, ...), custom_call_target="tpu_custom_call" | custom-call | flops 268435456 | bytes 1048576 | tf_op jit(solution)/shard_map/pallas_call | solution.py:300
  21.8 0.1 collective-permute-start.6
  21.9 0.5 collective-permute-start.7
  22.4 0.0 collective-permute-done.8
  22.4 0.0 collective-permute-done.9
  22.4 2.4 %collective-permute-done.10 = bf16[64,384]{1,0:T(8,128)(2,1)S(1)} collective-permute-done((bf16[64,384]{1,0:T(8,128)(2,1)S(1)}, bf16[64,384]{1,0:T(8,128)(2,1)S(1)}, u32[]{:S(2)}, u32[]{:S(2)}) %collective-permute-start.10) | collective-permute-done | bytes 49184 | tf_op jit(solution)/shard_map/ppermute | solution.py:235
  24.9 0.0 collective-permute-done.6
  24.9 0.0 collective-permute-done.7.dh_got
  24.9 1.1 %shard_map.54 = (bf16[64,1280]{1,0:T(8,128)(2,1)S(1)}, bf16[64,1280]{1,0:T(8,128)(2,1)S(1)}, bf16[64,1280]{1,0:T(8,128)(2,1)S(1)}, bf16[64,1280]{1,0:T(8,128)(2,1)S(1)}) custom-call(s32[5]{0:T(128)S(1)} %stack.73.where, bf16[2,128,512]{2,1,0:T(8,128)(2,1)S(1)} %bitcast.46, bf16[2,128,512]{2,1,0:T(8,128)(2,1)S(1)} %collective-permute-done.2.far, ...), custom_call_target="tpu_custom_call" | custom-call | flops 234881024 | bytes 1048576 | tf_op jit(solution)/shard_map/pallas_call | solution.py:311
  26.0 0.3 collective-permute-start.11
  26.3 2.6 %collective-permute-start.12 = (bf16[64,1280]{1,0:T(8,128)(2,1)S(1)}, bf16[64,1280]{1,0:T(8,128)(2,1)S(1)}, u32[]{:S(2)}, u32[]{:S(2)}) collective-permute-start(bf16[64,1280]{1,0:T(8,128)(2,1)S(1)} %get-tuple-element.36), channel_id=1, source_target_pairs={{0,4},{2,6},{4,0},{6,2},{1,5},{3,7},{5,1},{7,3},{8,12},{10,14},{12... | collective-permute-start | bytes 491528 | tf_op jit(solution)/shard_map/ppermute | solution.py:235
  28.9 1.5 %collective-permute-start.13 = (bf16[64,1280]{1,0:T(8,128)(2,1)S(1)}, bf16[64,1280]{1,0:T(8,128)(2,1)S(1)}, u32[]{:S(2)}, u32[]{:S(2)}) collective-permute-start(bf16[64,1280]{1,0:T(8,128)(2,1)S(1)} %get-tuple-element.37), channel_id=1, source_target_pairs={{0,6},{2,4},{4,2},{6,0},{1,7},{3,5},{5,3},{7,1},{8,14},{10,12},{12... | collective-permute-start | bytes 491528 | tf_op jit(solution)/shard_map/ppermute | solution.py:235
  30.5 3.9 %collective-permute-done.11 = bf16[64,1280]{1,0:T(8,128)(2,1)S(1)} collective-permute-done((bf16[64,1280]{1,0:T(8,128)(2,1)S(1)}, bf16[64,1280]{1,0:T(8,128)(2,1)S(1)}, u32[]{:S(2)}, u32[]{:S(2)}) %collective-permute-start.11) | collective-permute-done | bytes 163872 | tf_op jit(solution)/shard_map/ppermute | solution.py:235
  34.4 7.0 %collective-permute-done.12 = bf16[64,1280]{1,0:T(8,128)(2,1)S(1)} collective-permute-done((bf16[64,1280]{1,0:T(8,128)(2,1)S(1)}, bf16[64,1280]{1,0:T(8,128)(2,1)S(1)}, u32[]{:S(2)}, u32[]{:S(2)}) %collective-permute-start.12) | collective-permute-done | bytes 163872 | tf_op jit(solution)/shard_map/ppermute | solution.py:235
  41.4 0.0 collective-permute-done.13
  41.4 0.1 add_convert_fusion
  41.4 2.5 %collective-permute-start.16 = (bf16[64,896]{1,0:T(8,128)(2,1)S(1)}, bf16[64,896]{1,0:T(8,128)(2,1)S(1)}, u32[]{:S(2)}, u32[]{:S(2)}) collective-permute-start(bf16[64,896]{1,0:T(8,128)(2,1)S(1)} %add_convert_fusion), channel_id=1, source_target_pairs={{0,6},{2,4},{4,2},{6,0},{1,7},{3,5},{5,3},{7,1},{8,14},{10,12},{12... | collective-permute-start | bytes 344072 | tf_op jit(solution)/shard_map/ppermute | solution.py:235
  44.0 2.1 %collective-permute-start.15 = (bf16[64,896]{1,0:T(8,128)(2,1)S(1)}, bf16[64,896]{1,0:T(8,128)(2,1)S(1)}, u32[]{:S(2)}, u32[]{:S(2)}) collective-permute-start(bf16[64,896]{1,0:T(8,128)(2,1)S(1)} %add_convert_fusion), channel_id=1, source_target_pairs={{0,4},{2,6},{4,0},{6,2},{1,5},{3,7},{5,1},{7,3},{8,12},{10,14},{12... | collective-permute-start | bytes 344072 | tf_op jit(solution)/shard_map/ppermute | solution.py:235
  46.1 0.1 collective-permute-start.14
  46.3 1.6 %collective-permute-start.18 = (bf16[4,64,384]{2,1,0:T(8,128)(2,1)S(1)}, bf16[4,64,384]{2,1,0:T(8,128)(2,1)S(1)}, u32[]{:S(2)}, u32[]{:S(2)}) collective-permute-start(bf16[4,64,384]{2,1,0:T(8,128)(2,1)S(1)} %pad_maximum_fusion.1.mine), channel_id=1, source_target_pairs={{0,1},{1,0},{2,3},{3,2},{4,5},{5,4},{6,7},{7,6},{8,9},{9,8},{10,11... | collective-permute-start | bytes 589832 | tf_op jit(solution)/shard_map/ppermute | solution.py:320
  47.9 0.4 collective-permute-done.16
  48.3 6.2 %collective-permute-done.15 = bf16[64,896]{1,0:T(8,128)(2,1)S(1)} collective-permute-done((bf16[64,896]{1,0:T(8,128)(2,1)S(1)}, bf16[64,896]{1,0:T(8,128)(2,1)S(1)}, u32[]{:S(2)}, u32[]{:S(2)}) %collective-permute-start.15) | collective-permute-done | bytes 114720 | tf_op jit(solution)/shard_map/ppermute | solution.py:235
  54.5 0.0 collective-permute-done.14
  54.6 1.5 %collective-permute-start.19 = (bf16[4,64,384]{2,1,0:T(8,128)(2,1)S(1)}, bf16[4,64,384]{2,1,0:T(8,128)(2,1)S(1)}, u32[]{:S(2)}, u32[]{:S(2)}) collective-permute-start(bf16[4,64,384]{2,1,0:T(8,128)(2,1)S(1)} %pad_maximum_fusion.2.mine), channel_id=1, source_target_pairs={{0,1},{1,0},{2,3},{3,2},{4,5},{5,4},{6,7},{7,6},{8,9},{9,8},{10,11... | collective-permute-start | bytes 589832 | tf_op jit(solution)/shard_map/ppermute | solution.py:325
  56.2 0.6 collective-permute-start.17
  56.8 0.7 %maximum_bitcast_fusion = bf16[1,2,128,512]{3,2,1,0:T(8,128)(2,1)} fusion(bf16[1,128,512]{2,1,0:T(8,128)(2,1)S(1)} %get-tuple-element.39, bf16[1,128,512]{2,1,0:T(8,128)(2,1)S(1)} %get-tuple-element.38), kind=kLoop, calls=%fused_computation | loop fusion | flops 131072 | bytes 524288 | tf_op jit(solution)/shard_map/broadcast_in_dim | solution.py:346
  57.5 0.0 collective-permute-done.18.other
  57.5 4.9 %shard_map.55.act_inv = f32[512,512]{1,0:T(8,128)S(1)} custom-call(s32[5]{0:T(128)S(1)} %stack.73.where, bf16[4,64,384]{2,1,0:T(8,128)(2,1)S(1)} %pad_maximum_fusion.1.mine, bf16[4,64,384]{2,1,0:T(8,128)(2,1)S(1)} %collective-permute-done.18.other), custom_call_target="tpu_custom_call" | custom-call | flops 1073741824 | bytes 1048576 | tf_op jit(solution)/shard_map/pallas_call | solution.py:329
  62.5 0.0 collective-permute-done.19.other
  62.5 4.9 %shard_map.56.out_inv = f32[512,512]{1,0:T(8,128)S(1)} custom-call(s32[5]{0:T(128)S(1)} %stack.73.where, bf16[4,64,384]{2,1,0:T(8,128)(2,1)S(1)} %pad_maximum_fusion.2.mine, bf16[4,64,384]{2,1,0:T(8,128)(2,1)S(1)} %collective-permute-done.19.other), custom_call_target="tpu_custom_call" | custom-call | flops 1073741824 | bytes 1048576 | tf_op jit(solution)/shard_map/pallas_call | solution.py:329
  67.4 0.0 collective-permute-done.17.other
  67.4 3.2 %shard_map.57 = f32[512,512]{1,0:T(8,128)} custom-call(s32[5]{0:T(128)S(1)} %stack.73.where, bf16[4,64,512]{2,1,0:T(8,128)(2,1)S(1)} %pad_maximum_fusion.mine, bf16[4,64,512]{2,1,0:T(8,128)(2,1)S(1)} %collective-permute-done.17.other, f32[512,512]{1,0:T(8,128)S(1)} %shard_map.55.act_inv, f32[512,512]{1,0:T(8,128)S(1)} %shard_map.56.out_inv), custom_call_target="tpu_custom_call" | custom-call | flops 536870912 | bytes 1048576 | tf_op jit(solution)/shard_map/pallas_call | solution.py:339
  (17 shorter events, 0.2 us)
Async XLA Ops:
  0.6 5.6 %copy-start.2 = (bf16[1,2,128,512]{3,2,1,0:T(8,128)(2,1)S(1)}, bf16[1,2,128,512]{3,2,1,0:T(8,128)(2,1)}, u32[]{:S(2)}) copy-start(bf16[1,2,128,512]{3,2,1,0:T(8,128)(2,1)} %param.3) | copy-start | bytes 786436
  0.6 5.6 %collective-permute-start = (bf16[512,512]{1,0:T(8,128)(2,1)}, bf16[512,512]{1,0:T(8,128)(2,1)S(1)}, u32[]{:S(2)}, u32[]{:S(2)}) collective-permute-start(bf16[512,512]{1,0:T(8,128)(2,1)} %bitcast.39), channel_id=1, source_target_pairs={{0,8},{8,0},{1,9},{9,1},{2,10},{10,2},{3,11},{11,3},{4,12},{12,4},... | collective-permute-start | bytes 1572872 | tf_op jit(solution)/shard_map/ppermute | solution.py:258
  1.2 12.6 %collective-permute-start.2 = (bf16[2,128,512]{2,1,0:T(8,128)(2,1)}, bf16[2,128,512]{2,1,0:T(8,128)(2,1)S(1)}, u32[]{:S(2)}, u32[]{:S(2)}) collective-permute-start(bf16[2,128,512]{2,1,0:T(8,128)(2,1)} %bitcast.43), channel_id=1, source_target_pairs={{0,1},{1,0},{2,3},{3,2},{4,5},{5,4},{6,7},{7,6},{8,9},{9,8},{10,11... | collective-permute-start | bytes 786440 | tf_op jit(solution)/shard_map/ppermute | solution.py:260
  4.7 1.4 %collective-permute-start.1 = (bf16[128,512]{1,0:T(8,128)(2,1)S(1)}, bf16[128,512]{1,0:T(8,128)(2,1)S(1)}, u32[]{:S(2)}, u32[]{:S(2)}) collective-permute-start(bf16[128,512]{1,0:T(8,128)(2,1)S(1)} %select_bitcast_fusion.2), channel_id=1, source_target_pairs={{0,8},{8,0},{1,9},{9,1},{2,10},{10,2},{3,11},{11,3},{4,12},{12,4},... | collective-permute-start | bytes 393224 | tf_op jit(solution)/shard_map/ppermute | solution.py:259
  6.1 12.8 %collective-permute-start.3 = (bf16[128,512]{1,0:T(8,128)(2,1)S(1)}, bf16[128,512]{1,0:T(8,128)(2,1)S(1)}, u32[]{:S(2)}, u32[]{:S(2)}) collective-permute-start(bf16[128,512]{1,0:T(8,128)(2,1)S(1)} %collective-permute-done.1.partner_x), channel_id=1, source_target_pairs={{0,1},{1,0},{2,3},{3,2},{4,5},{5,4},{6,7},{7,6},{8,9},{9,8},{10,11... | collective-permute-start | bytes 393224 | tf_op jit(solution)/shard_map/ppermute | solution.py:261
  6.2 1.0 %copy-start = (bf16[1,512,512]{2,1,0:T(8,128)(2,1)S(1)}, bf16[1,512,512]{2,1,0:T(8,128)(2,1)}, u32[]{:S(2)}) copy-start(bf16[1,512,512]{2,1,0:T(8,128)(2,1)} %param.4) | copy-start | bytes 1572868
  7.3 0.9 %copy-start.3 = (bf16[2,128,512]{2,1,0:T(8,128)(2,1)S(1)}, bf16[2,128,512]{2,1,0:T(8,128)(2,1)}, u32[]{:S(2)}) copy-start(bf16[2,128,512]{2,1,0:T(8,128)(2,1)} %cot_last.3) | copy-start | bytes 786436
  9.5 9.7 %copy-start.1 = (bf16[1,512,512]{2,1,0:T(8,128)(2,1)S(1)}, bf16[1,512,512]{2,1,0:T(8,128)(2,1)}, u32[]{:S(2)}) copy-start(bf16[1,512,512]{2,1,0:T(8,128)(2,1)} %param.4) | copy-start | bytes 1572868
  9.5 10.6 %collective-permute-start.5 = (bf16[128,512]{1,0:T(8,128)(2,1)S(1)}, bf16[128,512]{1,0:T(8,128)(2,1)S(1)}, u32[]{:S(2)}, u32[]{:S(2)}) collective-permute-start(bf16[128,512]{1,0:T(8,128)(2,1)S(1)} %get-tuple-element.25), channel_id=1, source_target_pairs={{0,17},{1,16},{16,1},{17,0},{2,19},{3,18},{18,3},{19,2},{4,21},{5,... | collective-permute-start | bytes 393224 | tf_op jit(solution)/shard_map/ppermute | solution.py:272
  12.5 8.0 %collective-permute-start.4 = (bf16[128,512]{1,0:T(8,128)(2,1)S(1)}, bf16[128,512]{1,0:T(8,128)(2,1)S(1)}, u32[]{:S(2)}, u32[]{:S(2)}) collective-permute-start(bf16[128,512]{1,0:T(8,128)(2,1)S(1)} %get-tuple-element.24.after), channel_id=1, source_target_pairs={{16,0},{17,1},{18,2},{19,3},{20,4},{21,5},{22,6},{23,7},{24,8},{25... | collective-permute-start | bytes 393224 | tf_op jit(solution)/shard_map/ppermute | solution.py:271
  14.7 7.7 %collective-permute-start.8 = (bf16[64,384]{1,0:T(8,128)(2,1)S(1)}, bf16[64,384]{1,0:T(8,128)(2,1)S(1)}, u32[]{:S(2)}, u32[]{:S(2)}) collective-permute-start(bf16[64,384]{1,0:T(8,128)(2,1)S(1)} %get-tuple-element.31), channel_id=1, source_target_pairs={{0,2},{2,0},{4,6},{6,4},{1,3},{3,1},{5,7},{7,5},{8,10},{10,8},{12,... | collective-permute-start | bytes 147464 | tf_op jit(solution)/shard_map/ppermute | solution.py:235
  16.3 6.1 %collective-permute-start.9 = (bf16[64,384]{1,0:T(8,128)(2,1)S(1)}, bf16[64,384]{1,0:T(8,128)(2,1)S(1)}, u32[]{:S(2)}, u32[]{:S(2)}) collective-permute-start(bf16[64,384]{1,0:T(8,128)(2,1)S(1)} %get-tuple-element.32), channel_id=1, source_target_pairs={{0,4},{2,6},{4,0},{6,2},{1,5},{3,7},{5,1},{7,3},{8,12},{10,14},{12... | collective-permute-start | bytes 147464 | tf_op jit(solution)/shard_map/ppermute | solution.py:235
  18.9 1.5 %copy-start.4 = (bf16[2,128,512]{2,1,0:T(8,128)(2,1)S(1)}, bf16[2,128,512]{2,1,0:T(8,128)(2,1)}, u32[]{:S(2)}) copy-start(bf16[2,128,512]{2,1,0:T(8,128)(2,1)} %cot_last.3) | copy-start | bytes 786436
  18.9 5.9 %collective-permute-start.10 = (bf16[64,384]{1,0:T(8,128)(2,1)S(1)}, bf16[64,384]{1,0:T(8,128)(2,1)S(1)}, u32[]{:S(2)}, u32[]{:S(2)}) collective-permute-start(bf16[64,384]{1,0:T(8,128)(2,1)S(1)} %get-tuple-element.33), channel_id=1, source_target_pairs={{0,6},{2,4},{4,2},{6,0},{1,7},{3,5},{5,3},{7,1},{8,14},{10,12},{12... | collective-permute-start | bytes 147464 | tf_op jit(solution)/shard_map/ppermute | solution.py:235
  21.8 3.0 %collective-permute-start.6 = (bf16[128,512]{1,0:T(8,128)(2,1)S(1)}, bf16[128,512]{1,0:T(8,128)(2,1)S(1)}, u32[]{:S(2)}, u32[]{:S(2)}) collective-permute-start(bf16[128,512]{1,0:T(8,128)(2,1)S(1)} %get-tuple-element.26), channel_id=1, source_target_pairs={{0,8},{8,0},{1,9},{9,1},{2,10},{10,2},{3,11},{11,3},{4,12},{12,4},... | collective-permute-start | bytes 393224 | tf_op jit(solution)/shard_map/ppermute | solution.py:308
  21.9 3.0 %collective-permute-start.7 = (bf16[256,512]{1,0:T(8,128)(2,1)S(1)}, bf16[256,512]{1,0:T(8,128)(2,1)S(1)}, u32[]{:S(2)}, u32[]{:S(2)}) collective-permute-start(bf16[256,512]{1,0:T(8,128)(2,1)S(1)} %get-tuple-element.29), channel_id=1, source_target_pairs={{0,8},{8,0},{1,9},{9,1},{2,10},{10,2},{3,11},{11,3},{4,12},{12,4},... | collective-permute-start | bytes 786440 | tf_op jit(solution)/shard_map/ppermute | solution.py:307
  26.0 8.4 %collective-permute-start.11 = (bf16[64,1280]{1,0:T(8,128)(2,1)S(1)}, bf16[64,1280]{1,0:T(8,128)(2,1)S(1)}, u32[]{:S(2)}, u32[]{:S(2)}) collective-permute-start(bf16[64,1280]{1,0:T(8,128)(2,1)S(1)} %get-tuple-element.35), channel_id=1, source_target_pairs={{0,2},{2,0},{4,6},{6,4},{1,3},{3,1},{5,7},{7,5},{8,10},{10,8},{12,... | collective-permute-start | bytes 491528 | tf_op jit(solution)/shard_map/ppermute | solution.py:235
  26.3 15.0 %collective-permute-start.12 = (bf16[64,1280]{1,0:T(8,128)(2,1)S(1)}, bf16[64,1280]{1,0:T(8,128)(2,1)S(1)}, u32[]{:S(2)}, u32[]{:S(2)}) collective-permute-start(bf16[64,1280]{1,0:T(8,128)(2,1)S(1)} %get-tuple-element.36), channel_id=1, source_target_pairs={{0,4},{2,6},{4,0},{6,2},{1,5},{3,7},{5,1},{7,3},{8,12},{10,14},{12... | collective-permute-start | bytes 491528 | tf_op jit(solution)/shard_map/ppermute | solution.py:235
  28.9 12.4 %collective-permute-start.13 = (bf16[64,1280]{1,0:T(8,128)(2,1)S(1)}, bf16[64,1280]{1,0:T(8,128)(2,1)S(1)}, u32[]{:S(2)}, u32[]{:S(2)}) collective-permute-start(bf16[64,1280]{1,0:T(8,128)(2,1)S(1)} %get-tuple-element.37), channel_id=1, source_target_pairs={{0,6},{2,4},{4,2},{6,0},{1,7},{3,5},{5,3},{7,1},{8,14},{10,12},{12... | collective-permute-start | bytes 491528 | tf_op jit(solution)/shard_map/ppermute | solution.py:235
  41.4 6.8 %collective-permute-start.16 = (bf16[64,896]{1,0:T(8,128)(2,1)S(1)}, bf16[64,896]{1,0:T(8,128)(2,1)S(1)}, u32[]{:S(2)}, u32[]{:S(2)}) collective-permute-start(bf16[64,896]{1,0:T(8,128)(2,1)S(1)} %add_convert_fusion), channel_id=1, source_target_pairs={{0,6},{2,4},{4,2},{6,0},{1,7},{3,5},{5,3},{7,1},{8,14},{10,12},{12... | collective-permute-start | bytes 344072 | tf_op jit(solution)/shard_map/ppermute | solution.py:235
  44.0 10.5 %collective-permute-start.15 = (bf16[64,896]{1,0:T(8,128)(2,1)S(1)}, bf16[64,896]{1,0:T(8,128)(2,1)S(1)}, u32[]{:S(2)}, u32[]{:S(2)}) collective-permute-start(bf16[64,896]{1,0:T(8,128)(2,1)S(1)} %add_convert_fusion), channel_id=1, source_target_pairs={{0,4},{2,6},{4,0},{6,2},{1,5},{3,7},{5,1},{7,3},{8,12},{10,14},{12... | collective-permute-start | bytes 344072 | tf_op jit(solution)/shard_map/ppermute | solution.py:235
  46.1 8.4 %collective-permute-start.14 = (bf16[64,896]{1,0:T(8,128)(2,1)S(1)}, bf16[64,896]{1,0:T(8,128)(2,1)S(1)}, u32[]{:S(2)}, u32[]{:S(2)}) collective-permute-start(bf16[64,896]{1,0:T(8,128)(2,1)S(1)} %add_convert_fusion), channel_id=1, source_target_pairs={{0,2},{2,0},{4,6},{6,4},{1,3},{3,1},{5,7},{7,5},{8,10},{10,8},{12,... | collective-permute-start | bytes 344072 | tf_op jit(solution)/shard_map/ppermute | solution.py:235
  46.3 11.2 %collective-permute-start.18 = (bf16[4,64,384]{2,1,0:T(8,128)(2,1)S(1)}, bf16[4,64,384]{2,1,0:T(8,128)(2,1)S(1)}, u32[]{:S(2)}, u32[]{:S(2)}) collective-permute-start(bf16[4,64,384]{2,1,0:T(8,128)(2,1)S(1)} %pad_maximum_fusion.1.mine), channel_id=1, source_target_pairs={{0,1},{1,0},{2,3},{3,2},{4,5},{5,4},{6,7},{7,6},{8,9},{9,8},{10,11... | collective-permute-start | bytes 589832 | tf_op jit(solution)/shard_map/ppermute | solution.py:320
  54.6 7.9 %collective-permute-start.19 = (bf16[4,64,384]{2,1,0:T(8,128)(2,1)S(1)}, bf16[4,64,384]{2,1,0:T(8,128)(2,1)S(1)}, u32[]{:S(2)}, u32[]{:S(2)}) collective-permute-start(bf16[4,64,384]{2,1,0:T(8,128)(2,1)S(1)} %pad_maximum_fusion.2.mine), channel_id=1, source_target_pairs={{0,1},{1,0},{2,3},{3,2},{4,5},{5,4},{6,7},{7,6},{8,9},{9,8},{10,11... | collective-permute-start | bytes 589832 | tf_op jit(solution)/shard_map/ppermute | solution.py:325
  56.2 11.2 %collective-permute-start.17 = (bf16[4,64,512]{2,1,0:T(8,128)(2,1)S(1)}, bf16[4,64,512]{2,1,0:T(8,128)(2,1)S(1)}, u32[]{:S(2)}, u32[]{:S(2)}) collective-permute-start(bf16[4,64,512]{2,1,0:T(8,128)(2,1)S(1)} %pad_maximum_fusion.mine), channel_id=1, source_target_pairs={{0,1},{1,0},{2,3},{3,2},{4,5},{5,4},{6,7},{7,6},{8,9},{9,8},{10,11... | collective-permute-start | bytes 786440 | tf_op jit(solution)/shard_map/ppermute | solution.py:326

commit v5 on v4

v5 whole, which is shorter than its diff:
```python
import functools

import jax
import jax.numpy as jnp
import numpy as np
from jax import lax
from jax.experimental import pallas as pl
from jax.experimental.pallas import tpu as pltpu
from jax.sharding import Mesh, PartitionSpec as P

BF16 = jnp.bfloat16
F32 = jnp.float32
SWAP = [(0, 1), (1, 0)]
SMEM = pl.BlockSpec(memory_space=pltpu.SMEM)
VMEM = pl.BlockSpec(memory_space=pltpu.VMEM)
ANY = pl.BlockSpec(memory_space=pl.ANY)


def silu_slope(pre):
    sig = jax.nn.sigmoid(pre)
    return sig * (1.0 + pre * (1.0 - sig))


def slope_of(inputs, matrix):
    return silu_slope(jnp.dot(inputs, matrix, preferred_element_type=F32))


def layer(upstream, slope, matrix):
    dh = (upstream.astype(F32) * slope).astype(BF16)
    back = lax.dot_general(dh, matrix, (((1,), (1,)), ((), ())), preferred_element_type=F32)
    return dh, (upstream.astype(F32) + back).astype(BF16)


def by_core(core, run, own, partner):
    @pl.when(core == 1)
    def _():
        run(own, partner)

    @pl.when(core == 0)
    def _():
        run(partner, own)


def load_kernel(where, weight, local, cot_last, weight_copy, slope, cot):
    core = where[2]
    weight_copy[...] = weight[...]
    cot[...] = cot_last[core]
    slope[...] = slope_of(local[core], weight_copy[...])


def first_kernel(where, own, partner, slope_own, local, cot_last, slope_partner, inputs, down, cross):
    inputs[...] = local[where[2]]
    upstream = cot_last[...]
    slope_partner[...] = slope_of(inputs[...], partner[...])

    def run(odd, even):
        cot = layer(upstream, odd[1][...], odd[0][...])[1]
        down[...] = layer(cot, even[1][...], even[0][...])[1]

    by_core(where[2], run, (own, slope_own), (partner, slope_partner))
    cross[...] = jnp.where(where[3] == 0, upstream, down[...])


def far_kernel(where, own, partner, far, partner_far, slope_own, slope_partner):
    slope_own[...] = slope_of(far[where[2]], own[...])
    slope_partner[...] = slope_of(partner_far[...], partner[...])


def layers_kernel(
    where, own, partner, near_own, near_partner, far_own, far_partner, near, far, cot_last,
    own_dh, give_dh, own_cot, give_cot, upstream,
):
    rows = near.shape[0]
    top = where[3] == where[4] - 1
    upstream[:rows] = jnp.where(top, cot_last[...], near[...])
    upstream[rows:] = far[...]

    def step(incoming, matrix, near_slope, far_slope, dh_out, cot_out):
        slope = jnp.concatenate([near_slope[...], far_slope[...]])
        dh, cot = layer(incoming, slope, matrix[...])
        dh_out[...] = dh
        cot_out[...] = cot[:rows]
        return cot

    def run(odd, even):
        step(step(upstream[...], *odd), *even)

    by_core(
        where[2],
        run,
        (own, near_own, far_own, own_dh, own_cot),
        (partner, near_partner, far_partner, give_dh, give_cot),
    )


def moment(left, right):
    return lax.dot_general(left, right, (((0,), (0,)), ((), ())), preferred_element_type=F32)


def split(value):
    high = value.astype(BF16)
    return high, (value - high.astype(F32)).astype(BF16)


def product(left, right, dims=((1,), (0,))):
    def dot(a, b):
        return lax.dot_general(a, b, (dims, ((), ())), preferred_element_type=F32)

    total = dot(left[0], right[0])
    if len(right) > 1:
        total += dot(left[0], right[1])
    if len(left) > 1:
        total += dot(left[1], right[0])
    return total


def call(kernel, flops, out_shape, in_specs, scratch=()):
    return pl.pallas_call(
        kernel,
        out_shape=out_shape,
        in_specs=in_specs,
        out_specs=jax.tree.map(lambda _: VMEM, out_shape),
        scratch_shapes=list(scratch),
        cost_estimate=pl.CostEstimate(flops=flops, bytes_accessed=1 << 20, transcendentals=0),
        compiler_params=pltpu.CompilerParams(vmem_limit_bytes=32 << 20),
    )


def blocks_of(tokens, side):
    half = tokens.shape[1] // 2
    quarter = half // 2
    own = pl.multiple_of(side * half, half)
    other = pl.multiple_of(half - side * half, half)
    mine = tokens[:, pl.ds(own, half)]
    upper = moment(mine[:, :quarter], mine)
    near = tokens[:, pl.ds(other, quarter)]
    lower = moment(mine[:, quarter:], jnp.concatenate([mine[:, quarter:], near], axis=1))
    left = tokens[:, pl.ds(pl.multiple_of(own + side * quarter, quarter), quarter)]
    right = tokens[:, pl.ds(pl.multiple_of(other + side * quarter, quarter), quarter)]
    return mine, jnp.concatenate([upper, lower]), moment(left, right)


def act_kernel(where, local, far, after, blocks, extra, tokens):
    micro, rows = local.shape[:2]
    for m in range(micro):
        tokens[m * rows:(m + 1) * rows] = local[m]
        tokens[(micro + m) * rows:(micro + m + 1) * rows] = far[m]
    _, main, corner = blocks_of(tokens, where[1])
    blocks[...] = main.astype(BF16)
    extra[...] = corner


def grad_kernel(where, local, far, dh_own, dh_got, act_blocks, act_extra, *refs):
    parts, (inputs, tokens, corners, whole) = refs[:-4], refs[-4:]
    line = len(parts)
    rows, width = local.shape[1:]
    core = where[2]
    inputs[:rows] = local[core]
    inputs[rows:2 * rows] = far[core]
    inputs[2 * rows:3 * rows] = local[1 - core]
    inputs[3 * rows:] = far[1 - core]
    tokens[:2 * rows] = dh_own[...]
    tokens[2 * rows:] = dh_got[...]
    half, quarter = width // 2, width // 4
    mine, main, corner = blocks_of(tokens, where[1])
    whole[:, :half] = act_blocks[...]
    whole[:, half:width] = main.astype(BF16)
    few = quarter // line
    for j in range(line):
        corners[2 * j * few:(2 * j + 1) * few] = act_extra[j * few:(j + 1) * few]
        corners[(2 * j + 1) * few:(2 * j + 2) * few] = corner[j * few:(j + 1) * few]
    whole[:, width:width + quarter] = corners[...].astype(BF16)
    whole[:, width + quarter:] = moment(mine, inputs[...]).astype(BF16)
    for step, part in enumerate(parts):
        count = part.shape[0]
        part[...] = whole[pl.ds(pl.multiple_of((where[0] ^ step) * count, count), count)]


def invert(total, count):
    row = lax.broadcasted_iota(jnp.int32, total.shape, 0)
    column = lax.broadcasted_iota(jnp.int32, total.shape, 1)
    eye = (row == column).astype(F32)
    ridge = 0.01
    mean = total[...].astype(F32) * (1.0 / count)
    full = mean + ridge * eye
    scale = lax.rsqrt(jnp.sum(full * full, keepdims=True))
    squared = product((total[...],), (total[...],)) * (1.0 / count) ** 2 + ridge * (mean + full)
    first = full * scale
    second = 2.0 * first - squared * (scale * scale)
    second_terms = split(second)
    last = 2.0 * (eye - second) + product(second_terms, second_terms)
    tail = 2.0 * last - product(second_terms, split(last))
    return split((2.0 * tail - product(split(first), split(tail))) * scale)


def inverse_kernel(count, where, mine, other, act_high, act_low, out_high, out_low, blocks, corners, act, out):
    line, rows = mine.shape[:2]
    few = rows // 2
    side = where[1]
    half = line * rows
    q = half // 2
    width = 2 * half
    for source, part in enumerate((mine, other)):
        for step in range(line):
            place = where[0] ^ step
            start = pl.multiple_of(place * rows, rows)
            blocks[source, pl.ds(start, rows)] = part[step, :, :width].astype(F32)
            corner = part[step, :, width:].astype(F32)
            start = pl.multiple_of(place * few, few)
            corners[source, 0, pl.ds(start, few)] = corner[:few]
            corners[source, 1, pl.ds(start, few)] = corner[few:]

    for which, total in enumerate((act, out)):
        first = which * half

        def put(row, column, value):
            total[row * q:(row + 1) * q, column * q:(column + 1) * q] = value.astype(BF16)

        def both(row, column, value):
            put(row, column, value)
            put(column, row, value.T)

        for source, at in enumerate((0, 2)):
            put(at, at, blocks[source, :q, first:first + q])
            both(at, at + 1, blocks[source, :q, first + q:first + half])
            put(at + 1, at + 1, blocks[source, q:, first:first + q])
            both(at + 1, (at + 2) % 4, blocks[source, q:, first + q:first + half])
        ours, theirs = corners[0, which], corners[1, which].T
        both(0, 2, jnp.where(side == 0, ours, theirs))
        both(1, 3, jnp.where(side == 0, theirs, ours))

    own = pl.multiple_of(side * half, half)
    away = pl.multiple_of(half - side * half, half)
    for result, term in zip((out_high, out_low), invert(out, count)):
        result[...] = term
    for result, term in zip((act_high, act_low), invert(act, count)):
        for i, a in enumerate((own, away)):
            for j, b in enumerate((own, away)):
                result[pl.ds(a, half), pl.ds(b, half)] = term[i * half:(i + 1) * half, j * half:(j + 1) * half]


def half_update(where, grad, act_inv, out_inv, rows_of, part):
    line, rows = grad.shape[:2]
    for step in range(line):
        start = pl.multiple_of((where[0] ^ step) * rows, rows)
        rows_of[pl.ds(start, rows)] = grad[step]
    half = line * rows
    left = product((rows_of[...],), tuple(term[...] for term in act_inv))
    right = tuple(term[part * half:(part + 1) * half] for term in out_inv)
    return product(split(left), right, ((0,), (0,)))


def own_kernel(where, grad, act_high, act_low, out_high, out_low, result, rows_of):
    result[...] = half_update(where, grad, (act_high, act_low), (out_high, out_low), rows_of, 0)


def update_kernel(where, grad, act_high, act_low, out_high, out_low, own, result, rows_of):
    term = half_update(where, grad, (act_high, act_low), (out_high, out_low), rows_of, 1)
    half = term.shape[1] // 2
    result[:, pl.ds(pl.multiple_of(where[1] * half, half), half)] = own[:, :half] + term[:, :half]
    result[:, pl.ds(pl.multiple_of(half - where[1] * half, half), half)] = own[:, half:] + term[:, half:]


def send(parts):
    line = len(parts)
    got = {0: parts[0]}
    for step in sorted(range(1, line), key=lambda k: (-(k & (line // 2)), k)):
        got[step] = lax.ppermute(parts[step], "line", [(i, i ^ step) for i in range(line)])
    return [got[step] for step in range(line)]


def body(acts, weights, cot_last):
    pairs = lax.axis_size("row")
    line = lax.axis_size("line")
    row = lax.axis_index("row")
    core = lax.axis_index("core")
    side = lax.axis_index("side")
    weight = weights[0]
    local = acts[0]
    micro, rows, width = local.shape
    count = micro * rows * line * 2
    odd = core == 1
    where = jnp.stack([lax.axis_index("line"), side, core, row, pairs]).astype(jnp.int32)

    def mine_of(pair):
        return jnp.where(odd, pair[1], pair[0])

    partner = lax.ppermute(weight, "core", SWAP)
    partner_local = lax.ppermute(local, "core", SWAP)
    far = lax.ppermute(local, "side", SWAP)
    block = jax.ShapeDtypeStruct((rows, width), BF16)
    slope = jax.ShapeDtypeStruct((rows, width), F32)
    square = jax.ShapeDtypeStruct((width, width), BF16)
    own, near_own, last = call(
        load_kernel, 2 * rows * width**2, [square, slope, block], [SMEM] + [VMEM] * 3
    )(where, weight, local, cot_last)
    near_partner, partner_x, down, cross = call(
        first_kernel, 6 * rows * width**2, [slope, block, block, block], [SMEM] + [VMEM] * 5
    )(where, own, partner, near_own, partner_local, last)
    partner_far = lax.ppermute(partner_x, "side", SWAP)
    first = down
    for turn in range(1, pairs):
        straight = [(r, r - 1) for r in range(1, pairs)]
        diagonal = [(2 * r + s, 2 * ((r - 1) % pairs) + 1 - s) for r in range(pairs) for s in range(2)]
        upstream = lax.ppermute(down, "row", straight)
        crossing = lax.ppermute(cross, ("row", "side"), diagonal)
        here = row == pairs - 1 - turn
        if turn == 1:
            near_up, far_up = upstream, crossing
        else:
            near_up = jnp.where(here, upstream, near_up)
            far_up = jnp.where(here, crossing, far_up)
        if turn < pairs - 1:
            cot = layer(upstream, mine_of((near_partner, near_own)), mine_of((partner, own)))[1]
            down = layer(cot, mine_of((near_own, near_partner)), mine_of((own, partner)))[1]
            cross = jnp.where(row == 0, last, down)

    tokens = 2 * micro * rows
    half, quarter = width // 2, width // 4
    act_blocks, act_extra = call(
        act_kernel,
        2 * tokens * half * width,
        [jax.ShapeDtypeStruct((half, half), BF16), jax.ShapeDtypeStruct((quarter, quarter), F32)],
        [SMEM, VMEM, VMEM, ANY],
        [pltpu.VMEM((tokens, width), BF16)],
    )(where, local, far, first)

    far_own, far_partner = call(
        far_kernel, 4 * rows * width**2, [slope, slope], [SMEM] + [VMEM] * 4
    )(where, own, partner, far, partner_far)
    pair = jax.ShapeDtypeStruct((2 * rows, width), BF16)
    own_dh, give_dh, own_cot, give_cot = call(
        layers_kernel,
        8 * rows * width**2,
        [pair, pair, block, block],
        [SMEM] + [VMEM] * 9,
        [pltpu.VMEM((2 * rows, width), BF16)],
    )(where, own, partner, near_own, near_partner, far_own, far_partner, near_up, far_up, last)
    got_dh = lax.ppermute(give_dh, "core", SWAP)
    other_cot = lax.ppermute(give_cot, "core", SWAP)
    cot = jnp.stack([mine_of((own_cot, other_cot)), mine_of((other_cot, own_cot))])

    factors = width + quarter
    parts = call(
        grad_kernel,
        4 * tokens * half * width,
        [jax.ShapeDtypeStruct((half // line, factors + width), BF16)] * line,
        [SMEM] + [VMEM] * 6,
        [
            pltpu.VMEM((tokens, width), BF16),
            pltpu.VMEM((tokens, width), BF16),
            pltpu.VMEM((half, quarter), F32),
            pltpu.VMEM((half, factors + width), BF16),
        ],
    )(where, local, far, own_dh, got_dh, act_blocks, act_extra)
    total = sum(piece.astype(F32) for piece in send(parts)).astype(BF16)
    factors_mine = jnp.stack(send([total[:, :factors]] * line))
    factors_other = lax.ppermute(factors_mine, "side", SWAP)
    grad_mine = jnp.stack(send([total[:, factors:]] * line))
    grad_other = lax.ppermute(grad_mine, "side", SWAP)
    terms = call(
        functools.partial(inverse_kernel, count),
        40 * width**3,
        [square] * 4,
        [SMEM, VMEM, VMEM],
        [
            pltpu.VMEM((2, half, width), F32),
            pltpu.VMEM((2, 2, quarter, quarter), F32),
            pltpu.VMEM((width, width), BF16),
            pltpu.VMEM((width, width), BF16),
        ],
    )(where, factors_mine, factors_other)
    whole = jax.ShapeDtypeStruct((width, width), F32)
    rows_of = [pltpu.VMEM((half, width), BF16)]
    own_term = call(own_kernel, 5 * width**3, whole, [SMEM] + [VMEM] * 5, rows_of)(where, grad_mine, *terms)
    update = call(update_kernel, 5 * width**3, whole, [SMEM] + [VMEM] * 6, rows_of)(
        where, grad_other, *terms, own_term
    )
    return (cot[None], update[None])


def solution(mesh):
    sections, shards = mesh.devices.shape
    finer = Mesh(
        np.reshape(mesh.devices, (sections // 2, 2, shards // 2, 2)),
        ("row", "core", "line", "side"),
    )
    section, dp = ("row", "core"), ("line", "side")
    placed = (P(section, None, dp, None), P(section, None, None), P(None, dp, None))
    return jax.shard_map(
        body,
        mesh=finer,
        in_specs=placed,
        out_specs=(P(section, None, dp, None), P(section, None, None)),
        check_vma=False,
    )
```

time: 70.9 us -> 74.2 us (1.047)
  waiting for transfers between devices: 21.5 us -> 26.9 us
  starting transfers between devices: 25.6 us -> 24.2 us
  other arithmetic: 1.94 us -> 0.92 us
  local copies, waits for them, and re-layouts: 2.16 us -> 3.05 us
    ppermute x3 -> x2, starting transfers between devices: 3.34 us -> 0.95 us  [the longest x1 0.87 us: body(): factors_other = lax.ppermute(factors_mine, 'side', SWAP)]
    ppermute x1, waiting for transfers between devices: 0.01 us -> 2.11 us  [body(): partner_far = lax.ppermute(partner_x, 'side', SWAP)]
    ppermute x1, waiting for transfers between devices: 0.41 us -> 2.38 us  [body(): upstream = lax.ppermute(down, 'row', straight)]
    ppermute x1, waiting for transfers between devices: 0.01 us -> 1.78 us  [body(): crossing = lax.ppermute(cross, ('row', 'side'), diagonal)]
    ppermute x3 -> x2, waiting for transfers between devices: 1.11 us -> 0.01 us  [the longest x1 0.01 us: body(): partner_local = lax.ppermute(local, 'core', SWAP)]
    select_n x1 -> x0, other arithmetic: 0.99 us -> none  [others_of(): return jnp.where(odd, pair[0], pair[1])]
    unnamed x10 -> x8, local copies, waits for them, and re-layouts: 2.01 us -> 2.94 us
    pallas_call x6 -> x7, Pallas kernels: 16.4 us -> 16.1 us  [the longest x1 7.78 us: body(): call(functools.partial(inverse_kernel, count), 40 * width ** 3, [square]...]
  transfers between devices with their start and end apart: 20 -> 19, of which waited for: 7 -> 12; matrix products, arithmetic and copies ran while one was open for 3% -> 1% of each run, Pallas kernels for 20% -> 18%
where the time goes in v5:
time: 74.2 us; the launch traced here: 74 us
  waiting for transfers between devices  26.9 us (36%)
  starting transfers between devices  24.2 us (33%)
  Pallas kernels  18.1 us (24%)
  local copies, waits for them, and re-layouts  3.05 us (4%)
  other arithmetic  0.92 us (1%)
  between operations  0.8 us (1%)
    ppermute x9, waiting for transfers between devices, send(): lax.ppermute(parts[step], 'line', [(i, i ^ step) for i in range(line)])  19.9 us
    ppermute x9, starting transfers between devices, send(): lax.ppermute(parts[step], 'line', [(i, i ^ step) for i in range(line)])  14.2 us
    pallas_call x1, Pallas kernels, body(): call(functools.partial(inverse_kernel, count), 40 * width ** 3, [square]...  7.78 us
    ppermute x1, starting transfers between devices, body(): crossing = lax.ppermute(cross, ('row', 'side'), diagonal)  2.97 us
    unnamed x8, local copies, waits for them, and re-layouts  2.94 us
    ppermute x1, starting transfers between devices, body(): far = lax.ppermute(local, 'side', SWAP)  2.92 us
    pallas_call x1, Pallas kernels, body(): call(update_kernel, 5 * width ** 3, whole, [SMEM] + [VMEM] * 6, rows_of)  2.61 us
    ppermute x1, waiting for transfers between devices, body(): upstream = lax.ppermute(down, 'row', straight)  2.38 us
  transfers between devices with their start and end apart: 19, of which 12 were waited for; matrix products, arithmetic and copies ran while one was open for 1% of the time, Pallas kernels for 18%

profile of v5, /device:TPU:0, one launch (start us, length us, event | category | flops | bytes accessed | tf_op | source)
XLA Modules:
  0.0 74.0 jit_solution(5163297496840560314)
XLA Ops:
  0.6 0.5 collective-permute-start
  1.1 0.1 collective-permute-start.1
  1.2 2.9 %collective-permute-start.2 = (bf16[2,128,512]{2,1,0:T(8,128)(2,1)}, bf16[2,128,512]{2,1,0:T(8,128)(2,1)S(1)}, u32[]{:S(2)}, u32[]{:S(2)}) collective-permute-start(bf16[2,128,512]{2,1,0:T(8,128)(2,1)} %bitcast.24), channel_id=1, source_target_pairs={{0,1},{1,0},{2,3},{3,2},{4,5},{5,4},{6,7},{7,6},{8,9},{9,8},{10,11... | collective-permute-start | bytes 786440 | tf_op jit(solution)/shard_map/ppermute | solution.py:290
  4.1 0.1 stack.58.where
  4.2 0.0 copy-start
  4.2 0.9 %copy-done = bf16[1,2,128,512]{3,2,1,0:T(8,128)(2,1)S(1)} copy-done((bf16[1,2,128,512]{3,2,1,0:T(8,128)(2,1)S(1)}, bf16[1,2,128,512]{3,2,1,0:T(8,128)(2,1)}, u32[]{:S(2)}) %copy-start) | copy-done | bytes 262168
  5.2 0.0 copy-start.2
  5.2 1.0 %copy-done.2 = bf16[1,512,512]{2,1,0:T(8,128)(2,1)S(1)} copy-done((bf16[1,512,512]{2,1,0:T(8,128)(2,1)S(1)}, bf16[1,512,512]{2,1,0:T(8,128)(2,1)}, u32[]{:S(2)}) %copy-start.2) | copy-done | bytes 524312
  6.2 0.0 copy-start.3
  6.2 0.9 %copy-done.3 = bf16[2,128,512]{2,1,0:T(8,128)(2,1)S(1)} copy-done((bf16[2,128,512]{2,1,0:T(8,128)(2,1)S(1)}, bf16[2,128,512]{2,1,0:T(8,128)(2,1)}, u32[]{:S(2)}) %copy-start.3) | copy-done | bytes 262168
  7.2 0.8 %shard_map.50 = (bf16[512,512]{1,0:T(8,128)(2,1)S(1)}, f32[128,512]{1,0:T(8,128)S(1)}, bf16[128,512]{1,0:T(8,128)(2,1)S(1)}) custom-call(s32[5]{0:T(128)S(1)} %stack.58.where, bf16[512,512]{1,0:T(8,128)(2,1)S(1)} %bitcast.29, bf16[2,128,512]{2,1,0:T(8,128)(2,1)S(1)} %bitcast.25, bf16[2,128,512]{2,1,0:T(8,128)(2,1)S(1)} %copy-done.3), custom_call_target="tpu_custom_call" | custom-call | flops 67108864 | bytes 1048576 | tf_op jit(solution)/shard_map/pallas_call | solution.py:294
  8.0 0.0 collective-permute-done.1.local
  8.0 0.0 collective-permute-done.partner
  8.0 1.4 %shard_map.51 = (f32[128,512]{1,0:T(8,128)S(1)}, bf16[128,512]{1,0:T(8,128)(2,1)S(1)}, bf16[128,512]{1,0:T(8,128)(2,1)S(1)}, bf16[128,512]{1,0:T(8,128)(2,1)S(1)}) custom-call(s32[5]{0:T(128)S(1)} %stack.58.where, bf16[512,512]{1,0:T(8,128)(2,1)S(1)} %get-tuple-element.25.own, bf16[512,512]{1,0:T(8,128)(2,1)S(1)} %collective-permute-done.partner, ...), custom_call_target="tpu_custom_call" | custom-call | flops 201326592 | bytes 1048576 | tf_op jit(solution)/shard_map/pallas_call | solution.py:297
  9.4 0.1 collective-permute-start.3
  9.5 3.0 %collective-permute-start.5 = (bf16[128,512]{1,0:T(8,128)(2,1)S(1)}, bf16[128,512]{1,0:T(8,128)(2,1)S(1)}, u32[]{:S(2)}, u32[]{:S(2)}) collective-permute-start(bf16[128,512]{1,0:T(8,128)(2,1)S(1)} %get-tuple-element.33), channel_id=1, source_target_pairs={{0,17},{1,16},{16,1},{17,0},{2,19},{3,18},{18,3},{19,2},{4,21},{5,... | collective-permute-start | bytes 393224 | tf_op jit(solution)/shard_map/ppermute | solution.py:306
  12.4 1.3 %collective-permute-start.4 = (bf16[128,512]{1,0:T(8,128)(2,1)S(1)}, bf16[128,512]{1,0:T(8,128)(2,1)S(1)}, u32[]{:S(2)}, u32[]{:S(2)}) collective-permute-start(bf16[128,512]{1,0:T(8,128)(2,1)S(1)} %get-tuple-element.32.after), channel_id=1, source_target_pairs={{16,0},{17,1},{18,2},{19,3},{20,4},{21,5},{22,6},{23,7},{24,8},{25... | collective-permute-start | bytes 393224 | tf_op jit(solution)/shard_map/ppermute | solution.py:305
  13.7 0.0 collective-permute-done.2.far
  13.7 2.1 %collective-permute-done.3.partner_far = bf16[128,512]{1,0:T(8,128)(2,1)S(1)} collective-permute-done((bf16[128,512]{1,0:T(8,128)(2,1)S(1)}, bf16[128,512]{1,0:T(8,128)(2,1)S(1)}, u32[]{:S(2)}, u32[]{:S(2)}) %collective-permute-start.3) | collective-permute-done | bytes 131104 | tf_op jit(solution)/shard_map/ppermute | solution.py:300
  15.8 0.9 %shard_map.52 = (f32[128,512]{1,0:T(8,128)S(1)}, f32[128,512]{1,0:T(8,128)S(1)}) custom-call(s32[5]{0:T(128)S(1)} %stack.58.where, bf16[512,512]{1,0:T(8,128)(2,1)S(1)} %get-tuple-element.25.own, bf16[512,512]{1,0:T(8,128)(2,1)S(1)} %collective-permute-done.partner, bf16[2,128,512]{2,1,0:T(8,128)(2,1)S(1)} %collective-permute-done.2.far, ...), custom_call_target="tpu_custom_call" | custom-call | flops 134217728 | bytes 1048576 | tf_op jit(solution)/shard_map/pallas_call | solution.py:328
  16.7 1.8 %collective-permute-done.5.far = bf16[128,512]{1,0:T(8,128)(2,1)S(1)} collective-permute-done((bf16[128,512]{1,0:T(8,128)(2,1)S(1)}, bf16[128,512]{1,0:T(8,128)(2,1)S(1)}, u32[]{:S(2)}, u32[]{:S(2)}) %collective-permute-start.5) | collective-permute-done | bytes 131104 | tf_op jit(solution)/shard_map/ppermute | solution.py:306
  18.5 2.4 %collective-permute-done.4.near = bf16[128,512]{1,0:T(8,128)(2,1)S(1)} collective-permute-done((bf16[128,512]{1,0:T(8,128)(2,1)S(1)}, bf16[128,512]{1,0:T(8,128)(2,1)S(1)}, u32[]{:S(2)}, u32[]{:S(2)}) %collective-permute-start.4) | collective-permute-done | bytes 131104 | tf_op jit(solution)/shard_map/ppermute | solution.py:305
  20.9 0.0 copy-start.1
  20.9 1.2 %shard_map.53 = (bf16[256,512]{1,0:T(8,128)(2,1)S(1)}, bf16[256,512]{1,0:T(8,128)(2,1)S(1)}, bf16[128,512]{1,0:T(8,128)(2,1)S(1)}, bf16[128,512]{1,0:T(8,128)(2,1)S(1)}) custom-call(s32[5]{0:T(128)S(1)} %stack.58.where, bf16[512,512]{1,0:T(8,128)(2,1)S(1)} %get-tuple-element.25.own, bf16[512,512]{1,0:T(8,128)(2,1)S(1)} %collective-permute-done.partner, ...), custom_call_target="tpu_custom_call" | custom-call | flops 268435456 | bytes 1048576 | tf_op jit(solution)/shard_map/pallas_call | solution.py:332
  22.1 0.1 collective-permute-start.7
  22.1 0.0 copy-done.1
  22.1 0.9 %shard_map.54 = (bf16[256,256]{1,0:T(8,128)(2,1)S(1)}, f32[128,128]{1,0:T(8,128)S(1)}) custom-call(s32[5]{0:T(128)S(1)} %stack.58.where, bf16[2,128,512]{2,1,0:T(8,128)(2,1)S(1)} %bitcast.26, bf16[2,128,512]{2,1,0:T(8,128)(2,1)S(1)} %collective-permute-done.2.far, bf16[128,512]{1,0:T(8,128)(2,1)S(1)} %get-tuple-element.32.after), custom_call_target="tpu_custom_call" | custom-call | flops 134217728 | bytes 1048576 | tf_op jit(solution)/shard_map/pallas_call | solution.py:320
  23.0 0.6 collective-permute-done.7.dh_got
  23.7 1.1 %shard_map.55 = (bf16[64,1152]{1,0:T(8,128)(2,1)S(1)}, bf16[64,1152]{1,0:T(8,128)(2,1)S(1)}, bf16[64,1152]{1,0:T(8,128)(2,1)S(1)}, bf16[64,1152]{1,0:T(8,128)(2,1)S(1)}) custom-call(s32[5]{0:T(128)S(1)} %stack.58.where, bf16[2,128,512]{2,1,0:T(8,128)(2,1)S(1)} %bitcast.27, bf16[2,128,512]{2,1,0:T(8,128)(2,1)S(1)} %collective-permute-done.2.far, ...), custom_call_target="tpu_custom_call" | custom-call | flops 268435456 | bytes 1048576 | tf_op jit(solution)/shard_map/pallas_call | solution.py:344
  24.7 1.6 %collective-permute-start.8 = (bf16[64,1152]{1,0:T(8,128)(2,1)S(1)}, bf16[64,1152]{1,0:T(8,128)(2,1)S(1)}, u32[]{:S(2)}, u32[]{:S(2)}) collective-permute-start(bf16[64,1152]{1,0:T(8,128)(2,1)S(1)} %get-tuple-element.41), channel_id=1, source_target_pairs={{0,2},{2,0},{4,6},{6,4},{1,3},{3,1},{5,7},{7,5},{8,10},{10,8},{12,... | collective-permute-start | bytes 442376 | tf_op jit(solution)/shard_map/ppermute | solution.py:268
  26.4 2.6 %collective-permute-start.9 = (bf16[64,1152]{1,0:T(8,128)(2,1)S(1)}, bf16[64,1152]{1,0:T(8,128)(2,1)S(1)}, u32[]{:S(2)}, u32[]{:S(2)}) collective-permute-start(bf16[64,1152]{1,0:T(8,128)(2,1)S(1)} %get-tuple-element.42), channel_id=1, source_target_pairs={{0,4},{2,6},{4,0},{6,2},{1,5},{3,7},{5,1},{7,3},{8,12},{10,14},{12... | collective-permute-start | bytes 442376 | tf_op jit(solution)/shard_map/ppermute | solution.py:268
  29.0 0.2 collective-permute-start.10
  29.2 0.0 collective-permute-start.6
  29.2 3.9 %collective-permute-done.8 = bf16[64,1152]{1,0:T(8,128)(2,1)S(1)} collective-permute-done((bf16[64,1152]{1,0:T(8,128)(2,1)S(1)}, bf16[64,1152]{1,0:T(8,128)(2,1)S(1)}, u32[]{:S(2)}, u32[]{:S(2)}) %collective-permute-start.8) | collective-permute-done | bytes 147488 | tf_op jit(solution)/shard_map/ppermute | solution.py:268
  33.1 7.2 %collective-permute-done.9 = bf16[64,1152]{1,0:T(8,128)(2,1)S(1)} collective-permute-done((bf16[64,1152]{1,0:T(8,128)(2,1)S(1)}, bf16[64,1152]{1,0:T(8,128)(2,1)S(1)}, u32[]{:S(2)}, u32[]{:S(2)}) %collective-permute-start.9) | collective-permute-done | bytes 147488 | tf_op jit(solution)/shard_map/ppermute | solution.py:268
  40.3 0.0 collective-permute-done.10
  40.3 0.1 add_convert_fusion
  40.5 3.7 %collective-permute-start.16 = (bf16[64,640]{1,0:T(8,128)(2,1)S(1)}, bf16[64,640]{1,0:T(8,128)(2,1)S(1)}, u32[]{:S(2)}, u32[]{:S(2)}) collective-permute-start(bf16[64,640]{1,0:T(8,128)(2,1)S(1)} %get-tuple-element.51), channel_id=1, source_target_pairs={{0,4},{2,6},{4,0},{6,2},{1,5},{3,7},{5,1},{7,3},{8,12},{10,14},{12... | collective-permute-start | bytes 245768 | tf_op jit(solution)/shard_map/ppermute | solution.py:268
  44.2 0.0 collective-permute-start.15
  44.2 1.5 %collective-permute-start.17 = (bf16[64,640]{1,0:T(8,128)(2,1)S(1)}, bf16[64,640]{1,0:T(8,128)(2,1)S(1)}, u32[]{:S(2)}, u32[]{:S(2)}) collective-permute-start(bf16[64,640]{1,0:T(8,128)(2,1)S(1)} %get-tuple-element.51), channel_id=1, source_target_pairs={{0,6},{2,4},{4,2},{6,0},{1,7},{3,5},{5,3},{7,1},{8,14},{10,12},{12... | collective-permute-start | bytes 245768 | tf_op jit(solution)/shard_map/ppermute | solution.py:268
  45.7 0.0 collective-permute-done.6
  45.7 1.3 %collective-permute-done.16 = bf16[64,640]{1,0:T(8,128)(2,1)S(1)} collective-permute-done((bf16[64,640]{1,0:T(8,128)(2,1)S(1)}, bf16[64,640]{1,0:T(8,128)(2,1)S(1)}, u32[]{:S(2)}, u32[]{:S(2)}) %collective-permute-start.16) | collective-permute-done | bytes 81952 | tf_op jit(solution)/shard_map/ppermute | solution.py:268
  47.0 2.3 %collective-permute-done.15 = bf16[64,640]{1,0:T(8,128)(2,1)S(1)} collective-permute-done((bf16[64,640]{1,0:T(8,128)(2,1)S(1)}, bf16[64,640]{1,0:T(8,128)(2,1)S(1)}, u32[]{:S(2)}, u32[]{:S(2)}) %collective-permute-start.15) | collective-permute-done | bytes 81952 | tf_op jit(solution)/shard_map/ppermute | solution.py:268
  49.3 1.4 %collective-permute-done.17 = bf16[64,640]{1,0:T(8,128)(2,1)S(1)} collective-permute-done((bf16[64,640]{1,0:T(8,128)(2,1)S(1)}, bf16[64,640]{1,0:T(8,128)(2,1)S(1)}, u32[]{:S(2)}, u32[]{:S(2)}) %collective-permute-start.17) | collective-permute-done | bytes 81952 | tf_op jit(solution)/shard_map/ppermute | solution.py:268
  50.7 0.1 pad_maximum_fusion.mine
  50.8 0.9 %collective-permute-start.18 = (bf16[4,64,640]{2,1,0:T(8,128)(2,1)S(1)}, bf16[4,64,640]{2,1,0:T(8,128)(2,1)S(1)}, u32[]{:S(2)}, u32[]{:S(2)}) collective-permute-start(bf16[4,64,640]{2,1,0:T(8,128)(2,1)S(1)} %pad_maximum_fusion.mine), channel_id=1, source_target_pairs={{0,1},{1,0},{2,3},{3,2},{4,5},{5,4},{6,7},{7,6},{8,9},{9,8},{10,11... | collective-permute-start | bytes 983048 | tf_op jit(solution)/shard_map/ppermute | solution.py:358
  51.7 2.0 %collective-permute-start.12 = (bf16[64,512]{1,0:T(8,128)(2,1)S(1)}, bf16[64,512]{1,0:T(8,128)(2,1)S(1)}, u32[]{:S(2)}, u32[]{:S(2)}) collective-permute-start(bf16[64,512]{1,0:T(8,128)(2,1)S(1)} %get-tuple-element.53), channel_id=1, source_target_pairs={{0,4},{2,6},{4,0},{6,2},{1,5},{3,7},{5,1},{7,3},{8,12},{10,14},{12... | collective-permute-start | bytes 196616 | tf_op jit(solution)/shard_map/ppermute | solution.py:268
  53.7 0.9 %collective-permute-start.11 = (bf16[64,512]{1,0:T(8,128)(2,1)S(1)}, bf16[64,512]{1,0:T(8,128)(2,1)S(1)}, u32[]{:S(2)}, u32[]{:S(2)}) collective-permute-start(bf16[64,512]{1,0:T(8,128)(2,1)S(1)} %get-tuple-element.53), channel_id=1, source_target_pairs={{0,2},{2,0},{4,6},{6,4},{1,3},{3,1},{5,7},{7,5},{8,10},{10,8},{12,... | collective-permute-start | bytes 196616 | tf_op jit(solution)/shard_map/ppermute | solution.py:268
  54.6 1.5 %collective-permute-start.13 = (bf16[64,512]{1,0:T(8,128)(2,1)S(1)}, bf16[64,512]{1,0:T(8,128)(2,1)S(1)}, u32[]{:S(2)}, u32[]{:S(2)}) collective-permute-start(bf16[64,512]{1,0:T(8,128)(2,1)S(1)} %get-tuple-element.53), channel_id=1, source_target_pairs={{0,6},{2,4},{4,2},{6,0},{1,7},{3,5},{5,3},{7,1},{8,14},{10,12},{12... | collective-permute-start | bytes 196616 | tf_op jit(solution)/shard_map/ppermute | solution.py:268
  56.1 0.7 maximum_bitcast_fusion
  56.8 1.6 %collective-permute-done.12 = bf16[64,512]{1,0:T(8,128)(2,1)S(1)} collective-permute-done((bf16[64,512]{1,0:T(8,128)(2,1)S(1)}, bf16[64,512]{1,0:T(8,128)(2,1)S(1)}, u32[]{:S(2)}, u32[]{:S(2)}) %collective-permute-start.12) | collective-permute-done | bytes 65568 | tf_op jit(solution)/shard_map/ppermute | solution.py:268
  58.5 0.1 collective-permute-done.11
  58.6 2.1 %collective-permute-done.13 = bf16[64,512]{1,0:T(8,128)(2,1)S(1)} collective-permute-done((bf16[64,512]{1,0:T(8,128)(2,1)S(1)}, bf16[64,512]{1,0:T(8,128)(2,1)S(1)}, u32[]{:S(2)}, u32[]{:S(2)}) %collective-permute-start.13) | collective-permute-done | bytes 65568 | tf_op jit(solution)/shard_map/ppermute | solution.py:268
  60.7 1.3 %collective-permute-start.14 = (bf16[4,64,512]{2,1,0:T(8,128)(2,1)S(1)}, bf16[4,64,512]{2,1,0:T(8,128)(2,1)S(1)}, u32[]{:S(2)}, u32[]{:S(2)}) collective-permute-start(bf16[4,64,512]{2,1,0:T(8,128)(2,1)S(1)} %pad_maximum_fusion.1.grad), channel_id=1, source_target_pairs={{0,1},{1,0},{2,3},{3,2},{4,5},{5,4},{6,7},{7,6},{8,9},{9,8},{10,11... | collective-permute-start | bytes 786440 | tf_op jit(solution)/shard_map/ppermute | solution.py:360
  62.0 0.0 collective-permute-done.18.other
  62.0 7.8 %shard_map.56 = (bf16[512,512]{1,0:T(8,128)(2,1)S(1)}, bf16[512,512]{1,0:T(8,128)(2,1)S(1)}, bf16[512,512]{1,0:T(8,128)(2,1)S(1)}, bf16[512,512]{1,0:T(8,128)(2,1)S(1)}) custom-call(s32[5]{0:T(128)S(1)} %stack.58.where, bf16[4,64,640]{2,1,0:T(8,128)(2,1)S(1)} %pad_maximum_fusion.mine, bf16[4,64,640]{2,1,0:T(8,128)(2,1)S(1)} %collective-permute-done.18.other), custom_call_target="tpu_custom_call" | custom-call | flops 5368709120 | bytes 1048576 | tf_op jit(solution)/shard_map/pallas_call | solution.py:361
  69.8 1.6 %shard_map.57.own = f32[512,512]{1,0:T(8,128)S(1)} custom-call(s32[5]{0:T(128)S(1)} %stack.58.where, bf16[4,64,512]{2,1,0:T(8,128)(2,1)S(1)} %pad_maximum_fusion.1.grad, bf16[512,512]{1,0:T(8,128)(2,1)S(1)} %get-tuple-element.44.act_high, bf16[512,512]{1,0:T(8,128)(2,1)S(1)} %get-tuple-element.45.act_low, bf16[512,512]{1,0:T(8,128)(2,1)S(1)} %get-tuple-element.46.out_high, ...), custom_call_target="tpu_custom_call" | custom-call | flops 671088640 | bytes 1048576 | tf_op jit(solution)/shard_map/pallas_call | solution.py:375
  71.4 0.0 collective-permute-done.14.grad
  71.4 2.6 %shard_map.58 = f32[512,512]{1,0:T(8,128)} custom-call(s32[5]{0:T(128)S(1)} %stack.58.where, bf16[4,64,512]{2,1,0:T(8,128)(2,1)S(1)} %collective-permute-done.14.grad, bf16[512,512]{1,0:T(8,128)(2,1)S(1)} %get-tuple-element.44.act_high, bf16[512,512]{1,0:T(8,128)(2,1)S(1)} %get-tuple-element.45.act_low, bf16[512,512]{1,0:T(8,128)(2,1)S(1)} %get-tuple-element.46.out_high, ...), custom_call_target="tpu_custom_call" | custom-call | flops 671088640 | bytes 1048576 | tf_op jit(solution)/shard_map/pallas_call | solution.py:376
  (4 shorter events, 0.1 us)
Async XLA Ops:
  0.6 7.4 %collective-permute-start = (bf16[512,512]{1,0:T(8,128)(2,1)}, bf16[512,512]{1,0:T(8,128)(2,1)S(1)}, u32[]{:S(2)}, u32[]{:S(2)}) collective-permute-start(bf16[512,512]{1,0:T(8,128)(2,1)} %bitcast.28), channel_id=1, source_target_pairs={{0,8},{8,0},{1,9},{9,1},{2,10},{10,2},{3,11},{11,3},{4,12},{12,4},... | collective-permute-start | bytes 1572872 | tf_op jit(solution)/shard_map/ppermute | solution.py:288
  1.1 6.9 %collective-permute-start.1 = (bf16[2,128,512]{2,1,0:T(8,128)(2,1)}, bf16[2,128,512]{2,1,0:T(8,128)(2,1)S(1)}, u32[]{:S(2)}, u32[]{:S(2)}) collective-permute-start(bf16[2,128,512]{2,1,0:T(8,128)(2,1)} %bitcast.23), channel_id=1, source_target_pairs={{0,8},{8,0},{1,9},{9,1},{2,10},{10,2},{3,11},{11,3},{4,12},{12,4},... | collective-permute-start | bytes 786440 | tf_op jit(solution)/shard_map/ppermute | solution.py:289
  1.2 12.5 %collective-permute-start.2 = (bf16[2,128,512]{2,1,0:T(8,128)(2,1)}, bf16[2,128,512]{2,1,0:T(8,128)(2,1)S(1)}, u32[]{:S(2)}, u32[]{:S(2)}) collective-permute-start(bf16[2,128,512]{2,1,0:T(8,128)(2,1)} %bitcast.24), channel_id=1, source_target_pairs={{0,1},{1,0},{2,3},{3,2},{4,5},{5,4},{6,7},{7,6},{8,9},{9,8},{10,11... | collective-permute-start | bytes 786440 | tf_op jit(solution)/shard_map/ppermute | solution.py:290
  4.2 1.0 %copy-start = (bf16[1,2,128,512]{3,2,1,0:T(8,128)(2,1)S(1)}, bf16[1,2,128,512]{3,2,1,0:T(8,128)(2,1)}, u32[]{:S(2)}) copy-start(bf16[1,2,128,512]{3,2,1,0:T(8,128)(2,1)} %param.3) | copy-start | bytes 786436
  5.2 1.0 %copy-start.2 = (bf16[1,512,512]{2,1,0:T(8,128)(2,1)S(1)}, bf16[1,512,512]{2,1,0:T(8,128)(2,1)}, u32[]{:S(2)}) copy-start(bf16[1,512,512]{2,1,0:T(8,128)(2,1)} %param.4) | copy-start | bytes 1572868
  6.2 0.9 %copy-start.3 = (bf16[2,128,512]{2,1,0:T(8,128)(2,1)S(1)}, bf16[2,128,512]{2,1,0:T(8,128)(2,1)}, u32[]{:S(2)}) copy-start(bf16[2,128,512]{2,1,0:T(8,128)(2,1)} %cot_last.1) | copy-start | bytes 786436
  9.4 6.5 %collective-permute-start.3 = (bf16[128,512]{1,0:T(8,128)(2,1)S(1)}, bf16[128,512]{1,0:T(8,128)(2,1)S(1)}, u32[]{:S(2)}, u32[]{:S(2)}) collective-permute-start(bf16[128,512]{1,0:T(8,128)(2,1)S(1)} %get-tuple-element.29), channel_id=1, source_target_pairs={{0,1},{1,0},{2,3},{3,2},{4,5},{5,4},{6,7},{7,6},{8,9},{9,8},{10,11... | collective-permute-start | bytes 393224 | tf_op jit(solution)/shard_map/ppermute | solution.py:300
  9.5 9.1 %collective-permute-start.5 = (bf16[128,512]{1,0:T(8,128)(2,1)S(1)}, bf16[128,512]{1,0:T(8,128)(2,1)S(1)}, u32[]{:S(2)}, u32[]{:S(2)}) collective-permute-start(bf16[128,512]{1,0:T(8,128)(2,1)S(1)} %get-tuple-element.33), channel_id=1, source_target_pairs={{0,17},{1,16},{16,1},{17,0},{2,19},{3,18},{18,3},{19,2},{4,21},{5,... | collective-permute-start | bytes 393224 | tf_op jit(solution)/shard_map/ppermute | solution.py:306
  12.4 8.5 %collective-permute-start.4 = (bf16[128,512]{1,0:T(8,128)(2,1)S(1)}, bf16[128,512]{1,0:T(8,128)(2,1)S(1)}, u32[]{:S(2)}, u32[]{:S(2)}) collective-permute-start(bf16[128,512]{1,0:T(8,128)(2,1)S(1)} %get-tuple-element.32.after), channel_id=1, source_target_pairs={{16,0},{17,1},{18,2},{19,3},{20,4},{21,5},{22,6},{23,7},{24,8},{25... | collective-permute-start | bytes 393224 | tf_op jit(solution)/shard_map/ppermute | solution.py:305
  20.9 1.2 %copy-start.1 = (bf16[1,2,128,512]{3,2,1,0:T(8,128)(2,1)S(1)}, bf16[1,2,128,512]{3,2,1,0:T(8,128)(2,1)}, u32[]{:S(2)}) copy-start(bf16[1,2,128,512]{3,2,1,0:T(8,128)(2,1)} %param.3) | copy-start | bytes 786436
  22.1 1.6 %collective-permute-start.7 = (bf16[256,512]{1,0:T(8,128)(2,1)S(1)}, bf16[256,512]{1,0:T(8,128)(2,1)S(1)}, u32[]{:S(2)}, u32[]{:S(2)}) collective-permute-start(bf16[256,512]{1,0:T(8,128)(2,1)S(1)} %get-tuple-element.37), channel_id=1, source_target_pairs={{0,8},{8,0},{1,9},{9,1},{2,10},{10,2},{3,11},{11,3},{4,12},{12,4},... | collective-permute-start | bytes 786440 | tf_op jit(solution)/shard_map/ppermute | solution.py:339
  24.7 8.4 %collective-permute-start.8 = (bf16[64,1152]{1,0:T(8,128)(2,1)S(1)}, bf16[64,1152]{1,0:T(8,128)(2,1)S(1)}, u32[]{:S(2)}, u32[]{:S(2)}) collective-permute-start(bf16[64,1152]{1,0:T(8,128)(2,1)S(1)} %get-tuple-element.41), channel_id=1, source_target_pairs={{0,2},{2,0},{4,6},{6,4},{1,3},{3,1},{5,7},{7,5},{8,10},{10,8},{12,... | collective-permute-start | bytes 442376 | tf_op jit(solution)/shard_map/ppermute | solution.py:268
  26.4 14.0 %collective-permute-start.9 = (bf16[64,1152]{1,0:T(8,128)(2,1)S(1)}, bf16[64,1152]{1,0:T(8,128)(2,1)S(1)}, u32[]{:S(2)}, u32[]{:S(2)}) collective-permute-start(bf16[64,1152]{1,0:T(8,128)(2,1)S(1)} %get-tuple-element.42), channel_id=1, source_target_pairs={{0,4},{2,6},{4,0},{6,2},{1,5},{3,7},{5,1},{7,3},{8,12},{10,14},{12... | collective-permute-start | bytes 442376 | tf_op jit(solution)/shard_map/ppermute | solution.py:268
  29.0 11.4 %collective-permute-start.10 = (bf16[64,1152]{1,0:T(8,128)(2,1)S(1)}, bf16[64,1152]{1,0:T(8,128)(2,1)S(1)}, u32[]{:S(2)}, u32[]{:S(2)}) collective-permute-start(bf16[64,1152]{1,0:T(8,128)(2,1)S(1)} %get-tuple-element.43), channel_id=1, source_target_pairs={{0,6},{2,4},{4,2},{6,0},{1,7},{3,5},{5,3},{7,1},{8,14},{10,12},{12... | collective-permute-start | bytes 442376 | tf_op jit(solution)/shard_map/ppermute | solution.py:268
  29.2 16.5 %collective-permute-start.6 = (bf16[128,512]{1,0:T(8,128)(2,1)S(1)}, bf16[128,512]{1,0:T(8,128)(2,1)S(1)}, u32[]{:S(2)}, u32[]{:S(2)}) collective-permute-start(bf16[128,512]{1,0:T(8,128)(2,1)S(1)} %get-tuple-element.34), channel_id=1, source_target_pairs={{0,8},{8,0},{1,9},{9,1},{2,10},{10,2},{3,11},{11,3},{4,12},{12,4},... | collective-permute-start | bytes 393224 | tf_op jit(solution)/shard_map/ppermute | solution.py:340
  40.5 6.6 %collective-permute-start.16 = (bf16[64,640]{1,0:T(8,128)(2,1)S(1)}, bf16[64,640]{1,0:T(8,128)(2,1)S(1)}, u32[]{:S(2)}, u32[]{:S(2)}) collective-permute-start(bf16[64,640]{1,0:T(8,128)(2,1)S(1)} %get-tuple-element.51), channel_id=1, source_target_pairs={{0,4},{2,6},{4,0},{6,2},{1,5},{3,7},{5,1},{7,3},{8,12},{10,14},{12... | collective-permute-start | bytes 245768 | tf_op jit(solution)/shard_map/ppermute | solution.py:268
  44.2 5.2 %collective-permute-start.15 = (bf16[64,640]{1,0:T(8,128)(2,1)S(1)}, bf16[64,640]{1,0:T(8,128)(2,1)S(1)}, u32[]{:S(2)}, u32[]{:S(2)}) collective-permute-start(bf16[64,640]{1,0:T(8,128)(2,1)S(1)} %get-tuple-element.51), channel_id=1, source_target_pairs={{0,2},{2,0},{4,6},{6,4},{1,3},{3,1},{5,7},{7,5},{8,10},{10,8},{12,... | collective-permute-start | bytes 245768 | tf_op jit(solution)/shard_map/ppermute | solution.py:268
  44.2 6.5 %collective-permute-start.17 = (bf16[64,640]{1,0:T(8,128)(2,1)S(1)}, bf16[64,640]{1,0:T(8,128)(2,1)S(1)}, u32[]{:S(2)}, u32[]{:S(2)}) collective-permute-start(bf16[64,640]{1,0:T(8,128)(2,1)S(1)} %get-tuple-element.51), channel_id=1, source_target_pairs={{0,6},{2,4},{4,2},{6,0},{1,7},{3,5},{5,3},{7,1},{8,14},{10,12},{12... | collective-permute-start | bytes 245768 | tf_op jit(solution)/shard_map/ppermute | solution.py:268
  50.8 11.2 %collective-permute-start.18 = (bf16[4,64,640]{2,1,0:T(8,128)(2,1)S(1)}, bf16[4,64,640]{2,1,0:T(8,128)(2,1)S(1)}, u32[]{:S(2)}, u32[]{:S(2)}) collective-permute-start(bf16[4,64,640]{2,1,0:T(8,128)(2,1)S(1)} %pad_maximum_fusion.mine), channel_id=1, source_target_pairs={{0,1},{1,0},{2,3},{3,2},{4,5},{5,4},{6,7},{7,6},{8,9},{9,8},{10,11... | collective-permute-start | bytes 983048 | tf_op jit(solution)/shard_map/ppermute | solution.py:358
  51.7 6.8 %collective-permute-start.12 = (bf16[64,512]{1,0:T(8,128)(2,1)S(1)}, bf16[64,512]{1,0:T(8,128)(2,1)S(1)}, u32[]{:S(2)}, u32[]{:S(2)}) collective-permute-start(bf16[64,512]{1,0:T(8,128)(2,1)S(1)} %get-tuple-element.53), channel_id=1, source_target_pairs={{0,4},{2,6},{4,0},{6,2},{1,5},{3,7},{5,1},{7,3},{8,12},{10,14},{12... | collective-permute-start | bytes 196616 | tf_op jit(solution)/shard_map/ppermute | solution.py:268
  53.7 4.9 %collective-permute-start.11 = (bf16[64,512]{1,0:T(8,128)(2,1)S(1)}, bf16[64,512]{1,0:T(8,128)(2,1)S(1)}, u32[]{:S(2)}, u32[]{:S(2)}) collective-permute-start(bf16[64,512]{1,0:T(8,128)(2,1)S(1)} %get-tuple-element.53), channel_id=1, source_target_pairs={{0,2},{2,0},{4,6},{6,4},{1,3},{3,1},{5,7},{7,5},{8,10},{10,8},{12,... | collective-permute-start | bytes 196616 | tf_op jit(solution)/shard_map/ppermute | solution.py:268
  54.6 6.1 %collective-permute-start.13 = (bf16[64,512]{1,0:T(8,128)(2,1)S(1)}, bf16[64,512]{1,0:T(8,128)(2,1)S(1)}, u32[]{:S(2)}, u32[]{:S(2)}) collective-permute-start(bf16[64,512]{1,0:T(8,128)(2,1)S(1)} %get-tuple-element.53), channel_id=1, source_target_pairs={{0,6},{2,4},{4,2},{6,0},{1,7},{3,5},{5,3},{7,1},{8,14},{10,12},{12... | collective-permute-start | bytes 196616 | tf_op jit(solution)/shard_map/ppermute | solution.py:268
  60.7 10.7 %collective-permute-start.14 = (bf16[4,64,512]{2,1,0:T(8,128)(2,1)S(1)}, bf16[4,64,512]{2,1,0:T(8,128)(2,1)S(1)}, u32[]{:S(2)}, u32[]{:S(2)}) collective-permute-start(bf16[4,64,512]{2,1,0:T(8,128)(2,1)S(1)} %pad_maximum_fusion.1.grad), channel_id=1, source_target_pairs={{0,1},{1,0},{2,3},{3,2},{4,5},{5,4},{6,7},{7,6},{8,9},{9,8},{10,11... | collective-permute-start | bytes 786440 | tf_op jit(solution)/shard_map/ppermute | solution.py:360

commit v6 on v1

v6 whole, which is shorter than its diff:
```python
import functools

import jax
import jax.numpy as jnp
import numpy as np
from jax import lax
from jax.experimental import pallas as pl
from jax.experimental.pallas import tpu as pltpu
from jax.sharding import Mesh, PartitionSpec as P

BF16 = jnp.bfloat16
F32 = jnp.float32
SWAP = [(0, 1), (1, 0)]
SMEM = pl.BlockSpec(memory_space=pltpu.SMEM)
VMEM = pl.BlockSpec(memory_space=pltpu.VMEM)
ANY = pl.BlockSpec(memory_space=pl.ANY)
GROUP = 4


def silu_slope(pre):
    sig = jax.nn.sigmoid(pre)
    return sig * (1.0 + pre * (1.0 - sig))


def slope_of(inputs, matrix):
    return silu_slope(jnp.dot(inputs, matrix, preferred_element_type=F32))


def layer(upstream, slope, matrix):
    dh = (upstream.astype(F32) * slope).astype(BF16)
    back = lax.dot_general(dh, matrix, (((1,), (1,)), ((), ())), preferred_element_type=F32)
    return dh, (upstream.astype(F32) + back).astype(BF16)


def by_core(core, run, own, partner):
    @pl.when(core == 1)
    def _():
        run(own, partner)

    @pl.when(core == 0)
    def _():
        run(partner, own)


def moment(left, right):
    return lax.dot_general(left, right, (((0,), (0,)), ((), ())), preferred_element_type=F32)


def split(value):
    high = value.astype(BF16)
    return high, (value - high.astype(F32)).astype(BF16)


def product(left, right, dims=((1,), (0,))):
    def dot(a, b):
        return lax.dot_general(a, b, (dims, ((), ())), preferred_element_type=F32)

    total = dot(left[0], right[0])
    if len(right) > 1:
        total += dot(left[0], right[1])
    if len(left) > 1:
        total += dot(left[1], right[0])
    return total


def call(kernel, flops, out_shape, in_specs, scratch=()):
    return pl.pallas_call(
        kernel,
        out_shape=jax.tree.map(lambda v: jax.ShapeDtypeStruct(v.shape, v.dtype), out_shape),
        in_specs=in_specs,
        out_specs=jax.tree.map(lambda _: VMEM, out_shape),
        scratch_shapes=list(scratch),
        cost_estimate=pl.CostEstimate(flops=flops, bytes_accessed=1 << 20, transcendentals=0),
        compiler_params=pltpu.CompilerParams(vmem_limit_bytes=32 << 20),
    )


def load_kernel(where, weight, local, cot_last, weight_copy, local_copy, slope, cot, done):
    core = where[0]
    copies = [
        pltpu.make_async_copy(source, target, done.at[i])
        for i, (source, target) in enumerate(
            ((weight, weight_copy), (local, local_copy), (cot_last.at[core], cot))
        )
    ]
    for copy in copies:
        copy.start()
    for copy in copies:
        copy.wait()
    slope[...] = slope_of(local_copy[core], weight_copy[...])


def first_kernel(where, own, partner, slope_own, local, upstream, slope_partner, down):
    slope_partner[...] = slope_of(local[where[0]], partner[...])

    def run(odd, even):
        cot = layer(upstream[...], odd[1][...], odd[0][...])[1]
        down[...] = layer(cot, even[1][...], even[0][...])[1]

    by_core(where[0], run, (own, slope_own), (partner, slope_partner))


def odd_kernel(where, own, partner, slope_own, slope_partner, arrived, last, dh, cot):
    upstream = jnp.where(where[2] == 1, last[...], arrived[...])

    def run(odd, even):
        dh[...], cot[...] = layer(upstream, odd[1][...], odd[0][...])

    by_core(where[0], run, (own, slope_own), (partner, slope_partner))


def even_kernel(
    where, own, partner, slope_own, slope_partner, dh, cot, after, own_dh, give_dh, own_cot, give_cot
):
    def run(odd, even):
        odd[2][...], odd[3][...] = dh[...], cot[...]
        even[2][...], even[3][...] = layer(cot[...], even[1][...], even[0][...])

    by_core(
        where[0], run, (own, slope_own, own_dh, own_cot), (partner, slope_partner, give_dh, give_cot)
    )


def put_factor(tokens, whole):
    width = tokens.shape[1]
    size = width // GROUP
    half = size // 2
    columns = [tokens[:, u * size:(u + 1) * size] for u in range(GROUP)]
    for u in range(GROUP):
        pair = jnp.concatenate([columns[u], columns[(u + 1) % GROUP]], axis=1)
        main = moment(columns[u], pair).astype(BF16)
        whole[u, :, :2 * size] = main[:half]
        whole[u, :, 2 * size:4 * size] = main[half:]
    for u in range(2):
        corner = moment(columns[u], columns[u + 2]).astype(BF16)
        whole[u, :, 4 * size:5 * size] = corner[:half]
        whole[u + 2, :, 4 * size:5 * size] = corner[half:]


def act_kernel(where, local, after, *refs):
    parts, (tokens, whole) = refs[:GROUP], refs[GROUP:]
    micro, rows = local.shape[:2]
    for m in range(micro):
        tokens[m * rows:(m + 1) * rows] = local[m]
    put_factor(tokens, whole)
    for step, part in enumerate(parts):
        part[...] = whole[where[1] ^ step]


def add_kernel(left, right, after, result):
    result[...] = (left[...].astype(F32) + right[...].astype(F32)).astype(BF16)


def begin_kernel(left, right, result):
    result[...] = left[...].astype(F32) + right[...].astype(F32)


def sum_kernel(*refs):
    pieces, result = refs[:GROUP], refs[-1]
    result[...] = sum(piece[...].astype(F32) for piece in pieces).astype(BF16)


def grad_kernel(where, local, dh_own, dh_got, *refs):
    parts, (inputs, tokens, whole) = refs[:GROUP], refs[GROUP:]
    rows, width = local.shape[1:]
    inputs[:rows] = local[where[0]]
    inputs[rows:] = local[1 - where[0]]
    tokens[:rows] = dh_own[...]
    tokens[rows:] = dh_got[...]
    put_factor(tokens, whole)
    size = width // GROUP
    half = size // 2
    for u in range(GROUP):
        grad = moment(tokens[:, u * size:(u + 1) * size], inputs[...]).astype(BF16)
        whole[u, :, 5 * size:5 * size + width] = grad[:half]
        whole[u, :, 5 * size + width:] = grad[half:]
    for step, part in enumerate(parts):
        part[...] = whole[where[1] ^ step]


def invert(total, count):
    row = lax.broadcasted_iota(jnp.int32, total.shape, 0)
    column = lax.broadcasted_iota(jnp.int32, total.shape, 1)
    eye = (row == column).astype(F32)
    ridge = 0.01
    mean = total[...].astype(F32) * (1.0 / count)
    full = mean + ridge * eye
    scale = lax.rsqrt(jnp.sum(full * full, keepdims=True))
    squared = product((total[...],), (total[...],)) * (1.0 / count) ** 2 + ridge * (mean + full)
    first = full * scale
    second = 2.0 * first - squared * (scale * scale)
    second_terms = split(second)
    last = 2.0 * (eye - second) + product(second_terms, second_terms)
    tail = 2.0 * last - product(second_terms, split(last))
    return split((2.0 * tail - product(split(first), split(tail))) * scale)

def inverse_kernel(count, where, *refs):
    pieces, (high, low, blocks, total) = refs[:GROUP], refs[GROUP:]
    for step, piece in enumerate(pieces):
        blocks[where[1] ^ step] = piece[...].astype(F32)
    size = total.shape[0] // GROUP

    def both(row, column, value):
        total[row * size:(row + 1) * size, column * size:(column + 1) * size] = value.astype(BF16)
        if row != column:
            total[column * size:(column + 1) * size, row * size:(row + 1) * size] = value.T.astype(BF16)

    for u in range(GROUP):
        main = jnp.concatenate([blocks[u, :, :2 * size], blocks[u, :, 2 * size:4 * size]])
        both(u, u, main[:, :size])
        both(u, (u + 1) % GROUP, main[:, size:])
    for u in range(2):
        both(u, u + 2, jnp.concatenate([blocks[u, :, 4 * size:], blocks[u + 2, :, 4 * size:]]))
    for result, term in zip((high, low), invert(total, count)):
        result[...] = term


def update_kernel(where, act_high, act_low, out_high, out_low, *refs):
    pieces, (result, grad) = refs[:GROUP], refs[GROUP:]
    half, twice = pieces[0].shape
    width = twice // 2
    for step, piece in enumerate(pieces):
        start = pl.multiple_of((where[1] ^ step) * 2 * half, 2 * half)
        grad[pl.ds(start, half)] = piece[:, :width]
        grad[pl.ds(start + half, half)] = piece[:, width:]
    left = product((grad[...],), (act_high[...], act_low[...]))
    result[...] = product(split(left), (out_high[...], out_low[...]), ((0,), (0,)))


def send(parts):
    got = {0: parts[0]}
    for step in (3, 1, 2):
        got[step] = lax.ppermute(parts[step], ("near", "side"), [(i, i ^ step) for i in range(GROUP)])
    return [got[step] for step in range(GROUP)]


def exchange(value, after=None):
    step = 1
    while step < lax.axis_size("far"):
        route = [(i, i ^ step) for i in range(lax.axis_size("far"))]
        got = lax.ppermute(value, "far", route)
        if after is None:
            value = (value.astype(F32) + got.astype(F32)).astype(BF16)
        else:
            value = call(add_kernel, 0, value, [VMEM, VMEM, ANY])(value, got, after)
        step *= 2
    return value


def body(acts, weights, cot_last):
    pairs = lax.axis_size("row")
    row = lax.axis_index("row")
    core = lax.axis_index("core")
    weight = weights[0]
    local = acts[0]
    micro, rows, width = local.shape
    tokens = micro * rows
    count = tokens * GROUP * lax.axis_size("far")
    odd = core == 1
    top = row == pairs - 1
    where = jnp.stack([core, lax.axis_index(("near", "side")), top.astype(jnp.int32)]).astype(jnp.int32)

    def mine_of(pair):
        return jnp.where(odd, pair[1], pair[0])

    def array(*shape, dtype=BF16):
        return jax.ShapeDtypeStruct(shape, dtype)

    partner = lax.ppermute(weight, "core", SWAP)
    partner_local = lax.ppermute(local, "core", SWAP)
    block = array(rows, width)
    slope = array(rows, width, dtype=F32)
    own, kept, slope_own, last = call(
        load_kernel,
        2 * rows * width**2,
        [array(width, width), array(micro, rows, width), slope, block],
        [SMEM] + [ANY] * 3,
        [pltpu.SemaphoreType.DMA((3,))],
    )(where, weight, local, cot_last)
    slope_partner, down = call(first_kernel, 6 * rows * width**2, [slope, block], [SMEM] + [VMEM] * 5)(
        where, own, partner, slope_own, partner_local, last
    )
    first = down
    for turn in range(1, pairs):
        upstream = lax.ppermute(down, "row", [(r, r - 1) for r in range(1, pairs)])
        arrived = upstream if turn == 1 else jnp.where(row == pairs - 1 - turn, upstream, arrived)
        if turn < pairs - 1:
            cot = layer(upstream, mine_of((slope_partner, slope_own)), mine_of((partner, own)))[1]
            down = layer(cot, mine_of((slope_own, slope_partner)), mine_of((own, partner)))[1]

    size = width // GROUP
    factor = 5 * size
    act_parts = call(
        act_kernel,
        2 * tokens * width**2,
        [array(size // 2, factor)] * GROUP,
        [SMEM, VMEM, ANY],
        [pltpu.VMEM((tokens, width), BF16), pltpu.VMEM((GROUP, size // 2, factor), BF16)],
    )(where, kept, first)
    act_pieces = send(act_parts)

    dh_odd, cot_odd = call(odd_kernel, 64 * rows * width**2, [block] * 2, [SMEM] + [VMEM] * 6)(
        where, own, partner, slope_own, slope_partner, arrived, last
    )
    act_part = call(sum_kernel, 0, array(size // 2, factor), [VMEM] * GROUP + [ANY])(*act_pieces, cot_odd)
    own_dh, give_dh, own_cot, give_cot = call(
        even_kernel, 4 * rows * width**2, [block] * 4, [SMEM] + [VMEM] * 6 + [ANY]
    )(where, own, partner, slope_own, slope_partner, dh_odd, cot_odd, act_part)
    got_dh = lax.ppermute(give_dh, "core", SWAP)
    other_cot = lax.ppermute(give_cot, "core", SWAP)
    cot = jnp.stack([mine_of((own_cot, other_cot)), mine_of((other_cot, own_cot))])

    parts = call(
        grad_kernel,
        4 * tokens * width**2,
        [array(size // 2, factor + 2 * width)] * GROUP,
        [SMEM] + [VMEM] * 3,
        [pltpu.VMEM((tokens, width), BF16)] * 2
        + [pltpu.VMEM((GROUP, size // 2, factor + 2 * width), BF16)],
    )(where, kept, own_dh, got_dh)
    pieces = send(parts)
    begun = call(
        begin_kernel, 0, array(*parts[0].shape, dtype=F32), [VMEM] * 2
    )(pieces[0], pieces[3])
    total = (begun + pieces[1].astype(F32) + pieces[2].astype(F32)).astype(BF16)
    act = send([exchange(act_part, begun)] * GROUP)
    def inverse(pieces):
        return call(
            functools.partial(inverse_kernel, count),
            20 * width**3,
            [array(width, width)] * 2,
            [SMEM] + [VMEM] * GROUP,
            [pltpu.VMEM((GROUP, size // 2, factor), F32), pltpu.VMEM((width, width), BF16)],
        )(where, *pieces)

    act_inv = inverse(act)
    total = exchange(total, act_inv[0])
    out = send([total[:, :factor]] * GROUP)
    grad = send([total[:, factor:]] * GROUP)
    update = call(
        update_kernel,
        10 * width**3,
        array(width, width, dtype=F32),
        [SMEM] + [VMEM] * (4 + GROUP),
        [pltpu.VMEM((width, width), BF16)],
    )(where, *act_inv, *inverse(out), *grad)
    return (cot[None], update[None])


def solution(mesh):
    sections, shards = mesh.devices.shape
    finer = Mesh(
        np.reshape(mesh.devices, (sections // 2, 2, shards // GROUP, 2, 2)),
        ("row", "core", "far", "near", "side"),
    )
    section, dp = ("row", "core"), ("far", "near", "side")
    placed = (P(section, None, dp, None), P(section, None, None), P(None, dp, None))
    return jax.shard_map(
        body,
        mesh=finer,
        in_specs=placed,
        out_specs=(P(section, None, dp, None), P(section, None, None)),
        check_vma=False,
    )
```

time: 180 us -> 66.9 us (0.37)
  waiting for transfers between devices: 132 us -> 19 us
  matrix products: 24.9 us -> 0 us
  starting transfers between devices: 4.95 us -> 24.4 us
  Pallas kernels: 0 us -> 18.2 us
  between operations: 15.7 us -> 0.82 us
  local copies, waits for them, and re-layouts: 0.03 us -> 2.96 us
    psum x1 -> x0, waiting for transfers between devices: 78.4 us -> none  [body(): lax.psum((moment(dh, dh).astype(jnp.bfloat16), moment(flat, dh).astype(jn...]
    all_gather x1 -> x0, waiting for transfers between devices: 42.7 us -> none  [body(): every = lax.all_gather(flat, 'dp', tiled=True)]
    dot_general x19 -> x0, matrix products: 24.9 us -> none  [the longest x10 12.5 us: mul(): return jnp.dot(left, right, precision=lax.Precision.HIGH)]
    ppermute x4 -> x22, starting transfers between devices: 4.69 us -> 24.4 us  [the longest x15 18.4 us: send(): lax.ppermute(parts[step], ('near', 'side'), [(i, i ^ step) for i in range...]
    pallas_call x0 -> x13, Pallas kernels: none -> 18.2 us  [the longest x2 8.73 us: inverse(): call(functools.partial(inverse_kernel, count), 20 * width ** 3, [array(wi...]
    ppermute x4 -> x22, waiting for transfers between devices: 10.4 us -> 19 us  [the longest x15 12 us: send(): lax.ppermute(parts[step], ('near', 'side'), [(i, i ^ step) for i in range...]
    unnamed x12 -> x6, local copies, waits for them, and re-layouts: 0.03 us -> 2.94 us
    reduce_sum x1 -> x0, other arithmetic: 1.92 us -> none  [inverse(): scale = lax.rsqrt(jnp.sum(matrix * matrix))]
  transfers between devices with their start and end apart: 6 -> 22, of which waited for: 4 -> 11; matrix products, arithmetic and copies ran while one was open for 6% -> 1% of each run, Pallas kernels for 0% -> 19%
where the time goes in v6:
time: 66.9 us; the launch traced here: 66.2 us
  starting transfers between devices  24.4 us (36%)
  waiting for transfers between devices  19 us (28%)
  Pallas kernels  18.2 us (27%)
  local copies, waits for them, and re-layouts  2.96 us (4%)
  other arithmetic  0.9 us (1%)
  between operations  0.82 us (1%)
    ppermute x15, starting transfers between devices, send(): lax.ppermute(parts[step], ('near', 'side'), [(i, i ^ step) for i in range...  18.4 us
    ppermute x15, waiting for transfers between devices, send(): lax.ppermute(parts[step], ('near', 'side'), [(i, i ^ step) for i in range...  12 us
    pallas_call x2, Pallas kernels, inverse(): call(functools.partial(inverse_kernel, count), 20 * width ** 3, [array(wi...  8.73 us
    ppermute x2, waiting for transfers between devices, exchange(): got = lax.ppermute(value, 'far', route)  5.75 us
    ppermute x2, starting transfers between devices, exchange(): got = lax.ppermute(value, 'far', route)  3.52 us
    pallas_call x1, Pallas kernels, body(): call(update_kernel, 10 * width ** 3, array(width, width, dtype=F32), [SME...  3.19 us
    unnamed x6, local copies, waits for them, and re-layouts  2.94 us
  transfers between devices with their start and end apart: 22, of which 11 were waited for; matrix products, arithmetic and copies ran while one was open for 1% of the time, Pallas kernels for 19%

profile of v6, /device:TPU:0, one launch (start us, length us, event | category | flops | bytes accessed | tf_op | source)
XLA Modules:
  0.0 66.2 jit_solution(1668554694356972186)
XLA Ops:
  0.6 0.5 collective-permute-start
  1.1 0.1 collective-permute-start.1
  1.2 0.1 pad_add_fusion.where
  1.3 0.0 copy-start
  1.3 1.0 %copy-done = bf16[1,512,512]{2,1,0:T(8,128)(2,1)S(1)} copy-done((bf16[1,512,512]{2,1,0:T(8,128)(2,1)S(1)}, bf16[1,512,512]{2,1,0:T(8,128)(2,1)}, u32[]{:S(2)}) %copy-start) | copy-done | bytes 524312
  2.3 0.0 copy-start.1
  2.3 0.9 %copy-done.1 = bf16[2,128,512]{2,1,0:T(8,128)(2,1)S(1)} copy-done((bf16[2,128,512]{2,1,0:T(8,128)(2,1)S(1)}, bf16[2,128,512]{2,1,0:T(8,128)(2,1)}, u32[]{:S(2)}) %copy-start.1) | copy-done | bytes 262168
  3.3 0.0 copy-start.2
  3.3 0.9 %copy-done.2 = bf16[1,2,128,512]{3,2,1,0:T(8,128)(2,1)S(1)} copy-done((bf16[1,2,128,512]{3,2,1,0:T(8,128)(2,1)S(1)}, bf16[1,2,128,512]{3,2,1,0:T(8,128)(2,1)}, u32[]{:S(2)}) %copy-start.2) | copy-done | bytes 262168
  4.2 1.1 %shard_map.50 = (bf16[512,512]{1,0:T(8,128)(2,1)S(1)}, bf16[2,128,512]{2,1,0:T(8,128)(2,1)S(1)}, f32[128,512]{1,0:T(8,128)S(1)}, bf16[128,512]{1,0:T(8,128)(2,1)S(1)}) custom-call(s32[3]{0:T(128)S(1)} %pad_add_fusion.where, bf16[512,512]{1,0:T(8,128)(2,1)S(1)} %bitcast.13, bf16[2,128,512]{2,1,0:T(8,128)(2,1)S(1)} %bitcast.15, bf16[2,128,512]{2,1,0:T(8,128)(2,1)S(1)} %copy-done.1), custom_call_target="tpu_custom_call" | custom-call | flops 67108864 | bytes 1048576 | tf_op jit(solution)/shard_map/pallas_call | solution.py:273
  5.3 0.0 collective-permute-done.1.local
  5.3 0.0 collective-permute-done.partner
  5.3 1.3 %shard_map.51 = (f32[128,512]{1,0:T(8,128)S(1)}, bf16[128,512]{1,0:T(8,128)(2,1)S(1)}) custom-call(s32[3]{0:T(128)S(1)} %pad_add_fusion.where, bf16[512,512]{1,0:T(8,128)(2,1)S(1)} %get-tuple-element.26.own, bf16[512,512]{1,0:T(8,128)(2,1)S(1)} %collective-permute-done.partner, f32[128,512]{1,0:T(8,128)S(1)} %get-tuple-element.27.slope_own, ...), custom_call_target="tpu_custom_call" | custom-call | flops 201326592 | bytes 1048576 | tf_op jit(solution)/shard_map/pallas_call | solution.py:280
  6.7 1.3 %collective-permute-start.2 = (bf16[128,512]{1,0:T(8,128)(2,1)S(1)}, bf16[128,512]{1,0:T(8,128)(2,1)S(1)}, u32[]{:S(2)}, u32[]{:S(2)}) collective-permute-start(bf16[128,512]{1,0:T(8,128)(2,1)S(1)} %get-tuple-element.30.after), channel_id=1, source_target_pairs={{16,0},{17,1},{18,2},{19,3},{20,4},{21,5},{22,6},{23,7},{24,8},{25... | collective-permute-start | bytes 393224 | tf_op jit(solution)/shard_map/ppermute | solution.py:285
  8.0 0.9 %shard_map.53 = (bf16[64,640]{1,0:T(8,128)(2,1)S(1)}, bf16[64,640]{1,0:T(8,128)(2,1)S(1)}, bf16[64,640]{1,0:T(8,128)(2,1)S(1)}, bf16[64,640]{1,0:T(8,128)(2,1)S(1)}) custom-call(s32[3]{0:T(128)S(1)} %pad_add_fusion.where, bf16[2,128,512]{2,1,0:T(8,128)(2,1)S(1)} %get-tuple-element.33.local, bf16[128,512]{1,0:T(8,128)(2,1)S(1)} %get-tuple-element.30.after), custom_call_target="tpu_custom_call" | custom-call | flops 134217728 | bytes 1048576 | tf_op jit(solution)/shard_map/pallas_call | solution.py:293
  8.9 3.0 %collective-permute-start.3 = (bf16[64,640]{1,0:T(8,128)(2,1)S(1)}, bf16[64,640]{1,0:T(8,128)(2,1)S(1)}, u32[]{:S(2)}, u32[]{:S(2)}) collective-permute-start(bf16[64,640]{1,0:T(8,128)(2,1)S(1)} %get-tuple-element.35), channel_id=1, source_target_pairs={{0,1},{1,0},{2,3},{3,2},{4,5},{5,4},{6,7},{7,6},{8,9},{9,8},{10,11... | collective-permute-start | bytes 245768 | tf_op jit(solution)/shard_map/ppermute | solution.py:233
  11.9 1.6 %collective-permute-start.4 = (bf16[64,640]{1,0:T(8,128)(2,1)S(1)}, bf16[64,640]{1,0:T(8,128)(2,1)S(1)}, u32[]{:S(2)}, u32[]{:S(2)}) collective-permute-start(bf16[64,640]{1,0:T(8,128)(2,1)S(1)} %get-tuple-element.36), channel_id=1, source_target_pairs={{0,2},{1,3},{2,0},{3,1},{4,6},{5,7},{6,4},{7,5},{8,10},{9,11},{10,... | collective-permute-start | bytes 245768 | tf_op jit(solution)/shard_map/ppermute | solution.py:233
  13.4 0.0 collective-permute-start.5
  13.4 1.2 %collective-permute-done.2.arrived = bf16[128,512]{1,0:T(8,128)(2,1)S(1)} collective-permute-done((bf16[128,512]{1,0:T(8,128)(2,1)S(1)}, bf16[128,512]{1,0:T(8,128)(2,1)S(1)}, u32[]{:S(2)}, u32[]{:S(2)}) %collective-permute-start.2) | collective-permute-done | bytes 131104 | tf_op jit(solution)/shard_map/ppermute | solution.py:285
  14.6 0.9 %shard_map.52 = (bf16[128,512]{1,0:T(8,128)(2,1)S(1)}, bf16[128,512]{1,0:T(8,128)(2,1)S(1)}) custom-call(s32[3]{0:T(128)S(1)} %pad_add_fusion.where, bf16[512,512]{1,0:T(8,128)(2,1)S(1)} %get-tuple-element.26.own, bf16[512,512]{1,0:T(8,128)(2,1)S(1)} %collective-permute-done.partner, f32[128,512]{1,0:T(8,128)S(1)} %get-tuple-element.27.slope_own, ...), custom_call_target="tpu_custom_call" | custom-call | flops 2147483648 | bytes 1048576 | tf_op jit(solution)/shard_map/pallas_call | solution.py:302
  15.5 0.0 collective-permute-done.3.refs_1_
  15.5 1.6 %collective-permute-done.4.refs_2_ = bf16[64,640]{1,0:T(8,128)(2,1)S(1)} collective-permute-done((bf16[64,640]{1,0:T(8,128)(2,1)S(1)}, bf16[64,640]{1,0:T(8,128)(2,1)S(1)}, u32[]{:S(2)}, u32[]{:S(2)}) %collective-permute-start.4) | collective-permute-done | bytes 81952 | tf_op jit(solution)/shard_map/ppermute | solution.py:233
  17.1 1.7 %collective-permute-done.5.refs_3_ = bf16[64,640]{1,0:T(8,128)(2,1)S(1)} collective-permute-done((bf16[64,640]{1,0:T(8,128)(2,1)S(1)}, bf16[64,640]{1,0:T(8,128)(2,1)S(1)}, u32[]{:S(2)}, u32[]{:S(2)}) %collective-permute-start.5) | collective-permute-done | bytes 81952 | tf_op jit(solution)/shard_map/ppermute | solution.py:233
  18.8 0.9 %shard_map.55 = (bf16[128,512]{1,0:T(8,128)(2,1)S(1)}, bf16[128,512]{1,0:T(8,128)(2,1)S(1)}, bf16[128,512]{1,0:T(8,128)(2,1)S(1)}, bf16[128,512]{1,0:T(8,128)(2,1)S(1)}) custom-call(s32[3]{0:T(128)S(1)} %pad_add_fusion.where, bf16[512,512]{1,0:T(8,128)(2,1)S(1)} %get-tuple-element.26.own, bf16[512,512]{1,0:T(8,128)(2,1)S(1)} %collective-permute-done.partner, ...), custom_call_target="tpu_custom_call" | custom-call | flops 134217728 | bytes 1048576 | tf_op jit(solution)/shard_map/pallas_call | solution.py:306
  19.7 0.1 collective-permute-start.8
  19.8 0.5 collective-permute-start.6
  20.3 2.6 %collective-permute-start.7 = (bf16[64,640]{1,0:T(8,128)(2,1)S(1)}, bf16[64,640]{1,0:T(8,128)(2,1)S(1)}, u32[]{:S(2)}, u32[]{:S(2)}) collective-permute-start(bf16[64,640]{1,0:T(8,128)(2,1)S(1)} %shard_map.54.after.left), channel_id=1, source_target_pairs={{0,4},{4,0},{1,5},{5,1},{2,6},{6,2},{3,7},{7,3},{8,12},{12,8},{9,1... | collective-permute-start | bytes 245768 | tf_op jit(solution)/shard_map/ppermute | solution.py:241
  22.9 0.0 collective-permute-done.8.dh_got
  22.9 1.1 %shard_map.56 = (bf16[64,1664]{1,0:T(8,128)(2,1)S(1)}, bf16[64,1664]{1,0:T(8,128)(2,1)S(1)}, bf16[64,1664]{1,0:T(8,128)(2,1)S(1)}, bf16[64,1664]{1,0:T(8,128)(2,1)S(1)}) custom-call(s32[3]{0:T(128)S(1)} %pad_add_fusion.where, bf16[2,128,512]{2,1,0:T(8,128)(2,1)S(1)} %get-tuple-element.33.local, bf16[128,512]{1,0:T(8,128)(2,1)S(1)} %get-tuple-element.40.dh_own, ...), custom_call_target="tpu_custom_call" | custom-call | flops 268435456 | bytes 1048576 | tf_op jit(solution)/shard_map/pallas_call | solution.py:313
  24.0 1.5 %collective-permute-start.9 = (bf16[64,1664]{1,0:T(8,128)(2,1)S(1)}, bf16[64,1664]{1,0:T(8,128)(2,1)S(1)}, u32[]{:S(2)}, u32[]{:S(2)}) collective-permute-start(bf16[64,1664]{1,0:T(8,128)(2,1)S(1)} %get-tuple-element.43), channel_id=1, source_target_pairs={{0,3},{1,2},{2,1},{3,0},{4,7},{5,6},{6,5},{7,4},{8,11},{9,10},{10,... | collective-permute-start | bytes 638984 | tf_op jit(solution)/shard_map/ppermute | solution.py:233
  25.5 0.7 %collective-permute-start.13 = (bf16[64,1664]{1,0:T(8,128)(2,1)S(1)}, bf16[64,1664]{1,0:T(8,128)(2,1)S(1)}, u32[]{:S(2)}, u32[]{:S(2)}) collective-permute-start(bf16[64,1664]{1,0:T(8,128)(2,1)S(1)} %get-tuple-element.46), channel_id=1, source_target_pairs={{0,1},{1,0},{2,3},{3,2},{4,5},{5,4},{6,7},{7,6},{8,9},{9,8},{10,11... | collective-permute-start | bytes 638984 | tf_op jit(solution)/shard_map/ppermute | solution.py:233
  26.2 1.3 %collective-permute-start.14 = (bf16[64,1664]{1,0:T(8,128)(2,1)S(1)}, bf16[64,1664]{1,0:T(8,128)(2,1)S(1)}, u32[]{:S(2)}, u32[]{:S(2)}) collective-permute-start(bf16[64,1664]{1,0:T(8,128)(2,1)S(1)} %get-tuple-element.47), channel_id=1, source_target_pairs={{0,2},{1,3},{2,0},{3,1},{4,6},{5,7},{6,4},{7,5},{8,10},{9,11},{10,... | collective-permute-start | bytes 638984 | tf_op jit(solution)/shard_map/ppermute | solution.py:233
  27.5 0.0 collective-permute-done.6
  27.5 5.6 %collective-permute-done.9.right = bf16[64,1664]{1,0:T(8,128)(2,1)S(1)} collective-permute-done((bf16[64,1664]{1,0:T(8,128)(2,1)S(1)}, bf16[64,1664]{1,0:T(8,128)(2,1)S(1)}, u32[]{:S(2)}, u32[]{:S(2)}) %collective-permute-start.9) | collective-permute-done | bytes 213024 | tf_op jit(solution)/shard_map/ppermute | solution.py:233
  33.2 0.0 collective-permute-done.7.right
  33.2 1.5 %collective-permute-start.12 = (bf16[64,640]{1,0:T(8,128)(2,1)S(1)}, bf16[64,640]{1,0:T(8,128)(2,1)S(1)}, u32[]{:S(2)}, u32[]{:S(2)}) collective-permute-start(bf16[64,640]{1,0:T(8,128)(2,1)S(1)} %shard_map.58.refs_0_), channel_id=1, source_target_pairs={{0,3},{1,2},{2,1},{3,0},{4,7},{5,6},{6,5},{7,4},{8,11},{9,10},{10,... | collective-permute-start | bytes 245768 | tf_op jit(solution)/shard_map/ppermute | solution.py:233
  34.7 0.7 %collective-permute-start.11 = (bf16[64,640]{1,0:T(8,128)(2,1)S(1)}, bf16[64,640]{1,0:T(8,128)(2,1)S(1)}, u32[]{:S(2)}, u32[]{:S(2)}) collective-permute-start(bf16[64,640]{1,0:T(8,128)(2,1)S(1)} %shard_map.58.refs_0_), channel_id=1, source_target_pairs={{0,2},{1,3},{2,0},{3,1},{4,6},{5,7},{6,4},{7,5},{8,10},{9,11},{10,... | collective-permute-start | bytes 245768 | tf_op jit(solution)/shard_map/ppermute | solution.py:233
  35.5 1.3 %collective-permute-start.10 = (bf16[64,640]{1,0:T(8,128)(2,1)S(1)}, bf16[64,640]{1,0:T(8,128)(2,1)S(1)}, u32[]{:S(2)}, u32[]{:S(2)}) collective-permute-start(bf16[64,640]{1,0:T(8,128)(2,1)S(1)} %shard_map.58.refs_0_), channel_id=1, source_target_pairs={{0,1},{1,0},{2,3},{3,2},{4,5},{5,4},{6,7},{7,6},{8,9},{9,8},{10,11... | collective-permute-start | bytes 245768 | tf_op jit(solution)/shard_map/ppermute | solution.py:233
  36.8 0.9 %collective-permute-done.13 = bf16[64,1664]{1,0:T(8,128)(2,1)S(1)} collective-permute-done((bf16[64,1664]{1,0:T(8,128)(2,1)S(1)}, bf16[64,1664]{1,0:T(8,128)(2,1)S(1)}, u32[]{:S(2)}, u32[]{:S(2)}) %collective-permute-start.13) | collective-permute-done | bytes 213024 | tf_op jit(solution)/shard_map/ppermute | solution.py:233
  37.7 0.0 collective-permute-done.14
  37.7 0.1 add_convert_fusion.left
  37.7 0.9 %collective-permute-start.15 = (bf16[64,1664]{1,0:T(8,128)(2,1)S(1)}, bf16[64,1664]{1,0:T(8,128)(2,1)S(1)}, u32[]{:S(2)}, u32[]{:S(2)}) collective-permute-start(bf16[64,1664]{1,0:T(8,128)(2,1)S(1)} %add_convert_fusion.left), channel_id=1, source_target_pairs={{0,4},{4,0},{1,5},{5,1},{2,6},{6,2},{3,7},{7,3},{8,12},{12,8},{9,1... | collective-permute-start | bytes 638984 | tf_op jit(solution)/shard_map/ppermute | solution.py:241
  38.7 0.8 %collective-permute-done.12.refs_3_ = bf16[64,640]{1,0:T(8,128)(2,1)S(1)} collective-permute-done((bf16[64,640]{1,0:T(8,128)(2,1)S(1)}, bf16[64,640]{1,0:T(8,128)(2,1)S(1)}, u32[]{:S(2)}, u32[]{:S(2)}) %collective-permute-start.12) | collective-permute-done | bytes 81952 | tf_op jit(solution)/shard_map/ppermute | solution.py:233
  39.5 0.6 collective-permute-done.11.refs_2_
  40.1 0.1 collective-permute-done.10.refs_1_
  40.2 4.4 %shard_map.59 = (bf16[512,512]{1,0:T(8,128)(2,1)S(1)}, bf16[512,512]{1,0:T(8,128)(2,1)S(1)}) custom-call(s32[3]{0:T(128)S(1)} %pad_add_fusion.where, bf16[64,640]{1,0:T(8,128)(2,1)S(1)} %shard_map.58.refs_0_, bf16[64,640]{1,0:T(8,128)(2,1)S(1)} %collective-permute-done.10.refs_1_, bf16[64,640]{1,0:T(8,128)(2,1)S(1)} %collective-permute-done.11.refs_2_, ...), custom_call_target="tpu_custom_call" | custom-call | flops 2684354560 | bytes 1048576 | tf_op jit(solution)/shard_map/pallas_call | solution.py:328
  44.6 5.8 %collective-permute-done.15.right = bf16[64,1664]{1,0:T(8,128)(2,1)S(1)} collective-permute-done((bf16[64,1664]{1,0:T(8,128)(2,1)S(1)}, bf16[64,1664]{1,0:T(8,128)(2,1)S(1)}, u32[]{:S(2)}, u32[]{:S(2)}) %collective-permute-start.15) | collective-permute-done | bytes 213024 | tf_op jit(solution)/shard_map/ppermute | solution.py:241
  50.3 0.1 shard_map.60
  50.4 0.1 collective-permute-start.18
  50.5 0.8 %collective-permute-start.17 = (bf16[64,640]{1,0:T(8,128)(2,1)S(1)}, bf16[64,640]{1,0:T(8,128)(2,1)S(1)}, u32[]{:S(2)}, u32[]{:S(2)}) collective-permute-start(bf16[64,640]{1,0:T(8,128)(2,1)S(1)} %slice.8.refs_0_), channel_id=1, source_target_pairs={{0,2},{1,3},{2,0},{3,1},{4,6},{5,7},{6,4},{7,5},{8,10},{9,11},{10,... | collective-permute-start | bytes 245768 | tf_op jit(solution)/shard_map/ppermute | solution.py:233
  51.3 2.6 %collective-permute-start.16 = (bf16[64,640]{1,0:T(8,128)(2,1)S(1)}, bf16[64,640]{1,0:T(8,128)(2,1)S(1)}, u32[]{:S(2)}, u32[]{:S(2)}) collective-permute-start(bf16[64,640]{1,0:T(8,128)(2,1)S(1)} %slice.8.refs_0_), channel_id=1, source_target_pairs={{0,1},{1,0},{2,3},{3,2},{4,5},{5,4},{6,7},{7,6},{8,9},{9,8},{10,11... | collective-permute-start | bytes 245768 | tf_op jit(solution)/shard_map/ppermute | solution.py:233
  53.9 0.7 %maximum_bitcast_fusion = bf16[1,2,128,512]{3,2,1,0:T(8,128)(2,1)} fusion(bf16[1,128,512]{2,1,0:T(8,128)(2,1)S(1)} %get-tuple-element.51, bf16[1,128,512]{2,1,0:T(8,128)(2,1)S(1)} %get-tuple-element.50), kind=kLoop, calls=%fused_computation.1 | loop fusion | flops 131072 | bytes 524288 | tf_op jit(solution)/shard_map/broadcast_in_dim | solution.py:347
  54.7 0.1 collective-permute-start.21
  54.8 1.4 %collective-permute-start.20 = (bf16[64,1024]{1,0:T(8,128)(2,1)S(1)}, bf16[64,1024]{1,0:T(8,128)(2,1)S(1)}, u32[]{:S(2)}, u32[]{:S(2)}) collective-permute-start(bf16[64,1024]{1,0:T(8,128)(2,1)S(1)} %slice.9.refs_0_), channel_id=1, source_target_pairs={{0,2},{1,3},{2,0},{3,1},{4,6},{5,7},{6,4},{7,5},{8,10},{9,11},{10,... | collective-permute-start | bytes 393224 | tf_op jit(solution)/shard_map/ppermute | solution.py:233
  56.2 0.3 collective-permute-done.18.refs_3_
  56.6 1.7 %collective-permute-start.19 = (bf16[64,1024]{1,0:T(8,128)(2,1)S(1)}, bf16[64,1024]{1,0:T(8,128)(2,1)S(1)}, u32[]{:S(2)}, u32[]{:S(2)}) collective-permute-start(bf16[64,1024]{1,0:T(8,128)(2,1)S(1)} %slice.9.refs_0_), channel_id=1, source_target_pairs={{0,1},{1,0},{2,3},{3,2},{4,5},{5,4},{6,7},{7,6},{8,9},{9,8},{10,11... | collective-permute-start | bytes 393224 | tf_op jit(solution)/shard_map/ppermute | solution.py:233
  58.2 0.0 collective-permute-done.17.refs_2_
  58.2 0.0 collective-permute-done.16.refs_1_
  58.2 4.4 %shard_map.61 = (bf16[512,512]{1,0:T(8,128)(2,1)S(1)}, bf16[512,512]{1,0:T(8,128)(2,1)S(1)}) custom-call(s32[3]{0:T(128)S(1)} %pad_add_fusion.where, bf16[64,640]{1,0:T(8,128)(2,1)S(1)} %slice.8.refs_0_, bf16[64,640]{1,0:T(8,128)(2,1)S(1)} %collective-permute-done.16.refs_1_, bf16[64,640]{1,0:T(8,128)(2,1)S(1)} %collective-permute-done.17.refs_2_, ...), custom_call_target="tpu_custom_call" | custom-call | flops 2684354560 | bytes 1048576 | tf_op jit(solution)/shard_map/pallas_call | solution.py:328
  62.6 0.0 collective-permute-done.21.refs_3_
  62.6 0.0 collective-permute-done.20.refs_2_
  62.6 0.4 collective-permute-done.19.refs_1_
  63.0 3.2 %shard_map.62 = f32[512,512]{1,0:T(8,128)} custom-call(s32[3]{0:T(128)S(1)} %pad_add_fusion.where, bf16[512,512]{1,0:T(8,128)(2,1)S(1)} %get-tuple-element.44.after.act_high, bf16[512,512]{1,0:T(8,128)(2,1)S(1)} %get-tuple-element.45.act_low, bf16[512,512]{1,0:T(8,128)(2,1)S(1)} %get-tuple-element.48.out_high, ...), custom_call_target="tpu_custom_call" | custom-call | flops 1342177280 | bytes 1048576 | tf_op jit(solution)/shard_map/pallas_call | solution.py:340
  (6 shorter events, 0.2 us)
Async XLA Ops:
  0.6 4.7 %collective-permute-start = (bf16[512,512]{1,0:T(8,128)(2,1)}, bf16[512,512]{1,0:T(8,128)(2,1)S(1)}, u32[]{:S(2)}, u32[]{:S(2)}) collective-permute-start(bf16[512,512]{1,0:T(8,128)(2,1)} %bitcast.12), channel_id=1, source_target_pairs={{0,8},{8,0},{1,9},{9,1},{2,10},{10,2},{3,11},{11,3},{4,12},{12,4},... | collective-permute-start | bytes 1572872 | tf_op jit(solution)/shard_map/ppermute | solution.py:269
  1.1 4.2 %collective-permute-start.1 = (bf16[2,128,512]{2,1,0:T(8,128)(2,1)}, bf16[2,128,512]{2,1,0:T(8,128)(2,1)S(1)}, u32[]{:S(2)}, u32[]{:S(2)}) collective-permute-start(bf16[2,128,512]{2,1,0:T(8,128)(2,1)} %bitcast.14), channel_id=1, source_target_pairs={{0,8},{8,0},{1,9},{9,1},{2,10},{10,2},{3,11},{11,3},{4,12},{12,4},... | collective-permute-start | bytes 786440 | tf_op jit(solution)/shard_map/ppermute | solution.py:270
  1.3 1.0 %copy-start = (bf16[1,512,512]{2,1,0:T(8,128)(2,1)S(1)}, bf16[1,512,512]{2,1,0:T(8,128)(2,1)}, u32[]{:S(2)}) copy-start(bf16[1,512,512]{2,1,0:T(8,128)(2,1)} %param.4) | copy-start | bytes 1572868
  2.3 0.9 %copy-start.1 = (bf16[2,128,512]{2,1,0:T(8,128)(2,1)S(1)}, bf16[2,128,512]{2,1,0:T(8,128)(2,1)}, u32[]{:S(2)}) copy-start(bf16[2,128,512]{2,1,0:T(8,128)(2,1)} %cot_last.1) | copy-start | bytes 786436
  3.3 0.9 %copy-start.2 = (bf16[1,2,128,512]{3,2,1,0:T(8,128)(2,1)S(1)}, bf16[1,2,128,512]{3,2,1,0:T(8,128)(2,1)}, u32[]{:S(2)}) copy-start(bf16[1,2,128,512]{3,2,1,0:T(8,128)(2,1)} %param.3) | copy-start | bytes 786436
  6.7 8.0 %collective-permute-start.2 = (bf16[128,512]{1,0:T(8,128)(2,1)S(1)}, bf16[128,512]{1,0:T(8,128)(2,1)S(1)}, u32[]{:S(2)}, u32[]{:S(2)}) collective-permute-start(bf16[128,512]{1,0:T(8,128)(2,1)S(1)} %get-tuple-element.30.after), channel_id=1, source_target_pairs={{16,0},{17,1},{18,2},{19,3},{20,4},{21,5},{22,6},{23,7},{24,8},{25... | collective-permute-start | bytes 393224 | tf_op jit(solution)/shard_map/ppermute | solution.py:285
  8.9 6.6 %collective-permute-start.3 = (bf16[64,640]{1,0:T(8,128)(2,1)S(1)}, bf16[64,640]{1,0:T(8,128)(2,1)S(1)}, u32[]{:S(2)}, u32[]{:S(2)}) collective-permute-start(bf16[64,640]{1,0:T(8,128)(2,1)S(1)} %get-tuple-element.35), channel_id=1, source_target_pairs={{0,1},{1,0},{2,3},{3,2},{4,5},{5,4},{6,7},{7,6},{8,9},{9,8},{10,11... | collective-permute-start | bytes 245768 | tf_op jit(solution)/shard_map/ppermute | solution.py:233
  11.9 5.2 %collective-permute-start.4 = (bf16[64,640]{1,0:T(8,128)(2,1)S(1)}, bf16[64,640]{1,0:T(8,128)(2,1)S(1)}, u32[]{:S(2)}, u32[]{:S(2)}) collective-permute-start(bf16[64,640]{1,0:T(8,128)(2,1)S(1)} %get-tuple-element.36), channel_id=1, source_target_pairs={{0,2},{1,3},{2,0},{3,1},{4,6},{5,7},{6,4},{7,5},{8,10},{9,11},{10,... | collective-permute-start | bytes 245768 | tf_op jit(solution)/shard_map/ppermute | solution.py:233
  13.4 5.3 %collective-permute-start.5 = (bf16[64,640]{1,0:T(8,128)(2,1)S(1)}, bf16[64,640]{1,0:T(8,128)(2,1)S(1)}, u32[]{:S(2)}, u32[]{:S(2)}) collective-permute-start(bf16[64,640]{1,0:T(8,128)(2,1)S(1)} %get-tuple-element.37), channel_id=1, source_target_pairs={{0,3},{1,2},{2,1},{3,0},{4,7},{5,6},{6,5},{7,4},{8,11},{9,10},{10,... | collective-permute-start | bytes 245768 | tf_op jit(solution)/shard_map/ppermute | solution.py:233
  19.7 3.2 %collective-permute-start.8 = (bf16[128,512]{1,0:T(8,128)(2,1)S(1)}, bf16[128,512]{1,0:T(8,128)(2,1)S(1)}, u32[]{:S(2)}, u32[]{:S(2)}) collective-permute-start(bf16[128,512]{1,0:T(8,128)(2,1)S(1)} %get-tuple-element.41), channel_id=1, source_target_pairs={{0,8},{8,0},{1,9},{9,1},{2,10},{10,2},{3,11},{11,3},{4,12},{12,4},... | collective-permute-start | bytes 393224 | tf_op jit(solution)/shard_map/ppermute | solution.py:309
  19.8 7.7 %collective-permute-start.6 = (bf16[128,512]{1,0:T(8,128)(2,1)S(1)}, bf16[128,512]{1,0:T(8,128)(2,1)S(1)}, u32[]{:S(2)}, u32[]{:S(2)}) collective-permute-start(bf16[128,512]{1,0:T(8,128)(2,1)S(1)} %get-tuple-element.38), channel_id=1, source_target_pairs={{0,8},{8,0},{1,9},{9,1},{2,10},{10,2},{3,11},{11,3},{4,12},{12,4},... | collective-permute-start | bytes 393224 | tf_op jit(solution)/shard_map/ppermute | solution.py:310
  20.3 12.9 %collective-permute-start.7 = (bf16[64,640]{1,0:T(8,128)(2,1)S(1)}, bf16[64,640]{1,0:T(8,128)(2,1)S(1)}, u32[]{:S(2)}, u32[]{:S(2)}) collective-permute-start(bf16[64,640]{1,0:T(8,128)(2,1)S(1)} %shard_map.54.after.left), channel_id=1, source_target_pairs={{0,4},{4,0},{1,5},{5,1},{2,6},{6,2},{3,7},{7,3},{8,12},{12,8},{9,1... | collective-permute-start | bytes 245768 | tf_op jit(solution)/shard_map/ppermute | solution.py:241
  24.0 9.2 %collective-permute-start.9 = (bf16[64,1664]{1,0:T(8,128)(2,1)S(1)}, bf16[64,1664]{1,0:T(8,128)(2,1)S(1)}, u32[]{:S(2)}, u32[]{:S(2)}) collective-permute-start(bf16[64,1664]{1,0:T(8,128)(2,1)S(1)} %get-tuple-element.43), channel_id=1, source_target_pairs={{0,3},{1,2},{2,1},{3,0},{4,7},{5,6},{6,5},{7,4},{8,11},{9,10},{10,... | collective-permute-start | bytes 638984 | tf_op jit(solution)/shard_map/ppermute | solution.py:233
  25.5 12.2 %collective-permute-start.13 = (bf16[64,1664]{1,0:T(8,128)(2,1)S(1)}, bf16[64,1664]{1,0:T(8,128)(2,1)S(1)}, u32[]{:S(2)}, u32[]{:S(2)}) collective-permute-start(bf16[64,1664]{1,0:T(8,128)(2,1)S(1)} %get-tuple-element.46), channel_id=1, source_target_pairs={{0,1},{1,0},{2,3},{3,2},{4,5},{5,4},{6,7},{7,6},{8,9},{9,8},{10,11... | collective-permute-start | bytes 638984 | tf_op jit(solution)/shard_map/ppermute | solution.py:233
  26.2 11.4 %collective-permute-start.14 = (bf16[64,1664]{1,0:T(8,128)(2,1)S(1)}, bf16[64,1664]{1,0:T(8,128)(2,1)S(1)}, u32[]{:S(2)}, u32[]{:S(2)}) collective-permute-start(bf16[64,1664]{1,0:T(8,128)(2,1)S(1)} %get-tuple-element.47), channel_id=1, source_target_pairs={{0,2},{1,3},{2,0},{3,1},{4,6},{5,7},{6,4},{7,5},{8,10},{9,11},{10,... | collective-permute-start | bytes 638984 | tf_op jit(solution)/shard_map/ppermute | solution.py:233
  33.2 6.3 %collective-permute-start.12 = (bf16[64,640]{1,0:T(8,128)(2,1)S(1)}, bf16[64,640]{1,0:T(8,128)(2,1)S(1)}, u32[]{:S(2)}, u32[]{:S(2)}) collective-permute-start(bf16[64,640]{1,0:T(8,128)(2,1)S(1)} %shard_map.58.refs_0_), channel_id=1, source_target_pairs={{0,3},{1,2},{2,1},{3,0},{4,7},{5,6},{6,5},{7,4},{8,11},{9,10},{10,... | collective-permute-start | bytes 245768 | tf_op jit(solution)/shard_map/ppermute | solution.py:233
  34.7 5.3 %collective-permute-start.11 = (bf16[64,640]{1,0:T(8,128)(2,1)S(1)}, bf16[64,640]{1,0:T(8,128)(2,1)S(1)}, u32[]{:S(2)}, u32[]{:S(2)}) collective-permute-start(bf16[64,640]{1,0:T(8,128)(2,1)S(1)} %shard_map.58.refs_0_), channel_id=1, source_target_pairs={{0,2},{1,3},{2,0},{3,1},{4,6},{5,7},{6,4},{7,5},{8,10},{9,11},{10,... | collective-permute-start | bytes 245768 | tf_op jit(solution)/shard_map/ppermute | solution.py:233
  35.5 4.7 %collective-permute-start.10 = (bf16[64,640]{1,0:T(8,128)(2,1)S(1)}, bf16[64,640]{1,0:T(8,128)(2,1)S(1)}, u32[]{:S(2)}, u32[]{:S(2)}) collective-permute-start(bf16[64,640]{1,0:T(8,128)(2,1)S(1)} %shard_map.58.refs_0_), channel_id=1, source_target_pairs={{0,1},{1,0},{2,3},{3,2},{4,5},{5,4},{6,7},{7,6},{8,9},{9,8},{10,11... | collective-permute-start | bytes 245768 | tf_op jit(solution)/shard_map/ppermute | solution.py:233
  37.7 12.6 %collective-permute-start.15 = (bf16[64,1664]{1,0:T(8,128)(2,1)S(1)}, bf16[64,1664]{1,0:T(8,128)(2,1)S(1)}, u32[]{:S(2)}, u32[]{:S(2)}) collective-permute-start(bf16[64,1664]{1,0:T(8,128)(2,1)S(1)} %add_convert_fusion.left), channel_id=1, source_target_pairs={{0,4},{4,0},{1,5},{5,1},{2,6},{6,2},{3,7},{7,3},{8,12},{12,8},{9,1... | collective-permute-start | bytes 638984 | tf_op jit(solution)/shard_map/ppermute | solution.py:241
  50.4 6.2 %collective-permute-start.18 = (bf16[64,640]{1,0:T(8,128)(2,1)S(1)}, bf16[64,640]{1,0:T(8,128)(2,1)S(1)}, u32[]{:S(2)}, u32[]{:S(2)}) collective-permute-start(bf16[64,640]{1,0:T(8,128)(2,1)S(1)} %slice.8.refs_0_), channel_id=1, source_target_pairs={{0,3},{1,2},{2,1},{3,0},{4,7},{5,6},{6,5},{7,4},{8,11},{9,10},{10,... | collective-permute-start | bytes 245768 | tf_op jit(solution)/shard_map/ppermute | solution.py:233
  50.5 7.8 %collective-permute-start.17 = (bf16[64,640]{1,0:T(8,128)(2,1)S(1)}, bf16[64,640]{1,0:T(8,128)(2,1)S(1)}, u32[]{:S(2)}, u32[]{:S(2)}) collective-permute-start(bf16[64,640]{1,0:T(8,128)(2,1)S(1)} %slice.8.refs_0_), channel_id=1, source_target_pairs={{0,2},{1,3},{2,0},{3,1},{4,6},{5,7},{6,4},{7,5},{8,10},{9,11},{10,... | collective-permute-start | bytes 245768 | tf_op jit(solution)/shard_map/ppermute | solution.py:233
  51.3 6.9 %collective-permute-start.16 = (bf16[64,640]{1,0:T(8,128)(2,1)S(1)}, bf16[64,640]{1,0:T(8,128)(2,1)S(1)}, u32[]{:S(2)}, u32[]{:S(2)}) collective-permute-start(bf16[64,640]{1,0:T(8,128)(2,1)S(1)} %slice.8.refs_0_), channel_id=1, source_target_pairs={{0,1},{1,0},{2,3},{3,2},{4,5},{5,4},{6,7},{7,6},{8,9},{9,8},{10,11... | collective-permute-start | bytes 245768 | tf_op jit(solution)/shard_map/ppermute | solution.py:233
  54.7 7.9 %collective-permute-start.21 = (bf16[64,1024]{1,0:T(8,128)(2,1)S(1)}, bf16[64,1024]{1,0:T(8,128)(2,1)S(1)}, u32[]{:S(2)}, u32[]{:S(2)}) collective-permute-start(bf16[64,1024]{1,0:T(8,128)(2,1)S(1)} %slice.9.refs_0_), channel_id=1, source_target_pairs={{0,3},{1,2},{2,1},{3,0},{4,7},{5,6},{6,5},{7,4},{8,11},{9,10},{10,... | collective-permute-start | bytes 393224 | tf_op jit(solution)/shard_map/ppermute | solution.py:233
  54.8 7.8 %collective-permute-start.20 = (bf16[64,1024]{1,0:T(8,128)(2,1)S(1)}, bf16[64,1024]{1,0:T(8,128)(2,1)S(1)}, u32[]{:S(2)}, u32[]{:S(2)}) collective-permute-start(bf16[64,1024]{1,0:T(8,128)(2,1)S(1)} %slice.9.refs_0_), channel_id=1, source_target_pairs={{0,2},{1,3},{2,0},{3,1},{4,6},{5,7},{6,4},{7,5},{8,10},{9,11},{10,... | collective-permute-start | bytes 393224 | tf_op jit(solution)/shard_map/ppermute | solution.py:233
  56.6 6.5 %collective-permute-start.19 = (bf16[64,1024]{1,0:T(8,128)(2,1)S(1)}, bf16[64,1024]{1,0:T(8,128)(2,1)S(1)}, u32[]{:S(2)}, u32[]{:S(2)}) collective-permute-start(bf16[64,1024]{1,0:T(8,128)(2,1)S(1)} %slice.9.refs_0_), channel_id=1, source_target_pairs={{0,1},{1,0},{2,3},{3,2},{4,5},{5,4},{6,7},{7,6},{8,9},{9,8},{10,11... | collective-permute-start | bytes 393224 | tf_op jit(solution)/shard_map/ppermute | solution.py:233

commit v7 on v6

--- a/solution.py
+++ b/solution.py
@@ -14,6 +14,7 @@
 SMEM = pl.BlockSpec(memory_space=pltpu.SMEM)
 VMEM = pl.BlockSpec(memory_space=pltpu.VMEM)
 ANY = pl.BlockSpec(memory_space=pl.ANY)
+HBM = pl.BlockSpec(memory_space=pltpu.HBM)
 GROUP = 4
 
 
@@ -63,12 +64,12 @@
     return total
 
 
-def call(kernel, flops, out_shape, in_specs, scratch=()):
+def call(kernel, flops, out_shape, in_specs, scratch=(), out_spec=VMEM):
     return pl.pallas_call(
         kernel,
         out_shape=jax.tree.map(lambda v: jax.ShapeDtypeStruct(v.shape, v.dtype), out_shape),
         in_specs=in_specs,
-        out_specs=jax.tree.map(lambda _: VMEM, out_shape),
+        out_specs=jax.tree.map(lambda _: out_spec, out_shape),
         scratch_shapes=list(scratch),
         cost_estimate=pl.CostEstimate(flops=flops, bytes_accessed=1 << 20, transcendentals=0),
         compiler_params=pltpu.CompilerParams(vmem_limit_bytes=32 << 20),
@@ -109,6 +110,11 @@
     by_core(where[0], run, (own, slope_own), (partner, slope_partner))
 
 
+def sum_kernel(*refs):
+    pieces, result = refs[:GROUP], refs[-1]
+    result[...] = sum(piece[...].astype(F32) for piece in pieces).astype(BF16)
+
+
 def even_kernel(
     where, own, partner, slope_own, slope_partner, dh, cot, after, own_dh, give_dh, own_cot, give_cot
 ):
@@ -119,6 +125,11 @@
     by_core(
         where[0], run, (own, slope_own, own_dh, own_cot), (partner, slope_partner, give_dh, give_cot)
     )
+
+
+def cot_kernel(where, own_cot, other_cot, result):
+    result[where[0]] = own_cot[...]
+    result[1 - where[0]] = other_cot[...]
 
 
 def put_factor(tokens, whole):
@@ -147,21 +158,17 @@
         part[...] = whole[where[1] ^ step]
 
 
-def add_kernel(left, right, after, result):
-    result[...] = (left[...].astype(F32) + right[...].astype(F32)).astype(BF16)
-
-
-def begin_kernel(left, right, result):
+def add_kernel(left, right, *refs):
+    refs[-1][...] = (left[...].astype(F32) + right[...].astype(F32)).astype(BF16)
+
+
+def begin_kernel(left, right, after, result):
     result[...] = left[...].astype(F32) + right[...].astype(F32)
 
 
-def sum_kernel(*refs):
-    pieces, result = refs[:GROUP], refs[-1]
-    result[...] = sum(piece[...].astype(F32) for piece in pieces).astype(BF16)
-
-
-def grad_kernel(where, local, dh_own, dh_got, *refs):
-    parts, (inputs, tokens, whole) = refs[:GROUP], refs[GROUP:]
+def grad_kernel(where, local, dh_own, dh_got, act_sum, *refs):
+    parts, (act_part, inputs, tokens, whole) = refs[:GROUP], refs[GROUP:]
+    act_part[...] = act_sum[...]
     rows, width = local.shape[1:]
     inputs[:rows] = local[where[0]]
     inputs[rows:] = local[1 - where[0]]
@@ -171,7 +178,7 @@
     size = width // GROUP
     half = size // 2
     for u in range(GROUP):
-        grad = moment(tokens[:, u * size:(u + 1) * size], inputs[...]).astype(BF16)
+        grad = moment(inputs[:, u * size:(u + 1) * size], tokens[...]).astype(BF16)
         whole[u, :, 5 * size:5 * size + width] = grad[:half]
         whole[u, :, 5 * size + width:] = grad[half:]
     for step, part in enumerate(parts):
@@ -187,12 +194,12 @@
     full = mean + ridge * eye
     scale = lax.rsqrt(jnp.sum(full * full, keepdims=True))
     squared = product((total[...],), (total[...],)) * (1.0 / count) ** 2 + ridge * (mean + full)
-    first = full * scale
-    second = 2.0 * first - squared * (scale * scale)
+    second = (2.0 * scale) * full - squared * (scale * scale)
     second_terms = split(second)
     last = 2.0 * (eye - second) + product(second_terms, second_terms)
     tail = 2.0 * last - product(second_terms, split(last))
-    return split((2.0 * tail - product(split(first), split(tail))) * scale)
+    inner = product((total[...],), split(tail)) * (scale * (1.0 / count))
+    return split(((2.0 - ridge * scale) * tail - inner) * scale)
 
 def inverse_kernel(count, where, *refs):
     pieces, (high, low, blocks, total) = refs[:GROUP], refs[GROUP:]
@@ -216,15 +223,22 @@
 
 
 def update_kernel(where, act_high, act_low, out_high, out_low, *refs):
-    pieces, (result, grad) = refs[:GROUP], refs[GROUP:]
+    pieces, (result, grad, update, done) = refs[:GROUP], refs[GROUP:]
     half, twice = pieces[0].shape
     width = twice // 2
     for step, piece in enumerate(pieces):
         start = pl.multiple_of((where[1] ^ step) * 2 * half, 2 * half)
         grad[pl.ds(start, half)] = piece[:, :width]
         grad[pl.ds(start + half, half)] = piece[:, width:]
-    left = product((grad[...],), (act_high[...], act_low[...]))
-    result[...] = product(split(left), (out_high[...], out_low[...]), ((0,), (0,)))
+    copies = []
+    for u in range(GROUP):
+        rows = pl.ds(u * 2 * half, 2 * half)
+        left = product((act_high[rows], act_low[rows]), (grad[...],))
+        update[rows] = product(split(left), (out_high[...], out_low[...]))
+        copies.append(pltpu.make_async_copy(update.at[rows], result.at[rows], done.at[u]))
+        copies[-1].start()
+    for copy in copies:
+        copy.wait()
 
 
 def send(parts):
@@ -242,7 +256,7 @@
         if after is None:
             value = (value.astype(F32) + got.astype(F32)).astype(BF16)
         else:
-            value = call(add_kernel, 0, value, [VMEM, VMEM, ANY])(value, got, after)
+            value = call(add_kernel, 0, value, [VMEM] * 2 + [ANY] * len(after))(value, got, *after)
         step *= 2
     return value
 
@@ -274,7 +288,7 @@
         load_kernel,
         2 * rows * width**2,
         [array(width, width), array(micro, rows, width), slope, block],
-        [SMEM] + [ANY] * 3,
+        [SMEM] + [HBM] * 3,
         [pltpu.SemaphoreType.DMA((3,))],
     )(where, weight, local, cot_last)
     slope_partner, down = call(first_kernel, 6 * rows * width**2, [slope, block], [SMEM] + [VMEM] * 5)(
@@ -302,28 +316,31 @@
     dh_odd, cot_odd = call(odd_kernel, 64 * rows * width**2, [block] * 2, [SMEM] + [VMEM] * 6)(
         where, own, partner, slope_own, slope_partner, arrived, last
     )
-    act_part = call(sum_kernel, 0, array(size // 2, factor), [VMEM] * GROUP + [ANY])(*act_pieces, cot_odd)
+    act_sum = call(sum_kernel, 0, array(size // 2, factor), [VMEM] * GROUP + [ANY])(
+        *(act_pieces[step] for step in (0, 3, 1, 2)), cot_odd
+    )
     own_dh, give_dh, own_cot, give_cot = call(
         even_kernel, 4 * rows * width**2, [block] * 4, [SMEM] + [VMEM] * 6 + [ANY]
-    )(where, own, partner, slope_own, slope_partner, dh_odd, cot_odd, act_part)
+    )(where, own, partner, slope_own, slope_partner, dh_odd, cot_odd, act_sum)
     got_dh = lax.ppermute(give_dh, "core", SWAP)
     other_cot = lax.ppermute(give_cot, "core", SWAP)
-    cot = jnp.stack([mine_of((own_cot, other_cot)), mine_of((other_cot, own_cot))])
-
-    parts = call(
+    cot = call(cot_kernel, 0, array(micro, rows, width), [SMEM, VMEM, VMEM])(where, own_cot, other_cot)
+
+    *parts, act_part = call(
         grad_kernel,
         4 * tokens * width**2,
-        [array(size // 2, factor + 2 * width)] * GROUP,
-        [SMEM] + [VMEM] * 3,
+        [array(size // 2, factor + 2 * width)] * GROUP + [array(size // 2, factor)],
+        [SMEM] + [VMEM] * 4,
         [pltpu.VMEM((tokens, width), BF16)] * 2
         + [pltpu.VMEM((GROUP, size // 2, factor + 2 * width), BF16)],
-    )(where, kept, own_dh, got_dh)
+    )(where, kept, own_dh, got_dh, act_sum)
     pieces = send(parts)
-    begun = call(
-        begin_kernel, 0, array(*parts[0].shape, dtype=F32), [VMEM] * 2
-    )(pieces[0], pieces[3])
+    begun = call(begin_kernel, 0, array(*parts[0].shape, dtype=F32), [VMEM] * 2 + [ANY])(
+        pieces[0], pieces[3], cot
+    )
     total = (begun + pieces[1].astype(F32) + pieces[2].astype(F32)).astype(BF16)
-    act = send([exchange(act_part, begun)] * GROUP)
+    act = send([exchange(act_part, (begun,))] * GROUP)
+
     def inverse(pieces):
         return call(
             functools.partial(inverse_kernel, count),
@@ -334,7 +351,7 @@
         )(where, *pieces)
 
     act_inv = inverse(act)
-    total = exchange(total, act_inv[0])
+    total = exchange(total, (act_inv[0],))
     out = send([total[:, :factor]] * GROUP)
     grad = send([total[:, factor:]] * GROUP)
     update = call(
@@ -342,7 +359,12 @@
         10 * width**3,
         array(width, width, dtype=F32),
         [SMEM] + [VMEM] * (4 + GROUP),
-        [pltpu.VMEM((width, width), BF16)],
+        [
+            pltpu.VMEM((width, width), BF16),
+            pltpu.VMEM((width, width), F32),
+            pltpu.SemaphoreType.DMA((GROUP,)),
+        ],
+        HBM,
     )(where, *act_inv, *inverse(out), *grad)
     return (cot[None], update[None])
 

time: 66.9 us -> 68.4 us (1.022)
  starting transfers between devices: 24.4 us -> 26.8 us
  waiting for transfers between devices: 19 us -> 17.5 us
  local copies, waits for them, and re-layouts: 2.96 us -> 3.91 us
  other arithmetic: 0.9 us -> 0.15 us
  Pallas kernels: 18.2 us -> 18.9 us
    ppermute x15, starting transfers between devices: 18.4 us -> 21.4 us  [send(): lax.ppermute(parts[step], ('near', 'side'), [(i, i ^ step) for i in range...]
    ppermute x2, waiting for transfers between devices: 5.75 us -> 4.14 us  [exchange(): got = lax.ppermute(value, 'far', route)]
    ppermute x1, waiting for transfers between devices: 0.01 us -> 1.33 us  [body(): got_dh = lax.ppermute(give_dh, 'core', SWAP)]
    pallas_call x3 -> x4, Pallas kernels: 0.12 us -> 1.38 us  [the longest x1 1.26 us: body(): call(cot_kernel, 0, array(micro, rows, width), [SMEM, VMEM, VMEM])]
    ppermute x15, waiting for transfers between devices: 12 us -> 10.9 us  [send(): lax.ppermute(parts[step], ('near', 'side'), [(i, i ^ step) for i in range...]
    unnamed x6 -> x8, local copies, waits for them, and re-layouts: 2.94 us -> 3.89 us
    broadcast_in_dim x1 -> x0, other arithmetic: 0.73 us -> none  [body(): return (cot[None], update[None])]
  transfers between devices with their start and end apart: 22 -> 22, of which waited for: 11 -> 12; matrix products, arithmetic and copies ran while one was open for 1% -> 0% of each run, Pallas kernels for 19% -> 18%
where the time goes in v7:
time: 68.4 us; the launch traced here: 68.1 us
  starting transfers between devices  26.8 us (39%)
  Pallas kernels  18.9 us (28%)
  waiting for transfers between devices  17.5 us (26%)
  local copies, waits for them, and re-layouts  3.91 us (6%)
  between operations  0.8 us (1%)
    ppermute x15, starting transfers between devices, send(): lax.ppermute(parts[step], ('near', 'side'), [(i, i ^ step) for i in range...  21.4 us
    ppermute x15, waiting for transfers between devices, send(): lax.ppermute(parts[step], ('near', 'side'), [(i, i ^ step) for i in range...  10.9 us
    pallas_call x2, Pallas kernels, inverse(): call(functools.partial(inverse_kernel, count), 20 * width ** 3, [array(wi...  8.06 us
    ppermute x2, waiting for transfers between devices, exchange(): got = lax.ppermute(value, 'far', route)  4.14 us
    unnamed x8, local copies, waits for them, and re-layouts  3.89 us
    ppermute x2, starting transfers between devices, exchange(): got = lax.ppermute(value, 'far', route)  3.45 us
    pallas_call x1, Pallas kernels, body(): call(update_kernel, 10 * width ** 3, array(width, width, dtype=F32), [SME...  3.33 us
  transfers between devices with their start and end apart: 22, of which 12 were waited for; matrix products, arithmetic and copies ran while one was open for 0% of the time, Pallas kernels for 18%

profile of v7, /device:TPU:0, one launch (start us, length us, event | category | flops | bytes accessed | tf_op | source)
XLA Modules:
  0.0 68.1 jit_solution(4532523688092658566)
XLA Ops:
  0.6 0.5 collective-permute-start
  1.1 0.1 collective-permute-start.1
  1.2 0.1 pad_add_fusion.where
  1.3 1.0 %copy-done.1 = bf16[1,512,512]{2,1,0:T(8,128)(2,1)S(1)} copy-done((bf16[1,512,512]{2,1,0:T(8,128)(2,1)S(1)}, bf16[1,512,512]{2,1,0:T(8,128)(2,1)}, u32[]{:S(2)}) %copy-start.1) | copy-done | bytes 524312
  2.3 0.0 copy-start.2
  2.3 0.9 %copy-done.2 = bf16[2,128,512]{2,1,0:T(8,128)(2,1)S(1)} copy-done((bf16[2,128,512]{2,1,0:T(8,128)(2,1)S(1)}, bf16[2,128,512]{2,1,0:T(8,128)(2,1)}, u32[]{:S(2)}) %copy-start.2) | copy-done | bytes 262168
  3.3 0.0 copy-start.3
  3.3 0.9 %copy-done.3 = bf16[1,2,128,512]{3,2,1,0:T(8,128)(2,1)S(1)} copy-done((bf16[1,2,128,512]{3,2,1,0:T(8,128)(2,1)S(1)}, bf16[1,2,128,512]{3,2,1,0:T(8,128)(2,1)}, u32[]{:S(2)}) %copy-start.3) | copy-done | bytes 262168
  4.2 1.1 %shard_map.50 = (bf16[512,512]{1,0:T(8,128)(2,1)S(1)}, bf16[2,128,512]{2,1,0:T(8,128)(2,1)S(1)}, f32[128,512]{1,0:T(8,128)S(1)}, bf16[128,512]{1,0:T(8,128)(2,1)S(1)}) custom-call(s32[3]{0:T(128)S(1)} %pad_add_fusion.where, bf16[512,512]{1,0:T(8,128)(2,1)S(1)} %bitcast.9, bf16[2,128,512]{2,1,0:T(8,128)(2,1)S(1)} %bitcast.11, bf16[2,128,512]{2,1,0:T(8,128)(2,1)S(1)} %copy-done.2), custom_call_target="tpu_custom_call" | custom-call | flops 67108864 | bytes 1048576 | tf_op jit(solution)/shard_map/pallas_call | solution.py:287
  5.3 0.0 collective-permute-done.1.local
  5.3 0.0 collective-permute-done.partner
  5.3 1.3 %shard_map.51 = (f32[128,512]{1,0:T(8,128)S(1)}, bf16[128,512]{1,0:T(8,128)(2,1)S(1)}) custom-call(s32[3]{0:T(128)S(1)} %pad_add_fusion.where, bf16[512,512]{1,0:T(8,128)(2,1)S(1)} %get-tuple-element.27.own, bf16[512,512]{1,0:T(8,128)(2,1)S(1)} %collective-permute-done.partner, f32[128,512]{1,0:T(8,128)S(1)} %get-tuple-element.28.slope_own, ...), custom_call_target="tpu_custom_call" | custom-call | flops 201326592 | bytes 1048576 | tf_op jit(solution)/shard_map/pallas_call | solution.py:294
  6.7 1.3 %collective-permute-start.2 = (bf16[128,512]{1,0:T(8,128)(2,1)S(1)}, bf16[128,512]{1,0:T(8,128)(2,1)S(1)}, u32[]{:S(2)}, u32[]{:S(2)}) collective-permute-start(bf16[128,512]{1,0:T(8,128)(2,1)S(1)} %get-tuple-element.31.after), channel_id=1, source_target_pairs={{16,0},{17,1},{18,2},{19,3},{20,4},{21,5},{22,6},{23,7},{24,8},{25... | collective-permute-start | bytes 393224 | tf_op jit(solution)/shard_map/ppermute | solution.py:299
  8.0 0.9 %shard_map.53 = (bf16[64,640]{1,0:T(8,128)(2,1)S(1)}, bf16[64,640]{1,0:T(8,128)(2,1)S(1)}, bf16[64,640]{1,0:T(8,128)(2,1)S(1)}, bf16[64,640]{1,0:T(8,128)(2,1)S(1)}) custom-call(s32[3]{0:T(128)S(1)} %pad_add_fusion.where, bf16[2,128,512]{2,1,0:T(8,128)(2,1)S(1)} %get-tuple-element.34.local, bf16[128,512]{1,0:T(8,128)(2,1)S(1)} %get-tuple-element.31.after), custom_call_target="tpu_custom_call" | custom-call | flops 134217728 | bytes 1048576 | tf_op jit(solution)/shard_map/pallas_call | solution.py:307
  8.9 4.0 %collective-permute-start.3 = (bf16[64,640]{1,0:T(8,128)(2,1)S(1)}, bf16[64,640]{1,0:T(8,128)(2,1)S(1)}, u32[]{:S(2)}, u32[]{:S(2)}) collective-permute-start(bf16[64,640]{1,0:T(8,128)(2,1)S(1)} %get-tuple-element.36), channel_id=1, source_target_pairs={{0,3},{1,2},{2,1},{3,0},{4,7},{5,6},{6,5},{7,4},{8,11},{9,10},{10,... | collective-permute-start | bytes 245768 | tf_op jit(solution)/shard_map/ppermute | solution.py:247
  12.9 0.5 collective-permute-start.4
  13.4 0.1 collective-permute-start.5
  13.5 1.1 %collective-permute-done.2.arrived = bf16[128,512]{1,0:T(8,128)(2,1)S(1)} collective-permute-done((bf16[128,512]{1,0:T(8,128)(2,1)S(1)}, bf16[128,512]{1,0:T(8,128)(2,1)S(1)}, u32[]{:S(2)}, u32[]{:S(2)}) %collective-permute-start.2) | collective-permute-done | bytes 131104 | tf_op jit(solution)/shard_map/ppermute | solution.py:299
  14.6 0.9 %shard_map.52 = (bf16[128,512]{1,0:T(8,128)(2,1)S(1)}, bf16[128,512]{1,0:T(8,128)(2,1)S(1)}) custom-call(s32[3]{0:T(128)S(1)} %pad_add_fusion.where, bf16[512,512]{1,0:T(8,128)(2,1)S(1)} %get-tuple-element.27.own, bf16[512,512]{1,0:T(8,128)(2,1)S(1)} %collective-permute-done.partner, f32[128,512]{1,0:T(8,128)S(1)} %get-tuple-element.28.slope_own, ...), custom_call_target="tpu_custom_call" | custom-call | flops 2147483648 | bytes 1048576 | tf_op jit(solution)/shard_map/pallas_call | solution.py:316
  15.5 0.2 collective-permute-done.3.refs_1_
  15.7 1.6 %collective-permute-done.4.refs_2_ = bf16[64,640]{1,0:T(8,128)(2,1)S(1)} collective-permute-done((bf16[64,640]{1,0:T(8,128)(2,1)S(1)}, bf16[64,640]{1,0:T(8,128)(2,1)S(1)}, u32[]{:S(2)}, u32[]{:S(2)}) %collective-permute-start.4) | collective-permute-done | bytes 81952 | tf_op jit(solution)/shard_map/ppermute | solution.py:247
  17.3 0.5 collective-permute-done.5.refs_3_
  17.9 0.9 %shard_map.55 = (bf16[128,512]{1,0:T(8,128)(2,1)S(1)}, bf16[128,512]{1,0:T(8,128)(2,1)S(1)}, bf16[128,512]{1,0:T(8,128)(2,1)S(1)}, bf16[128,512]{1,0:T(8,128)(2,1)S(1)}) custom-call(s32[3]{0:T(128)S(1)} %pad_add_fusion.where, bf16[512,512]{1,0:T(8,128)(2,1)S(1)} %get-tuple-element.27.own, bf16[512,512]{1,0:T(8,128)(2,1)S(1)} %collective-permute-done.partner, ...), custom_call_target="tpu_custom_call" | custom-call | flops 134217728 | bytes 1048576 | tf_op jit(solution)/shard_map/pallas_call | solution.py:322
  18.8 0.1 collective-permute-start.7
  18.9 1.3 %collective-permute-done.7.dh_got = bf16[128,512]{1,0:T(8,128)(2,1)S(1)} collective-permute-done((bf16[128,512]{1,0:T(8,128)(2,1)S(1)}, bf16[128,512]{1,0:T(8,128)(2,1)S(1)}, u32[]{:S(2)}, u32[]{:S(2)}) %collective-permute-start.7) | collective-permute-done | bytes 131104 | tf_op jit(solution)/shard_map/ppermute | solution.py:325
  20.2 1.1 %shard_map.57 = (bf16[64,1664]{1,0:T(8,128)(2,1)S(1)}, bf16[64,1664]{1,0:T(8,128)(2,1)S(1)}, bf16[64,1664]{1,0:T(8,128)(2,1)S(1)}, bf16[64,1664]{1,0:T(8,128)(2,1)S(1)}, bf16[64,640]{1,0:T(8,128)(2,1)S(1)}) custom-call(s32[3]{0:T(128)S(1)} %pad_add_fusion.where, bf16[2,128,512]{2,1,0:T(8,128)(2,1)S(1)} %get-tuple-element.34.local, ...), custom_call_target="tpu_custom_call" | custom-call | flops 268435456 | bytes 1048576 | tf_op jit(solution)/shard_map/pallas_call | solution.py:329
  21.3 1.4 %collective-permute-start.9 = (bf16[64,1664]{1,0:T(8,128)(2,1)S(1)}, bf16[64,1664]{1,0:T(8,128)(2,1)S(1)}, u32[]{:S(2)}, u32[]{:S(2)}) collective-permute-start(bf16[64,1664]{1,0:T(8,128)(2,1)S(1)} %get-tuple-element.45), channel_id=1, source_target_pairs={{0,3},{1,2},{2,1},{3,0},{4,7},{5,6},{6,5},{7,4},{8,11},{9,10},{10,... | collective-permute-start | bytes 638984 | tf_op jit(solution)/shard_map/ppermute | solution.py:247
  22.7 1.3 %collective-permute-start.13 = (bf16[64,1664]{1,0:T(8,128)(2,1)S(1)}, bf16[64,1664]{1,0:T(8,128)(2,1)S(1)}, u32[]{:S(2)}, u32[]{:S(2)}) collective-permute-start(bf16[64,1664]{1,0:T(8,128)(2,1)S(1)} %get-tuple-element.48), channel_id=1, source_target_pairs={{0,1},{1,0},{2,3},{3,2},{4,5},{5,4},{6,7},{7,6},{8,9},{9,8},{10,11... | collective-permute-start | bytes 638984 | tf_op jit(solution)/shard_map/ppermute | solution.py:247
  24.0 0.8 %collective-permute-start.14 = (bf16[64,1664]{1,0:T(8,128)(2,1)S(1)}, bf16[64,1664]{1,0:T(8,128)(2,1)S(1)}, u32[]{:S(2)}, u32[]{:S(2)}) collective-permute-start(bf16[64,1664]{1,0:T(8,128)(2,1)S(1)} %get-tuple-element.49), channel_id=1, source_target_pairs={{0,2},{1,3},{2,0},{3,1},{4,6},{5,7},{6,4},{7,5},{8,10},{9,11},{10,... | collective-permute-start | bytes 638984 | tf_op jit(solution)/shard_map/ppermute | solution.py:247
  24.8 0.0 collective-permute-start.6
  24.8 2.6 %collective-permute-start.8 = (bf16[64,640]{1,0:T(8,128)(2,1)S(1)}, bf16[64,640]{1,0:T(8,128)(2,1)S(1)}, u32[]{:S(2)}, u32[]{:S(2)}) collective-permute-start(bf16[64,640]{1,0:T(8,128)(2,1)S(1)} %get-tuple-element.43.left), channel_id=1, source_target_pairs={{0,4},{4,0},{1,5},{5,1},{2,6},{6,2},{3,7},{7,3},{8,12},{12,8},{9,1... | collective-permute-start | bytes 245768 | tf_op jit(solution)/shard_map/ppermute | solution.py:255
  27.4 0.0 collective-permute-done.6.other_cot
  27.4 1.3 %shard_map.56.after = bf16[2,128,512]{2,1,0:T(8,128)(2,1)} custom-call(s32[3]{0:T(128)S(1)} %pad_add_fusion.where, bf16[128,512]{1,0:T(8,128)(2,1)S(1)} %get-tuple-element.39.own_cot, bf16[128,512]{1,0:T(8,128)(2,1)S(1)} %collective-permute-done.6.other_cot), custom_call_target="tpu_custom_call" | custom-call | bytes 1048576 | tf_op jit(solution)/shard_map/pallas_call | solution.py:327
  28.7 3.4 %collective-permute-done.9.right = bf16[64,1664]{1,0:T(8,128)(2,1)S(1)} collective-permute-done((bf16[64,1664]{1,0:T(8,128)(2,1)S(1)}, bf16[64,1664]{1,0:T(8,128)(2,1)S(1)}, u32[]{:S(2)}, u32[]{:S(2)}) %collective-permute-start.9) | collective-permute-done | bytes 213024 | tf_op jit(solution)/shard_map/ppermute | solution.py:247
  32.1 0.0 copy-start
  32.1 0.9 %copy-done = bf16[2,128,512]{2,1,0:T(8,128)(2,1)S(1)} copy-done((bf16[2,128,512]{2,1,0:T(8,128)(2,1)S(1)}, bf16[2,128,512]{2,1,0:T(8,128)(2,1)}, u32[]{:S(2)}) %copy-start) | copy-done | bytes 262168
  33.1 0.8 %collective-permute-done.8.right = bf16[64,640]{1,0:T(8,128)(2,1)S(1)} collective-permute-done((bf16[64,640]{1,0:T(8,128)(2,1)S(1)}, bf16[64,640]{1,0:T(8,128)(2,1)S(1)}, u32[]{:S(2)}, u32[]{:S(2)}) %collective-permute-start.8) | collective-permute-done | bytes 81952 | tf_op jit(solution)/shard_map/ppermute | solution.py:255
  33.9 4.7 %collective-permute-start.12 = (bf16[64,640]{1,0:T(8,128)(2,1)S(1)}, bf16[64,640]{1,0:T(8,128)(2,1)S(1)}, u32[]{:S(2)}, u32[]{:S(2)}) collective-permute-start(bf16[64,640]{1,0:T(8,128)(2,1)S(1)} %shard_map.59.refs_0_), channel_id=1, source_target_pairs={{0,3},{1,2},{2,1},{3,0},{4,7},{5,6},{6,5},{7,4},{8,11},{9,10},{10,... | collective-permute-start | bytes 245768 | tf_op jit(solution)/shard_map/ppermute | solution.py:247
  38.6 0.1 collective-permute-start.11
  38.7 1.4 %collective-permute-start.10 = (bf16[64,640]{1,0:T(8,128)(2,1)S(1)}, bf16[64,640]{1,0:T(8,128)(2,1)S(1)}, u32[]{:S(2)}, u32[]{:S(2)}) collective-permute-start(bf16[64,640]{1,0:T(8,128)(2,1)S(1)} %shard_map.59.refs_0_), channel_id=1, source_target_pairs={{0,1},{1,0},{2,3},{3,2},{4,5},{5,4},{6,7},{7,6},{8,9},{9,8},{10,11... | collective-permute-start | bytes 245768 | tf_op jit(solution)/shard_map/ppermute | solution.py:247
  40.1 0.0 collective-permute-done.13
  40.1 0.0 collective-permute-done.14
  40.1 0.1 add_convert_fusion.left
  40.2 0.9 %collective-permute-start.15 = (bf16[64,1664]{1,0:T(8,128)(2,1)S(1)}, bf16[64,1664]{1,0:T(8,128)(2,1)S(1)}, u32[]{:S(2)}, u32[]{:S(2)}) collective-permute-start(bf16[64,1664]{1,0:T(8,128)(2,1)S(1)} %add_convert_fusion.left), channel_id=1, source_target_pairs={{0,4},{4,0},{1,5},{5,1},{2,6},{6,2},{3,7},{7,3},{8,12},{12,8},{9,1... | collective-permute-start | bytes 638984 | tf_op jit(solution)/shard_map/ppermute | solution.py:255
  41.0 0.5 collective-permute-done.12.refs_3_
  41.5 2.8 %collective-permute-done.11.refs_2_ = bf16[64,640]{1,0:T(8,128)(2,1)S(1)} collective-permute-done((bf16[64,640]{1,0:T(8,128)(2,1)S(1)}, bf16[64,640]{1,0:T(8,128)(2,1)S(1)}, u32[]{:S(2)}, u32[]{:S(2)}) %collective-permute-start.11) | collective-permute-done | bytes 81952 | tf_op jit(solution)/shard_map/ppermute | solution.py:247
  44.3 0.0 collective-permute-done.10.refs_1_
  44.3 4.0 %shard_map.60 = (bf16[512,512]{1,0:T(8,128)(2,1)S(1)}, bf16[512,512]{1,0:T(8,128)(2,1)S(1)}) custom-call(s32[3]{0:T(128)S(1)} %pad_add_fusion.where, bf16[64,640]{1,0:T(8,128)(2,1)S(1)} %shard_map.59.refs_0_, bf16[64,640]{1,0:T(8,128)(2,1)S(1)} %collective-permute-done.10.refs_1_, bf16[64,640]{1,0:T(8,128)(2,1)S(1)} %collective-permute-done.11.refs_2_, ...), custom_call_target="tpu_custom_call" | custom-call | flops 2684354560 | bytes 1048576 | tf_op jit(solution)/shard_map/pallas_call | solution.py:345
  48.3 3.4 %collective-permute-done.15.right = bf16[64,1664]{1,0:T(8,128)(2,1)S(1)} collective-permute-done((bf16[64,1664]{1,0:T(8,128)(2,1)S(1)}, bf16[64,1664]{1,0:T(8,128)(2,1)S(1)}, u32[]{:S(2)}, u32[]{:S(2)}) %collective-permute-start.15) | collective-permute-done | bytes 213024 | tf_op jit(solution)/shard_map/ppermute | solution.py:255
  51.7 0.1 shard_map.61
  51.7 0.1 collective-permute-start.18
  51.8 2.0 %collective-permute-start.17 = (bf16[64,640]{1,0:T(8,128)(2,1)S(1)}, bf16[64,640]{1,0:T(8,128)(2,1)S(1)}, u32[]{:S(2)}, u32[]{:S(2)}) collective-permute-start(bf16[64,640]{1,0:T(8,128)(2,1)S(1)} %slice.8.refs_0_), channel_id=1, source_target_pairs={{0,2},{1,3},{2,0},{3,1},{4,6},{5,7},{6,4},{7,5},{8,10},{9,11},{10,... | collective-permute-start | bytes 245768 | tf_op jit(solution)/shard_map/ppermute | solution.py:247
  53.9 1.4 %collective-permute-start.16 = (bf16[64,640]{1,0:T(8,128)(2,1)S(1)}, bf16[64,640]{1,0:T(8,128)(2,1)S(1)}, u32[]{:S(2)}, u32[]{:S(2)}) collective-permute-start(bf16[64,640]{1,0:T(8,128)(2,1)S(1)} %slice.8.refs_0_), channel_id=1, source_target_pairs={{0,1},{1,0},{2,3},{3,2},{4,5},{5,4},{6,7},{7,6},{8,9},{9,8},{10,11... | collective-permute-start | bytes 245768 | tf_op jit(solution)/shard_map/ppermute | solution.py:247
  55.3 0.1 collective-permute-start.21
  55.4 2.0 %collective-permute-start.20 = (bf16[64,1024]{1,0:T(8,128)(2,1)S(1)}, bf16[64,1024]{1,0:T(8,128)(2,1)S(1)}, u32[]{:S(2)}, u32[]{:S(2)}) collective-permute-start(bf16[64,1024]{1,0:T(8,128)(2,1)S(1)} %slice.9.refs_0_), channel_id=1, source_target_pairs={{0,2},{1,3},{2,0},{3,1},{4,6},{5,7},{6,4},{7,5},{8,10},{9,11},{10,... | collective-permute-start | bytes 393224 | tf_op jit(solution)/shard_map/ppermute | solution.py:247
  57.4 0.1 collective-permute-done.18.refs_3_
  57.5 1.4 %collective-permute-start.19 = (bf16[64,1024]{1,0:T(8,128)(2,1)S(1)}, bf16[64,1024]{1,0:T(8,128)(2,1)S(1)}, u32[]{:S(2)}, u32[]{:S(2)}) collective-permute-start(bf16[64,1024]{1,0:T(8,128)(2,1)S(1)} %slice.9.refs_0_), channel_id=1, source_target_pairs={{0,1},{1,0},{2,3},{3,2},{4,5},{5,4},{6,7},{7,6},{8,9},{9,8},{10,11... | collective-permute-start | bytes 393224 | tf_op jit(solution)/shard_map/ppermute | solution.py:247
  58.9 0.0 collective-permute-done.17.refs_2_
  58.9 1.8 %collective-permute-done.16.refs_1_ = bf16[64,640]{1,0:T(8,128)(2,1)S(1)} collective-permute-done((bf16[64,640]{1,0:T(8,128)(2,1)S(1)}, bf16[64,640]{1,0:T(8,128)(2,1)S(1)}, u32[]{:S(2)}, u32[]{:S(2)}) %collective-permute-start.16) | collective-permute-done | bytes 81952 | tf_op jit(solution)/shard_map/ppermute | solution.py:247
  60.7 4.0 %shard_map.62 = (bf16[512,512]{1,0:T(8,128)(2,1)S(1)}, bf16[512,512]{1,0:T(8,128)(2,1)S(1)}) custom-call(s32[3]{0:T(128)S(1)} %pad_add_fusion.where, bf16[64,640]{1,0:T(8,128)(2,1)S(1)} %slice.8.refs_0_, bf16[64,640]{1,0:T(8,128)(2,1)S(1)} %collective-permute-done.16.refs_1_, bf16[64,640]{1,0:T(8,128)(2,1)S(1)} %collective-permute-done.17.refs_2_, ...), custom_call_target="tpu_custom_call" | custom-call | flops 2684354560 | bytes 1048576 | tf_op jit(solution)/shard_map/pallas_call | solution.py:345
  64.7 0.0 collective-permute-done.21.refs_3_
  64.7 0.0 collective-permute-done.20.refs_2_
  64.7 0.0 collective-permute-done.19.refs_1_
  64.8 3.3 %shard_map.63 = f32[512,512]{1,0:T(8,128)} custom-call(s32[3]{0:T(128)S(1)} %pad_add_fusion.where, bf16[512,512]{1,0:T(8,128)(2,1)S(1)} %get-tuple-element.46.refs_0_.act_high, bf16[512,512]{1,0:T(8,128)(2,1)S(1)} %get-tuple-element.47.act_low, bf16[512,512]{1,0:T(8,128)(2,1)S(1)} %get-tuple-element.50.out_high, ...), custom_call_target="tpu_custom_call" | custom-call | flops 1342177280 | bytes 1048576 | tf_op jit(solution)/shard_map/pallas_call | solution.py:357
  (6 shorter events, 0.1 us)
Async XLA Ops:
  0.6 4.7 %collective-permute-start = (bf16[512,512]{1,0:T(8,128)(2,1)}, bf16[512,512]{1,0:T(8,128)(2,1)S(1)}, u32[]{:S(2)}, u32[]{:S(2)}) collective-permute-start(bf16[512,512]{1,0:T(8,128)(2,1)} %bitcast.8), channel_id=1, source_target_pairs={{0,8},{8,0},{1,9},{9,1},{2,10},{10,2},{3,11},{11,3},{4,12},{12,4},... | collective-permute-start | bytes 1572872 | tf_op jit(solution)/shard_map/ppermute | solution.py:283
  1.1 4.2 %collective-permute-start.1 = (bf16[2,128,512]{2,1,0:T(8,128)(2,1)}, bf16[2,128,512]{2,1,0:T(8,128)(2,1)S(1)}, u32[]{:S(2)}, u32[]{:S(2)}) collective-permute-start(bf16[2,128,512]{2,1,0:T(8,128)(2,1)} %bitcast.10), channel_id=1, source_target_pairs={{0,8},{8,0},{1,9},{9,1},{2,10},{10,2},{3,11},{11,3},{4,12},{12,4},... | collective-permute-start | bytes 786440 | tf_op jit(solution)/shard_map/ppermute | solution.py:284
  1.3 1.0 %copy-start.1 = (bf16[1,512,512]{2,1,0:T(8,128)(2,1)S(1)}, bf16[1,512,512]{2,1,0:T(8,128)(2,1)}, u32[]{:S(2)}) copy-start(bf16[1,512,512]{2,1,0:T(8,128)(2,1)} %param.4) | copy-start | bytes 1572868
  2.3 0.9 %copy-start.2 = (bf16[2,128,512]{2,1,0:T(8,128)(2,1)S(1)}, bf16[2,128,512]{2,1,0:T(8,128)(2,1)}, u32[]{:S(2)}) copy-start(bf16[2,128,512]{2,1,0:T(8,128)(2,1)} %cot_last.1) | copy-start | bytes 786436
  3.3 0.9 %copy-start.3 = (bf16[1,2,128,512]{3,2,1,0:T(8,128)(2,1)S(1)}, bf16[1,2,128,512]{3,2,1,0:T(8,128)(2,1)}, u32[]{:S(2)}) copy-start(bf16[1,2,128,512]{3,2,1,0:T(8,128)(2,1)} %param.3) | copy-start | bytes 786436
  6.7 8.0 %collective-permute-start.2 = (bf16[128,512]{1,0:T(8,128)(2,1)S(1)}, bf16[128,512]{1,0:T(8,128)(2,1)S(1)}, u32[]{:S(2)}, u32[]{:S(2)}) collective-permute-start(bf16[128,512]{1,0:T(8,128)(2,1)S(1)} %get-tuple-element.31.after), channel_id=1, source_target_pairs={{16,0},{17,1},{18,2},{19,3},{20,4},{21,5},{22,6},{23,7},{24,8},{25... | collective-permute-start | bytes 393224 | tf_op jit(solution)/shard_map/ppermute | solution.py:299
  8.9 6.8 %collective-permute-start.3 = (bf16[64,640]{1,0:T(8,128)(2,1)S(1)}, bf16[64,640]{1,0:T(8,128)(2,1)S(1)}, u32[]{:S(2)}, u32[]{:S(2)}) collective-permute-start(bf16[64,640]{1,0:T(8,128)(2,1)S(1)} %get-tuple-element.36), channel_id=1, source_target_pairs={{0,3},{1,2},{2,1},{3,0},{4,7},{5,6},{6,5},{7,4},{8,11},{9,10},{10,... | collective-permute-start | bytes 245768 | tf_op jit(solution)/shard_map/ppermute | solution.py:247
  12.9 4.4 %collective-permute-start.4 = (bf16[64,640]{1,0:T(8,128)(2,1)S(1)}, bf16[64,640]{1,0:T(8,128)(2,1)S(1)}, u32[]{:S(2)}, u32[]{:S(2)}) collective-permute-start(bf16[64,640]{1,0:T(8,128)(2,1)S(1)} %get-tuple-element.37), channel_id=1, source_target_pairs={{0,1},{1,0},{2,3},{3,2},{4,5},{5,4},{6,7},{7,6},{8,9},{9,8},{10,11... | collective-permute-start | bytes 245768 | tf_op jit(solution)/shard_map/ppermute | solution.py:247
  13.4 4.4 %collective-permute-start.5 = (bf16[64,640]{1,0:T(8,128)(2,1)S(1)}, bf16[64,640]{1,0:T(8,128)(2,1)S(1)}, u32[]{:S(2)}, u32[]{:S(2)}) collective-permute-start(bf16[64,640]{1,0:T(8,128)(2,1)S(1)} %get-tuple-element.38), channel_id=1, source_target_pairs={{0,2},{1,3},{2,0},{3,1},{4,6},{5,7},{6,4},{7,5},{8,10},{9,11},{10,... | collective-permute-start | bytes 245768 | tf_op jit(solution)/shard_map/ppermute | solution.py:247
  18.8 1.4 %collective-permute-start.7 = (bf16[128,512]{1,0:T(8,128)(2,1)S(1)}, bf16[128,512]{1,0:T(8,128)(2,1)S(1)}, u32[]{:S(2)}, u32[]{:S(2)}) collective-permute-start(bf16[128,512]{1,0:T(8,128)(2,1)S(1)} %get-tuple-element.42), channel_id=1, source_target_pairs={{0,8},{8,0},{1,9},{9,1},{2,10},{10,2},{3,11},{11,3},{4,12},{12,4},... | collective-permute-start | bytes 393224 | tf_op jit(solution)/shard_map/ppermute | solution.py:325
  21.3 10.9 %collective-permute-start.9 = (bf16[64,1664]{1,0:T(8,128)(2,1)S(1)}, bf16[64,1664]{1,0:T(8,128)(2,1)S(1)}, u32[]{:S(2)}, u32[]{:S(2)}) collective-permute-start(bf16[64,1664]{1,0:T(8,128)(2,1)S(1)} %get-tuple-element.45), channel_id=1, source_target_pairs={{0,3},{1,2},{2,1},{3,0},{4,7},{5,6},{6,5},{7,4},{8,11},{9,10},{10,... | collective-permute-start | bytes 638984 | tf_op jit(solution)/shard_map/ppermute | solution.py:247
  22.7 17.4 %collective-permute-start.13 = (bf16[64,1664]{1,0:T(8,128)(2,1)S(1)}, bf16[64,1664]{1,0:T(8,128)(2,1)S(1)}, u32[]{:S(2)}, u32[]{:S(2)}) collective-permute-start(bf16[64,1664]{1,0:T(8,128)(2,1)S(1)} %get-tuple-element.48), channel_id=1, source_target_pairs={{0,1},{1,0},{2,3},{3,2},{4,5},{5,4},{6,7},{7,6},{8,9},{9,8},{10,11... | collective-permute-start | bytes 638984 | tf_op jit(solution)/shard_map/ppermute | solution.py:247
  24.0 16.1 %collective-permute-start.14 = (bf16[64,1664]{1,0:T(8,128)(2,1)S(1)}, bf16[64,1664]{1,0:T(8,128)(2,1)S(1)}, u32[]{:S(2)}, u32[]{:S(2)}) collective-permute-start(bf16[64,1664]{1,0:T(8,128)(2,1)S(1)} %get-tuple-element.49), channel_id=1, source_target_pairs={{0,2},{1,3},{2,0},{3,1},{4,6},{5,7},{6,4},{7,5},{8,10},{9,11},{10,... | collective-permute-start | bytes 638984 | tf_op jit(solution)/shard_map/ppermute | solution.py:247
  24.8 2.6 %collective-permute-start.6 = (bf16[128,512]{1,0:T(8,128)(2,1)S(1)}, bf16[128,512]{1,0:T(8,128)(2,1)S(1)}, u32[]{:S(2)}, u32[]{:S(2)}) collective-permute-start(bf16[128,512]{1,0:T(8,128)(2,1)S(1)} %get-tuple-element.40), channel_id=1, source_target_pairs={{0,8},{8,0},{1,9},{9,1},{2,10},{10,2},{3,11},{11,3},{4,12},{12,4},... | collective-permute-start | bytes 393224 | tf_op jit(solution)/shard_map/ppermute | solution.py:326
  24.8 9.1 %collective-permute-start.8 = (bf16[64,640]{1,0:T(8,128)(2,1)S(1)}, bf16[64,640]{1,0:T(8,128)(2,1)S(1)}, u32[]{:S(2)}, u32[]{:S(2)}) collective-permute-start(bf16[64,640]{1,0:T(8,128)(2,1)S(1)} %get-tuple-element.43.left), channel_id=1, source_target_pairs={{0,4},{4,0},{1,5},{5,1},{2,6},{6,2},{3,7},{7,3},{8,12},{12,8},{9,1... | collective-permute-start | bytes 245768 | tf_op jit(solution)/shard_map/ppermute | solution.py:255
  32.1 1.0 %copy-start = (bf16[2,128,512]{2,1,0:T(8,128)(2,1)S(1)}, bf16[2,128,512]{2,1,0:T(8,128)(2,1)}, u32[]{:S(2)}) copy-start(bf16[2,128,512]{2,1,0:T(8,128)(2,1)} %shard_map.56.after) | copy-start | bytes 786436
  33.9 7.6 %collective-permute-start.12 = (bf16[64,640]{1,0:T(8,128)(2,1)S(1)}, bf16[64,640]{1,0:T(8,128)(2,1)S(1)}, u32[]{:S(2)}, u32[]{:S(2)}) collective-permute-start(bf16[64,640]{1,0:T(8,128)(2,1)S(1)} %shard_map.59.refs_0_), channel_id=1, source_target_pairs={{0,3},{1,2},{2,1},{3,0},{4,7},{5,6},{6,5},{7,4},{8,11},{9,10},{10,... | collective-permute-start | bytes 245768 | tf_op jit(solution)/shard_map/ppermute | solution.py:247
  38.6 5.7 %collective-permute-start.11 = (bf16[64,640]{1,0:T(8,128)(2,1)S(1)}, bf16[64,640]{1,0:T(8,128)(2,1)S(1)}, u32[]{:S(2)}, u32[]{:S(2)}) collective-permute-start(bf16[64,640]{1,0:T(8,128)(2,1)S(1)} %shard_map.59.refs_0_), channel_id=1, source_target_pairs={{0,2},{1,3},{2,0},{3,1},{4,6},{5,7},{6,4},{7,5},{8,10},{9,11},{10,... | collective-permute-start | bytes 245768 | tf_op jit(solution)/shard_map/ppermute | solution.py:247
  38.7 5.6 %collective-permute-start.10 = (bf16[64,640]{1,0:T(8,128)(2,1)S(1)}, bf16[64,640]{1,0:T(8,128)(2,1)S(1)}, u32[]{:S(2)}, u32[]{:S(2)}) collective-permute-start(bf16[64,640]{1,0:T(8,128)(2,1)S(1)} %shard_map.59.refs_0_), channel_id=1, source_target_pairs={{0,1},{1,0},{2,3},{3,2},{4,5},{5,4},{6,7},{7,6},{8,9},{9,8},{10,11... | collective-permute-start | bytes 245768 | tf_op jit(solution)/shard_map/ppermute | solution.py:247
  40.2 11.5 %collective-permute-start.15 = (bf16[64,1664]{1,0:T(8,128)(2,1)S(1)}, bf16[64,1664]{1,0:T(8,128)(2,1)S(1)}, u32[]{:S(2)}, u32[]{:S(2)}) collective-permute-start(bf16[64,1664]{1,0:T(8,128)(2,1)S(1)} %add_convert_fusion.left), channel_id=1, source_target_pairs={{0,4},{4,0},{1,5},{5,1},{2,6},{6,2},{3,7},{7,3},{8,12},{12,8},{9,1... | collective-permute-start | bytes 638984 | tf_op jit(solution)/shard_map/ppermute | solution.py:255
  51.7 5.8 %collective-permute-start.18 = (bf16[64,640]{1,0:T(8,128)(2,1)S(1)}, bf16[64,640]{1,0:T(8,128)(2,1)S(1)}, u32[]{:S(2)}, u32[]{:S(2)}) collective-permute-start(bf16[64,640]{1,0:T(8,128)(2,1)S(1)} %slice.8.refs_0_), channel_id=1, source_target_pairs={{0,3},{1,2},{2,1},{3,0},{4,7},{5,6},{6,5},{7,4},{8,11},{9,10},{10,... | collective-permute-start | bytes 245768 | tf_op jit(solution)/shard_map/ppermute | solution.py:247
  51.8 7.1 %collective-permute-start.17 = (bf16[64,640]{1,0:T(8,128)(2,1)S(1)}, bf16[64,640]{1,0:T(8,128)(2,1)S(1)}, u32[]{:S(2)}, u32[]{:S(2)}) collective-permute-start(bf16[64,640]{1,0:T(8,128)(2,1)S(1)} %slice.8.refs_0_), channel_id=1, source_target_pairs={{0,2},{1,3},{2,0},{3,1},{4,6},{5,7},{6,4},{7,5},{8,10},{9,11},{10,... | collective-permute-start | bytes 245768 | tf_op jit(solution)/shard_map/ppermute | solution.py:247
  53.9 6.8 %collective-permute-start.16 = (bf16[64,640]{1,0:T(8,128)(2,1)S(1)}, bf16[64,640]{1,0:T(8,128)(2,1)S(1)}, u32[]{:S(2)}, u32[]{:S(2)}) collective-permute-start(bf16[64,640]{1,0:T(8,128)(2,1)S(1)} %slice.8.refs_0_), channel_id=1, source_target_pairs={{0,1},{1,0},{2,3},{3,2},{4,5},{5,4},{6,7},{7,6},{8,9},{9,8},{10,11... | collective-permute-start | bytes 245768 | tf_op jit(solution)/shard_map/ppermute | solution.py:247
  55.3 9.4 %collective-permute-start.21 = (bf16[64,1024]{1,0:T(8,128)(2,1)S(1)}, bf16[64,1024]{1,0:T(8,128)(2,1)S(1)}, u32[]{:S(2)}, u32[]{:S(2)}) collective-permute-start(bf16[64,1024]{1,0:T(8,128)(2,1)S(1)} %slice.9.refs_0_), channel_id=1, source_target_pairs={{0,3},{1,2},{2,1},{3,0},{4,7},{5,6},{6,5},{7,4},{8,11},{9,10},{10,... | collective-permute-start | bytes 393224 | tf_op jit(solution)/shard_map/ppermute | solution.py:247
  55.4 9.3 %collective-permute-start.20 = (bf16[64,1024]{1,0:T(8,128)(2,1)S(1)}, bf16[64,1024]{1,0:T(8,128)(2,1)S(1)}, u32[]{:S(2)}, u32[]{:S(2)}) collective-permute-start(bf16[64,1024]{1,0:T(8,128)(2,1)S(1)} %slice.9.refs_0_), channel_id=1, source_target_pairs={{0,2},{1,3},{2,0},{3,1},{4,6},{5,7},{6,4},{7,5},{8,10},{9,11},{10,... | collective-permute-start | bytes 393224 | tf_op jit(solution)/shard_map/ppermute | solution.py:247
  57.5 7.2 %collective-permute-start.19 = (bf16[64,1024]{1,0:T(8,128)(2,1)S(1)}, bf16[64,1024]{1,0:T(8,128)(2,1)S(1)}, u32[]{:S(2)}, u32[]{:S(2)}) collective-permute-start(bf16[64,1024]{1,0:T(8,128)(2,1)S(1)} %slice.9.refs_0_), channel_id=1, source_target_pairs={{0,1},{1,0},{2,3},{3,2},{4,5},{5,4},{6,7},{7,6},{8,9},{9,8},{10,11... | collective-permute-start | bytes 393224 | tf_op jit(solution)/shard_map/ppermute | solution.py:247

commit v8 on v7

--- a/solution.py
+++ b/solution.py
@@ -76,29 +76,22 @@
     )
 
 
-def load_kernel(where, weight, local, cot_last, weight_copy, local_copy, slope, cot, done):
+def first_kernel(
+    where, weight, local, cot_last, partner, partner_local,
+    own, kept, last, slope_own, slope_partner, down,
+):
     core = where[0]
-    copies = [
-        pltpu.make_async_copy(source, target, done.at[i])
-        for i, (source, target) in enumerate(
-            ((weight, weight_copy), (local, local_copy), (cot_last.at[core], cot))
-        )
-    ]
-    for copy in copies:
-        copy.start()
-    for copy in copies:
-        copy.wait()
-    slope[...] = slope_of(local_copy[core], weight_copy[...])
-
-
-def first_kernel(where, own, partner, slope_own, local, upstream, slope_partner, down):
-    slope_partner[...] = slope_of(local[where[0]], partner[...])
+    last[...] = cot_last[core]
+    slope_own[...] = slope_of(local[core], weight[...])
+    slope_partner[...] = slope_of(partner_local[core], partner[...])
 
     def run(odd, even):
-        cot = layer(upstream[...], odd[1][...], odd[0][...])[1]
+        cot = layer(last[...], odd[1][...], odd[0][...])[1]
         down[...] = layer(cot, even[1][...], even[0][...])[1]
 
-    by_core(where[0], run, (own, slope_own), (partner, slope_partner))
+    by_core(core, run, (weight, slope_own), (partner, slope_partner))
+    own[...] = weight[...]
+    kept[...] = local[...]
 
 
 def odd_kernel(where, own, partner, slope_own, slope_partner, arrived, last, dh, cot):
@@ -127,7 +120,7 @@
     )
 
 
-def cot_kernel(where, own_cot, other_cot, result):
+def cot_kernel(where, own_cot, other_cot, after, result):
     result[where[0]] = own_cot[...]
     result[1 - where[0]] = other_cot[...]
 
@@ -162,13 +155,13 @@
     refs[-1][...] = (left[...].astype(F32) + right[...].astype(F32)).astype(BF16)
 
 
-def begin_kernel(left, right, after, result):
+def begin_kernel(left, right, act, result, act_copy):
+    act_copy[...] = act[...]
     result[...] = left[...].astype(F32) + right[...].astype(F32)
 
 
-def grad_kernel(where, local, dh_own, dh_got, act_sum, *refs):
-    parts, (act_part, inputs, tokens, whole) = refs[:GROUP], refs[GROUP:]
-    act_part[...] = act_sum[...]
+def grad_kernel(where, local, dh_own, dh_got, *refs):
+    parts, (inputs, tokens, whole) = refs[:GROUP], refs[GROUP:]
     rows, width = local.shape[1:]
     inputs[:rows] = local[where[0]]
     inputs[rows:] = local[1 - where[0]]
@@ -230,12 +223,12 @@
         start = pl.multiple_of((where[1] ^ step) * 2 * half, 2 * half)
         grad[pl.ds(start, half)] = piece[:, :width]
         grad[pl.ds(start + half, half)] = piece[:, width:]
+    left = product((act_high[...], act_low[...]), (grad[...],))
     copies = []
-    for u in range(GROUP):
-        rows = pl.ds(u * 2 * half, 2 * half)
-        left = product((act_high[rows], act_low[rows]), (grad[...],))
-        update[rows] = product(split(left), (out_high[...], out_low[...]))
-        copies.append(pltpu.make_async_copy(update.at[rows], result.at[rows], done.at[u]))
+    for part in range(2):
+        rows = pl.ds(part * 4 * half, 4 * half)
+        update[rows] = product(split(left[part * 4 * half:(part + 1) * 4 * half]), (out_high[...], out_low[...]))
+        copies.append(pltpu.make_async_copy(update.at[rows], result.at[rows], done.at[part]))
         copies[-1].start()
     for copy in copies:
         copy.wait()
@@ -248,15 +241,12 @@
     return [got[step] for step in range(GROUP)]
 
 
-def exchange(value, after=None):
+def exchange(value, after=(), flops=0):
     step = 1
     while step < lax.axis_size("far"):
         route = [(i, i ^ step) for i in range(lax.axis_size("far"))]
         got = lax.ppermute(value, "far", route)
-        if after is None:
-            value = (value.astype(F32) + got.astype(F32)).astype(BF16)
-        else:
-            value = call(add_kernel, 0, value, [VMEM] * 2 + [ANY] * len(after))(value, got, *after)
+        value = call(add_kernel, flops, value, [VMEM] * 2 + [ANY] * len(after))(value, got, *after)
         step *= 2
     return value
 
@@ -284,16 +274,12 @@
     partner_local = lax.ppermute(local, "core", SWAP)
     block = array(rows, width)
     slope = array(rows, width, dtype=F32)
-    own, kept, slope_own, last = call(
-        load_kernel,
-        2 * rows * width**2,
-        [array(width, width), array(micro, rows, width), slope, block],
-        [SMEM] + [HBM] * 3,
-        [pltpu.SemaphoreType.DMA((3,))],
-    )(where, weight, local, cot_last)
-    slope_partner, down = call(first_kernel, 6 * rows * width**2, [slope, block], [SMEM] + [VMEM] * 5)(
-        where, own, partner, slope_own, partner_local, last
-    )
+    own, kept, last, slope_own, slope_partner, down = call(
+        first_kernel,
+        8 * rows * width**2,
+        [array(width, width), array(micro, rows, width), block, slope, slope, block],
+        [SMEM] + [VMEM] * 5,
+    )(where, weight, local, cot_last, partner, partner_local)
     first = down
     for turn in range(1, pairs):
         upstream = lax.ppermute(down, "row", [(r, r - 1) for r in range(1, pairs)])
@@ -324,22 +310,27 @@
     )(where, own, partner, slope_own, slope_partner, dh_odd, cot_odd, act_sum)
     got_dh = lax.ppermute(give_dh, "core", SWAP)
     other_cot = lax.ppermute(give_cot, "core", SWAP)
-    cot = call(cot_kernel, 0, array(micro, rows, width), [SMEM, VMEM, VMEM])(where, own_cot, other_cot)
-
-    *parts, act_part = call(
+
+    parts = call(
         grad_kernel,
         4 * tokens * width**2,
-        [array(size // 2, factor + 2 * width)] * GROUP + [array(size // 2, factor)],
-        [SMEM] + [VMEM] * 4,
+        [array(size // 2, factor + 2 * width)] * GROUP,
+        [SMEM] + [VMEM] * 3,
         [pltpu.VMEM((tokens, width), BF16)] * 2
         + [pltpu.VMEM((GROUP, size // 2, factor + 2 * width), BF16)],
-    )(where, kept, own_dh, got_dh, act_sum)
+    )(where, kept, own_dh, got_dh)
     pieces = send(parts)
-    begun = call(begin_kernel, 0, array(*parts[0].shape, dtype=F32), [VMEM] * 2 + [ANY])(
-        pieces[0], pieces[3], cot
-    )
+    begun, act_part = call(
+        begin_kernel,
+        0,
+        [array(*parts[0].shape, dtype=F32), array(size // 2, factor)],
+        [VMEM] * 3,
+    )(pieces[0], pieces[3], exchange(act_sum, flops=24 * width**3))
     total = (begun + pieces[1].astype(F32) + pieces[2].astype(F32)).astype(BF16)
-    act = send([exchange(act_part, (begun,))] * GROUP)
+    cot = call(cot_kernel, 0, array(micro, rows, width), [SMEM, VMEM, VMEM, ANY])(
+        where, own_cot, other_cot, total
+    )
+    act = send([act_part] * GROUP)
 
     def inverse(pieces):
         return call(
@@ -351,7 +342,7 @@
         )(where, *pieces)
 
     act_inv = inverse(act)
-    total = exchange(total, (act_inv[0],))
+    total = exchange(total, (act_inv[0], cot))
     out = send([total[:, :factor]] * GROUP)
     grad = send([total[:, factor:]] * GROUP)
     update = call(
@@ -362,7 +353,7 @@
         [
             pltpu.VMEM((width, width), BF16),
             pltpu.VMEM((width, width), F32),
-            pltpu.SemaphoreType.DMA((GROUP,)),
+            pltpu.SemaphoreType.DMA((2,)),
         ],
         HBM,
     )(where, *act_inv, *inverse(out), *grad)

time: 68.4 us -> 68 us (level)
  waiting for transfers between devices: 17.5 us -> 21 us
  starting transfers between devices: 26.8 us -> 25.2 us
  Pallas kernels: 18.9 us -> 17.6 us
  local copies, waits for them, and re-layouts: 3.91 us -> 2.96 us
    ppermute x15, starting transfers between devices: 21.4 us -> 19.2 us  [send(): lax.ppermute(parts[step], ('near', 'side'), [(i, i ^ step) for i in range...]
    ppermute x1, waiting for transfers between devices: 0.01 us -> 1.97 us  [body(): partner_local = lax.ppermute(local, 'core', SWAP)]
    ppermute x2, waiting for transfers between devices: 4.14 us -> 5.73 us  [exchange(): got = lax.ppermute(value, 'far', route)]
    ppermute x1, waiting for transfers between devices: 1.33 us -> 0.01 us  [body(): got_dh = lax.ppermute(give_dh, 'core', SWAP)]
    ppermute x15, waiting for transfers between devices: 10.9 us -> 12.2 us  [send(): lax.ppermute(parts[step], ('near', 'side'), [(i, i ^ step) for i in range...]
    unnamed x8, local copies, waits for them, and re-layouts: 3.89 us -> 2.94 us
    pallas_call x6 -> x5, Pallas kernels: 3.78 us -> 2.86 us  [the longest x1 1.46 us: body(): call(first_kernel, 8 * rows * width ** 2, [array(width, width), array(mic...]
  transfers between devices with their start and end apart: 22 -> 22, of which waited for: 12 -> 11; matrix products, arithmetic and copies ran while one was open for 0% -> 0% of each run, Pallas kernels for 18% -> 18%
where the time goes in v8:
time: 68 us; the launch traced here: 67.7 us
  starting transfers between devices  25.2 us (37%)
  waiting for transfers between devices  21 us (31%)
  Pallas kernels  17.6 us (26%)
  local copies, waits for them, and re-layouts  2.96 us (4%)
  between operations  0.78 us (1%)
    ppermute x15, starting transfers between devices, send(): lax.ppermute(parts[step], ('near', 'side'), [(i, i ^ step) for i in range...  19.2 us
    ppermute x15, waiting for transfers between devices, send(): lax.ppermute(parts[step], ('near', 'side'), [(i, i ^ step) for i in range...  12.2 us
    pallas_call x2, Pallas kernels, inverse(): call(functools.partial(inverse_kernel, count), 20 * width ** 3, [array(wi...  8.05 us
    ppermute x2, waiting for transfers between devices, exchange(): got = lax.ppermute(value, 'far', route)  5.73 us
    ppermute x2, starting transfers between devices, exchange(): got = lax.ppermute(value, 'far', route)  3.85 us
    unnamed x8, local copies, waits for them, and re-layouts  2.94 us
    pallas_call x1, Pallas kernels, body(): call(update_kernel, 10 * width ** 3, array(width, width, dtype=F32), [SME...  2.92 us
    ppermute x1, waiting for transfers between devices, body(): partner_local = lax.ppermute(local, 'core', SWAP)  1.97 us
  transfers between devices with their start and end apart: 22, of which 11 were waited for; matrix products, arithmetic and copies ran while one was open for 0% of the time, Pallas kernels for 18%

profile of v8, /device:TPU:0, one launch (start us, length us, event | category | flops | bytes accessed | tf_op | source)
XLA Modules:
  0.0 67.7 jit_solution(12726592199191301690)
XLA Ops:
  0.6 0.5 collective-permute-start
  1.1 0.1 collective-permute-start.1
  1.2 0.1 pad_add_fusion.where
  1.3 2.0 %collective-permute-done.1.partner_local = bf16[2,128,512]{2,1,0:T(8,128)(2,1)S(1)} collective-permute-done((bf16[2,128,512]{2,1,0:T(8,128)(2,1)}, bf16[2,128,512]{2,1,0:T(8,128)(2,1)S(1)}, u32[]{:S(2)}, u32[]{:S(2)}) %collective-permute-start.1) | collective-permute-done | bytes 262176 | tf_op jit(solution)/shard_map/ppermute | solution.py:274
  3.3 0.0 collective-permute-done.partner
  3.3 0.0 copy-start.1
  3.3 1.0 %copy-done.1 = bf16[1,512,512]{2,1,0:T(8,128)(2,1)S(1)} copy-done((bf16[1,512,512]{2,1,0:T(8,128)(2,1)S(1)}, bf16[1,512,512]{2,1,0:T(8,128)(2,1)}, u32[]{:S(2)}) %copy-start.1) | copy-done | bytes 524312
  4.3 0.0 copy-start.2
  4.3 0.9 %copy-done.2 = bf16[1,2,128,512]{3,2,1,0:T(8,128)(2,1)S(1)} copy-done((bf16[1,2,128,512]{3,2,1,0:T(8,128)(2,1)S(1)}, bf16[1,2,128,512]{3,2,1,0:T(8,128)(2,1)}, u32[]{:S(2)}) %copy-start.2) | copy-done | bytes 262168
  5.3 0.0 copy-start.3
  5.3 0.9 %copy-done.3 = bf16[2,128,512]{2,1,0:T(8,128)(2,1)S(1)} copy-done((bf16[2,128,512]{2,1,0:T(8,128)(2,1)S(1)}, bf16[2,128,512]{2,1,0:T(8,128)(2,1)}, u32[]{:S(2)}) %copy-start.3) | copy-done | bytes 262168
  6.2 1.5 %shard_map.50 = (bf16[512,512]{1,0:T(8,128)(2,1)S(1)}, bf16[2,128,512]{2,1,0:T(8,128)(2,1)S(1)}, bf16[128,512]{1,0:T(8,128)(2,1)S(1)}, f32[128,512]{1,0:T(8,128)...) custom-call(s32[3]{0:T(128)S(1)} %pad_add_fusion.where, bf16[512,512]{1,0:T(8,128)(2,1)S(1)} %bitcast.9, ...), custom_call_target="tpu_custom_call" | custom-call | flops 268435456 | bytes 1048576 | tf_op jit(solution)/shard_map/pallas_call | solution.py:277
  7.7 1.3 %collective-permute-start.2 = (bf16[128,512]{1,0:T(8,128)(2,1)S(1)}, bf16[128,512]{1,0:T(8,128)(2,1)S(1)}, u32[]{:S(2)}, u32[]{:S(2)}) collective-permute-start(bf16[128,512]{1,0:T(8,128)(2,1)S(1)} %get-tuple-element.31.after), channel_id=1, source_target_pairs={{16,0},{17,1},{18,2},{19,3},{20,4},{21,5},{22,6},{23,7},{24,8},{25... | collective-permute-start | bytes 393224 | tf_op jit(solution)/shard_map/ppermute | solution.py:285
  9.0 0.9 %shard_map.52 = (bf16[64,640]{1,0:T(8,128)(2,1)S(1)}, bf16[64,640]{1,0:T(8,128)(2,1)S(1)}, bf16[64,640]{1,0:T(8,128)(2,1)S(1)}, bf16[64,640]{1,0:T(8,128)(2,1)S(1)}) custom-call(s32[3]{0:T(128)S(1)} %pad_add_fusion.where, bf16[2,128,512]{2,1,0:T(8,128)(2,1)S(1)} %get-tuple-element.35.local, bf16[128,512]{1,0:T(8,128)(2,1)S(1)} %get-tuple-element.31.after), custom_call_target="tpu_custom_call" | custom-call | flops 134217728 | bytes 1048576 | tf_op jit(solution)/shard_map/pallas_call | solution.py:293
  9.9 3.9 %collective-permute-start.3 = (bf16[64,640]{1,0:T(8,128)(2,1)S(1)}, bf16[64,640]{1,0:T(8,128)(2,1)S(1)}, u32[]{:S(2)}, u32[]{:S(2)}) collective-permute-start(bf16[64,640]{1,0:T(8,128)(2,1)S(1)} %get-tuple-element.37), channel_id=1, source_target_pairs={{0,3},{1,2},{2,1},{3,0},{4,7},{5,6},{6,5},{7,4},{8,11},{9,10},{10,... | collective-permute-start | bytes 245768 | tf_op jit(solution)/shard_map/ppermute | solution.py:240
  13.8 0.5 collective-permute-start.4
  14.4 0.1 collective-permute-start.5
  14.5 1.2 %collective-permute-done.2.arrived = bf16[128,512]{1,0:T(8,128)(2,1)S(1)} collective-permute-done((bf16[128,512]{1,0:T(8,128)(2,1)S(1)}, bf16[128,512]{1,0:T(8,128)(2,1)S(1)}, u32[]{:S(2)}, u32[]{:S(2)}) %collective-permute-start.2) | collective-permute-done | bytes 131104 | tf_op jit(solution)/shard_map/ppermute | solution.py:285
  15.6 0.9 %shard_map.51 = (bf16[128,512]{1,0:T(8,128)(2,1)S(1)}, bf16[128,512]{1,0:T(8,128)(2,1)S(1)}) custom-call(s32[3]{0:T(128)S(1)} %pad_add_fusion.where, bf16[512,512]{1,0:T(8,128)(2,1)S(1)} %get-tuple-element.28.own, bf16[512,512]{1,0:T(8,128)(2,1)S(1)} %collective-permute-done.partner, f32[128,512]{1,0:T(8,128)S(1)} %get-tuple-element.29.slope_own, ...), custom_call_target="tpu_custom_call" | custom-call | flops 2147483648 | bytes 1048576 | tf_op jit(solution)/shard_map/pallas_call | solution.py:302
  16.5 0.1 collective-permute-done.3.refs_1_
  16.6 1.7 %collective-permute-done.4.refs_2_ = bf16[64,640]{1,0:T(8,128)(2,1)S(1)} collective-permute-done((bf16[64,640]{1,0:T(8,128)(2,1)S(1)}, bf16[64,640]{1,0:T(8,128)(2,1)S(1)}, u32[]{:S(2)}, u32[]{:S(2)}) %collective-permute-start.4) | collective-permute-done | bytes 81952 | tf_op jit(solution)/shard_map/ppermute | solution.py:240
  18.3 0.5 collective-permute-done.5.refs_3_
  18.8 0.9 %shard_map.54 = (bf16[128,512]{1,0:T(8,128)(2,1)S(1)}, bf16[128,512]{1,0:T(8,128)(2,1)S(1)}, bf16[128,512]{1,0:T(8,128)(2,1)S(1)}, bf16[128,512]{1,0:T(8,128)(2,1)S(1)}) custom-call(s32[3]{0:T(128)S(1)} %pad_add_fusion.where, bf16[512,512]{1,0:T(8,128)(2,1)S(1)} %get-tuple-element.28.own, bf16[512,512]{1,0:T(8,128)(2,1)S(1)} %collective-permute-done.partner, ...), custom_call_target="tpu_custom_call" | custom-call | flops 134217728 | bytes 1048576 | tf_op jit(solution)/shard_map/pallas_call | solution.py:308
  19.7 0.1 collective-permute-start.7
  19.8 2.7 %collective-permute-start.9 = (bf16[64,640]{1,0:T(8,128)(2,1)S(1)}, bf16[64,640]{1,0:T(8,128)(2,1)S(1)}, u32[]{:S(2)}, u32[]{:S(2)}) collective-permute-start(bf16[64,640]{1,0:T(8,128)(2,1)S(1)} %shard_map.53.after.left), channel_id=1, source_target_pairs={{0,4},{4,0},{1,5},{5,1},{2,6},{6,2},{3,7},{7,3},{8,12},{12,8},{9,1... | collective-permute-start | bytes 245768 | tf_op jit(solution)/shard_map/ppermute | solution.py:248
  22.5 0.2 collective-permute-start.6
  22.6 0.0 collective-permute-done.7.dh_got
  22.6 1.1 %shard_map.55 = (bf16[64,1664]{1,0:T(8,128)(2,1)S(1)}, bf16[64,1664]{1,0:T(8,128)(2,1)S(1)}, bf16[64,1664]{1,0:T(8,128)(2,1)S(1)}, bf16[64,1664]{1,0:T(8,128)(2,1)S(1)}) custom-call(s32[3]{0:T(128)S(1)} %pad_add_fusion.where, bf16[2,128,512]{2,1,0:T(8,128)(2,1)S(1)} %get-tuple-element.35.local, bf16[128,512]{1,0:T(8,128)(2,1)S(1)} %get-tuple-element.42.dh_own, ...), custom_call_target="tpu_custom_call" | custom-call | flops 268435456 | bytes 1048576 | tf_op jit(solution)/shard_map/pallas_call | solution.py:314
  23.7 1.5 %collective-permute-start.8 = (bf16[64,1664]{1,0:T(8,128)(2,1)S(1)}, bf16[64,1664]{1,0:T(8,128)(2,1)S(1)}, u32[]{:S(2)}, u32[]{:S(2)}) collective-permute-start(bf16[64,1664]{1,0:T(8,128)(2,1)S(1)} %get-tuple-element.45), channel_id=1, source_target_pairs={{0,3},{1,2},{2,1},{3,0},{4,7},{5,6},{6,5},{7,4},{8,11},{9,10},{10,... | collective-permute-start | bytes 638984 | tf_op jit(solution)/shard_map/ppermute | solution.py:240
  25.2 1.3 %collective-permute-start.10 = (bf16[64,1664]{1,0:T(8,128)(2,1)S(1)}, bf16[64,1664]{1,0:T(8,128)(2,1)S(1)}, u32[]{:S(2)}, u32[]{:S(2)}) collective-permute-start(bf16[64,1664]{1,0:T(8,128)(2,1)S(1)} %get-tuple-element.47), channel_id=1, source_target_pairs={{0,1},{1,0},{2,3},{3,2},{4,5},{5,4},{6,7},{7,6},{8,9},{9,8},{10,11... | collective-permute-start | bytes 638984 | tf_op jit(solution)/shard_map/ppermute | solution.py:240
  26.5 0.7 %collective-permute-start.11 = (bf16[64,1664]{1,0:T(8,128)(2,1)S(1)}, bf16[64,1664]{1,0:T(8,128)(2,1)S(1)}, u32[]{:S(2)}, u32[]{:S(2)}) collective-permute-start(bf16[64,1664]{1,0:T(8,128)(2,1)S(1)} %get-tuple-element.48), channel_id=1, source_target_pairs={{0,2},{1,3},{2,0},{3,1},{4,6},{5,7},{6,4},{7,5},{8,10},{9,11},{10,... | collective-permute-start | bytes 638984 | tf_op jit(solution)/shard_map/ppermute | solution.py:240
  27.3 0.0 collective-permute-done.9.right
  27.4 5.5 %collective-permute-done.8.right = bf16[64,1664]{1,0:T(8,128)(2,1)S(1)} collective-permute-done((bf16[64,1664]{1,0:T(8,128)(2,1)S(1)}, bf16[64,1664]{1,0:T(8,128)(2,1)S(1)}, u32[]{:S(2)}, u32[]{:S(2)}) %collective-permute-start.8) | collective-permute-done | bytes 213024 | tf_op jit(solution)/shard_map/ppermute | solution.py:240
  32.9 0.1 shard_map.57
  32.9 1.4 %collective-permute-start.14 = (bf16[64,640]{1,0:T(8,128)(2,1)S(1)}, bf16[64,640]{1,0:T(8,128)(2,1)S(1)}, u32[]{:S(2)}, u32[]{:S(2)}) collective-permute-start(bf16[64,640]{1,0:T(8,128)(2,1)S(1)} %get-tuple-element.49.refs_0_), channel_id=1, source_target_pairs={{0,3},{1,2},{2,1},{3,0},{4,7},{5,6},{6,5},{7,4},{8,11},{9,10},{10,... | collective-permute-start | bytes 245768 | tf_op jit(solution)/shard_map/ppermute | solution.py:240
  34.3 1.5 %collective-permute-start.13 = (bf16[64,640]{1,0:T(8,128)(2,1)S(1)}, bf16[64,640]{1,0:T(8,128)(2,1)S(1)}, u32[]{:S(2)}, u32[]{:S(2)}) collective-permute-start(bf16[64,640]{1,0:T(8,128)(2,1)S(1)} %get-tuple-element.49.refs_0_), channel_id=1, source_target_pairs={{0,2},{1,3},{2,0},{3,1},{4,6},{5,7},{6,4},{7,5},{8,10},{9,11},{10,... | collective-permute-start | bytes 245768 | tf_op jit(solution)/shard_map/ppermute | solution.py:240
  35.9 1.1 %collective-permute-done.10 = bf16[64,1664]{1,0:T(8,128)(2,1)S(1)} collective-permute-done((bf16[64,1664]{1,0:T(8,128)(2,1)S(1)}, bf16[64,1664]{1,0:T(8,128)(2,1)S(1)}, u32[]{:S(2)}, u32[]{:S(2)}) %collective-permute-start.10) | collective-permute-done | bytes 213024 | tf_op jit(solution)/shard_map/ppermute | solution.py:240
  37.0 1.8 %collective-permute-start.12 = (bf16[64,640]{1,0:T(8,128)(2,1)S(1)}, bf16[64,640]{1,0:T(8,128)(2,1)S(1)}, u32[]{:S(2)}, u32[]{:S(2)}) collective-permute-start(bf16[64,640]{1,0:T(8,128)(2,1)S(1)} %get-tuple-element.49.refs_0_), channel_id=1, source_target_pairs={{0,1},{1,0},{2,3},{3,2},{4,5},{5,4},{6,7},{7,6},{8,9},{9,8},{10,11... | collective-permute-start | bytes 245768 | tf_op jit(solution)/shard_map/ppermute | solution.py:240
  38.8 0.0 collective-permute-done.11
  38.8 0.1 add_convert_fusion.after.left
  38.8 1.2 %collective-permute-start.15 = (bf16[64,1664]{1,0:T(8,128)(2,1)S(1)}, bf16[64,1664]{1,0:T(8,128)(2,1)S(1)}, u32[]{:S(2)}, u32[]{:S(2)}) collective-permute-start(bf16[64,1664]{1,0:T(8,128)(2,1)S(1)} %add_convert_fusion.after.left), channel_id=1, source_target_pairs={{0,4},{4,0},{1,5},{5,1},{2,6},{6,2},{3,7},{7,3},{8,12},{12,8},{9,1... | collective-permute-start | bytes 638984 | tf_op jit(solution)/shard_map/ppermute | solution.py:248
  40.0 0.0 collective-permute-done.6.other_cot
  40.0 1.3 %shard_map.58.refs_1_ = bf16[2,128,512]{2,1,0:T(8,128)(2,1)} custom-call(s32[3]{0:T(128)S(1)} %pad_add_fusion.where, bf16[128,512]{1,0:T(8,128)(2,1)S(1)} %get-tuple-element.40.own_cot, bf16[128,512]{1,0:T(8,128)(2,1)S(1)} %collective-permute-done.6.other_cot, bf16[64,1664]{1,0:T(8,128)(2,1)S(1)} %add_convert_fusion.after.left), custom_call_target="tpu_custom_call" | custom-call | bytes 1048576 | tf_op jit(solution)/shard_map/pallas_call | solution.py:330
  41.3 0.0 collective-permute-done.14.refs_3_
  41.3 0.0 collective-permute-done.13.refs_2_
  41.3 0.1 collective-permute-done.12.refs_1_
  41.4 4.0 %shard_map.59 = (bf16[512,512]{1,0:T(8,128)(2,1)S(1)}, bf16[512,512]{1,0:T(8,128)(2,1)S(1)}) custom-call(s32[3]{0:T(128)S(1)} %pad_add_fusion.where, bf16[64,640]{1,0:T(8,128)(2,1)S(1)} %get-tuple-element.49.refs_0_, bf16[64,640]{1,0:T(8,128)(2,1)S(1)} %collective-permute-done.12.refs_1_, bf16[64,640]{1,0:T(8,128)(2,1)S(1)} %collective-permute-done.13.refs_2_, ...), custom_call_target="tpu_custom_call" | custom-call | flops 2684354560 | bytes 1048576 | tf_op jit(solution)/shard_map/pallas_call | solution.py:336
  45.4 5.7 %collective-permute-done.15.right = bf16[64,1664]{1,0:T(8,128)(2,1)S(1)} collective-permute-done((bf16[64,1664]{1,0:T(8,128)(2,1)S(1)}, bf16[64,1664]{1,0:T(8,128)(2,1)S(1)}, u32[]{:S(2)}, u32[]{:S(2)}) %collective-permute-start.15) | collective-permute-done | bytes 213024 | tf_op jit(solution)/shard_map/ppermute | solution.py:248
  51.1 0.0 copy-done
  51.1 0.1 shard_map.60
  51.2 0.1 collective-permute-start.18
  51.3 1.8 %collective-permute-start.17 = (bf16[64,640]{1,0:T(8,128)(2,1)S(1)}, bf16[64,640]{1,0:T(8,128)(2,1)S(1)}, u32[]{:S(2)}, u32[]{:S(2)}) collective-permute-start(bf16[64,640]{1,0:T(8,128)(2,1)S(1)} %slice.8.refs_0_), channel_id=1, source_target_pairs={{0,2},{1,3},{2,0},{3,1},{4,6},{5,7},{6,4},{7,5},{8,10},{9,11},{10,... | collective-permute-start | bytes 245768 | tf_op jit(solution)/shard_map/ppermute | solution.py:240
  53.1 1.7 %collective-permute-start.16 = (bf16[64,640]{1,0:T(8,128)(2,1)S(1)}, bf16[64,640]{1,0:T(8,128)(2,1)S(1)}, u32[]{:S(2)}, u32[]{:S(2)}) collective-permute-start(bf16[64,640]{1,0:T(8,128)(2,1)S(1)} %slice.8.refs_0_), channel_id=1, source_target_pairs={{0,1},{1,0},{2,3},{3,2},{4,5},{5,4},{6,7},{7,6},{8,9},{9,8},{10,11... | collective-permute-start | bytes 245768 | tf_op jit(solution)/shard_map/ppermute | solution.py:240
  54.8 0.1 collective-permute-start.21
  54.9 1.8 %collective-permute-start.20 = (bf16[64,1024]{1,0:T(8,128)(2,1)S(1)}, bf16[64,1024]{1,0:T(8,128)(2,1)S(1)}, u32[]{:S(2)}, u32[]{:S(2)}) collective-permute-start(bf16[64,1024]{1,0:T(8,128)(2,1)S(1)} %slice.9.refs_0_), channel_id=1, source_target_pairs={{0,2},{1,3},{2,0},{3,1},{4,6},{5,7},{6,4},{7,5},{8,10},{9,11},{10,... | collective-permute-start | bytes 393224 | tf_op jit(solution)/shard_map/ppermute | solution.py:240
  56.7 0.8 %collective-permute-done.18.refs_3_ = bf16[64,640]{1,0:T(8,128)(2,1)S(1)} collective-permute-done((bf16[64,640]{1,0:T(8,128)(2,1)S(1)}, bf16[64,640]{1,0:T(8,128)(2,1)S(1)}, u32[]{:S(2)}, u32[]{:S(2)}) %collective-permute-start.18) | collective-permute-done | bytes 81952 | tf_op jit(solution)/shard_map/ppermute | solution.py:240
  57.4 0.9 %collective-permute-start.19 = (bf16[64,1024]{1,0:T(8,128)(2,1)S(1)}, bf16[64,1024]{1,0:T(8,128)(2,1)S(1)}, u32[]{:S(2)}, u32[]{:S(2)}) collective-permute-start(bf16[64,1024]{1,0:T(8,128)(2,1)S(1)} %slice.9.refs_0_), channel_id=1, source_target_pairs={{0,1},{1,0},{2,3},{3,2},{4,5},{5,4},{6,7},{7,6},{8,9},{9,8},{10,11... | collective-permute-start | bytes 393224 | tf_op jit(solution)/shard_map/ppermute | solution.py:240
  58.3 0.0 collective-permute-done.17.refs_2_
  58.3 2.4 %collective-permute-done.16.refs_1_ = bf16[64,640]{1,0:T(8,128)(2,1)S(1)} collective-permute-done((bf16[64,640]{1,0:T(8,128)(2,1)S(1)}, bf16[64,640]{1,0:T(8,128)(2,1)S(1)}, u32[]{:S(2)}, u32[]{:S(2)}) %collective-permute-start.16) | collective-permute-done | bytes 81952 | tf_op jit(solution)/shard_map/ppermute | solution.py:240
  60.7 4.0 %shard_map.61 = (bf16[512,512]{1,0:T(8,128)(2,1)S(1)}, bf16[512,512]{1,0:T(8,128)(2,1)S(1)}) custom-call(s32[3]{0:T(128)S(1)} %pad_add_fusion.where, bf16[64,640]{1,0:T(8,128)(2,1)S(1)} %slice.8.refs_0_, bf16[64,640]{1,0:T(8,128)(2,1)S(1)} %collective-permute-done.16.refs_1_, bf16[64,640]{1,0:T(8,128)(2,1)S(1)} %collective-permute-done.17.refs_2_, ...), custom_call_target="tpu_custom_call" | custom-call | flops 2684354560 | bytes 1048576 | tf_op jit(solution)/shard_map/pallas_call | solution.py:336
  64.8 0.0 collective-permute-done.21.refs_3_
  64.8 0.0 collective-permute-done.20.refs_2_
  64.8 0.0 collective-permute-done.19.refs_1_
  64.8 2.9 %shard_map.62 = f32[512,512]{1,0:T(8,128)} custom-call(s32[3]{0:T(128)S(1)} %pad_add_fusion.where, bf16[512,512]{1,0:T(8,128)(2,1)S(1)} %get-tuple-element.50.refs_0_.act_high, bf16[512,512]{1,0:T(8,128)(2,1)S(1)} %get-tuple-element.51.act_low, bf16[512,512]{1,0:T(8,128)(2,1)S(1)} %get-tuple-element.52.out_high, ...), custom_call_target="tpu_custom_call" | custom-call | flops 1342177280 | bytes 1048576 | tf_op jit(solution)/shard_map/pallas_call | solution.py:348
  (5 shorter events, 0.1 us)
Async XLA Ops:
  0.6 2.6 %collective-permute-start = (bf16[512,512]{1,0:T(8,128)(2,1)}, bf16[512,512]{1,0:T(8,128)(2,1)S(1)}, u32[]{:S(2)}, u32[]{:S(2)}) collective-permute-start(bf16[512,512]{1,0:T(8,128)(2,1)} %bitcast.8), channel_id=1, source_target_pairs={{0,8},{8,0},{1,9},{9,1},{2,10},{10,2},{3,11},{11,3},{4,12},{12,4},... | collective-permute-start | bytes 1572872 | tf_op jit(solution)/shard_map/ppermute | solution.py:273
  1.1 2.1 %collective-permute-start.1 = (bf16[2,128,512]{2,1,0:T(8,128)(2,1)}, bf16[2,128,512]{2,1,0:T(8,128)(2,1)S(1)}, u32[]{:S(2)}, u32[]{:S(2)}) collective-permute-start(bf16[2,128,512]{2,1,0:T(8,128)(2,1)} %bitcast.10), channel_id=1, source_target_pairs={{0,8},{8,0},{1,9},{9,1},{2,10},{10,2},{3,11},{11,3},{4,12},{12,4},... | collective-permute-start | bytes 786440 | tf_op jit(solution)/shard_map/ppermute | solution.py:274
  3.3 1.0 %copy-start.1 = (bf16[1,512,512]{2,1,0:T(8,128)(2,1)S(1)}, bf16[1,512,512]{2,1,0:T(8,128)(2,1)}, u32[]{:S(2)}) copy-start(bf16[1,512,512]{2,1,0:T(8,128)(2,1)} %param.4) | copy-start | bytes 1572868
  4.3 0.9 %copy-start.2 = (bf16[1,2,128,512]{3,2,1,0:T(8,128)(2,1)S(1)}, bf16[1,2,128,512]{3,2,1,0:T(8,128)(2,1)}, u32[]{:S(2)}) copy-start(bf16[1,2,128,512]{3,2,1,0:T(8,128)(2,1)} %param.3) | copy-start | bytes 786436
  5.3 0.9 %copy-start.3 = (bf16[2,128,512]{2,1,0:T(8,128)(2,1)S(1)}, bf16[2,128,512]{2,1,0:T(8,128)(2,1)}, u32[]{:S(2)}) copy-start(bf16[2,128,512]{2,1,0:T(8,128)(2,1)} %cot_last.1) | copy-start | bytes 786436
  7.7 7.9 %collective-permute-start.2 = (bf16[128,512]{1,0:T(8,128)(2,1)S(1)}, bf16[128,512]{1,0:T(8,128)(2,1)S(1)}, u32[]{:S(2)}, u32[]{:S(2)}) collective-permute-start(bf16[128,512]{1,0:T(8,128)(2,1)S(1)} %get-tuple-element.31.after), channel_id=1, source_target_pairs={{16,0},{17,1},{18,2},{19,3},{20,4},{21,5},{22,6},{23,7},{24,8},{25... | collective-permute-start | bytes 393224 | tf_op jit(solution)/shard_map/ppermute | solution.py:285
  9.9 6.8 %collective-permute-start.3 = (bf16[64,640]{1,0:T(8,128)(2,1)S(1)}, bf16[64,640]{1,0:T(8,128)(2,1)S(1)}, u32[]{:S(2)}, u32[]{:S(2)}) collective-permute-start(bf16[64,640]{1,0:T(8,128)(2,1)S(1)} %get-tuple-element.37), channel_id=1, source_target_pairs={{0,3},{1,2},{2,1},{3,0},{4,7},{5,6},{6,5},{7,4},{8,11},{9,10},{10,... | collective-permute-start | bytes 245768 | tf_op jit(solution)/shard_map/ppermute | solution.py:240
  13.8 4.5 %collective-permute-start.4 = (bf16[64,640]{1,0:T(8,128)(2,1)S(1)}, bf16[64,640]{1,0:T(8,128)(2,1)S(1)}, u32[]{:S(2)}, u32[]{:S(2)}) collective-permute-start(bf16[64,640]{1,0:T(8,128)(2,1)S(1)} %get-tuple-element.38), channel_id=1, source_target_pairs={{0,1},{1,0},{2,3},{3,2},{4,5},{5,4},{6,7},{7,6},{8,9},{9,8},{10,11... | collective-permute-start | bytes 245768 | tf_op jit(solution)/shard_map/ppermute | solution.py:240
  14.4 4.4 %collective-permute-start.5 = (bf16[64,640]{1,0:T(8,128)(2,1)S(1)}, bf16[64,640]{1,0:T(8,128)(2,1)S(1)}, u32[]{:S(2)}, u32[]{:S(2)}) collective-permute-start(bf16[64,640]{1,0:T(8,128)(2,1)S(1)} %get-tuple-element.39), channel_id=1, source_target_pairs={{0,2},{1,3},{2,0},{3,1},{4,6},{5,7},{6,4},{7,5},{8,10},{9,11},{10,... | collective-permute-start | bytes 245768 | tf_op jit(solution)/shard_map/ppermute | solution.py:240
  19.7 2.9 %collective-permute-start.7 = (bf16[128,512]{1,0:T(8,128)(2,1)S(1)}, bf16[128,512]{1,0:T(8,128)(2,1)S(1)}, u32[]{:S(2)}, u32[]{:S(2)}) collective-permute-start(bf16[128,512]{1,0:T(8,128)(2,1)S(1)} %get-tuple-element.43), channel_id=1, source_target_pairs={{0,8},{8,0},{1,9},{9,1},{2,10},{10,2},{3,11},{11,3},{4,12},{12,4},... | collective-permute-start | bytes 393224 | tf_op jit(solution)/shard_map/ppermute | solution.py:311
  19.8 7.5 %collective-permute-start.9 = (bf16[64,640]{1,0:T(8,128)(2,1)S(1)}, bf16[64,640]{1,0:T(8,128)(2,1)S(1)}, u32[]{:S(2)}, u32[]{:S(2)}) collective-permute-start(bf16[64,640]{1,0:T(8,128)(2,1)S(1)} %shard_map.53.after.left), channel_id=1, source_target_pairs={{0,4},{4,0},{1,5},{5,1},{2,6},{6,2},{3,7},{7,3},{8,12},{12,8},{9,1... | collective-permute-start | bytes 245768 | tf_op jit(solution)/shard_map/ppermute | solution.py:248
  22.5 17.6 %collective-permute-start.6 = (bf16[128,512]{1,0:T(8,128)(2,1)S(1)}, bf16[128,512]{1,0:T(8,128)(2,1)S(1)}, u32[]{:S(2)}, u32[]{:S(2)}) collective-permute-start(bf16[128,512]{1,0:T(8,128)(2,1)S(1)} %get-tuple-element.41), channel_id=1, source_target_pairs={{0,8},{8,0},{1,9},{9,1},{2,10},{10,2},{3,11},{11,3},{4,12},{12,4},... | collective-permute-start | bytes 393224 | tf_op jit(solution)/shard_map/ppermute | solution.py:312
  23.7 9.1 %collective-permute-start.8 = (bf16[64,1664]{1,0:T(8,128)(2,1)S(1)}, bf16[64,1664]{1,0:T(8,128)(2,1)S(1)}, u32[]{:S(2)}, u32[]{:S(2)}) collective-permute-start(bf16[64,1664]{1,0:T(8,128)(2,1)S(1)} %get-tuple-element.45), channel_id=1, source_target_pairs={{0,3},{1,2},{2,1},{3,0},{4,7},{5,6},{6,5},{7,4},{8,11},{9,10},{10,... | collective-permute-start | bytes 638984 | tf_op jit(solution)/shard_map/ppermute | solution.py:240
  25.2 11.8 %collective-permute-start.10 = (bf16[64,1664]{1,0:T(8,128)(2,1)S(1)}, bf16[64,1664]{1,0:T(8,128)(2,1)S(1)}, u32[]{:S(2)}, u32[]{:S(2)}) collective-permute-start(bf16[64,1664]{1,0:T(8,128)(2,1)S(1)} %get-tuple-element.47), channel_id=1, source_target_pairs={{0,1},{1,0},{2,3},{3,2},{4,5},{5,4},{6,7},{7,6},{8,9},{9,8},{10,11... | collective-permute-start | bytes 638984 | tf_op jit(solution)/shard_map/ppermute | solution.py:240
  26.5 12.2 %collective-permute-start.11 = (bf16[64,1664]{1,0:T(8,128)(2,1)S(1)}, bf16[64,1664]{1,0:T(8,128)(2,1)S(1)}, u32[]{:S(2)}, u32[]{:S(2)}) collective-permute-start(bf16[64,1664]{1,0:T(8,128)(2,1)S(1)} %get-tuple-element.48), channel_id=1, source_target_pairs={{0,2},{1,3},{2,0},{3,1},{4,6},{5,7},{6,4},{7,5},{8,10},{9,11},{10,... | collective-permute-start | bytes 638984 | tf_op jit(solution)/shard_map/ppermute | solution.py:240
  32.9 8.4 %collective-permute-start.14 = (bf16[64,640]{1,0:T(8,128)(2,1)S(1)}, bf16[64,640]{1,0:T(8,128)(2,1)S(1)}, u32[]{:S(2)}, u32[]{:S(2)}) collective-permute-start(bf16[64,640]{1,0:T(8,128)(2,1)S(1)} %get-tuple-element.49.refs_0_), channel_id=1, source_target_pairs={{0,3},{1,2},{2,1},{3,0},{4,7},{5,6},{6,5},{7,4},{8,11},{9,10},{10,... | collective-permute-start | bytes 245768 | tf_op jit(solution)/shard_map/ppermute | solution.py:240
  34.3 7.0 %collective-permute-start.13 = (bf16[64,640]{1,0:T(8,128)(2,1)S(1)}, bf16[64,640]{1,0:T(8,128)(2,1)S(1)}, u32[]{:S(2)}, u32[]{:S(2)}) collective-permute-start(bf16[64,640]{1,0:T(8,128)(2,1)S(1)} %get-tuple-element.49.refs_0_), channel_id=1, source_target_pairs={{0,2},{1,3},{2,0},{3,1},{4,6},{5,7},{6,4},{7,5},{8,10},{9,11},{10,... | collective-permute-start | bytes 245768 | tf_op jit(solution)/shard_map/ppermute | solution.py:240
  37.0 4.4 %collective-permute-start.12 = (bf16[64,640]{1,0:T(8,128)(2,1)S(1)}, bf16[64,640]{1,0:T(8,128)(2,1)S(1)}, u32[]{:S(2)}, u32[]{:S(2)}) collective-permute-start(bf16[64,640]{1,0:T(8,128)(2,1)S(1)} %get-tuple-element.49.refs_0_), channel_id=1, source_target_pairs={{0,1},{1,0},{2,3},{3,2},{4,5},{5,4},{6,7},{7,6},{8,9},{9,8},{10,11... | collective-permute-start | bytes 245768 | tf_op jit(solution)/shard_map/ppermute | solution.py:240
  38.8 12.3 %collective-permute-start.15 = (bf16[64,1664]{1,0:T(8,128)(2,1)S(1)}, bf16[64,1664]{1,0:T(8,128)(2,1)S(1)}, u32[]{:S(2)}, u32[]{:S(2)}) collective-permute-start(bf16[64,1664]{1,0:T(8,128)(2,1)S(1)} %add_convert_fusion.after.left), channel_id=1, source_target_pairs={{0,4},{4,0},{1,5},{5,1},{2,6},{6,2},{3,7},{7,3},{8,12},{12,8},{9,1... | collective-permute-start | bytes 638984 | tf_op jit(solution)/shard_map/ppermute | solution.py:248
  41.3 9.8 %copy-start = (bf16[2,128,512]{2,1,0:T(8,128)(2,1)S(1)}, bf16[2,128,512]{2,1,0:T(8,128)(2,1)}, u32[]{:S(2)}) copy-start(bf16[2,128,512]{2,1,0:T(8,128)(2,1)} %shard_map.58.refs_1_) | copy-start | bytes 786436
  51.2 6.2 %collective-permute-start.18 = (bf16[64,640]{1,0:T(8,128)(2,1)S(1)}, bf16[64,640]{1,0:T(8,128)(2,1)S(1)}, u32[]{:S(2)}, u32[]{:S(2)}) collective-permute-start(bf16[64,640]{1,0:T(8,128)(2,1)S(1)} %slice.8.refs_0_), channel_id=1, source_target_pairs={{0,3},{1,2},{2,1},{3,0},{4,7},{5,6},{6,5},{7,4},{8,11},{9,10},{10,... | collective-permute-start | bytes 245768 | tf_op jit(solution)/shard_map/ppermute | solution.py:240
  51.3 7.1 %collective-permute-start.17 = (bf16[64,640]{1,0:T(8,128)(2,1)S(1)}, bf16[64,640]{1,0:T(8,128)(2,1)S(1)}, u32[]{:S(2)}, u32[]{:S(2)}) collective-permute-start(bf16[64,640]{1,0:T(8,128)(2,1)S(1)} %slice.8.refs_0_), channel_id=1, source_target_pairs={{0,2},{1,3},{2,0},{3,1},{4,6},{5,7},{6,4},{7,5},{8,10},{9,11},{10,... | collective-permute-start | bytes 245768 | tf_op jit(solution)/shard_map/ppermute | solution.py:240
  53.1 7.7 %collective-permute-start.16 = (bf16[64,640]{1,0:T(8,128)(2,1)S(1)}, bf16[64,640]{1,0:T(8,128)(2,1)S(1)}, u32[]{:S(2)}, u32[]{:S(2)}) collective-permute-start(bf16[64,640]{1,0:T(8,128)(2,1)S(1)} %slice.8.refs_0_), channel_id=1, source_target_pairs={{0,1},{1,0},{2,3},{3,2},{4,5},{5,4},{6,7},{7,6},{8,9},{9,8},{10,11... | collective-permute-start | bytes 245768 | tf_op jit(solution)/shard_map/ppermute | solution.py:240
  54.8 10.0 %collective-permute-start.21 = (bf16[64,1024]{1,0:T(8,128)(2,1)S(1)}, bf16[64,1024]{1,0:T(8,128)(2,1)S(1)}, u32[]{:S(2)}, u32[]{:S(2)}) collective-permute-start(bf16[64,1024]{1,0:T(8,128)(2,1)S(1)} %slice.9.refs_0_), channel_id=1, source_target_pairs={{0,3},{1,2},{2,1},{3,0},{4,7},{5,6},{6,5},{7,4},{8,11},{9,10},{10,... | collective-permute-start | bytes 393224 | tf_op jit(solution)/shard_map/ppermute | solution.py:240
  54.9 9.9 %collective-permute-start.20 = (bf16[64,1024]{1,0:T(8,128)(2,1)S(1)}, bf16[64,1024]{1,0:T(8,128)(2,1)S(1)}, u32[]{:S(2)}, u32[]{:S(2)}) collective-permute-start(bf16[64,1024]{1,0:T(8,128)(2,1)S(1)} %slice.9.refs_0_), channel_id=1, source_target_pairs={{0,2},{1,3},{2,0},{3,1},{4,6},{5,7},{6,4},{7,5},{8,10},{9,11},{10,... | collective-permute-start | bytes 393224 | tf_op jit(solution)/shard_map/ppermute | solution.py:240
  57.4 7.4 %collective-permute-start.19 = (bf16[64,1024]{1,0:T(8,128)(2,1)S(1)}, bf16[64,1024]{1,0:T(8,128)(2,1)S(1)}, u32[]{:S(2)}, u32[]{:S(2)}) collective-permute-start(bf16[64,1024]{1,0:T(8,128)(2,1)S(1)} %slice.9.refs_0_), channel_id=1, source_target_pairs={{0,1},{1,0},{2,3},{3,2},{4,5},{5,4},{6,7},{7,6},{8,9},{9,8},{10,11... | collective-permute-start | bytes 393224 | tf_op jit(solution)/shard_map/ppermute | solution.py:240

commit v9 on v8

--- a/solution.py
+++ b/solution.py
@@ -120,7 +120,7 @@
     )
 
 
-def cot_kernel(where, own_cot, other_cot, after, result):
+def cot_kernel(where, own_cot, other_cot, result):
     result[where[0]] = own_cot[...]
     result[1 - where[0]] = other_cot[...]
 
@@ -155,7 +155,7 @@
     refs[-1][...] = (left[...].astype(F32) + right[...].astype(F32)).astype(BF16)
 
 
-def begin_kernel(left, right, act, result, act_copy):
+def begin_kernel(left, right, act, after, result, act_copy):
     act_copy[...] = act[...]
     result[...] = left[...].astype(F32) + right[...].astype(F32)
 
@@ -270,6 +270,9 @@
     def array(*shape, dtype=BF16):
         return jax.ShapeDtypeStruct(shape, dtype)
 
+    def near_copy(value):
+        return jnp.where(core > 1, jnp.zeros_like(value), value)
+
     partner = lax.ppermute(weight, "core", SWAP)
     partner_local = lax.ppermute(local, "core", SWAP)
     block = array(rows, width)
@@ -279,7 +282,7 @@
         8 * rows * width**2,
         [array(width, width), array(micro, rows, width), block, slope, slope, block],
         [SMEM] + [VMEM] * 5,
-    )(where, weight, local, cot_last, partner, partner_local)
+    )(where, near_copy(weight), near_copy(local), near_copy(cot_last), partner, partner_local)
     first = down
     for turn in range(1, pairs):
         upstream = lax.ppermute(down, "row", [(r, r - 1) for r in range(1, pairs)])
@@ -319,30 +322,28 @@
         [pltpu.VMEM((tokens, width), BF16)] * 2
         + [pltpu.VMEM((GROUP, size // 2, factor + 2 * width), BF16)],
     )(where, kept, own_dh, got_dh)
+    cot = call(cot_kernel, 0, array(micro, rows, width), [SMEM, VMEM, VMEM])(where, own_cot, other_cot)
     pieces = send(parts)
     begun, act_part = call(
         begin_kernel,
         0,
         [array(*parts[0].shape, dtype=F32), array(size // 2, factor)],
-        [VMEM] * 3,
-    )(pieces[0], pieces[3], exchange(act_sum, flops=24 * width**3))
+        [VMEM] * 3 + [ANY],
+    )(pieces[0], pieces[3], exchange(act_sum, flops=24 * width**3), cot)
     total = (begun + pieces[1].astype(F32) + pieces[2].astype(F32)).astype(BF16)
-    cot = call(cot_kernel, 0, array(micro, rows, width), [SMEM, VMEM, VMEM, ANY])(
-        where, own_cot, other_cot, total
-    )
     act = send([act_part] * GROUP)
 
-    def inverse(pieces):
+    def inverse(pieces, flops):
         return call(
             functools.partial(inverse_kernel, count),
-            20 * width**3,
+            flops,
             [array(width, width)] * 2,
             [SMEM] + [VMEM] * GROUP,
             [pltpu.VMEM((GROUP, size // 2, factor), F32), pltpu.VMEM((width, width), BF16)],
         )(where, *pieces)
 
-    act_inv = inverse(act)
-    total = exchange(total, (act_inv[0], cot))
+    act_inv = inverse(act, 0)
+    total = exchange(total, (act_inv[0],))
     out = send([total[:, :factor]] * GROUP)
     grad = send([total[:, factor:]] * GROUP)
     update = call(
@@ -356,7 +357,7 @@
             pltpu.SemaphoreType.DMA((2,)),
         ],
         HBM,
-    )(where, *act_inv, *inverse(out), *grad)
+    )(where, *act_inv, *inverse(out, 20 * width**3), *grad)
     return (cot[None], update[None])
 
 

time: 68 us -> 64.8 us (0.953)
  waiting for transfers between devices: 21 us -> 19 us
  local copies, waits for them, and re-layouts: 2.96 us -> 0.98 us
  other arithmetic: 0.15 us -> 1.33 us
    ppermute x2, waiting for transfers between devices: 5.73 us -> 0.06 us  [exchange(): got = lax.ppermute(value, 'far', route)]
    ppermute x15, waiting for transfers between devices: 12.2 us -> 17 us  [send(): lax.ppermute(parts[step], ('near', 'side'), [(i, i ^ step) for i in range...]
    unnamed x8 -> x6, local copies, waits for them, and re-layouts: 2.94 us -> 0.96 us
    ppermute x1, waiting for transfers between devices: 1.97 us -> 0.02 us  [body(): partner_local = lax.ppermute(local, 'core', SWAP)]
    select_n x0 -> x2, other arithmetic: none -> 1.18 us  [near_copy(): return jnp.where(core > 1, jnp.zeros_like(value), value)]
    ppermute x1, waiting for transfers between devices: 0.01 us -> 0.75 us  [body(): partner = lax.ppermute(weight, 'core', SWAP)]
  transfers between devices with their start and end apart: 22 -> 22, of which waited for: 11 -> 12; matrix products, arithmetic and copies ran while one was open for 0% -> 2% of each run, Pallas kernels for 18% -> 19%
where the time goes in v9:
time: 64.8 us; the launch traced here: 64.6 us
  starting transfers between devices  24.9 us (38%)
  waiting for transfers between devices  19 us (29%)
  Pallas kernels  17.6 us (27%)
  other arithmetic  1.33 us (2%)
  local copies, waits for them, and re-layouts  0.98 us (2%)
  between operations  0.8 us (1%)
    ppermute x15, starting transfers between devices, send(): lax.ppermute(parts[step], ('near', 'side'), [(i, i ^ step) for i in range...  19.3 us
    ppermute x15, waiting for transfers between devices, send(): lax.ppermute(parts[step], ('near', 'side'), [(i, i ^ step) for i in range...  17 us
    pallas_call x2, Pallas kernels, inverse(): call(functools.partial(inverse_kernel, count), flops, [array(width, width...  8.06 us
    ppermute x2, starting transfers between devices, exchange(): got = lax.ppermute(value, 'far', route)  3.48 us
    pallas_call x1, Pallas kernels, body(): call(update_kernel, 10 * width ** 3, array(width, width, dtype=F32), [SME...  2.92 us
    pallas_call x1, Pallas kernels, body(): call(first_kernel, 8 * rows * width ** 2, [array(width, width), array(mic...  1.46 us
  transfers between devices with their start and end apart: 22, of which 12 were waited for; matrix products, arithmetic and copies ran while one was open for 2% of the time, Pallas kernels for 19%

profile of v9, /device:TPU:0, one launch (start us, length us, event | category | flops | bytes accessed | tf_op | source)
XLA Modules:
  0.0 64.6 jit_solution(539727162692909927)
XLA Ops:
  0.6 0.5 collective-permute-start.1
  1.1 0.1 collective-permute-start
  1.2 0.0 copy-start.1
  1.2 0.0 copy-start.2
  1.2 1.1 %broadcast_select_fusion.weight = bf16[512,512]{1,0:T(8,128)(2,1)S(1)} fusion(pred[]{:T(512)S(6)} %gt.2, bf16[1,512,512]{2,1,0:T(8,128)(2,1)} %param.4), kind=kLoop, calls=%fused_computation | loop fusion | flops 262144 | bytes 1048577 | tf_op jit(solution)/shard_map/jit(_where)/select_n | solution.py:274
  2.4 0.1 pad_add_fusion.where
  2.5 0.0 copy-done.1
  2.5 0.0 copy-done.2
  2.5 0.0 collective-permute-done.1.partner_local
  2.5 0.7 %collective-permute-done.partner = bf16[512,512]{1,0:T(8,128)(2,1)S(1)} collective-permute-done((bf16[512,512]{1,0:T(8,128)(2,1)}, bf16[512,512]{1,0:T(8,128)(2,1)S(1)}, u32[]{:S(2)}, u32[]{:S(2)}) %collective-permute-start) | collective-permute-done | bytes 524320 | tf_op jit(solution)/shard_map/ppermute | solution.py:276
  3.3 1.5 %shard_map.50 = (bf16[512,512]{1,0:T(8,128)(2,1)S(1)}, bf16[2,128,512]{2,1,0:T(8,128)(2,1)S(1)}, bf16[128,512]{1,0:T(8,128)(2,1)S(1)}, f32[128,512]{1,0:T(8,128)...) custom-call(s32[3]{0:T(128)S(1)} %pad_add_fusion.where, bf16[512,512]{1,0:T(8,128)(2,1)S(1)} %broadcast_select_fusion.weight, ...), custom_call_target="tpu_custom_call" | custom-call | flops 268435456 | bytes 1048576 | tf_op jit(solution)/shard_map/pallas_call | solution.py:280
  4.7 1.3 %collective-permute-start.2 = (bf16[128,512]{1,0:T(8,128)(2,1)S(1)}, bf16[128,512]{1,0:T(8,128)(2,1)S(1)}, u32[]{:S(2)}, u32[]{:S(2)}) collective-permute-start(bf16[128,512]{1,0:T(8,128)(2,1)S(1)} %get-tuple-element.31.after), channel_id=1, source_target_pairs={{16,0},{17,1},{18,2},{19,3},{20,4},{21,5},{22,6},{23,7},{24,8},{25... | collective-permute-start | bytes 393224 | tf_op jit(solution)/shard_map/ppermute | solution.py:288
  6.0 0.9 %shard_map.52 = (bf16[64,640]{1,0:T(8,128)(2,1)S(1)}, bf16[64,640]{1,0:T(8,128)(2,1)S(1)}, bf16[64,640]{1,0:T(8,128)(2,1)S(1)}, bf16[64,640]{1,0:T(8,128)(2,1)S(1)}) custom-call(s32[3]{0:T(128)S(1)} %pad_add_fusion.where, bf16[2,128,512]{2,1,0:T(8,128)(2,1)S(1)} %get-tuple-element.35.local, bf16[128,512]{1,0:T(8,128)(2,1)S(1)} %get-tuple-element.31.after), custom_call_target="tpu_custom_call" | custom-call | flops 134217728 | bytes 1048576 | tf_op jit(solution)/shard_map/pallas_call | solution.py:296
  6.9 3.9 %collective-permute-start.3 = (bf16[64,640]{1,0:T(8,128)(2,1)S(1)}, bf16[64,640]{1,0:T(8,128)(2,1)S(1)}, u32[]{:S(2)}, u32[]{:S(2)}) collective-permute-start(bf16[64,640]{1,0:T(8,128)(2,1)S(1)} %get-tuple-element.37), channel_id=1, source_target_pairs={{0,3},{1,2},{2,1},{3,0},{4,7},{5,6},{6,5},{7,4},{8,11},{9,10},{10,... | collective-permute-start | bytes 245768 | tf_op jit(solution)/shard_map/ppermute | solution.py:240
  10.9 0.5 collective-permute-start.4
  11.4 0.1 collective-permute-start.5
  11.5 1.2 %collective-permute-done.2.arrived = bf16[128,512]{1,0:T(8,128)(2,1)S(1)} collective-permute-done((bf16[128,512]{1,0:T(8,128)(2,1)S(1)}, bf16[128,512]{1,0:T(8,128)(2,1)S(1)}, u32[]{:S(2)}, u32[]{:S(2)}) %collective-permute-start.2) | collective-permute-done | bytes 131104 | tf_op jit(solution)/shard_map/ppermute | solution.py:288
  12.7 0.9 %shard_map.51 = (bf16[128,512]{1,0:T(8,128)(2,1)S(1)}, bf16[128,512]{1,0:T(8,128)(2,1)S(1)}) custom-call(s32[3]{0:T(128)S(1)} %pad_add_fusion.where, bf16[512,512]{1,0:T(8,128)(2,1)S(1)} %get-tuple-element.28.own, bf16[512,512]{1,0:T(8,128)(2,1)S(1)} %collective-permute-done.partner, f32[128,512]{1,0:T(8,128)S(1)} %get-tuple-element.29.slope_own, ...), custom_call_target="tpu_custom_call" | custom-call | flops 2147483648 | bytes 1048576 | tf_op jit(solution)/shard_map/pallas_call | solution.py:305
  13.6 0.1 collective-permute-done.3.refs_1_
  13.7 1.7 %collective-permute-done.4.refs_2_ = bf16[64,640]{1,0:T(8,128)(2,1)S(1)} collective-permute-done((bf16[64,640]{1,0:T(8,128)(2,1)S(1)}, bf16[64,640]{1,0:T(8,128)(2,1)S(1)}, u32[]{:S(2)}, u32[]{:S(2)}) %collective-permute-start.4) | collective-permute-done | bytes 81952 | tf_op jit(solution)/shard_map/ppermute | solution.py:240
  15.4 0.5 collective-permute-done.5.refs_3_
  15.9 0.9 %shard_map.54 = (bf16[128,512]{1,0:T(8,128)(2,1)S(1)}, bf16[128,512]{1,0:T(8,128)(2,1)S(1)}, bf16[128,512]{1,0:T(8,128)(2,1)S(1)}, bf16[128,512]{1,0:T(8,128)(2,1)S(1)}) custom-call(s32[3]{0:T(128)S(1)} %pad_add_fusion.where, bf16[512,512]{1,0:T(8,128)(2,1)S(1)} %get-tuple-element.28.own, bf16[512,512]{1,0:T(8,128)(2,1)S(1)} %collective-permute-done.partner, ...), custom_call_target="tpu_custom_call" | custom-call | flops 134217728 | bytes 1048576 | tf_op jit(solution)/shard_map/pallas_call | solution.py:311
  16.8 0.1 collective-permute-start.7
  16.9 2.7 %collective-permute-start.9 = (bf16[64,640]{1,0:T(8,128)(2,1)S(1)}, bf16[64,640]{1,0:T(8,128)(2,1)S(1)}, u32[]{:S(2)}, u32[]{:S(2)}) collective-permute-start(bf16[64,640]{1,0:T(8,128)(2,1)S(1)} %shard_map.53.after.left), channel_id=1, source_target_pairs={{0,4},{4,0},{1,5},{5,1},{2,6},{6,2},{3,7},{7,3},{8,12},{12,8},{9,1... | collective-permute-start | bytes 245768 | tf_op jit(solution)/shard_map/ppermute | solution.py:248
  19.5 0.2 collective-permute-start.6
  19.7 0.0 collective-permute-done.7.dh_got
  19.7 1.1 %shard_map.56 = (bf16[64,1664]{1,0:T(8,128)(2,1)S(1)}, bf16[64,1664]{1,0:T(8,128)(2,1)S(1)}, bf16[64,1664]{1,0:T(8,128)(2,1)S(1)}, bf16[64,1664]{1,0:T(8,128)(2,1)S(1)}) custom-call(s32[3]{0:T(128)S(1)} %pad_add_fusion.where, bf16[2,128,512]{2,1,0:T(8,128)(2,1)S(1)} %get-tuple-element.35.local, bf16[128,512]{1,0:T(8,128)(2,1)S(1)} %get-tuple-element.42.dh_own, ...), custom_call_target="tpu_custom_call" | custom-call | flops 268435456 | bytes 1048576 | tf_op jit(solution)/shard_map/pallas_call | solution.py:317
  20.8 1.5 %collective-permute-start.8 = (bf16[64,1664]{1,0:T(8,128)(2,1)S(1)}, bf16[64,1664]{1,0:T(8,128)(2,1)S(1)}, u32[]{:S(2)}, u32[]{:S(2)}) collective-permute-start(bf16[64,1664]{1,0:T(8,128)(2,1)S(1)} %get-tuple-element.45), channel_id=1, source_target_pairs={{0,3},{1,2},{2,1},{3,0},{4,7},{5,6},{6,5},{7,4},{8,11},{9,10},{10,... | collective-permute-start | bytes 638984 | tf_op jit(solution)/shard_map/ppermute | solution.py:240
  22.2 1.3 %collective-permute-start.13 = (bf16[64,1664]{1,0:T(8,128)(2,1)S(1)}, bf16[64,1664]{1,0:T(8,128)(2,1)S(1)}, u32[]{:S(2)}, u32[]{:S(2)}) collective-permute-start(bf16[64,1664]{1,0:T(8,128)(2,1)S(1)} %get-tuple-element.50), channel_id=1, source_target_pairs={{0,1},{1,0},{2,3},{3,2},{4,5},{5,4},{6,7},{7,6},{8,9},{9,8},{10,11... | collective-permute-start | bytes 638984 | tf_op jit(solution)/shard_map/ppermute | solution.py:240
  23.6 0.7 %collective-permute-start.14 = (bf16[64,1664]{1,0:T(8,128)(2,1)S(1)}, bf16[64,1664]{1,0:T(8,128)(2,1)S(1)}, u32[]{:S(2)}, u32[]{:S(2)}) collective-permute-start(bf16[64,1664]{1,0:T(8,128)(2,1)S(1)} %get-tuple-element.51), channel_id=1, source_target_pairs={{0,2},{1,3},{2,0},{3,1},{4,6},{5,7},{6,4},{7,5},{8,10},{9,11},{10,... | collective-permute-start | bytes 638984 | tf_op jit(solution)/shard_map/ppermute | solution.py:240
  24.3 0.1 collective-permute-done.9.right
  24.4 0.0 collective-permute-done.6.other_cot
  24.4 1.3 %shard_map.55.after = bf16[2,128,512]{2,1,0:T(8,128)(2,1)} custom-call(s32[3]{0:T(128)S(1)} %pad_add_fusion.where, bf16[128,512]{1,0:T(8,128)(2,1)S(1)} %get-tuple-element.40.own_cot, bf16[128,512]{1,0:T(8,128)(2,1)S(1)} %collective-permute-done.6.other_cot), custom_call_target="tpu_custom_call" | custom-call | bytes 1048576 | tf_op jit(solution)/shard_map/pallas_call | solution.py:325
  25.7 4.2 %collective-permute-done.8.right = bf16[64,1664]{1,0:T(8,128)(2,1)S(1)} collective-permute-done((bf16[64,1664]{1,0:T(8,128)(2,1)S(1)}, bf16[64,1664]{1,0:T(8,128)(2,1)S(1)}, u32[]{:S(2)}, u32[]{:S(2)}) %collective-permute-start.8) | collective-permute-done | bytes 213024 | tf_op jit(solution)/shard_map/ppermute | solution.py:240
  29.9 0.0 copy-start
  29.9 0.9 %copy-done = bf16[2,128,512]{2,1,0:T(8,128)(2,1)S(1)} copy-done((bf16[2,128,512]{2,1,0:T(8,128)(2,1)S(1)}, bf16[2,128,512]{2,1,0:T(8,128)(2,1)}, u32[]{:S(2)}) %copy-start) | copy-done | bytes 262168
  30.8 0.1 shard_map.58
  30.9 3.1 %collective-permute-done.13 = bf16[64,1664]{1,0:T(8,128)(2,1)S(1)} collective-permute-done((bf16[64,1664]{1,0:T(8,128)(2,1)S(1)}, bf16[64,1664]{1,0:T(8,128)(2,1)S(1)}, u32[]{:S(2)}, u32[]{:S(2)}) %collective-permute-start.13) | collective-permute-done | bytes 213024 | tf_op jit(solution)/shard_map/ppermute | solution.py:240
  34.0 0.0 collective-permute-done.14
  34.0 0.1 add_convert_fusion.left
  34.1 0.8 %collective-permute-start.15 = (bf16[64,1664]{1,0:T(8,128)(2,1)S(1)}, bf16[64,1664]{1,0:T(8,128)(2,1)S(1)}, u32[]{:S(2)}, u32[]{:S(2)}) collective-permute-start(bf16[64,1664]{1,0:T(8,128)(2,1)S(1)} %add_convert_fusion.left), channel_id=1, source_target_pairs={{0,4},{4,0},{1,5},{5,1},{2,6},{6,2},{3,7},{7,3},{8,12},{12,8},{9,1... | collective-permute-start | bytes 638984 | tf_op jit(solution)/shard_map/ppermute | solution.py:248
  34.9 1.9 %collective-permute-start.12 = (bf16[64,640]{1,0:T(8,128)(2,1)S(1)}, bf16[64,640]{1,0:T(8,128)(2,1)S(1)}, u32[]{:S(2)}, u32[]{:S(2)}) collective-permute-start(bf16[64,640]{1,0:T(8,128)(2,1)S(1)} %get-tuple-element.46.refs_0_), channel_id=1, source_target_pairs={{0,3},{1,2},{2,1},{3,0},{4,7},{5,6},{6,5},{7,4},{8,11},{9,10},{10,... | collective-permute-start | bytes 245768 | tf_op jit(solution)/shard_map/ppermute | solution.py:240
  36.8 1.0 %collective-permute-start.11 = (bf16[64,640]{1,0:T(8,128)(2,1)S(1)}, bf16[64,640]{1,0:T(8,128)(2,1)S(1)}, u32[]{:S(2)}, u32[]{:S(2)}) collective-permute-start(bf16[64,640]{1,0:T(8,128)(2,1)S(1)} %get-tuple-element.46.refs_0_), channel_id=1, source_target_pairs={{0,2},{1,3},{2,0},{3,1},{4,6},{5,7},{6,4},{7,5},{8,10},{9,11},{10,... | collective-permute-start | bytes 245768 | tf_op jit(solution)/shard_map/ppermute | solution.py:240
  37.8 0.6 collective-permute-start.10
  38.4 3.8 %collective-permute-done.12.refs_3_ = bf16[64,640]{1,0:T(8,128)(2,1)S(1)} collective-permute-done((bf16[64,640]{1,0:T(8,128)(2,1)S(1)}, bf16[64,640]{1,0:T(8,128)(2,1)S(1)}, u32[]{:S(2)}, u32[]{:S(2)}) %collective-permute-start.12) | collective-permute-done | bytes 81952 | tf_op jit(solution)/shard_map/ppermute | solution.py:240
  42.2 0.9 %collective-permute-done.11.refs_2_ = bf16[64,640]{1,0:T(8,128)(2,1)S(1)} collective-permute-done((bf16[64,640]{1,0:T(8,128)(2,1)S(1)}, bf16[64,640]{1,0:T(8,128)(2,1)S(1)}, u32[]{:S(2)}, u32[]{:S(2)}) %collective-permute-start.11) | collective-permute-done | bytes 81952 | tf_op jit(solution)/shard_map/ppermute | solution.py:240
  43.1 0.0 collective-permute-done.10.refs_1_
  43.1 4.0 %shard_map.59 = (bf16[512,512]{1,0:T(8,128)(2,1)S(1)}, bf16[512,512]{1,0:T(8,128)(2,1)S(1)}) custom-call(s32[3]{0:T(128)S(1)} %pad_add_fusion.where, bf16[64,640]{1,0:T(8,128)(2,1)S(1)} %get-tuple-element.46.refs_0_, bf16[64,640]{1,0:T(8,128)(2,1)S(1)} %collective-permute-done.10.refs_1_, bf16[64,640]{1,0:T(8,128)(2,1)S(1)} %collective-permute-done.11.refs_2_, ...), custom_call_target="tpu_custom_call" | custom-call | bytes 1048576 | tf_op jit(solution)/shard_map/pallas_call | solution.py:337
  47.1 0.0 collective-permute-done.15.right
  47.1 0.1 shard_map.60
  47.2 3.5 %collective-permute-start.18 = (bf16[64,640]{1,0:T(8,128)(2,1)S(1)}, bf16[64,640]{1,0:T(8,128)(2,1)S(1)}, u32[]{:S(2)}, u32[]{:S(2)}) collective-permute-start(bf16[64,640]{1,0:T(8,128)(2,1)S(1)} %slice.8.refs_0_), channel_id=1, source_target_pairs={{0,3},{1,2},{2,1},{3,0},{4,7},{5,6},{6,5},{7,4},{8,11},{9,10},{10,... | collective-permute-start | bytes 245768 | tf_op jit(solution)/shard_map/ppermute | solution.py:240
  50.7 0.0 collective-permute-start.17
  50.7 0.6 collective-permute-start.16
  51.3 2.9 %collective-permute-start.21 = (bf16[64,1024]{1,0:T(8,128)(2,1)S(1)}, bf16[64,1024]{1,0:T(8,128)(2,1)S(1)}, u32[]{:S(2)}, u32[]{:S(2)}) collective-permute-start(bf16[64,1024]{1,0:T(8,128)(2,1)S(1)} %slice.9.refs_0_), channel_id=1, source_target_pairs={{0,3},{1,2},{2,1},{3,0},{4,7},{5,6},{6,5},{7,4},{8,11},{9,10},{10,... | collective-permute-start | bytes 393224 | tf_op jit(solution)/shard_map/ppermute | solution.py:240
  54.3 0.0 collective-permute-start.20
  54.3 0.0 collective-permute-done.18.refs_3_
  54.3 0.6 collective-permute-start.19
  54.9 1.2 %collective-permute-done.17.refs_2_ = bf16[64,640]{1,0:T(8,128)(2,1)S(1)} collective-permute-done((bf16[64,640]{1,0:T(8,128)(2,1)S(1)}, bf16[64,640]{1,0:T(8,128)(2,1)S(1)}, u32[]{:S(2)}, u32[]{:S(2)}) %collective-permute-start.17) | collective-permute-done | bytes 81952 | tf_op jit(solution)/shard_map/ppermute | solution.py:240
  56.1 1.5 %collective-permute-done.16.refs_1_ = bf16[64,640]{1,0:T(8,128)(2,1)S(1)} collective-permute-done((bf16[64,640]{1,0:T(8,128)(2,1)S(1)}, bf16[64,640]{1,0:T(8,128)(2,1)S(1)}, u32[]{:S(2)}, u32[]{:S(2)}) %collective-permute-start.16) | collective-permute-done | bytes 81952 | tf_op jit(solution)/shard_map/ppermute | solution.py:240
  57.6 4.0 %shard_map.61 = (bf16[512,512]{1,0:T(8,128)(2,1)S(1)}, bf16[512,512]{1,0:T(8,128)(2,1)S(1)}) custom-call(s32[3]{0:T(128)S(1)} %pad_add_fusion.where, bf16[64,640]{1,0:T(8,128)(2,1)S(1)} %slice.8.refs_0_, bf16[64,640]{1,0:T(8,128)(2,1)S(1)} %collective-permute-done.16.refs_1_, bf16[64,640]{1,0:T(8,128)(2,1)S(1)} %collective-permute-done.17.refs_2_, ...), custom_call_target="tpu_custom_call" | custom-call | flops 2684354560 | bytes 1048576 | tf_op jit(solution)/shard_map/pallas_call | solution.py:337
  61.7 0.0 collective-permute-done.21.refs_3_
  61.7 0.0 collective-permute-done.20.refs_2_
  61.7 0.0 collective-permute-done.19.refs_1_
  61.7 2.9 %shard_map.62 = f32[512,512]{1,0:T(8,128)} custom-call(s32[3]{0:T(128)S(1)} %pad_add_fusion.where, bf16[512,512]{1,0:T(8,128)(2,1)S(1)} %get-tuple-element.47.refs_0_.act_high, bf16[512,512]{1,0:T(8,128)(2,1)S(1)} %get-tuple-element.48.act_low, bf16[512,512]{1,0:T(8,128)(2,1)S(1)} %get-tuple-element.52.out_high, ...), custom_call_target="tpu_custom_call" | custom-call | flops 1342177280 | bytes 1048576 | tf_op jit(solution)/shard_map/pallas_call | solution.py:349
  (5 shorter events, 0.1 us)
Async XLA Ops:
  0.6 1.9 %collective-permute-start.1 = (bf16[2,128,512]{2,1,0:T(8,128)(2,1)}, bf16[2,128,512]{2,1,0:T(8,128)(2,1)S(1)}, u32[]{:S(2)}, u32[]{:S(2)}) collective-permute-start(bf16[2,128,512]{2,1,0:T(8,128)(2,1)} %bitcast.11), channel_id=1, source_target_pairs={{0,8},{8,0},{1,9},{9,1},{2,10},{10,2},{3,11},{11,3},{4,12},{12,4},... | collective-permute-start | bytes 786440 | tf_op jit(solution)/shard_map/ppermute | solution.py:277
  1.1 2.1 %collective-permute-start = (bf16[512,512]{1,0:T(8,128)(2,1)}, bf16[512,512]{1,0:T(8,128)(2,1)S(1)}, u32[]{:S(2)}, u32[]{:S(2)}) collective-permute-start(bf16[512,512]{1,0:T(8,128)(2,1)} %bitcast.10), channel_id=1, source_target_pairs={{0,8},{8,0},{1,9},{9,1},{2,10},{10,2},{3,11},{11,3},{4,12},{12,4},... | collective-permute-start | bytes 1572872 | tf_op jit(solution)/shard_map/ppermute | solution.py:276
  1.2 1.2 %copy-start.1 = (bf16[2,128,512]{2,1,0:T(8,128)(2,1)S(1)}, bf16[2,128,512]{2,1,0:T(8,128)(2,1)}, u32[]{:S(2)}) copy-start(bf16[2,128,512]{2,1,0:T(8,128)(2,1)} %param.5) | copy-start | bytes 786436
  1.2 1.2 %copy-start.2 = (bf16[1,2,128,512]{3,2,1,0:T(8,128)(2,1)S(1)}, bf16[1,2,128,512]{3,2,1,0:T(8,128)(2,1)}, u32[]{:S(2)}) copy-start(bf16[1,2,128,512]{3,2,1,0:T(8,128)(2,1)} %param.3) | copy-start | bytes 786436
  4.7 7.9 %collective-permute-start.2 = (bf16[128,512]{1,0:T(8,128)(2,1)S(1)}, bf16[128,512]{1,0:T(8,128)(2,1)S(1)}, u32[]{:S(2)}, u32[]{:S(2)}) collective-permute-start(bf16[128,512]{1,0:T(8,128)(2,1)S(1)} %get-tuple-element.31.after), channel_id=1, source_target_pairs={{16,0},{17,1},{18,2},{19,3},{20,4},{21,5},{22,6},{23,7},{24,8},{25... | collective-permute-start | bytes 393224 | tf_op jit(solution)/shard_map/ppermute | solution.py:288
  6.9 6.8 %collective-permute-start.3 = (bf16[64,640]{1,0:T(8,128)(2,1)S(1)}, bf16[64,640]{1,0:T(8,128)(2,1)S(1)}, u32[]{:S(2)}, u32[]{:S(2)}) collective-permute-start(bf16[64,640]{1,0:T(8,128)(2,1)S(1)} %get-tuple-element.37), channel_id=1, source_target_pairs={{0,3},{1,2},{2,1},{3,0},{4,7},{5,6},{6,5},{7,4},{8,11},{9,10},{10,... | collective-permute-start | bytes 245768 | tf_op jit(solution)/shard_map/ppermute | solution.py:240
  10.9 4.5 %collective-permute-start.4 = (bf16[64,640]{1,0:T(8,128)(2,1)S(1)}, bf16[64,640]{1,0:T(8,128)(2,1)S(1)}, u32[]{:S(2)}, u32[]{:S(2)}) collective-permute-start(bf16[64,640]{1,0:T(8,128)(2,1)S(1)} %get-tuple-element.38), channel_id=1, source_target_pairs={{0,1},{1,0},{2,3},{3,2},{4,5},{5,4},{6,7},{7,6},{8,9},{9,8},{10,11... | collective-permute-start | bytes 245768 | tf_op jit(solution)/shard_map/ppermute | solution.py:240
  11.4 4.4 %collective-permute-start.5 = (bf16[64,640]{1,0:T(8,128)(2,1)S(1)}, bf16[64,640]{1,0:T(8,128)(2,1)S(1)}, u32[]{:S(2)}, u32[]{:S(2)}) collective-permute-start(bf16[64,640]{1,0:T(8,128)(2,1)S(1)} %get-tuple-element.39), channel_id=1, source_target_pairs={{0,2},{1,3},{2,0},{3,1},{4,6},{5,7},{6,4},{7,5},{8,10},{9,11},{10,... | collective-permute-start | bytes 245768 | tf_op jit(solution)/shard_map/ppermute | solution.py:240
  16.8 2.9 %collective-permute-start.7 = (bf16[128,512]{1,0:T(8,128)(2,1)S(1)}, bf16[128,512]{1,0:T(8,128)(2,1)S(1)}, u32[]{:S(2)}, u32[]{:S(2)}) collective-permute-start(bf16[128,512]{1,0:T(8,128)(2,1)S(1)} %get-tuple-element.43), channel_id=1, source_target_pairs={{0,8},{8,0},{1,9},{9,1},{2,10},{10,2},{3,11},{11,3},{4,12},{12,4},... | collective-permute-start | bytes 393224 | tf_op jit(solution)/shard_map/ppermute | solution.py:314
  16.9 7.5 %collective-permute-start.9 = (bf16[64,640]{1,0:T(8,128)(2,1)S(1)}, bf16[64,640]{1,0:T(8,128)(2,1)S(1)}, u32[]{:S(2)}, u32[]{:S(2)}) collective-permute-start(bf16[64,640]{1,0:T(8,128)(2,1)S(1)} %shard_map.53.after.left), channel_id=1, source_target_pairs={{0,4},{4,0},{1,5},{5,1},{2,6},{6,2},{3,7},{7,3},{8,12},{12,8},{9,1... | collective-permute-start | bytes 245768 | tf_op jit(solution)/shard_map/ppermute | solution.py:248
  19.5 4.9 %collective-permute-start.6 = (bf16[128,512]{1,0:T(8,128)(2,1)S(1)}, bf16[128,512]{1,0:T(8,128)(2,1)S(1)}, u32[]{:S(2)}, u32[]{:S(2)}) collective-permute-start(bf16[128,512]{1,0:T(8,128)(2,1)S(1)} %get-tuple-element.41), channel_id=1, source_target_pairs={{0,8},{8,0},{1,9},{9,1},{2,10},{10,2},{3,11},{11,3},{4,12},{12,4},... | collective-permute-start | bytes 393224 | tf_op jit(solution)/shard_map/ppermute | solution.py:315
  20.8 9.1 %collective-permute-start.8 = (bf16[64,1664]{1,0:T(8,128)(2,1)S(1)}, bf16[64,1664]{1,0:T(8,128)(2,1)S(1)}, u32[]{:S(2)}, u32[]{:S(2)}) collective-permute-start(bf16[64,1664]{1,0:T(8,128)(2,1)S(1)} %get-tuple-element.45), channel_id=1, source_target_pairs={{0,3},{1,2},{2,1},{3,0},{4,7},{5,6},{6,5},{7,4},{8,11},{9,10},{10,... | collective-permute-start | bytes 638984 | tf_op jit(solution)/shard_map/ppermute | solution.py:240
  22.2 11.8 %collective-permute-start.13 = (bf16[64,1664]{1,0:T(8,128)(2,1)S(1)}, bf16[64,1664]{1,0:T(8,128)(2,1)S(1)}, u32[]{:S(2)}, u32[]{:S(2)}) collective-permute-start(bf16[64,1664]{1,0:T(8,128)(2,1)S(1)} %get-tuple-element.50), channel_id=1, source_target_pairs={{0,1},{1,0},{2,3},{3,2},{4,5},{5,4},{6,7},{7,6},{8,9},{9,8},{10,11... | collective-permute-start | bytes 638984 | tf_op jit(solution)/shard_map/ppermute | solution.py:240
  23.6 10.4 %collective-permute-start.14 = (bf16[64,1664]{1,0:T(8,128)(2,1)S(1)}, bf16[64,1664]{1,0:T(8,128)(2,1)S(1)}, u32[]{:S(2)}, u32[]{:S(2)}) collective-permute-start(bf16[64,1664]{1,0:T(8,128)(2,1)S(1)} %get-tuple-element.51), channel_id=1, source_target_pairs={{0,2},{1,3},{2,0},{3,1},{4,6},{5,7},{6,4},{7,5},{8,10},{9,11},{10,... | collective-permute-start | bytes 638984 | tf_op jit(solution)/shard_map/ppermute | solution.py:240
  29.9 1.0 %copy-start = (bf16[2,128,512]{2,1,0:T(8,128)(2,1)S(1)}, bf16[2,128,512]{2,1,0:T(8,128)(2,1)}, u32[]{:S(2)}) copy-start(bf16[2,128,512]{2,1,0:T(8,128)(2,1)} %shard_map.55.after) | copy-start | bytes 786436
  34.1 13.1 %collective-permute-start.15 = (bf16[64,1664]{1,0:T(8,128)(2,1)S(1)}, bf16[64,1664]{1,0:T(8,128)(2,1)S(1)}, u32[]{:S(2)}, u32[]{:S(2)}) collective-permute-start(bf16[64,1664]{1,0:T(8,128)(2,1)S(1)} %add_convert_fusion.left), channel_id=1, source_target_pairs={{0,4},{4,0},{1,5},{5,1},{2,6},{6,2},{3,7},{7,3},{8,12},{12,8},{9,1... | collective-permute-start | bytes 638984 | tf_op jit(solution)/shard_map/ppermute | solution.py:248
  34.9 7.3 %collective-permute-start.12 = (bf16[64,640]{1,0:T(8,128)(2,1)S(1)}, bf16[64,640]{1,0:T(8,128)(2,1)S(1)}, u32[]{:S(2)}, u32[]{:S(2)}) collective-permute-start(bf16[64,640]{1,0:T(8,128)(2,1)S(1)} %get-tuple-element.46.refs_0_), channel_id=1, source_target_pairs={{0,3},{1,2},{2,1},{3,0},{4,7},{5,6},{6,5},{7,4},{8,11},{9,10},{10,... | collective-permute-start | bytes 245768 | tf_op jit(solution)/shard_map/ppermute | solution.py:240
  36.8 6.3 %collective-permute-start.11 = (bf16[64,640]{1,0:T(8,128)(2,1)S(1)}, bf16[64,640]{1,0:T(8,128)(2,1)S(1)}, u32[]{:S(2)}, u32[]{:S(2)}) collective-permute-start(bf16[64,640]{1,0:T(8,128)(2,1)S(1)} %get-tuple-element.46.refs_0_), channel_id=1, source_target_pairs={{0,2},{1,3},{2,0},{3,1},{4,6},{5,7},{6,4},{7,5},{8,10},{9,11},{10,... | collective-permute-start | bytes 245768 | tf_op jit(solution)/shard_map/ppermute | solution.py:240
  37.8 5.3 %collective-permute-start.10 = (bf16[64,640]{1,0:T(8,128)(2,1)S(1)}, bf16[64,640]{1,0:T(8,128)(2,1)S(1)}, u32[]{:S(2)}, u32[]{:S(2)}) collective-permute-start(bf16[64,640]{1,0:T(8,128)(2,1)S(1)} %get-tuple-element.46.refs_0_), channel_id=1, source_target_pairs={{0,1},{1,0},{2,3},{3,2},{4,5},{5,4},{6,7},{7,6},{8,9},{9,8},{10,11... | collective-permute-start | bytes 245768 | tf_op jit(solution)/shard_map/ppermute | solution.py:240
  47.2 7.0 %collective-permute-start.18 = (bf16[64,640]{1,0:T(8,128)(2,1)S(1)}, bf16[64,640]{1,0:T(8,128)(2,1)S(1)}, u32[]{:S(2)}, u32[]{:S(2)}) collective-permute-start(bf16[64,640]{1,0:T(8,128)(2,1)S(1)} %slice.8.refs_0_), channel_id=1, source_target_pairs={{0,3},{1,2},{2,1},{3,0},{4,7},{5,6},{6,5},{7,4},{8,11},{9,10},{10,... | collective-permute-start | bytes 245768 | tf_op jit(solution)/shard_map/ppermute | solution.py:240
  50.7 5.4 %collective-permute-start.17 = (bf16[64,640]{1,0:T(8,128)(2,1)S(1)}, bf16[64,640]{1,0:T(8,128)(2,1)S(1)}, u32[]{:S(2)}, u32[]{:S(2)}) collective-permute-start(bf16[64,640]{1,0:T(8,128)(2,1)S(1)} %slice.8.refs_0_), channel_id=1, source_target_pairs={{0,2},{1,3},{2,0},{3,1},{4,6},{5,7},{6,4},{7,5},{8,10},{9,11},{10,... | collective-permute-start | bytes 245768 | tf_op jit(solution)/shard_map/ppermute | solution.py:240
  50.7 6.9 %collective-permute-start.16 = (bf16[64,640]{1,0:T(8,128)(2,1)S(1)}, bf16[64,640]{1,0:T(8,128)(2,1)S(1)}, u32[]{:S(2)}, u32[]{:S(2)}) collective-permute-start(bf16[64,640]{1,0:T(8,128)(2,1)S(1)} %slice.8.refs_0_), channel_id=1, source_target_pairs={{0,1},{1,0},{2,3},{3,2},{4,5},{5,4},{6,7},{7,6},{8,9},{9,8},{10,11... | collective-permute-start | bytes 245768 | tf_op jit(solution)/shard_map/ppermute | solution.py:240
  51.3 10.3 %collective-permute-start.21 = (bf16[64,1024]{1,0:T(8,128)(2,1)S(1)}, bf16[64,1024]{1,0:T(8,128)(2,1)S(1)}, u32[]{:S(2)}, u32[]{:S(2)}) collective-permute-start(bf16[64,1024]{1,0:T(8,128)(2,1)S(1)} %slice.9.refs_0_), channel_id=1, source_target_pairs={{0,3},{1,2},{2,1},{3,0},{4,7},{5,6},{6,5},{7,4},{8,11},{9,10},{10,... | collective-permute-start | bytes 393224 | tf_op jit(solution)/shard_map/ppermute | solution.py:240
  54.3 7.4 %collective-permute-start.20 = (bf16[64,1024]{1,0:T(8,128)(2,1)S(1)}, bf16[64,1024]{1,0:T(8,128)(2,1)S(1)}, u32[]{:S(2)}, u32[]{:S(2)}) collective-permute-start(bf16[64,1024]{1,0:T(8,128)(2,1)S(1)} %slice.9.refs_0_), channel_id=1, source_target_pairs={{0,2},{1,3},{2,0},{3,1},{4,6},{5,7},{6,4},{7,5},{8,10},{9,11},{10,... | collective-permute-start | bytes 393224 | tf_op jit(solution)/shard_map/ppermute | solution.py:240
  54.3 7.4 %collective-permute-start.19 = (bf16[64,1024]{1,0:T(8,128)(2,1)S(1)}, bf16[64,1024]{1,0:T(8,128)(2,1)S(1)}, u32[]{:S(2)}, u32[]{:S(2)}) collective-permute-start(bf16[64,1024]{1,0:T(8,128)(2,1)S(1)} %slice.9.refs_0_), channel_id=1, source_target_pairs={{0,1},{1,0},{2,3},{3,2},{4,5},{5,4},{6,7},{7,6},{8,9},{9,8},{10,11... | collective-permute-start | bytes 393224 | tf_op jit(solution)/shard_map/ppermute | solution.py:240

commit v10 on v9

--- a/solution.py
+++ b/solution.py
@@ -108,9 +108,7 @@
     result[...] = sum(piece[...].astype(F32) for piece in pieces).astype(BF16)
 
 
-def even_kernel(
-    where, own, partner, slope_own, slope_partner, dh, cot, after, own_dh, give_dh, own_cot, give_cot
-):
+def even_kernel(where, own, partner, slope_own, slope_partner, dh, cot, own_dh, give_dh, own_cot, give_cot):
     def run(odd, even):
         odd[2][...], odd[3][...] = dh[...], cot[...]
         even[2][...], even[3][...] = layer(cot[...], even[1][...], even[0][...])
@@ -160,7 +158,7 @@
     result[...] = left[...].astype(F32) + right[...].astype(F32)
 
 
-def grad_kernel(where, local, dh_own, dh_got, *refs):
+def grad_kernel(where, local, dh_own, dh_got, after, *refs):
     parts, (inputs, tokens, whole) = refs[:GROUP], refs[GROUP:]
     rows, width = local.shape[1:]
     inputs[:rows] = local[where[0]]
@@ -305,12 +303,12 @@
     dh_odd, cot_odd = call(odd_kernel, 64 * rows * width**2, [block] * 2, [SMEM] + [VMEM] * 6)(
         where, own, partner, slope_own, slope_partner, arrived, last
     )
+    own_dh, give_dh, own_cot, give_cot = call(
+        even_kernel, 4 * rows * width**2, [block] * 4, [SMEM] + [VMEM] * 6
+    )(where, own, partner, slope_own, slope_partner, dh_odd, cot_odd)
     act_sum = call(sum_kernel, 0, array(size // 2, factor), [VMEM] * GROUP + [ANY])(
-        *(act_pieces[step] for step in (0, 3, 1, 2)), cot_odd
-    )
-    own_dh, give_dh, own_cot, give_cot = call(
-        even_kernel, 4 * rows * width**2, [block] * 4, [SMEM] + [VMEM] * 6 + [ANY]
-    )(where, own, partner, slope_own, slope_partner, dh_odd, cot_odd, act_sum)
+        *(act_pieces[step] for step in (0, 3, 1, 2)), own_dh
+    )
     got_dh = lax.ppermute(give_dh, "core", SWAP)
     other_cot = lax.ppermute(give_cot, "core", SWAP)
 
@@ -318,10 +316,10 @@
         grad_kernel,
         4 * tokens * width**2,
         [array(size // 2, factor + 2 * width)] * GROUP,
-        [SMEM] + [VMEM] * 3,
+        [SMEM] + [VMEM] * 3 + [ANY],
         [pltpu.VMEM((tokens, width), BF16)] * 2
         + [pltpu.VMEM((GROUP, size // 2, factor + 2 * width), BF16)],
-    )(where, kept, own_dh, got_dh)
+    )(where, kept, own_dh, got_dh, act_sum)
     cot = call(cot_kernel, 0, array(micro, rows, width), [SMEM, VMEM, VMEM])(where, own_cot, other_cot)
     pieces = send(parts)
     begun, act_part = call(
@@ -343,9 +341,8 @@
         )(where, *pieces)
 
     act_inv = inverse(act, 0)
-    total = exchange(total, (act_inv[0],))
-    out = send([total[:, :factor]] * GROUP)
-    grad = send([total[:, factor:]] * GROUP)
+    out = send([exchange(total[:, :factor])] * GROUP)
+    grad = send([exchange(total[:, factor:], (act_inv[0], *out))] * GROUP)
     update = call(
         update_kernel,
         10 * width**3,

time: 64.8 us -> 61.3 us (0.946)
  waiting for transfers between devices: 19 us -> 16.5 us
  starting transfers between devices: 24.9 us -> 23.9 us
    ppermute x15, waiting for transfers between devices: 17 us -> 13.5 us  [send(): lax.ppermute(parts[step], ('near', 'side'), [(i, i ^ step) for i in range...]
    ppermute x15, starting transfers between devices: 19.3 us -> 16.3 us  [send(): lax.ppermute(parts[step], ('near', 'side'), [(i, i ^ step) for i in range...]
    ppermute x2 -> x3, starting transfers between devices: 3.48 us -> 5.65 us  [exchange(): got = lax.ppermute(value, 'far', route)]
    ppermute x2 -> x3, waiting for transfers between devices: 0.06 us -> 1.07 us  [exchange(): got = lax.ppermute(value, 'far', route)]
  transfers between devices with their start and end apart: 22 -> 23, of which waited for: 12 -> 10; matrix products, arithmetic and copies ran while one was open for 2% -> 2% of each run, Pallas kernels for 19% -> 22%
where the time goes in v10:
time: 61.3 us; the launch traced here: 61.1 us
  starting transfers between devices  23.9 us (39%)
  Pallas kernels  17.6 us (29%)
  waiting for transfers between devices  16.5 us (27%)
  other arithmetic  1.33 us (2%)
  local copies, waits for them, and re-layouts  0.98 us (2%)
  between operations  0.83 us (1%)
    ppermute x15, starting transfers between devices, send(): lax.ppermute(parts[step], ('near', 'side'), [(i, i ^ step) for i in range...  16.3 us
    ppermute x15, waiting for transfers between devices, send(): lax.ppermute(parts[step], ('near', 'side'), [(i, i ^ step) for i in range...  13.5 us
    pallas_call x2, Pallas kernels, inverse(): call(functools.partial(inverse_kernel, count), flops, [array(width, width...  8.06 us
    ppermute x3, starting transfers between devices, exchange(): got = lax.ppermute(value, 'far', route)  5.65 us
    pallas_call x1, Pallas kernels, body(): call(update_kernel, 10 * width ** 3, array(width, width, dtype=F32), [SME...  2.91 us
    pallas_call x1, Pallas kernels, body(): call(first_kernel, 8 * rows * width ** 2, [array(width, width), array(mic...  1.46 us
    ppermute x1, starting transfers between devices, body(): upstream = lax.ppermute(down, 'row', [(r, r - 1) for r in range(1, pairs)])  1.29 us
    pallas_call x1, Pallas kernels, body(): call(cot_kernel, 0, array(micro, rows, width), [SMEM, VMEM, VMEM])  1.26 us
  transfers between devices with their start and end apart: 23, of which 10 were waited for; matrix products, arithmetic and copies ran while one was open for 2% of the time, Pallas kernels for 22%

profile of v10, /device:TPU:0, one launch (start us, length us, event | category | flops | bytes accessed | tf_op | source)
XLA Modules:
  0.0 61.1 jit_solution(13961598709660023884)
XLA Ops:
  0.6 0.5 collective-permute-start.1
  1.1 0.1 collective-permute-start
  1.2 0.0 copy-start.1
  1.2 0.0 copy-start.2
  1.2 1.1 %broadcast_select_fusion.weight = bf16[512,512]{1,0:T(8,128)(2,1)S(1)} fusion(pred[]{:T(512)S(6)} %gt.2, bf16[1,512,512]{2,1,0:T(8,128)(2,1)} %param.4), kind=kLoop, calls=%fused_computation | loop fusion | flops 262144 | bytes 1048577 | tf_op jit(solution)/shard_map/jit(_where)/select_n | solution.py:272
  2.4 0.1 pad_add_fusion.where
  2.5 0.0 copy-done.1
  2.5 0.0 copy-done.2
  2.5 0.0 collective-permute-done.1.partner_local
  2.5 0.7 %collective-permute-done.partner = bf16[512,512]{1,0:T(8,128)(2,1)S(1)} collective-permute-done((bf16[512,512]{1,0:T(8,128)(2,1)}, bf16[512,512]{1,0:T(8,128)(2,1)S(1)}, u32[]{:S(2)}, u32[]{:S(2)}) %collective-permute-start) | collective-permute-done | bytes 524320 | tf_op jit(solution)/shard_map/ppermute | solution.py:274
  3.3 1.5 %shard_map.50 = (bf16[512,512]{1,0:T(8,128)(2,1)S(1)}, bf16[2,128,512]{2,1,0:T(8,128)(2,1)S(1)}, bf16[128,512]{1,0:T(8,128)(2,1)S(1)}, f32[128,512]{1,0:T(8,128)...) custom-call(s32[3]{0:T(128)S(1)} %pad_add_fusion.where, bf16[512,512]{1,0:T(8,128)(2,1)S(1)} %broadcast_select_fusion.weight, ...), custom_call_target="tpu_custom_call" | custom-call | flops 268435456 | bytes 1048576 | tf_op jit(solution)/shard_map/pallas_call | solution.py:278
  4.7 1.3 %collective-permute-start.2 = (bf16[128,512]{1,0:T(8,128)(2,1)S(1)}, bf16[128,512]{1,0:T(8,128)(2,1)S(1)}, u32[]{:S(2)}, u32[]{:S(2)}) collective-permute-start(bf16[128,512]{1,0:T(8,128)(2,1)S(1)} %get-tuple-element.31.after), channel_id=1, source_target_pairs={{16,0},{17,1},{18,2},{19,3},{20,4},{21,5},{22,6},{23,7},{24,8},{25... | collective-permute-start | bytes 393224 | tf_op jit(solution)/shard_map/ppermute | solution.py:286
  6.0 0.9 %shard_map.54 = (bf16[64,640]{1,0:T(8,128)(2,1)S(1)}, bf16[64,640]{1,0:T(8,128)(2,1)S(1)}, bf16[64,640]{1,0:T(8,128)(2,1)S(1)}, bf16[64,640]{1,0:T(8,128)(2,1)S(1)}) custom-call(s32[3]{0:T(128)S(1)} %pad_add_fusion.where, bf16[2,128,512]{2,1,0:T(8,128)(2,1)S(1)} %get-tuple-element.37.local, bf16[128,512]{1,0:T(8,128)(2,1)S(1)} %get-tuple-element.31.after), custom_call_target="tpu_custom_call" | custom-call | flops 134217728 | bytes 1048576 | tf_op jit(solution)/shard_map/pallas_call | solution.py:294
  6.9 3.9 %collective-permute-start.5 = (bf16[64,640]{1,0:T(8,128)(2,1)S(1)}, bf16[64,640]{1,0:T(8,128)(2,1)S(1)}, u32[]{:S(2)}, u32[]{:S(2)}) collective-permute-start(bf16[64,640]{1,0:T(8,128)(2,1)S(1)} %get-tuple-element.41), channel_id=1, source_target_pairs={{0,3},{1,2},{2,1},{3,0},{4,7},{5,6},{6,5},{7,4},{8,11},{9,10},{10,... | collective-permute-start | bytes 245768 | tf_op jit(solution)/shard_map/ppermute | solution.py:238
  10.9 0.5 collective-permute-start.6
  11.4 0.1 collective-permute-start.7
  11.5 1.2 %collective-permute-done.2.arrived = bf16[128,512]{1,0:T(8,128)(2,1)S(1)} collective-permute-done((bf16[128,512]{1,0:T(8,128)(2,1)S(1)}, bf16[128,512]{1,0:T(8,128)(2,1)S(1)}, u32[]{:S(2)}, u32[]{:S(2)}) %collective-permute-start.2) | collective-permute-done | bytes 131104 | tf_op jit(solution)/shard_map/ppermute | solution.py:286
  12.7 0.9 %shard_map.51 = (bf16[128,512]{1,0:T(8,128)(2,1)S(1)}, bf16[128,512]{1,0:T(8,128)(2,1)S(1)}) custom-call(s32[3]{0:T(128)S(1)} %pad_add_fusion.where, bf16[512,512]{1,0:T(8,128)(2,1)S(1)} %get-tuple-element.28.own, bf16[512,512]{1,0:T(8,128)(2,1)S(1)} %collective-permute-done.partner, f32[128,512]{1,0:T(8,128)S(1)} %get-tuple-element.29.slope_own, ...), custom_call_target="tpu_custom_call" | custom-call | flops 2147483648 | bytes 1048576 | tf_op jit(solution)/shard_map/pallas_call | solution.py:303
  13.6 0.9 %shard_map.52 = (bf16[128,512]{1,0:T(8,128)(2,1)S(1)}, bf16[128,512]{1,0:T(8,128)(2,1)S(1)}, bf16[128,512]{1,0:T(8,128)(2,1)S(1)}, bf16[128,512]{1,0:T(8,128)(2,1)S(1)}) custom-call(s32[3]{0:T(128)S(1)} %pad_add_fusion.where, bf16[512,512]{1,0:T(8,128)(2,1)S(1)} %get-tuple-element.28.own, bf16[512,512]{1,0:T(8,128)(2,1)S(1)} %collective-permute-done.partner, ...), custom_call_target="tpu_custom_call" | custom-call | flops 134217728 | bytes 1048576 | tf_op jit(solution)/shard_map/pallas_call | solution.py:306
  14.4 0.1 collective-permute-start.4
  14.5 0.0 collective-permute-done.5.refs_1_
  14.5 0.8 %collective-permute-done.6.refs_2_ = bf16[64,640]{1,0:T(8,128)(2,1)S(1)} collective-permute-done((bf16[64,640]{1,0:T(8,128)(2,1)S(1)}, bf16[64,640]{1,0:T(8,128)(2,1)S(1)}, u32[]{:S(2)}, u32[]{:S(2)}) %collective-permute-start.6) | collective-permute-done | bytes 81952 | tf_op jit(solution)/shard_map/ppermute | solution.py:238
  15.4 0.5 collective-permute-done.7.refs_3_
  15.9 2.7 %collective-permute-start.9 = (bf16[64,640]{1,0:T(8,128)(2,1)S(1)}, bf16[64,640]{1,0:T(8,128)(2,1)S(1)}, u32[]{:S(2)}, u32[]{:S(2)}) collective-permute-start(bf16[64,640]{1,0:T(8,128)(2,1)S(1)} %shard_map.55.after.left), channel_id=1, source_target_pairs={{0,4},{4,0},{1,5},{5,1},{2,6},{6,2},{3,7},{7,3},{8,12},{12,8},{9,1... | collective-permute-start | bytes 245768 | tf_op jit(solution)/shard_map/ppermute | solution.py:246
  18.5 0.0 collective-permute-start.3
  18.6 0.0 collective-permute-done.4.dh_got
  18.6 1.1 %shard_map.56 = (bf16[64,1664]{1,0:T(8,128)(2,1)S(1)}, bf16[64,1664]{1,0:T(8,128)(2,1)S(1)}, bf16[64,1664]{1,0:T(8,128)(2,1)S(1)}, bf16[64,1664]{1,0:T(8,128)(2,1)S(1)}) custom-call(s32[3]{0:T(128)S(1)} %pad_add_fusion.where, bf16[2,128,512]{2,1,0:T(8,128)(2,1)S(1)} %get-tuple-element.37.local, bf16[128,512]{1,0:T(8,128)(2,1)S(1)} %get-tuple-element.38.refs_4_.dh_own, ...), custom_call_target="tpu_custom_call" | custom-call | flops 268435456 | bytes 1048576 | tf_op jit(solution)/shard_map/pallas_call | solution.py:315
  19.6 2.3 %collective-permute-start.8 = (bf16[64,1664]{1,0:T(8,128)(2,1)S(1)}, bf16[64,1664]{1,0:T(8,128)(2,1)S(1)}, u32[]{:S(2)}, u32[]{:S(2)}) collective-permute-start(bf16[64,1664]{1,0:T(8,128)(2,1)S(1)} %get-tuple-element.45), channel_id=1, source_target_pairs={{0,3},{1,2},{2,1},{3,0},{4,7},{5,6},{6,5},{7,4},{8,11},{9,10},{10,... | collective-permute-start | bytes 638984 | tf_op jit(solution)/shard_map/ppermute | solution.py:238
  22.0 0.5 collective-permute-start.13
  22.5 0.7 %collective-permute-start.14 = (bf16[64,1664]{1,0:T(8,128)(2,1)S(1)}, bf16[64,1664]{1,0:T(8,128)(2,1)S(1)}, u32[]{:S(2)}, u32[]{:S(2)}) collective-permute-start(bf16[64,1664]{1,0:T(8,128)(2,1)S(1)} %get-tuple-element.51), channel_id=1, source_target_pairs={{0,2},{1,3},{2,0},{3,1},{4,6},{5,7},{6,4},{7,5},{8,10},{9,11},{10,... | collective-permute-start | bytes 638984 | tf_op jit(solution)/shard_map/ppermute | solution.py:238
  23.2 0.0 collective-permute-done.9.right
  23.2 0.0 collective-permute-done.3.other_cot
  23.2 1.3 %shard_map.53.after = bf16[2,128,512]{2,1,0:T(8,128)(2,1)} custom-call(s32[3]{0:T(128)S(1)} %pad_add_fusion.where, bf16[128,512]{1,0:T(8,128)(2,1)S(1)} %get-tuple-element.35.own_cot, bf16[128,512]{1,0:T(8,128)(2,1)S(1)} %collective-permute-done.3.other_cot), custom_call_target="tpu_custom_call" | custom-call | bytes 1048576 | tf_op jit(solution)/shard_map/pallas_call | solution.py:323
  24.5 4.3 %collective-permute-done.8.right = bf16[64,1664]{1,0:T(8,128)(2,1)S(1)} collective-permute-done((bf16[64,1664]{1,0:T(8,128)(2,1)S(1)}, bf16[64,1664]{1,0:T(8,128)(2,1)S(1)}, u32[]{:S(2)}, u32[]{:S(2)}) %collective-permute-start.8) | collective-permute-done | bytes 213024 | tf_op jit(solution)/shard_map/ppermute | solution.py:238
  28.8 0.9 %copy-done = bf16[2,128,512]{2,1,0:T(8,128)(2,1)S(1)} copy-done((bf16[2,128,512]{2,1,0:T(8,128)(2,1)S(1)}, bf16[2,128,512]{2,1,0:T(8,128)(2,1)}, u32[]{:S(2)}) %copy-start) | copy-done | bytes 262168
  29.7 0.1 shard_map.58
  29.8 3.3 %collective-permute-done.13 = bf16[64,1664]{1,0:T(8,128)(2,1)S(1)} collective-permute-done((bf16[64,1664]{1,0:T(8,128)(2,1)S(1)}, bf16[64,1664]{1,0:T(8,128)(2,1)S(1)}, u32[]{:S(2)}, u32[]{:S(2)}) %collective-permute-start.13) | collective-permute-done | bytes 213024 | tf_op jit(solution)/shard_map/ppermute | solution.py:238
  33.1 0.0 collective-permute-done.14
  33.1 0.1 add_convert_fusion
  33.2 0.7 %collective-permute-start.15 = (bf16[64,640]{1,0:T(8,128)(2,1)S(1)}, bf16[64,640]{1,0:T(8,128)(2,1)S(1)}, u32[]{:S(2)}, u32[]{:S(2)}) collective-permute-start(bf16[64,640]{1,0:T(8,128)(2,1)S(1)} %slice.8.left), channel_id=1, source_target_pairs={{0,4},{4,0},{1,5},{5,1},{2,6},{6,2},{3,7},{7,3},{8,12},{12,8},{9,1... | collective-permute-start | bytes 245768 | tf_op jit(solution)/shard_map/ppermute | solution.py:246
  33.9 2.7 %collective-permute-start.12 = (bf16[64,640]{1,0:T(8,128)(2,1)S(1)}, bf16[64,640]{1,0:T(8,128)(2,1)S(1)}, u32[]{:S(2)}, u32[]{:S(2)}) collective-permute-start(bf16[64,640]{1,0:T(8,128)(2,1)S(1)} %get-tuple-element.46.refs_0_), channel_id=1, source_target_pairs={{0,3},{1,2},{2,1},{3,0},{4,7},{5,6},{6,5},{7,4},{8,11},{9,10},{10,... | collective-permute-start | bytes 245768 | tf_op jit(solution)/shard_map/ppermute | solution.py:238
  36.6 0.0 collective-permute-start.11
  36.7 2.3 %collective-permute-start.19 = (bf16[64,1024]{1,0:T(8,128)(2,1)S(1)}, bf16[64,1024]{1,0:T(8,128)(2,1)S(1)}, u32[]{:S(2)}, u32[]{:S(2)}) collective-permute-start(bf16[64,1024]{1,0:T(8,128)(2,1)S(1)} %slice.9.left), channel_id=1, source_target_pairs={{0,4},{4,0},{1,5},{5,1},{2,6},{6,2},{3,7},{7,3},{8,12},{12,8},{9,1... | collective-permute-start | bytes 393224 | tf_op jit(solution)/shard_map/ppermute | solution.py:246
  39.0 0.8 %collective-permute-start.10 = (bf16[64,640]{1,0:T(8,128)(2,1)S(1)}, bf16[64,640]{1,0:T(8,128)(2,1)S(1)}, u32[]{:S(2)}, u32[]{:S(2)}) collective-permute-start(bf16[64,640]{1,0:T(8,128)(2,1)S(1)} %get-tuple-element.46.refs_0_), channel_id=1, source_target_pairs={{0,1},{1,0},{2,3},{3,2},{4,5},{5,4},{6,7},{7,6},{8,9},{9,8},{10,11... | collective-permute-start | bytes 245768 | tf_op jit(solution)/shard_map/ppermute | solution.py:238
  39.8 1.1 %collective-permute-done.15.right = bf16[64,640]{1,0:T(8,128)(2,1)S(1)} collective-permute-done((bf16[64,640]{1,0:T(8,128)(2,1)S(1)}, bf16[64,640]{1,0:T(8,128)(2,1)S(1)}, u32[]{:S(2)}, u32[]{:S(2)}) %collective-permute-start.15) | collective-permute-done | bytes 81952 | tf_op jit(solution)/shard_map/ppermute | solution.py:246
  40.9 0.5 collective-permute-start.18
  41.3 1.9 %collective-permute-done.12.refs_3_ = bf16[64,640]{1,0:T(8,128)(2,1)S(1)} collective-permute-done((bf16[64,640]{1,0:T(8,128)(2,1)S(1)}, bf16[64,640]{1,0:T(8,128)(2,1)S(1)}, u32[]{:S(2)}, u32[]{:S(2)}) %collective-permute-start.12) | collective-permute-done | bytes 81952 | tf_op jit(solution)/shard_map/ppermute | solution.py:238
  43.2 0.0 collective-permute-start.17
  43.2 2.1 %collective-permute-done.11.refs_2_ = bf16[64,640]{1,0:T(8,128)(2,1)S(1)} collective-permute-done((bf16[64,640]{1,0:T(8,128)(2,1)S(1)}, bf16[64,640]{1,0:T(8,128)(2,1)S(1)}, u32[]{:S(2)}, u32[]{:S(2)}) %collective-permute-start.11) | collective-permute-done | bytes 81952 | tf_op jit(solution)/shard_map/ppermute | solution.py:238
  45.3 0.6 collective-permute-start.16
  45.9 0.0 collective-permute-done.10.refs_1_
  45.9 4.0 %shard_map.59 = (bf16[512,512]{1,0:T(8,128)(2,1)S(1)}, bf16[512,512]{1,0:T(8,128)(2,1)S(1)}) custom-call(s32[3]{0:T(128)S(1)} %pad_add_fusion.where, bf16[64,640]{1,0:T(8,128)(2,1)S(1)} %get-tuple-element.46.refs_0_, bf16[64,640]{1,0:T(8,128)(2,1)S(1)} %collective-permute-done.10.refs_1_, bf16[64,640]{1,0:T(8,128)(2,1)S(1)} %collective-permute-done.11.refs_2_, ...), custom_call_target="tpu_custom_call" | custom-call | bytes 1048576 | tf_op jit(solution)/shard_map/pallas_call | solution.py:335
  49.9 0.0 collective-permute-done.19.right
  49.9 0.0 collective-permute-done.18.refs_3_.refs_4_
  49.9 0.0 collective-permute-done.17.refs_2_.refs_3_
  49.9 0.0 collective-permute-done.16.refs_1_.refs_2_
  50.0 0.9 %collective-permute-start.22 = (bf16[64,1024]{1,0:T(8,128)(2,1)S(1)}, bf16[64,1024]{1,0:T(8,128)(2,1)S(1)}, u32[]{:S(2)}, u32[]{:S(2)}) collective-permute-start(bf16[64,1024]{1,0:T(8,128)(2,1)S(1)} %shard_map.62.refs_0_), channel_id=1, source_target_pairs={{0,3},{1,2},{2,1},{3,0},{4,7},{5,6},{6,5},{7,4},{8,11},{9,10},{10,... | collective-permute-start | bytes 393224 | tf_op jit(solution)/shard_map/ppermute | solution.py:238
  50.9 2.1 %collective-permute-start.21 = (bf16[64,1024]{1,0:T(8,128)(2,1)S(1)}, bf16[64,1024]{1,0:T(8,128)(2,1)S(1)}, u32[]{:S(2)}, u32[]{:S(2)}) collective-permute-start(bf16[64,1024]{1,0:T(8,128)(2,1)S(1)} %shard_map.62.refs_0_), channel_id=1, source_target_pairs={{0,2},{1,3},{2,0},{3,1},{4,6},{5,7},{6,4},{7,5},{8,10},{9,11},{10,... | collective-permute-start | bytes 393224 | tf_op jit(solution)/shard_map/ppermute | solution.py:238
  52.9 0.6 collective-permute-start.20
  53.5 4.0 %shard_map.61 = (bf16[512,512]{1,0:T(8,128)(2,1)S(1)}, bf16[512,512]{1,0:T(8,128)(2,1)S(1)}) custom-call(s32[3]{0:T(128)S(1)} %pad_add_fusion.where, bf16[64,640]{1,0:T(8,128)(2,1)S(1)} %shard_map.60.refs_0_.refs_1_, bf16[64,640]{1,0:T(8,128)(2,1)S(1)} %collective-permute-done.16.refs_1_.refs_2_, ...), custom_call_target="tpu_custom_call" | custom-call | flops 2684354560 | bytes 1048576 | tf_op jit(solution)/shard_map/pallas_call | solution.py:335
  57.6 0.0 collective-permute-done.22.refs_3_
  57.6 0.0 collective-permute-done.21.refs_2_
  57.6 0.6 collective-permute-done.20.refs_1_
  58.2 2.9 %shard_map.63 = f32[512,512]{1,0:T(8,128)} custom-call(s32[3]{0:T(128)S(1)} %pad_add_fusion.where, bf16[512,512]{1,0:T(8,128)(2,1)S(1)} %get-tuple-element.47.refs_0_.act_high, bf16[512,512]{1,0:T(8,128)(2,1)S(1)} %get-tuple-element.48.act_low, bf16[512,512]{1,0:T(8,128)(2,1)S(1)} %get-tuple-element.52.out_high, ...), custom_call_target="tpu_custom_call" | custom-call | flops 1342177280 | bytes 1048576 | tf_op jit(solution)/shard_map/pallas_call | solution.py:346
  (8 shorter events, 0.2 us)
Async XLA Ops:
  0.6 1.9 %collective-permute-start.1 = (bf16[2,128,512]{2,1,0:T(8,128)(2,1)}, bf16[2,128,512]{2,1,0:T(8,128)(2,1)S(1)}, u32[]{:S(2)}, u32[]{:S(2)}) collective-permute-start(bf16[2,128,512]{2,1,0:T(8,128)(2,1)} %bitcast.11), channel_id=1, source_target_pairs={{0,8},{8,0},{1,9},{9,1},{2,10},{10,2},{3,11},{11,3},{4,12},{12,4},... | collective-permute-start | bytes 786440 | tf_op jit(solution)/shard_map/ppermute | solution.py:275
  1.1 2.1 %collective-permute-start = (bf16[512,512]{1,0:T(8,128)(2,1)}, bf16[512,512]{1,0:T(8,128)(2,1)S(1)}, u32[]{:S(2)}, u32[]{:S(2)}) collective-permute-start(bf16[512,512]{1,0:T(8,128)(2,1)} %bitcast.10), channel_id=1, source_target_pairs={{0,8},{8,0},{1,9},{9,1},{2,10},{10,2},{3,11},{11,3},{4,12},{12,4},... | collective-permute-start | bytes 1572872 | tf_op jit(solution)/shard_map/ppermute | solution.py:274
  1.2 1.2 %copy-start.1 = (bf16[2,128,512]{2,1,0:T(8,128)(2,1)S(1)}, bf16[2,128,512]{2,1,0:T(8,128)(2,1)}, u32[]{:S(2)}) copy-start(bf16[2,128,512]{2,1,0:T(8,128)(2,1)} %param.5) | copy-start | bytes 786436
  1.2 1.2 %copy-start.2 = (bf16[1,2,128,512]{3,2,1,0:T(8,128)(2,1)S(1)}, bf16[1,2,128,512]{3,2,1,0:T(8,128)(2,1)}, u32[]{:S(2)}) copy-start(bf16[1,2,128,512]{3,2,1,0:T(8,128)(2,1)} %param.3) | copy-start | bytes 786436
  4.7 7.9 %collective-permute-start.2 = (bf16[128,512]{1,0:T(8,128)(2,1)S(1)}, bf16[128,512]{1,0:T(8,128)(2,1)S(1)}, u32[]{:S(2)}, u32[]{:S(2)}) collective-permute-start(bf16[128,512]{1,0:T(8,128)(2,1)S(1)} %get-tuple-element.31.after), channel_id=1, source_target_pairs={{16,0},{17,1},{18,2},{19,3},{20,4},{21,5},{22,6},{23,7},{24,8},{25... | collective-permute-start | bytes 393224 | tf_op jit(solution)/shard_map/ppermute | solution.py:286
  6.9 7.6 %collective-permute-start.5 = (bf16[64,640]{1,0:T(8,128)(2,1)S(1)}, bf16[64,640]{1,0:T(8,128)(2,1)S(1)}, u32[]{:S(2)}, u32[]{:S(2)}) collective-permute-start(bf16[64,640]{1,0:T(8,128)(2,1)S(1)} %get-tuple-element.41), channel_id=1, source_target_pairs={{0,3},{1,2},{2,1},{3,0},{4,7},{5,6},{6,5},{7,4},{8,11},{9,10},{10,... | collective-permute-start | bytes 245768 | tf_op jit(solution)/shard_map/ppermute | solution.py:238
  10.9 4.5 %collective-permute-start.6 = (bf16[64,640]{1,0:T(8,128)(2,1)S(1)}, bf16[64,640]{1,0:T(8,128)(2,1)S(1)}, u32[]{:S(2)}, u32[]{:S(2)}) collective-permute-start(bf16[64,640]{1,0:T(8,128)(2,1)S(1)} %get-tuple-element.42), channel_id=1, source_target_pairs={{0,1},{1,0},{2,3},{3,2},{4,5},{5,4},{6,7},{7,6},{8,9},{9,8},{10,11... | collective-permute-start | bytes 245768 | tf_op jit(solution)/shard_map/ppermute | solution.py:238
  11.4 4.4 %collective-permute-start.7 = (bf16[64,640]{1,0:T(8,128)(2,1)S(1)}, bf16[64,640]{1,0:T(8,128)(2,1)S(1)}, u32[]{:S(2)}, u32[]{:S(2)}) collective-permute-start(bf16[64,640]{1,0:T(8,128)(2,1)S(1)} %get-tuple-element.43), channel_id=1, source_target_pairs={{0,2},{1,3},{2,0},{3,1},{4,6},{5,7},{6,4},{7,5},{8,10},{9,11},{10,... | collective-permute-start | bytes 245768 | tf_op jit(solution)/shard_map/ppermute | solution.py:238
  14.4 4.1 %collective-permute-start.4 = (bf16[128,512]{1,0:T(8,128)(2,1)S(1)}, bf16[128,512]{1,0:T(8,128)(2,1)S(1)}, u32[]{:S(2)}, u32[]{:S(2)}) collective-permute-start(bf16[128,512]{1,0:T(8,128)(2,1)S(1)} %get-tuple-element.39), channel_id=1, source_target_pairs={{0,8},{8,0},{1,9},{9,1},{2,10},{10,2},{3,11},{11,3},{4,12},{12,4},... | collective-permute-start | bytes 393224 | tf_op jit(solution)/shard_map/ppermute | solution.py:312
  15.9 7.3 %collective-permute-start.9 = (bf16[64,640]{1,0:T(8,128)(2,1)S(1)}, bf16[64,640]{1,0:T(8,128)(2,1)S(1)}, u32[]{:S(2)}, u32[]{:S(2)}) collective-permute-start(bf16[64,640]{1,0:T(8,128)(2,1)S(1)} %shard_map.55.after.left), channel_id=1, source_target_pairs={{0,4},{4,0},{1,5},{5,1},{2,6},{6,2},{3,7},{7,3},{8,12},{12,8},{9,1... | collective-permute-start | bytes 245768 | tf_op jit(solution)/shard_map/ppermute | solution.py:246
  18.5 4.7 %collective-permute-start.3 = (bf16[128,512]{1,0:T(8,128)(2,1)S(1)}, bf16[128,512]{1,0:T(8,128)(2,1)S(1)}, u32[]{:S(2)}, u32[]{:S(2)}) collective-permute-start(bf16[128,512]{1,0:T(8,128)(2,1)S(1)} %get-tuple-element.36), channel_id=1, source_target_pairs={{0,8},{8,0},{1,9},{9,1},{2,10},{10,2},{3,11},{11,3},{4,12},{12,4},... | collective-permute-start | bytes 393224 | tf_op jit(solution)/shard_map/ppermute | solution.py:313
  19.6 9.1 %collective-permute-start.8 = (bf16[64,1664]{1,0:T(8,128)(2,1)S(1)}, bf16[64,1664]{1,0:T(8,128)(2,1)S(1)}, u32[]{:S(2)}, u32[]{:S(2)}) collective-permute-start(bf16[64,1664]{1,0:T(8,128)(2,1)S(1)} %get-tuple-element.45), channel_id=1, source_target_pairs={{0,3},{1,2},{2,1},{3,0},{4,7},{5,6},{6,5},{7,4},{8,11},{9,10},{10,... | collective-permute-start | bytes 638984 | tf_op jit(solution)/shard_map/ppermute | solution.py:238
  22.0 11.2 %collective-permute-start.13 = (bf16[64,1664]{1,0:T(8,128)(2,1)S(1)}, bf16[64,1664]{1,0:T(8,128)(2,1)S(1)}, u32[]{:S(2)}, u32[]{:S(2)}) collective-permute-start(bf16[64,1664]{1,0:T(8,128)(2,1)S(1)} %get-tuple-element.50), channel_id=1, source_target_pairs={{0,1},{1,0},{2,3},{3,2},{4,5},{5,4},{6,7},{7,6},{8,9},{9,8},{10,11... | collective-permute-start | bytes 638984 | tf_op jit(solution)/shard_map/ppermute | solution.py:238
  22.5 10.6 %collective-permute-start.14 = (bf16[64,1664]{1,0:T(8,128)(2,1)S(1)}, bf16[64,1664]{1,0:T(8,128)(2,1)S(1)}, u32[]{:S(2)}, u32[]{:S(2)}) collective-permute-start(bf16[64,1664]{1,0:T(8,128)(2,1)S(1)} %get-tuple-element.51), channel_id=1, source_target_pairs={{0,2},{1,3},{2,0},{3,1},{4,6},{5,7},{6,4},{7,5},{8,10},{9,11},{10,... | collective-permute-start | bytes 638984 | tf_op jit(solution)/shard_map/ppermute | solution.py:238
  28.8 1.0 %copy-start = (bf16[2,128,512]{2,1,0:T(8,128)(2,1)S(1)}, bf16[2,128,512]{2,1,0:T(8,128)(2,1)}, u32[]{:S(2)}) copy-start(bf16[2,128,512]{2,1,0:T(8,128)(2,1)} %shard_map.53.after) | copy-start | bytes 786436
  33.2 7.6 %collective-permute-start.15 = (bf16[64,640]{1,0:T(8,128)(2,1)S(1)}, bf16[64,640]{1,0:T(8,128)(2,1)S(1)}, u32[]{:S(2)}, u32[]{:S(2)}) collective-permute-start(bf16[64,640]{1,0:T(8,128)(2,1)S(1)} %slice.8.left), channel_id=1, source_target_pairs={{0,4},{4,0},{1,5},{5,1},{2,6},{6,2},{3,7},{7,3},{8,12},{12,8},{9,1... | collective-permute-start | bytes 245768 | tf_op jit(solution)/shard_map/ppermute | solution.py:246
  33.9 9.3 %collective-permute-start.12 = (bf16[64,640]{1,0:T(8,128)(2,1)S(1)}, bf16[64,640]{1,0:T(8,128)(2,1)S(1)}, u32[]{:S(2)}, u32[]{:S(2)}) collective-permute-start(bf16[64,640]{1,0:T(8,128)(2,1)S(1)} %get-tuple-element.46.refs_0_), channel_id=1, source_target_pairs={{0,3},{1,2},{2,1},{3,0},{4,7},{5,6},{6,5},{7,4},{8,11},{9,10},{10,... | collective-permute-start | bytes 245768 | tf_op jit(solution)/shard_map/ppermute | solution.py:238
  36.6 8.6 %collective-permute-start.11 = (bf16[64,640]{1,0:T(8,128)(2,1)S(1)}, bf16[64,640]{1,0:T(8,128)(2,1)S(1)}, u32[]{:S(2)}, u32[]{:S(2)}) collective-permute-start(bf16[64,640]{1,0:T(8,128)(2,1)S(1)} %get-tuple-element.46.refs_0_), channel_id=1, source_target_pairs={{0,2},{1,3},{2,0},{3,1},{4,6},{5,7},{6,4},{7,5},{8,10},{9,11},{10,... | collective-permute-start | bytes 245768 | tf_op jit(solution)/shard_map/ppermute | solution.py:238
  36.7 13.2 %collective-permute-start.19 = (bf16[64,1024]{1,0:T(8,128)(2,1)S(1)}, bf16[64,1024]{1,0:T(8,128)(2,1)S(1)}, u32[]{:S(2)}, u32[]{:S(2)}) collective-permute-start(bf16[64,1024]{1,0:T(8,128)(2,1)S(1)} %slice.9.left), channel_id=1, source_target_pairs={{0,4},{4,0},{1,5},{5,1},{2,6},{6,2},{3,7},{7,3},{8,12},{12,8},{9,1... | collective-permute-start | bytes 393224 | tf_op jit(solution)/shard_map/ppermute | solution.py:246
  39.0 6.9 %collective-permute-start.10 = (bf16[64,640]{1,0:T(8,128)(2,1)S(1)}, bf16[64,640]{1,0:T(8,128)(2,1)S(1)}, u32[]{:S(2)}, u32[]{:S(2)}) collective-permute-start(bf16[64,640]{1,0:T(8,128)(2,1)S(1)} %get-tuple-element.46.refs_0_), channel_id=1, source_target_pairs={{0,1},{1,0},{2,3},{3,2},{4,5},{5,4},{6,7},{7,6},{8,9},{9,8},{10,11... | collective-permute-start | bytes 245768 | tf_op jit(solution)/shard_map/ppermute | solution.py:238
  40.9 9.0 %collective-permute-start.18 = (bf16[64,640]{1,0:T(8,128)(2,1)S(1)}, bf16[64,640]{1,0:T(8,128)(2,1)S(1)}, u32[]{:S(2)}, u32[]{:S(2)}) collective-permute-start(bf16[64,640]{1,0:T(8,128)(2,1)S(1)} %shard_map.60.refs_0_.refs_1_), channel_id=1, source_target_pairs={{0,3},{1,2},{2,1},{3,0},{4,7},{5,6},{6,5},{7,4},{8,11},{9,10},{10,... | collective-permute-start | bytes 245768 | tf_op jit(solution)/shard_map/ppermute | solution.py:238
  43.2 6.7 %collective-permute-start.17 = (bf16[64,640]{1,0:T(8,128)(2,1)S(1)}, bf16[64,640]{1,0:T(8,128)(2,1)S(1)}, u32[]{:S(2)}, u32[]{:S(2)}) collective-permute-start(bf16[64,640]{1,0:T(8,128)(2,1)S(1)} %shard_map.60.refs_0_.refs_1_), channel_id=1, source_target_pairs={{0,2},{1,3},{2,0},{3,1},{4,6},{5,7},{6,4},{7,5},{8,10},{9,11},{10,... | collective-permute-start | bytes 245768 | tf_op jit(solution)/shard_map/ppermute | solution.py:238
  45.3 4.7 %collective-permute-start.16 = (bf16[64,640]{1,0:T(8,128)(2,1)S(1)}, bf16[64,640]{1,0:T(8,128)(2,1)S(1)}, u32[]{:S(2)}, u32[]{:S(2)}) collective-permute-start(bf16[64,640]{1,0:T(8,128)(2,1)S(1)} %shard_map.60.refs_0_.refs_1_), channel_id=1, source_target_pairs={{0,1},{1,0},{2,3},{3,2},{4,5},{5,4},{6,7},{7,6},{8,9},{9,8},{10,11... | collective-permute-start | bytes 245768 | tf_op jit(solution)/shard_map/ppermute | solution.py:238
  50.0 7.6 %collective-permute-start.22 = (bf16[64,1024]{1,0:T(8,128)(2,1)S(1)}, bf16[64,1024]{1,0:T(8,128)(2,1)S(1)}, u32[]{:S(2)}, u32[]{:S(2)}) collective-permute-start(bf16[64,1024]{1,0:T(8,128)(2,1)S(1)} %shard_map.62.refs_0_), channel_id=1, source_target_pairs={{0,3},{1,2},{2,1},{3,0},{4,7},{5,6},{6,5},{7,4},{8,11},{9,10},{10,... | collective-permute-start | bytes 393224 | tf_op jit(solution)/shard_map/ppermute | solution.py:238
  50.9 6.7 %collective-permute-start.21 = (bf16[64,1024]{1,0:T(8,128)(2,1)S(1)}, bf16[64,1024]{1,0:T(8,128)(2,1)S(1)}, u32[]{:S(2)}, u32[]{:S(2)}) collective-permute-start(bf16[64,1024]{1,0:T(8,128)(2,1)S(1)} %shard_map.62.refs_0_), channel_id=1, source_target_pairs={{0,2},{1,3},{2,0},{3,1},{4,6},{5,7},{6,4},{7,5},{8,10},{9,11},{10,... | collective-permute-start | bytes 393224 | tf_op jit(solution)/shard_map/ppermute | solution.py:238
  52.9 5.2 %collective-permute-start.20 = (bf16[64,1024]{1,0:T(8,128)(2,1)S(1)}, bf16[64,1024]{1,0:T(8,128)(2,1)S(1)}, u32[]{:S(2)}, u32[]{:S(2)}) collective-permute-start(bf16[64,1024]{1,0:T(8,128)(2,1)S(1)} %shard_map.62.refs_0_), channel_id=1, source_target_pairs={{0,1},{1,0},{2,3},{3,2},{4,5},{5,4},{6,7},{7,6},{8,9},{9,8},{10,11... | collective-permute-start | bytes 393224 | tf_op jit(solution)/shard_map/ppermute | solution.py:238

commit v11 on v10

--- a/solution.py
+++ b/solution.py
@@ -94,24 +94,25 @@
     kept[...] = local[...]
 
 
-def odd_kernel(where, own, partner, slope_own, slope_partner, arrived, last, dh, cot):
+def sum_kernel(*refs):
+    result = refs[-1]
+    result[...] = sum(piece[...].astype(F32) for piece in refs[:GROUP]).astype(BF16)
+
+
+def pass_kernel(*refs):
+    refs[-2][...] = sum(piece[...].astype(F32) for piece in refs[:GROUP]).astype(BF16)
+    refs[-1][...] = refs[GROUP][...]
+
+
+def layers_kernel(
+    where, own, partner, slope_own, slope_partner, arrived, last, own_dh, give_dh, own_cot, give_cot
+):
     upstream = jnp.where(where[2] == 1, last[...], arrived[...])
 
     def run(odd, even):
-        dh[...], cot[...] = layer(upstream, odd[1][...], odd[0][...])
-
-    by_core(where[0], run, (own, slope_own), (partner, slope_partner))
-
-
-def sum_kernel(*refs):
-    pieces, result = refs[:GROUP], refs[-1]
-    result[...] = sum(piece[...].astype(F32) for piece in pieces).astype(BF16)
-
-
-def even_kernel(where, own, partner, slope_own, slope_partner, dh, cot, own_dh, give_dh, own_cot, give_cot):
-    def run(odd, even):
-        odd[2][...], odd[3][...] = dh[...], cot[...]
-        even[2][...], even[3][...] = layer(cot[...], even[1][...], even[0][...])
+        dh, cot = layer(upstream, odd[1][...], odd[0][...])
+        odd[2][...], odd[3][...] = dh, cot
+        even[2][...], even[3][...] = layer(cot, even[1][...], even[0][...])
 
     by_core(
         where[0], run, (own, slope_own, own_dh, own_cot), (partner, slope_partner, give_dh, give_cot)
@@ -153,13 +154,8 @@
     refs[-1][...] = (left[...].astype(F32) + right[...].astype(F32)).astype(BF16)
 
 
-def begin_kernel(left, right, act, after, result, act_copy):
-    act_copy[...] = act[...]
-    result[...] = left[...].astype(F32) + right[...].astype(F32)
-
-
 def grad_kernel(where, local, dh_own, dh_got, after, *refs):
-    parts, (inputs, tokens, whole) = refs[:GROUP], refs[GROUP:]
+    factors, grads, (inputs, tokens, whole, rest) = refs[:GROUP], refs[GROUP:2 * GROUP], refs[2 * GROUP:]
     rows, width = local.shape[1:]
     inputs[:rows] = local[where[0]]
     inputs[rows:] = local[1 - where[0]]
@@ -170,10 +166,11 @@
     half = size // 2
     for u in range(GROUP):
         grad = moment(inputs[:, u * size:(u + 1) * size], tokens[...]).astype(BF16)
-        whole[u, :, 5 * size:5 * size + width] = grad[:half]
-        whole[u, :, 5 * size + width:] = grad[half:]
-    for step, part in enumerate(parts):
-        part[...] = whole[where[1] ^ step]
+        rest[u, :, :width] = grad[:half]
+        rest[u, :, width:] = grad[half:]
+    for step in range(GROUP):
+        factors[step][...] = whole[where[1] ^ step]
+        grads[step][...] = rest[where[1] ^ step]
 
 
 def invert(total, count):
@@ -300,13 +297,10 @@
     )(where, kept, first)
     act_pieces = send(act_parts)
 
-    dh_odd, cot_odd = call(odd_kernel, 64 * rows * width**2, [block] * 2, [SMEM] + [VMEM] * 6)(
-        where, own, partner, slope_own, slope_partner, arrived, last
-    )
     own_dh, give_dh, own_cot, give_cot = call(
-        even_kernel, 4 * rows * width**2, [block] * 4, [SMEM] + [VMEM] * 6
-    )(where, own, partner, slope_own, slope_partner, dh_odd, cot_odd)
-    act_sum = call(sum_kernel, 0, array(size // 2, factor), [VMEM] * GROUP + [ANY])(
+        layers_kernel, 64 * rows * width**2, [block] * 4, [SMEM] + [VMEM] * 6
+    )(where, own, partner, slope_own, slope_partner, arrived, last)
+    act_sum = call(sum_kernel, 24 * width**3, array(size // 2, factor), [VMEM] * GROUP + [ANY])(
         *(act_pieces[step] for step in (0, 3, 1, 2)), own_dh
     )
     got_dh = lax.ppermute(give_dh, "core", SWAP)
@@ -315,21 +309,24 @@
     parts = call(
         grad_kernel,
         4 * tokens * width**2,
-        [array(size // 2, factor + 2 * width)] * GROUP,
+        [array(size // 2, factor)] * GROUP + [array(size // 2, 2 * width)] * GROUP,
         [SMEM] + [VMEM] * 3 + [ANY],
         [pltpu.VMEM((tokens, width), BF16)] * 2
-        + [pltpu.VMEM((GROUP, size // 2, factor + 2 * width), BF16)],
+        + [pltpu.VMEM((GROUP, size // 2, factor), BF16), pltpu.VMEM((GROUP, size // 2, 2 * width), BF16)],
     )(where, kept, own_dh, got_dh, act_sum)
     cot = call(cot_kernel, 0, array(micro, rows, width), [SMEM, VMEM, VMEM])(where, own_cot, other_cot)
-    pieces = send(parts)
-    begun, act_part = call(
-        begin_kernel,
-        0,
-        [array(*parts[0].shape, dtype=F32), array(size // 2, factor)],
-        [VMEM] * 3 + [ANY],
-    )(pieces[0], pieces[3], exchange(act_sum, flops=24 * width**3), cot)
-    total = (begun + pieces[1].astype(F32) + pieces[2].astype(F32)).astype(BF16)
+
+    def summed(pieces):
+        shape = array(*pieces[0].shape)
+        return call(sum_kernel, 0, shape, [VMEM] * GROUP)(*(pieces[step] for step in (0, 3, 1, 2)))
+
+    pieces = send(parts[:GROUP])
+    factors, act_part = call(
+        pass_kernel, 0, [array(size // 2, factor)] * 2, [VMEM] * (GROUP + 1) + [ANY]
+    )(*(pieces[step] for step in (0, 3, 1, 2)), exchange(act_sum, flops=16 * width**3), cot)
+    out = send([exchange(factors)] * GROUP)
     act = send([act_part] * GROUP)
+    total = summed(send(parts[GROUP:]))
 
     def inverse(pieces, flops):
         return call(
@@ -341,8 +338,7 @@
         )(where, *pieces)
 
     act_inv = inverse(act, 0)
-    out = send([exchange(total[:, :factor])] * GROUP)
-    grad = send([exchange(total[:, factor:], (act_inv[0], *out))] * GROUP)
+    grad = send([exchange(total, (act_inv[0], *out))] * GROUP)
     update = call(
         update_kernel,
         10 * width**3,

time: 61.3 us -> 57.4 us (0.936)
  waiting for transfers between devices: 16.5 us -> 5.34 us
  starting transfers between devices: 23.9 us -> 31.8 us
    ppermute x15 -> x18, waiting for transfers between devices: 13.5 us -> 3.39 us  [send(): lax.ppermute(parts[step], ('near', 'side'), [(i, i ^ step) for i in range...]
    ppermute x15 -> x18, starting transfers between devices: 16.3 us -> 23.4 us  [send(): lax.ppermute(parts[step], ('near', 'side'), [(i, i ^ step) for i in range...]
    ppermute x3, waiting for transfers between devices: 1.07 us -> 0.01 us  [exchange(): got = lax.ppermute(value, 'far', route)]
  transfers between devices with their start and end apart: 23 -> 26, of which waited for: 10 -> 5; matrix products, arithmetic and copies ran while one was open for 2% -> 2% of each run, Pallas kernels for 22% -> 22%
where the time goes in v11:
time: 57.4 us; the launch traced here: 57.2 us
  starting transfers between devices  31.8 us (55%)
  Pallas kernels  17 us (30%)
  waiting for transfers between devices  5.34 us (9%)
  other arithmetic  1.26 us (2%)
  local copies, waits for them, and re-layouts  0.96 us (2%)
  between operations  0.8 us (1%)
    ppermute x18, starting transfers between devices, send(): lax.ppermute(parts[step], ('near', 'side'), [(i, i ^ step) for i in range...  23.4 us
    pallas_call x2, Pallas kernels, inverse(): call(functools.partial(inverse_kernel, count), flops, [array(width, width...  8.06 us
    ppermute x3, starting transfers between devices, exchange(): got = lax.ppermute(value, 'far', route)  5.98 us
    ppermute x18, waiting for transfers between devices, send(): lax.ppermute(parts[step], ('near', 'side'), [(i, i ^ step) for i in range...  3.39 us
    pallas_call x1, Pallas kernels, body(): call(update_kernel, 10 * width ** 3, array(width, width, dtype=F32), [SME...  2.91 us
    pallas_call x1, Pallas kernels, body(): call(first_kernel, 8 * rows * width ** 2, [array(width, width), array(mic...  1.46 us
    ppermute x1, starting transfers between devices, body(): upstream = lax.ppermute(down, 'row', [(r, r - 1) for r in range(1, pairs)])  1.29 us
    pallas_call x1, Pallas kernels, body(): call(cot_kernel, 0, array(micro, rows, width), [SMEM, VMEM, VMEM])  1.26 us
  transfers between devices with their start and end apart: 26, of which 5 were waited for; matrix products, arithmetic and copies ran while one was open for 2% of the time, Pallas kernels for 22%

profile of v11, /device:TPU:0, one launch (start us, length us, event | category | flops | bytes accessed | tf_op | source)
XLA Modules:
  0.0 57.2 jit_solution(15515595397014037213)
XLA Ops:
  0.6 0.5 collective-permute-start.1
  1.1 0.1 collective-permute-start
  1.2 1.1 %broadcast_select_fusion.weight = bf16[512,512]{1,0:T(8,128)(2,1)S(1)} fusion(pred[]{:T(512)S(6)} %gt.2, bf16[1,512,512]{2,1,0:T(8,128)(2,1)} %param.4), kind=kLoop, calls=%fused_computation | loop fusion | flops 262144 | bytes 1048577 | tf_op jit(solution)/shard_map/jit(_where)/select_n | solution.py:269
  2.4 0.1 pad_add_fusion.where
  2.5 0.0 collective-permute-done.1.partner_local
  2.5 0.7 %collective-permute-done.partner = bf16[512,512]{1,0:T(8,128)(2,1)S(1)} collective-permute-done((bf16[512,512]{1,0:T(8,128)(2,1)}, bf16[512,512]{1,0:T(8,128)(2,1)S(1)}, u32[]{:S(2)}, u32[]{:S(2)}) %collective-permute-start) | collective-permute-done | bytes 524320 | tf_op jit(solution)/shard_map/ppermute | solution.py:271
  3.3 1.5 %shard_map.50 = (bf16[512,512]{1,0:T(8,128)(2,1)S(1)}, bf16[2,128,512]{2,1,0:T(8,128)(2,1)S(1)}, bf16[128,512]{1,0:T(8,128)(2,1)S(1)}, f32[128,512]{1,0:T(8,128)...) custom-call(s32[3]{0:T(128)S(1)} %pad_add_fusion.where, bf16[512,512]{1,0:T(8,128)(2,1)S(1)} %broadcast_select_fusion.weight, ...), custom_call_target="tpu_custom_call" | custom-call | flops 268435456 | bytes 1048576 | tf_op jit(solution)/shard_map/pallas_call | solution.py:275
  4.7 1.3 %collective-permute-start.2 = (bf16[128,512]{1,0:T(8,128)(2,1)S(1)}, bf16[128,512]{1,0:T(8,128)(2,1)S(1)}, u32[]{:S(2)}, u32[]{:S(2)}) collective-permute-start(bf16[128,512]{1,0:T(8,128)(2,1)S(1)} %get-tuple-element.33.after), channel_id=1, source_target_pairs={{16,0},{17,1},{18,2},{19,3},{20,4},{21,5},{22,6},{23,7},{24,8},{25... | collective-permute-start | bytes 393224 | tf_op jit(solution)/shard_map/ppermute | solution.py:283
  6.0 0.9 %shard_map.53 = (bf16[64,640]{1,0:T(8,128)(2,1)S(1)}, bf16[64,640]{1,0:T(8,128)(2,1)S(1)}, bf16[64,640]{1,0:T(8,128)(2,1)S(1)}, bf16[64,640]{1,0:T(8,128)(2,1)S(1)}) custom-call(s32[3]{0:T(128)S(1)} %pad_add_fusion.where, bf16[2,128,512]{2,1,0:T(8,128)(2,1)S(1)} %get-tuple-element.37.local, bf16[128,512]{1,0:T(8,128)(2,1)S(1)} %get-tuple-element.33.after), custom_call_target="tpu_custom_call" | custom-call | flops 134217728 | bytes 1048576 | tf_op jit(solution)/shard_map/pallas_call | solution.py:291
  6.9 3.9 %collective-permute-start.5 = (bf16[64,640]{1,0:T(8,128)(2,1)S(1)}, bf16[64,640]{1,0:T(8,128)(2,1)S(1)}, u32[]{:S(2)}, u32[]{:S(2)}) collective-permute-start(bf16[64,640]{1,0:T(8,128)(2,1)S(1)} %get-tuple-element.41), channel_id=1, source_target_pairs={{0,3},{1,2},{2,1},{3,0},{4,7},{5,6},{6,5},{7,4},{8,11},{9,10},{10,... | collective-permute-start | bytes 245768 | tf_op jit(solution)/shard_map/ppermute | solution.py:235
  10.9 0.5 collective-permute-start.6
  11.4 0.1 collective-permute-start.7
  11.5 1.2 %collective-permute-done.2.arrived = bf16[128,512]{1,0:T(8,128)(2,1)S(1)} collective-permute-done((bf16[128,512]{1,0:T(8,128)(2,1)S(1)}, bf16[128,512]{1,0:T(8,128)(2,1)S(1)}, u32[]{:S(2)}, u32[]{:S(2)}) %collective-permute-start.2) | collective-permute-done | bytes 131104 | tf_op jit(solution)/shard_map/ppermute | solution.py:283
  12.7 1.1 %shard_map.51 = (bf16[128,512]{1,0:T(8,128)(2,1)S(1)}, bf16[128,512]{1,0:T(8,128)(2,1)S(1)}, bf16[128,512]{1,0:T(8,128)(2,1)S(1)}, bf16[128,512]{1,0:T(8,128)(2,1)S(1)}) custom-call(s32[3]{0:T(128)S(1)} %pad_add_fusion.where, bf16[512,512]{1,0:T(8,128)(2,1)S(1)} %get-tuple-element.30.own, bf16[512,512]{1,0:T(8,128)(2,1)S(1)} %collective-permute-done.partner, ...), custom_call_target="tpu_custom_call" | custom-call | flops 2147483648 | bytes 1048576 | tf_op jit(solution)/shard_map/pallas_call | solution.py:300
  13.8 0.1 collective-permute-start.3
  13.9 0.5 collective-permute-start.4
  14.4 0.0 collective-permute-done.5.refs_1_
  14.4 1.0 %collective-permute-done.6.refs_2_ = bf16[64,640]{1,0:T(8,128)(2,1)S(1)} collective-permute-done((bf16[64,640]{1,0:T(8,128)(2,1)S(1)}, bf16[64,640]{1,0:T(8,128)(2,1)S(1)}, u32[]{:S(2)}, u32[]{:S(2)}) %collective-permute-start.6) | collective-permute-done | bytes 81952 | tf_op jit(solution)/shard_map/ppermute | solution.py:235
  15.4 0.5 collective-permute-done.7.refs_3_
  15.9 2.7 %collective-permute-start.11 = (bf16[64,640]{1,0:T(8,128)(2,1)S(1)}, bf16[64,640]{1,0:T(8,128)(2,1)S(1)}, u32[]{:S(2)}, u32[]{:S(2)}) collective-permute-start(bf16[64,640]{1,0:T(8,128)(2,1)S(1)} %shard_map.54.after.left), channel_id=1, source_target_pairs={{0,4},{4,0},{1,5},{5,1},{2,6},{6,2},{3,7},{7,3},{8,12},{12,8},{9,1... | collective-permute-start | bytes 245768 | tf_op jit(solution)/shard_map/ppermute | solution.py:243
  18.6 0.0 collective-permute-done.4.dh_got
  18.6 1.0 %shard_map.55 = (bf16[64,640]{1,0:T(8,128)(2,1)S(1)}, bf16[64,640]{1,0:T(8,128)(2,1)S(1)}, bf16[64,640]{1,0:T(8,128)(2,1)S(1)}, bf16[64,640]{1,0:T(8,128)(2,1)S(...) custom-call(s32[3]{0:T(128)S(1)} %pad_add_fusion.where, ...), custom_call_target="tpu_custom_call" | custom-call | flops 268435456 | bytes 1048576 | tf_op jit(solution)/shard_map/pallas_call | solution.py:309
  19.6 1.9 %collective-permute-start.8 = (bf16[64,640]{1,0:T(8,128)(2,1)S(1)}, bf16[64,640]{1,0:T(8,128)(2,1)S(1)}, u32[]{:S(2)}, u32[]{:S(2)}) collective-permute-start(bf16[64,640]{1,0:T(8,128)(2,1)S(1)} %get-tuple-element.45), channel_id=1, source_target_pairs={{0,3},{1,2},{2,1},{3,0},{4,7},{5,6},{6,5},{7,4},{8,11},{9,10},{10,... | collective-permute-start | bytes 245768 | tf_op jit(solution)/shard_map/ppermute | solution.py:235
  21.6 0.9 %collective-permute-start.9 = (bf16[64,640]{1,0:T(8,128)(2,1)S(1)}, bf16[64,640]{1,0:T(8,128)(2,1)S(1)}, u32[]{:S(2)}, u32[]{:S(2)}) collective-permute-start(bf16[64,640]{1,0:T(8,128)(2,1)S(1)} %get-tuple-element.46), channel_id=1, source_target_pairs={{0,1},{1,0},{2,3},{3,2},{4,5},{5,4},{6,7},{7,6},{8,9},{9,8},{10,11... | collective-permute-start | bytes 245768 | tf_op jit(solution)/shard_map/ppermute | solution.py:235
  22.4 0.7 %collective-permute-start.10 = (bf16[64,640]{1,0:T(8,128)(2,1)S(1)}, bf16[64,640]{1,0:T(8,128)(2,1)S(1)}, u32[]{:S(2)}, u32[]{:S(2)}) collective-permute-start(bf16[64,640]{1,0:T(8,128)(2,1)S(1)} %get-tuple-element.47), channel_id=1, source_target_pairs={{0,2},{1,3},{2,0},{3,1},{4,6},{5,7},{6,4},{7,5},{8,10},{9,11},{10,... | collective-permute-start | bytes 245768 | tf_op jit(solution)/shard_map/ppermute | solution.py:235
  23.2 0.0 collective-permute-done.11.right
  23.2 1.9 %collective-permute-start.19 = (bf16[64,1024]{1,0:T(8,128)(2,1)S(1)}, bf16[64,1024]{1,0:T(8,128)(2,1)S(1)}, u32[]{:S(2)}, u32[]{:S(2)}) collective-permute-start(bf16[64,1024]{1,0:T(8,128)(2,1)S(1)} %get-tuple-element.55), channel_id=1, source_target_pairs={{0,3},{1,2},{2,1},{3,0},{4,7},{5,6},{6,5},{7,4},{8,11},{9,10},{10,... | collective-permute-start | bytes 393224 | tf_op jit(solution)/shard_map/ppermute | solution.py:235
  25.1 0.0 collective-permute-done.3.other_cot
  25.1 0.9 %collective-permute-start.20 = (bf16[64,1024]{1,0:T(8,128)(2,1)S(1)}, bf16[64,1024]{1,0:T(8,128)(2,1)S(1)}, u32[]{:S(2)}, u32[]{:S(2)}) collective-permute-start(bf16[64,1024]{1,0:T(8,128)(2,1)S(1)} %get-tuple-element.56), channel_id=1, source_target_pairs={{0,1},{1,0},{2,3},{3,2},{4,5},{5,4},{6,7},{7,6},{8,9},{9,8},{10,11... | collective-permute-start | bytes 393224 | tf_op jit(solution)/shard_map/ppermute | solution.py:235
  25.9 0.0 collective-permute-done.8.refs_1_
  25.9 1.2 %collective-permute-start.21 = (bf16[64,1024]{1,0:T(8,128)(2,1)S(1)}, bf16[64,1024]{1,0:T(8,128)(2,1)S(1)}, u32[]{:S(2)}, u32[]{:S(2)}) collective-permute-start(bf16[64,1024]{1,0:T(8,128)(2,1)S(1)} %get-tuple-element.57), channel_id=1, source_target_pairs={{0,2},{1,3},{2,0},{3,1},{4,6},{5,7},{6,4},{7,5},{8,10},{9,11},{10,... | collective-permute-start | bytes 393224 | tf_op jit(solution)/shard_map/ppermute | solution.py:235
  27.1 1.3 %shard_map.52.refs_5_ = bf16[2,128,512]{2,1,0:T(8,128)(2,1)} custom-call(s32[3]{0:T(128)S(1)} %pad_add_fusion.where, bf16[128,512]{1,0:T(8,128)(2,1)S(1)} %get-tuple-element.35.own_cot, bf16[128,512]{1,0:T(8,128)(2,1)S(1)} %collective-permute-done.3.other_cot), custom_call_target="tpu_custom_call" | custom-call | bytes 1048576 | tf_op jit(solution)/shard_map/pallas_call | solution.py:317
  28.4 0.0 collective-permute-done.9.refs_2_
  28.4 0.0 collective-permute-done.10.refs_3_
  28.4 0.9 %copy-done = bf16[2,128,512]{2,1,0:T(8,128)(2,1)S(1)} copy-done((bf16[2,128,512]{2,1,0:T(8,128)(2,1)S(1)}, bf16[2,128,512]{2,1,0:T(8,128)(2,1)}, u32[]{:S(2)}) %copy-start) | copy-done | bytes 262168
  29.4 1.9 %collective-permute-start.15 = (bf16[64,640]{1,0:T(8,128)(2,1)S(1)}, bf16[64,640]{1,0:T(8,128)(2,1)S(1)}, u32[]{:S(2)}, u32[]{:S(2)}) collective-permute-start(bf16[64,640]{1,0:T(8,128)(2,1)S(1)} %get-tuple-element.51.left), channel_id=1, source_target_pairs={{0,4},{4,0},{1,5},{5,1},{2,6},{6,2},{3,7},{7,3},{8,12},{12,8},{9,1... | collective-permute-start | bytes 245768 | tf_op jit(solution)/shard_map/ppermute | solution.py:243
  31.3 2.2 %collective-permute-start.14 = (bf16[64,640]{1,0:T(8,128)(2,1)S(1)}, bf16[64,640]{1,0:T(8,128)(2,1)S(1)}, u32[]{:S(2)}, u32[]{:S(2)}) collective-permute-start(bf16[64,640]{1,0:T(8,128)(2,1)S(1)} %get-tuple-element.48.refs_0_), channel_id=1, source_target_pairs={{0,3},{1,2},{2,1},{3,0},{4,7},{5,6},{6,5},{7,4},{8,11},{9,10},{10,... | collective-permute-start | bytes 245768 | tf_op jit(solution)/shard_map/ppermute | solution.py:235
  33.5 0.0 collective-permute-done.19.refs_1_
  33.5 0.1 collective-permute-start.13
  33.6 0.0 collective-permute-done.20.refs_2_
  33.6 0.0 collective-permute-done.21.refs_3_
  33.6 0.1 shard_map.61.left
  33.7 1.4 %collective-permute-start.22 = (bf16[64,1024]{1,0:T(8,128)(2,1)S(1)}, bf16[64,1024]{1,0:T(8,128)(2,1)S(1)}, u32[]{:S(2)}, u32[]{:S(2)}) collective-permute-start(bf16[64,1024]{1,0:T(8,128)(2,1)S(1)} %shard_map.61.left), channel_id=1, source_target_pairs={{0,4},{4,0},{1,5},{5,1},{2,6},{6,2},{3,7},{7,3},{8,12},{12,8},{9,1... | collective-permute-start | bytes 393224 | tf_op jit(solution)/shard_map/ppermute | solution.py:243
  35.1 0.9 %collective-permute-start.12 = (bf16[64,640]{1,0:T(8,128)(2,1)S(1)}, bf16[64,640]{1,0:T(8,128)(2,1)S(1)}, u32[]{:S(2)}, u32[]{:S(2)}) collective-permute-start(bf16[64,640]{1,0:T(8,128)(2,1)S(1)} %get-tuple-element.48.refs_0_), channel_id=1, source_target_pairs={{0,1},{1,0},{2,3},{3,2},{4,5},{5,4},{6,7},{7,6},{8,9},{9,8},{10,11... | collective-permute-start | bytes 245768 | tf_op jit(solution)/shard_map/ppermute | solution.py:235
  36.0 0.0 collective-permute-done.15.right
  36.0 3.6 %collective-permute-start.18 = (bf16[64,640]{1,0:T(8,128)(2,1)S(1)}, bf16[64,640]{1,0:T(8,128)(2,1)S(1)}, u32[]{:S(2)}, u32[]{:S(2)}) collective-permute-start(bf16[64,640]{1,0:T(8,128)(2,1)S(1)} %shard_map.59.refs_0_.refs_1_), channel_id=1, source_target_pairs={{0,3},{1,2},{2,1},{3,0},{4,7},{5,6},{6,5},{7,4},{8,11},{9,10},{10,... | collective-permute-start | bytes 245768 | tf_op jit(solution)/shard_map/ppermute | solution.py:235
  39.7 0.0 collective-permute-done.14.refs_3_
  39.7 0.0 collective-permute-start.17
  39.7 1.9 %collective-permute-done.13.refs_2_ = bf16[64,640]{1,0:T(8,128)(2,1)S(1)} collective-permute-done((bf16[64,640]{1,0:T(8,128)(2,1)S(1)}, bf16[64,640]{1,0:T(8,128)(2,1)S(1)}, u32[]{:S(2)}, u32[]{:S(2)}) %collective-permute-start.13) | collective-permute-done | bytes 81952 | tf_op jit(solution)/shard_map/ppermute | solution.py:235
  41.5 1.0 %collective-permute-start.16 = (bf16[64,640]{1,0:T(8,128)(2,1)S(1)}, bf16[64,640]{1,0:T(8,128)(2,1)S(1)}, u32[]{:S(2)}, u32[]{:S(2)}) collective-permute-start(bf16[64,640]{1,0:T(8,128)(2,1)S(1)} %shard_map.59.refs_0_.refs_1_), channel_id=1, source_target_pairs={{0,1},{1,0},{2,3},{3,2},{4,5},{5,4},{6,7},{7,6},{8,9},{9,8},{10,11... | collective-permute-start | bytes 245768 | tf_op jit(solution)/shard_map/ppermute | solution.py:235
  42.5 0.0 collective-permute-done.12.refs_1_
  42.5 4.0 %shard_map.58 = (bf16[512,512]{1,0:T(8,128)(2,1)S(1)}, bf16[512,512]{1,0:T(8,128)(2,1)S(1)}) custom-call(s32[3]{0:T(128)S(1)} %pad_add_fusion.where, bf16[64,640]{1,0:T(8,128)(2,1)S(1)} %get-tuple-element.48.refs_0_, bf16[64,640]{1,0:T(8,128)(2,1)S(1)} %collective-permute-done.12.refs_1_, bf16[64,640]{1,0:T(8,128)(2,1)S(1)} %collective-permute-done.13.refs_2_, ...), custom_call_target="tpu_custom_call" | custom-call | bytes 1048576 | tf_op jit(solution)/shard_map/pallas_call | solution.py:332
  46.5 0.0 collective-permute-done.18.refs_3_.refs_4_
  46.6 0.0 collective-permute-done.17.refs_2_.refs_3_
  46.6 0.0 collective-permute-done.16.refs_1_.refs_2_
  46.6 0.0 collective-permute-done.22.right
  46.6 1.1 %collective-permute-start.25 = (bf16[64,1024]{1,0:T(8,128)(2,1)S(1)}, bf16[64,1024]{1,0:T(8,128)(2,1)S(1)}, u32[]{:S(2)}, u32[]{:S(2)}) collective-permute-start(bf16[64,1024]{1,0:T(8,128)(2,1)S(1)} %shard_map.62.refs_0_), channel_id=1, source_target_pairs={{0,3},{1,2},{2,1},{3,0},{4,7},{5,6},{6,5},{7,4},{8,11},{9,10},{10,... | collective-permute-start | bytes 393224 | tf_op jit(solution)/shard_map/ppermute | solution.py:235
  47.8 1.5 %collective-permute-start.24 = (bf16[64,1024]{1,0:T(8,128)(2,1)S(1)}, bf16[64,1024]{1,0:T(8,128)(2,1)S(1)}, u32[]{:S(2)}, u32[]{:S(2)}) collective-permute-start(bf16[64,1024]{1,0:T(8,128)(2,1)S(1)} %shard_map.62.refs_0_), channel_id=1, source_target_pairs={{0,2},{1,3},{2,0},{3,1},{4,6},{5,7},{6,4},{7,5},{8,10},{9,11},{10,... | collective-permute-start | bytes 393224 | tf_op jit(solution)/shard_map/ppermute | solution.py:235
  49.2 1.0 %collective-permute-start.23 = (bf16[64,1024]{1,0:T(8,128)(2,1)S(1)}, bf16[64,1024]{1,0:T(8,128)(2,1)S(1)}, u32[]{:S(2)}, u32[]{:S(2)}) collective-permute-start(bf16[64,1024]{1,0:T(8,128)(2,1)S(1)} %shard_map.62.refs_0_), channel_id=1, source_target_pairs={{0,1},{1,0},{2,3},{3,2},{4,5},{5,4},{6,7},{7,6},{8,9},{9,8},{10,11... | collective-permute-start | bytes 393224 | tf_op jit(solution)/shard_map/ppermute | solution.py:235
  50.2 4.0 %shard_map.60 = (bf16[512,512]{1,0:T(8,128)(2,1)S(1)}, bf16[512,512]{1,0:T(8,128)(2,1)S(1)}) custom-call(s32[3]{0:T(128)S(1)} %pad_add_fusion.where, bf16[64,640]{1,0:T(8,128)(2,1)S(1)} %shard_map.59.refs_0_.refs_1_, bf16[64,640]{1,0:T(8,128)(2,1)S(1)} %collective-permute-done.16.refs_1_.refs_2_, ...), custom_call_target="tpu_custom_call" | custom-call | flops 2684354560 | bytes 1048576 | tf_op jit(solution)/shard_map/pallas_call | solution.py:332
  54.2 0.0 collective-permute-done.25.refs_3_
  54.2 0.0 collective-permute-done.24.refs_2_
  54.2 0.0 collective-permute-done.23.refs_1_
  54.3 2.9 %shard_map.63 = f32[512,512]{1,0:T(8,128)} custom-call(s32[3]{0:T(128)S(1)} %pad_add_fusion.where, bf16[512,512]{1,0:T(8,128)(2,1)S(1)} %get-tuple-element.49.refs_0_.act_high, bf16[512,512]{1,0:T(8,128)(2,1)S(1)} %get-tuple-element.50.act_low, bf16[512,512]{1,0:T(8,128)(2,1)S(1)} %get-tuple-element.52.out_high, ...), custom_call_target="tpu_custom_call" | custom-call | flops 1342177280 | bytes 1048576 | tf_op jit(solution)/shard_map/pallas_call | solution.py:342
  (11 shorter events, 0.2 us)
Async XLA Ops:
  0.6 1.9 %collective-permute-start.1 = (bf16[2,128,512]{2,1,0:T(8,128)(2,1)}, bf16[2,128,512]{2,1,0:T(8,128)(2,1)S(1)}, u32[]{:S(2)}, u32[]{:S(2)}) collective-permute-start(bf16[2,128,512]{2,1,0:T(8,128)(2,1)} %bitcast.11), channel_id=1, source_target_pairs={{0,8},{8,0},{1,9},{9,1},{2,10},{10,2},{3,11},{11,3},{4,12},{12,4},... | collective-permute-start | bytes 786440 | tf_op jit(solution)/shard_map/ppermute | solution.py:272
  1.1 2.1 %collective-permute-start = (bf16[512,512]{1,0:T(8,128)(2,1)}, bf16[512,512]{1,0:T(8,128)(2,1)S(1)}, u32[]{:S(2)}, u32[]{:S(2)}) collective-permute-start(bf16[512,512]{1,0:T(8,128)(2,1)} %bitcast.10), channel_id=1, source_target_pairs={{0,8},{8,0},{1,9},{9,1},{2,10},{10,2},{3,11},{11,3},{4,12},{12,4},... | collective-permute-start | bytes 1572872 | tf_op jit(solution)/shard_map/ppermute | solution.py:271
  1.2 1.2 %copy-start.1 = (bf16[2,128,512]{2,1,0:T(8,128)(2,1)S(1)}, bf16[2,128,512]{2,1,0:T(8,128)(2,1)}, u32[]{:S(2)}) copy-start(bf16[2,128,512]{2,1,0:T(8,128)(2,1)} %param.5) | copy-start | bytes 786436
  1.2 1.2 %copy-start.2 = (bf16[1,2,128,512]{3,2,1,0:T(8,128)(2,1)S(1)}, bf16[1,2,128,512]{3,2,1,0:T(8,128)(2,1)}, u32[]{:S(2)}) copy-start(bf16[1,2,128,512]{3,2,1,0:T(8,128)(2,1)} %param.3) | copy-start | bytes 786436
  4.7 7.9 %collective-permute-start.2 = (bf16[128,512]{1,0:T(8,128)(2,1)S(1)}, bf16[128,512]{1,0:T(8,128)(2,1)S(1)}, u32[]{:S(2)}, u32[]{:S(2)}) collective-permute-start(bf16[128,512]{1,0:T(8,128)(2,1)S(1)} %get-tuple-element.33.after), channel_id=1, source_target_pairs={{16,0},{17,1},{18,2},{19,3},{20,4},{21,5},{22,6},{23,7},{24,8},{25... | collective-permute-start | bytes 393224 | tf_op jit(solution)/shard_map/ppermute | solution.py:283
  6.9 7.4 %collective-permute-start.5 = (bf16[64,640]{1,0:T(8,128)(2,1)S(1)}, bf16[64,640]{1,0:T(8,128)(2,1)S(1)}, u32[]{:S(2)}, u32[]{:S(2)}) collective-permute-start(bf16[64,640]{1,0:T(8,128)(2,1)S(1)} %get-tuple-element.41), channel_id=1, source_target_pairs={{0,3},{1,2},{2,1},{3,0},{4,7},{5,6},{6,5},{7,4},{8,11},{9,10},{10,... | collective-permute-start | bytes 245768 | tf_op jit(solution)/shard_map/ppermute | solution.py:235
  10.9 4.5 %collective-permute-start.6 = (bf16[64,640]{1,0:T(8,128)(2,1)S(1)}, bf16[64,640]{1,0:T(8,128)(2,1)S(1)}, u32[]{:S(2)}, u32[]{:S(2)}) collective-permute-start(bf16[64,640]{1,0:T(8,128)(2,1)S(1)} %get-tuple-element.42), channel_id=1, source_target_pairs={{0,1},{1,0},{2,3},{3,2},{4,5},{5,4},{6,7},{7,6},{8,9},{9,8},{10,11... | collective-permute-start | bytes 245768 | tf_op jit(solution)/shard_map/ppermute | solution.py:235
  11.4 4.4 %collective-permute-start.7 = (bf16[64,640]{1,0:T(8,128)(2,1)S(1)}, bf16[64,640]{1,0:T(8,128)(2,1)S(1)}, u32[]{:S(2)}, u32[]{:S(2)}) collective-permute-start(bf16[64,640]{1,0:T(8,128)(2,1)S(1)} %get-tuple-element.43), channel_id=1, source_target_pairs={{0,2},{1,3},{2,0},{3,1},{4,6},{5,7},{6,4},{7,5},{8,10},{9,11},{10,... | collective-permute-start | bytes 245768 | tf_op jit(solution)/shard_map/ppermute | solution.py:235
  13.8 11.3 %collective-permute-start.3 = (bf16[128,512]{1,0:T(8,128)(2,1)S(1)}, bf16[128,512]{1,0:T(8,128)(2,1)S(1)}, u32[]{:S(2)}, u32[]{:S(2)}) collective-permute-start(bf16[128,512]{1,0:T(8,128)(2,1)S(1)} %get-tuple-element.36), channel_id=1, source_target_pairs={{0,8},{8,0},{1,9},{9,1},{2,10},{10,2},{3,11},{11,3},{4,12},{12,4},... | collective-permute-start | bytes 393224 | tf_op jit(solution)/shard_map/ppermute | solution.py:307
  13.9 4.7 %collective-permute-start.4 = (bf16[128,512]{1,0:T(8,128)(2,1)S(1)}, bf16[128,512]{1,0:T(8,128)(2,1)S(1)}, u32[]{:S(2)}, u32[]{:S(2)}) collective-permute-start(bf16[128,512]{1,0:T(8,128)(2,1)S(1)} %get-tuple-element.39), channel_id=1, source_target_pairs={{0,8},{8,0},{1,9},{9,1},{2,10},{10,2},{3,11},{11,3},{4,12},{12,4},... | collective-permute-start | bytes 393224 | tf_op jit(solution)/shard_map/ppermute | solution.py:306
  15.9 7.3 %collective-permute-start.11 = (bf16[64,640]{1,0:T(8,128)(2,1)S(1)}, bf16[64,640]{1,0:T(8,128)(2,1)S(1)}, u32[]{:S(2)}, u32[]{:S(2)}) collective-permute-start(bf16[64,640]{1,0:T(8,128)(2,1)S(1)} %shard_map.54.after.left), channel_id=1, source_target_pairs={{0,4},{4,0},{1,5},{5,1},{2,6},{6,2},{3,7},{7,3},{8,12},{12,8},{9,1... | collective-permute-start | bytes 245768 | tf_op jit(solution)/shard_map/ppermute | solution.py:243
  19.6 6.3 %collective-permute-start.8 = (bf16[64,640]{1,0:T(8,128)(2,1)S(1)}, bf16[64,640]{1,0:T(8,128)(2,1)S(1)}, u32[]{:S(2)}, u32[]{:S(2)}) collective-permute-start(bf16[64,640]{1,0:T(8,128)(2,1)S(1)} %get-tuple-element.45), channel_id=1, source_target_pairs={{0,3},{1,2},{2,1},{3,0},{4,7},{5,6},{6,5},{7,4},{8,11},{9,10},{10,... | collective-permute-start | bytes 245768 | tf_op jit(solution)/shard_map/ppermute | solution.py:235
  21.6 6.8 %collective-permute-start.9 = (bf16[64,640]{1,0:T(8,128)(2,1)S(1)}, bf16[64,640]{1,0:T(8,128)(2,1)S(1)}, u32[]{:S(2)}, u32[]{:S(2)}) collective-permute-start(bf16[64,640]{1,0:T(8,128)(2,1)S(1)} %get-tuple-element.46), channel_id=1, source_target_pairs={{0,1},{1,0},{2,3},{3,2},{4,5},{5,4},{6,7},{7,6},{8,9},{9,8},{10,11... | collective-permute-start | bytes 245768 | tf_op jit(solution)/shard_map/ppermute | solution.py:235
  22.4 6.0 %collective-permute-start.10 = (bf16[64,640]{1,0:T(8,128)(2,1)S(1)}, bf16[64,640]{1,0:T(8,128)(2,1)S(1)}, u32[]{:S(2)}, u32[]{:S(2)}) collective-permute-start(bf16[64,640]{1,0:T(8,128)(2,1)S(1)} %get-tuple-element.47), channel_id=1, source_target_pairs={{0,2},{1,3},{2,0},{3,1},{4,6},{5,7},{6,4},{7,5},{8,10},{9,11},{10,... | collective-permute-start | bytes 245768 | tf_op jit(solution)/shard_map/ppermute | solution.py:235
  23.2 10.3 %collective-permute-start.19 = (bf16[64,1024]{1,0:T(8,128)(2,1)S(1)}, bf16[64,1024]{1,0:T(8,128)(2,1)S(1)}, u32[]{:S(2)}, u32[]{:S(2)}) collective-permute-start(bf16[64,1024]{1,0:T(8,128)(2,1)S(1)} %get-tuple-element.55), channel_id=1, source_target_pairs={{0,3},{1,2},{2,1},{3,0},{4,7},{5,6},{6,5},{7,4},{8,11},{9,10},{10,... | collective-permute-start | bytes 393224 | tf_op jit(solution)/shard_map/ppermute | solution.py:235
  25.1 8.6 %collective-permute-start.20 = (bf16[64,1024]{1,0:T(8,128)(2,1)S(1)}, bf16[64,1024]{1,0:T(8,128)(2,1)S(1)}, u32[]{:S(2)}, u32[]{:S(2)}) collective-permute-start(bf16[64,1024]{1,0:T(8,128)(2,1)S(1)} %get-tuple-element.56), channel_id=1, source_target_pairs={{0,1},{1,0},{2,3},{3,2},{4,5},{5,4},{6,7},{7,6},{8,9},{9,8},{10,11... | collective-permute-start | bytes 393224 | tf_op jit(solution)/shard_map/ppermute | solution.py:235
  25.9 7.7 %collective-permute-start.21 = (bf16[64,1024]{1,0:T(8,128)(2,1)S(1)}, bf16[64,1024]{1,0:T(8,128)(2,1)S(1)}, u32[]{:S(2)}, u32[]{:S(2)}) collective-permute-start(bf16[64,1024]{1,0:T(8,128)(2,1)S(1)} %get-tuple-element.57), channel_id=1, source_target_pairs={{0,2},{1,3},{2,0},{3,1},{4,6},{5,7},{6,4},{7,5},{8,10},{9,11},{10,... | collective-permute-start | bytes 393224 | tf_op jit(solution)/shard_map/ppermute | solution.py:235
  28.4 1.0 %copy-start = (bf16[2,128,512]{2,1,0:T(8,128)(2,1)S(1)}, bf16[2,128,512]{2,1,0:T(8,128)(2,1)}, u32[]{:S(2)}) copy-start(bf16[2,128,512]{2,1,0:T(8,128)(2,1)} %shard_map.52.refs_5_) | copy-start | bytes 786436
  29.4 6.6 %collective-permute-start.15 = (bf16[64,640]{1,0:T(8,128)(2,1)S(1)}, bf16[64,640]{1,0:T(8,128)(2,1)S(1)}, u32[]{:S(2)}, u32[]{:S(2)}) collective-permute-start(bf16[64,640]{1,0:T(8,128)(2,1)S(1)} %get-tuple-element.51.left), channel_id=1, source_target_pairs={{0,4},{4,0},{1,5},{5,1},{2,6},{6,2},{3,7},{7,3},{8,12},{12,8},{9,1... | collective-permute-start | bytes 245768 | tf_op jit(solution)/shard_map/ppermute | solution.py:243
  31.3 8.4 %collective-permute-start.14 = (bf16[64,640]{1,0:T(8,128)(2,1)S(1)}, bf16[64,640]{1,0:T(8,128)(2,1)S(1)}, u32[]{:S(2)}, u32[]{:S(2)}) collective-permute-start(bf16[64,640]{1,0:T(8,128)(2,1)S(1)} %get-tuple-element.48.refs_0_), channel_id=1, source_target_pairs={{0,3},{1,2},{2,1},{3,0},{4,7},{5,6},{6,5},{7,4},{8,11},{9,10},{10,... | collective-permute-start | bytes 245768 | tf_op jit(solution)/shard_map/ppermute | solution.py:235
  33.5 8.1 %collective-permute-start.13 = (bf16[64,640]{1,0:T(8,128)(2,1)S(1)}, bf16[64,640]{1,0:T(8,128)(2,1)S(1)}, u32[]{:S(2)}, u32[]{:S(2)}) collective-permute-start(bf16[64,640]{1,0:T(8,128)(2,1)S(1)} %get-tuple-element.48.refs_0_), channel_id=1, source_target_pairs={{0,2},{1,3},{2,0},{3,1},{4,6},{5,7},{6,4},{7,5},{8,10},{9,11},{10,... | collective-permute-start | bytes 245768 | tf_op jit(solution)/shard_map/ppermute | solution.py:235
  33.7 12.9 %collective-permute-start.22 = (bf16[64,1024]{1,0:T(8,128)(2,1)S(1)}, bf16[64,1024]{1,0:T(8,128)(2,1)S(1)}, u32[]{:S(2)}, u32[]{:S(2)}) collective-permute-start(bf16[64,1024]{1,0:T(8,128)(2,1)S(1)} %shard_map.61.left), channel_id=1, source_target_pairs={{0,4},{4,0},{1,5},{5,1},{2,6},{6,2},{3,7},{7,3},{8,12},{12,8},{9,1... | collective-permute-start | bytes 393224 | tf_op jit(solution)/shard_map/ppermute | solution.py:243
  35.1 7.4 %collective-permute-start.12 = (bf16[64,640]{1,0:T(8,128)(2,1)S(1)}, bf16[64,640]{1,0:T(8,128)(2,1)S(1)}, u32[]{:S(2)}, u32[]{:S(2)}) collective-permute-start(bf16[64,640]{1,0:T(8,128)(2,1)S(1)} %get-tuple-element.48.refs_0_), channel_id=1, source_target_pairs={{0,1},{1,0},{2,3},{3,2},{4,5},{5,4},{6,7},{7,6},{8,9},{9,8},{10,11... | collective-permute-start | bytes 245768 | tf_op jit(solution)/shard_map/ppermute | solution.py:235
  36.0 10.5 %collective-permute-start.18 = (bf16[64,640]{1,0:T(8,128)(2,1)S(1)}, bf16[64,640]{1,0:T(8,128)(2,1)S(1)}, u32[]{:S(2)}, u32[]{:S(2)}) collective-permute-start(bf16[64,640]{1,0:T(8,128)(2,1)S(1)} %shard_map.59.refs_0_.refs_1_), channel_id=1, source_target_pairs={{0,3},{1,2},{2,1},{3,0},{4,7},{5,6},{6,5},{7,4},{8,11},{9,10},{10,... | collective-permute-start | bytes 245768 | tf_op jit(solution)/shard_map/ppermute | solution.py:235
  39.7 6.9 %collective-permute-start.17 = (bf16[64,640]{1,0:T(8,128)(2,1)S(1)}, bf16[64,640]{1,0:T(8,128)(2,1)S(1)}, u32[]{:S(2)}, u32[]{:S(2)}) collective-permute-start(bf16[64,640]{1,0:T(8,128)(2,1)S(1)} %shard_map.59.refs_0_.refs_1_), channel_id=1, source_target_pairs={{0,2},{1,3},{2,0},{3,1},{4,6},{5,7},{6,4},{7,5},{8,10},{9,11},{10,... | collective-permute-start | bytes 245768 | tf_op jit(solution)/shard_map/ppermute | solution.py:235
  41.5 5.0 %collective-permute-start.16 = (bf16[64,640]{1,0:T(8,128)(2,1)S(1)}, bf16[64,640]{1,0:T(8,128)(2,1)S(1)}, u32[]{:S(2)}, u32[]{:S(2)}) collective-permute-start(bf16[64,640]{1,0:T(8,128)(2,1)S(1)} %shard_map.59.refs_0_.refs_1_), channel_id=1, source_target_pairs={{0,1},{1,0},{2,3},{3,2},{4,5},{5,4},{6,7},{7,6},{8,9},{9,8},{10,11... | collective-permute-start | bytes 245768 | tf_op jit(solution)/shard_map/ppermute | solution.py:235
  46.6 7.6 %collective-permute-start.25 = (bf16[64,1024]{1,0:T(8,128)(2,1)S(1)}, bf16[64,1024]{1,0:T(8,128)(2,1)S(1)}, u32[]{:S(2)}, u32[]{:S(2)}) collective-permute-start(bf16[64,1024]{1,0:T(8,128)(2,1)S(1)} %shard_map.62.refs_0_), channel_id=1, source_target_pairs={{0,3},{1,2},{2,1},{3,0},{4,7},{5,6},{6,5},{7,4},{8,11},{9,10},{10,... | collective-permute-start | bytes 393224 | tf_op jit(solution)/shard_map/ppermute | solution.py:235
  47.8 6.5 %collective-permute-start.24 = (bf16[64,1024]{1,0:T(8,128)(2,1)S(1)}, bf16[64,1024]{1,0:T(8,128)(2,1)S(1)}, u32[]{:S(2)}, u32[]{:S(2)}) collective-permute-start(bf16[64,1024]{1,0:T(8,128)(2,1)S(1)} %shard_map.62.refs_0_), channel_id=1, source_target_pairs={{0,2},{1,3},{2,0},{3,1},{4,6},{5,7},{6,4},{7,5},{8,10},{9,11},{10,... | collective-permute-start | bytes 393224 | tf_op jit(solution)/shard_map/ppermute | solution.py:235
  49.2 5.0 %collective-permute-start.23 = (bf16[64,1024]{1,0:T(8,128)(2,1)S(1)}, bf16[64,1024]{1,0:T(8,128)(2,1)S(1)}, u32[]{:S(2)}, u32[]{:S(2)}) collective-permute-start(bf16[64,1024]{1,0:T(8,128)(2,1)S(1)} %shard_map.62.refs_0_), channel_id=1, source_target_pairs={{0,1},{1,0},{2,3},{3,2},{4,5},{5,4},{6,7},{7,6},{8,9},{9,8},{10,11... | collective-permute-start | bytes 393224 | tf_op jit(solution)/shard_map/ppermute | solution.py:235

commit v12 on v11

--- a/solution.py
+++ b/solution.py
@@ -52,16 +52,8 @@
     return high, (value - high.astype(F32)).astype(BF16)
 
 
-def product(left, right, dims=((1,), (0,))):
-    def dot(a, b):
-        return lax.dot_general(a, b, (dims, ((), ())), preferred_element_type=F32)
-
-    total = dot(left[0], right[0])
-    if len(right) > 1:
-        total += dot(left[0], right[1])
-    if len(left) > 1:
-        total += dot(left[1], right[0])
-    return total
+def dot(left, right):
+    return jnp.dot(left.astype(BF16), right.astype(BF16), preferred_element_type=F32)
 
 
 def call(kernel, flops, out_shape, in_specs, scratch=(), out_spec=VMEM):
@@ -117,11 +109,6 @@
     by_core(
         where[0], run, (own, slope_own, own_dh, own_cot), (partner, slope_partner, give_dh, give_cot)
     )
-
-
-def cot_kernel(where, own_cot, other_cot, result):
-    result[where[0]] = own_cot[...]
-    result[1 - where[0]] = other_cot[...]
 
 
 def put_factor(tokens, whole):
@@ -181,24 +168,25 @@
     mean = total[...].astype(F32) * (1.0 / count)
     full = mean + ridge * eye
     scale = lax.rsqrt(jnp.sum(full * full, keepdims=True))
-    squared = product((total[...],), (total[...],)) * (1.0 / count) ** 2 + ridge * (mean + full)
+    squared = dot(total[...], total[...]) * (1.0 / count) ** 2 + ridge * (mean + full)
     second = (2.0 * scale) * full - squared * (scale * scale)
-    second_terms = split(second)
-    last = 2.0 * (eye - second) + product(second_terms, second_terms)
-    tail = 2.0 * last - product(second_terms, split(last))
-    inner = product((total[...],), split(tail)) * (scale * (1.0 / count))
+    last = 2.0 * (eye - second) + dot(second, second)
+    tail = 2.0 * last - dot(second, last)
+    inner = dot(total[...], tail) * (scale * (1.0 / count))
     return split(((2.0 - ridge * scale) * tail - inner) * scale)
+
 
 def inverse_kernel(count, where, *refs):
     pieces, (high, low, blocks, total) = refs[:GROUP], refs[GROUP:]
     for step, piece in enumerate(pieces):
-        blocks[where[1] ^ step] = piece[...].astype(F32)
+        blocks[where[1] ^ step] = piece[...]
     size = total.shape[0] // GROUP
 
     def both(row, column, value):
-        total[row * size:(row + 1) * size, column * size:(column + 1) * size] = value.astype(BF16)
+        total[row * size:(row + 1) * size, column * size:(column + 1) * size] = value
         if row != column:
-            total[column * size:(column + 1) * size, row * size:(row + 1) * size] = value.T.astype(BF16)
+            turned = value.astype(F32).T.astype(BF16)
+            total[column * size:(column + 1) * size, row * size:(row + 1) * size] = turned
 
     for u in range(GROUP):
         main = jnp.concatenate([blocks[u, :, :2 * size], blocks[u, :, 2 * size:4 * size]])
@@ -210,20 +198,25 @@
         result[...] = term
 
 
-def update_kernel(where, act_high, act_low, out_high, out_low, *refs):
-    pieces, (result, grad, update, done) = refs[:GROUP], refs[GROUP:]
+def update_kernel(where, act_high, act_low, out_high, out_low, own_cot, other_cot, *refs):
+    pieces, (result, cot, grad, update, done) = refs[:GROUP], refs[GROUP:]
+    copies = [
+        pltpu.make_async_copy(own_cot, cot.at[where[0]], done.at[0]),
+        pltpu.make_async_copy(other_cot, cot.at[1 - where[0]], done.at[1]),
+    ]
+    for copy in copies:
+        copy.start()
     half, twice = pieces[0].shape
     width = twice // 2
     for step, piece in enumerate(pieces):
         start = pl.multiple_of((where[1] ^ step) * 2 * half, 2 * half)
         grad[pl.ds(start, half)] = piece[:, :width]
         grad[pl.ds(start + half, half)] = piece[:, width:]
-    left = product((act_high[...], act_low[...]), (grad[...],))
-    copies = []
+    left = (dot(act_high[...], grad[...]) + dot(act_low[...], grad[...])).astype(BF16)
     for part in range(2):
-        rows = pl.ds(part * 4 * half, 4 * half)
-        update[rows] = product(split(left[part * 4 * half:(part + 1) * 4 * half]), (out_high[...], out_low[...]))
-        copies.append(pltpu.make_async_copy(update.at[rows], result.at[rows], done.at[part]))
+        rows = slice(part * width // 2, (part + 1) * width // 2)
+        update[rows] = dot(left[rows], out_high[...]) + dot(left[rows], out_low[...])
+        copies.append(pltpu.make_async_copy(update.at[rows], result.at[rows], done.at[2 + part]))
         copies[-1].start()
     for copy in copies:
         copy.wait()
@@ -314,7 +307,6 @@
         [pltpu.VMEM((tokens, width), BF16)] * 2
         + [pltpu.VMEM((GROUP, size // 2, factor), BF16), pltpu.VMEM((GROUP, size // 2, 2 * width), BF16)],
     )(where, kept, own_dh, got_dh, act_sum)
-    cot = call(cot_kernel, 0, array(micro, rows, width), [SMEM, VMEM, VMEM])(where, own_cot, other_cot)
 
     def summed(pieces):
         shape = array(*pieces[0].shape)
@@ -322,8 +314,8 @@
 
     pieces = send(parts[:GROUP])
     factors, act_part = call(
-        pass_kernel, 0, [array(size // 2, factor)] * 2, [VMEM] * (GROUP + 1) + [ANY]
-    )(*(pieces[step] for step in (0, 3, 1, 2)), exchange(act_sum, flops=16 * width**3), cot)
+        pass_kernel, 0, [array(size // 2, factor)] * 2, [VMEM] * (GROUP + 1)
+    )(*(pieces[step] for step in (0, 3, 1, 2)), exchange(act_sum, flops=16 * width**3))
     out = send([exchange(factors)] * GROUP)
     act = send([act_part] * GROUP)
     total = summed(send(parts[GROUP:]))
@@ -334,23 +326,23 @@
             flops,
             [array(width, width)] * 2,
             [SMEM] + [VMEM] * GROUP,
-            [pltpu.VMEM((GROUP, size // 2, factor), F32), pltpu.VMEM((width, width), BF16)],
+            [pltpu.VMEM((GROUP, size // 2, factor), BF16), pltpu.VMEM((width, width), BF16)],
         )(where, *pieces)
 
     act_inv = inverse(act, 0)
     grad = send([exchange(total, (act_inv[0], *out))] * GROUP)
-    update = call(
+    update, cot = call(
         update_kernel,
         10 * width**3,
-        array(width, width, dtype=F32),
-        [SMEM] + [VMEM] * (4 + GROUP),
+        [array(width, width, dtype=F32), array(micro, rows, width)],
+        [SMEM] + [VMEM] * (6 + GROUP),
         [
             pltpu.VMEM((width, width), BF16),
             pltpu.VMEM((width, width), F32),
-            pltpu.SemaphoreType.DMA((2,)),
+            pltpu.SemaphoreType.DMA((4,)),
         ],
         HBM,
-    )(where, *act_inv, *inverse(out, 20 * width**3), *grad)
+    )(where, *act_inv, *inverse(out, 20 * width**3), own_cot, other_cot, *grad)
     return (cot[None], update[None])
 
 

time: 57.4 us -> 56.3 us (0.981)
  waiting for transfers between devices: 5.34 us -> 14.5 us
  starting transfers between devices: 31.8 us -> 26.9 us
  Pallas kernels: 17 us -> 12.8 us
  local copies, waits for them, and re-layouts: 0.96 us -> 0.01 us
    ppermute x18, waiting for transfers between devices: 3.39 us -> 12.5 us  [send(): lax.ppermute(parts[step], ('near', 'side'), [(i, i ^ step) for i in range...]
    ppermute x3, starting transfers between devices: 5.98 us -> 3.16 us  [exchange(): got = lax.ppermute(value, 'far', route)]
    pallas_call x2, Pallas kernels: 8.06 us -> 5.35 us  [inverse(): call(functools.partial(inverse_kernel, count), flops, [array(width, width...]
    ppermute x18, starting transfers between devices: 23.4 us -> 21.7 us  [send(): lax.ppermute(parts[step], ('near', 'side'), [(i, i ^ step) for i in range...]
    pallas_call x3 -> x2, Pallas kernels: 4.22 us -> 2.75 us  [the longest x1 2.71 us: body(): call(update_kernel, 10 * width ** 3, [array(width, width, dtype=F32), arr...]
    unnamed x6 -> x4, local copies, waits for them, and re-layouts: 0.96 us -> 0.01 us
  transfers between devices with their start and end apart: 26 -> 26, of which waited for: 5 -> 16; matrix products, arithmetic and copies ran while one was open for 2% -> 2% of each run, Pallas kernels for 22% -> 15%
where the time goes in v12:
time: 56.3 us; the launch traced here: 56.2 us
  starting transfers between devices  26.9 us (48%)
  waiting for transfers between devices  14.5 us (26%)
  Pallas kernels  12.8 us (23%)
  other arithmetic  1.26 us (2%)
  between operations  0.77 us (1%)
    ppermute x18, starting transfers between devices, send(): lax.ppermute(parts[step], ('near', 'side'), [(i, i ^ step) for i in range...  21.7 us
    ppermute x18, waiting for transfers between devices, send(): lax.ppermute(parts[step], ('near', 'side'), [(i, i ^ step) for i in range...  12.5 us
    pallas_call x2, Pallas kernels, inverse(): call(functools.partial(inverse_kernel, count), flops, [array(width, width...  5.35 us
    ppermute x3, starting transfers between devices, exchange(): got = lax.ppermute(value, 'far', route)  3.16 us
    pallas_call x1, Pallas kernels, body(): call(update_kernel, 10 * width ** 3, [array(width, width, dtype=F32), arr...  2.71 us
    pallas_call x1, Pallas kernels, body(): call(first_kernel, 8 * rows * width ** 2, [array(width, width), array(mic...  1.46 us
    ppermute x1, starting transfers between devices, body(): upstream = lax.ppermute(down, 'row', [(r, r - 1) for r in range(1, pairs)])  1.29 us
    select_n x2, other arithmetic, near_copy(): return jnp.where(core > 1, jnp.zeros_like(value), value)  1.18 us
  transfers between devices with their start and end apart: 26, of which 16 were waited for; matrix products, arithmetic and copies ran while one was open for 2% of the time, Pallas kernels for 15%

profile of v12, /device:TPU:0, one launch (start us, length us, event | category | flops | bytes accessed | tf_op | source)
XLA Modules:
  0.0 56.2 jit_solution(8375452470912250300)
XLA Ops:
  0.6 0.5 collective-permute-start.1
  1.1 0.1 collective-permute-start
  1.2 1.1 %broadcast_select_fusion.weight = bf16[512,512]{1,0:T(8,128)(2,1)S(1)} fusion(pred[]{:T(512)S(6)} %gt.2, bf16[1,512,512]{2,1,0:T(8,128)(2,1)} %param.4), kind=kLoop, calls=%fused_computation | loop fusion | flops 262144 | bytes 1048577 | tf_op jit(solution)/shard_map/jit(_where)/select_n | solution.py:262
  2.4 0.1 pad_add_fusion.where
  2.5 0.0 copy-done
  2.5 0.0 copy-done.1
  2.5 0.0 collective-permute-done.1.partner_local
  2.5 0.7 %collective-permute-done.partner = bf16[512,512]{1,0:T(8,128)(2,1)S(1)} collective-permute-done((bf16[512,512]{1,0:T(8,128)(2,1)}, bf16[512,512]{1,0:T(8,128)(2,1)S(1)}, u32[]{:S(2)}, u32[]{:S(2)}) %collective-permute-start) | collective-permute-done | bytes 524320 | tf_op jit(solution)/shard_map/ppermute | solution.py:264
  3.3 1.5 %shard_map.50 = (bf16[512,512]{1,0:T(8,128)(2,1)S(1)}, bf16[2,128,512]{2,1,0:T(8,128)(2,1)S(1)}, bf16[128,512]{1,0:T(8,128)(2,1)S(1)}, f32[128,512]{1,0:T(8,128)...) custom-call(s32[3]{0:T(128)S(1)} %pad_add_fusion.where, bf16[512,512]{1,0:T(8,128)(2,1)S(1)} %broadcast_select_fusion.weight, ...), custom_call_target="tpu_custom_call" | custom-call | flops 268435456 | bytes 1048576 | tf_op jit(solution)/shard_map/pallas_call | solution.py:268
  4.7 1.3 %collective-permute-start.2 = (bf16[128,512]{1,0:T(8,128)(2,1)S(1)}, bf16[128,512]{1,0:T(8,128)(2,1)S(1)}, u32[]{:S(2)}, u32[]{:S(2)}) collective-permute-start(bf16[128,512]{1,0:T(8,128)(2,1)S(1)} %get-tuple-element.36.after), channel_id=1, source_target_pairs={{16,0},{17,1},{18,2},{19,3},{20,4},{21,5},{22,6},{23,7},{24,8},{25... | collective-permute-start | bytes 393224 | tf_op jit(solution)/shard_map/ppermute | solution.py:276
  6.0 0.9 %shard_map.52 = (bf16[64,640]{1,0:T(8,128)(2,1)S(1)}, bf16[64,640]{1,0:T(8,128)(2,1)S(1)}, bf16[64,640]{1,0:T(8,128)(2,1)S(1)}, bf16[64,640]{1,0:T(8,128)(2,1)S(1)}) custom-call(s32[3]{0:T(128)S(1)} %pad_add_fusion.where, bf16[2,128,512]{2,1,0:T(8,128)(2,1)S(1)} %get-tuple-element.32.local, bf16[128,512]{1,0:T(8,128)(2,1)S(1)} %get-tuple-element.36.after), custom_call_target="tpu_custom_call" | custom-call | flops 134217728 | bytes 1048576 | tf_op jit(solution)/shard_map/pallas_call | solution.py:284
  6.9 3.9 %collective-permute-start.4 = (bf16[64,640]{1,0:T(8,128)(2,1)S(1)}, bf16[64,640]{1,0:T(8,128)(2,1)S(1)}, u32[]{:S(2)}, u32[]{:S(2)}) collective-permute-start(bf16[64,640]{1,0:T(8,128)(2,1)S(1)} %get-tuple-element.41), channel_id=1, source_target_pairs={{0,3},{1,2},{2,1},{3,0},{4,7},{5,6},{6,5},{7,4},{8,11},{9,10},{10,... | collective-permute-start | bytes 245768 | tf_op jit(solution)/shard_map/ppermute | solution.py:228
  10.9 0.5 collective-permute-start.5
  11.4 0.1 collective-permute-start.6
  11.5 1.2 %collective-permute-done.2.arrived = bf16[128,512]{1,0:T(8,128)(2,1)S(1)} collective-permute-done((bf16[128,512]{1,0:T(8,128)(2,1)S(1)}, bf16[128,512]{1,0:T(8,128)(2,1)S(1)}, u32[]{:S(2)}, u32[]{:S(2)}) %collective-permute-start.2) | collective-permute-done | bytes 131104 | tf_op jit(solution)/shard_map/ppermute | solution.py:276
  12.7 1.1 %shard_map.51 = (bf16[128,512]{1,0:T(8,128)(2,1)S(1)}, bf16[128,512]{1,0:T(8,128)(2,1)S(1)}, bf16[128,512]{1,0:T(8,128)(2,1)S(1)}, bf16[128,512]{1,0:T(8,128)(2,1)S(1)}) custom-call(s32[3]{0:T(128)S(1)} %pad_add_fusion.where, bf16[512,512]{1,0:T(8,128)(2,1)S(1)} %get-tuple-element.33.own, bf16[512,512]{1,0:T(8,128)(2,1)S(1)} %collective-permute-done.partner, ...), custom_call_target="tpu_custom_call" | custom-call | flops 2147483648 | bytes 1048576 | tf_op jit(solution)/shard_map/pallas_call | solution.py:293
  13.8 0.1 collective-permute-start.3
  13.9 0.0 collective-permute-done.4.refs_1_
  13.9 1.5 %collective-permute-done.5.refs_2_ = bf16[64,640]{1,0:T(8,128)(2,1)S(1)} collective-permute-done((bf16[64,640]{1,0:T(8,128)(2,1)S(1)}, bf16[64,640]{1,0:T(8,128)(2,1)S(1)}, u32[]{:S(2)}, u32[]{:S(2)}) %collective-permute-start.5) | collective-permute-done | bytes 81952 | tf_op jit(solution)/shard_map/ppermute | solution.py:228
  15.4 0.5 collective-permute-done.6.refs_3_
  15.9 2.7 %collective-permute-start.10 = (bf16[64,640]{1,0:T(8,128)(2,1)S(1)}, bf16[64,640]{1,0:T(8,128)(2,1)S(1)}, u32[]{:S(2)}, u32[]{:S(2)}) collective-permute-start(bf16[64,640]{1,0:T(8,128)(2,1)S(1)} %shard_map.53.after.left), channel_id=1, source_target_pairs={{0,4},{4,0},{1,5},{5,1},{2,6},{6,2},{3,7},{7,3},{8,12},{12,8},{9,1... | collective-permute-start | bytes 245768 | tf_op jit(solution)/shard_map/ppermute | solution.py:236
  18.6 0.0 collective-permute-done.3.dh_got
  18.6 1.0 %shard_map.54 = (bf16[64,640]{1,0:T(8,128)(2,1)S(1)}, bf16[64,640]{1,0:T(8,128)(2,1)S(1)}, bf16[64,640]{1,0:T(8,128)(2,1)S(1)}, bf16[64,640]{1,0:T(8,128)(2,1)S(...) custom-call(s32[3]{0:T(128)S(1)} %pad_add_fusion.where, ...), custom_call_target="tpu_custom_call" | custom-call | flops 268435456 | bytes 1048576 | tf_op jit(solution)/shard_map/pallas_call | solution.py:302
  19.6 1.5 %collective-permute-start.7 = (bf16[64,640]{1,0:T(8,128)(2,1)S(1)}, bf16[64,640]{1,0:T(8,128)(2,1)S(1)}, u32[]{:S(2)}, u32[]{:S(2)}) collective-permute-start(bf16[64,640]{1,0:T(8,128)(2,1)S(1)} %get-tuple-element.45), channel_id=1, source_target_pairs={{0,3},{1,2},{2,1},{3,0},{4,7},{5,6},{6,5},{7,4},{8,11},{9,10},{10,... | collective-permute-start | bytes 245768 | tf_op jit(solution)/shard_map/ppermute | solution.py:228
  21.1 1.3 %collective-permute-start.8 = (bf16[64,640]{1,0:T(8,128)(2,1)S(1)}, bf16[64,640]{1,0:T(8,128)(2,1)S(1)}, u32[]{:S(2)}, u32[]{:S(2)}) collective-permute-start(bf16[64,640]{1,0:T(8,128)(2,1)S(1)} %get-tuple-element.46), channel_id=1, source_target_pairs={{0,1},{1,0},{2,3},{3,2},{4,5},{5,4},{6,7},{7,6},{8,9},{9,8},{10,11... | collective-permute-start | bytes 245768 | tf_op jit(solution)/shard_map/ppermute | solution.py:228
  22.4 0.7 %collective-permute-start.9 = (bf16[64,640]{1,0:T(8,128)(2,1)S(1)}, bf16[64,640]{1,0:T(8,128)(2,1)S(1)}, u32[]{:S(2)}, u32[]{:S(2)}) collective-permute-start(bf16[64,640]{1,0:T(8,128)(2,1)S(1)} %get-tuple-element.47), channel_id=1, source_target_pairs={{0,2},{1,3},{2,0},{3,1},{4,6},{5,7},{6,4},{7,5},{8,10},{9,11},{10,... | collective-permute-start | bytes 245768 | tf_op jit(solution)/shard_map/ppermute | solution.py:228
  23.2 1.4 %collective-permute-start.19 = (bf16[64,1024]{1,0:T(8,128)(2,1)S(1)}, bf16[64,1024]{1,0:T(8,128)(2,1)S(1)}, u32[]{:S(2)}, u32[]{:S(2)}) collective-permute-start(bf16[64,1024]{1,0:T(8,128)(2,1)S(1)} %get-tuple-element.57), channel_id=1, source_target_pairs={{0,3},{1,2},{2,1},{3,0},{4,7},{5,6},{6,5},{7,4},{8,11},{9,10},{10,... | collective-permute-start | bytes 393224 | tf_op jit(solution)/shard_map/ppermute | solution.py:228
  24.6 0.0 collective-permute-done.10.right
  24.6 1.3 %collective-permute-start.20 = (bf16[64,1024]{1,0:T(8,128)(2,1)S(1)}, bf16[64,1024]{1,0:T(8,128)(2,1)S(1)}, u32[]{:S(2)}, u32[]{:S(2)}) collective-permute-start(bf16[64,1024]{1,0:T(8,128)(2,1)S(1)} %get-tuple-element.58), channel_id=1, source_target_pairs={{0,1},{1,0},{2,3},{3,2},{4,5},{5,4},{6,7},{7,6},{8,9},{9,8},{10,11... | collective-permute-start | bytes 393224 | tf_op jit(solution)/shard_map/ppermute | solution.py:228
  25.9 0.0 collective-permute-done.7.refs_1_
  25.9 1.2 %collective-permute-start.21 = (bf16[64,1024]{1,0:T(8,128)(2,1)S(1)}, bf16[64,1024]{1,0:T(8,128)(2,1)S(1)}, u32[]{:S(2)}, u32[]{:S(2)}) collective-permute-start(bf16[64,1024]{1,0:T(8,128)(2,1)S(1)} %get-tuple-element.59), channel_id=1, source_target_pairs={{0,2},{1,3},{2,0},{3,1},{4,6},{5,7},{6,4},{7,5},{8,10},{9,11},{10,... | collective-permute-start | bytes 393224 | tf_op jit(solution)/shard_map/ppermute | solution.py:228
  27.1 1.2 %collective-permute-done.8.refs_2_ = bf16[64,640]{1,0:T(8,128)(2,1)S(1)} collective-permute-done((bf16[64,640]{1,0:T(8,128)(2,1)S(1)}, bf16[64,640]{1,0:T(8,128)(2,1)S(1)}, u32[]{:S(2)}, u32[]{:S(2)}) %collective-permute-start.8) | collective-permute-done | bytes 81952 | tf_op jit(solution)/shard_map/ppermute | solution.py:228
  28.3 0.0 collective-permute-done.9.refs_3_
  28.4 0.4 collective-permute-start.14
  28.8 1.7 %collective-permute-start.13 = (bf16[64,640]{1,0:T(8,128)(2,1)S(1)}, bf16[64,640]{1,0:T(8,128)(2,1)S(1)}, u32[]{:S(2)}, u32[]{:S(2)}) collective-permute-start(bf16[64,640]{1,0:T(8,128)(2,1)S(1)} %get-tuple-element.48.refs_0_), channel_id=1, source_target_pairs={{0,3},{1,2},{2,1},{3,0},{4,7},{5,6},{6,5},{7,4},{8,11},{9,10},{10,... | collective-permute-start | bytes 245768 | tf_op jit(solution)/shard_map/ppermute | solution.py:228
  30.5 1.1 %collective-permute-done.19.refs_1_ = bf16[64,1024]{1,0:T(8,128)(2,1)S(1)} collective-permute-done((bf16[64,1024]{1,0:T(8,128)(2,1)S(1)}, bf16[64,1024]{1,0:T(8,128)(2,1)S(1)}, u32[]{:S(2)}, u32[]{:S(2)}) %collective-permute-start.19) | collective-permute-done | bytes 131104 | tf_op jit(solution)/shard_map/ppermute | solution.py:228
  31.6 0.7 %collective-permute-start.12 = (bf16[64,640]{1,0:T(8,128)(2,1)S(1)}, bf16[64,640]{1,0:T(8,128)(2,1)S(1)}, u32[]{:S(2)}, u32[]{:S(2)}) collective-permute-start(bf16[64,640]{1,0:T(8,128)(2,1)S(1)} %get-tuple-element.48.refs_0_), channel_id=1, source_target_pairs={{0,2},{1,3},{2,0},{3,1},{4,6},{5,7},{6,4},{7,5},{8,10},{9,11},{10,... | collective-permute-start | bytes 245768 | tf_op jit(solution)/shard_map/ppermute | solution.py:228
  32.3 0.1 collective-permute-done.20.refs_2_
  32.4 2.8 %collective-permute-done.21.refs_3_ = bf16[64,1024]{1,0:T(8,128)(2,1)S(1)} collective-permute-done((bf16[64,1024]{1,0:T(8,128)(2,1)S(1)}, bf16[64,1024]{1,0:T(8,128)(2,1)S(1)}, u32[]{:S(2)}, u32[]{:S(2)}) %collective-permute-start.21) | collective-permute-done | bytes 131104 | tf_op jit(solution)/shard_map/ppermute | solution.py:228
  35.2 0.1 shard_map.60.left
  35.2 0.1 collective-permute-start.22
  35.3 0.7 %collective-permute-start.11 = (bf16[64,640]{1,0:T(8,128)(2,1)S(1)}, bf16[64,640]{1,0:T(8,128)(2,1)S(1)}, u32[]{:S(2)}, u32[]{:S(2)}) collective-permute-start(bf16[64,640]{1,0:T(8,128)(2,1)S(1)} %get-tuple-element.48.refs_0_), channel_id=1, source_target_pairs={{0,1},{1,0},{2,3},{3,2},{4,5},{5,4},{6,7},{7,6},{8,9},{9,8},{10,11... | collective-permute-start | bytes 245768 | tf_op jit(solution)/shard_map/ppermute | solution.py:228
  36.1 0.0 collective-permute-done.14.right
  36.1 3.0 %collective-permute-start.17 = (bf16[64,640]{1,0:T(8,128)(2,1)S(1)}, bf16[64,640]{1,0:T(8,128)(2,1)S(1)}, u32[]{:S(2)}, u32[]{:S(2)}) collective-permute-start(bf16[64,640]{1,0:T(8,128)(2,1)S(1)} %shard_map.58.refs_0_.refs_1_), channel_id=1, source_target_pairs={{0,3},{1,2},{2,1},{3,0},{4,7},{5,6},{6,5},{7,4},{8,11},{9,10},{10,... | collective-permute-start | bytes 245768 | tf_op jit(solution)/shard_map/ppermute | solution.py:228
  39.1 0.0 collective-permute-done.13.refs_3_
  39.1 0.0 collective-permute-start.16
  39.1 1.1 %collective-permute-done.12.refs_2_ = bf16[64,640]{1,0:T(8,128)(2,1)S(1)} collective-permute-done((bf16[64,640]{1,0:T(8,128)(2,1)S(1)}, bf16[64,640]{1,0:T(8,128)(2,1)S(1)}, u32[]{:S(2)}, u32[]{:S(2)}) %collective-permute-start.12) | collective-permute-done | bytes 81952 | tf_op jit(solution)/shard_map/ppermute | solution.py:228
  40.2 0.0 collective-permute-start.15
  40.2 0.3 collective-permute-done.11.refs_1_
  40.5 0.0 collective-permute-start.18
  40.5 2.7 %shard_map.57 = (bf16[512,512]{1,0:T(8,128)(2,1)S(1)}, bf16[512,512]{1,0:T(8,128)(2,1)S(1)}) custom-call(s32[3]{0:T(128)S(1)} %pad_add_fusion.where, bf16[64,640]{1,0:T(8,128)(2,1)S(1)} %get-tuple-element.48.refs_0_, bf16[64,640]{1,0:T(8,128)(2,1)S(1)} %collective-permute-done.11.refs_1_, bf16[64,640]{1,0:T(8,128)(2,1)S(1)} %collective-permute-done.12.refs_2_, ...), custom_call_target="tpu_custom_call" | custom-call | bytes 1048576 | tf_op jit(solution)/shard_map/pallas_call | solution.py:324
  43.2 0.2 collective-permute-done.17.refs_3_.refs_4_
  43.3 0.7 %collective-permute-done.16.refs_2_.refs_3_ = bf16[64,640]{1,0:T(8,128)(2,1)S(1)} collective-permute-done((bf16[64,640]{1,0:T(8,128)(2,1)S(1)}, bf16[64,640]{1,0:T(8,128)(2,1)S(1)}, u32[]{:S(2)}, u32[]{:S(2)}) %collective-permute-start.16) | collective-permute-done | bytes 81952 | tf_op jit(solution)/shard_map/ppermute | solution.py:228
  44.0 0.6 %collective-permute-done.15.refs_1_.refs_2_ = bf16[64,640]{1,0:T(8,128)(2,1)S(1)} collective-permute-done((bf16[64,640]{1,0:T(8,128)(2,1)S(1)}, bf16[64,640]{1,0:T(8,128)(2,1)S(1)}, u32[]{:S(2)}, u32[]{:S(2)}) %collective-permute-start.15) | collective-permute-done | bytes 81952 | tf_op jit(solution)/shard_map/ppermute | solution.py:228
  44.6 0.0 collective-permute-done.22.right
  44.6 1.9 %collective-permute-start.25 = (bf16[64,1024]{1,0:T(8,128)(2,1)S(1)}, bf16[64,1024]{1,0:T(8,128)(2,1)S(1)}, u32[]{:S(2)}, u32[]{:S(2)}) collective-permute-start(bf16[64,1024]{1,0:T(8,128)(2,1)S(1)} %shard_map.61.refs_0_), channel_id=1, source_target_pairs={{0,3},{1,2},{2,1},{3,0},{4,7},{5,6},{6,5},{7,4},{8,11},{9,10},{10,... | collective-permute-start | bytes 393224 | tf_op jit(solution)/shard_map/ppermute | solution.py:228
  46.5 0.2 collective-permute-start.24
  46.7 1.5 %collective-permute-start.23 = (bf16[64,1024]{1,0:T(8,128)(2,1)S(1)}, bf16[64,1024]{1,0:T(8,128)(2,1)S(1)}, u32[]{:S(2)}, u32[]{:S(2)}) collective-permute-start(bf16[64,1024]{1,0:T(8,128)(2,1)S(1)} %shard_map.61.refs_0_), channel_id=1, source_target_pairs={{0,1},{1,0},{2,3},{3,2},{4,5},{5,4},{6,7},{7,6},{8,9},{9,8},{10,11... | collective-permute-start | bytes 393224 | tf_op jit(solution)/shard_map/ppermute | solution.py:228
  48.2 2.7 %shard_map.59 = (bf16[512,512]{1,0:T(8,128)(2,1)S(1)}, bf16[512,512]{1,0:T(8,128)(2,1)S(1)}) custom-call(s32[3]{0:T(128)S(1)} %pad_add_fusion.where, bf16[64,640]{1,0:T(8,128)(2,1)S(1)} %shard_map.58.refs_0_.refs_1_, bf16[64,640]{1,0:T(8,128)(2,1)S(1)} %collective-permute-done.15.refs_1_.refs_2_, ...), custom_call_target="tpu_custom_call" | custom-call | flops 2684354560 | bytes 1048576 | tf_op jit(solution)/shard_map/pallas_call | solution.py:324
  50.9 0.0 collective-permute-done.18.other_cot
  50.9 0.5 collective-permute-done.25.refs_3_
  51.4 1.9 %collective-permute-done.24.refs_2_ = bf16[64,1024]{1,0:T(8,128)(2,1)S(1)} collective-permute-done((bf16[64,1024]{1,0:T(8,128)(2,1)S(1)}, bf16[64,1024]{1,0:T(8,128)(2,1)S(1)}, u32[]{:S(2)}, u32[]{:S(2)}) %collective-permute-start.24) | collective-permute-done | bytes 131104 | tf_op jit(solution)/shard_map/ppermute | solution.py:228
  53.2 0.2 collective-permute-done.23.refs_1_
  53.5 2.7 %shard_map.62 = (f32[512,512]{1,0:T(8,128)}, bf16[2,128,512]{2,1,0:T(8,128)(2,1)}) custom-call(s32[3]{0:T(128)S(1)} %pad_add_fusion.where, bf16[512,512]{1,0:T(8,128)(2,1)S(1)} %get-tuple-element.49.refs_0_.act_high, bf16[512,512]{1,0:T(8,128)(2,1)S(1)} %get-tuple-element.50.act_low, bf16[512,512]{1,0:T(8,128)(2,1)S(1)} %get-tuple-element.52.out_high, ...), custom_call_target="tpu_custom_call" | custom-call | flops 1342177280 | bytes 1048576 | tf_op jit(solution)/shard_map/pallas_call | solution.py:334
  (8 shorter events, 0.2 us)
Async XLA Ops:
  0.6 1.9 %collective-permute-start.1 = (bf16[2,128,512]{2,1,0:T(8,128)(2,1)}, bf16[2,128,512]{2,1,0:T(8,128)(2,1)S(1)}, u32[]{:S(2)}, u32[]{:S(2)}) collective-permute-start(bf16[2,128,512]{2,1,0:T(8,128)(2,1)} %bitcast.10), channel_id=1, source_target_pairs={{0,8},{8,0},{1,9},{9,1},{2,10},{10,2},{3,11},{11,3},{4,12},{12,4},... | collective-permute-start | bytes 786440 | tf_op jit(solution)/shard_map/ppermute | solution.py:265
  1.1 2.1 %collective-permute-start = (bf16[512,512]{1,0:T(8,128)(2,1)}, bf16[512,512]{1,0:T(8,128)(2,1)S(1)}, u32[]{:S(2)}, u32[]{:S(2)}) collective-permute-start(bf16[512,512]{1,0:T(8,128)(2,1)} %bitcast.9), channel_id=1, source_target_pairs={{0,8},{8,0},{1,9},{9,1},{2,10},{10,2},{3,11},{11,3},{4,12},{12,4},... | collective-permute-start | bytes 1572872 | tf_op jit(solution)/shard_map/ppermute | solution.py:264
  1.2 1.2 %copy-start = (bf16[2,128,512]{2,1,0:T(8,128)(2,1)S(1)}, bf16[2,128,512]{2,1,0:T(8,128)(2,1)}, u32[]{:S(2)}) copy-start(bf16[2,128,512]{2,1,0:T(8,128)(2,1)} %param.5) | copy-start | bytes 786436
  1.2 1.2 %copy-start.1 = (bf16[1,2,128,512]{3,2,1,0:T(8,128)(2,1)S(1)}, bf16[1,2,128,512]{3,2,1,0:T(8,128)(2,1)}, u32[]{:S(2)}) copy-start(bf16[1,2,128,512]{3,2,1,0:T(8,128)(2,1)} %param.3) | copy-start | bytes 786436
  4.7 7.9 %collective-permute-start.2 = (bf16[128,512]{1,0:T(8,128)(2,1)S(1)}, bf16[128,512]{1,0:T(8,128)(2,1)S(1)}, u32[]{:S(2)}, u32[]{:S(2)}) collective-permute-start(bf16[128,512]{1,0:T(8,128)(2,1)S(1)} %get-tuple-element.36.after), channel_id=1, source_target_pairs={{16,0},{17,1},{18,2},{19,3},{20,4},{21,5},{22,6},{23,7},{24,8},{25... | collective-permute-start | bytes 393224 | tf_op jit(solution)/shard_map/ppermute | solution.py:276
  6.9 6.9 %collective-permute-start.4 = (bf16[64,640]{1,0:T(8,128)(2,1)S(1)}, bf16[64,640]{1,0:T(8,128)(2,1)S(1)}, u32[]{:S(2)}, u32[]{:S(2)}) collective-permute-start(bf16[64,640]{1,0:T(8,128)(2,1)S(1)} %get-tuple-element.41), channel_id=1, source_target_pairs={{0,3},{1,2},{2,1},{3,0},{4,7},{5,6},{6,5},{7,4},{8,11},{9,10},{10,... | collective-permute-start | bytes 245768 | tf_op jit(solution)/shard_map/ppermute | solution.py:228
  10.9 4.5 %collective-permute-start.5 = (bf16[64,640]{1,0:T(8,128)(2,1)S(1)}, bf16[64,640]{1,0:T(8,128)(2,1)S(1)}, u32[]{:S(2)}, u32[]{:S(2)}) collective-permute-start(bf16[64,640]{1,0:T(8,128)(2,1)S(1)} %get-tuple-element.42), channel_id=1, source_target_pairs={{0,1},{1,0},{2,3},{3,2},{4,5},{5,4},{6,7},{7,6},{8,9},{9,8},{10,11... | collective-permute-start | bytes 245768 | tf_op jit(solution)/shard_map/ppermute | solution.py:228
  11.4 4.4 %collective-permute-start.6 = (bf16[64,640]{1,0:T(8,128)(2,1)S(1)}, bf16[64,640]{1,0:T(8,128)(2,1)S(1)}, u32[]{:S(2)}, u32[]{:S(2)}) collective-permute-start(bf16[64,640]{1,0:T(8,128)(2,1)S(1)} %get-tuple-element.43), channel_id=1, source_target_pairs={{0,2},{1,3},{2,0},{3,1},{4,6},{5,7},{6,4},{7,5},{8,10},{9,11},{10,... | collective-permute-start | bytes 245768 | tf_op jit(solution)/shard_map/ppermute | solution.py:228
  13.8 4.8 %collective-permute-start.3 = (bf16[128,512]{1,0:T(8,128)(2,1)S(1)}, bf16[128,512]{1,0:T(8,128)(2,1)S(1)}, u32[]{:S(2)}, u32[]{:S(2)}) collective-permute-start(bf16[128,512]{1,0:T(8,128)(2,1)S(1)} %get-tuple-element.39), channel_id=1, source_target_pairs={{0,8},{8,0},{1,9},{9,1},{2,10},{10,2},{3,11},{11,3},{4,12},{12,4},... | collective-permute-start | bytes 393224 | tf_op jit(solution)/shard_map/ppermute | solution.py:299
  15.9 8.7 %collective-permute-start.10 = (bf16[64,640]{1,0:T(8,128)(2,1)S(1)}, bf16[64,640]{1,0:T(8,128)(2,1)S(1)}, u32[]{:S(2)}, u32[]{:S(2)}) collective-permute-start(bf16[64,640]{1,0:T(8,128)(2,1)S(1)} %shard_map.53.after.left), channel_id=1, source_target_pairs={{0,4},{4,0},{1,5},{5,1},{2,6},{6,2},{3,7},{7,3},{8,12},{12,8},{9,1... | collective-permute-start | bytes 245768 | tf_op jit(solution)/shard_map/ppermute | solution.py:236
  19.6 6.3 %collective-permute-start.7 = (bf16[64,640]{1,0:T(8,128)(2,1)S(1)}, bf16[64,640]{1,0:T(8,128)(2,1)S(1)}, u32[]{:S(2)}, u32[]{:S(2)}) collective-permute-start(bf16[64,640]{1,0:T(8,128)(2,1)S(1)} %get-tuple-element.45), channel_id=1, source_target_pairs={{0,3},{1,2},{2,1},{3,0},{4,7},{5,6},{6,5},{7,4},{8,11},{9,10},{10,... | collective-permute-start | bytes 245768 | tf_op jit(solution)/shard_map/ppermute | solution.py:228
  21.1 7.3 %collective-permute-start.8 = (bf16[64,640]{1,0:T(8,128)(2,1)S(1)}, bf16[64,640]{1,0:T(8,128)(2,1)S(1)}, u32[]{:S(2)}, u32[]{:S(2)}) collective-permute-start(bf16[64,640]{1,0:T(8,128)(2,1)S(1)} %get-tuple-element.46), channel_id=1, source_target_pairs={{0,1},{1,0},{2,3},{3,2},{4,5},{5,4},{6,7},{7,6},{8,9},{9,8},{10,11... | collective-permute-start | bytes 245768 | tf_op jit(solution)/shard_map/ppermute | solution.py:228
  22.4 5.9 %collective-permute-start.9 = (bf16[64,640]{1,0:T(8,128)(2,1)S(1)}, bf16[64,640]{1,0:T(8,128)(2,1)S(1)}, u32[]{:S(2)}, u32[]{:S(2)}) collective-permute-start(bf16[64,640]{1,0:T(8,128)(2,1)S(1)} %get-tuple-element.47), channel_id=1, source_target_pairs={{0,2},{1,3},{2,0},{3,1},{4,6},{5,7},{6,4},{7,5},{8,10},{9,11},{10,... | collective-permute-start | bytes 245768 | tf_op jit(solution)/shard_map/ppermute | solution.py:228
  23.2 8.4 %collective-permute-start.19 = (bf16[64,1024]{1,0:T(8,128)(2,1)S(1)}, bf16[64,1024]{1,0:T(8,128)(2,1)S(1)}, u32[]{:S(2)}, u32[]{:S(2)}) collective-permute-start(bf16[64,1024]{1,0:T(8,128)(2,1)S(1)} %get-tuple-element.57), channel_id=1, source_target_pairs={{0,3},{1,2},{2,1},{3,0},{4,7},{5,6},{6,5},{7,4},{8,11},{9,10},{10,... | collective-permute-start | bytes 393224 | tf_op jit(solution)/shard_map/ppermute | solution.py:228
  24.6 7.8 %collective-permute-start.20 = (bf16[64,1024]{1,0:T(8,128)(2,1)S(1)}, bf16[64,1024]{1,0:T(8,128)(2,1)S(1)}, u32[]{:S(2)}, u32[]{:S(2)}) collective-permute-start(bf16[64,1024]{1,0:T(8,128)(2,1)S(1)} %get-tuple-element.58), channel_id=1, source_target_pairs={{0,1},{1,0},{2,3},{3,2},{4,5},{5,4},{6,7},{7,6},{8,9},{9,8},{10,11... | collective-permute-start | bytes 393224 | tf_op jit(solution)/shard_map/ppermute | solution.py:228
  25.9 9.3 %collective-permute-start.21 = (bf16[64,1024]{1,0:T(8,128)(2,1)S(1)}, bf16[64,1024]{1,0:T(8,128)(2,1)S(1)}, u32[]{:S(2)}, u32[]{:S(2)}) collective-permute-start(bf16[64,1024]{1,0:T(8,128)(2,1)S(1)} %get-tuple-element.59), channel_id=1, source_target_pairs={{0,2},{1,3},{2,0},{3,1},{4,6},{5,7},{6,4},{7,5},{8,10},{9,11},{10,... | collective-permute-start | bytes 393224 | tf_op jit(solution)/shard_map/ppermute | solution.py:228
  28.4 7.7 %collective-permute-start.14 = (bf16[64,640]{1,0:T(8,128)(2,1)S(1)}, bf16[64,640]{1,0:T(8,128)(2,1)S(1)}, u32[]{:S(2)}, u32[]{:S(2)}) collective-permute-start(bf16[64,640]{1,0:T(8,128)(2,1)S(1)} %get-tuple-element.51.left), channel_id=1, source_target_pairs={{0,4},{4,0},{1,5},{5,1},{2,6},{6,2},{3,7},{7,3},{8,12},{12,8},{9,1... | collective-permute-start | bytes 245768 | tf_op jit(solution)/shard_map/ppermute | solution.py:236
  28.8 10.3 %collective-permute-start.13 = (bf16[64,640]{1,0:T(8,128)(2,1)S(1)}, bf16[64,640]{1,0:T(8,128)(2,1)S(1)}, u32[]{:S(2)}, u32[]{:S(2)}) collective-permute-start(bf16[64,640]{1,0:T(8,128)(2,1)S(1)} %get-tuple-element.48.refs_0_), channel_id=1, source_target_pairs={{0,3},{1,2},{2,1},{3,0},{4,7},{5,6},{6,5},{7,4},{8,11},{9,10},{10,... | collective-permute-start | bytes 245768 | tf_op jit(solution)/shard_map/ppermute | solution.py:228
  31.6 8.6 %collective-permute-start.12 = (bf16[64,640]{1,0:T(8,128)(2,1)S(1)}, bf16[64,640]{1,0:T(8,128)(2,1)S(1)}, u32[]{:S(2)}, u32[]{:S(2)}) collective-permute-start(bf16[64,640]{1,0:T(8,128)(2,1)S(1)} %get-tuple-element.48.refs_0_), channel_id=1, source_target_pairs={{0,2},{1,3},{2,0},{3,1},{4,6},{5,7},{6,4},{7,5},{8,10},{9,11},{10,... | collective-permute-start | bytes 245768 | tf_op jit(solution)/shard_map/ppermute | solution.py:228
  35.2 9.3 %collective-permute-start.22 = (bf16[64,1024]{1,0:T(8,128)(2,1)S(1)}, bf16[64,1024]{1,0:T(8,128)(2,1)S(1)}, u32[]{:S(2)}, u32[]{:S(2)}) collective-permute-start(bf16[64,1024]{1,0:T(8,128)(2,1)S(1)} %shard_map.60.left), channel_id=1, source_target_pairs={{0,4},{4,0},{1,5},{5,1},{2,6},{6,2},{3,7},{7,3},{8,12},{12,8},{9,1... | collective-permute-start | bytes 393224 | tf_op jit(solution)/shard_map/ppermute | solution.py:236
  35.3 5.2 %collective-permute-start.11 = (bf16[64,640]{1,0:T(8,128)(2,1)S(1)}, bf16[64,640]{1,0:T(8,128)(2,1)S(1)}, u32[]{:S(2)}, u32[]{:S(2)}) collective-permute-start(bf16[64,640]{1,0:T(8,128)(2,1)S(1)} %get-tuple-element.48.refs_0_), channel_id=1, source_target_pairs={{0,1},{1,0},{2,3},{3,2},{4,5},{5,4},{6,7},{7,6},{8,9},{9,8},{10,11... | collective-permute-start | bytes 245768 | tf_op jit(solution)/shard_map/ppermute | solution.py:228
  36.1 7.2 %collective-permute-start.17 = (bf16[64,640]{1,0:T(8,128)(2,1)S(1)}, bf16[64,640]{1,0:T(8,128)(2,1)S(1)}, u32[]{:S(2)}, u32[]{:S(2)}) collective-permute-start(bf16[64,640]{1,0:T(8,128)(2,1)S(1)} %shard_map.58.refs_0_.refs_1_), channel_id=1, source_target_pairs={{0,3},{1,2},{2,1},{3,0},{4,7},{5,6},{6,5},{7,4},{8,11},{9,10},{10,... | collective-permute-start | bytes 245768 | tf_op jit(solution)/shard_map/ppermute | solution.py:228
  39.1 4.9 %collective-permute-start.16 = (bf16[64,640]{1,0:T(8,128)(2,1)S(1)}, bf16[64,640]{1,0:T(8,128)(2,1)S(1)}, u32[]{:S(2)}, u32[]{:S(2)}) collective-permute-start(bf16[64,640]{1,0:T(8,128)(2,1)S(1)} %shard_map.58.refs_0_.refs_1_), channel_id=1, source_target_pairs={{0,2},{1,3},{2,0},{3,1},{4,6},{5,7},{6,4},{7,5},{8,10},{9,11},{10,... | collective-permute-start | bytes 245768 | tf_op jit(solution)/shard_map/ppermute | solution.py:228
  40.2 4.4 %collective-permute-start.15 = (bf16[64,640]{1,0:T(8,128)(2,1)S(1)}, bf16[64,640]{1,0:T(8,128)(2,1)S(1)}, u32[]{:S(2)}, u32[]{:S(2)}) collective-permute-start(bf16[64,640]{1,0:T(8,128)(2,1)S(1)} %shard_map.58.refs_0_.refs_1_), channel_id=1, source_target_pairs={{0,1},{1,0},{2,3},{3,2},{4,5},{5,4},{6,7},{7,6},{8,9},{9,8},{10,11... | collective-permute-start | bytes 245768 | tf_op jit(solution)/shard_map/ppermute | solution.py:228
  40.5 10.4 %collective-permute-start.18 = (bf16[128,512]{1,0:T(8,128)(2,1)S(1)}, bf16[128,512]{1,0:T(8,128)(2,1)S(1)}, u32[]{:S(2)}, u32[]{:S(2)}) collective-permute-start(bf16[128,512]{1,0:T(8,128)(2,1)S(1)} %get-tuple-element.55), channel_id=1, source_target_pairs={{0,8},{8,0},{1,9},{9,1},{2,10},{10,2},{3,11},{11,3},{4,12},{12,4},... | collective-permute-start | bytes 393224 | tf_op jit(solution)/shard_map/ppermute | solution.py:300
  44.6 6.7 %collective-permute-start.25 = (bf16[64,1024]{1,0:T(8,128)(2,1)S(1)}, bf16[64,1024]{1,0:T(8,128)(2,1)S(1)}, u32[]{:S(2)}, u32[]{:S(2)}) collective-permute-start(bf16[64,1024]{1,0:T(8,128)(2,1)S(1)} %shard_map.61.refs_0_), channel_id=1, source_target_pairs={{0,3},{1,2},{2,1},{3,0},{4,7},{5,6},{6,5},{7,4},{8,11},{9,10},{10,... | collective-permute-start | bytes 393224 | tf_op jit(solution)/shard_map/ppermute | solution.py:228
  46.5 6.8 %collective-permute-start.24 = (bf16[64,1024]{1,0:T(8,128)(2,1)S(1)}, bf16[64,1024]{1,0:T(8,128)(2,1)S(1)}, u32[]{:S(2)}, u32[]{:S(2)}) collective-permute-start(bf16[64,1024]{1,0:T(8,128)(2,1)S(1)} %shard_map.61.refs_0_), channel_id=1, source_target_pairs={{0,2},{1,3},{2,0},{3,1},{4,6},{5,7},{6,4},{7,5},{8,10},{9,11},{10,... | collective-permute-start | bytes 393224 | tf_op jit(solution)/shard_map/ppermute | solution.py:228
  46.7 6.7 %collective-permute-start.23 = (bf16[64,1024]{1,0:T(8,128)(2,1)S(1)}, bf16[64,1024]{1,0:T(8,128)(2,1)S(1)}, u32[]{:S(2)}, u32[]{:S(2)}) collective-permute-start(bf16[64,1024]{1,0:T(8,128)(2,1)S(1)} %shard_map.61.refs_0_), channel_id=1, source_target_pairs={{0,1},{1,0},{2,3},{3,2},{4,5},{5,4},{6,7},{7,6},{8,9},{9,8},{10,11... | collective-permute-start | bytes 393224 | tf_op jit(solution)/shard_map/ppermute | solution.py:228

commit v13 on v12

--- a/solution.py
+++ b/solution.py
@@ -68,22 +68,19 @@
     )
 
 
-def first_kernel(
-    where, weight, local, cot_last, partner, partner_local,
-    own, kept, last, slope_own, slope_partner, down,
-):
+def near_kernel(where, weight, local, slope):
+    slope[...] = slope_of(local[where[0]], weight[...])
+
+
+def first_kernel(where, own, partner, slope_own, partner_local, cot_last, slope_partner, down):
     core = where[0]
-    last[...] = cot_last[core]
-    slope_own[...] = slope_of(local[core], weight[...])
     slope_partner[...] = slope_of(partner_local[core], partner[...])
 
     def run(odd, even):
-        cot = layer(last[...], odd[1][...], odd[0][...])[1]
+        cot = layer(cot_last[core], odd[1][...], odd[0][...])[1]
         down[...] = layer(cot, even[1][...], even[0][...])[1]
 
-    by_core(core, run, (weight, slope_own), (partner, slope_partner))
-    own[...] = weight[...]
-    kept[...] = local[...]
+    by_core(core, run, (own, slope_own), (partner, slope_partner))
 
 
 def sum_kernel(*refs):
@@ -97,9 +94,9 @@
 
 
 def layers_kernel(
-    where, own, partner, slope_own, slope_partner, arrived, last, own_dh, give_dh, own_cot, give_cot
+    where, own, partner, slope_own, slope_partner, arrived, cot_last, own_dh, give_dh, own_cot, give_cot
 ):
-    upstream = jnp.where(where[2] == 1, last[...], arrived[...])
+    upstream = jnp.where(where[2] == 1, cot_last[where[0]], arrived[...])
 
     def run(odd, even):
         dh, cot = layer(upstream, odd[1][...], odd[0][...])
@@ -265,12 +262,11 @@
     partner_local = lax.ppermute(local, "core", SWAP)
     block = array(rows, width)
     slope = array(rows, width, dtype=F32)
-    own, kept, last, slope_own, slope_partner, down = call(
-        first_kernel,
-        8 * rows * width**2,
-        [array(width, width), array(micro, rows, width), block, slope, slope, block],
-        [SMEM] + [VMEM] * 5,
-    )(where, near_copy(weight), near_copy(local), near_copy(cot_last), partner, partner_local)
+    own, kept, last = near_copy(weight), near_copy(local), near_copy(cot_last)
+    slope_own = call(near_kernel, 2 * rows * width**2, slope, [SMEM] + [VMEM] * 2)(where, own, kept)
+    slope_partner, down = call(first_kernel, 6 * rows * width**2, [slope, block], [SMEM] + [VMEM] * 5)(
+        where, own, partner, slope_own, partner_local, last
+    )
     first = down
     for turn in range(1, pairs):
         upstream = lax.ppermute(down, "row", [(r, r - 1) for r in range(1, pairs)])

time: 56.3 us -> 56.4 us (level)
  waiting for transfers between devices: 14.5 us -> 13.4 us
  Pallas kernels: 12.8 us -> 13.5 us
    ppermute x1, waiting for transfers between devices: 0.75 us -> 0.01 us  [body(): partner = lax.ppermute(weight, 'core', SWAP)]
    pallas_call x1 -> x2, Pallas kernels: 1.46 us -> 2.13 us  [the longest x1 1.33 us: body(): call(first_kernel, 6 * rows * width ** 2, [slope, block], [SMEM] + [VMEM]...]
    ppermute x18, starting transfers between devices: 21.7 us -> 22.4 us  [send(): lax.ppermute(parts[step], ('near', 'side'), [(i, i ^ step) for i in range...]
  transfers between devices with their start and end apart: 26 -> 26, of which waited for: 16 -> 11; matrix products, arithmetic and copies ran while one was open for 2% -> 2% of each run, Pallas kernels for 15% -> 17%
where the time goes in v13:
time: 56.4 us; the launch traced here: 56.3 us
  starting transfers between devices  27.4 us (49%)
  Pallas kernels  13.5 us (24%)
  waiting for transfers between devices  13.4 us (24%)
  other arithmetic  1.26 us (2%)
  between operations  0.8 us (1%)
    ppermute x18, starting transfers between devices, send(): lax.ppermute(parts[step], ('near', 'side'), [(i, i ^ step) for i in range...  22.4 us
    ppermute x18, waiting for transfers between devices, send(): lax.ppermute(parts[step], ('near', 'side'), [(i, i ^ step) for i in range...  12.2 us
    pallas_call x2, Pallas kernels, inverse(): call(functools.partial(inverse_kernel, count), flops, [array(width, width...  5.35 us
    ppermute x3, starting transfers between devices, exchange(): got = lax.ppermute(value, 'far', route)  3.06 us
    pallas_call x1, Pallas kernels, body(): call(update_kernel, 10 * width ** 3, [array(width, width, dtype=F32), arr...  2.71 us
    pallas_call x1, Pallas kernels, body(): call(first_kernel, 6 * rows * width ** 2, [slope, block], [SMEM] + [VMEM]...  1.33 us
    ppermute x1, starting transfers between devices, body(): upstream = lax.ppermute(down, 'row', [(r, r - 1) for r in range(1, pairs)])  1.29 us
    select_n x2, other arithmetic, near_copy(): return jnp.where(core > 1, jnp.zeros_like(value), value)  1.18 us
  transfers between devices with their start and end apart: 26, of which 11 were waited for; matrix products, arithmetic and copies ran while one was open for 2% of the time, Pallas kernels for 17%

profile of v13, /device:TPU:0, one launch (start us, length us, event | category | flops | bytes accessed | tf_op | source)
XLA Modules:
  0.0 56.3 jit_solution(16838233269242946175)
XLA Ops:
  0.6 0.5 collective-permute-start.1
  1.1 0.1 collective-permute-start
  1.2 1.1 %broadcast_select_fusion.weight.own = bf16[512,512]{1,0:T(8,128)(2,1)S(1)} fusion(pred[]{:T(512)S(6)} %gt.2, bf16[1,512,512]{2,1,0:T(8,128)(2,1)} %param.4), kind=kLoop, calls=%fused_computation | loop fusion | flops 262144 | bytes 1048577 | tf_op jit(solution)/shard_map/jit(_where)/select_n | solution.py:259
  2.4 0.1 pad_add_fusion.where
  2.5 0.0 copy-done
  2.5 0.8 %shard_map.50.slope_own = f32[128,512]{1,0:T(8,128)S(1)} custom-call(s32[3]{0:T(128)S(1)} %pad_add_fusion.where, bf16[512,512]{1,0:T(8,128)(2,1)S(1)} %broadcast_select_fusion.weight.own, bf16[2,128,512]{2,1,0:T(8,128)(2,1)S(1)} %get-tuple-element.55.local), custom_call_target="tpu_custom_call" | custom-call | flops 67108864 | bytes 1048576 | tf_op jit(solution)/shard_map/pallas_call | solution.py:266
  3.3 0.0 collective-permute-done.1.partner_local
  3.3 0.0 collective-permute-done.partner
  3.3 1.3 %shard_map.51 = (f32[128,512]{1,0:T(8,128)S(1)}, bf16[128,512]{1,0:T(8,128)(2,1)S(1)}) custom-call(s32[3]{0:T(128)S(1)} %pad_add_fusion.where, bf16[512,512]{1,0:T(8,128)(2,1)S(1)} %broadcast_select_fusion.weight.own, bf16[512,512]{1,0:T(8,128)(2,1)S(1)} %collective-permute-done.partner, f32[128,512]{1,0:T(8,128)S(1)} %shard_map.50.slope_own, ...), custom_call_target="tpu_custom_call" | custom-call | flops 201326592 | bytes 1048576 | tf_op jit(solution)/shard_map/pallas_call | solution.py:267
  4.7 1.3 %collective-permute-start.2 = (bf16[128,512]{1,0:T(8,128)(2,1)S(1)}, bf16[128,512]{1,0:T(8,128)(2,1)S(1)}, u32[]{:S(2)}, u32[]{:S(2)}) collective-permute-start(bf16[128,512]{1,0:T(8,128)(2,1)S(1)} %get-tuple-element.29.after), channel_id=1, source_target_pairs={{16,0},{17,1},{18,2},{19,3},{20,4},{21,5},{22,6},{23,7},{24,8},{25... | collective-permute-start | bytes 393224 | tf_op jit(solution)/shard_map/ppermute | solution.py:272
  6.0 0.9 %shard_map.53 = (bf16[64,640]{1,0:T(8,128)(2,1)S(1)}, bf16[64,640]{1,0:T(8,128)(2,1)S(1)}, bf16[64,640]{1,0:T(8,128)(2,1)S(1)}, bf16[64,640]{1,0:T(8,128)(2,1)S(1)}) custom-call(s32[3]{0:T(128)S(1)} %pad_add_fusion.where, bf16[2,128,512]{2,1,0:T(8,128)(2,1)S(1)} %get-tuple-element.55.local, bf16[128,512]{1,0:T(8,128)(2,1)S(1)} %get-tuple-element.29.after), custom_call_target="tpu_custom_call" | custom-call | flops 134217728 | bytes 1048576 | tf_op jit(solution)/shard_map/pallas_call | solution.py:280
  6.9 4.0 %collective-permute-start.4 = (bf16[64,640]{1,0:T(8,128)(2,1)S(1)}, bf16[64,640]{1,0:T(8,128)(2,1)S(1)}, u32[]{:S(2)}, u32[]{:S(2)}) collective-permute-start(bf16[64,640]{1,0:T(8,128)(2,1)S(1)} %get-tuple-element.33), channel_id=1, source_target_pairs={{0,3},{1,2},{2,1},{3,0},{4,7},{5,6},{6,5},{7,4},{8,11},{9,10},{10,... | collective-permute-start | bytes 245768 | tf_op jit(solution)/shard_map/ppermute | solution.py:225
  10.9 0.5 collective-permute-start.5
  11.4 0.1 collective-permute-start.6
  11.5 1.1 %collective-permute-done.2.arrived = bf16[128,512]{1,0:T(8,128)(2,1)S(1)} collective-permute-done((bf16[128,512]{1,0:T(8,128)(2,1)S(1)}, bf16[128,512]{1,0:T(8,128)(2,1)S(1)}, u32[]{:S(2)}, u32[]{:S(2)}) %collective-permute-start.2) | collective-permute-done | bytes 131104 | tf_op jit(solution)/shard_map/ppermute | solution.py:272
  12.6 1.1 %shard_map.52 = (bf16[128,512]{1,0:T(8,128)(2,1)S(1)}, bf16[128,512]{1,0:T(8,128)(2,1)S(1)}, bf16[128,512]{1,0:T(8,128)(2,1)S(1)}, bf16[128,512]{1,0:T(8,128)(2,1)S(1)}) custom-call(s32[3]{0:T(128)S(1)} %pad_add_fusion.where, bf16[512,512]{1,0:T(8,128)(2,1)S(1)} %broadcast_select_fusion.weight.own, bf16[512,512]{1,0:T(8,128)(2,1)S(1)} %collective-permute-done.partner, ...), custom_call_target="tpu_custom_call" | custom-call | flops 2147483648 | bytes 1048576 | tf_op jit(solution)/shard_map/pallas_call | solution.py:289
  13.7 0.1 collective-permute-start.3
  13.8 0.0 collective-permute-done.4.refs_1_
  13.8 1.5 %collective-permute-done.5.refs_2_ = bf16[64,640]{1,0:T(8,128)(2,1)S(1)} collective-permute-done((bf16[64,640]{1,0:T(8,128)(2,1)S(1)}, bf16[64,640]{1,0:T(8,128)(2,1)S(1)}, u32[]{:S(2)}, u32[]{:S(2)}) %collective-permute-start.5) | collective-permute-done | bytes 81952 | tf_op jit(solution)/shard_map/ppermute | solution.py:225
  15.3 0.5 collective-permute-done.6.refs_3_
  15.9 2.6 %collective-permute-start.10 = (bf16[64,640]{1,0:T(8,128)(2,1)S(1)}, bf16[64,640]{1,0:T(8,128)(2,1)S(1)}, u32[]{:S(2)}, u32[]{:S(2)}) collective-permute-start(bf16[64,640]{1,0:T(8,128)(2,1)S(1)} %shard_map.54.after.left), channel_id=1, source_target_pairs={{0,4},{4,0},{1,5},{5,1},{2,6},{6,2},{3,7},{7,3},{8,12},{12,8},{9,1... | collective-permute-start | bytes 245768 | tf_op jit(solution)/shard_map/ppermute | solution.py:233
  18.5 0.0 collective-permute-done.3.dh_got
  18.5 1.0 %shard_map.55 = (bf16[64,640]{1,0:T(8,128)(2,1)S(1)}, bf16[64,640]{1,0:T(8,128)(2,1)S(1)}, bf16[64,640]{1,0:T(8,128)(2,1)S(1)}, bf16[64,640]{1,0:T(8,128)(2,1)S(...) custom-call(s32[3]{0:T(128)S(1)} %pad_add_fusion.where, ...), custom_call_target="tpu_custom_call" | custom-call | flops 268435456 | bytes 1048576 | tf_op jit(solution)/shard_map/pallas_call | solution.py:298
  19.6 1.4 %collective-permute-start.7 = (bf16[64,640]{1,0:T(8,128)(2,1)S(1)}, bf16[64,640]{1,0:T(8,128)(2,1)S(1)}, u32[]{:S(2)}, u32[]{:S(2)}) collective-permute-start(bf16[64,640]{1,0:T(8,128)(2,1)S(1)} %get-tuple-element.37), channel_id=1, source_target_pairs={{0,3},{1,2},{2,1},{3,0},{4,7},{5,6},{6,5},{7,4},{8,11},{9,10},{10,... | collective-permute-start | bytes 245768 | tf_op jit(solution)/shard_map/ppermute | solution.py:225
  21.1 1.3 %collective-permute-start.8 = (bf16[64,640]{1,0:T(8,128)(2,1)S(1)}, bf16[64,640]{1,0:T(8,128)(2,1)S(1)}, u32[]{:S(2)}, u32[]{:S(2)}) collective-permute-start(bf16[64,640]{1,0:T(8,128)(2,1)S(1)} %get-tuple-element.38), channel_id=1, source_target_pairs={{0,1},{1,0},{2,3},{3,2},{4,5},{5,4},{6,7},{7,6},{8,9},{9,8},{10,11... | collective-permute-start | bytes 245768 | tf_op jit(solution)/shard_map/ppermute | solution.py:225
  22.3 0.8 %collective-permute-start.9 = (bf16[64,640]{1,0:T(8,128)(2,1)S(1)}, bf16[64,640]{1,0:T(8,128)(2,1)S(1)}, u32[]{:S(2)}, u32[]{:S(2)}) collective-permute-start(bf16[64,640]{1,0:T(8,128)(2,1)S(1)} %get-tuple-element.39), channel_id=1, source_target_pairs={{0,2},{1,3},{2,0},{3,1},{4,6},{5,7},{6,4},{7,5},{8,10},{9,11},{10,... | collective-permute-start | bytes 245768 | tf_op jit(solution)/shard_map/ppermute | solution.py:225
  23.2 1.4 %collective-permute-start.19 = (bf16[64,1024]{1,0:T(8,128)(2,1)S(1)}, bf16[64,1024]{1,0:T(8,128)(2,1)S(1)}, u32[]{:S(2)}, u32[]{:S(2)}) collective-permute-start(bf16[64,1024]{1,0:T(8,128)(2,1)S(1)} %get-tuple-element.49), channel_id=1, source_target_pairs={{0,3},{1,2},{2,1},{3,0},{4,7},{5,6},{6,5},{7,4},{8,11},{9,10},{10,... | collective-permute-start | bytes 393224 | tf_op jit(solution)/shard_map/ppermute | solution.py:225
  24.5 0.0 collective-permute-done.10.right
  24.5 1.3 %collective-permute-start.20 = (bf16[64,1024]{1,0:T(8,128)(2,1)S(1)}, bf16[64,1024]{1,0:T(8,128)(2,1)S(1)}, u32[]{:S(2)}, u32[]{:S(2)}) collective-permute-start(bf16[64,1024]{1,0:T(8,128)(2,1)S(1)} %get-tuple-element.50), channel_id=1, source_target_pairs={{0,1},{1,0},{2,3},{3,2},{4,5},{5,4},{6,7},{7,6},{8,9},{9,8},{10,11... | collective-permute-start | bytes 393224 | tf_op jit(solution)/shard_map/ppermute | solution.py:225
  25.8 0.0 collective-permute-done.7.refs_1_
  25.8 1.1 %collective-permute-start.21 = (bf16[64,1024]{1,0:T(8,128)(2,1)S(1)}, bf16[64,1024]{1,0:T(8,128)(2,1)S(1)}, u32[]{:S(2)}, u32[]{:S(2)}) collective-permute-start(bf16[64,1024]{1,0:T(8,128)(2,1)S(1)} %get-tuple-element.51), channel_id=1, source_target_pairs={{0,2},{1,3},{2,0},{3,1},{4,6},{5,7},{6,4},{7,5},{8,10},{9,11},{10,... | collective-permute-start | bytes 393224 | tf_op jit(solution)/shard_map/ppermute | solution.py:225
  27.0 1.3 %collective-permute-done.8.refs_2_ = bf16[64,640]{1,0:T(8,128)(2,1)S(1)} collective-permute-done((bf16[64,640]{1,0:T(8,128)(2,1)S(1)}, bf16[64,640]{1,0:T(8,128)(2,1)S(1)}, u32[]{:S(2)}, u32[]{:S(2)}) %collective-permute-start.8) | collective-permute-done | bytes 81952 | tf_op jit(solution)/shard_map/ppermute | solution.py:225
  28.3 0.0 collective-permute-done.9.refs_3_
  28.4 0.3 collective-permute-start.14
  28.7 1.7 %collective-permute-start.13 = (bf16[64,640]{1,0:T(8,128)(2,1)S(1)}, bf16[64,640]{1,0:T(8,128)(2,1)S(1)}, u32[]{:S(2)}, u32[]{:S(2)}) collective-permute-start(bf16[64,640]{1,0:T(8,128)(2,1)S(1)} %get-tuple-element.40.refs_0_), channel_id=1, source_target_pairs={{0,3},{1,2},{2,1},{3,0},{4,7},{5,6},{6,5},{7,4},{8,11},{9,10},{10,... | collective-permute-start | bytes 245768 | tf_op jit(solution)/shard_map/ppermute | solution.py:225
  30.4 1.1 %collective-permute-done.19.refs_1_ = bf16[64,1024]{1,0:T(8,128)(2,1)S(1)} collective-permute-done((bf16[64,1024]{1,0:T(8,128)(2,1)S(1)}, bf16[64,1024]{1,0:T(8,128)(2,1)S(1)}, u32[]{:S(2)}, u32[]{:S(2)}) %collective-permute-start.19) | collective-permute-done | bytes 131104 | tf_op jit(solution)/shard_map/ppermute | solution.py:225
  31.6 0.7 %collective-permute-start.12 = (bf16[64,640]{1,0:T(8,128)(2,1)S(1)}, bf16[64,640]{1,0:T(8,128)(2,1)S(1)}, u32[]{:S(2)}, u32[]{:S(2)}) collective-permute-start(bf16[64,640]{1,0:T(8,128)(2,1)S(1)} %get-tuple-element.40.refs_0_), channel_id=1, source_target_pairs={{0,2},{1,3},{2,0},{3,1},{4,6},{5,7},{6,4},{7,5},{8,10},{9,11},{10,... | collective-permute-start | bytes 245768 | tf_op jit(solution)/shard_map/ppermute | solution.py:225
  32.3 0.0 collective-permute-done.20.refs_2_
  32.3 2.8 %collective-permute-done.21.refs_3_ = bf16[64,1024]{1,0:T(8,128)(2,1)S(1)} collective-permute-done((bf16[64,1024]{1,0:T(8,128)(2,1)S(1)}, bf16[64,1024]{1,0:T(8,128)(2,1)S(1)}, u32[]{:S(2)}, u32[]{:S(2)}) %collective-permute-start.21) | collective-permute-done | bytes 131104 | tf_op jit(solution)/shard_map/ppermute | solution.py:225
  35.0 0.1 shard_map.61.left
  35.1 0.1 collective-permute-start.22
  35.2 0.8 %collective-permute-start.11 = (bf16[64,640]{1,0:T(8,128)(2,1)S(1)}, bf16[64,640]{1,0:T(8,128)(2,1)S(1)}, u32[]{:S(2)}, u32[]{:S(2)}) collective-permute-start(bf16[64,640]{1,0:T(8,128)(2,1)S(1)} %get-tuple-element.40.refs_0_), channel_id=1, source_target_pairs={{0,1},{1,0},{2,3},{3,2},{4,5},{5,4},{6,7},{7,6},{8,9},{9,8},{10,11... | collective-permute-start | bytes 245768 | tf_op jit(solution)/shard_map/ppermute | solution.py:225
  36.0 0.0 collective-permute-done.14.right
  36.1 3.0 %collective-permute-start.17 = (bf16[64,640]{1,0:T(8,128)(2,1)S(1)}, bf16[64,640]{1,0:T(8,128)(2,1)S(1)}, u32[]{:S(2)}, u32[]{:S(2)}) collective-permute-start(bf16[64,640]{1,0:T(8,128)(2,1)S(1)} %shard_map.59.refs_0_.refs_1_), channel_id=1, source_target_pairs={{0,3},{1,2},{2,1},{3,0},{4,7},{5,6},{6,5},{7,4},{8,11},{9,10},{10,... | collective-permute-start | bytes 245768 | tf_op jit(solution)/shard_map/ppermute | solution.py:225
  39.0 0.0 collective-permute-done.13.refs_3_
  39.0 0.0 collective-permute-start.16
  39.0 0.9 %collective-permute-done.12.refs_2_ = bf16[64,640]{1,0:T(8,128)(2,1)S(1)} collective-permute-done((bf16[64,640]{1,0:T(8,128)(2,1)S(1)}, bf16[64,640]{1,0:T(8,128)(2,1)S(1)}, u32[]{:S(2)}, u32[]{:S(2)}) %collective-permute-start.12) | collective-permute-done | bytes 81952 | tf_op jit(solution)/shard_map/ppermute | solution.py:225
  40.0 0.6 collective-permute-start.15
  40.5 0.0 collective-permute-done.11.refs_1_
  40.5 0.0 collective-permute-start.18
  40.5 2.7 %shard_map.58 = (bf16[512,512]{1,0:T(8,128)(2,1)S(1)}, bf16[512,512]{1,0:T(8,128)(2,1)S(1)}) custom-call(s32[3]{0:T(128)S(1)} %pad_add_fusion.where, bf16[64,640]{1,0:T(8,128)(2,1)S(1)} %get-tuple-element.40.refs_0_, bf16[64,640]{1,0:T(8,128)(2,1)S(1)} %collective-permute-done.11.refs_1_, bf16[64,640]{1,0:T(8,128)(2,1)S(1)} %collective-permute-done.12.refs_2_, ...), custom_call_target="tpu_custom_call" | custom-call | bytes 1048576 | tf_op jit(solution)/shard_map/pallas_call | solution.py:320
  43.2 0.1 collective-permute-done.17.refs_3_.refs_4_
  43.3 0.6 %collective-permute-done.16.refs_2_.refs_3_ = bf16[64,640]{1,0:T(8,128)(2,1)S(1)} collective-permute-done((bf16[64,640]{1,0:T(8,128)(2,1)S(1)}, bf16[64,640]{1,0:T(8,128)(2,1)S(1)}, u32[]{:S(2)}, u32[]{:S(2)}) %collective-permute-start.16) | collective-permute-done | bytes 81952 | tf_op jit(solution)/shard_map/ppermute | solution.py:225
  43.9 0.5 collective-permute-done.15.refs_1_.refs_2_
  44.4 0.0 collective-permute-done.22.right
  44.5 1.7 %collective-permute-start.25 = (bf16[64,1024]{1,0:T(8,128)(2,1)S(1)}, bf16[64,1024]{1,0:T(8,128)(2,1)S(1)}, u32[]{:S(2)}, u32[]{:S(2)}) collective-permute-start(bf16[64,1024]{1,0:T(8,128)(2,1)S(1)} %shard_map.62.refs_0_), channel_id=1, source_target_pairs={{0,3},{1,2},{2,1},{3,0},{4,7},{5,6},{6,5},{7,4},{8,11},{9,10},{10,... | collective-permute-start | bytes 393224 | tf_op jit(solution)/shard_map/ppermute | solution.py:225
  46.2 0.6 %collective-permute-start.24 = (bf16[64,1024]{1,0:T(8,128)(2,1)S(1)}, bf16[64,1024]{1,0:T(8,128)(2,1)S(1)}, u32[]{:S(2)}, u32[]{:S(2)}) collective-permute-start(bf16[64,1024]{1,0:T(8,128)(2,1)S(1)} %shard_map.62.refs_0_), channel_id=1, source_target_pairs={{0,2},{1,3},{2,0},{3,1},{4,6},{5,7},{6,4},{7,5},{8,10},{9,11},{10,... | collective-permute-start | bytes 393224 | tf_op jit(solution)/shard_map/ppermute | solution.py:225
  46.9 1.2 %collective-permute-start.23 = (bf16[64,1024]{1,0:T(8,128)(2,1)S(1)}, bf16[64,1024]{1,0:T(8,128)(2,1)S(1)}, u32[]{:S(2)}, u32[]{:S(2)}) collective-permute-start(bf16[64,1024]{1,0:T(8,128)(2,1)S(1)} %shard_map.62.refs_0_), channel_id=1, source_target_pairs={{0,1},{1,0},{2,3},{3,2},{4,5},{5,4},{6,7},{7,6},{8,9},{9,8},{10,11... | collective-permute-start | bytes 393224 | tf_op jit(solution)/shard_map/ppermute | solution.py:225
  48.0 2.7 %shard_map.60 = (bf16[512,512]{1,0:T(8,128)(2,1)S(1)}, bf16[512,512]{1,0:T(8,128)(2,1)S(1)}) custom-call(s32[3]{0:T(128)S(1)} %pad_add_fusion.where, bf16[64,640]{1,0:T(8,128)(2,1)S(1)} %shard_map.59.refs_0_.refs_1_, bf16[64,640]{1,0:T(8,128)(2,1)S(1)} %collective-permute-done.15.refs_1_.refs_2_, ...), custom_call_target="tpu_custom_call" | custom-call | flops 2684354560 | bytes 1048576 | tf_op jit(solution)/shard_map/pallas_call | solution.py:320
  50.7 0.0 collective-permute-done.18.other_cot
  50.7 0.0 collective-permute-done.25.refs_3_
  50.7 2.8 %collective-permute-done.24.refs_2_ = bf16[64,1024]{1,0:T(8,128)(2,1)S(1)} collective-permute-done((bf16[64,1024]{1,0:T(8,128)(2,1)S(1)}, bf16[64,1024]{1,0:T(8,128)(2,1)S(1)}, u32[]{:S(2)}, u32[]{:S(2)}) %collective-permute-start.24) | collective-permute-done | bytes 131104 | tf_op jit(solution)/shard_map/ppermute | solution.py:225
  53.6 0.0 collective-permute-done.23.refs_1_
  53.6 2.7 %shard_map.63 = (f32[512,512]{1,0:T(8,128)}, bf16[2,128,512]{2,1,0:T(8,128)(2,1)}) custom-call(s32[3]{0:T(128)S(1)} %pad_add_fusion.where, bf16[512,512]{1,0:T(8,128)(2,1)S(1)} %get-tuple-element.41.refs_0_.act_high, bf16[512,512]{1,0:T(8,128)(2,1)S(1)} %get-tuple-element.42.act_low, bf16[512,512]{1,0:T(8,128)(2,1)S(1)} %get-tuple-element.44.out_high, ...), custom_call_target="tpu_custom_call" | custom-call | flops 1342177280 | bytes 1048576 | tf_op jit(solution)/shard_map/pallas_call | solution.py:330
  (9 shorter events, 0.2 us)
Async XLA Ops:
  0.6 2.7 %collective-permute-start.1 = (bf16[2,128,512]{2,1,0:T(8,128)(2,1)}, bf16[2,128,512]{2,1,0:T(8,128)(2,1)S(1)}, u32[]{:S(2)}, u32[]{:S(2)}) collective-permute-start(bf16[2,128,512]{2,1,0:T(8,128)(2,1)} %bitcast.10), channel_id=1, source_target_pairs={{0,8},{8,0},{1,9},{9,1},{2,10},{10,2},{3,11},{11,3},{4,12},{12,4},... | collective-permute-start | bytes 786440 | tf_op jit(solution)/shard_map/ppermute | solution.py:262
  1.1 2.2 %collective-permute-start = (bf16[512,512]{1,0:T(8,128)(2,1)}, bf16[512,512]{1,0:T(8,128)(2,1)S(1)}, u32[]{:S(2)}, u32[]{:S(2)}) collective-permute-start(bf16[512,512]{1,0:T(8,128)(2,1)} %bitcast.9), channel_id=1, source_target_pairs={{0,8},{8,0},{1,9},{9,1},{2,10},{10,2},{3,11},{11,3},{4,12},{12,4},... | collective-permute-start | bytes 1572872 | tf_op jit(solution)/shard_map/ppermute | solution.py:261
  1.2 1.2 %copy-start = (bf16[2,128,512]{2,1,0:T(8,128)(2,1)S(1)}, bf16[2,128,512]{2,1,0:T(8,128)(2,1)}, u32[]{:S(2)}) copy-start(bf16[2,128,512]{2,1,0:T(8,128)(2,1)} %param.5) | copy-start | bytes 786436
  1.2 1.2 %copy-start.1 = (bf16[1,2,128,512]{3,2,1,0:T(8,128)(2,1)S(1)}, bf16[1,2,128,512]{3,2,1,0:T(8,128)(2,1)}, u32[]{:S(2)}) copy-start(bf16[1,2,128,512]{3,2,1,0:T(8,128)(2,1)} %param.3) | copy-start | bytes 786436
  4.7 8.0 %collective-permute-start.2 = (bf16[128,512]{1,0:T(8,128)(2,1)S(1)}, bf16[128,512]{1,0:T(8,128)(2,1)S(1)}, u32[]{:S(2)}, u32[]{:S(2)}) collective-permute-start(bf16[128,512]{1,0:T(8,128)(2,1)S(1)} %get-tuple-element.29.after), channel_id=1, source_target_pairs={{16,0},{17,1},{18,2},{19,3},{20,4},{21,5},{22,6},{23,7},{24,8},{25... | collective-permute-start | bytes 393224 | tf_op jit(solution)/shard_map/ppermute | solution.py:272
  6.9 6.9 %collective-permute-start.4 = (bf16[64,640]{1,0:T(8,128)(2,1)S(1)}, bf16[64,640]{1,0:T(8,128)(2,1)S(1)}, u32[]{:S(2)}, u32[]{:S(2)}) collective-permute-start(bf16[64,640]{1,0:T(8,128)(2,1)S(1)} %get-tuple-element.33), channel_id=1, source_target_pairs={{0,3},{1,2},{2,1},{3,0},{4,7},{5,6},{6,5},{7,4},{8,11},{9,10},{10,... | collective-permute-start | bytes 245768 | tf_op jit(solution)/shard_map/ppermute | solution.py:225
  10.9 4.4 %collective-permute-start.5 = (bf16[64,640]{1,0:T(8,128)(2,1)S(1)}, bf16[64,640]{1,0:T(8,128)(2,1)S(1)}, u32[]{:S(2)}, u32[]{:S(2)}) collective-permute-start(bf16[64,640]{1,0:T(8,128)(2,1)S(1)} %get-tuple-element.34), channel_id=1, source_target_pairs={{0,1},{1,0},{2,3},{3,2},{4,5},{5,4},{6,7},{7,6},{8,9},{9,8},{10,11... | collective-permute-start | bytes 245768 | tf_op jit(solution)/shard_map/ppermute | solution.py:225
  11.4 4.4 %collective-permute-start.6 = (bf16[64,640]{1,0:T(8,128)(2,1)S(1)}, bf16[64,640]{1,0:T(8,128)(2,1)S(1)}, u32[]{:S(2)}, u32[]{:S(2)}) collective-permute-start(bf16[64,640]{1,0:T(8,128)(2,1)S(1)} %get-tuple-element.35), channel_id=1, source_target_pairs={{0,2},{1,3},{2,0},{3,1},{4,6},{5,7},{6,4},{7,5},{8,10},{9,11},{10,... | collective-permute-start | bytes 245768 | tf_op jit(solution)/shard_map/ppermute | solution.py:225
  13.7 4.8 %collective-permute-start.3 = (bf16[128,512]{1,0:T(8,128)(2,1)S(1)}, bf16[128,512]{1,0:T(8,128)(2,1)S(1)}, u32[]{:S(2)}, u32[]{:S(2)}) collective-permute-start(bf16[128,512]{1,0:T(8,128)(2,1)S(1)} %get-tuple-element.31), channel_id=1, source_target_pairs={{0,8},{8,0},{1,9},{9,1},{2,10},{10,2},{3,11},{11,3},{4,12},{12,4},... | collective-permute-start | bytes 393224 | tf_op jit(solution)/shard_map/ppermute | solution.py:295
  15.9 8.6 %collective-permute-start.10 = (bf16[64,640]{1,0:T(8,128)(2,1)S(1)}, bf16[64,640]{1,0:T(8,128)(2,1)S(1)}, u32[]{:S(2)}, u32[]{:S(2)}) collective-permute-start(bf16[64,640]{1,0:T(8,128)(2,1)S(1)} %shard_map.54.after.left), channel_id=1, source_target_pairs={{0,4},{4,0},{1,5},{5,1},{2,6},{6,2},{3,7},{7,3},{8,12},{12,8},{9,1... | collective-permute-start | bytes 245768 | tf_op jit(solution)/shard_map/ppermute | solution.py:233
  19.6 6.2 %collective-permute-start.7 = (bf16[64,640]{1,0:T(8,128)(2,1)S(1)}, bf16[64,640]{1,0:T(8,128)(2,1)S(1)}, u32[]{:S(2)}, u32[]{:S(2)}) collective-permute-start(bf16[64,640]{1,0:T(8,128)(2,1)S(1)} %get-tuple-element.37), channel_id=1, source_target_pairs={{0,3},{1,2},{2,1},{3,0},{4,7},{5,6},{6,5},{7,4},{8,11},{9,10},{10,... | collective-permute-start | bytes 245768 | tf_op jit(solution)/shard_map/ppermute | solution.py:225
  21.1 7.3 %collective-permute-start.8 = (bf16[64,640]{1,0:T(8,128)(2,1)S(1)}, bf16[64,640]{1,0:T(8,128)(2,1)S(1)}, u32[]{:S(2)}, u32[]{:S(2)}) collective-permute-start(bf16[64,640]{1,0:T(8,128)(2,1)S(1)} %get-tuple-element.38), channel_id=1, source_target_pairs={{0,1},{1,0},{2,3},{3,2},{4,5},{5,4},{6,7},{7,6},{8,9},{9,8},{10,11... | collective-permute-start | bytes 245768 | tf_op jit(solution)/shard_map/ppermute | solution.py:225
  22.3 6.0 %collective-permute-start.9 = (bf16[64,640]{1,0:T(8,128)(2,1)S(1)}, bf16[64,640]{1,0:T(8,128)(2,1)S(1)}, u32[]{:S(2)}, u32[]{:S(2)}) collective-permute-start(bf16[64,640]{1,0:T(8,128)(2,1)S(1)} %get-tuple-element.39), channel_id=1, source_target_pairs={{0,2},{1,3},{2,0},{3,1},{4,6},{5,7},{6,4},{7,5},{8,10},{9,11},{10,... | collective-permute-start | bytes 245768 | tf_op jit(solution)/shard_map/ppermute | solution.py:225
  23.2 8.4 %collective-permute-start.19 = (bf16[64,1024]{1,0:T(8,128)(2,1)S(1)}, bf16[64,1024]{1,0:T(8,128)(2,1)S(1)}, u32[]{:S(2)}, u32[]{:S(2)}) collective-permute-start(bf16[64,1024]{1,0:T(8,128)(2,1)S(1)} %get-tuple-element.49), channel_id=1, source_target_pairs={{0,3},{1,2},{2,1},{3,0},{4,7},{5,6},{6,5},{7,4},{8,11},{9,10},{10,... | collective-permute-start | bytes 393224 | tf_op jit(solution)/shard_map/ppermute | solution.py:225
  24.5 7.7 %collective-permute-start.20 = (bf16[64,1024]{1,0:T(8,128)(2,1)S(1)}, bf16[64,1024]{1,0:T(8,128)(2,1)S(1)}, u32[]{:S(2)}, u32[]{:S(2)}) collective-permute-start(bf16[64,1024]{1,0:T(8,128)(2,1)S(1)} %get-tuple-element.50), channel_id=1, source_target_pairs={{0,1},{1,0},{2,3},{3,2},{4,5},{5,4},{6,7},{7,6},{8,9},{9,8},{10,11... | collective-permute-start | bytes 393224 | tf_op jit(solution)/shard_map/ppermute | solution.py:225
  25.8 9.2 %collective-permute-start.21 = (bf16[64,1024]{1,0:T(8,128)(2,1)S(1)}, bf16[64,1024]{1,0:T(8,128)(2,1)S(1)}, u32[]{:S(2)}, u32[]{:S(2)}) collective-permute-start(bf16[64,1024]{1,0:T(8,128)(2,1)S(1)} %get-tuple-element.51), channel_id=1, source_target_pairs={{0,2},{1,3},{2,0},{3,1},{4,6},{5,7},{6,4},{7,5},{8,10},{9,11},{10,... | collective-permute-start | bytes 393224 | tf_op jit(solution)/shard_map/ppermute | solution.py:225
  28.4 7.7 %collective-permute-start.14 = (bf16[64,640]{1,0:T(8,128)(2,1)S(1)}, bf16[64,640]{1,0:T(8,128)(2,1)S(1)}, u32[]{:S(2)}, u32[]{:S(2)}) collective-permute-start(bf16[64,640]{1,0:T(8,128)(2,1)S(1)} %get-tuple-element.43.left), channel_id=1, source_target_pairs={{0,4},{4,0},{1,5},{5,1},{2,6},{6,2},{3,7},{7,3},{8,12},{12,8},{9,1... | collective-permute-start | bytes 245768 | tf_op jit(solution)/shard_map/ppermute | solution.py:233
  28.7 10.3 %collective-permute-start.13 = (bf16[64,640]{1,0:T(8,128)(2,1)S(1)}, bf16[64,640]{1,0:T(8,128)(2,1)S(1)}, u32[]{:S(2)}, u32[]{:S(2)}) collective-permute-start(bf16[64,640]{1,0:T(8,128)(2,1)S(1)} %get-tuple-element.40.refs_0_), channel_id=1, source_target_pairs={{0,3},{1,2},{2,1},{3,0},{4,7},{5,6},{6,5},{7,4},{8,11},{9,10},{10,... | collective-permute-start | bytes 245768 | tf_op jit(solution)/shard_map/ppermute | solution.py:225
  31.6 8.4 %collective-permute-start.12 = (bf16[64,640]{1,0:T(8,128)(2,1)S(1)}, bf16[64,640]{1,0:T(8,128)(2,1)S(1)}, u32[]{:S(2)}, u32[]{:S(2)}) collective-permute-start(bf16[64,640]{1,0:T(8,128)(2,1)S(1)} %get-tuple-element.40.refs_0_), channel_id=1, source_target_pairs={{0,2},{1,3},{2,0},{3,1},{4,6},{5,7},{6,4},{7,5},{8,10},{9,11},{10,... | collective-permute-start | bytes 245768 | tf_op jit(solution)/shard_map/ppermute | solution.py:225
  35.1 9.3 %collective-permute-start.22 = (bf16[64,1024]{1,0:T(8,128)(2,1)S(1)}, bf16[64,1024]{1,0:T(8,128)(2,1)S(1)}, u32[]{:S(2)}, u32[]{:S(2)}) collective-permute-start(bf16[64,1024]{1,0:T(8,128)(2,1)S(1)} %shard_map.61.left), channel_id=1, source_target_pairs={{0,4},{4,0},{1,5},{5,1},{2,6},{6,2},{3,7},{7,3},{8,12},{12,8},{9,1... | collective-permute-start | bytes 393224 | tf_op jit(solution)/shard_map/ppermute | solution.py:233
  35.2 5.3 %collective-permute-start.11 = (bf16[64,640]{1,0:T(8,128)(2,1)S(1)}, bf16[64,640]{1,0:T(8,128)(2,1)S(1)}, u32[]{:S(2)}, u32[]{:S(2)}) collective-permute-start(bf16[64,640]{1,0:T(8,128)(2,1)S(1)} %get-tuple-element.40.refs_0_), channel_id=1, source_target_pairs={{0,1},{1,0},{2,3},{3,2},{4,5},{5,4},{6,7},{7,6},{8,9},{9,8},{10,11... | collective-permute-start | bytes 245768 | tf_op jit(solution)/shard_map/ppermute | solution.py:225
  36.1 7.3 %collective-permute-start.17 = (bf16[64,640]{1,0:T(8,128)(2,1)S(1)}, bf16[64,640]{1,0:T(8,128)(2,1)S(1)}, u32[]{:S(2)}, u32[]{:S(2)}) collective-permute-start(bf16[64,640]{1,0:T(8,128)(2,1)S(1)} %shard_map.59.refs_0_.refs_1_), channel_id=1, source_target_pairs={{0,3},{1,2},{2,1},{3,0},{4,7},{5,6},{6,5},{7,4},{8,11},{9,10},{10,... | collective-permute-start | bytes 245768 | tf_op jit(solution)/shard_map/ppermute | solution.py:225
  39.0 4.9 %collective-permute-start.16 = (bf16[64,640]{1,0:T(8,128)(2,1)S(1)}, bf16[64,640]{1,0:T(8,128)(2,1)S(1)}, u32[]{:S(2)}, u32[]{:S(2)}) collective-permute-start(bf16[64,640]{1,0:T(8,128)(2,1)S(1)} %shard_map.59.refs_0_.refs_1_), channel_id=1, source_target_pairs={{0,2},{1,3},{2,0},{3,1},{4,6},{5,7},{6,4},{7,5},{8,10},{9,11},{10,... | collective-permute-start | bytes 245768 | tf_op jit(solution)/shard_map/ppermute | solution.py:225
  40.0 4.4 %collective-permute-start.15 = (bf16[64,640]{1,0:T(8,128)(2,1)S(1)}, bf16[64,640]{1,0:T(8,128)(2,1)S(1)}, u32[]{:S(2)}, u32[]{:S(2)}) collective-permute-start(bf16[64,640]{1,0:T(8,128)(2,1)S(1)} %shard_map.59.refs_0_.refs_1_), channel_id=1, source_target_pairs={{0,1},{1,0},{2,3},{3,2},{4,5},{5,4},{6,7},{7,6},{8,9},{9,8},{10,11... | collective-permute-start | bytes 245768 | tf_op jit(solution)/shard_map/ppermute | solution.py:225
  40.5 10.2 %collective-permute-start.18 = (bf16[128,512]{1,0:T(8,128)(2,1)S(1)}, bf16[128,512]{1,0:T(8,128)(2,1)S(1)}, u32[]{:S(2)}, u32[]{:S(2)}) collective-permute-start(bf16[128,512]{1,0:T(8,128)(2,1)S(1)} %get-tuple-element.47), channel_id=1, source_target_pairs={{0,8},{8,0},{1,9},{9,1},{2,10},{10,2},{3,11},{11,3},{4,12},{12,4},... | collective-permute-start | bytes 393224 | tf_op jit(solution)/shard_map/ppermute | solution.py:296
  44.5 6.3 %collective-permute-start.25 = (bf16[64,1024]{1,0:T(8,128)(2,1)S(1)}, bf16[64,1024]{1,0:T(8,128)(2,1)S(1)}, u32[]{:S(2)}, u32[]{:S(2)}) collective-permute-start(bf16[64,1024]{1,0:T(8,128)(2,1)S(1)} %shard_map.62.refs_0_), channel_id=1, source_target_pairs={{0,3},{1,2},{2,1},{3,0},{4,7},{5,6},{6,5},{7,4},{8,11},{9,10},{10,... | collective-permute-start | bytes 393224 | tf_op jit(solution)/shard_map/ppermute | solution.py:225
  46.2 7.3 %collective-permute-start.24 = (bf16[64,1024]{1,0:T(8,128)(2,1)S(1)}, bf16[64,1024]{1,0:T(8,128)(2,1)S(1)}, u32[]{:S(2)}, u32[]{:S(2)}) collective-permute-start(bf16[64,1024]{1,0:T(8,128)(2,1)S(1)} %shard_map.62.refs_0_), channel_id=1, source_target_pairs={{0,2},{1,3},{2,0},{3,1},{4,6},{5,7},{6,4},{7,5},{8,10},{9,11},{10,... | collective-permute-start | bytes 393224 | tf_op jit(solution)/shard_map/ppermute | solution.py:225
  46.9 6.7 %collective-permute-start.23 = (bf16[64,1024]{1,0:T(8,128)(2,1)S(1)}, bf16[64,1024]{1,0:T(8,128)(2,1)S(1)}, u32[]{:S(2)}, u32[]{:S(2)}) collective-permute-start(bf16[64,1024]{1,0:T(8,128)(2,1)S(1)} %shard_map.62.refs_0_), channel_id=1, source_target_pairs={{0,1},{1,0},{2,3},{3,2},{4,5},{5,4},{6,7},{7,6},{8,9},{9,8},{10,11... | collective-permute-start | bytes 393224 | tf_op jit(solution)/shard_map/ppermute | solution.py:225

commit v14 on v12

--- a/solution.py
+++ b/solution.py
@@ -11,7 +11,6 @@
 BF16 = jnp.bfloat16
 F32 = jnp.float32
 SWAP = [(0, 1), (1, 0)]
-SMEM = pl.BlockSpec(memory_space=pltpu.SMEM)
 VMEM = pl.BlockSpec(memory_space=pltpu.VMEM)
 ANY = pl.BlockSpec(memory_space=pl.ANY)
 HBM = pl.BlockSpec(memory_space=pltpu.HBM)
@@ -45,6 +44,10 @@
 
 def moment(left, right):
     return lax.dot_general(left, right, (((0,), (0,)), ((), ())), preferred_element_type=F32)
+
+
+def group_place():
+    return 2 * lax.axis_index("near") + lax.axis_index("side")
 
 
 def split(value):
@@ -69,10 +72,10 @@
 
 
 def first_kernel(
-    where, weight, local, cot_last, partner, partner_local,
+    weight, local, cot_last, partner, partner_local,
     own, kept, last, slope_own, slope_partner, down,
 ):
-    core = where[0]
+    core = lax.axis_index("core")
     last[...] = cot_last[core]
     slope_own[...] = slope_of(local[core], weight[...])
     slope_partner[...] = slope_of(partner_local[core], partner[...])
@@ -97,9 +100,9 @@
 
 
 def layers_kernel(
-    where, own, partner, slope_own, slope_partner, arrived, last, own_dh, give_dh, own_cot, give_cot
+    own, partner, slope_own, slope_partner, arrived, last, own_dh, give_dh, own_cot, give_cot
 ):
-    upstream = jnp.where(where[2] == 1, last[...], arrived[...])
+    upstream = jnp.where(lax.axis_index("row") == lax.axis_size("row") - 1, last[...], arrived[...])
 
     def run(odd, even):
         dh, cot = layer(upstream, odd[1][...], odd[0][...])
@@ -107,7 +110,7 @@
         even[2][...], even[3][...] = layer(cot, even[1][...], even[0][...])
 
     by_core(
-        where[0], run, (own, slope_own, own_dh, own_cot), (partner, slope_partner, give_dh, give_cot)
+        lax.axis_index("core"), run, (own, slope_own, own_dh, own_cot), (partner, slope_partner, give_dh, give_cot)
     )
 
 
@@ -127,25 +130,25 @@
         whole[u + 2, :, 4 * size:5 * size] = corner[half:]
 
 
-def act_kernel(where, local, after, *refs):
+def act_kernel(local, after, *refs):
     parts, (tokens, whole) = refs[:GROUP], refs[GROUP:]
     micro, rows = local.shape[:2]
     for m in range(micro):
         tokens[m * rows:(m + 1) * rows] = local[m]
     put_factor(tokens, whole)
     for step, part in enumerate(parts):
-        part[...] = whole[where[1] ^ step]
+        part[...] = whole[group_place() ^ step]
 
 
 def add_kernel(left, right, *refs):
     refs[-1][...] = (left[...].astype(F32) + right[...].astype(F32)).astype(BF16)
 
 
-def grad_kernel(where, local, dh_own, dh_got, after, *refs):
+def grad_kernel(local, dh_own, dh_got, after, *refs):
     factors, grads, (inputs, tokens, whole, rest) = refs[:GROUP], refs[GROUP:2 * GROUP], refs[2 * GROUP:]
     rows, width = local.shape[1:]
-    inputs[:rows] = local[where[0]]
-    inputs[rows:] = local[1 - where[0]]
+    inputs[:rows] = local[lax.axis_index("core")]
+    inputs[rows:] = local[1 - lax.axis_index("core")]
     tokens[:rows] = dh_own[...]
     tokens[rows:] = dh_got[...]
     put_factor(tokens, whole)
@@ -156,8 +159,8 @@
         rest[u, :, :width] = grad[:half]
         rest[u, :, width:] = grad[half:]
     for step in range(GROUP):
-        factors[step][...] = whole[where[1] ^ step]
-        grads[step][...] = rest[where[1] ^ step]
+        factors[step][...] = whole[group_place() ^ step]
+        grads[step][...] = rest[group_place() ^ step]
 
 
 def invert(total, count):
@@ -176,10 +179,10 @@
     return split(((2.0 - ridge * scale) * tail - inner) * scale)
 
 
-def inverse_kernel(count, where, *refs):
+def inverse_kernel(count, *refs):
     pieces, (high, low, blocks, total) = refs[:GROUP], refs[GROUP:]
     for step, piece in enumerate(pieces):
-        blocks[where[1] ^ step] = piece[...]
+        blocks[group_place() ^ step] = piece[...]
     size = total.shape[0] // GROUP
 
     def both(row, column, value):
@@ -198,18 +201,18 @@
         result[...] = term
 
 
-def update_kernel(where, act_high, act_low, out_high, out_low, own_cot, other_cot, *refs):
+def update_kernel(act_high, act_low, out_high, out_low, own_cot, other_cot, *refs):
     pieces, (result, cot, grad, update, done) = refs[:GROUP], refs[GROUP:]
     copies = [
-        pltpu.make_async_copy(own_cot, cot.at[where[0]], done.at[0]),
-        pltpu.make_async_copy(other_cot, cot.at[1 - where[0]], done.at[1]),
+        pltpu.make_async_copy(own_cot, cot.at[lax.axis_index("core")], done.at[0]),
+        pltpu.make_async_copy(other_cot, cot.at[1 - lax.axis_index("core")], done.at[1]),
     ]
     for copy in copies:
         copy.start()
     half, twice = pieces[0].shape
     width = twice // 2
     for step, piece in enumerate(pieces):
-        start = pl.multiple_of((where[1] ^ step) * 2 * half, 2 * half)
+        start = pl.multiple_of((group_place() ^ step) * 2 * half, 2 * half)
         grad[pl.ds(start, half)] = piece[:, :width]
         grad[pl.ds(start + half, half)] = piece[:, width:]
     left = (dot(act_high[...], grad[...]) + dot(act_low[...], grad[...])).astype(BF16)
@@ -249,8 +252,6 @@
     tokens = micro * rows
     count = tokens * GROUP * lax.axis_size("far")
     odd = core == 1
-    top = row == pairs - 1
-    where = jnp.stack([core, lax.axis_index(("near", "side")), top.astype(jnp.int32)]).astype(jnp.int32)
 
     def mine_of(pair):
         return jnp.where(odd, pair[1], pair[0])
@@ -269,8 +270,8 @@
         first_kernel,
         8 * rows * width**2,
         [array(width, width), array(micro, rows, width), block, slope, slope, block],
-        [SMEM] + [VMEM] * 5,
-    )(where, near_copy(weight), near_copy(local), near_copy(cot_last), partner, partner_local)
+        [VMEM] * 5,
+    )(near_copy(weight), near_copy(local), near_copy(cot_last), partner, partner_local)
     first = down
     for turn in range(1, pairs):
         upstream = lax.ppermute(down, "row", [(r, r - 1) for r in range(1, pairs)])
@@ -285,14 +286,14 @@
         act_kernel,
         2 * tokens * width**2,
         [array(size // 2, factor)] * GROUP,
-        [SMEM, VMEM, ANY],
+        [VMEM, ANY],
         [pltpu.VMEM((tokens, width), BF16), pltpu.VMEM((GROUP, size // 2, factor), BF16)],
-    )(where, kept, first)
+    )(kept, first)
     act_pieces = send(act_parts)
 
     own_dh, give_dh, own_cot, give_cot = call(
-        layers_kernel, 64 * rows * width**2, [block] * 4, [SMEM] + [VMEM] * 6
-    )(where, own, partner, slope_own, slope_partner, arrived, last)
+        layers_kernel, 64 * rows * width**2, [block] * 4, [VMEM] * 6
+    )(own, partner, slope_own, slope_partner, arrived, last)
     act_sum = call(sum_kernel, 24 * width**3, array(size // 2, factor), [VMEM] * GROUP + [ANY])(
         *(act_pieces[step] for step in (0, 3, 1, 2)), own_dh
     )
@@ -303,10 +304,10 @@
         grad_kernel,
         4 * tokens * width**2,
         [array(size // 2, factor)] * GROUP + [array(size // 2, 2 * width)] * GROUP,
-        [SMEM] + [VMEM] * 3 + [ANY],
+        [VMEM] * 3 + [ANY],
         [pltpu.VMEM((tokens, width), BF16)] * 2
         + [pltpu.VMEM((GROUP, size // 2, factor), BF16), pltpu.VMEM((GROUP, size // 2, 2 * width), BF16)],
-    )(where, kept, own_dh, got_dh, act_sum)
+    )(kept, own_dh, got_dh, act_sum)
 
     def summed(pieces):
         shape = array(*pieces[0].shape)
@@ -325,9 +326,9 @@
             functools.partial(inverse_kernel, count),
             flops,
             [array(width, width)] * 2,
-            [SMEM] + [VMEM] * GROUP,
+            [VMEM] * GROUP,
             [pltpu.VMEM((GROUP, size // 2, factor), BF16), pltpu.VMEM((width, width), BF16)],
-        )(where, *pieces)
+        )(*pieces)
 
     act_inv = inverse(act, 0)
     grad = send([exchange(total, (act_inv[0], *out))] * GROUP)
@@ -335,14 +336,14 @@
         update_kernel,
         10 * width**3,
         [array(width, width, dtype=F32), array(micro, rows, width)],
-        [SMEM] + [VMEM] * (6 + GROUP),
+        [VMEM] * (6 + GROUP),
         [
             pltpu.VMEM((width, width), BF16),
             pltpu.VMEM((width, width), F32),
             pltpu.SemaphoreType.DMA((4,)),
         ],
         HBM,
-    )(where, *act_inv, *inverse(out, 20 * width**3), own_cot, other_cot, *grad)
+    )(*act_inv, *inverse(out, 20 * width**3), own_cot, other_cot, *grad)
     return (cot[None], update[None])
 
 

time: 56.3 us -> 54.8 us (0.973)
  Pallas kernels: 12.8 us -> 9.02 us
  starting transfers between devices: 26.9 us -> 28.4 us
  waiting for transfers between devices: 14.5 us -> 15.2 us
    pallas_call x2, Pallas kernels: 5.35 us -> 4.27 us  [inverse(): call(functools.partial(inverse_kernel, count), flops, [array(width, width...]
    ppermute x3, starting transfers between devices: 3.16 us -> 4.02 us  [exchange(): got = lax.ppermute(value, 'far', route)]
    ppermute x1, waiting for transfers between devices: 0.02 us -> 0.82 us  [body(): partner_local = lax.ppermute(local, 'core', SWAP)]
    ppermute x1, waiting for transfers between devices: 0.75 us -> 0.01 us  [body(): partner = lax.ppermute(weight, 'core', SWAP)]
    ppermute x18, starting transfers between devices: 21.7 us -> 22.5 us  [send(): lax.ppermute(parts[step], ('near', 'side'), [(i, i ^ step) for i in range...]
  transfers between devices with their start and end apart: 26 -> 26, of which waited for: 16 -> 14; matrix products, arithmetic and copies ran while one was open for 2% -> 2% of each run, Pallas kernels for 15% -> 11%
where the time goes in v14:
time: 54.8 us; the launch traced here: 54.6 us
  starting transfers between devices  28.4 us (52%)
  waiting for transfers between devices  15.2 us (28%)
  Pallas kernels  9.02 us (16%)
  other arithmetic  1.18 us (2%)
  between operations  0.77 us (1%)
    ppermute x18, starting transfers between devices, send(): lax.ppermute(parts[step], ('near', 'side'), [(i, i ^ step) for i in range...  22.5 us
    ppermute x18, waiting for transfers between devices, send(): lax.ppermute(parts[step], ('near', 'side'), [(i, i ^ step) for i in range...  12.7 us
    pallas_call x2, Pallas kernels, inverse(): call(functools.partial(inverse_kernel, count), flops, [array(width, width...  4.27 us
    ppermute x3, starting transfers between devices, exchange(): got = lax.ppermute(value, 'far', route)  4.02 us
    pallas_call x1, Pallas kernels, body(): call(update_kernel, 10 * width ** 3, [array(width, width, dtype=F32), arr...  2.17 us
    ppermute x1, waiting for transfers between devices, body(): upstream = lax.ppermute(down, 'row', [(r, r - 1) for r in range(1, pairs)])  1.69 us
    ppermute x1, starting transfers between devices, body(): upstream = lax.ppermute(down, 'row', [(r, r - 1) for r in range(1, pairs)])  1.29 us
    select_n x2, other arithmetic, near_copy(): return jnp.where(core > 1, jnp.zeros_like(value), value)  1.18 us
  transfers between devices with their start and end apart: 26, of which 14 were waited for; matrix products, arithmetic and copies ran while one was open for 2% of the time, Pallas kernels for 11%

profile of v14, /device:TPU:0, one launch (start us, length us, event | category | flops | bytes accessed | tf_op | source)
XLA Modules:
  0.0 54.6 jit_solution(14144808752404247220)
XLA Ops:
  0.6 0.5 collective-permute-start
  1.1 0.1 collective-permute-start.1
  1.2 0.0 copy-start
  1.2 1.1 %broadcast_select_fusion.weight = bf16[512,512]{1,0:T(8,128)(2,1)S(1)} fusion(pred[]{:T(512)S(6)} %gt.2, bf16[1,512,512]{2,1,0:T(8,128)(2,1)} %param.4), kind=kLoop, calls=%fused_computation | loop fusion | flops 262144 | bytes 1048577 | tf_op jit(solution)/shard_map/jit(_where)/select_n | solution.py:263
  2.4 0.0 copy-done
  2.4 0.0 copy-done.1
  2.5 0.8 %collective-permute-done.1.partner_local = bf16[2,128,512]{2,1,0:T(8,128)(2,1)S(1)} collective-permute-done((bf16[2,128,512]{2,1,0:T(8,128)(2,1)}, bf16[2,128,512]{2,1,0:T(8,128)(2,1)S(1)}, u32[]{:S(2)}, u32[]{:S(2)}) %collective-permute-start.1) | collective-permute-done | bytes 262176 | tf_op jit(solution)/shard_map/ppermute | solution.py:266
  3.3 0.0 collective-permute-done.partner
  3.3 0.9 %shard_map.50 = (bf16[512,512]{1,0:T(8,128)(2,1)S(1)}, bf16[2,128,512]{2,1,0:T(8,128)(2,1)S(1)}, bf16[128,512]{1,0:T(8,128)(2,1)S(1)}, f32[128,512]{1,0:T(8,128)...) custom-call(bf16[512,512]{1,0:T(8,128)(2,1)S(1)} %broadcast_select_fusion.weight, ...), custom_call_target="tpu_custom_call" | custom-call | flops 268435456 | bytes 1048576 | tf_op jit(solution)/shard_map/pallas_call | solution.py:269
  4.2 1.3 %collective-permute-start.2 = (bf16[128,512]{1,0:T(8,128)(2,1)S(1)}, bf16[128,512]{1,0:T(8,128)(2,1)S(1)}, u32[]{:S(2)}, u32[]{:S(2)}) collective-permute-start(bf16[128,512]{1,0:T(8,128)(2,1)S(1)} %get-tuple-element.36.after), channel_id=1, source_target_pairs={{16,0},{17,1},{18,2},{19,3},{20,4},{21,5},{22,6},{23,7},{24,8},{25... | collective-permute-start | bytes 393224 | tf_op jit(solution)/shard_map/ppermute | solution.py:277
  5.5 0.4 shard_map.52
  5.9 4.0 %collective-permute-start.4 = (bf16[64,640]{1,0:T(8,128)(2,1)S(1)}, bf16[64,640]{1,0:T(8,128)(2,1)S(1)}, u32[]{:S(2)}, u32[]{:S(2)}) collective-permute-start(bf16[64,640]{1,0:T(8,128)(2,1)S(1)} %get-tuple-element.41), channel_id=1, source_target_pairs={{0,3},{1,2},{2,1},{3,0},{4,7},{5,6},{6,5},{7,4},{8,11},{9,10},{10,... | collective-permute-start | bytes 245768 | tf_op jit(solution)/shard_map/ppermute | solution.py:231
  9.8 0.5 collective-permute-start.5
  10.4 0.1 collective-permute-start.6
  10.5 1.7 %collective-permute-done.2.arrived = bf16[128,512]{1,0:T(8,128)(2,1)S(1)} collective-permute-done((bf16[128,512]{1,0:T(8,128)(2,1)S(1)}, bf16[128,512]{1,0:T(8,128)(2,1)S(1)}, u32[]{:S(2)}, u32[]{:S(2)}) %collective-permute-start.2) | collective-permute-done | bytes 131104 | tf_op jit(solution)/shard_map/ppermute | solution.py:277
  12.2 0.5 shard_map.51
  12.7 0.1 collective-permute-start.3
  12.8 0.0 collective-permute-done.4.refs_1_
  12.8 1.5 %collective-permute-done.5.refs_2_ = bf16[64,640]{1,0:T(8,128)(2,1)S(1)} collective-permute-done((bf16[64,640]{1,0:T(8,128)(2,1)S(1)}, bf16[64,640]{1,0:T(8,128)(2,1)S(1)}, u32[]{:S(2)}, u32[]{:S(2)}) %collective-permute-start.5) | collective-permute-done | bytes 81952 | tf_op jit(solution)/shard_map/ppermute | solution.py:231
  14.3 0.5 collective-permute-done.6.refs_3_
  14.8 2.7 %collective-permute-start.10 = (bf16[64,640]{1,0:T(8,128)(2,1)S(1)}, bf16[64,640]{1,0:T(8,128)(2,1)S(1)}, u32[]{:S(2)}, u32[]{:S(2)}) collective-permute-start(bf16[64,640]{1,0:T(8,128)(2,1)S(1)} %shard_map.53.after.left), channel_id=1, source_target_pairs={{0,4},{4,0},{1,5},{5,1},{2,6},{6,2},{3,7},{7,3},{8,12},{12,8},{9,1... | collective-permute-start | bytes 245768 | tf_op jit(solution)/shard_map/ppermute | solution.py:239
  17.5 0.0 collective-permute-done.3.dh_got
  17.5 0.5 shard_map.54
  18.0 1.5 %collective-permute-start.7 = (bf16[64,640]{1,0:T(8,128)(2,1)S(1)}, bf16[64,640]{1,0:T(8,128)(2,1)S(1)}, u32[]{:S(2)}, u32[]{:S(2)}) collective-permute-start(bf16[64,640]{1,0:T(8,128)(2,1)S(1)} %get-tuple-element.45), channel_id=1, source_target_pairs={{0,3},{1,2},{2,1},{3,0},{4,7},{5,6},{6,5},{7,4},{8,11},{9,10},{10,... | collective-permute-start | bytes 245768 | tf_op jit(solution)/shard_map/ppermute | solution.py:231
  19.5 1.3 %collective-permute-start.8 = (bf16[64,640]{1,0:T(8,128)(2,1)S(1)}, bf16[64,640]{1,0:T(8,128)(2,1)S(1)}, u32[]{:S(2)}, u32[]{:S(2)}) collective-permute-start(bf16[64,640]{1,0:T(8,128)(2,1)S(1)} %get-tuple-element.46), channel_id=1, source_target_pairs={{0,1},{1,0},{2,3},{3,2},{4,5},{5,4},{6,7},{7,6},{8,9},{9,8},{10,11... | collective-permute-start | bytes 245768 | tf_op jit(solution)/shard_map/ppermute | solution.py:231
  20.8 0.8 %collective-permute-start.9 = (bf16[64,640]{1,0:T(8,128)(2,1)S(1)}, bf16[64,640]{1,0:T(8,128)(2,1)S(1)}, u32[]{:S(2)}, u32[]{:S(2)}) collective-permute-start(bf16[64,640]{1,0:T(8,128)(2,1)S(1)} %get-tuple-element.47), channel_id=1, source_target_pairs={{0,2},{1,3},{2,0},{3,1},{4,6},{5,7},{6,4},{7,5},{8,10},{9,11},{10,... | collective-permute-start | bytes 245768 | tf_op jit(solution)/shard_map/ppermute | solution.py:231
  21.6 1.4 %collective-permute-start.19 = (bf16[64,1024]{1,0:T(8,128)(2,1)S(1)}, bf16[64,1024]{1,0:T(8,128)(2,1)S(1)}, u32[]{:S(2)}, u32[]{:S(2)}) collective-permute-start(bf16[64,1024]{1,0:T(8,128)(2,1)S(1)} %get-tuple-element.57), channel_id=1, source_target_pairs={{0,3},{1,2},{2,1},{3,0},{4,7},{5,6},{6,5},{7,4},{8,11},{9,10},{10,... | collective-permute-start | bytes 393224 | tf_op jit(solution)/shard_map/ppermute | solution.py:231
  23.0 0.0 collective-permute-done.10.right
  23.0 1.3 %collective-permute-start.20 = (bf16[64,1024]{1,0:T(8,128)(2,1)S(1)}, bf16[64,1024]{1,0:T(8,128)(2,1)S(1)}, u32[]{:S(2)}, u32[]{:S(2)}) collective-permute-start(bf16[64,1024]{1,0:T(8,128)(2,1)S(1)} %get-tuple-element.58), channel_id=1, source_target_pairs={{0,1},{1,0},{2,3},{3,2},{4,5},{5,4},{6,7},{7,6},{8,9},{9,8},{10,11... | collective-permute-start | bytes 393224 | tf_op jit(solution)/shard_map/ppermute | solution.py:231
  24.3 0.0 collective-permute-done.7.refs_1_
  24.3 1.2 %collective-permute-start.21 = (bf16[64,1024]{1,0:T(8,128)(2,1)S(1)}, bf16[64,1024]{1,0:T(8,128)(2,1)S(1)}, u32[]{:S(2)}, u32[]{:S(2)}) collective-permute-start(bf16[64,1024]{1,0:T(8,128)(2,1)S(1)} %get-tuple-element.59), channel_id=1, source_target_pairs={{0,2},{1,3},{2,0},{3,1},{4,6},{5,7},{6,4},{7,5},{8,10},{9,11},{10,... | collective-permute-start | bytes 393224 | tf_op jit(solution)/shard_map/ppermute | solution.py:231
  25.5 0.0 collective-permute-done.8.refs_2_
  25.5 0.6 %collective-permute-done.9.refs_3_ = bf16[64,640]{1,0:T(8,128)(2,1)S(1)} collective-permute-done((bf16[64,640]{1,0:T(8,128)(2,1)S(1)}, bf16[64,640]{1,0:T(8,128)(2,1)S(1)}, u32[]{:S(2)}, u32[]{:S(2)}) %collective-permute-start.9) | collective-permute-done | bytes 81952 | tf_op jit(solution)/shard_map/ppermute | solution.py:231
  26.2 1.2 %collective-permute-start.14 = (bf16[64,640]{1,0:T(8,128)(2,1)S(1)}, bf16[64,640]{1,0:T(8,128)(2,1)S(1)}, u32[]{:S(2)}, u32[]{:S(2)}) collective-permute-start(bf16[64,640]{1,0:T(8,128)(2,1)S(1)} %get-tuple-element.51.left), channel_id=1, source_target_pairs={{0,4},{4,0},{1,5},{5,1},{2,6},{6,2},{3,7},{7,3},{8,12},{12,8},{9,1... | collective-permute-start | bytes 245768 | tf_op jit(solution)/shard_map/ppermute | solution.py:239
  27.5 1.7 %collective-permute-start.13 = (bf16[64,640]{1,0:T(8,128)(2,1)S(1)}, bf16[64,640]{1,0:T(8,128)(2,1)S(1)}, u32[]{:S(2)}, u32[]{:S(2)}) collective-permute-start(bf16[64,640]{1,0:T(8,128)(2,1)S(1)} %get-tuple-element.48.refs_0_), channel_id=1, source_target_pairs={{0,3},{1,2},{2,1},{3,0},{4,7},{5,6},{6,5},{7,4},{8,11},{9,10},{10,... | collective-permute-start | bytes 245768 | tf_op jit(solution)/shard_map/ppermute | solution.py:231
  29.2 0.9 %collective-permute-done.19.refs_1_ = bf16[64,1024]{1,0:T(8,128)(2,1)S(1)} collective-permute-done((bf16[64,1024]{1,0:T(8,128)(2,1)S(1)}, bf16[64,1024]{1,0:T(8,128)(2,1)S(1)}, u32[]{:S(2)}, u32[]{:S(2)}) %collective-permute-start.19) | collective-permute-done | bytes 131104 | tf_op jit(solution)/shard_map/ppermute | solution.py:231
  30.0 0.7 %collective-permute-start.12 = (bf16[64,640]{1,0:T(8,128)(2,1)S(1)}, bf16[64,640]{1,0:T(8,128)(2,1)S(1)}, u32[]{:S(2)}, u32[]{:S(2)}) collective-permute-start(bf16[64,640]{1,0:T(8,128)(2,1)S(1)} %get-tuple-element.48.refs_0_), channel_id=1, source_target_pairs={{0,2},{1,3},{2,0},{3,1},{4,6},{5,7},{6,4},{7,5},{8,10},{9,11},{10,... | collective-permute-start | bytes 245768 | tf_op jit(solution)/shard_map/ppermute | solution.py:231
  30.8 0.0 collective-permute-done.20.refs_2_
  30.8 2.8 %collective-permute-done.21.refs_3_ = bf16[64,1024]{1,0:T(8,128)(2,1)S(1)} collective-permute-done((bf16[64,1024]{1,0:T(8,128)(2,1)S(1)}, bf16[64,1024]{1,0:T(8,128)(2,1)S(1)}, u32[]{:S(2)}, u32[]{:S(2)}) %collective-permute-start.21) | collective-permute-done | bytes 131104 | tf_op jit(solution)/shard_map/ppermute | solution.py:231
  33.5 0.1 shard_map.60.left
  33.6 0.1 collective-permute-start.22
  33.7 0.9 %collective-permute-start.11 = (bf16[64,640]{1,0:T(8,128)(2,1)S(1)}, bf16[64,640]{1,0:T(8,128)(2,1)S(1)}, u32[]{:S(2)}, u32[]{:S(2)}) collective-permute-start(bf16[64,640]{1,0:T(8,128)(2,1)S(1)} %get-tuple-element.48.refs_0_), channel_id=1, source_target_pairs={{0,1},{1,0},{2,3},{3,2},{4,5},{5,4},{6,7},{7,6},{8,9},{9,8},{10,11... | collective-permute-start | bytes 245768 | tf_op jit(solution)/shard_map/ppermute | solution.py:231
  34.7 0.0 collective-permute-done.14.right
  34.7 3.0 %collective-permute-start.17 = (bf16[64,640]{1,0:T(8,128)(2,1)S(1)}, bf16[64,640]{1,0:T(8,128)(2,1)S(1)}, u32[]{:S(2)}, u32[]{:S(2)}) collective-permute-start(bf16[64,640]{1,0:T(8,128)(2,1)S(1)} %shard_map.58.refs_0_.refs_1_), channel_id=1, source_target_pairs={{0,3},{1,2},{2,1},{3,0},{4,7},{5,6},{6,5},{7,4},{8,11},{9,10},{10,... | collective-permute-start | bytes 245768 | tf_op jit(solution)/shard_map/ppermute | solution.py:231
  37.7 0.0 collective-permute-done.13.refs_3_
  37.7 0.0 collective-permute-start.16
  37.7 1.0 %collective-permute-done.12.refs_2_ = bf16[64,640]{1,0:T(8,128)(2,1)S(1)} collective-permute-done((bf16[64,640]{1,0:T(8,128)(2,1)S(1)}, bf16[64,640]{1,0:T(8,128)(2,1)S(1)}, u32[]{:S(2)}, u32[]{:S(2)}) %collective-permute-start.12) | collective-permute-done | bytes 81952 | tf_op jit(solution)/shard_map/ppermute | solution.py:231
  38.8 0.5 collective-permute-start.15
  39.3 0.0 collective-permute-done.11.refs_1_
  39.3 0.0 collective-permute-start.18
  39.3 2.1 %shard_map.57 = (bf16[512,512]{1,0:T(8,128)(2,1)S(1)}, bf16[512,512]{1,0:T(8,128)(2,1)S(1)}) custom-call(bf16[64,640]{1,0:T(8,128)(2,1)S(1)} %get-tuple-element.48.refs_0_, bf16[64,640]{1,0:T(8,128)(2,1)S(1)} %collective-permute-done.11.refs_1_, bf16[64,640]{1,0:T(8,128)(2,1)S(1)} %collective-permute-done.12.refs_2_, ...), custom_call_target="tpu_custom_call" | custom-call | bytes 1048576 | tf_op jit(solution)/shard_map/pallas_call | solution.py:325
  41.4 0.1 collective-permute-done.17.refs_3_.refs_4_
  41.5 0.9 %collective-permute-done.16.refs_2_.refs_3_ = bf16[64,640]{1,0:T(8,128)(2,1)S(1)} collective-permute-done((bf16[64,640]{1,0:T(8,128)(2,1)S(1)}, bf16[64,640]{1,0:T(8,128)(2,1)S(1)}, u32[]{:S(2)}, u32[]{:S(2)}) %collective-permute-start.16) | collective-permute-done | bytes 81952 | tf_op jit(solution)/shard_map/ppermute | solution.py:231
  42.4 0.8 %collective-permute-done.15.refs_1_.refs_2_ = bf16[64,640]{1,0:T(8,128)(2,1)S(1)} collective-permute-done((bf16[64,640]{1,0:T(8,128)(2,1)S(1)}, bf16[64,640]{1,0:T(8,128)(2,1)S(1)}, u32[]{:S(2)}, u32[]{:S(2)}) %collective-permute-start.15) | collective-permute-done | bytes 81952 | tf_op jit(solution)/shard_map/ppermute | solution.py:231
  43.2 0.0 collective-permute-done.22.right
  43.3 2.2 %collective-permute-start.25 = (bf16[64,1024]{1,0:T(8,128)(2,1)S(1)}, bf16[64,1024]{1,0:T(8,128)(2,1)S(1)}, u32[]{:S(2)}, u32[]{:S(2)}) collective-permute-start(bf16[64,1024]{1,0:T(8,128)(2,1)S(1)} %shard_map.61.refs_0_), channel_id=1, source_target_pairs={{0,3},{1,2},{2,1},{3,0},{4,7},{5,6},{6,5},{7,4},{8,11},{9,10},{10,... | collective-permute-start | bytes 393224 | tf_op jit(solution)/shard_map/ppermute | solution.py:231
  45.5 0.0 collective-permute-start.24
  45.5 1.3 %collective-permute-start.23 = (bf16[64,1024]{1,0:T(8,128)(2,1)S(1)}, bf16[64,1024]{1,0:T(8,128)(2,1)S(1)}, u32[]{:S(2)}, u32[]{:S(2)}) collective-permute-start(bf16[64,1024]{1,0:T(8,128)(2,1)S(1)} %shard_map.61.refs_0_), channel_id=1, source_target_pairs={{0,1},{1,0},{2,3},{3,2},{4,5},{5,4},{6,7},{7,6},{8,9},{9,8},{10,11... | collective-permute-start | bytes 393224 | tf_op jit(solution)/shard_map/ppermute | solution.py:231
  46.8 2.1 %shard_map.59 = (bf16[512,512]{1,0:T(8,128)(2,1)S(1)}, bf16[512,512]{1,0:T(8,128)(2,1)S(1)}) custom-call(bf16[64,640]{1,0:T(8,128)(2,1)S(1)} %shard_map.58.refs_0_.refs_1_, bf16[64,640]{1,0:T(8,128)(2,1)S(1)} %collective-permute-done.15.refs_1_.refs_2_, bf16[64,640]{1,0:T(8,128)(2,1)S(1)} %collective-permute-done.16.refs_2_.refs_3_, ...), custom_call_target="tpu_custom_call" | custom-call | flops 2684354560 | bytes 1048576 | tf_op jit(solution)/shard_map/pallas_call | solution.py:325
  49.0 0.0 collective-permute-done.18.other_cot
  49.0 1.6 %collective-permute-done.25.refs_3_ = bf16[64,1024]{1,0:T(8,128)(2,1)S(1)} collective-permute-done((bf16[64,1024]{1,0:T(8,128)(2,1)S(1)}, bf16[64,1024]{1,0:T(8,128)(2,1)S(1)}, u32[]{:S(2)}, u32[]{:S(2)}) %collective-permute-start.25) | collective-permute-done | bytes 131104 | tf_op jit(solution)/shard_map/ppermute | solution.py:231
  50.6 1.2 %collective-permute-done.24.refs_2_ = bf16[64,1024]{1,0:T(8,128)(2,1)S(1)} collective-permute-done((bf16[64,1024]{1,0:T(8,128)(2,1)S(1)}, bf16[64,1024]{1,0:T(8,128)(2,1)S(1)}, u32[]{:S(2)}, u32[]{:S(2)}) %collective-permute-start.24) | collective-permute-done | bytes 131104 | tf_op jit(solution)/shard_map/ppermute | solution.py:231
  51.8 0.7 %collective-permute-done.23.refs_1_ = bf16[64,1024]{1,0:T(8,128)(2,1)S(1)} collective-permute-done((bf16[64,1024]{1,0:T(8,128)(2,1)S(1)}, bf16[64,1024]{1,0:T(8,128)(2,1)S(1)}, u32[]{:S(2)}, u32[]{:S(2)}) %collective-permute-start.23) | collective-permute-done | bytes 131104 | tf_op jit(solution)/shard_map/ppermute | solution.py:231
  52.5 2.2 %shard_map.62 = (f32[512,512]{1,0:T(8,128)}, bf16[2,128,512]{2,1,0:T(8,128)(2,1)}) custom-call(bf16[512,512]{1,0:T(8,128)(2,1)S(1)} %get-tuple-element.49.refs_0_.act_high, bf16[512,512]{1,0:T(8,128)(2,1)S(1)} %get-tuple-element.50.act_low, bf16[512,512]{1,0:T(8,128)(2,1)S(1)} %get-tuple-element.52.out_high, bf16[512,512]{1,0:T(8,128)(2,1)S(1)} %get-tuple-element.53.out_low, ...), custom_call_target="tpu_custom_call" | custom-call | flops 1342177280 | bytes 1048576 | tf_op jit(solution)/shard_map/pallas_call | solution.py:335
  (7 shorter events, 0.2 us)
Async XLA Ops:
  0.6 2.6 %collective-permute-start = (bf16[512,512]{1,0:T(8,128)(2,1)}, bf16[512,512]{1,0:T(8,128)(2,1)S(1)}, u32[]{:S(2)}, u32[]{:S(2)}) collective-permute-start(bf16[512,512]{1,0:T(8,128)(2,1)} %bitcast.6), channel_id=1, source_target_pairs={{0,8},{8,0},{1,9},{9,1},{2,10},{10,2},{3,11},{11,3},{4,12},{12,4},... | collective-permute-start | bytes 1572872 | tf_op jit(solution)/shard_map/ppermute | solution.py:265
  1.1 2.1 %collective-permute-start.1 = (bf16[2,128,512]{2,1,0:T(8,128)(2,1)}, bf16[2,128,512]{2,1,0:T(8,128)(2,1)S(1)}, u32[]{:S(2)}, u32[]{:S(2)}) collective-permute-start(bf16[2,128,512]{2,1,0:T(8,128)(2,1)} %bitcast.7), channel_id=1, source_target_pairs={{0,8},{8,0},{1,9},{9,1},{2,10},{10,2},{3,11},{11,3},{4,12},{12,4},... | collective-permute-start | bytes 786440 | tf_op jit(solution)/shard_map/ppermute | solution.py:266
  1.2 1.1 %copy-start = (bf16[2,128,512]{2,1,0:T(8,128)(2,1)S(1)}, bf16[2,128,512]{2,1,0:T(8,128)(2,1)}, u32[]{:S(2)}) copy-start(bf16[2,128,512]{2,1,0:T(8,128)(2,1)} %param.5) | copy-start | bytes 786436
  1.2 1.2 %copy-start.1 = (bf16[1,2,128,512]{3,2,1,0:T(8,128)(2,1)S(1)}, bf16[1,2,128,512]{3,2,1,0:T(8,128)(2,1)}, u32[]{:S(2)}) copy-start(bf16[1,2,128,512]{3,2,1,0:T(8,128)(2,1)} %param.3) | copy-start | bytes 786436
  4.2 8.0 %collective-permute-start.2 = (bf16[128,512]{1,0:T(8,128)(2,1)S(1)}, bf16[128,512]{1,0:T(8,128)(2,1)S(1)}, u32[]{:S(2)}, u32[]{:S(2)}) collective-permute-start(bf16[128,512]{1,0:T(8,128)(2,1)S(1)} %get-tuple-element.36.after), channel_id=1, source_target_pairs={{16,0},{17,1},{18,2},{19,3},{20,4},{21,5},{22,6},{23,7},{24,8},{25... | collective-permute-start | bytes 393224 | tf_op jit(solution)/shard_map/ppermute | solution.py:277
  5.9 6.9 %collective-permute-start.4 = (bf16[64,640]{1,0:T(8,128)(2,1)S(1)}, bf16[64,640]{1,0:T(8,128)(2,1)S(1)}, u32[]{:S(2)}, u32[]{:S(2)}) collective-permute-start(bf16[64,640]{1,0:T(8,128)(2,1)S(1)} %get-tuple-element.41), channel_id=1, source_target_pairs={{0,3},{1,2},{2,1},{3,0},{4,7},{5,6},{6,5},{7,4},{8,11},{9,10},{10,... | collective-permute-start | bytes 245768 | tf_op jit(solution)/shard_map/ppermute | solution.py:231
  9.8 4.5 %collective-permute-start.5 = (bf16[64,640]{1,0:T(8,128)(2,1)S(1)}, bf16[64,640]{1,0:T(8,128)(2,1)S(1)}, u32[]{:S(2)}, u32[]{:S(2)}) collective-permute-start(bf16[64,640]{1,0:T(8,128)(2,1)S(1)} %get-tuple-element.42), channel_id=1, source_target_pairs={{0,1},{1,0},{2,3},{3,2},{4,5},{5,4},{6,7},{7,6},{8,9},{9,8},{10,11... | collective-permute-start | bytes 245768 | tf_op jit(solution)/shard_map/ppermute | solution.py:231
  10.4 4.4 %collective-permute-start.6 = (bf16[64,640]{1,0:T(8,128)(2,1)S(1)}, bf16[64,640]{1,0:T(8,128)(2,1)S(1)}, u32[]{:S(2)}, u32[]{:S(2)}) collective-permute-start(bf16[64,640]{1,0:T(8,128)(2,1)S(1)} %get-tuple-element.43), channel_id=1, source_target_pairs={{0,2},{1,3},{2,0},{3,1},{4,6},{5,7},{6,4},{7,5},{8,10},{9,11},{10,... | collective-permute-start | bytes 245768 | tf_op jit(solution)/shard_map/ppermute | solution.py:231
  12.7 4.8 %collective-permute-start.3 = (bf16[128,512]{1,0:T(8,128)(2,1)S(1)}, bf16[128,512]{1,0:T(8,128)(2,1)S(1)}, u32[]{:S(2)}, u32[]{:S(2)}) collective-permute-start(bf16[128,512]{1,0:T(8,128)(2,1)S(1)} %get-tuple-element.39), channel_id=1, source_target_pairs={{0,8},{8,0},{1,9},{9,1},{2,10},{10,2},{3,11},{11,3},{4,12},{12,4},... | collective-permute-start | bytes 393224 | tf_op jit(solution)/shard_map/ppermute | solution.py:300
  14.8 8.2 %collective-permute-start.10 = (bf16[64,640]{1,0:T(8,128)(2,1)S(1)}, bf16[64,640]{1,0:T(8,128)(2,1)S(1)}, u32[]{:S(2)}, u32[]{:S(2)}) collective-permute-start(bf16[64,640]{1,0:T(8,128)(2,1)S(1)} %shard_map.53.after.left), channel_id=1, source_target_pairs={{0,4},{4,0},{1,5},{5,1},{2,6},{6,2},{3,7},{7,3},{8,12},{12,8},{9,1... | collective-permute-start | bytes 245768 | tf_op jit(solution)/shard_map/ppermute | solution.py:239
  18.0 6.3 %collective-permute-start.7 = (bf16[64,640]{1,0:T(8,128)(2,1)S(1)}, bf16[64,640]{1,0:T(8,128)(2,1)S(1)}, u32[]{:S(2)}, u32[]{:S(2)}) collective-permute-start(bf16[64,640]{1,0:T(8,128)(2,1)S(1)} %get-tuple-element.45), channel_id=1, source_target_pairs={{0,3},{1,2},{2,1},{3,0},{4,7},{5,6},{6,5},{7,4},{8,11},{9,10},{10,... | collective-permute-start | bytes 245768 | tf_op jit(solution)/shard_map/ppermute | solution.py:231
  19.5 6.0 %collective-permute-start.8 = (bf16[64,640]{1,0:T(8,128)(2,1)S(1)}, bf16[64,640]{1,0:T(8,128)(2,1)S(1)}, u32[]{:S(2)}, u32[]{:S(2)}) collective-permute-start(bf16[64,640]{1,0:T(8,128)(2,1)S(1)} %get-tuple-element.46), channel_id=1, source_target_pairs={{0,1},{1,0},{2,3},{3,2},{4,5},{5,4},{6,7},{7,6},{8,9},{9,8},{10,11... | collective-permute-start | bytes 245768 | tf_op jit(solution)/shard_map/ppermute | solution.py:231
  20.8 5.3 %collective-permute-start.9 = (bf16[64,640]{1,0:T(8,128)(2,1)S(1)}, bf16[64,640]{1,0:T(8,128)(2,1)S(1)}, u32[]{:S(2)}, u32[]{:S(2)}) collective-permute-start(bf16[64,640]{1,0:T(8,128)(2,1)S(1)} %get-tuple-element.47), channel_id=1, source_target_pairs={{0,2},{1,3},{2,0},{3,1},{4,6},{5,7},{6,4},{7,5},{8,10},{9,11},{10,... | collective-permute-start | bytes 245768 | tf_op jit(solution)/shard_map/ppermute | solution.py:231
  21.6 8.4 %collective-permute-start.19 = (bf16[64,1024]{1,0:T(8,128)(2,1)S(1)}, bf16[64,1024]{1,0:T(8,128)(2,1)S(1)}, u32[]{:S(2)}, u32[]{:S(2)}) collective-permute-start(bf16[64,1024]{1,0:T(8,128)(2,1)S(1)} %get-tuple-element.57), channel_id=1, source_target_pairs={{0,3},{1,2},{2,1},{3,0},{4,7},{5,6},{6,5},{7,4},{8,11},{9,10},{10,... | collective-permute-start | bytes 393224 | tf_op jit(solution)/shard_map/ppermute | solution.py:231
  23.0 7.7 %collective-permute-start.20 = (bf16[64,1024]{1,0:T(8,128)(2,1)S(1)}, bf16[64,1024]{1,0:T(8,128)(2,1)S(1)}, u32[]{:S(2)}, u32[]{:S(2)}) collective-permute-start(bf16[64,1024]{1,0:T(8,128)(2,1)S(1)} %get-tuple-element.58), channel_id=1, source_target_pairs={{0,1},{1,0},{2,3},{3,2},{4,5},{5,4},{6,7},{7,6},{8,9},{9,8},{10,11... | collective-permute-start | bytes 393224 | tf_op jit(solution)/shard_map/ppermute | solution.py:231
  24.3 9.2 %collective-permute-start.21 = (bf16[64,1024]{1,0:T(8,128)(2,1)S(1)}, bf16[64,1024]{1,0:T(8,128)(2,1)S(1)}, u32[]{:S(2)}, u32[]{:S(2)}) collective-permute-start(bf16[64,1024]{1,0:T(8,128)(2,1)S(1)} %get-tuple-element.59), channel_id=1, source_target_pairs={{0,2},{1,3},{2,0},{3,1},{4,6},{5,7},{6,4},{7,5},{8,10},{9,11},{10,... | collective-permute-start | bytes 393224 | tf_op jit(solution)/shard_map/ppermute | solution.py:231
  26.2 8.5 %collective-permute-start.14 = (bf16[64,640]{1,0:T(8,128)(2,1)S(1)}, bf16[64,640]{1,0:T(8,128)(2,1)S(1)}, u32[]{:S(2)}, u32[]{:S(2)}) collective-permute-start(bf16[64,640]{1,0:T(8,128)(2,1)S(1)} %get-tuple-element.51.left), channel_id=1, source_target_pairs={{0,4},{4,0},{1,5},{5,1},{2,6},{6,2},{3,7},{7,3},{8,12},{12,8},{9,1... | collective-permute-start | bytes 245768 | tf_op jit(solution)/shard_map/ppermute | solution.py:239
  27.5 10.3 %collective-permute-start.13 = (bf16[64,640]{1,0:T(8,128)(2,1)S(1)}, bf16[64,640]{1,0:T(8,128)(2,1)S(1)}, u32[]{:S(2)}, u32[]{:S(2)}) collective-permute-start(bf16[64,640]{1,0:T(8,128)(2,1)S(1)} %get-tuple-element.48.refs_0_), channel_id=1, source_target_pairs={{0,3},{1,2},{2,1},{3,0},{4,7},{5,6},{6,5},{7,4},{8,11},{9,10},{10,... | collective-permute-start | bytes 245768 | tf_op jit(solution)/shard_map/ppermute | solution.py:231
  30.0 8.7 %collective-permute-start.12 = (bf16[64,640]{1,0:T(8,128)(2,1)S(1)}, bf16[64,640]{1,0:T(8,128)(2,1)S(1)}, u32[]{:S(2)}, u32[]{:S(2)}) collective-permute-start(bf16[64,640]{1,0:T(8,128)(2,1)S(1)} %get-tuple-element.48.refs_0_), channel_id=1, source_target_pairs={{0,2},{1,3},{2,0},{3,1},{4,6},{5,7},{6,4},{7,5},{8,10},{9,11},{10,... | collective-permute-start | bytes 245768 | tf_op jit(solution)/shard_map/ppermute | solution.py:231
  33.6 9.6 %collective-permute-start.22 = (bf16[64,1024]{1,0:T(8,128)(2,1)S(1)}, bf16[64,1024]{1,0:T(8,128)(2,1)S(1)}, u32[]{:S(2)}, u32[]{:S(2)}) collective-permute-start(bf16[64,1024]{1,0:T(8,128)(2,1)S(1)} %shard_map.60.left), channel_id=1, source_target_pairs={{0,4},{4,0},{1,5},{5,1},{2,6},{6,2},{3,7},{7,3},{8,12},{12,8},{9,1... | collective-permute-start | bytes 393224 | tf_op jit(solution)/shard_map/ppermute | solution.py:239
  33.7 5.5 %collective-permute-start.11 = (bf16[64,640]{1,0:T(8,128)(2,1)S(1)}, bf16[64,640]{1,0:T(8,128)(2,1)S(1)}, u32[]{:S(2)}, u32[]{:S(2)}) collective-permute-start(bf16[64,640]{1,0:T(8,128)(2,1)S(1)} %get-tuple-element.48.refs_0_), channel_id=1, source_target_pairs={{0,1},{1,0},{2,3},{3,2},{4,5},{5,4},{6,7},{7,6},{8,9},{9,8},{10,11... | collective-permute-start | bytes 245768 | tf_op jit(solution)/shard_map/ppermute | solution.py:231
  34.7 6.8 %collective-permute-start.17 = (bf16[64,640]{1,0:T(8,128)(2,1)S(1)}, bf16[64,640]{1,0:T(8,128)(2,1)S(1)}, u32[]{:S(2)}, u32[]{:S(2)}) collective-permute-start(bf16[64,640]{1,0:T(8,128)(2,1)S(1)} %shard_map.58.refs_0_.refs_1_), channel_id=1, source_target_pairs={{0,3},{1,2},{2,1},{3,0},{4,7},{5,6},{6,5},{7,4},{8,11},{9,10},{10,... | collective-permute-start | bytes 245768 | tf_op jit(solution)/shard_map/ppermute | solution.py:231
  37.7 4.7 %collective-permute-start.16 = (bf16[64,640]{1,0:T(8,128)(2,1)S(1)}, bf16[64,640]{1,0:T(8,128)(2,1)S(1)}, u32[]{:S(2)}, u32[]{:S(2)}) collective-permute-start(bf16[64,640]{1,0:T(8,128)(2,1)S(1)} %shard_map.58.refs_0_.refs_1_), channel_id=1, source_target_pairs={{0,2},{1,3},{2,0},{3,1},{4,6},{5,7},{6,4},{7,5},{8,10},{9,11},{10,... | collective-permute-start | bytes 245768 | tf_op jit(solution)/shard_map/ppermute | solution.py:231
  38.8 4.4 %collective-permute-start.15 = (bf16[64,640]{1,0:T(8,128)(2,1)S(1)}, bf16[64,640]{1,0:T(8,128)(2,1)S(1)}, u32[]{:S(2)}, u32[]{:S(2)}) collective-permute-start(bf16[64,640]{1,0:T(8,128)(2,1)S(1)} %shard_map.58.refs_0_.refs_1_), channel_id=1, source_target_pairs={{0,1},{1,0},{2,3},{3,2},{4,5},{5,4},{6,7},{7,6},{8,9},{9,8},{10,11... | collective-permute-start | bytes 245768 | tf_op jit(solution)/shard_map/ppermute | solution.py:231
  39.3 9.7 %collective-permute-start.18 = (bf16[128,512]{1,0:T(8,128)(2,1)S(1)}, bf16[128,512]{1,0:T(8,128)(2,1)S(1)}, u32[]{:S(2)}, u32[]{:S(2)}) collective-permute-start(bf16[128,512]{1,0:T(8,128)(2,1)S(1)} %get-tuple-element.55), channel_id=1, source_target_pairs={{0,8},{8,0},{1,9},{9,1},{2,10},{10,2},{3,11},{11,3},{4,12},{12,4},... | collective-permute-start | bytes 393224 | tf_op jit(solution)/shard_map/ppermute | solution.py:301
  43.3 7.3 %collective-permute-start.25 = (bf16[64,1024]{1,0:T(8,128)(2,1)S(1)}, bf16[64,1024]{1,0:T(8,128)(2,1)S(1)}, u32[]{:S(2)}, u32[]{:S(2)}) collective-permute-start(bf16[64,1024]{1,0:T(8,128)(2,1)S(1)} %shard_map.61.refs_0_), channel_id=1, source_target_pairs={{0,3},{1,2},{2,1},{3,0},{4,7},{5,6},{6,5},{7,4},{8,11},{9,10},{10,... | collective-permute-start | bytes 393224 | tf_op jit(solution)/shard_map/ppermute | solution.py:231
  45.5 6.3 %collective-permute-start.24 = (bf16[64,1024]{1,0:T(8,128)(2,1)S(1)}, bf16[64,1024]{1,0:T(8,128)(2,1)S(1)}, u32[]{:S(2)}, u32[]{:S(2)}) collective-permute-start(bf16[64,1024]{1,0:T(8,128)(2,1)S(1)} %shard_map.61.refs_0_), channel_id=1, source_target_pairs={{0,2},{1,3},{2,0},{3,1},{4,6},{5,7},{6,4},{7,5},{8,10},{9,11},{10,... | collective-permute-start | bytes 393224 | tf_op jit(solution)/shard_map/ppermute | solution.py:231
  45.5 7.0 %collective-permute-start.23 = (bf16[64,1024]{1,0:T(8,128)(2,1)S(1)}, bf16[64,1024]{1,0:T(8,128)(2,1)S(1)}, u32[]{:S(2)}, u32[]{:S(2)}) collective-permute-start(bf16[64,1024]{1,0:T(8,128)(2,1)S(1)} %shard_map.61.refs_0_), channel_id=1, source_target_pairs={{0,1},{1,0},{2,3},{3,2},{4,5},{5,4},{6,7},{7,6},{8,9},{9,8},{10,11... | collective-permute-start | bytes 393224 | tf_op jit(solution)/shard_map/ppermute | solution.py:231

commit v15 on v14

--- a/solution.py
+++ b/solution.py
@@ -179,8 +179,9 @@
     return split(((2.0 - ridge * scale) * tail - inner) * scale)
 
 
-def inverse_kernel(count, *refs):
-    pieces, (high, low, blocks, total) = refs[:GROUP], refs[GROUP:]
+def inverse_kernel(count, through, after, *refs):
+    pieces, (high, low, through_copy, blocks, total) = refs[:GROUP], refs[GROUP:]
+    through_copy[...] = through[...]
     for step, piece in enumerate(pieces):
         blocks[group_place() ^ step] = piece[...]
     size = total.shape[0] // GROUP
@@ -298,7 +299,6 @@
         *(act_pieces[step] for step in (0, 3, 1, 2)), own_dh
     )
     got_dh = lax.ppermute(give_dh, "core", SWAP)
-    other_cot = lax.ppermute(give_cot, "core", SWAP)
 
     parts = call(
         grad_kernel,
@@ -309,29 +309,31 @@
         + [pltpu.VMEM((GROUP, size // 2, factor), BF16), pltpu.VMEM((GROUP, size // 2, 2 * width), BF16)],
     )(kept, own_dh, got_dh, act_sum)
 
-    def summed(pieces):
-        shape = array(*pieces[0].shape)
-        return call(sum_kernel, 0, shape, [VMEM] * GROUP)(*(pieces[step] for step in (0, 3, 1, 2)))
-
     pieces = send(parts[:GROUP])
     factors, act_part = call(
         pass_kernel, 0, [array(size // 2, factor)] * 2, [VMEM] * (GROUP + 1)
     )(*(pieces[step] for step in (0, 3, 1, 2)), exchange(act_sum, flops=16 * width**3))
     out = send([exchange(factors)] * GROUP)
+    pieces = send(parts[GROUP:])
+    total, act_part = call(
+        pass_kernel, 0, [array(size // 2, 2 * width), array(size // 2, factor)], [VMEM] * (GROUP + 1)
+    )(*(pieces[step] for step in (0, 3, 1, 2)), act_part)
     act = send([act_part] * GROUP)
-    total = summed(send(parts[GROUP:]))
-
-    def inverse(pieces, flops):
+
+    def inverse(pieces, through, after):
         return call(
             functools.partial(inverse_kernel, count),
-            flops,
-            [array(width, width)] * 2,
-            [VMEM] * GROUP,
+            20 * width**3,
+            [array(width, width)] * 2 + [array(*through.shape)],
+            [VMEM, ANY] + [VMEM] * GROUP,
             [pltpu.VMEM((GROUP, size // 2, factor), BF16), pltpu.VMEM((width, width), BF16)],
-        )(*pieces)
-
-    act_inv = inverse(act, 0)
-    grad = send([exchange(total, (act_inv[0], *out))] * GROUP)
+        )(through, after, *pieces)
+
+    total = exchange(total, (*out, act[1]))
+    grad = send([total] * GROUP)
+    *out_inv, give_cot = inverse(out, give_cot, total)
+    *act_inv, _ = inverse(act, act_part, total)
+    other_cot = lax.ppermute(give_cot, "core", SWAP)
     update, cot = call(
         update_kernel,
         10 * width**3,
@@ -343,7 +345,7 @@
             pltpu.SemaphoreType.DMA((4,)),
         ],
         HBM,
-    )(*act_inv, *inverse(out, 20 * width**3), own_cot, other_cot, *grad)
+    )(*act_inv, *out_inv, own_cot, other_cot, *grad)
     return (cot[None], update[None])
 
 

time: 54.8 us -> 54.3 us (level)
  waiting for transfers between devices: 15.2 us -> 10.7 us
  starting transfers between devices: 28.4 us -> 31.7 us
  Pallas kernels: 9.02 us -> 9.6 us
    ppermute x18, waiting for transfers between devices: 12.7 us -> 8.17 us  [send(): lax.ppermute(parts[step], ('near', 'side'), [(i, i ^ step) for i in range...]
    ppermute x18, starting transfers between devices: 22.5 us -> 25.4 us  [send(): lax.ppermute(parts[step], ('near', 'side'), [(i, i ^ step) for i in range...]
    pallas_call x3, Pallas kernels: 4.34 us -> 4.92 us  [the longest x2 4.85 us: inverse(): call(functools.partial(inverse_kernel, count), 20 * width ** 3, [array(wi...]
  transfers between devices with their start and end apart: 26 -> 26, of which waited for: 14 -> 9; matrix products, arithmetic and copies ran while one was open for 2% -> 2% of each run, Pallas kernels for 11% -> 12%
where the time goes in v15:
time: 54.3 us; the launch traced here: 54.1 us
  starting transfers between devices  31.7 us (58%)
  waiting for transfers between devices  10.7 us (20%)
  Pallas kernels  9.6 us (18%)
  other arithmetic  1.18 us (2%)
  between operations  0.8 us (1%)
    ppermute x18, starting transfers between devices, send(): lax.ppermute(parts[step], ('near', 'side'), [(i, i ^ step) for i in range...  25.4 us
    ppermute x18, waiting for transfers between devices, send(): lax.ppermute(parts[step], ('near', 'side'), [(i, i ^ step) for i in range...  8.17 us
    pallas_call x2, Pallas kernels, inverse(): call(functools.partial(inverse_kernel, count), 20 * width ** 3, [array(wi...  4.85 us
    ppermute x3, starting transfers between devices, exchange(): got = lax.ppermute(value, 'far', route)  4.27 us
    pallas_call x1, Pallas kernels, body(): call(update_kernel, 10 * width ** 3, [array(width, width, dtype=F32), arr...  2.17 us
    ppermute x1, waiting for transfers between devices, body(): upstream = lax.ppermute(down, 'row', [(r, r - 1) for r in range(1, pairs)])  1.69 us
    ppermute x1, starting transfers between devices, body(): upstream = lax.ppermute(down, 'row', [(r, r - 1) for r in range(1, pairs)])  1.29 us
    select_n x2, other arithmetic, near_copy(): return jnp.where(core > 1, jnp.zeros_like(value), value)  1.18 us
  transfers between devices with their start and end apart: 26, of which 9 were waited for; matrix products, arithmetic and copies ran while one was open for 2% of the time, Pallas kernels for 12%

profile of v15, /device:TPU:0, one launch (start us, length us, event | category | flops | bytes accessed | tf_op | source)
XLA Modules:
  0.0 54.1 jit_solution(7982614061179995430)
XLA Ops:
  0.6 0.5 collective-permute-start
  1.1 0.1 collective-permute-start.1
  1.2 0.0 copy-start.1
  1.2 1.1 %broadcast_select_fusion.weight = bf16[512,512]{1,0:T(8,128)(2,1)S(1)} fusion(pred[]{:T(512)S(6)} %gt.2, bf16[1,512,512]{2,1,0:T(8,128)(2,1)} %param.4), kind=kLoop, calls=%fused_computation | loop fusion | flops 262144 | bytes 1048577 | tf_op jit(solution)/shard_map/jit(_where)/select_n | solution.py:264
  2.4 0.0 copy-done
  2.4 0.0 copy-done.1
  2.5 0.8 %collective-permute-done.1.partner_local = bf16[2,128,512]{2,1,0:T(8,128)(2,1)S(1)} collective-permute-done((bf16[2,128,512]{2,1,0:T(8,128)(2,1)}, bf16[2,128,512]{2,1,0:T(8,128)(2,1)S(1)}, u32[]{:S(2)}, u32[]{:S(2)}) %collective-permute-start.1) | collective-permute-done | bytes 262176 | tf_op jit(solution)/shard_map/ppermute | solution.py:267
  3.3 0.0 collective-permute-done.partner
  3.3 0.9 %shard_map.50 = (bf16[512,512]{1,0:T(8,128)(2,1)S(1)}, bf16[2,128,512]{2,1,0:T(8,128)(2,1)S(1)}, bf16[128,512]{1,0:T(8,128)(2,1)S(1)}, f32[128,512]{1,0:T(8,128)...) custom-call(bf16[512,512]{1,0:T(8,128)(2,1)S(1)} %broadcast_select_fusion.weight, ...), custom_call_target="tpu_custom_call" | custom-call | flops 268435456 | bytes 1048576 | tf_op jit(solution)/shard_map/pallas_call | solution.py:270
  4.2 1.3 %collective-permute-start.2 = (bf16[128,512]{1,0:T(8,128)(2,1)S(1)}, bf16[128,512]{1,0:T(8,128)(2,1)S(1)}, u32[]{:S(2)}, u32[]{:S(2)}) collective-permute-start(bf16[128,512]{1,0:T(8,128)(2,1)S(1)} %get-tuple-element.39.after), channel_id=1, source_target_pairs={{16,0},{17,1},{18,2},{19,3},{20,4},{21,5},{22,6},{23,7},{24,8},{25... | collective-permute-start | bytes 393224 | tf_op jit(solution)/shard_map/ppermute | solution.py:278
  5.5 0.4 shard_map.52
  5.9 4.0 %collective-permute-start.4 = (bf16[64,640]{1,0:T(8,128)(2,1)S(1)}, bf16[64,640]{1,0:T(8,128)(2,1)S(1)}, u32[]{:S(2)}, u32[]{:S(2)}) collective-permute-start(bf16[64,640]{1,0:T(8,128)(2,1)S(1)} %get-tuple-element.44), channel_id=1, source_target_pairs={{0,3},{1,2},{2,1},{3,0},{4,7},{5,6},{6,5},{7,4},{8,11},{9,10},{10,... | collective-permute-start | bytes 245768 | tf_op jit(solution)/shard_map/ppermute | solution.py:232
  9.8 0.5 collective-permute-start.5
  10.4 0.1 collective-permute-start.6
  10.5 1.7 %collective-permute-done.2.arrived = bf16[128,512]{1,0:T(8,128)(2,1)S(1)} collective-permute-done((bf16[128,512]{1,0:T(8,128)(2,1)S(1)}, bf16[128,512]{1,0:T(8,128)(2,1)S(1)}, u32[]{:S(2)}, u32[]{:S(2)}) %collective-permute-start.2) | collective-permute-done | bytes 131104 | tf_op jit(solution)/shard_map/ppermute | solution.py:278
  12.2 0.5 %shard_map.51 = (bf16[128,512]{1,0:T(8,128)(2,1)S(1)}, bf16[128,512]{1,0:T(8,128)(2,1)S(1)}, bf16[128,512]{1,0:T(8,128)(2,1)S(1)}, bf16[128,512]{1,0:T(8,128)(2,1)S(1)}) custom-call(bf16[512,512]{1,0:T(8,128)(2,1)S(1)} %get-tuple-element.36.own, bf16[512,512]{1,0:T(8,128)(2,1)S(1)} %collective-permute-done.partner, ...), custom_call_target="tpu_custom_call" | custom-call | flops 2147483648 | bytes 1048576 | tf_op jit(solution)/shard_map/pallas_call | solution.py:295
  12.7 0.1 collective-permute-start.3
  12.8 0.0 collective-permute-done.4.refs_1_
  12.8 1.5 %collective-permute-done.5.refs_2_ = bf16[64,640]{1,0:T(8,128)(2,1)S(1)} collective-permute-done((bf16[64,640]{1,0:T(8,128)(2,1)S(1)}, bf16[64,640]{1,0:T(8,128)(2,1)S(1)}, u32[]{:S(2)}, u32[]{:S(2)}) %collective-permute-start.5) | collective-permute-done | bytes 81952 | tf_op jit(solution)/shard_map/ppermute | solution.py:232
  14.3 0.5 collective-permute-done.6.refs_3_
  14.8 2.7 %collective-permute-start.13 = (bf16[64,640]{1,0:T(8,128)(2,1)S(1)}, bf16[64,640]{1,0:T(8,128)(2,1)S(1)}, u32[]{:S(2)}, u32[]{:S(2)}) collective-permute-start(bf16[64,640]{1,0:T(8,128)(2,1)S(1)} %shard_map.53.after.left), channel_id=1, source_target_pairs={{0,4},{4,0},{1,5},{5,1},{2,6},{6,2},{3,7},{7,3},{8,12},{12,8},{9,1... | collective-permute-start | bytes 245768 | tf_op jit(solution)/shard_map/ppermute | solution.py:240
  17.5 0.0 collective-permute-done.3.dh_got
  17.5 0.5 shard_map.54
  18.0 1.5 %collective-permute-start.10 = (bf16[64,640]{1,0:T(8,128)(2,1)S(1)}, bf16[64,640]{1,0:T(8,128)(2,1)S(1)}, u32[]{:S(2)}, u32[]{:S(2)}) collective-permute-start(bf16[64,640]{1,0:T(8,128)(2,1)S(1)} %get-tuple-element.52), channel_id=1, source_target_pairs={{0,3},{1,2},{2,1},{3,0},{4,7},{5,6},{6,5},{7,4},{8,11},{9,10},{10,... | collective-permute-start | bytes 245768 | tf_op jit(solution)/shard_map/ppermute | solution.py:232
  19.5 1.3 %collective-permute-start.11 = (bf16[64,640]{1,0:T(8,128)(2,1)S(1)}, bf16[64,640]{1,0:T(8,128)(2,1)S(1)}, u32[]{:S(2)}, u32[]{:S(2)}) collective-permute-start(bf16[64,640]{1,0:T(8,128)(2,1)S(1)} %get-tuple-element.53), channel_id=1, source_target_pairs={{0,1},{1,0},{2,3},{3,2},{4,5},{5,4},{6,7},{7,6},{8,9},{9,8},{10,11... | collective-permute-start | bytes 245768 | tf_op jit(solution)/shard_map/ppermute | solution.py:232
  20.8 0.8 %collective-permute-start.12 = (bf16[64,640]{1,0:T(8,128)(2,1)S(1)}, bf16[64,640]{1,0:T(8,128)(2,1)S(1)}, u32[]{:S(2)}, u32[]{:S(2)}) collective-permute-start(bf16[64,640]{1,0:T(8,128)(2,1)S(1)} %get-tuple-element.54), channel_id=1, source_target_pairs={{0,2},{1,3},{2,0},{3,1},{4,6},{5,7},{6,4},{7,5},{8,10},{9,11},{10,... | collective-permute-start | bytes 245768 | tf_op jit(solution)/shard_map/ppermute | solution.py:232
  21.6 1.4 %collective-permute-start.7 = (bf16[64,1024]{1,0:T(8,128)(2,1)S(1)}, bf16[64,1024]{1,0:T(8,128)(2,1)S(1)}, u32[]{:S(2)}, u32[]{:S(2)}) collective-permute-start(bf16[64,1024]{1,0:T(8,128)(2,1)S(1)} %get-tuple-element.48), channel_id=1, source_target_pairs={{0,3},{1,2},{2,1},{3,0},{4,7},{5,6},{6,5},{7,4},{8,11},{9,10},{10,... | collective-permute-start | bytes 393224 | tf_op jit(solution)/shard_map/ppermute | solution.py:232
  23.0 0.0 collective-permute-done.13.right
  23.0 1.3 %collective-permute-start.8 = (bf16[64,1024]{1,0:T(8,128)(2,1)S(1)}, bf16[64,1024]{1,0:T(8,128)(2,1)S(1)}, u32[]{:S(2)}, u32[]{:S(2)}) collective-permute-start(bf16[64,1024]{1,0:T(8,128)(2,1)S(1)} %get-tuple-element.49), channel_id=1, source_target_pairs={{0,1},{1,0},{2,3},{3,2},{4,5},{5,4},{6,7},{7,6},{8,9},{9,8},{10,11... | collective-permute-start | bytes 393224 | tf_op jit(solution)/shard_map/ppermute | solution.py:232
  24.3 0.0 collective-permute-done.10.refs_1_
  24.3 1.2 %collective-permute-start.9 = (bf16[64,1024]{1,0:T(8,128)(2,1)S(1)}, bf16[64,1024]{1,0:T(8,128)(2,1)S(1)}, u32[]{:S(2)}, u32[]{:S(2)}) collective-permute-start(bf16[64,1024]{1,0:T(8,128)(2,1)S(1)} %get-tuple-element.50), channel_id=1, source_target_pairs={{0,2},{1,3},{2,0},{3,1},{4,6},{5,7},{6,4},{7,5},{8,10},{9,11},{10,... | collective-permute-start | bytes 393224 | tf_op jit(solution)/shard_map/ppermute | solution.py:232
  25.5 0.0 collective-permute-done.11.refs_2_
  25.5 0.6 %collective-permute-done.12.refs_3_ = bf16[64,640]{1,0:T(8,128)(2,1)S(1)} collective-permute-done((bf16[64,640]{1,0:T(8,128)(2,1)S(1)}, bf16[64,640]{1,0:T(8,128)(2,1)S(1)}, u32[]{:S(2)}, u32[]{:S(2)}) %collective-permute-start.12) | collective-permute-done | bytes 81952 | tf_op jit(solution)/shard_map/ppermute | solution.py:232
  26.2 1.2 %collective-permute-start.15 = (bf16[64,640]{1,0:T(8,128)(2,1)S(1)}, bf16[64,640]{1,0:T(8,128)(2,1)S(1)}, u32[]{:S(2)}, u32[]{:S(2)}) collective-permute-start(bf16[64,640]{1,0:T(8,128)(2,1)S(1)} %get-tuple-element.58.left), channel_id=1, source_target_pairs={{0,4},{4,0},{1,5},{5,1},{2,6},{6,2},{3,7},{7,3},{8,12},{12,8},{9,1... | collective-permute-start | bytes 245768 | tf_op jit(solution)/shard_map/ppermute | solution.py:240
  27.5 2.6 %collective-permute-done.7.refs_1_ = bf16[64,1024]{1,0:T(8,128)(2,1)S(1)} collective-permute-done((bf16[64,1024]{1,0:T(8,128)(2,1)S(1)}, bf16[64,1024]{1,0:T(8,128)(2,1)S(1)}, u32[]{:S(2)}, u32[]{:S(2)}) %collective-permute-start.7) | collective-permute-done | bytes 131104 | tf_op jit(solution)/shard_map/ppermute | solution.py:232
  30.0 0.2 collective-permute-done.8.refs_2_
  30.3 2.3 %collective-permute-done.9.refs_3_ = bf16[64,1024]{1,0:T(8,128)(2,1)S(1)} collective-permute-done((bf16[64,1024]{1,0:T(8,128)(2,1)S(1)}, bf16[64,1024]{1,0:T(8,128)(2,1)S(1)}, u32[]{:S(2)}, u32[]{:S(2)}) %collective-permute-start.9) | collective-permute-done | bytes 131104 | tf_op jit(solution)/shard_map/ppermute | solution.py:232
  32.6 0.1 shard_map.57
  32.7 0.4 collective-permute-start.14
  33.0 1.0 %collective-permute-start.19 = (bf16[64,640]{1,0:T(8,128)(2,1)S(1)}, bf16[64,640]{1,0:T(8,128)(2,1)S(1)}, u32[]{:S(2)}, u32[]{:S(2)}) collective-permute-start(bf16[64,640]{1,0:T(8,128)(2,1)S(1)} %get-tuple-element.56.through.refs_0_), channel_id=1, source_target_pairs={{0,1},{1,0},{2,3},{3,2},{4,5},{5,4},{6,7},{7,6},{8,9},{9,8},{10,11... | collective-permute-start | bytes 245768 | tf_op jit(solution)/shard_map/ppermute | solution.py:232
  34.0 0.0 collective-permute-done.15.right
  34.0 3.0 %collective-permute-start.18 = (bf16[64,640]{1,0:T(8,128)(2,1)S(1)}, bf16[64,640]{1,0:T(8,128)(2,1)S(1)}, u32[]{:S(2)}, u32[]{:S(2)}) collective-permute-start(bf16[64,640]{1,0:T(8,128)(2,1)S(1)} %shard_map.58.refs_0_), channel_id=1, source_target_pairs={{0,3},{1,2},{2,1},{3,0},{4,7},{5,6},{6,5},{7,4},{8,11},{9,10},{10,... | collective-permute-start | bytes 245768 | tf_op jit(solution)/shard_map/ppermute | solution.py:232
  37.0 0.0 collective-permute-start.17
  37.1 1.0 %collective-permute-start.16 = (bf16[64,640]{1,0:T(8,128)(2,1)S(1)}, bf16[64,640]{1,0:T(8,128)(2,1)S(1)}, u32[]{:S(2)}, u32[]{:S(2)}) collective-permute-start(bf16[64,640]{1,0:T(8,128)(2,1)S(1)} %shard_map.58.refs_0_), channel_id=1, source_target_pairs={{0,1},{1,0},{2,3},{3,2},{4,5},{5,4},{6,7},{7,6},{8,9},{9,8},{10,11... | collective-permute-start | bytes 245768 | tf_op jit(solution)/shard_map/ppermute | solution.py:232
  38.0 0.4 collective-permute-done.19.refs_4_.refs_1_
  38.4 4.9 %collective-permute-start.21 = (bf16[64,640]{1,0:T(8,128)(2,1)S(1)}, bf16[64,640]{1,0:T(8,128)(2,1)S(1)}, u32[]{:S(2)}, u32[]{:S(2)}) collective-permute-start(bf16[64,640]{1,0:T(8,128)(2,1)S(1)} %get-tuple-element.56.through.refs_0_), channel_id=1, source_target_pairs={{0,3},{1,2},{2,1},{3,0},{4,7},{5,6},{6,5},{7,4},{8,11},{9,10},{10,... | collective-permute-start | bytes 245768 | tf_op jit(solution)/shard_map/ppermute | solution.py:232
  43.3 0.0 collective-permute-done.18.refs_3_
  43.3 0.0 collective-permute-start.20
  43.3 0.0 collective-permute-done.17.refs_2_
  43.3 0.0 collective-permute-done.16.refs_1_
  43.3 0.0 collective-permute-done.14.right
  43.4 1.3 %collective-permute-start.25 = (bf16[64,1024]{1,0:T(8,128)(2,1)S(1)}, bf16[64,1024]{1,0:T(8,128)(2,1)S(1)}, u32[]{:S(2)}, u32[]{:S(2)}) collective-permute-start(bf16[64,1024]{1,0:T(8,128)(2,1)S(1)} %shard_map.59.after.refs_0_), channel_id=1, source_target_pairs={{0,3},{1,2},{2,1},{3,0},{4,7},{5,6},{6,5},{7,4},{8,11},{9,10},{10,... | collective-permute-start | bytes 393224 | tf_op jit(solution)/shard_map/ppermute | solution.py:232
  44.7 0.8 %collective-permute-start.24 = (bf16[64,1024]{1,0:T(8,128)(2,1)S(1)}, bf16[64,1024]{1,0:T(8,128)(2,1)S(1)}, u32[]{:S(2)}, u32[]{:S(2)}) collective-permute-start(bf16[64,1024]{1,0:T(8,128)(2,1)S(1)} %shard_map.59.after.refs_0_), channel_id=1, source_target_pairs={{0,2},{1,3},{2,0},{3,1},{4,6},{5,7},{6,4},{7,5},{8,10},{9,11},{10,... | collective-permute-start | bytes 393224 | tf_op jit(solution)/shard_map/ppermute | solution.py:232
  45.5 1.4 %collective-permute-start.23 = (bf16[64,1024]{1,0:T(8,128)(2,1)S(1)}, bf16[64,1024]{1,0:T(8,128)(2,1)S(1)}, u32[]{:S(2)}, u32[]{:S(2)}) collective-permute-start(bf16[64,1024]{1,0:T(8,128)(2,1)S(1)} %shard_map.59.after.refs_0_), channel_id=1, source_target_pairs={{0,1},{1,0},{2,3},{3,2},{4,5},{5,4},{6,7},{7,6},{8,9},{9,8},{10,11... | collective-permute-start | bytes 393224 | tf_op jit(solution)/shard_map/ppermute | solution.py:232
  46.9 2.1 %shard_map.61 = (bf16[512,512]{1,0:T(8,128)(2,1)S(1)}, bf16[512,512]{1,0:T(8,128)(2,1)S(1)}, bf16[128,512]{1,0:T(8,128)(2,1)S(1)}) custom-call(bf16[128,512]{1,0:T(8,128)(2,1)S(1)} %get-tuple-element.61.through, bf16[64,1024]{1,0:T(8,128)(2,1)S(1)} %shard_map.59.after.refs_0_, bf16[64,640]{1,0:T(8,128)(2,1)S(1)} %shard_map.58.refs_0_, ...), custom_call_target="tpu_custom_call" | custom-call | flops 2684354560 | bytes 1048576 | tf_op jit(solution)/shard_map/pallas_call | solution.py:324
  49.1 0.0 collective-permute-done.21.refs_3_
  49.1 0.1 collective-permute-start.22
  49.1 0.0 collective-permute-done.20.refs_2_
  49.2 2.7 %shard_map.60 = (bf16[512,512]{1,0:T(8,128)(2,1)S(1)}, bf16[512,512]{1,0:T(8,128)(2,1)S(1)}, bf16[64,640]{1,0:T(8,128)(2,1)}) custom-call(bf16[64,640]{1,0:T(8,128)(2,1)S(1)} %get-tuple-element.56.through.refs_0_, bf16[64,1024]{1,0:T(8,128)(2,1)S(1)} %shard_map.59.after.refs_0_, bf16[64,640]{1,0:T(8,128)(2,1)S(1)} %get-tuple-element.56.through.refs_0_, ...), custom_call_target="tpu_custom_call" | custom-call | flops 2684354560 | bytes 1048576 | tf_op jit(solution)/shard_map/pallas_call | solution.py:324
  51.9 0.0 collective-permute-done.25.refs_3_
  51.9 0.0 collective-permute-done.24.refs_2_
  51.9 0.0 collective-permute-done.23.refs_1_
  51.9 0.0 collective-permute-done.22.other_cot
  51.9 2.2 %shard_map.62 = (f32[512,512]{1,0:T(8,128)}, bf16[2,128,512]{2,1,0:T(8,128)(2,1)}) custom-call(bf16[512,512]{1,0:T(8,128)(2,1)S(1)} %get-tuple-element.59.act_high, bf16[512,512]{1,0:T(8,128)(2,1)S(1)} %get-tuple-element.60.act_low, bf16[512,512]{1,0:T(8,128)(2,1)S(1)} %get-tuple-element.62.out_high, bf16[512,512]{1,0:T(8,128)(2,1)S(1)} %get-tuple-element.63.out_low, ...), custom_call_target="tpu_custom_call" | custom-call | flops 1342177280 | bytes 1048576 | tf_op jit(solution)/shard_map/pallas_call | solution.py:337
  (7 shorter events, 0.2 us)
Async XLA Ops:
  0.6 2.6 %collective-permute-start = (bf16[512,512]{1,0:T(8,128)(2,1)}, bf16[512,512]{1,0:T(8,128)(2,1)S(1)}, u32[]{:S(2)}, u32[]{:S(2)}) collective-permute-start(bf16[512,512]{1,0:T(8,128)(2,1)} %bitcast.6), channel_id=1, source_target_pairs={{0,8},{8,0},{1,9},{9,1},{2,10},{10,2},{3,11},{11,3},{4,12},{12,4},... | collective-permute-start | bytes 1572872 | tf_op jit(solution)/shard_map/ppermute | solution.py:266
  1.1 2.1 %collective-permute-start.1 = (bf16[2,128,512]{2,1,0:T(8,128)(2,1)}, bf16[2,128,512]{2,1,0:T(8,128)(2,1)S(1)}, u32[]{:S(2)}, u32[]{:S(2)}) collective-permute-start(bf16[2,128,512]{2,1,0:T(8,128)(2,1)} %bitcast.7), channel_id=1, source_target_pairs={{0,8},{8,0},{1,9},{9,1},{2,10},{10,2},{3,11},{11,3},{4,12},{12,4},... | collective-permute-start | bytes 786440 | tf_op jit(solution)/shard_map/ppermute | solution.py:267
  1.2 1.1 %copy-start = (bf16[2,128,512]{2,1,0:T(8,128)(2,1)S(1)}, bf16[2,128,512]{2,1,0:T(8,128)(2,1)}, u32[]{:S(2)}) copy-start(bf16[2,128,512]{2,1,0:T(8,128)(2,1)} %param.5) | copy-start | bytes 786436
  1.2 1.2 %copy-start.1 = (bf16[1,2,128,512]{3,2,1,0:T(8,128)(2,1)S(1)}, bf16[1,2,128,512]{3,2,1,0:T(8,128)(2,1)}, u32[]{:S(2)}) copy-start(bf16[1,2,128,512]{3,2,1,0:T(8,128)(2,1)} %param.3) | copy-start | bytes 786436
  4.2 8.0 %collective-permute-start.2 = (bf16[128,512]{1,0:T(8,128)(2,1)S(1)}, bf16[128,512]{1,0:T(8,128)(2,1)S(1)}, u32[]{:S(2)}, u32[]{:S(2)}) collective-permute-start(bf16[128,512]{1,0:T(8,128)(2,1)S(1)} %get-tuple-element.39.after), channel_id=1, source_target_pairs={{16,0},{17,1},{18,2},{19,3},{20,4},{21,5},{22,6},{23,7},{24,8},{25... | collective-permute-start | bytes 393224 | tf_op jit(solution)/shard_map/ppermute | solution.py:278
  5.9 6.9 %collective-permute-start.4 = (bf16[64,640]{1,0:T(8,128)(2,1)S(1)}, bf16[64,640]{1,0:T(8,128)(2,1)S(1)}, u32[]{:S(2)}, u32[]{:S(2)}) collective-permute-start(bf16[64,640]{1,0:T(8,128)(2,1)S(1)} %get-tuple-element.44), channel_id=1, source_target_pairs={{0,3},{1,2},{2,1},{3,0},{4,7},{5,6},{6,5},{7,4},{8,11},{9,10},{10,... | collective-permute-start | bytes 245768 | tf_op jit(solution)/shard_map/ppermute | solution.py:232
  9.8 4.5 %collective-permute-start.5 = (bf16[64,640]{1,0:T(8,128)(2,1)S(1)}, bf16[64,640]{1,0:T(8,128)(2,1)S(1)}, u32[]{:S(2)}, u32[]{:S(2)}) collective-permute-start(bf16[64,640]{1,0:T(8,128)(2,1)S(1)} %get-tuple-element.45), channel_id=1, source_target_pairs={{0,1},{1,0},{2,3},{3,2},{4,5},{5,4},{6,7},{7,6},{8,9},{9,8},{10,11... | collective-permute-start | bytes 245768 | tf_op jit(solution)/shard_map/ppermute | solution.py:232
  10.4 4.4 %collective-permute-start.6 = (bf16[64,640]{1,0:T(8,128)(2,1)S(1)}, bf16[64,640]{1,0:T(8,128)(2,1)S(1)}, u32[]{:S(2)}, u32[]{:S(2)}) collective-permute-start(bf16[64,640]{1,0:T(8,128)(2,1)S(1)} %get-tuple-element.46), channel_id=1, source_target_pairs={{0,2},{1,3},{2,0},{3,1},{4,6},{5,7},{6,4},{7,5},{8,10},{9,11},{10,... | collective-permute-start | bytes 245768 | tf_op jit(solution)/shard_map/ppermute | solution.py:232
  12.7 4.8 %collective-permute-start.3 = (bf16[128,512]{1,0:T(8,128)(2,1)S(1)}, bf16[128,512]{1,0:T(8,128)(2,1)S(1)}, u32[]{:S(2)}, u32[]{:S(2)}) collective-permute-start(bf16[128,512]{1,0:T(8,128)(2,1)S(1)} %get-tuple-element.42), channel_id=1, source_target_pairs={{0,8},{8,0},{1,9},{9,1},{2,10},{10,2},{3,11},{11,3},{4,12},{12,4},... | collective-permute-start | bytes 393224 | tf_op jit(solution)/shard_map/ppermute | solution.py:301
  14.8 8.2 %collective-permute-start.13 = (bf16[64,640]{1,0:T(8,128)(2,1)S(1)}, bf16[64,640]{1,0:T(8,128)(2,1)S(1)}, u32[]{:S(2)}, u32[]{:S(2)}) collective-permute-start(bf16[64,640]{1,0:T(8,128)(2,1)S(1)} %shard_map.53.after.left), channel_id=1, source_target_pairs={{0,4},{4,0},{1,5},{5,1},{2,6},{6,2},{3,7},{7,3},{8,12},{12,8},{9,1... | collective-permute-start | bytes 245768 | tf_op jit(solution)/shard_map/ppermute | solution.py:240
  18.0 6.3 %collective-permute-start.10 = (bf16[64,640]{1,0:T(8,128)(2,1)S(1)}, bf16[64,640]{1,0:T(8,128)(2,1)S(1)}, u32[]{:S(2)}, u32[]{:S(2)}) collective-permute-start(bf16[64,640]{1,0:T(8,128)(2,1)S(1)} %get-tuple-element.52), channel_id=1, source_target_pairs={{0,3},{1,2},{2,1},{3,0},{4,7},{5,6},{6,5},{7,4},{8,11},{9,10},{10,... | collective-permute-start | bytes 245768 | tf_op jit(solution)/shard_map/ppermute | solution.py:232
  19.5 6.0 %collective-permute-start.11 = (bf16[64,640]{1,0:T(8,128)(2,1)S(1)}, bf16[64,640]{1,0:T(8,128)(2,1)S(1)}, u32[]{:S(2)}, u32[]{:S(2)}) collective-permute-start(bf16[64,640]{1,0:T(8,128)(2,1)S(1)} %get-tuple-element.53), channel_id=1, source_target_pairs={{0,1},{1,0},{2,3},{3,2},{4,5},{5,4},{6,7},{7,6},{8,9},{9,8},{10,11... | collective-permute-start | bytes 245768 | tf_op jit(solution)/shard_map/ppermute | solution.py:232
  20.8 5.3 %collective-permute-start.12 = (bf16[64,640]{1,0:T(8,128)(2,1)S(1)}, bf16[64,640]{1,0:T(8,128)(2,1)S(1)}, u32[]{:S(2)}, u32[]{:S(2)}) collective-permute-start(bf16[64,640]{1,0:T(8,128)(2,1)S(1)} %get-tuple-element.54), channel_id=1, source_target_pairs={{0,2},{1,3},{2,0},{3,1},{4,6},{5,7},{6,4},{7,5},{8,10},{9,11},{10,... | collective-permute-start | bytes 245768 | tf_op jit(solution)/shard_map/ppermute | solution.py:232
  21.6 8.4 %collective-permute-start.7 = (bf16[64,1024]{1,0:T(8,128)(2,1)S(1)}, bf16[64,1024]{1,0:T(8,128)(2,1)S(1)}, u32[]{:S(2)}, u32[]{:S(2)}) collective-permute-start(bf16[64,1024]{1,0:T(8,128)(2,1)S(1)} %get-tuple-element.48), channel_id=1, source_target_pairs={{0,3},{1,2},{2,1},{3,0},{4,7},{5,6},{6,5},{7,4},{8,11},{9,10},{10,... | collective-permute-start | bytes 393224 | tf_op jit(solution)/shard_map/ppermute | solution.py:232
  23.0 7.3 %collective-permute-start.8 = (bf16[64,1024]{1,0:T(8,128)(2,1)S(1)}, bf16[64,1024]{1,0:T(8,128)(2,1)S(1)}, u32[]{:S(2)}, u32[]{:S(2)}) collective-permute-start(bf16[64,1024]{1,0:T(8,128)(2,1)S(1)} %get-tuple-element.49), channel_id=1, source_target_pairs={{0,1},{1,0},{2,3},{3,2},{4,5},{5,4},{6,7},{7,6},{8,9},{9,8},{10,11... | collective-permute-start | bytes 393224 | tf_op jit(solution)/shard_map/ppermute | solution.py:232
  24.3 8.3 %collective-permute-start.9 = (bf16[64,1024]{1,0:T(8,128)(2,1)S(1)}, bf16[64,1024]{1,0:T(8,128)(2,1)S(1)}, u32[]{:S(2)}, u32[]{:S(2)}) collective-permute-start(bf16[64,1024]{1,0:T(8,128)(2,1)S(1)} %get-tuple-element.50), channel_id=1, source_target_pairs={{0,2},{1,3},{2,0},{3,1},{4,6},{5,7},{6,4},{7,5},{8,10},{9,11},{10,... | collective-permute-start | bytes 393224 | tf_op jit(solution)/shard_map/ppermute | solution.py:232
  26.2 7.8 %collective-permute-start.15 = (bf16[64,640]{1,0:T(8,128)(2,1)S(1)}, bf16[64,640]{1,0:T(8,128)(2,1)S(1)}, u32[]{:S(2)}, u32[]{:S(2)}) collective-permute-start(bf16[64,640]{1,0:T(8,128)(2,1)S(1)} %get-tuple-element.58.left), channel_id=1, source_target_pairs={{0,4},{4,0},{1,5},{5,1},{2,6},{6,2},{3,7},{7,3},{8,12},{12,8},{9,1... | collective-permute-start | bytes 245768 | tf_op jit(solution)/shard_map/ppermute | solution.py:240
  32.7 10.6 %collective-permute-start.14 = (bf16[64,1024]{1,0:T(8,128)(2,1)S(1)}, bf16[64,1024]{1,0:T(8,128)(2,1)S(1)}, u32[]{:S(2)}, u32[]{:S(2)}) collective-permute-start(bf16[64,1024]{1,0:T(8,128)(2,1)S(1)} %get-tuple-element.57.left), channel_id=1, source_target_pairs={{0,4},{4,0},{1,5},{5,1},{2,6},{6,2},{3,7},{7,3},{8,12},{12,8},{9,1... | collective-permute-start | bytes 393224 | tf_op jit(solution)/shard_map/ppermute | solution.py:240
  33.0 5.3 %collective-permute-start.19 = (bf16[64,640]{1,0:T(8,128)(2,1)S(1)}, bf16[64,640]{1,0:T(8,128)(2,1)S(1)}, u32[]{:S(2)}, u32[]{:S(2)}) collective-permute-start(bf16[64,640]{1,0:T(8,128)(2,1)S(1)} %get-tuple-element.56.through.refs_0_), channel_id=1, source_target_pairs={{0,1},{1,0},{2,3},{3,2},{4,5},{5,4},{6,7},{7,6},{8,9},{9,8},{10,11... | collective-permute-start | bytes 245768 | tf_op jit(solution)/shard_map/ppermute | solution.py:232
  34.0 9.2 %collective-permute-start.18 = (bf16[64,640]{1,0:T(8,128)(2,1)S(1)}, bf16[64,640]{1,0:T(8,128)(2,1)S(1)}, u32[]{:S(2)}, u32[]{:S(2)}) collective-permute-start(bf16[64,640]{1,0:T(8,128)(2,1)S(1)} %shard_map.58.refs_0_), channel_id=1, source_target_pairs={{0,3},{1,2},{2,1},{3,0},{4,7},{5,6},{6,5},{7,4},{8,11},{9,10},{10,... | collective-permute-start | bytes 245768 | tf_op jit(solution)/shard_map/ppermute | solution.py:232
  37.0 6.3 %collective-permute-start.17 = (bf16[64,640]{1,0:T(8,128)(2,1)S(1)}, bf16[64,640]{1,0:T(8,128)(2,1)S(1)}, u32[]{:S(2)}, u32[]{:S(2)}) collective-permute-start(bf16[64,640]{1,0:T(8,128)(2,1)S(1)} %shard_map.58.refs_0_), channel_id=1, source_target_pairs={{0,2},{1,3},{2,0},{3,1},{4,6},{5,7},{6,4},{7,5},{8,10},{9,11},{10,... | collective-permute-start | bytes 245768 | tf_op jit(solution)/shard_map/ppermute | solution.py:232
  37.1 6.3 %collective-permute-start.16 = (bf16[64,640]{1,0:T(8,128)(2,1)S(1)}, bf16[64,640]{1,0:T(8,128)(2,1)S(1)}, u32[]{:S(2)}, u32[]{:S(2)}) collective-permute-start(bf16[64,640]{1,0:T(8,128)(2,1)S(1)} %shard_map.58.refs_0_), channel_id=1, source_target_pairs={{0,1},{1,0},{2,3},{3,2},{4,5},{5,4},{6,7},{7,6},{8,9},{9,8},{10,11... | collective-permute-start | bytes 245768 | tf_op jit(solution)/shard_map/ppermute | solution.py:232
  38.4 10.7 %collective-permute-start.21 = (bf16[64,640]{1,0:T(8,128)(2,1)S(1)}, bf16[64,640]{1,0:T(8,128)(2,1)S(1)}, u32[]{:S(2)}, u32[]{:S(2)}) collective-permute-start(bf16[64,640]{1,0:T(8,128)(2,1)S(1)} %get-tuple-element.56.through.refs_0_), channel_id=1, source_target_pairs={{0,3},{1,2},{2,1},{3,0},{4,7},{5,6},{6,5},{7,4},{8,11},{9,10},{10,... | collective-permute-start | bytes 245768 | tf_op jit(solution)/shard_map/ppermute | solution.py:232
  43.3 5.9 %collective-permute-start.20 = (bf16[64,640]{1,0:T(8,128)(2,1)S(1)}, bf16[64,640]{1,0:T(8,128)(2,1)S(1)}, u32[]{:S(2)}, u32[]{:S(2)}) collective-permute-start(bf16[64,640]{1,0:T(8,128)(2,1)S(1)} %get-tuple-element.56.through.refs_0_), channel_id=1, source_target_pairs={{0,2},{1,3},{2,0},{3,1},{4,6},{5,7},{6,4},{7,5},{8,10},{9,11},{10,... | collective-permute-start | bytes 245768 | tf_op jit(solution)/shard_map/ppermute | solution.py:232
  43.4 8.5 %collective-permute-start.25 = (bf16[64,1024]{1,0:T(8,128)(2,1)S(1)}, bf16[64,1024]{1,0:T(8,128)(2,1)S(1)}, u32[]{:S(2)}, u32[]{:S(2)}) collective-permute-start(bf16[64,1024]{1,0:T(8,128)(2,1)S(1)} %shard_map.59.after.refs_0_), channel_id=1, source_target_pairs={{0,3},{1,2},{2,1},{3,0},{4,7},{5,6},{6,5},{7,4},{8,11},{9,10},{10,... | collective-permute-start | bytes 393224 | tf_op jit(solution)/shard_map/ppermute | solution.py:232
  44.7 7.2 %collective-permute-start.24 = (bf16[64,1024]{1,0:T(8,128)(2,1)S(1)}, bf16[64,1024]{1,0:T(8,128)(2,1)S(1)}, u32[]{:S(2)}, u32[]{:S(2)}) collective-permute-start(bf16[64,1024]{1,0:T(8,128)(2,1)S(1)} %shard_map.59.after.refs_0_), channel_id=1, source_target_pairs={{0,2},{1,3},{2,0},{3,1},{4,6},{5,7},{6,4},{7,5},{8,10},{9,11},{10,... | collective-permute-start | bytes 393224 | tf_op jit(solution)/shard_map/ppermute | solution.py:232
  45.5 6.4 %collective-permute-start.23 = (bf16[64,1024]{1,0:T(8,128)(2,1)S(1)}, bf16[64,1024]{1,0:T(8,128)(2,1)S(1)}, u32[]{:S(2)}, u32[]{:S(2)}) collective-permute-start(bf16[64,1024]{1,0:T(8,128)(2,1)S(1)} %shard_map.59.after.refs_0_), channel_id=1, source_target_pairs={{0,1},{1,0},{2,3},{3,2},{4,5},{5,4},{6,7},{7,6},{8,9},{9,8},{10,11... | collective-permute-start | bytes 393224 | tf_op jit(solution)/shard_map/ppermute | solution.py:232
  49.1 2.8 %collective-permute-start.22 = (bf16[128,512]{1,0:T(8,128)(2,1)S(1)}, bf16[128,512]{1,0:T(8,128)(2,1)S(1)}, u32[]{:S(2)}, u32[]{:S(2)}) collective-permute-start(bf16[128,512]{1,0:T(8,128)(2,1)S(1)} %get-tuple-element.65), channel_id=1, source_target_pairs={{0,8},{8,0},{1,9},{9,1},{2,10},{10,2},{3,11},{11,3},{4,12},{12,4},... | collective-permute-start | bytes 393224 | tf_op jit(solution)/shard_map/ppermute | solution.py:336

commit v16 on v15

--- a/solution.py
+++ b/solution.py
@@ -179,9 +179,14 @@
     return split(((2.0 - ridge * scale) * tail - inner) * scale)
 
 
-def inverse_kernel(count, through, after, *refs):
-    pieces, (high, low, through_copy, blocks, total) = refs[:GROUP], refs[GROUP:]
+def through_kernel(count, through, after, *refs):
+    through_copy = refs[GROUP + 2]
     through_copy[...] = through[...]
+    inverse_kernel(count, after, *refs[:GROUP + 2], *refs[GROUP + 3:])
+
+
+def inverse_kernel(count, after, *refs):
+    pieces, (high, low, blocks, total) = refs[:GROUP], refs[GROUP:]
     for step, piece in enumerate(pieces):
         blocks[group_place() ^ step] = piece[...]
     size = total.shape[0] // GROUP
@@ -320,19 +325,19 @@
     )(*(pieces[step] for step in (0, 3, 1, 2)), act_part)
     act = send([act_part] * GROUP)
 
-    def inverse(pieces, through, after):
+    def inverse(pieces, after, *through):
         return call(
-            functools.partial(inverse_kernel, count),
+            functools.partial(through_kernel if through else inverse_kernel, count),
             20 * width**3,
-            [array(width, width)] * 2 + [array(*through.shape)],
-            [VMEM, ANY] + [VMEM] * GROUP,
+            [array(width, width)] * 2 + [array(*value.shape) for value in through],
+            [VMEM] * len(through) + [ANY] + [VMEM] * GROUP,
             [pltpu.VMEM((GROUP, size // 2, factor), BF16), pltpu.VMEM((width, width), BF16)],
-        )(through, after, *pieces)
+        )(*through, after, *pieces)
 
     total = exchange(total, (*out, act[1]))
     grad = send([total] * GROUP)
-    *out_inv, give_cot = inverse(out, give_cot, total)
-    *act_inv, _ = inverse(act, act_part, total)
+    *out_inv, give_cot = inverse(out, total, give_cot)
+    act_inv = inverse(act, total)
     other_cot = lax.ppermute(give_cot, "core", SWAP)
     update, cot = call(
         update_kernel,

time: 54.3 us -> 53.8 us (level)
  Pallas kernels: 9.6 us -> 9.03 us
    pallas_call x2, Pallas kernels: 4.85 us -> 4.28 us  [inverse(): call(functools.partial(through_kernel if through else inverse_kernel, cou...]
  transfers between devices with their start and end apart: 26 -> 26, of which waited for: 9 -> 10; matrix products, arithmetic and copies ran while one was open for 2% -> 2% of each run, Pallas kernels for 12% -> 11%
where the time goes in v16:
time: 53.8 us; the launch traced here: 53.6 us
  starting transfers between devices  31.7 us (59%)
  waiting for transfers between devices  10.8 us (20%)
  Pallas kernels  9.03 us (17%)
  other arithmetic  1.18 us (2%)
  between operations  0.8 us (1%)
    ppermute x18, starting transfers between devices, send(): lax.ppermute(parts[step], ('near', 'side'), [(i, i ^ step) for i in range...  25.4 us
    ppermute x18, waiting for transfers between devices, send(): lax.ppermute(parts[step], ('near', 'side'), [(i, i ^ step) for i in range...  8.3 us
    pallas_call x2, Pallas kernels, inverse(): call(functools.partial(through_kernel if through else inverse_kernel, cou...  4.28 us
    ppermute x3, starting transfers between devices, exchange(): got = lax.ppermute(value, 'far', route)  4.27 us
    pallas_call x1, Pallas kernels, body(): call(update_kernel, 10 * width ** 3, [array(width, width, dtype=F32), arr...  2.17 us
    ppermute x1, waiting for transfers between devices, body(): upstream = lax.ppermute(down, 'row', [(r, r - 1) for r in range(1, pairs)])  1.69 us
    ppermute x1, starting transfers between devices, body(): upstream = lax.ppermute(down, 'row', [(r, r - 1) for r in range(1, pairs)])  1.29 us
    select_n x2, other arithmetic, near_copy(): return jnp.where(core > 1, jnp.zeros_like(value), value)  1.18 us
  transfers between devices with their start and end apart: 26, of which 10 were waited for; matrix products, arithmetic and copies ran while one was open for 2% of the time, Pallas kernels for 11%

profile of v16, /device:TPU:0, one launch (start us, length us, event | category | flops | bytes accessed | tf_op | source)
XLA Modules:
  0.0 53.6 jit_solution(10612607493607106937)
XLA Ops:
  0.6 0.5 collective-permute-start
  1.1 0.1 collective-permute-start.1
  1.2 0.0 copy-start
  1.2 1.1 %broadcast_select_fusion.weight = bf16[512,512]{1,0:T(8,128)(2,1)S(1)} fusion(pred[]{:T(512)S(6)} %gt.2, bf16[1,512,512]{2,1,0:T(8,128)(2,1)} %param.4), kind=kLoop, calls=%fused_computation | loop fusion | flops 262144 | bytes 1048577 | tf_op jit(solution)/shard_map/jit(_where)/select_n | solution.py:269
  2.4 0.0 copy-done
  2.4 0.0 copy-done.1
  2.5 0.8 %collective-permute-done.1.partner_local = bf16[2,128,512]{2,1,0:T(8,128)(2,1)S(1)} collective-permute-done((bf16[2,128,512]{2,1,0:T(8,128)(2,1)}, bf16[2,128,512]{2,1,0:T(8,128)(2,1)S(1)}, u32[]{:S(2)}, u32[]{:S(2)}) %collective-permute-start.1) | collective-permute-done | bytes 262176 | tf_op jit(solution)/shard_map/ppermute | solution.py:272
  3.3 0.0 collective-permute-done.partner
  3.3 0.9 %shard_map.50 = (bf16[512,512]{1,0:T(8,128)(2,1)S(1)}, bf16[2,128,512]{2,1,0:T(8,128)(2,1)S(1)}, bf16[128,512]{1,0:T(8,128)(2,1)S(1)}, f32[128,512]{1,0:T(8,128)...) custom-call(bf16[512,512]{1,0:T(8,128)(2,1)S(1)} %broadcast_select_fusion.weight, ...), custom_call_target="tpu_custom_call" | custom-call | flops 268435456 | bytes 1048576 | tf_op jit(solution)/shard_map/pallas_call | solution.py:275
  4.2 1.3 %collective-permute-start.2 = (bf16[128,512]{1,0:T(8,128)(2,1)S(1)}, bf16[128,512]{1,0:T(8,128)(2,1)S(1)}, u32[]{:S(2)}, u32[]{:S(2)}) collective-permute-start(bf16[128,512]{1,0:T(8,128)(2,1)S(1)} %get-tuple-element.39.after), channel_id=1, source_target_pairs={{16,0},{17,1},{18,2},{19,3},{20,4},{21,5},{22,6},{23,7},{24,8},{25... | collective-permute-start | bytes 393224 | tf_op jit(solution)/shard_map/ppermute | solution.py:283
  5.5 0.4 shard_map.52
  5.9 4.0 %collective-permute-start.4 = (bf16[64,640]{1,0:T(8,128)(2,1)S(1)}, bf16[64,640]{1,0:T(8,128)(2,1)S(1)}, u32[]{:S(2)}, u32[]{:S(2)}) collective-permute-start(bf16[64,640]{1,0:T(8,128)(2,1)S(1)} %get-tuple-element.44), channel_id=1, source_target_pairs={{0,3},{1,2},{2,1},{3,0},{4,7},{5,6},{6,5},{7,4},{8,11},{9,10},{10,... | collective-permute-start | bytes 245768 | tf_op jit(solution)/shard_map/ppermute | solution.py:237
  9.8 0.5 %collective-permute-start.5 = (bf16[64,640]{1,0:T(8,128)(2,1)S(1)}, bf16[64,640]{1,0:T(8,128)(2,1)S(1)}, u32[]{:S(2)}, u32[]{:S(2)}) collective-permute-start(bf16[64,640]{1,0:T(8,128)(2,1)S(1)} %get-tuple-element.45), channel_id=1, source_target_pairs={{0,1},{1,0},{2,3},{3,2},{4,5},{5,4},{6,7},{7,6},{8,9},{9,8},{10,11... | collective-permute-start | bytes 245768 | tf_op jit(solution)/shard_map/ppermute | solution.py:237
  10.4 0.1 collective-permute-start.6
  10.5 1.7 %collective-permute-done.2.arrived = bf16[128,512]{1,0:T(8,128)(2,1)S(1)} collective-permute-done((bf16[128,512]{1,0:T(8,128)(2,1)S(1)}, bf16[128,512]{1,0:T(8,128)(2,1)S(1)}, u32[]{:S(2)}, u32[]{:S(2)}) %collective-permute-start.2) | collective-permute-done | bytes 131104 | tf_op jit(solution)/shard_map/ppermute | solution.py:283
  12.2 0.5 %shard_map.51 = (bf16[128,512]{1,0:T(8,128)(2,1)S(1)}, bf16[128,512]{1,0:T(8,128)(2,1)S(1)}, bf16[128,512]{1,0:T(8,128)(2,1)S(1)}, bf16[128,512]{1,0:T(8,128)(2,1)S(1)}) custom-call(bf16[512,512]{1,0:T(8,128)(2,1)S(1)} %get-tuple-element.36.own, bf16[512,512]{1,0:T(8,128)(2,1)S(1)} %collective-permute-done.partner, ...), custom_call_target="tpu_custom_call" | custom-call | flops 2147483648 | bytes 1048576 | tf_op jit(solution)/shard_map/pallas_call | solution.py:300
  12.7 0.1 collective-permute-start.3
  12.8 0.0 collective-permute-done.4.refs_1_
  12.8 1.5 %collective-permute-done.5.refs_2_ = bf16[64,640]{1,0:T(8,128)(2,1)S(1)} collective-permute-done((bf16[64,640]{1,0:T(8,128)(2,1)S(1)}, bf16[64,640]{1,0:T(8,128)(2,1)S(1)}, u32[]{:S(2)}, u32[]{:S(2)}) %collective-permute-start.5) | collective-permute-done | bytes 81952 | tf_op jit(solution)/shard_map/ppermute | solution.py:237
  14.3 0.5 collective-permute-done.6.refs_3_
  14.8 2.7 %collective-permute-start.13 = (bf16[64,640]{1,0:T(8,128)(2,1)S(1)}, bf16[64,640]{1,0:T(8,128)(2,1)S(1)}, u32[]{:S(2)}, u32[]{:S(2)}) collective-permute-start(bf16[64,640]{1,0:T(8,128)(2,1)S(1)} %shard_map.53.after.left), channel_id=1, source_target_pairs={{0,4},{4,0},{1,5},{5,1},{2,6},{6,2},{3,7},{7,3},{8,12},{12,8},{9,1... | collective-permute-start | bytes 245768 | tf_op jit(solution)/shard_map/ppermute | solution.py:245
  17.5 0.0 collective-permute-done.3.dh_got
  17.5 0.5 %shard_map.54 = (bf16[64,640]{1,0:T(8,128)(2,1)S(1)}, bf16[64,640]{1,0:T(8,128)(2,1)S(1)}, bf16[64,640]{1,0:T(8,128)(2,1)S(1)}, bf16[64,640]{1,0:T(8,128)(2,1)S(...) custom-call(bf16[2,128,512]{2,1,0:T(8,128)(2,1)S(1)} %get-tuple-elem, ...), custom_call_target="tpu_custom_call" | custom-call | flops 268435456 | bytes 1048576 | tf_op jit(solution)/shard_map/pallas_call | solution.py:308
  18.0 1.5 %collective-permute-start.10 = (bf16[64,640]{1,0:T(8,128)(2,1)S(1)}, bf16[64,640]{1,0:T(8,128)(2,1)S(1)}, u32[]{:S(2)}, u32[]{:S(2)}) collective-permute-start(bf16[64,640]{1,0:T(8,128)(2,1)S(1)} %get-tuple-element.52), channel_id=1, source_target_pairs={{0,3},{1,2},{2,1},{3,0},{4,7},{5,6},{6,5},{7,4},{8,11},{9,10},{10,... | collective-permute-start | bytes 245768 | tf_op jit(solution)/shard_map/ppermute | solution.py:237
  19.5 1.3 %collective-permute-start.11 = (bf16[64,640]{1,0:T(8,128)(2,1)S(1)}, bf16[64,640]{1,0:T(8,128)(2,1)S(1)}, u32[]{:S(2)}, u32[]{:S(2)}) collective-permute-start(bf16[64,640]{1,0:T(8,128)(2,1)S(1)} %get-tuple-element.53), channel_id=1, source_target_pairs={{0,1},{1,0},{2,3},{3,2},{4,5},{5,4},{6,7},{7,6},{8,9},{9,8},{10,11... | collective-permute-start | bytes 245768 | tf_op jit(solution)/shard_map/ppermute | solution.py:237
  20.8 0.8 %collective-permute-start.12 = (bf16[64,640]{1,0:T(8,128)(2,1)S(1)}, bf16[64,640]{1,0:T(8,128)(2,1)S(1)}, u32[]{:S(2)}, u32[]{:S(2)}) collective-permute-start(bf16[64,640]{1,0:T(8,128)(2,1)S(1)} %get-tuple-element.54), channel_id=1, source_target_pairs={{0,2},{1,3},{2,0},{3,1},{4,6},{5,7},{6,4},{7,5},{8,10},{9,11},{10,... | collective-permute-start | bytes 245768 | tf_op jit(solution)/shard_map/ppermute | solution.py:237
  21.6 1.4 %collective-permute-start.7 = (bf16[64,1024]{1,0:T(8,128)(2,1)S(1)}, bf16[64,1024]{1,0:T(8,128)(2,1)S(1)}, u32[]{:S(2)}, u32[]{:S(2)}) collective-permute-start(bf16[64,1024]{1,0:T(8,128)(2,1)S(1)} %get-tuple-element.48), channel_id=1, source_target_pairs={{0,3},{1,2},{2,1},{3,0},{4,7},{5,6},{6,5},{7,4},{8,11},{9,10},{10,... | collective-permute-start | bytes 393224 | tf_op jit(solution)/shard_map/ppermute | solution.py:237
  23.0 0.0 collective-permute-done.13.right
  23.0 1.3 %collective-permute-start.8 = (bf16[64,1024]{1,0:T(8,128)(2,1)S(1)}, bf16[64,1024]{1,0:T(8,128)(2,1)S(1)}, u32[]{:S(2)}, u32[]{:S(2)}) collective-permute-start(bf16[64,1024]{1,0:T(8,128)(2,1)S(1)} %get-tuple-element.49), channel_id=1, source_target_pairs={{0,1},{1,0},{2,3},{3,2},{4,5},{5,4},{6,7},{7,6},{8,9},{9,8},{10,11... | collective-permute-start | bytes 393224 | tf_op jit(solution)/shard_map/ppermute | solution.py:237
  24.3 0.0 collective-permute-done.10.refs_1_
  24.3 1.2 %collective-permute-start.9 = (bf16[64,1024]{1,0:T(8,128)(2,1)S(1)}, bf16[64,1024]{1,0:T(8,128)(2,1)S(1)}, u32[]{:S(2)}, u32[]{:S(2)}) collective-permute-start(bf16[64,1024]{1,0:T(8,128)(2,1)S(1)} %get-tuple-element.50), channel_id=1, source_target_pairs={{0,2},{1,3},{2,0},{3,1},{4,6},{5,7},{6,4},{7,5},{8,10},{9,11},{10,... | collective-permute-start | bytes 393224 | tf_op jit(solution)/shard_map/ppermute | solution.py:237
  25.5 0.0 collective-permute-done.11.refs_2_
  25.5 0.6 %collective-permute-done.12.refs_3_ = bf16[64,640]{1,0:T(8,128)(2,1)S(1)} collective-permute-done((bf16[64,640]{1,0:T(8,128)(2,1)S(1)}, bf16[64,640]{1,0:T(8,128)(2,1)S(1)}, u32[]{:S(2)}, u32[]{:S(2)}) %collective-permute-start.12) | collective-permute-done | bytes 81952 | tf_op jit(solution)/shard_map/ppermute | solution.py:237
  26.2 1.2 %collective-permute-start.15 = (bf16[64,640]{1,0:T(8,128)(2,1)S(1)}, bf16[64,640]{1,0:T(8,128)(2,1)S(1)}, u32[]{:S(2)}, u32[]{:S(2)}) collective-permute-start(bf16[64,640]{1,0:T(8,128)(2,1)S(1)} %get-tuple-element.57.left), channel_id=1, source_target_pairs={{0,4},{4,0},{1,5},{5,1},{2,6},{6,2},{3,7},{7,3},{8,12},{12,8},{9,1... | collective-permute-start | bytes 245768 | tf_op jit(solution)/shard_map/ppermute | solution.py:245
  27.5 2.6 %collective-permute-done.7.refs_1_ = bf16[64,1024]{1,0:T(8,128)(2,1)S(1)} collective-permute-done((bf16[64,1024]{1,0:T(8,128)(2,1)S(1)}, bf16[64,1024]{1,0:T(8,128)(2,1)S(1)}, u32[]{:S(2)}, u32[]{:S(2)}) %collective-permute-start.7) | collective-permute-done | bytes 131104 | tf_op jit(solution)/shard_map/ppermute | solution.py:237
  30.0 0.2 collective-permute-done.8.refs_2_
  30.3 2.3 %collective-permute-done.9.refs_3_ = bf16[64,1024]{1,0:T(8,128)(2,1)S(1)} collective-permute-done((bf16[64,1024]{1,0:T(8,128)(2,1)S(1)}, bf16[64,1024]{1,0:T(8,128)(2,1)S(1)}, u32[]{:S(2)}, u32[]{:S(2)}) %collective-permute-start.9) | collective-permute-done | bytes 131104 | tf_op jit(solution)/shard_map/ppermute | solution.py:237
  32.6 0.1 shard_map.57
  32.7 0.4 collective-permute-start.14
  33.0 1.0 %collective-permute-start.19 = (bf16[64,640]{1,0:T(8,128)(2,1)S(1)}, bf16[64,640]{1,0:T(8,128)(2,1)S(1)}, u32[]{:S(2)}, u32[]{:S(2)}) collective-permute-start(bf16[64,640]{1,0:T(8,128)(2,1)S(1)} %get-tuple-element.58.refs_0_), channel_id=1, source_target_pairs={{0,1},{1,0},{2,3},{3,2},{4,5},{5,4},{6,7},{7,6},{8,9},{9,8},{10,11... | collective-permute-start | bytes 245768 | tf_op jit(solution)/shard_map/ppermute | solution.py:237
  34.0 0.0 collective-permute-done.15.right
  34.0 3.0 %collective-permute-start.18 = (bf16[64,640]{1,0:T(8,128)(2,1)S(1)}, bf16[64,640]{1,0:T(8,128)(2,1)S(1)}, u32[]{:S(2)}, u32[]{:S(2)}) collective-permute-start(bf16[64,640]{1,0:T(8,128)(2,1)S(1)} %shard_map.58.refs_0_), channel_id=1, source_target_pairs={{0,3},{1,2},{2,1},{3,0},{4,7},{5,6},{6,5},{7,4},{8,11},{9,10},{10,... | collective-permute-start | bytes 245768 | tf_op jit(solution)/shard_map/ppermute | solution.py:237
  37.0 0.0 collective-permute-start.17
  37.1 1.0 %collective-permute-start.16 = (bf16[64,640]{1,0:T(8,128)(2,1)S(1)}, bf16[64,640]{1,0:T(8,128)(2,1)S(1)}, u32[]{:S(2)}, u32[]{:S(2)}) collective-permute-start(bf16[64,640]{1,0:T(8,128)(2,1)S(1)} %shard_map.58.refs_0_), channel_id=1, source_target_pairs={{0,1},{1,0},{2,3},{3,2},{4,5},{5,4},{6,7},{7,6},{8,9},{9,8},{10,11... | collective-permute-start | bytes 245768 | tf_op jit(solution)/shard_map/ppermute | solution.py:237
  38.0 0.4 collective-permute-done.19.refs_4_.refs_1_
  38.4 4.9 %collective-permute-start.21 = (bf16[64,640]{1,0:T(8,128)(2,1)S(1)}, bf16[64,640]{1,0:T(8,128)(2,1)S(1)}, u32[]{:S(2)}, u32[]{:S(2)}) collective-permute-start(bf16[64,640]{1,0:T(8,128)(2,1)S(1)} %get-tuple-element.58.refs_0_), channel_id=1, source_target_pairs={{0,3},{1,2},{2,1},{3,0},{4,7},{5,6},{6,5},{7,4},{8,11},{9,10},{10,... | collective-permute-start | bytes 245768 | tf_op jit(solution)/shard_map/ppermute | solution.py:237
  43.3 0.0 collective-permute-done.18.refs_3_
  43.3 0.0 collective-permute-start.20
  43.3 0.0 collective-permute-done.17.refs_2_
  43.3 0.0 collective-permute-done.16.refs_1_
  43.3 0.0 collective-permute-done.14.right
  43.4 1.3 %collective-permute-start.25 = (bf16[64,1024]{1,0:T(8,128)(2,1)S(1)}, bf16[64,1024]{1,0:T(8,128)(2,1)S(1)}, u32[]{:S(2)}, u32[]{:S(2)}) collective-permute-start(bf16[64,1024]{1,0:T(8,128)(2,1)S(1)} %shard_map.59.after.refs_0_), channel_id=1, source_target_pairs={{0,3},{1,2},{2,1},{3,0},{4,7},{5,6},{6,5},{7,4},{8,11},{9,10},{10,... | collective-permute-start | bytes 393224 | tf_op jit(solution)/shard_map/ppermute | solution.py:237
  44.7 0.8 %collective-permute-start.24 = (bf16[64,1024]{1,0:T(8,128)(2,1)S(1)}, bf16[64,1024]{1,0:T(8,128)(2,1)S(1)}, u32[]{:S(2)}, u32[]{:S(2)}) collective-permute-start(bf16[64,1024]{1,0:T(8,128)(2,1)S(1)} %shard_map.59.after.refs_0_), channel_id=1, source_target_pairs={{0,2},{1,3},{2,0},{3,1},{4,6},{5,7},{6,4},{7,5},{8,10},{9,11},{10,... | collective-permute-start | bytes 393224 | tf_op jit(solution)/shard_map/ppermute | solution.py:237
  45.5 1.4 %collective-permute-start.23 = (bf16[64,1024]{1,0:T(8,128)(2,1)S(1)}, bf16[64,1024]{1,0:T(8,128)(2,1)S(1)}, u32[]{:S(2)}, u32[]{:S(2)}) collective-permute-start(bf16[64,1024]{1,0:T(8,128)(2,1)S(1)} %shard_map.59.after.refs_0_), channel_id=1, source_target_pairs={{0,1},{1,0},{2,3},{3,2},{4,5},{5,4},{6,7},{7,6},{8,9},{9,8},{10,11... | collective-permute-start | bytes 393224 | tf_op jit(solution)/shard_map/ppermute | solution.py:237
  46.9 2.1 %shard_map.61 = (bf16[512,512]{1,0:T(8,128)(2,1)S(1)}, bf16[512,512]{1,0:T(8,128)(2,1)S(1)}, bf16[128,512]{1,0:T(8,128)(2,1)S(1)}) custom-call(bf16[128,512]{1,0:T(8,128)(2,1)S(1)} %get-tuple-element.61.through, bf16[64,1024]{1,0:T(8,128)(2,1)S(1)} %shard_map.59.after.refs_0_, bf16[64,640]{1,0:T(8,128)(2,1)S(1)} %shard_map.58.refs_0_, ...), custom_call_target="tpu_custom_call" | custom-call | flops 2684354560 | bytes 1048576 | tf_op jit(solution)/shard_map/pallas_call | solution.py:329
  49.1 0.0 collective-permute-done.21.refs_3_
  49.1 0.1 collective-permute-start.22
  49.1 0.0 collective-permute-done.20.refs_2_
  49.2 2.1 %shard_map.60 = (bf16[512,512]{1,0:T(8,128)(2,1)S(1)}, bf16[512,512]{1,0:T(8,128)(2,1)S(1)}) custom-call(bf16[64,1024]{1,0:T(8,128)(2,1)S(1)} %shard_map.59.after.refs_0_, bf16[64,640]{1,0:T(8,128)(2,1)S(1)} %get-tuple-element.58.refs_0_, bf16[64,640]{1,0:T(8,128)(2,1)S(1)} %collective-permute-done.19.refs_4_.refs_1_, ...), custom_call_target="tpu_custom_call" | custom-call | flops 2684354560 | bytes 1048576 | tf_op jit(solution)/shard_map/pallas_call | solution.py:329
  51.3 0.0 collective-permute-done.25.refs_3_
  51.3 0.1 collective-permute-done.24.refs_2_
  51.4 0.0 collective-permute-done.23.refs_1_
  51.4 0.0 collective-permute-done.22.other_cot
  51.4 2.2 %shard_map.62 = (f32[512,512]{1,0:T(8,128)}, bf16[2,128,512]{2,1,0:T(8,128)(2,1)}) custom-call(bf16[512,512]{1,0:T(8,128)(2,1)S(1)} %get-tuple-element.59.act_high, bf16[512,512]{1,0:T(8,128)(2,1)S(1)} %get-tuple-element.60.act_low, bf16[512,512]{1,0:T(8,128)(2,1)S(1)} %get-tuple-element.62.out_high, bf16[512,512]{1,0:T(8,128)(2,1)S(1)} %get-tuple-element.63.out_low, ...), custom_call_target="tpu_custom_call" | custom-call | flops 1342177280 | bytes 1048576 | tf_op jit(solution)/shard_map/pallas_call | solution.py:342
  (7 shorter events, 0.2 us)
Async XLA Ops:
  0.6 2.6 %collective-permute-start = (bf16[512,512]{1,0:T(8,128)(2,1)}, bf16[512,512]{1,0:T(8,128)(2,1)S(1)}, u32[]{:S(2)}, u32[]{:S(2)}) collective-permute-start(bf16[512,512]{1,0:T(8,128)(2,1)} %bitcast.6), channel_id=1, source_target_pairs={{0,8},{8,0},{1,9},{9,1},{2,10},{10,2},{3,11},{11,3},{4,12},{12,4},... | collective-permute-start | bytes 1572872 | tf_op jit(solution)/shard_map/ppermute | solution.py:271
  1.1 2.1 %collective-permute-start.1 = (bf16[2,128,512]{2,1,0:T(8,128)(2,1)}, bf16[2,128,512]{2,1,0:T(8,128)(2,1)S(1)}, u32[]{:S(2)}, u32[]{:S(2)}) collective-permute-start(bf16[2,128,512]{2,1,0:T(8,128)(2,1)} %bitcast.7), channel_id=1, source_target_pairs={{0,8},{8,0},{1,9},{9,1},{2,10},{10,2},{3,11},{11,3},{4,12},{12,4},... | collective-permute-start | bytes 786440 | tf_op jit(solution)/shard_map/ppermute | solution.py:272
  1.2 1.1 %copy-start = (bf16[2,128,512]{2,1,0:T(8,128)(2,1)S(1)}, bf16[2,128,512]{2,1,0:T(8,128)(2,1)}, u32[]{:S(2)}) copy-start(bf16[2,128,512]{2,1,0:T(8,128)(2,1)} %param.5) | copy-start | bytes 786436
  1.2 1.2 %copy-start.1 = (bf16[1,2,128,512]{3,2,1,0:T(8,128)(2,1)S(1)}, bf16[1,2,128,512]{3,2,1,0:T(8,128)(2,1)}, u32[]{:S(2)}) copy-start(bf16[1,2,128,512]{3,2,1,0:T(8,128)(2,1)} %param.3) | copy-start | bytes 786436
  4.2 8.0 %collective-permute-start.2 = (bf16[128,512]{1,0:T(8,128)(2,1)S(1)}, bf16[128,512]{1,0:T(8,128)(2,1)S(1)}, u32[]{:S(2)}, u32[]{:S(2)}) collective-permute-start(bf16[128,512]{1,0:T(8,128)(2,1)S(1)} %get-tuple-element.39.after), channel_id=1, source_target_pairs={{16,0},{17,1},{18,2},{19,3},{20,4},{21,5},{22,6},{23,7},{24,8},{25... | collective-permute-start | bytes 393224 | tf_op jit(solution)/shard_map/ppermute | solution.py:283
  5.9 6.9 %collective-permute-start.4 = (bf16[64,640]{1,0:T(8,128)(2,1)S(1)}, bf16[64,640]{1,0:T(8,128)(2,1)S(1)}, u32[]{:S(2)}, u32[]{:S(2)}) collective-permute-start(bf16[64,640]{1,0:T(8,128)(2,1)S(1)} %get-tuple-element.44), channel_id=1, source_target_pairs={{0,3},{1,2},{2,1},{3,0},{4,7},{5,6},{6,5},{7,4},{8,11},{9,10},{10,... | collective-permute-start | bytes 245768 | tf_op jit(solution)/shard_map/ppermute | solution.py:237
  9.8 4.5 %collective-permute-start.5 = (bf16[64,640]{1,0:T(8,128)(2,1)S(1)}, bf16[64,640]{1,0:T(8,128)(2,1)S(1)}, u32[]{:S(2)}, u32[]{:S(2)}) collective-permute-start(bf16[64,640]{1,0:T(8,128)(2,1)S(1)} %get-tuple-element.45), channel_id=1, source_target_pairs={{0,1},{1,0},{2,3},{3,2},{4,5},{5,4},{6,7},{7,6},{8,9},{9,8},{10,11... | collective-permute-start | bytes 245768 | tf_op jit(solution)/shard_map/ppermute | solution.py:237
  10.4 4.4 %collective-permute-start.6 = (bf16[64,640]{1,0:T(8,128)(2,1)S(1)}, bf16[64,640]{1,0:T(8,128)(2,1)S(1)}, u32[]{:S(2)}, u32[]{:S(2)}) collective-permute-start(bf16[64,640]{1,0:T(8,128)(2,1)S(1)} %get-tuple-element.46), channel_id=1, source_target_pairs={{0,2},{1,3},{2,0},{3,1},{4,6},{5,7},{6,4},{7,5},{8,10},{9,11},{10,... | collective-permute-start | bytes 245768 | tf_op jit(solution)/shard_map/ppermute | solution.py:237
  12.7 4.8 %collective-permute-start.3 = (bf16[128,512]{1,0:T(8,128)(2,1)S(1)}, bf16[128,512]{1,0:T(8,128)(2,1)S(1)}, u32[]{:S(2)}, u32[]{:S(2)}) collective-permute-start(bf16[128,512]{1,0:T(8,128)(2,1)S(1)} %get-tuple-element.42), channel_id=1, source_target_pairs={{0,8},{8,0},{1,9},{9,1},{2,10},{10,2},{3,11},{11,3},{4,12},{12,4},... | collective-permute-start | bytes 393224 | tf_op jit(solution)/shard_map/ppermute | solution.py:306
  14.8 8.2 %collective-permute-start.13 = (bf16[64,640]{1,0:T(8,128)(2,1)S(1)}, bf16[64,640]{1,0:T(8,128)(2,1)S(1)}, u32[]{:S(2)}, u32[]{:S(2)}) collective-permute-start(bf16[64,640]{1,0:T(8,128)(2,1)S(1)} %shard_map.53.after.left), channel_id=1, source_target_pairs={{0,4},{4,0},{1,5},{5,1},{2,6},{6,2},{3,7},{7,3},{8,12},{12,8},{9,1... | collective-permute-start | bytes 245768 | tf_op jit(solution)/shard_map/ppermute | solution.py:245
  18.0 6.3 %collective-permute-start.10 = (bf16[64,640]{1,0:T(8,128)(2,1)S(1)}, bf16[64,640]{1,0:T(8,128)(2,1)S(1)}, u32[]{:S(2)}, u32[]{:S(2)}) collective-permute-start(bf16[64,640]{1,0:T(8,128)(2,1)S(1)} %get-tuple-element.52), channel_id=1, source_target_pairs={{0,3},{1,2},{2,1},{3,0},{4,7},{5,6},{6,5},{7,4},{8,11},{9,10},{10,... | collective-permute-start | bytes 245768 | tf_op jit(solution)/shard_map/ppermute | solution.py:237
  19.5 6.0 %collective-permute-start.11 = (bf16[64,640]{1,0:T(8,128)(2,1)S(1)}, bf16[64,640]{1,0:T(8,128)(2,1)S(1)}, u32[]{:S(2)}, u32[]{:S(2)}) collective-permute-start(bf16[64,640]{1,0:T(8,128)(2,1)S(1)} %get-tuple-element.53), channel_id=1, source_target_pairs={{0,1},{1,0},{2,3},{3,2},{4,5},{5,4},{6,7},{7,6},{8,9},{9,8},{10,11... | collective-permute-start | bytes 245768 | tf_op jit(solution)/shard_map/ppermute | solution.py:237
  20.8 5.3 %collective-permute-start.12 = (bf16[64,640]{1,0:T(8,128)(2,1)S(1)}, bf16[64,640]{1,0:T(8,128)(2,1)S(1)}, u32[]{:S(2)}, u32[]{:S(2)}) collective-permute-start(bf16[64,640]{1,0:T(8,128)(2,1)S(1)} %get-tuple-element.54), channel_id=1, source_target_pairs={{0,2},{1,3},{2,0},{3,1},{4,6},{5,7},{6,4},{7,5},{8,10},{9,11},{10,... | collective-permute-start | bytes 245768 | tf_op jit(solution)/shard_map/ppermute | solution.py:237
  21.6 8.4 %collective-permute-start.7 = (bf16[64,1024]{1,0:T(8,128)(2,1)S(1)}, bf16[64,1024]{1,0:T(8,128)(2,1)S(1)}, u32[]{:S(2)}, u32[]{:S(2)}) collective-permute-start(bf16[64,1024]{1,0:T(8,128)(2,1)S(1)} %get-tuple-element.48), channel_id=1, source_target_pairs={{0,3},{1,2},{2,1},{3,0},{4,7},{5,6},{6,5},{7,4},{8,11},{9,10},{10,... | collective-permute-start | bytes 393224 | tf_op jit(solution)/shard_map/ppermute | solution.py:237
  23.0 7.3 %collective-permute-start.8 = (bf16[64,1024]{1,0:T(8,128)(2,1)S(1)}, bf16[64,1024]{1,0:T(8,128)(2,1)S(1)}, u32[]{:S(2)}, u32[]{:S(2)}) collective-permute-start(bf16[64,1024]{1,0:T(8,128)(2,1)S(1)} %get-tuple-element.49), channel_id=1, source_target_pairs={{0,1},{1,0},{2,3},{3,2},{4,5},{5,4},{6,7},{7,6},{8,9},{9,8},{10,11... | collective-permute-start | bytes 393224 | tf_op jit(solution)/shard_map/ppermute | solution.py:237
  24.3 8.3 %collective-permute-start.9 = (bf16[64,1024]{1,0:T(8,128)(2,1)S(1)}, bf16[64,1024]{1,0:T(8,128)(2,1)S(1)}, u32[]{:S(2)}, u32[]{:S(2)}) collective-permute-start(bf16[64,1024]{1,0:T(8,128)(2,1)S(1)} %get-tuple-element.50), channel_id=1, source_target_pairs={{0,2},{1,3},{2,0},{3,1},{4,6},{5,7},{6,4},{7,5},{8,10},{9,11},{10,... | collective-permute-start | bytes 393224 | tf_op jit(solution)/shard_map/ppermute | solution.py:237
  26.2 7.8 %collective-permute-start.15 = (bf16[64,640]{1,0:T(8,128)(2,1)S(1)}, bf16[64,640]{1,0:T(8,128)(2,1)S(1)}, u32[]{:S(2)}, u32[]{:S(2)}) collective-permute-start(bf16[64,640]{1,0:T(8,128)(2,1)S(1)} %get-tuple-element.57.left), channel_id=1, source_target_pairs={{0,4},{4,0},{1,5},{5,1},{2,6},{6,2},{3,7},{7,3},{8,12},{12,8},{9,1... | collective-permute-start | bytes 245768 | tf_op jit(solution)/shard_map/ppermute | solution.py:245
  32.7 10.6 %collective-permute-start.14 = (bf16[64,1024]{1,0:T(8,128)(2,1)S(1)}, bf16[64,1024]{1,0:T(8,128)(2,1)S(1)}, u32[]{:S(2)}, u32[]{:S(2)}) collective-permute-start(bf16[64,1024]{1,0:T(8,128)(2,1)S(1)} %get-tuple-element.56.left), channel_id=1, source_target_pairs={{0,4},{4,0},{1,5},{5,1},{2,6},{6,2},{3,7},{7,3},{8,12},{12,8},{9,1... | collective-permute-start | bytes 393224 | tf_op jit(solution)/shard_map/ppermute | solution.py:245
  33.0 5.3 %collective-permute-start.19 = (bf16[64,640]{1,0:T(8,128)(2,1)S(1)}, bf16[64,640]{1,0:T(8,128)(2,1)S(1)}, u32[]{:S(2)}, u32[]{:S(2)}) collective-permute-start(bf16[64,640]{1,0:T(8,128)(2,1)S(1)} %get-tuple-element.58.refs_0_), channel_id=1, source_target_pairs={{0,1},{1,0},{2,3},{3,2},{4,5},{5,4},{6,7},{7,6},{8,9},{9,8},{10,11... | collective-permute-start | bytes 245768 | tf_op jit(solution)/shard_map/ppermute | solution.py:237
  34.0 9.2 %collective-permute-start.18 = (bf16[64,640]{1,0:T(8,128)(2,1)S(1)}, bf16[64,640]{1,0:T(8,128)(2,1)S(1)}, u32[]{:S(2)}, u32[]{:S(2)}) collective-permute-start(bf16[64,640]{1,0:T(8,128)(2,1)S(1)} %shard_map.58.refs_0_), channel_id=1, source_target_pairs={{0,3},{1,2},{2,1},{3,0},{4,7},{5,6},{6,5},{7,4},{8,11},{9,10},{10,... | collective-permute-start | bytes 245768 | tf_op jit(solution)/shard_map/ppermute | solution.py:237
  37.0 6.3 %collective-permute-start.17 = (bf16[64,640]{1,0:T(8,128)(2,1)S(1)}, bf16[64,640]{1,0:T(8,128)(2,1)S(1)}, u32[]{:S(2)}, u32[]{:S(2)}) collective-permute-start(bf16[64,640]{1,0:T(8,128)(2,1)S(1)} %shard_map.58.refs_0_), channel_id=1, source_target_pairs={{0,2},{1,3},{2,0},{3,1},{4,6},{5,7},{6,4},{7,5},{8,10},{9,11},{10,... | collective-permute-start | bytes 245768 | tf_op jit(solution)/shard_map/ppermute | solution.py:237
  37.1 6.3 %collective-permute-start.16 = (bf16[64,640]{1,0:T(8,128)(2,1)S(1)}, bf16[64,640]{1,0:T(8,128)(2,1)S(1)}, u32[]{:S(2)}, u32[]{:S(2)}) collective-permute-start(bf16[64,640]{1,0:T(8,128)(2,1)S(1)} %shard_map.58.refs_0_), channel_id=1, source_target_pairs={{0,1},{1,0},{2,3},{3,2},{4,5},{5,4},{6,7},{7,6},{8,9},{9,8},{10,11... | collective-permute-start | bytes 245768 | tf_op jit(solution)/shard_map/ppermute | solution.py:237
  38.4 10.7 %collective-permute-start.21 = (bf16[64,640]{1,0:T(8,128)(2,1)S(1)}, bf16[64,640]{1,0:T(8,128)(2,1)S(1)}, u32[]{:S(2)}, u32[]{:S(2)}) collective-permute-start(bf16[64,640]{1,0:T(8,128)(2,1)S(1)} %get-tuple-element.58.refs_0_), channel_id=1, source_target_pairs={{0,3},{1,2},{2,1},{3,0},{4,7},{5,6},{6,5},{7,4},{8,11},{9,10},{10,... | collective-permute-start | bytes 245768 | tf_op jit(solution)/shard_map/ppermute | solution.py:237
  43.3 5.9 %collective-permute-start.20 = (bf16[64,640]{1,0:T(8,128)(2,1)S(1)}, bf16[64,640]{1,0:T(8,128)(2,1)S(1)}, u32[]{:S(2)}, u32[]{:S(2)}) collective-permute-start(bf16[64,640]{1,0:T(8,128)(2,1)S(1)} %get-tuple-element.58.refs_0_), channel_id=1, source_target_pairs={{0,2},{1,3},{2,0},{3,1},{4,6},{5,7},{6,4},{7,5},{8,10},{9,11},{10,... | collective-permute-start | bytes 245768 | tf_op jit(solution)/shard_map/ppermute | solution.py:237
  43.4 8.0 %collective-permute-start.25 = (bf16[64,1024]{1,0:T(8,128)(2,1)S(1)}, bf16[64,1024]{1,0:T(8,128)(2,1)S(1)}, u32[]{:S(2)}, u32[]{:S(2)}) collective-permute-start(bf16[64,1024]{1,0:T(8,128)(2,1)S(1)} %shard_map.59.after.refs_0_), channel_id=1, source_target_pairs={{0,3},{1,2},{2,1},{3,0},{4,7},{5,6},{6,5},{7,4},{8,11},{9,10},{10,... | collective-permute-start | bytes 393224 | tf_op jit(solution)/shard_map/ppermute | solution.py:237
  44.7 6.7 %collective-permute-start.24 = (bf16[64,1024]{1,0:T(8,128)(2,1)S(1)}, bf16[64,1024]{1,0:T(8,128)(2,1)S(1)}, u32[]{:S(2)}, u32[]{:S(2)}) collective-permute-start(bf16[64,1024]{1,0:T(8,128)(2,1)S(1)} %shard_map.59.after.refs_0_), channel_id=1, source_target_pairs={{0,2},{1,3},{2,0},{3,1},{4,6},{5,7},{6,4},{7,5},{8,10},{9,11},{10,... | collective-permute-start | bytes 393224 | tf_op jit(solution)/shard_map/ppermute | solution.py:237
  45.5 5.9 %collective-permute-start.23 = (bf16[64,1024]{1,0:T(8,128)(2,1)S(1)}, bf16[64,1024]{1,0:T(8,128)(2,1)S(1)}, u32[]{:S(2)}, u32[]{:S(2)}) collective-permute-start(bf16[64,1024]{1,0:T(8,128)(2,1)S(1)} %shard_map.59.after.refs_0_), channel_id=1, source_target_pairs={{0,1},{1,0},{2,3},{3,2},{4,5},{5,4},{6,7},{7,6},{8,9},{9,8},{10,11... | collective-permute-start | bytes 393224 | tf_op jit(solution)/shard_map/ppermute | solution.py:237
  49.1 2.4 %collective-permute-start.22 = (bf16[128,512]{1,0:T(8,128)(2,1)S(1)}, bf16[128,512]{1,0:T(8,128)(2,1)S(1)}, u32[]{:S(2)}, u32[]{:S(2)}) collective-permute-start(bf16[128,512]{1,0:T(8,128)(2,1)S(1)} %get-tuple-element.65), channel_id=1, source_target_pairs={{0,8},{8,0},{1,9},{9,1},{2,10},{10,2},{3,11},{11,3},{4,12},{12,4},... | collective-permute-start | bytes 393224 | tf_op jit(solution)/shard_map/ppermute | solution.py:341

commit v17 on v16

--- a/solution.py
+++ b/solution.py
@@ -48,11 +48,6 @@
 
 def group_place():
     return 2 * lax.axis_index("near") + lax.axis_index("side")
-
-
-def split(value):
-    high = value.astype(BF16)
-    return high, (value - high.astype(F32)).astype(BF16)
 
 
 def dot(left, right):
@@ -176,17 +171,17 @@
     last = 2.0 * (eye - second) + dot(second, second)
     tail = 2.0 * last - dot(second, last)
     inner = dot(total[...], tail) * (scale * (1.0 / count))
-    return split(((2.0 - ridge * scale) * tail - inner) * scale)
+    return (((2.0 - ridge * scale) * tail - inner) * scale).astype(BF16)
 
 
 def through_kernel(count, through, after, *refs):
-    through_copy = refs[GROUP + 2]
+    through_copy = refs[GROUP + 1]
     through_copy[...] = through[...]
-    inverse_kernel(count, after, *refs[:GROUP + 2], *refs[GROUP + 3:])
+    inverse_kernel(count, after, *refs[:GROUP + 1], *refs[GROUP + 2:])
 
 
 def inverse_kernel(count, after, *refs):
-    pieces, (high, low, blocks, total) = refs[:GROUP], refs[GROUP:]
+    pieces, (result, blocks, total) = refs[:GROUP], refs[GROUP:]
     for step, piece in enumerate(pieces):
         blocks[group_place() ^ step] = piece[...]
     size = total.shape[0] // GROUP
@@ -203,11 +198,10 @@
         both(u, (u + 1) % GROUP, main[:, size:])
     for u in range(2):
         both(u, u + 2, jnp.concatenate([blocks[u, :, 4 * size:], blocks[u + 2, :, 4 * size:]]))
-    for result, term in zip((high, low), invert(total, count)):
-        result[...] = term
-
-
-def update_kernel(act_high, act_low, out_high, out_low, own_cot, other_cot, *refs):
+    result[...] = invert(total, count)
+
+
+def update_kernel(act_inv, out_inv, own_cot, other_cot, *refs):
     pieces, (result, cot, grad, update, done) = refs[:GROUP], refs[GROUP:]
     copies = [
         pltpu.make_async_copy(own_cot, cot.at[lax.axis_index("core")], done.at[0]),
@@ -221,10 +215,10 @@
         start = pl.multiple_of((group_place() ^ step) * 2 * half, 2 * half)
         grad[pl.ds(start, half)] = piece[:, :width]
         grad[pl.ds(start + half, half)] = piece[:, width:]
-    left = (dot(act_high[...], grad[...]) + dot(act_low[...], grad[...])).astype(BF16)
+    left = dot(act_inv[...], grad[...]).astype(BF16)
     for part in range(2):
         rows = slice(part * width // 2, (part + 1) * width // 2)
-        update[rows] = dot(left[rows], out_high[...]) + dot(left[rows], out_low[...])
+        update[rows] = dot(left[rows], out_inv[...])
         copies.append(pltpu.make_async_copy(update.at[rows], result.at[rows], done.at[2 + part]))
         copies[-1].start()
     for copy in copies:
@@ -329,28 +323,28 @@
         return call(
             functools.partial(through_kernel if through else inverse_kernel, count),
             20 * width**3,
-            [array(width, width)] * 2 + [array(*value.shape) for value in through],
+            [array(width, width)] + [array(*value.shape) for value in through],
             [VMEM] * len(through) + [ANY] + [VMEM] * GROUP,
             [pltpu.VMEM((GROUP, size // 2, factor), BF16), pltpu.VMEM((width, width), BF16)],
         )(*through, after, *pieces)
 
     total = exchange(total, (*out, act[1]))
     grad = send([total] * GROUP)
-    *out_inv, give_cot = inverse(out, total, give_cot)
-    act_inv = inverse(act, total)
+    out_inv, give_cot = inverse(out, total, give_cot)
+    (act_inv,) = inverse(act, total)
     other_cot = lax.ppermute(give_cot, "core", SWAP)
     update, cot = call(
         update_kernel,
         10 * width**3,
         [array(width, width, dtype=F32), array(micro, rows, width)],
-        [VMEM] * (6 + GROUP),
+        [VMEM] * (4 + GROUP),
         [
             pltpu.VMEM((width, width), BF16),
             pltpu.VMEM((width, width), F32),
             pltpu.SemaphoreType.DMA((4,)),
         ],
         HBM,
-    )(*act_inv, *out_inv, own_cot, other_cot, *grad)
+    )(act_inv, out_inv, own_cot, other_cot, *grad)
     return (cot[None], update[None])
 
 

time: 53.8 us -> 53.2 us (0.989)
  Pallas kernels: 9.03 us -> 8.26 us
    pallas_call x1, Pallas kernels: 2.17 us -> 1.63 us  [body(): call(update_kernel, 10 * width ** 3, [array(width, width, dtype=F32), arr...]
where the time goes in v17:
time: 53.2 us; the launch traced here: 53.1 us
  starting transfers between devices  31.7 us (60%)
  waiting for transfers between devices  11.1 us (21%)
  Pallas kernels  8.26 us (16%)
  other arithmetic  1.18 us (2%)
  between operations  0.8 us (2%)
    ppermute x18, starting transfers between devices, send(): lax.ppermute(parts[step], ('near', 'side'), [(i, i ^ step) for i in range...  25.4 us
    ppermute x18, waiting for transfers between devices, send(): lax.ppermute(parts[step], ('near', 'side'), [(i, i ^ step) for i in range...  8.53 us
    ppermute x3, starting transfers between devices, exchange(): got = lax.ppermute(value, 'far', route)  4.27 us
    pallas_call x2, Pallas kernels, inverse(): call(functools.partial(through_kernel if through else inverse_kernel, cou...  4.05 us
    ppermute x1, waiting for transfers between devices, body(): upstream = lax.ppermute(down, 'row', [(r, r - 1) for r in range(1, pairs)])  1.69 us
    pallas_call x1, Pallas kernels, body(): call(update_kernel, 10 * width ** 3, [array(width, width, dtype=F32), arr...  1.63 us
    ppermute x1, starting transfers between devices, body(): upstream = lax.ppermute(down, 'row', [(r, r - 1) for r in range(1, pairs)])  1.29 us
    select_n x2, other arithmetic, near_copy(): return jnp.where(core > 1, jnp.zeros_like(value), value)  1.18 us
  transfers between devices with their start and end apart: 26, of which 10 were waited for; matrix products, arithmetic and copies ran while one was open for 2% of the time, Pallas kernels for 11%

profile of v17, /device:TPU:0, one launch (start us, length us, event | category | flops | bytes accessed | tf_op | source)
XLA Modules:
  0.0 53.1 jit_solution(1691492279694826901)
XLA Ops:
  0.6 0.5 collective-permute-start
  1.1 0.1 collective-permute-start.1
  1.2 0.0 copy-start
  1.2 1.1 %broadcast_select_fusion.weight = bf16[512,512]{1,0:T(8,128)(2,1)S(1)} fusion(pred[]{:T(512)S(6)} %gt.2, bf16[1,512,512]{2,1,0:T(8,128)(2,1)} %param.4), kind=kLoop, calls=%fused_computation | loop fusion | flops 262144 | bytes 1048577 | tf_op jit(solution)/shard_map/jit(_where)/select_n | solution.py:263
  2.4 0.0 copy-done
  2.4 0.0 copy-done.1
  2.5 0.8 %collective-permute-done.1.partner_local = bf16[2,128,512]{2,1,0:T(8,128)(2,1)S(1)} collective-permute-done((bf16[2,128,512]{2,1,0:T(8,128)(2,1)}, bf16[2,128,512]{2,1,0:T(8,128)(2,1)S(1)}, u32[]{:S(2)}, u32[]{:S(2)}) %collective-permute-start.1) | collective-permute-done | bytes 262176 | tf_op jit(solution)/shard_map/ppermute | solution.py:266
  3.3 0.0 collective-permute-done.partner
  3.3 0.9 %shard_map.50 = (bf16[512,512]{1,0:T(8,128)(2,1)S(1)}, bf16[2,128,512]{2,1,0:T(8,128)(2,1)S(1)}, bf16[128,512]{1,0:T(8,128)(2,1)S(1)}, f32[128,512]{1,0:T(8,128)...) custom-call(bf16[512,512]{1,0:T(8,128)(2,1)S(1)} %broadcast_select_fusion.weight, ...), custom_call_target="tpu_custom_call" | custom-call | flops 268435456 | bytes 1048576 | tf_op jit(solution)/shard_map/pallas_call | solution.py:269
  4.2 1.3 %collective-permute-start.2 = (bf16[128,512]{1,0:T(8,128)(2,1)S(1)}, bf16[128,512]{1,0:T(8,128)(2,1)S(1)}, u32[]{:S(2)}, u32[]{:S(2)}) collective-permute-start(bf16[128,512]{1,0:T(8,128)(2,1)S(1)} %get-tuple-element.36.after), channel_id=1, source_target_pairs={{16,0},{17,1},{18,2},{19,3},{20,4},{21,5},{22,6},{23,7},{24,8},{25... | collective-permute-start | bytes 393224 | tf_op jit(solution)/shard_map/ppermute | solution.py:277
  5.5 0.4 shard_map.52
  5.9 4.0 %collective-permute-start.4 = (bf16[64,640]{1,0:T(8,128)(2,1)S(1)}, bf16[64,640]{1,0:T(8,128)(2,1)S(1)}, u32[]{:S(2)}, u32[]{:S(2)}) collective-permute-start(bf16[64,640]{1,0:T(8,128)(2,1)S(1)} %get-tuple-element.41), channel_id=1, source_target_pairs={{0,3},{1,2},{2,1},{3,0},{4,7},{5,6},{6,5},{7,4},{8,11},{9,10},{10,... | collective-permute-start | bytes 245768 | tf_op jit(solution)/shard_map/ppermute | solution.py:231
  9.8 0.5 %collective-permute-start.5 = (bf16[64,640]{1,0:T(8,128)(2,1)S(1)}, bf16[64,640]{1,0:T(8,128)(2,1)S(1)}, u32[]{:S(2)}, u32[]{:S(2)}) collective-permute-start(bf16[64,640]{1,0:T(8,128)(2,1)S(1)} %get-tuple-element.42), channel_id=1, source_target_pairs={{0,1},{1,0},{2,3},{3,2},{4,5},{5,4},{6,7},{7,6},{8,9},{9,8},{10,11... | collective-permute-start | bytes 245768 | tf_op jit(solution)/shard_map/ppermute | solution.py:231
  10.4 0.1 collective-permute-start.6
  10.5 1.7 %collective-permute-done.2.arrived = bf16[128,512]{1,0:T(8,128)(2,1)S(1)} collective-permute-done((bf16[128,512]{1,0:T(8,128)(2,1)S(1)}, bf16[128,512]{1,0:T(8,128)(2,1)S(1)}, u32[]{:S(2)}, u32[]{:S(2)}) %collective-permute-start.2) | collective-permute-done | bytes 131104 | tf_op jit(solution)/shard_map/ppermute | solution.py:277
  12.2 0.5 %shard_map.51 = (bf16[128,512]{1,0:T(8,128)(2,1)S(1)}, bf16[128,512]{1,0:T(8,128)(2,1)S(1)}, bf16[128,512]{1,0:T(8,128)(2,1)S(1)}, bf16[128,512]{1,0:T(8,128)(2,1)S(1)}) custom-call(bf16[512,512]{1,0:T(8,128)(2,1)S(1)} %get-tuple-element.33.own, bf16[512,512]{1,0:T(8,128)(2,1)S(1)} %collective-permute-done.partner, ...), custom_call_target="tpu_custom_call" | custom-call | flops 2147483648 | bytes 1048576 | tf_op jit(solution)/shard_map/pallas_call | solution.py:294
  12.7 0.1 collective-permute-start.3
  12.8 0.0 collective-permute-done.4.refs_1_
  12.8 1.5 %collective-permute-done.5.refs_2_ = bf16[64,640]{1,0:T(8,128)(2,1)S(1)} collective-permute-done((bf16[64,640]{1,0:T(8,128)(2,1)S(1)}, bf16[64,640]{1,0:T(8,128)(2,1)S(1)}, u32[]{:S(2)}, u32[]{:S(2)}) %collective-permute-start.5) | collective-permute-done | bytes 81952 | tf_op jit(solution)/shard_map/ppermute | solution.py:231
  14.3 0.5 collective-permute-done.6.refs_3_
  14.8 2.7 %collective-permute-start.13 = (bf16[64,640]{1,0:T(8,128)(2,1)S(1)}, bf16[64,640]{1,0:T(8,128)(2,1)S(1)}, u32[]{:S(2)}, u32[]{:S(2)}) collective-permute-start(bf16[64,640]{1,0:T(8,128)(2,1)S(1)} %shard_map.53.after.left), channel_id=1, source_target_pairs={{0,4},{4,0},{1,5},{5,1},{2,6},{6,2},{3,7},{7,3},{8,12},{12,8},{9,1... | collective-permute-start | bytes 245768 | tf_op jit(solution)/shard_map/ppermute | solution.py:239
  17.5 0.0 collective-permute-done.3.dh_got
  17.5 0.5 %shard_map.54 = (bf16[64,640]{1,0:T(8,128)(2,1)S(1)}, bf16[64,640]{1,0:T(8,128)(2,1)S(1)}, bf16[64,640]{1,0:T(8,128)(2,1)S(1)}, bf16[64,640]{1,0:T(8,128)(2,1)S(...) custom-call(bf16[2,128,512]{2,1,0:T(8,128)(2,1)S(1)} %get-tuple-elem, ...), custom_call_target="tpu_custom_call" | custom-call | flops 268435456 | bytes 1048576 | tf_op jit(solution)/shard_map/pallas_call | solution.py:302
  18.0 1.5 %collective-permute-start.10 = (bf16[64,640]{1,0:T(8,128)(2,1)S(1)}, bf16[64,640]{1,0:T(8,128)(2,1)S(1)}, u32[]{:S(2)}, u32[]{:S(2)}) collective-permute-start(bf16[64,640]{1,0:T(8,128)(2,1)S(1)} %get-tuple-element.49), channel_id=1, source_target_pairs={{0,3},{1,2},{2,1},{3,0},{4,7},{5,6},{6,5},{7,4},{8,11},{9,10},{10,... | collective-permute-start | bytes 245768 | tf_op jit(solution)/shard_map/ppermute | solution.py:231
  19.5 1.3 %collective-permute-start.11 = (bf16[64,640]{1,0:T(8,128)(2,1)S(1)}, bf16[64,640]{1,0:T(8,128)(2,1)S(1)}, u32[]{:S(2)}, u32[]{:S(2)}) collective-permute-start(bf16[64,640]{1,0:T(8,128)(2,1)S(1)} %get-tuple-element.50), channel_id=1, source_target_pairs={{0,1},{1,0},{2,3},{3,2},{4,5},{5,4},{6,7},{7,6},{8,9},{9,8},{10,11... | collective-permute-start | bytes 245768 | tf_op jit(solution)/shard_map/ppermute | solution.py:231
  20.8 0.8 %collective-permute-start.12 = (bf16[64,640]{1,0:T(8,128)(2,1)S(1)}, bf16[64,640]{1,0:T(8,128)(2,1)S(1)}, u32[]{:S(2)}, u32[]{:S(2)}) collective-permute-start(bf16[64,640]{1,0:T(8,128)(2,1)S(1)} %get-tuple-element.51), channel_id=1, source_target_pairs={{0,2},{1,3},{2,0},{3,1},{4,6},{5,7},{6,4},{7,5},{8,10},{9,11},{10,... | collective-permute-start | bytes 245768 | tf_op jit(solution)/shard_map/ppermute | solution.py:231
  21.6 1.4 %collective-permute-start.7 = (bf16[64,1024]{1,0:T(8,128)(2,1)S(1)}, bf16[64,1024]{1,0:T(8,128)(2,1)S(1)}, u32[]{:S(2)}, u32[]{:S(2)}) collective-permute-start(bf16[64,1024]{1,0:T(8,128)(2,1)S(1)} %get-tuple-element.45), channel_id=1, source_target_pairs={{0,3},{1,2},{2,1},{3,0},{4,7},{5,6},{6,5},{7,4},{8,11},{9,10},{10,... | collective-permute-start | bytes 393224 | tf_op jit(solution)/shard_map/ppermute | solution.py:231
  23.0 0.0 collective-permute-done.13.right
  23.0 1.3 %collective-permute-start.8 = (bf16[64,1024]{1,0:T(8,128)(2,1)S(1)}, bf16[64,1024]{1,0:T(8,128)(2,1)S(1)}, u32[]{:S(2)}, u32[]{:S(2)}) collective-permute-start(bf16[64,1024]{1,0:T(8,128)(2,1)S(1)} %get-tuple-element.46), channel_id=1, source_target_pairs={{0,1},{1,0},{2,3},{3,2},{4,5},{5,4},{6,7},{7,6},{8,9},{9,8},{10,11... | collective-permute-start | bytes 393224 | tf_op jit(solution)/shard_map/ppermute | solution.py:231
  24.3 0.0 collective-permute-done.10.refs_1_
  24.3 1.2 %collective-permute-start.9 = (bf16[64,1024]{1,0:T(8,128)(2,1)S(1)}, bf16[64,1024]{1,0:T(8,128)(2,1)S(1)}, u32[]{:S(2)}, u32[]{:S(2)}) collective-permute-start(bf16[64,1024]{1,0:T(8,128)(2,1)S(1)} %get-tuple-element.47), channel_id=1, source_target_pairs={{0,2},{1,3},{2,0},{3,1},{4,6},{5,7},{6,4},{7,5},{8,10},{9,11},{10,... | collective-permute-start | bytes 393224 | tf_op jit(solution)/shard_map/ppermute | solution.py:231
  25.5 0.0 collective-permute-done.11.refs_2_
  25.5 0.6 %collective-permute-done.12.refs_3_ = bf16[64,640]{1,0:T(8,128)(2,1)S(1)} collective-permute-done((bf16[64,640]{1,0:T(8,128)(2,1)S(1)}, bf16[64,640]{1,0:T(8,128)(2,1)S(1)}, u32[]{:S(2)}, u32[]{:S(2)}) %collective-permute-start.12) | collective-permute-done | bytes 81952 | tf_op jit(solution)/shard_map/ppermute | solution.py:231
  26.2 1.2 %collective-permute-start.15 = (bf16[64,640]{1,0:T(8,128)(2,1)S(1)}, bf16[64,640]{1,0:T(8,128)(2,1)S(1)}, u32[]{:S(2)}, u32[]{:S(2)}) collective-permute-start(bf16[64,640]{1,0:T(8,128)(2,1)S(1)} %get-tuple-element.54.left), channel_id=1, source_target_pairs={{0,4},{4,0},{1,5},{5,1},{2,6},{6,2},{3,7},{7,3},{8,12},{12,8},{9,1... | collective-permute-start | bytes 245768 | tf_op jit(solution)/shard_map/ppermute | solution.py:239
  27.5 2.6 %collective-permute-done.7.refs_1_ = bf16[64,1024]{1,0:T(8,128)(2,1)S(1)} collective-permute-done((bf16[64,1024]{1,0:T(8,128)(2,1)S(1)}, bf16[64,1024]{1,0:T(8,128)(2,1)S(1)}, u32[]{:S(2)}, u32[]{:S(2)}) %collective-permute-start.7) | collective-permute-done | bytes 131104 | tf_op jit(solution)/shard_map/ppermute | solution.py:231
  30.0 0.2 collective-permute-done.8.refs_2_
  30.3 2.3 %collective-permute-done.9.refs_3_ = bf16[64,1024]{1,0:T(8,128)(2,1)S(1)} collective-permute-done((bf16[64,1024]{1,0:T(8,128)(2,1)S(1)}, bf16[64,1024]{1,0:T(8,128)(2,1)S(1)}, u32[]{:S(2)}, u32[]{:S(2)}) %collective-permute-start.9) | collective-permute-done | bytes 131104 | tf_op jit(solution)/shard_map/ppermute | solution.py:231
  32.6 0.1 shard_map.57
  32.7 0.4 collective-permute-start.14
  33.0 1.0 %collective-permute-start.19 = (bf16[64,640]{1,0:T(8,128)(2,1)S(1)}, bf16[64,640]{1,0:T(8,128)(2,1)S(1)}, u32[]{:S(2)}, u32[]{:S(2)}) collective-permute-start(bf16[64,640]{1,0:T(8,128)(2,1)S(1)} %get-tuple-element.55.refs_0_), channel_id=1, source_target_pairs={{0,1},{1,0},{2,3},{3,2},{4,5},{5,4},{6,7},{7,6},{8,9},{9,8},{10,11... | collective-permute-start | bytes 245768 | tf_op jit(solution)/shard_map/ppermute | solution.py:231
  34.0 0.0 collective-permute-done.15.right
  34.0 3.0 %collective-permute-start.18 = (bf16[64,640]{1,0:T(8,128)(2,1)S(1)}, bf16[64,640]{1,0:T(8,128)(2,1)S(1)}, u32[]{:S(2)}, u32[]{:S(2)}) collective-permute-start(bf16[64,640]{1,0:T(8,128)(2,1)S(1)} %shard_map.58.refs_0_), channel_id=1, source_target_pairs={{0,3},{1,2},{2,1},{3,0},{4,7},{5,6},{6,5},{7,4},{8,11},{9,10},{10,... | collective-permute-start | bytes 245768 | tf_op jit(solution)/shard_map/ppermute | solution.py:231
  37.0 0.0 collective-permute-start.17
  37.1 1.0 %collective-permute-start.16 = (bf16[64,640]{1,0:T(8,128)(2,1)S(1)}, bf16[64,640]{1,0:T(8,128)(2,1)S(1)}, u32[]{:S(2)}, u32[]{:S(2)}) collective-permute-start(bf16[64,640]{1,0:T(8,128)(2,1)S(1)} %shard_map.58.refs_0_), channel_id=1, source_target_pairs={{0,1},{1,0},{2,3},{3,2},{4,5},{5,4},{6,7},{7,6},{8,9},{9,8},{10,11... | collective-permute-start | bytes 245768 | tf_op jit(solution)/shard_map/ppermute | solution.py:231
  38.0 0.4 collective-permute-done.19.refs_4_.refs_1_
  38.4 4.9 %collective-permute-start.21 = (bf16[64,640]{1,0:T(8,128)(2,1)S(1)}, bf16[64,640]{1,0:T(8,128)(2,1)S(1)}, u32[]{:S(2)}, u32[]{:S(2)}) collective-permute-start(bf16[64,640]{1,0:T(8,128)(2,1)S(1)} %get-tuple-element.55.refs_0_), channel_id=1, source_target_pairs={{0,3},{1,2},{2,1},{3,0},{4,7},{5,6},{6,5},{7,4},{8,11},{9,10},{10,... | collective-permute-start | bytes 245768 | tf_op jit(solution)/shard_map/ppermute | solution.py:231
  43.3 0.0 collective-permute-done.18.refs_3_
  43.3 0.0 collective-permute-start.20
  43.3 0.0 collective-permute-done.17.refs_2_
  43.3 0.0 collective-permute-done.16.refs_1_
  43.3 0.0 collective-permute-done.14.right
  43.4 1.3 %collective-permute-start.25 = (bf16[64,1024]{1,0:T(8,128)(2,1)S(1)}, bf16[64,1024]{1,0:T(8,128)(2,1)S(1)}, u32[]{:S(2)}, u32[]{:S(2)}) collective-permute-start(bf16[64,1024]{1,0:T(8,128)(2,1)S(1)} %shard_map.59.after.refs_0_), channel_id=1, source_target_pairs={{0,3},{1,2},{2,1},{3,0},{4,7},{5,6},{6,5},{7,4},{8,11},{9,10},{10,... | collective-permute-start | bytes 393224 | tf_op jit(solution)/shard_map/ppermute | solution.py:231
  44.7 0.8 %collective-permute-start.24 = (bf16[64,1024]{1,0:T(8,128)(2,1)S(1)}, bf16[64,1024]{1,0:T(8,128)(2,1)S(1)}, u32[]{:S(2)}, u32[]{:S(2)}) collective-permute-start(bf16[64,1024]{1,0:T(8,128)(2,1)S(1)} %shard_map.59.after.refs_0_), channel_id=1, source_target_pairs={{0,2},{1,3},{2,0},{3,1},{4,6},{5,7},{6,4},{7,5},{8,10},{9,11},{10,... | collective-permute-start | bytes 393224 | tf_op jit(solution)/shard_map/ppermute | solution.py:231
  45.5 1.4 %collective-permute-start.23 = (bf16[64,1024]{1,0:T(8,128)(2,1)S(1)}, bf16[64,1024]{1,0:T(8,128)(2,1)S(1)}, u32[]{:S(2)}, u32[]{:S(2)}) collective-permute-start(bf16[64,1024]{1,0:T(8,128)(2,1)S(1)} %shard_map.59.after.refs_0_), channel_id=1, source_target_pairs={{0,1},{1,0},{2,3},{3,2},{4,5},{5,4},{6,7},{7,6},{8,9},{9,8},{10,11... | collective-permute-start | bytes 393224 | tf_op jit(solution)/shard_map/ppermute | solution.py:231
  46.9 2.0 %shard_map.61 = (bf16[512,512]{1,0:T(8,128)(2,1)S(1)}, bf16[128,512]{1,0:T(8,128)(2,1)S(1)}) custom-call(bf16[128,512]{1,0:T(8,128)(2,1)S(1)} %get-tuple-element.56.through, bf16[64,1024]{1,0:T(8,128)(2,1)S(1)} %shard_map.59.after.refs_0_, bf16[64,640]{1,0:T(8,128)(2,1)S(1)} %shard_map.58.refs_0_, bf16[64,640]{1,0:T(8,128)(2,1)S(1)} %collective-permute-done.16.refs_1_, ...), custom_call_target="tpu_custom_call" | custom-call | flops 2684354560 | bytes 1048576 | tf_op jit(solution)/shard_map/pallas_call | solution.py:323
  48.9 0.0 collective-permute-done.21.refs_3_
  49.0 0.1 collective-permute-start.22
  49.0 0.0 collective-permute-done.20.refs_2_
  49.0 2.0 %shard_map.60.act_inv = bf16[512,512]{1,0:T(8,128)(2,1)S(1)} custom-call(bf16[64,1024]{1,0:T(8,128)(2,1)S(1)} %shard_map.59.after.refs_0_, bf16[64,640]{1,0:T(8,128)(2,1)S(1)} %get-tuple-element.55.refs_0_, bf16[64,640]{1,0:T(8,128)(2,1)S(1)} %collective-permute-done.19.refs_4_.refs_1_, bf16[64,640]{1,0:T(8,128)(2,1)S(1)} %collective-permute-done.20.refs_2_, ...), custom_call_target="tpu_custom_call" | custom-call | flops 2684354560 | bytes 1048576 | tf_op jit(solution)/shard_map/pallas_call | solution.py:323
  51.1 0.0 collective-permute-done.25.refs_3_
  51.1 0.4 collective-permute-done.24.refs_2_
  51.4 0.0 collective-permute-done.23.refs_1_
  51.4 0.0 collective-permute-done.22.other_cot
  51.4 1.6 %shard_map.62 = (f32[512,512]{1,0:T(8,128)}, bf16[2,128,512]{2,1,0:T(8,128)(2,1)}) custom-call(bf16[512,512]{1,0:T(8,128)(2,1)S(1)} %shard_map.60.act_inv, bf16[512,512]{1,0:T(8,128)(2,1)S(1)} %get-tuple-element.57.out_inv, bf16[128,512]{1,0:T(8,128)(2,1)S(1)} %get-tuple-element.58.own_cot, bf16[128,512]{1,0:T(8,128)(2,1)S(1)} %collective-permute-done.22.other_cot, ...), custom_call_target="tpu_custom_call" | custom-call | flops 1342177280 | bytes 1048576 | tf_op jit(solution)/shard_map/pallas_call | solution.py:336
  (7 shorter events, 0.2 us)
Async XLA Ops:
  0.6 2.6 %collective-permute-start = (bf16[512,512]{1,0:T(8,128)(2,1)}, bf16[512,512]{1,0:T(8,128)(2,1)S(1)}, u32[]{:S(2)}, u32[]{:S(2)}) collective-permute-start(bf16[512,512]{1,0:T(8,128)(2,1)} %bitcast.6), channel_id=1, source_target_pairs={{0,8},{8,0},{1,9},{9,1},{2,10},{10,2},{3,11},{11,3},{4,12},{12,4},... | collective-permute-start | bytes 1572872 | tf_op jit(solution)/shard_map/ppermute | solution.py:265
  1.1 2.1 %collective-permute-start.1 = (bf16[2,128,512]{2,1,0:T(8,128)(2,1)}, bf16[2,128,512]{2,1,0:T(8,128)(2,1)S(1)}, u32[]{:S(2)}, u32[]{:S(2)}) collective-permute-start(bf16[2,128,512]{2,1,0:T(8,128)(2,1)} %bitcast.7), channel_id=1, source_target_pairs={{0,8},{8,0},{1,9},{9,1},{2,10},{10,2},{3,11},{11,3},{4,12},{12,4},... | collective-permute-start | bytes 786440 | tf_op jit(solution)/shard_map/ppermute | solution.py:266
  1.2 1.1 %copy-start = (bf16[2,128,512]{2,1,0:T(8,128)(2,1)S(1)}, bf16[2,128,512]{2,1,0:T(8,128)(2,1)}, u32[]{:S(2)}) copy-start(bf16[2,128,512]{2,1,0:T(8,128)(2,1)} %param.5) | copy-start | bytes 786436
  1.2 1.2 %copy-start.1 = (bf16[1,2,128,512]{3,2,1,0:T(8,128)(2,1)S(1)}, bf16[1,2,128,512]{3,2,1,0:T(8,128)(2,1)}, u32[]{:S(2)}) copy-start(bf16[1,2,128,512]{3,2,1,0:T(8,128)(2,1)} %param.3) | copy-start | bytes 786436
  4.2 8.0 %collective-permute-start.2 = (bf16[128,512]{1,0:T(8,128)(2,1)S(1)}, bf16[128,512]{1,0:T(8,128)(2,1)S(1)}, u32[]{:S(2)}, u32[]{:S(2)}) collective-permute-start(bf16[128,512]{1,0:T(8,128)(2,1)S(1)} %get-tuple-element.36.after), channel_id=1, source_target_pairs={{16,0},{17,1},{18,2},{19,3},{20,4},{21,5},{22,6},{23,7},{24,8},{25... | collective-permute-start | bytes 393224 | tf_op jit(solution)/shard_map/ppermute | solution.py:277
  5.9 6.9 %collective-permute-start.4 = (bf16[64,640]{1,0:T(8,128)(2,1)S(1)}, bf16[64,640]{1,0:T(8,128)(2,1)S(1)}, u32[]{:S(2)}, u32[]{:S(2)}) collective-permute-start(bf16[64,640]{1,0:T(8,128)(2,1)S(1)} %get-tuple-element.41), channel_id=1, source_target_pairs={{0,3},{1,2},{2,1},{3,0},{4,7},{5,6},{6,5},{7,4},{8,11},{9,10},{10,... | collective-permute-start | bytes 245768 | tf_op jit(solution)/shard_map/ppermute | solution.py:231
  9.8 4.5 %collective-permute-start.5 = (bf16[64,640]{1,0:T(8,128)(2,1)S(1)}, bf16[64,640]{1,0:T(8,128)(2,1)S(1)}, u32[]{:S(2)}, u32[]{:S(2)}) collective-permute-start(bf16[64,640]{1,0:T(8,128)(2,1)S(1)} %get-tuple-element.42), channel_id=1, source_target_pairs={{0,1},{1,0},{2,3},{3,2},{4,5},{5,4},{6,7},{7,6},{8,9},{9,8},{10,11... | collective-permute-start | bytes 245768 | tf_op jit(solution)/shard_map/ppermute | solution.py:231
  10.4 4.4 %collective-permute-start.6 = (bf16[64,640]{1,0:T(8,128)(2,1)S(1)}, bf16[64,640]{1,0:T(8,128)(2,1)S(1)}, u32[]{:S(2)}, u32[]{:S(2)}) collective-permute-start(bf16[64,640]{1,0:T(8,128)(2,1)S(1)} %get-tuple-element.43), channel_id=1, source_target_pairs={{0,2},{1,3},{2,0},{3,1},{4,6},{5,7},{6,4},{7,5},{8,10},{9,11},{10,... | collective-permute-start | bytes 245768 | tf_op jit(solution)/shard_map/ppermute | solution.py:231
  12.7 4.8 %collective-permute-start.3 = (bf16[128,512]{1,0:T(8,128)(2,1)S(1)}, bf16[128,512]{1,0:T(8,128)(2,1)S(1)}, u32[]{:S(2)}, u32[]{:S(2)}) collective-permute-start(bf16[128,512]{1,0:T(8,128)(2,1)S(1)} %get-tuple-element.39), channel_id=1, source_target_pairs={{0,8},{8,0},{1,9},{9,1},{2,10},{10,2},{3,11},{11,3},{4,12},{12,4},... | collective-permute-start | bytes 393224 | tf_op jit(solution)/shard_map/ppermute | solution.py:300
  14.8 8.2 %collective-permute-start.13 = (bf16[64,640]{1,0:T(8,128)(2,1)S(1)}, bf16[64,640]{1,0:T(8,128)(2,1)S(1)}, u32[]{:S(2)}, u32[]{:S(2)}) collective-permute-start(bf16[64,640]{1,0:T(8,128)(2,1)S(1)} %shard_map.53.after.left), channel_id=1, source_target_pairs={{0,4},{4,0},{1,5},{5,1},{2,6},{6,2},{3,7},{7,3},{8,12},{12,8},{9,1... | collective-permute-start | bytes 245768 | tf_op jit(solution)/shard_map/ppermute | solution.py:239
  18.0 6.3 %collective-permute-start.10 = (bf16[64,640]{1,0:T(8,128)(2,1)S(1)}, bf16[64,640]{1,0:T(8,128)(2,1)S(1)}, u32[]{:S(2)}, u32[]{:S(2)}) collective-permute-start(bf16[64,640]{1,0:T(8,128)(2,1)S(1)} %get-tuple-element.49), channel_id=1, source_target_pairs={{0,3},{1,2},{2,1},{3,0},{4,7},{5,6},{6,5},{7,4},{8,11},{9,10},{10,... | collective-permute-start | bytes 245768 | tf_op jit(solution)/shard_map/ppermute | solution.py:231
  19.5 6.0 %collective-permute-start.11 = (bf16[64,640]{1,0:T(8,128)(2,1)S(1)}, bf16[64,640]{1,0:T(8,128)(2,1)S(1)}, u32[]{:S(2)}, u32[]{:S(2)}) collective-permute-start(bf16[64,640]{1,0:T(8,128)(2,1)S(1)} %get-tuple-element.50), channel_id=1, source_target_pairs={{0,1},{1,0},{2,3},{3,2},{4,5},{5,4},{6,7},{7,6},{8,9},{9,8},{10,11... | collective-permute-start | bytes 245768 | tf_op jit(solution)/shard_map/ppermute | solution.py:231
  20.8 5.3 %collective-permute-start.12 = (bf16[64,640]{1,0:T(8,128)(2,1)S(1)}, bf16[64,640]{1,0:T(8,128)(2,1)S(1)}, u32[]{:S(2)}, u32[]{:S(2)}) collective-permute-start(bf16[64,640]{1,0:T(8,128)(2,1)S(1)} %get-tuple-element.51), channel_id=1, source_target_pairs={{0,2},{1,3},{2,0},{3,1},{4,6},{5,7},{6,4},{7,5},{8,10},{9,11},{10,... | collective-permute-start | bytes 245768 | tf_op jit(solution)/shard_map/ppermute | solution.py:231
  21.6 8.4 %collective-permute-start.7 = (bf16[64,1024]{1,0:T(8,128)(2,1)S(1)}, bf16[64,1024]{1,0:T(8,128)(2,1)S(1)}, u32[]{:S(2)}, u32[]{:S(2)}) collective-permute-start(bf16[64,1024]{1,0:T(8,128)(2,1)S(1)} %get-tuple-element.45), channel_id=1, source_target_pairs={{0,3},{1,2},{2,1},{3,0},{4,7},{5,6},{6,5},{7,4},{8,11},{9,10},{10,... | collective-permute-start | bytes 393224 | tf_op jit(solution)/shard_map/ppermute | solution.py:231
  23.0 7.3 %collective-permute-start.8 = (bf16[64,1024]{1,0:T(8,128)(2,1)S(1)}, bf16[64,1024]{1,0:T(8,128)(2,1)S(1)}, u32[]{:S(2)}, u32[]{:S(2)}) collective-permute-start(bf16[64,1024]{1,0:T(8,128)(2,1)S(1)} %get-tuple-element.46), channel_id=1, source_target_pairs={{0,1},{1,0},{2,3},{3,2},{4,5},{5,4},{6,7},{7,6},{8,9},{9,8},{10,11... | collective-permute-start | bytes 393224 | tf_op jit(solution)/shard_map/ppermute | solution.py:231
  24.3 8.3 %collective-permute-start.9 = (bf16[64,1024]{1,0:T(8,128)(2,1)S(1)}, bf16[64,1024]{1,0:T(8,128)(2,1)S(1)}, u32[]{:S(2)}, u32[]{:S(2)}) collective-permute-start(bf16[64,1024]{1,0:T(8,128)(2,1)S(1)} %get-tuple-element.47), channel_id=1, source_target_pairs={{0,2},{1,3},{2,0},{3,1},{4,6},{5,7},{6,4},{7,5},{8,10},{9,11},{10,... | collective-permute-start | bytes 393224 | tf_op jit(solution)/shard_map/ppermute | solution.py:231
  26.2 7.8 %collective-permute-start.15 = (bf16[64,640]{1,0:T(8,128)(2,1)S(1)}, bf16[64,640]{1,0:T(8,128)(2,1)S(1)}, u32[]{:S(2)}, u32[]{:S(2)}) collective-permute-start(bf16[64,640]{1,0:T(8,128)(2,1)S(1)} %get-tuple-element.54.left), channel_id=1, source_target_pairs={{0,4},{4,0},{1,5},{5,1},{2,6},{6,2},{3,7},{7,3},{8,12},{12,8},{9,1... | collective-permute-start | bytes 245768 | tf_op jit(solution)/shard_map/ppermute | solution.py:239
  32.7 10.6 %collective-permute-start.14 = (bf16[64,1024]{1,0:T(8,128)(2,1)S(1)}, bf16[64,1024]{1,0:T(8,128)(2,1)S(1)}, u32[]{:S(2)}, u32[]{:S(2)}) collective-permute-start(bf16[64,1024]{1,0:T(8,128)(2,1)S(1)} %get-tuple-element.53.left), channel_id=1, source_target_pairs={{0,4},{4,0},{1,5},{5,1},{2,6},{6,2},{3,7},{7,3},{8,12},{12,8},{9,1... | collective-permute-start | bytes 393224 | tf_op jit(solution)/shard_map/ppermute | solution.py:239
  33.0 5.3 %collective-permute-start.19 = (bf16[64,640]{1,0:T(8,128)(2,1)S(1)}, bf16[64,640]{1,0:T(8,128)(2,1)S(1)}, u32[]{:S(2)}, u32[]{:S(2)}) collective-permute-start(bf16[64,640]{1,0:T(8,128)(2,1)S(1)} %get-tuple-element.55.refs_0_), channel_id=1, source_target_pairs={{0,1},{1,0},{2,3},{3,2},{4,5},{5,4},{6,7},{7,6},{8,9},{9,8},{10,11... | collective-permute-start | bytes 245768 | tf_op jit(solution)/shard_map/ppermute | solution.py:231
  34.0 9.2 %collective-permute-start.18 = (bf16[64,640]{1,0:T(8,128)(2,1)S(1)}, bf16[64,640]{1,0:T(8,128)(2,1)S(1)}, u32[]{:S(2)}, u32[]{:S(2)}) collective-permute-start(bf16[64,640]{1,0:T(8,128)(2,1)S(1)} %shard_map.58.refs_0_), channel_id=1, source_target_pairs={{0,3},{1,2},{2,1},{3,0},{4,7},{5,6},{6,5},{7,4},{8,11},{9,10},{10,... | collective-permute-start | bytes 245768 | tf_op jit(solution)/shard_map/ppermute | solution.py:231
  37.0 6.3 %collective-permute-start.17 = (bf16[64,640]{1,0:T(8,128)(2,1)S(1)}, bf16[64,640]{1,0:T(8,128)(2,1)S(1)}, u32[]{:S(2)}, u32[]{:S(2)}) collective-permute-start(bf16[64,640]{1,0:T(8,128)(2,1)S(1)} %shard_map.58.refs_0_), channel_id=1, source_target_pairs={{0,2},{1,3},{2,0},{3,1},{4,6},{5,7},{6,4},{7,5},{8,10},{9,11},{10,... | collective-permute-start | bytes 245768 | tf_op jit(solution)/shard_map/ppermute | solution.py:231
  37.1 6.3 %collective-permute-start.16 = (bf16[64,640]{1,0:T(8,128)(2,1)S(1)}, bf16[64,640]{1,0:T(8,128)(2,1)S(1)}, u32[]{:S(2)}, u32[]{:S(2)}) collective-permute-start(bf16[64,640]{1,0:T(8,128)(2,1)S(1)} %shard_map.58.refs_0_), channel_id=1, source_target_pairs={{0,1},{1,0},{2,3},{3,2},{4,5},{5,4},{6,7},{7,6},{8,9},{9,8},{10,11... | collective-permute-start | bytes 245768 | tf_op jit(solution)/shard_map/ppermute | solution.py:231
  38.4 10.6 %collective-permute-start.21 = (bf16[64,640]{1,0:T(8,128)(2,1)S(1)}, bf16[64,640]{1,0:T(8,128)(2,1)S(1)}, u32[]{:S(2)}, u32[]{:S(2)}) collective-permute-start(bf16[64,640]{1,0:T(8,128)(2,1)S(1)} %get-tuple-element.55.refs_0_), channel_id=1, source_target_pairs={{0,3},{1,2},{2,1},{3,0},{4,7},{5,6},{6,5},{7,4},{8,11},{9,10},{10,... | collective-permute-start | bytes 245768 | tf_op jit(solution)/shard_map/ppermute | solution.py:231
  43.3 5.8 %collective-permute-start.20 = (bf16[64,640]{1,0:T(8,128)(2,1)S(1)}, bf16[64,640]{1,0:T(8,128)(2,1)S(1)}, u32[]{:S(2)}, u32[]{:S(2)}) collective-permute-start(bf16[64,640]{1,0:T(8,128)(2,1)S(1)} %get-tuple-element.55.refs_0_), channel_id=1, source_target_pairs={{0,2},{1,3},{2,0},{3,1},{4,6},{5,7},{6,4},{7,5},{8,10},{9,11},{10,... | collective-permute-start | bytes 245768 | tf_op jit(solution)/shard_map/ppermute | solution.py:231
  43.4 7.7 %collective-permute-start.25 = (bf16[64,1024]{1,0:T(8,128)(2,1)S(1)}, bf16[64,1024]{1,0:T(8,128)(2,1)S(1)}, u32[]{:S(2)}, u32[]{:S(2)}) collective-permute-start(bf16[64,1024]{1,0:T(8,128)(2,1)S(1)} %shard_map.59.after.refs_0_), channel_id=1, source_target_pairs={{0,3},{1,2},{2,1},{3,0},{4,7},{5,6},{6,5},{7,4},{8,11},{9,10},{10,... | collective-permute-start | bytes 393224 | tf_op jit(solution)/shard_map/ppermute | solution.py:231
  44.7 6.7 %collective-permute-start.24 = (bf16[64,1024]{1,0:T(8,128)(2,1)S(1)}, bf16[64,1024]{1,0:T(8,128)(2,1)S(1)}, u32[]{:S(2)}, u32[]{:S(2)}) collective-permute-start(bf16[64,1024]{1,0:T(8,128)(2,1)S(1)} %shard_map.59.after.refs_0_), channel_id=1, source_target_pairs={{0,2},{1,3},{2,0},{3,1},{4,6},{5,7},{6,4},{7,5},{8,10},{9,11},{10,... | collective-permute-start | bytes 393224 | tf_op jit(solution)/shard_map/ppermute | solution.py:231
  45.5 5.9 %collective-permute-start.23 = (bf16[64,1024]{1,0:T(8,128)(2,1)S(1)}, bf16[64,1024]{1,0:T(8,128)(2,1)S(1)}, u32[]{:S(2)}, u32[]{:S(2)}) collective-permute-start(bf16[64,1024]{1,0:T(8,128)(2,1)S(1)} %shard_map.59.after.refs_0_), channel_id=1, source_target_pairs={{0,1},{1,0},{2,3},{3,2},{4,5},{5,4},{6,7},{7,6},{8,9},{9,8},{10,11... | collective-permute-start | bytes 393224 | tf_op jit(solution)/shard_map/ppermute | solution.py:231
  49.0 2.5 %collective-permute-start.22 = (bf16[128,512]{1,0:T(8,128)(2,1)S(1)}, bf16[128,512]{1,0:T(8,128)(2,1)S(1)}, u32[]{:S(2)}, u32[]{:S(2)}) collective-permute-start(bf16[128,512]{1,0:T(8,128)(2,1)S(1)} %get-tuple-element.59), channel_id=1, source_target_pairs={{0,8},{8,0},{1,9},{9,1},{2,10},{10,2},{3,11},{11,3},{4,12},{12,4},... | collective-permute-start | bytes 393224 | tf_op jit(solution)/shard_map/ppermute | solution.py:335

commit v18 on v17

--- a/solution.py
+++ b/solution.py
@@ -328,7 +328,7 @@
             [pltpu.VMEM((GROUP, size // 2, factor), BF16), pltpu.VMEM((width, width), BF16)],
         )(*through, after, *pieces)
 
-    total = exchange(total, (*out, act[1]))
+    total = exchange(total, (*out, act[2]))
     grad = send([total] * GROUP)
     out_inv, give_cot = inverse(out, total, give_cot)
     (act_inv,) = inverse(act, total)

time: 53.2 us -> 54.3 us (1.021)
  waiting for transfers between devices: 11.1 us -> 13.8 us
  starting transfers between devices: 31.7 us -> 30.1 us
    ppermute x18, waiting for transfers between devices: 8.53 us -> 11.3 us  [send(): lax.ppermute(parts[step], ('near', 'side'), [(i, i ^ step) for i in range...]
    ppermute x18, starting transfers between devices: 25.4 us -> 23.8 us  [send(): lax.ppermute(parts[step], ('near', 'side'), [(i, i ^ step) for i in range...]
  transfers between devices with their start and end apart: 26 -> 26, of which waited for: 10 -> 12; matrix products, arithmetic and copies ran while one was open for 2% -> 2% of each run, Pallas kernels for 11% -> 11%
where the time goes in v18:
time: 54.3 us; the launch traced here: 54.2 us
  starting transfers between devices  30.1 us (55%)
  waiting for transfers between devices  13.8 us (25%)
  Pallas kernels  8.26 us (15%)
  other arithmetic  1.18 us (2%)
  between operations  0.81 us (1%)
    ppermute x18, starting transfers between devices, send(): lax.ppermute(parts[step], ('near', 'side'), [(i, i ^ step) for i in range...  23.8 us
    ppermute x18, waiting for transfers between devices, send(): lax.ppermute(parts[step], ('near', 'side'), [(i, i ^ step) for i in range...  11.3 us
    ppermute x3, starting transfers between devices, exchange(): got = lax.ppermute(value, 'far', route)  4.27 us
    pallas_call x2, Pallas kernels, inverse(): call(functools.partial(through_kernel if through else inverse_kernel, cou...  4.05 us
    ppermute x1, waiting for transfers between devices, body(): upstream = lax.ppermute(down, 'row', [(r, r - 1) for r in range(1, pairs)])  1.69 us
    pallas_call x1, Pallas kernels, body(): call(update_kernel, 10 * width ** 3, [array(width, width, dtype=F32), arr...  1.63 us
    ppermute x1, starting transfers between devices, body(): upstream = lax.ppermute(down, 'row', [(r, r - 1) for r in range(1, pairs)])  1.29 us
    select_n x2, other arithmetic, near_copy(): return jnp.where(core > 1, jnp.zeros_like(value), value)  1.18 us
  transfers between devices with their start and end apart: 26, of which 12 were waited for; matrix products, arithmetic and copies ran while one was open for 2% of the time, Pallas kernels for 11%

profile of v18, /device:TPU:0, one launch (start us, length us, event | category | flops | bytes accessed | tf_op | source)
XLA Modules:
  0.0 54.2 jit_solution(15179042698693197371)
XLA Ops:
  0.6 0.5 collective-permute-start
  1.1 0.1 collective-permute-start.1
  1.2 0.0 copy-start
  1.2 1.1 %broadcast_select_fusion.weight = bf16[512,512]{1,0:T(8,128)(2,1)S(1)} fusion(pred[]{:T(512)S(6)} %gt.2, bf16[1,512,512]{2,1,0:T(8,128)(2,1)} %param.4), kind=kLoop, calls=%fused_computation | loop fusion | flops 262144 | bytes 1048577 | tf_op jit(solution)/shard_map/jit(_where)/select_n | solution.py:263
  2.4 0.0 copy-done
  2.4 0.0 copy-done.1
  2.5 0.8 %collective-permute-done.1.partner_local = bf16[2,128,512]{2,1,0:T(8,128)(2,1)S(1)} collective-permute-done((bf16[2,128,512]{2,1,0:T(8,128)(2,1)}, bf16[2,128,512]{2,1,0:T(8,128)(2,1)S(1)}, u32[]{:S(2)}, u32[]{:S(2)}) %collective-permute-start.1) | collective-permute-done | bytes 262176 | tf_op jit(solution)/shard_map/ppermute | solution.py:266
  3.3 0.0 collective-permute-done.partner
  3.3 0.9 %shard_map.50 = (bf16[512,512]{1,0:T(8,128)(2,1)S(1)}, bf16[2,128,512]{2,1,0:T(8,128)(2,1)S(1)}, bf16[128,512]{1,0:T(8,128)(2,1)S(1)}, f32[128,512]{1,0:T(8,128)...) custom-call(bf16[512,512]{1,0:T(8,128)(2,1)S(1)} %broadcast_select_fusion.weight, ...), custom_call_target="tpu_custom_call" | custom-call | flops 268435456 | bytes 1048576 | tf_op jit(solution)/shard_map/pallas_call | solution.py:269
  4.2 1.3 %collective-permute-start.2 = (bf16[128,512]{1,0:T(8,128)(2,1)S(1)}, bf16[128,512]{1,0:T(8,128)(2,1)S(1)}, u32[]{:S(2)}, u32[]{:S(2)}) collective-permute-start(bf16[128,512]{1,0:T(8,128)(2,1)S(1)} %get-tuple-element.36.after), channel_id=1, source_target_pairs={{16,0},{17,1},{18,2},{19,3},{20,4},{21,5},{22,6},{23,7},{24,8},{25... | collective-permute-start | bytes 393224 | tf_op jit(solution)/shard_map/ppermute | solution.py:277
  5.5 0.4 shard_map.52
  5.9 4.0 %collective-permute-start.4 = (bf16[64,640]{1,0:T(8,128)(2,1)S(1)}, bf16[64,640]{1,0:T(8,128)(2,1)S(1)}, u32[]{:S(2)}, u32[]{:S(2)}) collective-permute-start(bf16[64,640]{1,0:T(8,128)(2,1)S(1)} %get-tuple-element.41), channel_id=1, source_target_pairs={{0,3},{1,2},{2,1},{3,0},{4,7},{5,6},{6,5},{7,4},{8,11},{9,10},{10,... | collective-permute-start | bytes 245768 | tf_op jit(solution)/shard_map/ppermute | solution.py:231
  9.8 0.5 collective-permute-start.5
  10.4 0.1 collective-permute-start.6
  10.5 1.7 %collective-permute-done.2.arrived = bf16[128,512]{1,0:T(8,128)(2,1)S(1)} collective-permute-done((bf16[128,512]{1,0:T(8,128)(2,1)S(1)}, bf16[128,512]{1,0:T(8,128)(2,1)S(1)}, u32[]{:S(2)}, u32[]{:S(2)}) %collective-permute-start.2) | collective-permute-done | bytes 131104 | tf_op jit(solution)/shard_map/ppermute | solution.py:277
  12.2 0.5 %shard_map.51 = (bf16[128,512]{1,0:T(8,128)(2,1)S(1)}, bf16[128,512]{1,0:T(8,128)(2,1)S(1)}, bf16[128,512]{1,0:T(8,128)(2,1)S(1)}, bf16[128,512]{1,0:T(8,128)(2,1)S(1)}) custom-call(bf16[512,512]{1,0:T(8,128)(2,1)S(1)} %get-tuple-element.33.own, bf16[512,512]{1,0:T(8,128)(2,1)S(1)} %collective-permute-done.partner, ...), custom_call_target="tpu_custom_call" | custom-call | flops 2147483648 | bytes 1048576 | tf_op jit(solution)/shard_map/pallas_call | solution.py:294
  12.7 0.1 collective-permute-start.3
  12.8 0.0 collective-permute-done.4.refs_1_
  12.8 1.5 %collective-permute-done.5.refs_2_ = bf16[64,640]{1,0:T(8,128)(2,1)S(1)} collective-permute-done((bf16[64,640]{1,0:T(8,128)(2,1)S(1)}, bf16[64,640]{1,0:T(8,128)(2,1)S(1)}, u32[]{:S(2)}, u32[]{:S(2)}) %collective-permute-start.5) | collective-permute-done | bytes 81952 | tf_op jit(solution)/shard_map/ppermute | solution.py:231
  14.3 0.5 collective-permute-done.6.refs_3_
  14.8 2.7 %collective-permute-start.13 = (bf16[64,640]{1,0:T(8,128)(2,1)S(1)}, bf16[64,640]{1,0:T(8,128)(2,1)S(1)}, u32[]{:S(2)}, u32[]{:S(2)}) collective-permute-start(bf16[64,640]{1,0:T(8,128)(2,1)S(1)} %shard_map.53.after.left), channel_id=1, source_target_pairs={{0,4},{4,0},{1,5},{5,1},{2,6},{6,2},{3,7},{7,3},{8,12},{12,8},{9,1... | collective-permute-start | bytes 245768 | tf_op jit(solution)/shard_map/ppermute | solution.py:239
  17.5 0.0 collective-permute-done.3.dh_got
  17.5 0.5 shard_map.54
  18.0 1.5 %collective-permute-start.10 = (bf16[64,640]{1,0:T(8,128)(2,1)S(1)}, bf16[64,640]{1,0:T(8,128)(2,1)S(1)}, u32[]{:S(2)}, u32[]{:S(2)}) collective-permute-start(bf16[64,640]{1,0:T(8,128)(2,1)S(1)} %get-tuple-element.49), channel_id=1, source_target_pairs={{0,3},{1,2},{2,1},{3,0},{4,7},{5,6},{6,5},{7,4},{8,11},{9,10},{10,... | collective-permute-start | bytes 245768 | tf_op jit(solution)/shard_map/ppermute | solution.py:231
  19.5 1.3 %collective-permute-start.11 = (bf16[64,640]{1,0:T(8,128)(2,1)S(1)}, bf16[64,640]{1,0:T(8,128)(2,1)S(1)}, u32[]{:S(2)}, u32[]{:S(2)}) collective-permute-start(bf16[64,640]{1,0:T(8,128)(2,1)S(1)} %get-tuple-element.50), channel_id=1, source_target_pairs={{0,1},{1,0},{2,3},{3,2},{4,5},{5,4},{6,7},{7,6},{8,9},{9,8},{10,11... | collective-permute-start | bytes 245768 | tf_op jit(solution)/shard_map/ppermute | solution.py:231
  20.8 0.8 %collective-permute-start.12 = (bf16[64,640]{1,0:T(8,128)(2,1)S(1)}, bf16[64,640]{1,0:T(8,128)(2,1)S(1)}, u32[]{:S(2)}, u32[]{:S(2)}) collective-permute-start(bf16[64,640]{1,0:T(8,128)(2,1)S(1)} %get-tuple-element.51), channel_id=1, source_target_pairs={{0,2},{1,3},{2,0},{3,1},{4,6},{5,7},{6,4},{7,5},{8,10},{9,11},{10,... | collective-permute-start | bytes 245768 | tf_op jit(solution)/shard_map/ppermute | solution.py:231
  21.6 1.4 %collective-permute-start.7 = (bf16[64,1024]{1,0:T(8,128)(2,1)S(1)}, bf16[64,1024]{1,0:T(8,128)(2,1)S(1)}, u32[]{:S(2)}, u32[]{:S(2)}) collective-permute-start(bf16[64,1024]{1,0:T(8,128)(2,1)S(1)} %get-tuple-element.45), channel_id=1, source_target_pairs={{0,3},{1,2},{2,1},{3,0},{4,7},{5,6},{6,5},{7,4},{8,11},{9,10},{10,... | collective-permute-start | bytes 393224 | tf_op jit(solution)/shard_map/ppermute | solution.py:231
  23.0 0.0 collective-permute-done.13.right
  23.0 1.3 %collective-permute-start.8 = (bf16[64,1024]{1,0:T(8,128)(2,1)S(1)}, bf16[64,1024]{1,0:T(8,128)(2,1)S(1)}, u32[]{:S(2)}, u32[]{:S(2)}) collective-permute-start(bf16[64,1024]{1,0:T(8,128)(2,1)S(1)} %get-tuple-element.46), channel_id=1, source_target_pairs={{0,1},{1,0},{2,3},{3,2},{4,5},{5,4},{6,7},{7,6},{8,9},{9,8},{10,11... | collective-permute-start | bytes 393224 | tf_op jit(solution)/shard_map/ppermute | solution.py:231
  24.3 0.0 collective-permute-done.10.refs_1_
  24.3 1.2 %collective-permute-start.9 = (bf16[64,1024]{1,0:T(8,128)(2,1)S(1)}, bf16[64,1024]{1,0:T(8,128)(2,1)S(1)}, u32[]{:S(2)}, u32[]{:S(2)}) collective-permute-start(bf16[64,1024]{1,0:T(8,128)(2,1)S(1)} %get-tuple-element.47), channel_id=1, source_target_pairs={{0,2},{1,3},{2,0},{3,1},{4,6},{5,7},{6,4},{7,5},{8,10},{9,11},{10,... | collective-permute-start | bytes 393224 | tf_op jit(solution)/shard_map/ppermute | solution.py:231
  25.5 0.0 collective-permute-done.11.refs_2_
  25.5 0.6 %collective-permute-done.12.refs_3_ = bf16[64,640]{1,0:T(8,128)(2,1)S(1)} collective-permute-done((bf16[64,640]{1,0:T(8,128)(2,1)S(1)}, bf16[64,640]{1,0:T(8,128)(2,1)S(1)}, u32[]{:S(2)}, u32[]{:S(2)}) %collective-permute-start.12) | collective-permute-done | bytes 81952 | tf_op jit(solution)/shard_map/ppermute | solution.py:231
  26.2 1.2 %collective-permute-start.15 = (bf16[64,640]{1,0:T(8,128)(2,1)S(1)}, bf16[64,640]{1,0:T(8,128)(2,1)S(1)}, u32[]{:S(2)}, u32[]{:S(2)}) collective-permute-start(bf16[64,640]{1,0:T(8,128)(2,1)S(1)} %get-tuple-element.54.left), channel_id=1, source_target_pairs={{0,4},{4,0},{1,5},{5,1},{2,6},{6,2},{3,7},{7,3},{8,12},{12,8},{9,1... | collective-permute-start | bytes 245768 | tf_op jit(solution)/shard_map/ppermute | solution.py:239
  27.5 2.6 %collective-permute-done.7.refs_1_ = bf16[64,1024]{1,0:T(8,128)(2,1)S(1)} collective-permute-done((bf16[64,1024]{1,0:T(8,128)(2,1)S(1)}, bf16[64,1024]{1,0:T(8,128)(2,1)S(1)}, u32[]{:S(2)}, u32[]{:S(2)}) %collective-permute-start.7) | collective-permute-done | bytes 131104 | tf_op jit(solution)/shard_map/ppermute | solution.py:231
  30.0 0.2 collective-permute-done.8.refs_2_
  30.3 2.3 %collective-permute-done.9.refs_3_ = bf16[64,1024]{1,0:T(8,128)(2,1)S(1)} collective-permute-done((bf16[64,1024]{1,0:T(8,128)(2,1)S(1)}, bf16[64,1024]{1,0:T(8,128)(2,1)S(1)}, u32[]{:S(2)}, u32[]{:S(2)}) %collective-permute-start.9) | collective-permute-done | bytes 131104 | tf_op jit(solution)/shard_map/ppermute | solution.py:231
  32.6 0.1 shard_map.57
  32.7 0.4 collective-permute-start.14
  33.0 2.4 %collective-permute-start.19 = (bf16[64,640]{1,0:T(8,128)(2,1)S(1)}, bf16[64,640]{1,0:T(8,128)(2,1)S(1)}, u32[]{:S(2)}, u32[]{:S(2)}) collective-permute-start(bf16[64,640]{1,0:T(8,128)(2,1)S(1)} %get-tuple-element.55.refs_0_), channel_id=1, source_target_pairs={{0,2},{1,3},{2,0},{3,1},{4,6},{5,7},{6,4},{7,5},{8,10},{9,11},{10,... | collective-permute-start | bytes 245768 | tf_op jit(solution)/shard_map/ppermute | solution.py:231
  35.5 0.0 collective-permute-done.15.right
  35.5 0.5 collective-permute-start.18
  36.0 2.0 %collective-permute-start.17 = (bf16[64,640]{1,0:T(8,128)(2,1)S(1)}, bf16[64,640]{1,0:T(8,128)(2,1)S(1)}, u32[]{:S(2)}, u32[]{:S(2)}) collective-permute-start(bf16[64,640]{1,0:T(8,128)(2,1)S(1)} %shard_map.58.refs_0_), channel_id=1, source_target_pairs={{0,2},{1,3},{2,0},{3,1},{4,6},{5,7},{6,4},{7,5},{8,10},{9,11},{10,... | collective-permute-start | bytes 245768 | tf_op jit(solution)/shard_map/ppermute | solution.py:231
  38.0 1.1 %collective-permute-start.16 = (bf16[64,640]{1,0:T(8,128)(2,1)S(1)}, bf16[64,640]{1,0:T(8,128)(2,1)S(1)}, u32[]{:S(2)}, u32[]{:S(2)}) collective-permute-start(bf16[64,640]{1,0:T(8,128)(2,1)S(1)} %shard_map.58.refs_0_), channel_id=1, source_target_pairs={{0,1},{1,0},{2,3},{3,2},{4,5},{5,4},{6,7},{7,6},{8,9},{9,8},{10,11... | collective-permute-start | bytes 245768 | tf_op jit(solution)/shard_map/ppermute | solution.py:231
  39.1 1.6 %collective-permute-done.19.refs_4_.refs_2_ = bf16[64,640]{1,0:T(8,128)(2,1)S(1)} collective-permute-done((bf16[64,640]{1,0:T(8,128)(2,1)S(1)}, bf16[64,640]{1,0:T(8,128)(2,1)S(1)}, u32[]{:S(2)}, u32[]{:S(2)}) %collective-permute-start.19) | collective-permute-done | bytes 81952 | tf_op jit(solution)/shard_map/ppermute | solution.py:231
  40.7 0.6 %collective-permute-start.21 = (bf16[64,640]{1,0:T(8,128)(2,1)S(1)}, bf16[64,640]{1,0:T(8,128)(2,1)S(1)}, u32[]{:S(2)}, u32[]{:S(2)}) collective-permute-start(bf16[64,640]{1,0:T(8,128)(2,1)S(1)} %get-tuple-element.55.refs_0_), channel_id=1, source_target_pairs={{0,3},{1,2},{2,1},{3,0},{4,7},{5,6},{6,5},{7,4},{8,11},{9,10},{10,... | collective-permute-start | bytes 245768 | tf_op jit(solution)/shard_map/ppermute | solution.py:231
  41.3 1.0 %collective-permute-done.18.refs_3_ = bf16[64,640]{1,0:T(8,128)(2,1)S(1)} collective-permute-done((bf16[64,640]{1,0:T(8,128)(2,1)S(1)}, bf16[64,640]{1,0:T(8,128)(2,1)S(1)}, u32[]{:S(2)}, u32[]{:S(2)}) %collective-permute-start.18) | collective-permute-done | bytes 81952 | tf_op jit(solution)/shard_map/ppermute | solution.py:231
  42.3 1.6 %collective-permute-start.20 = (bf16[64,640]{1,0:T(8,128)(2,1)S(1)}, bf16[64,640]{1,0:T(8,128)(2,1)S(1)}, u32[]{:S(2)}, u32[]{:S(2)}) collective-permute-start(bf16[64,640]{1,0:T(8,128)(2,1)S(1)} %get-tuple-element.55.refs_0_), channel_id=1, source_target_pairs={{0,1},{1,0},{2,3},{3,2},{4,5},{5,4},{6,7},{7,6},{8,9},{9,8},{10,11... | collective-permute-start | bytes 245768 | tf_op jit(solution)/shard_map/ppermute | solution.py:231
  43.9 0.3 collective-permute-done.17.refs_2_
  44.2 0.0 collective-permute-done.16.refs_1_
  44.2 0.0 collective-permute-done.14.right
  44.2 0.5 collective-permute-start.25
  44.7 1.5 %collective-permute-start.24 = (bf16[64,1024]{1,0:T(8,128)(2,1)S(1)}, bf16[64,1024]{1,0:T(8,128)(2,1)S(1)}, u32[]{:S(2)}, u32[]{:S(2)}) collective-permute-start(bf16[64,1024]{1,0:T(8,128)(2,1)S(1)} %shard_map.59.after.refs_0_), channel_id=1, source_target_pairs={{0,2},{1,3},{2,0},{3,1},{4,6},{5,7},{6,4},{7,5},{8,10},{9,11},{10,... | collective-permute-start | bytes 393224 | tf_op jit(solution)/shard_map/ppermute | solution.py:231
  46.2 1.6 %collective-permute-start.23 = (bf16[64,1024]{1,0:T(8,128)(2,1)S(1)}, bf16[64,1024]{1,0:T(8,128)(2,1)S(1)}, u32[]{:S(2)}, u32[]{:S(2)}) collective-permute-start(bf16[64,1024]{1,0:T(8,128)(2,1)S(1)} %shard_map.59.after.refs_0_), channel_id=1, source_target_pairs={{0,1},{1,0},{2,3},{3,2},{4,5},{5,4},{6,7},{7,6},{8,9},{9,8},{10,11... | collective-permute-start | bytes 393224 | tf_op jit(solution)/shard_map/ppermute | solution.py:231
  47.8 2.0 %shard_map.61 = (bf16[512,512]{1,0:T(8,128)(2,1)S(1)}, bf16[128,512]{1,0:T(8,128)(2,1)S(1)}) custom-call(bf16[128,512]{1,0:T(8,128)(2,1)S(1)} %get-tuple-element.56.through, bf16[64,1024]{1,0:T(8,128)(2,1)S(1)} %shard_map.59.after.refs_0_, bf16[64,640]{1,0:T(8,128)(2,1)S(1)} %shard_map.58.refs_0_, bf16[64,640]{1,0:T(8,128)(2,1)S(1)} %collective-permute-done.16.refs_1_, ...), custom_call_target="tpu_custom_call" | custom-call | flops 2684354560 | bytes 1048576 | tf_op jit(solution)/shard_map/pallas_call | solution.py:323
  49.8 0.0 collective-permute-done.21.refs_3_
  49.8 0.1 collective-permute-start.22
  49.9 0.0 collective-permute-done.20.refs_1_
  49.9 2.0 %shard_map.60.act_inv = bf16[512,512]{1,0:T(8,128)(2,1)S(1)} custom-call(bf16[64,1024]{1,0:T(8,128)(2,1)S(1)} %shard_map.59.after.refs_0_, bf16[64,640]{1,0:T(8,128)(2,1)S(1)} %get-tuple-element.55.refs_0_, bf16[64,640]{1,0:T(8,128)(2,1)S(1)} %collective-permute-done.20.refs_1_, bf16[64,640]{1,0:T(8,128)(2,1)S(1)} %collective-permute-done.19.refs_4_.refs_2_, ...), custom_call_target="tpu_custom_call" | custom-call | flops 2684354560 | bytes 1048576 | tf_op jit(solution)/shard_map/pallas_call | solution.py:323
  52.0 0.0 collective-permute-done.25.refs_3_
  52.0 0.0 collective-permute-done.24.refs_2_
  52.0 0.5 %collective-permute-done.23.refs_1_ = bf16[64,1024]{1,0:T(8,128)(2,1)S(1)} collective-permute-done((bf16[64,1024]{1,0:T(8,128)(2,1)S(1)}, bf16[64,1024]{1,0:T(8,128)(2,1)S(1)}, u32[]{:S(2)}, u32[]{:S(2)}) %collective-permute-start.23) | collective-permute-done | bytes 131104 | tf_op jit(solution)/shard_map/ppermute | solution.py:231
  52.5 0.0 collective-permute-done.22.other_cot
  52.5 1.6 %shard_map.62 = (f32[512,512]{1,0:T(8,128)}, bf16[2,128,512]{2,1,0:T(8,128)(2,1)}) custom-call(bf16[512,512]{1,0:T(8,128)(2,1)S(1)} %shard_map.60.act_inv, bf16[512,512]{1,0:T(8,128)(2,1)S(1)} %get-tuple-element.57.out_inv, bf16[128,512]{1,0:T(8,128)(2,1)S(1)} %get-tuple-element.58.own_cot, bf16[128,512]{1,0:T(8,128)(2,1)S(1)} %collective-permute-done.22.other_cot, ...), custom_call_target="tpu_custom_call" | custom-call | flops 1342177280 | bytes 1048576 | tf_op jit(solution)/shard_map/pallas_call | solution.py:336
  (7 shorter events, 0.2 us)
Async XLA Ops:
  0.6 2.6 %collective-permute-start = (bf16[512,512]{1,0:T(8,128)(2,1)}, bf16[512,512]{1,0:T(8,128)(2,1)S(1)}, u32[]{:S(2)}, u32[]{:S(2)}) collective-permute-start(bf16[512,512]{1,0:T(8,128)(2,1)} %bitcast.6), channel_id=1, source_target_pairs={{0,8},{8,0},{1,9},{9,1},{2,10},{10,2},{3,11},{11,3},{4,12},{12,4},... | collective-permute-start | bytes 1572872 | tf_op jit(solution)/shard_map/ppermute | solution.py:265
  1.1 2.1 %collective-permute-start.1 = (bf16[2,128,512]{2,1,0:T(8,128)(2,1)}, bf16[2,128,512]{2,1,0:T(8,128)(2,1)S(1)}, u32[]{:S(2)}, u32[]{:S(2)}) collective-permute-start(bf16[2,128,512]{2,1,0:T(8,128)(2,1)} %bitcast.7), channel_id=1, source_target_pairs={{0,8},{8,0},{1,9},{9,1},{2,10},{10,2},{3,11},{11,3},{4,12},{12,4},... | collective-permute-start | bytes 786440 | tf_op jit(solution)/shard_map/ppermute | solution.py:266
  1.2 1.1 %copy-start = (bf16[2,128,512]{2,1,0:T(8,128)(2,1)S(1)}, bf16[2,128,512]{2,1,0:T(8,128)(2,1)}, u32[]{:S(2)}) copy-start(bf16[2,128,512]{2,1,0:T(8,128)(2,1)} %param.5) | copy-start | bytes 786436
  1.2 1.2 %copy-start.1 = (bf16[1,2,128,512]{3,2,1,0:T(8,128)(2,1)S(1)}, bf16[1,2,128,512]{3,2,1,0:T(8,128)(2,1)}, u32[]{:S(2)}) copy-start(bf16[1,2,128,512]{3,2,1,0:T(8,128)(2,1)} %param.3) | copy-start | bytes 786436
  4.2 8.0 %collective-permute-start.2 = (bf16[128,512]{1,0:T(8,128)(2,1)S(1)}, bf16[128,512]{1,0:T(8,128)(2,1)S(1)}, u32[]{:S(2)}, u32[]{:S(2)}) collective-permute-start(bf16[128,512]{1,0:T(8,128)(2,1)S(1)} %get-tuple-element.36.after), channel_id=1, source_target_pairs={{16,0},{17,1},{18,2},{19,3},{20,4},{21,5},{22,6},{23,7},{24,8},{25... | collective-permute-start | bytes 393224 | tf_op jit(solution)/shard_map/ppermute | solution.py:277
  5.9 6.9 %collective-permute-start.4 = (bf16[64,640]{1,0:T(8,128)(2,1)S(1)}, bf16[64,640]{1,0:T(8,128)(2,1)S(1)}, u32[]{:S(2)}, u32[]{:S(2)}) collective-permute-start(bf16[64,640]{1,0:T(8,128)(2,1)S(1)} %get-tuple-element.41), channel_id=1, source_target_pairs={{0,3},{1,2},{2,1},{3,0},{4,7},{5,6},{6,5},{7,4},{8,11},{9,10},{10,... | collective-permute-start | bytes 245768 | tf_op jit(solution)/shard_map/ppermute | solution.py:231
  9.8 4.5 %collective-permute-start.5 = (bf16[64,640]{1,0:T(8,128)(2,1)S(1)}, bf16[64,640]{1,0:T(8,128)(2,1)S(1)}, u32[]{:S(2)}, u32[]{:S(2)}) collective-permute-start(bf16[64,640]{1,0:T(8,128)(2,1)S(1)} %get-tuple-element.42), channel_id=1, source_target_pairs={{0,1},{1,0},{2,3},{3,2},{4,5},{5,4},{6,7},{7,6},{8,9},{9,8},{10,11... | collective-permute-start | bytes 245768 | tf_op jit(solution)/shard_map/ppermute | solution.py:231
  10.4 4.4 %collective-permute-start.6 = (bf16[64,640]{1,0:T(8,128)(2,1)S(1)}, bf16[64,640]{1,0:T(8,128)(2,1)S(1)}, u32[]{:S(2)}, u32[]{:S(2)}) collective-permute-start(bf16[64,640]{1,0:T(8,128)(2,1)S(1)} %get-tuple-element.43), channel_id=1, source_target_pairs={{0,2},{1,3},{2,0},{3,1},{4,6},{5,7},{6,4},{7,5},{8,10},{9,11},{10,... | collective-permute-start | bytes 245768 | tf_op jit(solution)/shard_map/ppermute | solution.py:231
  12.7 4.8 %collective-permute-start.3 = (bf16[128,512]{1,0:T(8,128)(2,1)S(1)}, bf16[128,512]{1,0:T(8,128)(2,1)S(1)}, u32[]{:S(2)}, u32[]{:S(2)}) collective-permute-start(bf16[128,512]{1,0:T(8,128)(2,1)S(1)} %get-tuple-element.39), channel_id=1, source_target_pairs={{0,8},{8,0},{1,9},{9,1},{2,10},{10,2},{3,11},{11,3},{4,12},{12,4},... | collective-permute-start | bytes 393224 | tf_op jit(solution)/shard_map/ppermute | solution.py:300
  14.8 8.2 %collective-permute-start.13 = (bf16[64,640]{1,0:T(8,128)(2,1)S(1)}, bf16[64,640]{1,0:T(8,128)(2,1)S(1)}, u32[]{:S(2)}, u32[]{:S(2)}) collective-permute-start(bf16[64,640]{1,0:T(8,128)(2,1)S(1)} %shard_map.53.after.left), channel_id=1, source_target_pairs={{0,4},{4,0},{1,5},{5,1},{2,6},{6,2},{3,7},{7,3},{8,12},{12,8},{9,1... | collective-permute-start | bytes 245768 | tf_op jit(solution)/shard_map/ppermute | solution.py:239
  18.0 6.3 %collective-permute-start.10 = (bf16[64,640]{1,0:T(8,128)(2,1)S(1)}, bf16[64,640]{1,0:T(8,128)(2,1)S(1)}, u32[]{:S(2)}, u32[]{:S(2)}) collective-permute-start(bf16[64,640]{1,0:T(8,128)(2,1)S(1)} %get-tuple-element.49), channel_id=1, source_target_pairs={{0,3},{1,2},{2,1},{3,0},{4,7},{5,6},{6,5},{7,4},{8,11},{9,10},{10,... | collective-permute-start | bytes 245768 | tf_op jit(solution)/shard_map/ppermute | solution.py:231
  19.5 6.0 %collective-permute-start.11 = (bf16[64,640]{1,0:T(8,128)(2,1)S(1)}, bf16[64,640]{1,0:T(8,128)(2,1)S(1)}, u32[]{:S(2)}, u32[]{:S(2)}) collective-permute-start(bf16[64,640]{1,0:T(8,128)(2,1)S(1)} %get-tuple-element.50), channel_id=1, source_target_pairs={{0,1},{1,0},{2,3},{3,2},{4,5},{5,4},{6,7},{7,6},{8,9},{9,8},{10,11... | collective-permute-start | bytes 245768 | tf_op jit(solution)/shard_map/ppermute | solution.py:231
  20.8 5.3 %collective-permute-start.12 = (bf16[64,640]{1,0:T(8,128)(2,1)S(1)}, bf16[64,640]{1,0:T(8,128)(2,1)S(1)}, u32[]{:S(2)}, u32[]{:S(2)}) collective-permute-start(bf16[64,640]{1,0:T(8,128)(2,1)S(1)} %get-tuple-element.51), channel_id=1, source_target_pairs={{0,2},{1,3},{2,0},{3,1},{4,6},{5,7},{6,4},{7,5},{8,10},{9,11},{10,... | collective-permute-start | bytes 245768 | tf_op jit(solution)/shard_map/ppermute | solution.py:231
  21.6 8.4 %collective-permute-start.7 = (bf16[64,1024]{1,0:T(8,128)(2,1)S(1)}, bf16[64,1024]{1,0:T(8,128)(2,1)S(1)}, u32[]{:S(2)}, u32[]{:S(2)}) collective-permute-start(bf16[64,1024]{1,0:T(8,128)(2,1)S(1)} %get-tuple-element.45), channel_id=1, source_target_pairs={{0,3},{1,2},{2,1},{3,0},{4,7},{5,6},{6,5},{7,4},{8,11},{9,10},{10,... | collective-permute-start | bytes 393224 | tf_op jit(solution)/shard_map/ppermute | solution.py:231
  23.0 7.3 %collective-permute-start.8 = (bf16[64,1024]{1,0:T(8,128)(2,1)S(1)}, bf16[64,1024]{1,0:T(8,128)(2,1)S(1)}, u32[]{:S(2)}, u32[]{:S(2)}) collective-permute-start(bf16[64,1024]{1,0:T(8,128)(2,1)S(1)} %get-tuple-element.46), channel_id=1, source_target_pairs={{0,1},{1,0},{2,3},{3,2},{4,5},{5,4},{6,7},{7,6},{8,9},{9,8},{10,11... | collective-permute-start | bytes 393224 | tf_op jit(solution)/shard_map/ppermute | solution.py:231
  24.3 8.3 %collective-permute-start.9 = (bf16[64,1024]{1,0:T(8,128)(2,1)S(1)}, bf16[64,1024]{1,0:T(8,128)(2,1)S(1)}, u32[]{:S(2)}, u32[]{:S(2)}) collective-permute-start(bf16[64,1024]{1,0:T(8,128)(2,1)S(1)} %get-tuple-element.47), channel_id=1, source_target_pairs={{0,2},{1,3},{2,0},{3,1},{4,6},{5,7},{6,4},{7,5},{8,10},{9,11},{10,... | collective-permute-start | bytes 393224 | tf_op jit(solution)/shard_map/ppermute | solution.py:231
  26.2 9.3 %collective-permute-start.15 = (bf16[64,640]{1,0:T(8,128)(2,1)S(1)}, bf16[64,640]{1,0:T(8,128)(2,1)S(1)}, u32[]{:S(2)}, u32[]{:S(2)}) collective-permute-start(bf16[64,640]{1,0:T(8,128)(2,1)S(1)} %get-tuple-element.54.left), channel_id=1, source_target_pairs={{0,4},{4,0},{1,5},{5,1},{2,6},{6,2},{3,7},{7,3},{8,12},{12,8},{9,1... | collective-permute-start | bytes 245768 | tf_op jit(solution)/shard_map/ppermute | solution.py:239
  32.7 11.5 %collective-permute-start.14 = (bf16[64,1024]{1,0:T(8,128)(2,1)S(1)}, bf16[64,1024]{1,0:T(8,128)(2,1)S(1)}, u32[]{:S(2)}, u32[]{:S(2)}) collective-permute-start(bf16[64,1024]{1,0:T(8,128)(2,1)S(1)} %get-tuple-element.53.left), channel_id=1, source_target_pairs={{0,4},{4,0},{1,5},{5,1},{2,6},{6,2},{3,7},{7,3},{8,12},{12,8},{9,1... | collective-permute-start | bytes 393224 | tf_op jit(solution)/shard_map/ppermute | solution.py:239
  33.0 7.6 %collective-permute-start.19 = (bf16[64,640]{1,0:T(8,128)(2,1)S(1)}, bf16[64,640]{1,0:T(8,128)(2,1)S(1)}, u32[]{:S(2)}, u32[]{:S(2)}) collective-permute-start(bf16[64,640]{1,0:T(8,128)(2,1)S(1)} %get-tuple-element.55.refs_0_), channel_id=1, source_target_pairs={{0,2},{1,3},{2,0},{3,1},{4,6},{5,7},{6,4},{7,5},{8,10},{9,11},{10,... | collective-permute-start | bytes 245768 | tf_op jit(solution)/shard_map/ppermute | solution.py:231
  35.5 6.8 %collective-permute-start.18 = (bf16[64,640]{1,0:T(8,128)(2,1)S(1)}, bf16[64,640]{1,0:T(8,128)(2,1)S(1)}, u32[]{:S(2)}, u32[]{:S(2)}) collective-permute-start(bf16[64,640]{1,0:T(8,128)(2,1)S(1)} %shard_map.58.refs_0_), channel_id=1, source_target_pairs={{0,3},{1,2},{2,1},{3,0},{4,7},{5,6},{6,5},{7,4},{8,11},{9,10},{10,... | collective-permute-start | bytes 245768 | tf_op jit(solution)/shard_map/ppermute | solution.py:231
  36.0 8.2 %collective-permute-start.17 = (bf16[64,640]{1,0:T(8,128)(2,1)S(1)}, bf16[64,640]{1,0:T(8,128)(2,1)S(1)}, u32[]{:S(2)}, u32[]{:S(2)}) collective-permute-start(bf16[64,640]{1,0:T(8,128)(2,1)S(1)} %shard_map.58.refs_0_), channel_id=1, source_target_pairs={{0,2},{1,3},{2,0},{3,1},{4,6},{5,7},{6,4},{7,5},{8,10},{9,11},{10,... | collective-permute-start | bytes 245768 | tf_op jit(solution)/shard_map/ppermute | solution.py:231
  38.0 6.2 %collective-permute-start.16 = (bf16[64,640]{1,0:T(8,128)(2,1)S(1)}, bf16[64,640]{1,0:T(8,128)(2,1)S(1)}, u32[]{:S(2)}, u32[]{:S(2)}) collective-permute-start(bf16[64,640]{1,0:T(8,128)(2,1)S(1)} %shard_map.58.refs_0_), channel_id=1, source_target_pairs={{0,1},{1,0},{2,3},{3,2},{4,5},{5,4},{6,7},{7,6},{8,9},{9,8},{10,11... | collective-permute-start | bytes 245768 | tf_op jit(solution)/shard_map/ppermute | solution.py:231
  40.7 9.1 %collective-permute-start.21 = (bf16[64,640]{1,0:T(8,128)(2,1)S(1)}, bf16[64,640]{1,0:T(8,128)(2,1)S(1)}, u32[]{:S(2)}, u32[]{:S(2)}) collective-permute-start(bf16[64,640]{1,0:T(8,128)(2,1)S(1)} %get-tuple-element.55.refs_0_), channel_id=1, source_target_pairs={{0,3},{1,2},{2,1},{3,0},{4,7},{5,6},{6,5},{7,4},{8,11},{9,10},{10,... | collective-permute-start | bytes 245768 | tf_op jit(solution)/shard_map/ppermute | solution.py:231
  42.3 7.6 %collective-permute-start.20 = (bf16[64,640]{1,0:T(8,128)(2,1)S(1)}, bf16[64,640]{1,0:T(8,128)(2,1)S(1)}, u32[]{:S(2)}, u32[]{:S(2)}) collective-permute-start(bf16[64,640]{1,0:T(8,128)(2,1)S(1)} %get-tuple-element.55.refs_0_), channel_id=1, source_target_pairs={{0,1},{1,0},{2,3},{3,2},{4,5},{5,4},{6,7},{7,6},{8,9},{9,8},{10,11... | collective-permute-start | bytes 245768 | tf_op jit(solution)/shard_map/ppermute | solution.py:231
  44.2 7.7 %collective-permute-start.25 = (bf16[64,1024]{1,0:T(8,128)(2,1)S(1)}, bf16[64,1024]{1,0:T(8,128)(2,1)S(1)}, u32[]{:S(2)}, u32[]{:S(2)}) collective-permute-start(bf16[64,1024]{1,0:T(8,128)(2,1)S(1)} %shard_map.59.after.refs_0_), channel_id=1, source_target_pairs={{0,3},{1,2},{2,1},{3,0},{4,7},{5,6},{6,5},{7,4},{8,11},{9,10},{10,... | collective-permute-start | bytes 393224 | tf_op jit(solution)/shard_map/ppermute | solution.py:231
  44.7 7.2 %collective-permute-start.24 = (bf16[64,1024]{1,0:T(8,128)(2,1)S(1)}, bf16[64,1024]{1,0:T(8,128)(2,1)S(1)}, u32[]{:S(2)}, u32[]{:S(2)}) collective-permute-start(bf16[64,1024]{1,0:T(8,128)(2,1)S(1)} %shard_map.59.after.refs_0_), channel_id=1, source_target_pairs={{0,2},{1,3},{2,0},{3,1},{4,6},{5,7},{6,4},{7,5},{8,10},{9,11},{10,... | collective-permute-start | bytes 393224 | tf_op jit(solution)/shard_map/ppermute | solution.py:231
  46.2 6.3 %collective-permute-start.23 = (bf16[64,1024]{1,0:T(8,128)(2,1)S(1)}, bf16[64,1024]{1,0:T(8,128)(2,1)S(1)}, u32[]{:S(2)}, u32[]{:S(2)}) collective-permute-start(bf16[64,1024]{1,0:T(8,128)(2,1)S(1)} %shard_map.59.after.refs_0_), channel_id=1, source_target_pairs={{0,1},{1,0},{2,3},{3,2},{4,5},{5,4},{6,7},{7,6},{8,9},{9,8},{10,11... | collective-permute-start | bytes 393224 | tf_op jit(solution)/shard_map/ppermute | solution.py:231
  49.8 2.7 %collective-permute-start.22 = (bf16[128,512]{1,0:T(8,128)(2,1)S(1)}, bf16[128,512]{1,0:T(8,128)(2,1)S(1)}, u32[]{:S(2)}, u32[]{:S(2)}) collective-permute-start(bf16[128,512]{1,0:T(8,128)(2,1)S(1)} %get-tuple-element.59), channel_id=1, source_target_pairs={{0,8},{8,0},{1,9},{9,1},{2,10},{10,2},{3,11},{11,3},{4,12},{12,4},... | collective-permute-start | bytes 393224 | tf_op jit(solution)/shard_map/ppermute | solution.py:335

commit v19 on v18

--- a/solution.py
+++ b/solution.py
@@ -328,7 +328,7 @@
             [pltpu.VMEM((GROUP, size // 2, factor), BF16), pltpu.VMEM((width, width), BF16)],
         )(*through, after, *pieces)
 
-    total = exchange(total, (*out, act[2]))
+    total = exchange(total, (*out, act[3]))
     grad = send([total] * GROUP)
     out_inv, give_cot = inverse(out, total, give_cot)
     (act_inv,) = inverse(act, total)

time: 54.3 us -> 54.1 us (level)
  waiting for transfers between devices: 13.8 us -> 12.7 us
  starting transfers between devices: 30.1 us -> 31 us
    ppermute x18, waiting for transfers between devices: 11.3 us -> 10.2 us  [send(): lax.ppermute(parts[step], ('near', 'side'), [(i, i ^ step) for i in range...]
    ppermute x18, starting transfers between devices: 23.8 us -> 24.7 us  [send(): lax.ppermute(parts[step], ('near', 'side'), [(i, i ^ step) for i in range...]
where the time goes in v19:
time: 54.1 us; the launch traced here: 54 us
  starting transfers between devices  31 us (57%)
  waiting for transfers between devices  12.7 us (23%)
  Pallas kernels  8.27 us (15%)
  other arithmetic  1.18 us (2%)
  between operations  0.81 us (1%)
    ppermute x18, starting transfers between devices, send(): lax.ppermute(parts[step], ('near', 'side'), [(i, i ^ step) for i in range...  24.7 us
    ppermute x18, waiting for transfers between devices, send(): lax.ppermute(parts[step], ('near', 'side'), [(i, i ^ step) for i in range...  10.2 us
    ppermute x3, starting transfers between devices, exchange(): got = lax.ppermute(value, 'far', route)  4.27 us
    pallas_call x2, Pallas kernels, inverse(): call(functools.partial(through_kernel if through else inverse_kernel, cou...  4.06 us
    ppermute x1, waiting for transfers between devices, body(): upstream = lax.ppermute(down, 'row', [(r, r - 1) for r in range(1, pairs)])  1.69 us
    pallas_call x1, Pallas kernels, body(): call(update_kernel, 10 * width ** 3, [array(width, width, dtype=F32), arr...  1.63 us
    ppermute x1, starting transfers between devices, body(): upstream = lax.ppermute(down, 'row', [(r, r - 1) for r in range(1, pairs)])  1.29 us
    select_n x2, other arithmetic, near_copy(): return jnp.where(core > 1, jnp.zeros_like(value), value)  1.18 us
  transfers between devices with their start and end apart: 26, of which 12 were waited for; matrix products, arithmetic and copies ran while one was open for 2% of the time, Pallas kernels for 11%

profile of v19, /device:TPU:0, one launch (start us, length us, event | category | flops | bytes accessed | tf_op | source)
XLA Modules:
  0.0 54.0 jit_solution(6606334582165665640)
XLA Ops:
  0.6 0.5 collective-permute-start
  1.1 0.1 collective-permute-start.1
  1.2 0.0 copy-start
  1.2 1.1 %broadcast_select_fusion.weight = bf16[512,512]{1,0:T(8,128)(2,1)S(1)} fusion(pred[]{:T(512)S(6)} %gt.2, bf16[1,512,512]{2,1,0:T(8,128)(2,1)} %param.4), kind=kLoop, calls=%fused_computation | loop fusion | flops 262144 | bytes 1048577 | tf_op jit(solution)/shard_map/jit(_where)/select_n | solution.py:263
  2.4 0.0 copy-done
  2.4 0.0 copy-done.1
  2.5 0.8 %collective-permute-done.1.partner_local = bf16[2,128,512]{2,1,0:T(8,128)(2,1)S(1)} collective-permute-done((bf16[2,128,512]{2,1,0:T(8,128)(2,1)}, bf16[2,128,512]{2,1,0:T(8,128)(2,1)S(1)}, u32[]{:S(2)}, u32[]{:S(2)}) %collective-permute-start.1) | collective-permute-done | bytes 262176 | tf_op jit(solution)/shard_map/ppermute | solution.py:266
  3.3 0.0 collective-permute-done.partner
  3.3 0.9 %shard_map.50 = (bf16[512,512]{1,0:T(8,128)(2,1)S(1)}, bf16[2,128,512]{2,1,0:T(8,128)(2,1)S(1)}, bf16[128,512]{1,0:T(8,128)(2,1)S(1)}, f32[128,512]{1,0:T(8,128)...) custom-call(bf16[512,512]{1,0:T(8,128)(2,1)S(1)} %broadcast_select_fusion.weight, ...), custom_call_target="tpu_custom_call" | custom-call | flops 268435456 | bytes 1048576 | tf_op jit(solution)/shard_map/pallas_call | solution.py:269
  4.2 1.3 %collective-permute-start.2 = (bf16[128,512]{1,0:T(8,128)(2,1)S(1)}, bf16[128,512]{1,0:T(8,128)(2,1)S(1)}, u32[]{:S(2)}, u32[]{:S(2)}) collective-permute-start(bf16[128,512]{1,0:T(8,128)(2,1)S(1)} %get-tuple-element.36.after), channel_id=1, source_target_pairs={{16,0},{17,1},{18,2},{19,3},{20,4},{21,5},{22,6},{23,7},{24,8},{25... | collective-permute-start | bytes 393224 | tf_op jit(solution)/shard_map/ppermute | solution.py:277
  5.5 0.4 shard_map.52
  5.9 4.0 %collective-permute-start.4 = (bf16[64,640]{1,0:T(8,128)(2,1)S(1)}, bf16[64,640]{1,0:T(8,128)(2,1)S(1)}, u32[]{:S(2)}, u32[]{:S(2)}) collective-permute-start(bf16[64,640]{1,0:T(8,128)(2,1)S(1)} %get-tuple-element.41), channel_id=1, source_target_pairs={{0,3},{1,2},{2,1},{3,0},{4,7},{5,6},{6,5},{7,4},{8,11},{9,10},{10,... | collective-permute-start | bytes 245768 | tf_op jit(solution)/shard_map/ppermute | solution.py:231
  9.8 0.5 collective-permute-start.5
  10.4 0.1 collective-permute-start.6
  10.5 1.7 %collective-permute-done.2.arrived = bf16[128,512]{1,0:T(8,128)(2,1)S(1)} collective-permute-done((bf16[128,512]{1,0:T(8,128)(2,1)S(1)}, bf16[128,512]{1,0:T(8,128)(2,1)S(1)}, u32[]{:S(2)}, u32[]{:S(2)}) %collective-permute-start.2) | collective-permute-done | bytes 131104 | tf_op jit(solution)/shard_map/ppermute | solution.py:277
  12.2 0.5 %shard_map.51 = (bf16[128,512]{1,0:T(8,128)(2,1)S(1)}, bf16[128,512]{1,0:T(8,128)(2,1)S(1)}, bf16[128,512]{1,0:T(8,128)(2,1)S(1)}, bf16[128,512]{1,0:T(8,128)(2,1)S(1)}) custom-call(bf16[512,512]{1,0:T(8,128)(2,1)S(1)} %get-tuple-element.33.own, bf16[512,512]{1,0:T(8,128)(2,1)S(1)} %collective-permute-done.partner, ...), custom_call_target="tpu_custom_call" | custom-call | flops 2147483648 | bytes 1048576 | tf_op jit(solution)/shard_map/pallas_call | solution.py:294
  12.7 0.1 collective-permute-start.3
  12.8 0.0 collective-permute-done.4.refs_1_
  12.8 1.5 %collective-permute-done.5.refs_2_ = bf16[64,640]{1,0:T(8,128)(2,1)S(1)} collective-permute-done((bf16[64,640]{1,0:T(8,128)(2,1)S(1)}, bf16[64,640]{1,0:T(8,128)(2,1)S(1)}, u32[]{:S(2)}, u32[]{:S(2)}) %collective-permute-start.5) | collective-permute-done | bytes 81952 | tf_op jit(solution)/shard_map/ppermute | solution.py:231
  14.3 0.5 collective-permute-done.6.refs_3_
  14.8 2.7 %collective-permute-start.13 = (bf16[64,640]{1,0:T(8,128)(2,1)S(1)}, bf16[64,640]{1,0:T(8,128)(2,1)S(1)}, u32[]{:S(2)}, u32[]{:S(2)}) collective-permute-start(bf16[64,640]{1,0:T(8,128)(2,1)S(1)} %shard_map.53.after.left), channel_id=1, source_target_pairs={{0,4},{4,0},{1,5},{5,1},{2,6},{6,2},{3,7},{7,3},{8,12},{12,8},{9,1... | collective-permute-start | bytes 245768 | tf_op jit(solution)/shard_map/ppermute | solution.py:239
  17.5 0.0 collective-permute-done.3.dh_got
  17.5 0.5 shard_map.54
  18.0 1.5 %collective-permute-start.10 = (bf16[64,640]{1,0:T(8,128)(2,1)S(1)}, bf16[64,640]{1,0:T(8,128)(2,1)S(1)}, u32[]{:S(2)}, u32[]{:S(2)}) collective-permute-start(bf16[64,640]{1,0:T(8,128)(2,1)S(1)} %get-tuple-element.49), channel_id=1, source_target_pairs={{0,3},{1,2},{2,1},{3,0},{4,7},{5,6},{6,5},{7,4},{8,11},{9,10},{10,... | collective-permute-start | bytes 245768 | tf_op jit(solution)/shard_map/ppermute | solution.py:231
  19.5 1.3 %collective-permute-start.11 = (bf16[64,640]{1,0:T(8,128)(2,1)S(1)}, bf16[64,640]{1,0:T(8,128)(2,1)S(1)}, u32[]{:S(2)}, u32[]{:S(2)}) collective-permute-start(bf16[64,640]{1,0:T(8,128)(2,1)S(1)} %get-tuple-element.50), channel_id=1, source_target_pairs={{0,1},{1,0},{2,3},{3,2},{4,5},{5,4},{6,7},{7,6},{8,9},{9,8},{10,11... | collective-permute-start | bytes 245768 | tf_op jit(solution)/shard_map/ppermute | solution.py:231
  20.8 0.8 %collective-permute-start.12 = (bf16[64,640]{1,0:T(8,128)(2,1)S(1)}, bf16[64,640]{1,0:T(8,128)(2,1)S(1)}, u32[]{:S(2)}, u32[]{:S(2)}) collective-permute-start(bf16[64,640]{1,0:T(8,128)(2,1)S(1)} %get-tuple-element.51), channel_id=1, source_target_pairs={{0,2},{1,3},{2,0},{3,1},{4,6},{5,7},{6,4},{7,5},{8,10},{9,11},{10,... | collective-permute-start | bytes 245768 | tf_op jit(solution)/shard_map/ppermute | solution.py:231
  21.6 1.4 %collective-permute-start.7 = (bf16[64,1024]{1,0:T(8,128)(2,1)S(1)}, bf16[64,1024]{1,0:T(8,128)(2,1)S(1)}, u32[]{:S(2)}, u32[]{:S(2)}) collective-permute-start(bf16[64,1024]{1,0:T(8,128)(2,1)S(1)} %get-tuple-element.45), channel_id=1, source_target_pairs={{0,3},{1,2},{2,1},{3,0},{4,7},{5,6},{6,5},{7,4},{8,11},{9,10},{10,... | collective-permute-start | bytes 393224 | tf_op jit(solution)/shard_map/ppermute | solution.py:231
  23.0 0.0 collective-permute-done.13.right
  23.0 1.3 %collective-permute-start.8 = (bf16[64,1024]{1,0:T(8,128)(2,1)S(1)}, bf16[64,1024]{1,0:T(8,128)(2,1)S(1)}, u32[]{:S(2)}, u32[]{:S(2)}) collective-permute-start(bf16[64,1024]{1,0:T(8,128)(2,1)S(1)} %get-tuple-element.46), channel_id=1, source_target_pairs={{0,1},{1,0},{2,3},{3,2},{4,5},{5,4},{6,7},{7,6},{8,9},{9,8},{10,11... | collective-permute-start | bytes 393224 | tf_op jit(solution)/shard_map/ppermute | solution.py:231
  24.3 0.0 collective-permute-done.10.refs_1_
  24.3 1.2 %collective-permute-start.9 = (bf16[64,1024]{1,0:T(8,128)(2,1)S(1)}, bf16[64,1024]{1,0:T(8,128)(2,1)S(1)}, u32[]{:S(2)}, u32[]{:S(2)}) collective-permute-start(bf16[64,1024]{1,0:T(8,128)(2,1)S(1)} %get-tuple-element.47), channel_id=1, source_target_pairs={{0,2},{1,3},{2,0},{3,1},{4,6},{5,7},{6,4},{7,5},{8,10},{9,11},{10,... | collective-permute-start | bytes 393224 | tf_op jit(solution)/shard_map/ppermute | solution.py:231
  25.5 0.0 collective-permute-done.11.refs_2_
  25.5 0.6 %collective-permute-done.12.refs_3_ = bf16[64,640]{1,0:T(8,128)(2,1)S(1)} collective-permute-done((bf16[64,640]{1,0:T(8,128)(2,1)S(1)}, bf16[64,640]{1,0:T(8,128)(2,1)S(1)}, u32[]{:S(2)}, u32[]{:S(2)}) %collective-permute-start.12) | collective-permute-done | bytes 81952 | tf_op jit(solution)/shard_map/ppermute | solution.py:231
  26.2 1.2 %collective-permute-start.15 = (bf16[64,640]{1,0:T(8,128)(2,1)S(1)}, bf16[64,640]{1,0:T(8,128)(2,1)S(1)}, u32[]{:S(2)}, u32[]{:S(2)}) collective-permute-start(bf16[64,640]{1,0:T(8,128)(2,1)S(1)} %get-tuple-element.54.left), channel_id=1, source_target_pairs={{0,4},{4,0},{1,5},{5,1},{2,6},{6,2},{3,7},{7,3},{8,12},{12,8},{9,1... | collective-permute-start | bytes 245768 | tf_op jit(solution)/shard_map/ppermute | solution.py:239
  27.5 2.6 %collective-permute-done.7.refs_1_ = bf16[64,1024]{1,0:T(8,128)(2,1)S(1)} collective-permute-done((bf16[64,1024]{1,0:T(8,128)(2,1)S(1)}, bf16[64,1024]{1,0:T(8,128)(2,1)S(1)}, u32[]{:S(2)}, u32[]{:S(2)}) %collective-permute-start.7) | collective-permute-done | bytes 131104 | tf_op jit(solution)/shard_map/ppermute | solution.py:231
  30.0 0.2 collective-permute-done.8.refs_2_
  30.3 2.3 %collective-permute-done.9.refs_3_ = bf16[64,1024]{1,0:T(8,128)(2,1)S(1)} collective-permute-done((bf16[64,1024]{1,0:T(8,128)(2,1)S(1)}, bf16[64,1024]{1,0:T(8,128)(2,1)S(1)}, u32[]{:S(2)}, u32[]{:S(2)}) %collective-permute-start.9) | collective-permute-done | bytes 131104 | tf_op jit(solution)/shard_map/ppermute | solution.py:231
  32.6 0.1 shard_map.57
  32.7 0.4 collective-permute-start.14
  33.0 2.9 %collective-permute-start.19 = (bf16[64,640]{1,0:T(8,128)(2,1)S(1)}, bf16[64,640]{1,0:T(8,128)(2,1)S(1)}, u32[]{:S(2)}, u32[]{:S(2)}) collective-permute-start(bf16[64,640]{1,0:T(8,128)(2,1)S(1)} %get-tuple-element.55.refs_0_), channel_id=1, source_target_pairs={{0,3},{1,2},{2,1},{3,0},{4,7},{5,6},{6,5},{7,4},{8,11},{9,10},{10,... | collective-permute-start | bytes 245768 | tf_op jit(solution)/shard_map/ppermute | solution.py:231
  35.9 0.0 collective-permute-done.15.right
  35.9 0.1 collective-permute-start.18
  36.1 2.4 %collective-permute-start.17 = (bf16[64,640]{1,0:T(8,128)(2,1)S(1)}, bf16[64,640]{1,0:T(8,128)(2,1)S(1)}, u32[]{:S(2)}, u32[]{:S(2)}) collective-permute-start(bf16[64,640]{1,0:T(8,128)(2,1)S(1)} %shard_map.58.refs_0_), channel_id=1, source_target_pairs={{0,2},{1,3},{2,0},{3,1},{4,6},{5,7},{6,4},{7,5},{8,10},{9,11},{10,... | collective-permute-start | bytes 245768 | tf_op jit(solution)/shard_map/ppermute | solution.py:231
  38.5 1.0 %collective-permute-start.16 = (bf16[64,640]{1,0:T(8,128)(2,1)S(1)}, bf16[64,640]{1,0:T(8,128)(2,1)S(1)}, u32[]{:S(2)}, u32[]{:S(2)}) collective-permute-start(bf16[64,640]{1,0:T(8,128)(2,1)S(1)} %shard_map.58.refs_0_), channel_id=1, source_target_pairs={{0,1},{1,0},{2,3},{3,2},{4,5},{5,4},{6,7},{7,6},{8,9},{9,8},{10,11... | collective-permute-start | bytes 245768 | tf_op jit(solution)/shard_map/ppermute | solution.py:231
  39.5 1.0 %collective-permute-done.19.refs_4_.refs_3_ = bf16[64,640]{1,0:T(8,128)(2,1)S(1)} collective-permute-done((bf16[64,640]{1,0:T(8,128)(2,1)S(1)}, bf16[64,640]{1,0:T(8,128)(2,1)S(1)}, u32[]{:S(2)}, u32[]{:S(2)}) %collective-permute-start.19) | collective-permute-done | bytes 81952 | tf_op jit(solution)/shard_map/ppermute | solution.py:231
  40.5 1.3 %collective-permute-start.21 = (bf16[64,640]{1,0:T(8,128)(2,1)S(1)}, bf16[64,640]{1,0:T(8,128)(2,1)S(1)}, u32[]{:S(2)}, u32[]{:S(2)}) collective-permute-start(bf16[64,640]{1,0:T(8,128)(2,1)S(1)} %get-tuple-element.55.refs_0_), channel_id=1, source_target_pairs={{0,2},{1,3},{2,0},{3,1},{4,6},{5,7},{6,4},{7,5},{8,10},{9,11},{10,... | collective-permute-start | bytes 245768 | tf_op jit(solution)/shard_map/ppermute | solution.py:231
  41.8 0.5 collective-permute-done.18.refs_3_
  42.3 1.4 %collective-permute-start.20 = (bf16[64,640]{1,0:T(8,128)(2,1)S(1)}, bf16[64,640]{1,0:T(8,128)(2,1)S(1)}, u32[]{:S(2)}, u32[]{:S(2)}) collective-permute-start(bf16[64,640]{1,0:T(8,128)(2,1)S(1)} %get-tuple-element.55.refs_0_), channel_id=1, source_target_pairs={{0,1},{1,0},{2,3},{3,2},{4,5},{5,4},{6,7},{7,6},{8,9},{9,8},{10,11... | collective-permute-start | bytes 245768 | tf_op jit(solution)/shard_map/ppermute | solution.py:231
  43.6 0.3 collective-permute-done.17.refs_2_
  43.9 0.0 collective-permute-done.16.refs_1_
  43.9 0.0 collective-permute-done.14.right
  44.0 0.9 %collective-permute-start.25 = (bf16[64,1024]{1,0:T(8,128)(2,1)S(1)}, bf16[64,1024]{1,0:T(8,128)(2,1)S(1)}, u32[]{:S(2)}, u32[]{:S(2)}) collective-permute-start(bf16[64,1024]{1,0:T(8,128)(2,1)S(1)} %shard_map.59.after.refs_0_), channel_id=1, source_target_pairs={{0,3},{1,2},{2,1},{3,0},{4,7},{5,6},{6,5},{7,4},{8,11},{9,10},{10,... | collective-permute-start | bytes 393224 | tf_op jit(solution)/shard_map/ppermute | solution.py:231
  44.8 1.3 %collective-permute-start.24 = (bf16[64,1024]{1,0:T(8,128)(2,1)S(1)}, bf16[64,1024]{1,0:T(8,128)(2,1)S(1)}, u32[]{:S(2)}, u32[]{:S(2)}) collective-permute-start(bf16[64,1024]{1,0:T(8,128)(2,1)S(1)} %shard_map.59.after.refs_0_), channel_id=1, source_target_pairs={{0,2},{1,3},{2,0},{3,1},{4,6},{5,7},{6,4},{7,5},{8,10},{9,11},{10,... | collective-permute-start | bytes 393224 | tf_op jit(solution)/shard_map/ppermute | solution.py:231
  46.2 1.4 %collective-permute-start.23 = (bf16[64,1024]{1,0:T(8,128)(2,1)S(1)}, bf16[64,1024]{1,0:T(8,128)(2,1)S(1)}, u32[]{:S(2)}, u32[]{:S(2)}) collective-permute-start(bf16[64,1024]{1,0:T(8,128)(2,1)S(1)} %shard_map.59.after.refs_0_), channel_id=1, source_target_pairs={{0,1},{1,0},{2,3},{3,2},{4,5},{5,4},{6,7},{7,6},{8,9},{9,8},{10,11... | collective-permute-start | bytes 393224 | tf_op jit(solution)/shard_map/ppermute | solution.py:231
  47.5 2.0 %shard_map.61 = (bf16[512,512]{1,0:T(8,128)(2,1)S(1)}, bf16[128,512]{1,0:T(8,128)(2,1)S(1)}) custom-call(bf16[128,512]{1,0:T(8,128)(2,1)S(1)} %get-tuple-element.56.through, bf16[64,1024]{1,0:T(8,128)(2,1)S(1)} %shard_map.59.after.refs_0_, bf16[64,640]{1,0:T(8,128)(2,1)S(1)} %shard_map.58.refs_0_, bf16[64,640]{1,0:T(8,128)(2,1)S(1)} %collective-permute-done.16.refs_1_, ...), custom_call_target="tpu_custom_call" | custom-call | flops 2684354560 | bytes 1048576 | tf_op jit(solution)/shard_map/pallas_call | solution.py:323
  49.6 0.0 collective-permute-done.21.refs_2_
  49.6 0.1 collective-permute-start.22
  49.7 0.0 collective-permute-done.20.refs_1_
  49.7 2.0 %shard_map.60.act_inv = bf16[512,512]{1,0:T(8,128)(2,1)S(1)} custom-call(bf16[64,1024]{1,0:T(8,128)(2,1)S(1)} %shard_map.59.after.refs_0_, bf16[64,640]{1,0:T(8,128)(2,1)S(1)} %get-tuple-element.55.refs_0_, bf16[64,640]{1,0:T(8,128)(2,1)S(1)} %collective-permute-done.20.refs_1_, bf16[64,640]{1,0:T(8,128)(2,1)S(1)} %collective-permute-done.21.refs_2_, ...), custom_call_target="tpu_custom_call" | custom-call | flops 2684354560 | bytes 1048576 | tf_op jit(solution)/shard_map/pallas_call | solution.py:323
  51.7 0.0 collective-permute-done.25.refs_3_
  51.7 0.0 collective-permute-done.24.refs_2_
  51.7 0.6 %collective-permute-done.23.refs_1_ = bf16[64,1024]{1,0:T(8,128)(2,1)S(1)} collective-permute-done((bf16[64,1024]{1,0:T(8,128)(2,1)S(1)}, bf16[64,1024]{1,0:T(8,128)(2,1)S(1)}, u32[]{:S(2)}, u32[]{:S(2)}) %collective-permute-start.23) | collective-permute-done | bytes 131104 | tf_op jit(solution)/shard_map/ppermute | solution.py:231
  52.3 0.0 collective-permute-done.22.other_cot
  52.3 1.6 %shard_map.62 = (f32[512,512]{1,0:T(8,128)}, bf16[2,128,512]{2,1,0:T(8,128)(2,1)}) custom-call(bf16[512,512]{1,0:T(8,128)(2,1)S(1)} %shard_map.60.act_inv, bf16[512,512]{1,0:T(8,128)(2,1)S(1)} %get-tuple-element.57.out_inv, bf16[128,512]{1,0:T(8,128)(2,1)S(1)} %get-tuple-element.58.own_cot, bf16[128,512]{1,0:T(8,128)(2,1)S(1)} %collective-permute-done.22.other_cot, ...), custom_call_target="tpu_custom_call" | custom-call | flops 1342177280 | bytes 1048576 | tf_op jit(solution)/shard_map/pallas_call | solution.py:336
  (7 shorter events, 0.2 us)
Async XLA Ops:
  0.6 2.6 %collective-permute-start = (bf16[512,512]{1,0:T(8,128)(2,1)}, bf16[512,512]{1,0:T(8,128)(2,1)S(1)}, u32[]{:S(2)}, u32[]{:S(2)}) collective-permute-start(bf16[512,512]{1,0:T(8,128)(2,1)} %bitcast.6), channel_id=1, source_target_pairs={{0,8},{8,0},{1,9},{9,1},{2,10},{10,2},{3,11},{11,3},{4,12},{12,4},... | collective-permute-start | bytes 1572872 | tf_op jit(solution)/shard_map/ppermute | solution.py:265
  1.1 2.1 %collective-permute-start.1 = (bf16[2,128,512]{2,1,0:T(8,128)(2,1)}, bf16[2,128,512]{2,1,0:T(8,128)(2,1)S(1)}, u32[]{:S(2)}, u32[]{:S(2)}) collective-permute-start(bf16[2,128,512]{2,1,0:T(8,128)(2,1)} %bitcast.7), channel_id=1, source_target_pairs={{0,8},{8,0},{1,9},{9,1},{2,10},{10,2},{3,11},{11,3},{4,12},{12,4},... | collective-permute-start | bytes 786440 | tf_op jit(solution)/shard_map/ppermute | solution.py:266
  1.2 1.1 %copy-start = (bf16[2,128,512]{2,1,0:T(8,128)(2,1)S(1)}, bf16[2,128,512]{2,1,0:T(8,128)(2,1)}, u32[]{:S(2)}) copy-start(bf16[2,128,512]{2,1,0:T(8,128)(2,1)} %param.5) | copy-start | bytes 786436
  1.2 1.2 %copy-start.1 = (bf16[1,2,128,512]{3,2,1,0:T(8,128)(2,1)S(1)}, bf16[1,2,128,512]{3,2,1,0:T(8,128)(2,1)}, u32[]{:S(2)}) copy-start(bf16[1,2,128,512]{3,2,1,0:T(8,128)(2,1)} %param.3) | copy-start | bytes 786436
  4.2 8.0 %collective-permute-start.2 = (bf16[128,512]{1,0:T(8,128)(2,1)S(1)}, bf16[128,512]{1,0:T(8,128)(2,1)S(1)}, u32[]{:S(2)}, u32[]{:S(2)}) collective-permute-start(bf16[128,512]{1,0:T(8,128)(2,1)S(1)} %get-tuple-element.36.after), channel_id=1, source_target_pairs={{16,0},{17,1},{18,2},{19,3},{20,4},{21,5},{22,6},{23,7},{24,8},{25... | collective-permute-start | bytes 393224 | tf_op jit(solution)/shard_map/ppermute | solution.py:277
  5.9 6.9 %collective-permute-start.4 = (bf16[64,640]{1,0:T(8,128)(2,1)S(1)}, bf16[64,640]{1,0:T(8,128)(2,1)S(1)}, u32[]{:S(2)}, u32[]{:S(2)}) collective-permute-start(bf16[64,640]{1,0:T(8,128)(2,1)S(1)} %get-tuple-element.41), channel_id=1, source_target_pairs={{0,3},{1,2},{2,1},{3,0},{4,7},{5,6},{6,5},{7,4},{8,11},{9,10},{10,... | collective-permute-start | bytes 245768 | tf_op jit(solution)/shard_map/ppermute | solution.py:231
  9.8 4.5 %collective-permute-start.5 = (bf16[64,640]{1,0:T(8,128)(2,1)S(1)}, bf16[64,640]{1,0:T(8,128)(2,1)S(1)}, u32[]{:S(2)}, u32[]{:S(2)}) collective-permute-start(bf16[64,640]{1,0:T(8,128)(2,1)S(1)} %get-tuple-element.42), channel_id=1, source_target_pairs={{0,1},{1,0},{2,3},{3,2},{4,5},{5,4},{6,7},{7,6},{8,9},{9,8},{10,11... | collective-permute-start | bytes 245768 | tf_op jit(solution)/shard_map/ppermute | solution.py:231
  10.4 4.4 %collective-permute-start.6 = (bf16[64,640]{1,0:T(8,128)(2,1)S(1)}, bf16[64,640]{1,0:T(8,128)(2,1)S(1)}, u32[]{:S(2)}, u32[]{:S(2)}) collective-permute-start(bf16[64,640]{1,0:T(8,128)(2,1)S(1)} %get-tuple-element.43), channel_id=1, source_target_pairs={{0,2},{1,3},{2,0},{3,1},{4,6},{5,7},{6,4},{7,5},{8,10},{9,11},{10,... | collective-permute-start | bytes 245768 | tf_op jit(solution)/shard_map/ppermute | solution.py:231
  12.7 4.8 %collective-permute-start.3 = (bf16[128,512]{1,0:T(8,128)(2,1)S(1)}, bf16[128,512]{1,0:T(8,128)(2,1)S(1)}, u32[]{:S(2)}, u32[]{:S(2)}) collective-permute-start(bf16[128,512]{1,0:T(8,128)(2,1)S(1)} %get-tuple-element.39), channel_id=1, source_target_pairs={{0,8},{8,0},{1,9},{9,1},{2,10},{10,2},{3,11},{11,3},{4,12},{12,4},... | collective-permute-start | bytes 393224 | tf_op jit(solution)/shard_map/ppermute | solution.py:300
  14.8 8.2 %collective-permute-start.13 = (bf16[64,640]{1,0:T(8,128)(2,1)S(1)}, bf16[64,640]{1,0:T(8,128)(2,1)S(1)}, u32[]{:S(2)}, u32[]{:S(2)}) collective-permute-start(bf16[64,640]{1,0:T(8,128)(2,1)S(1)} %shard_map.53.after.left), channel_id=1, source_target_pairs={{0,4},{4,0},{1,5},{5,1},{2,6},{6,2},{3,7},{7,3},{8,12},{12,8},{9,1... | collective-permute-start | bytes 245768 | tf_op jit(solution)/shard_map/ppermute | solution.py:239
  18.0 6.3 %collective-permute-start.10 = (bf16[64,640]{1,0:T(8,128)(2,1)S(1)}, bf16[64,640]{1,0:T(8,128)(2,1)S(1)}, u32[]{:S(2)}, u32[]{:S(2)}) collective-permute-start(bf16[64,640]{1,0:T(8,128)(2,1)S(1)} %get-tuple-element.49), channel_id=1, source_target_pairs={{0,3},{1,2},{2,1},{3,0},{4,7},{5,6},{6,5},{7,4},{8,11},{9,10},{10,... | collective-permute-start | bytes 245768 | tf_op jit(solution)/shard_map/ppermute | solution.py:231
  19.5 6.0 %collective-permute-start.11 = (bf16[64,640]{1,0:T(8,128)(2,1)S(1)}, bf16[64,640]{1,0:T(8,128)(2,1)S(1)}, u32[]{:S(2)}, u32[]{:S(2)}) collective-permute-start(bf16[64,640]{1,0:T(8,128)(2,1)S(1)} %get-tuple-element.50), channel_id=1, source_target_pairs={{0,1},{1,0},{2,3},{3,2},{4,5},{5,4},{6,7},{7,6},{8,9},{9,8},{10,11... | collective-permute-start | bytes 245768 | tf_op jit(solution)/shard_map/ppermute | solution.py:231
  20.8 5.3 %collective-permute-start.12 = (bf16[64,640]{1,0:T(8,128)(2,1)S(1)}, bf16[64,640]{1,0:T(8,128)(2,1)S(1)}, u32[]{:S(2)}, u32[]{:S(2)}) collective-permute-start(bf16[64,640]{1,0:T(8,128)(2,1)S(1)} %get-tuple-element.51), channel_id=1, source_target_pairs={{0,2},{1,3},{2,0},{3,1},{4,6},{5,7},{6,4},{7,5},{8,10},{9,11},{10,... | collective-permute-start | bytes 245768 | tf_op jit(solution)/shard_map/ppermute | solution.py:231
  21.6 8.4 %collective-permute-start.7 = (bf16[64,1024]{1,0:T(8,128)(2,1)S(1)}, bf16[64,1024]{1,0:T(8,128)(2,1)S(1)}, u32[]{:S(2)}, u32[]{:S(2)}) collective-permute-start(bf16[64,1024]{1,0:T(8,128)(2,1)S(1)} %get-tuple-element.45), channel_id=1, source_target_pairs={{0,3},{1,2},{2,1},{3,0},{4,7},{5,6},{6,5},{7,4},{8,11},{9,10},{10,... | collective-permute-start | bytes 393224 | tf_op jit(solution)/shard_map/ppermute | solution.py:231
  23.0 7.3 %collective-permute-start.8 = (bf16[64,1024]{1,0:T(8,128)(2,1)S(1)}, bf16[64,1024]{1,0:T(8,128)(2,1)S(1)}, u32[]{:S(2)}, u32[]{:S(2)}) collective-permute-start(bf16[64,1024]{1,0:T(8,128)(2,1)S(1)} %get-tuple-element.46), channel_id=1, source_target_pairs={{0,1},{1,0},{2,3},{3,2},{4,5},{5,4},{6,7},{7,6},{8,9},{9,8},{10,11... | collective-permute-start | bytes 393224 | tf_op jit(solution)/shard_map/ppermute | solution.py:231
  24.3 8.3 %collective-permute-start.9 = (bf16[64,1024]{1,0:T(8,128)(2,1)S(1)}, bf16[64,1024]{1,0:T(8,128)(2,1)S(1)}, u32[]{:S(2)}, u32[]{:S(2)}) collective-permute-start(bf16[64,1024]{1,0:T(8,128)(2,1)S(1)} %get-tuple-element.47), channel_id=1, source_target_pairs={{0,2},{1,3},{2,0},{3,1},{4,6},{5,7},{6,4},{7,5},{8,10},{9,11},{10,... | collective-permute-start | bytes 393224 | tf_op jit(solution)/shard_map/ppermute | solution.py:231
  26.2 9.7 %collective-permute-start.15 = (bf16[64,640]{1,0:T(8,128)(2,1)S(1)}, bf16[64,640]{1,0:T(8,128)(2,1)S(1)}, u32[]{:S(2)}, u32[]{:S(2)}) collective-permute-start(bf16[64,640]{1,0:T(8,128)(2,1)S(1)} %get-tuple-element.54.left), channel_id=1, source_target_pairs={{0,4},{4,0},{1,5},{5,1},{2,6},{6,2},{3,7},{7,3},{8,12},{12,8},{9,1... | collective-permute-start | bytes 245768 | tf_op jit(solution)/shard_map/ppermute | solution.py:239
  32.7 11.3 %collective-permute-start.14 = (bf16[64,1024]{1,0:T(8,128)(2,1)S(1)}, bf16[64,1024]{1,0:T(8,128)(2,1)S(1)}, u32[]{:S(2)}, u32[]{:S(2)}) collective-permute-start(bf16[64,1024]{1,0:T(8,128)(2,1)S(1)} %get-tuple-element.53.left), channel_id=1, source_target_pairs={{0,4},{4,0},{1,5},{5,1},{2,6},{6,2},{3,7},{7,3},{8,12},{12,8},{9,1... | collective-permute-start | bytes 393224 | tf_op jit(solution)/shard_map/ppermute | solution.py:239
  33.0 7.4 %collective-permute-start.19 = (bf16[64,640]{1,0:T(8,128)(2,1)S(1)}, bf16[64,640]{1,0:T(8,128)(2,1)S(1)}, u32[]{:S(2)}, u32[]{:S(2)}) collective-permute-start(bf16[64,640]{1,0:T(8,128)(2,1)S(1)} %get-tuple-element.55.refs_0_), channel_id=1, source_target_pairs={{0,3},{1,2},{2,1},{3,0},{4,7},{5,6},{6,5},{7,4},{8,11},{9,10},{10,... | collective-permute-start | bytes 245768 | tf_op jit(solution)/shard_map/ppermute | solution.py:231
  35.9 6.4 %collective-permute-start.18 = (bf16[64,640]{1,0:T(8,128)(2,1)S(1)}, bf16[64,640]{1,0:T(8,128)(2,1)S(1)}, u32[]{:S(2)}, u32[]{:S(2)}) collective-permute-start(bf16[64,640]{1,0:T(8,128)(2,1)S(1)} %shard_map.58.refs_0_), channel_id=1, source_target_pairs={{0,3},{1,2},{2,1},{3,0},{4,7},{5,6},{6,5},{7,4},{8,11},{9,10},{10,... | collective-permute-start | bytes 245768 | tf_op jit(solution)/shard_map/ppermute | solution.py:231
  36.1 7.9 %collective-permute-start.17 = (bf16[64,640]{1,0:T(8,128)(2,1)S(1)}, bf16[64,640]{1,0:T(8,128)(2,1)S(1)}, u32[]{:S(2)}, u32[]{:S(2)}) collective-permute-start(bf16[64,640]{1,0:T(8,128)(2,1)S(1)} %shard_map.58.refs_0_), channel_id=1, source_target_pairs={{0,2},{1,3},{2,0},{3,1},{4,6},{5,7},{6,4},{7,5},{8,10},{9,11},{10,... | collective-permute-start | bytes 245768 | tf_op jit(solution)/shard_map/ppermute | solution.py:231
  38.5 5.4 %collective-permute-start.16 = (bf16[64,640]{1,0:T(8,128)(2,1)S(1)}, bf16[64,640]{1,0:T(8,128)(2,1)S(1)}, u32[]{:S(2)}, u32[]{:S(2)}) collective-permute-start(bf16[64,640]{1,0:T(8,128)(2,1)S(1)} %shard_map.58.refs_0_), channel_id=1, source_target_pairs={{0,1},{1,0},{2,3},{3,2},{4,5},{5,4},{6,7},{7,6},{8,9},{9,8},{10,11... | collective-permute-start | bytes 245768 | tf_op jit(solution)/shard_map/ppermute | solution.py:231
  40.5 9.1 %collective-permute-start.21 = (bf16[64,640]{1,0:T(8,128)(2,1)S(1)}, bf16[64,640]{1,0:T(8,128)(2,1)S(1)}, u32[]{:S(2)}, u32[]{:S(2)}) collective-permute-start(bf16[64,640]{1,0:T(8,128)(2,1)S(1)} %get-tuple-element.55.refs_0_), channel_id=1, source_target_pairs={{0,2},{1,3},{2,0},{3,1},{4,6},{5,7},{6,4},{7,5},{8,10},{9,11},{10,... | collective-permute-start | bytes 245768 | tf_op jit(solution)/shard_map/ppermute | solution.py:231
  42.3 7.4 %collective-permute-start.20 = (bf16[64,640]{1,0:T(8,128)(2,1)S(1)}, bf16[64,640]{1,0:T(8,128)(2,1)S(1)}, u32[]{:S(2)}, u32[]{:S(2)}) collective-permute-start(bf16[64,640]{1,0:T(8,128)(2,1)S(1)} %get-tuple-element.55.refs_0_), channel_id=1, source_target_pairs={{0,1},{1,0},{2,3},{3,2},{4,5},{5,4},{6,7},{7,6},{8,9},{9,8},{10,11... | collective-permute-start | bytes 245768 | tf_op jit(solution)/shard_map/ppermute | solution.py:231
  44.0 7.7 %collective-permute-start.25 = (bf16[64,1024]{1,0:T(8,128)(2,1)S(1)}, bf16[64,1024]{1,0:T(8,128)(2,1)S(1)}, u32[]{:S(2)}, u32[]{:S(2)}) collective-permute-start(bf16[64,1024]{1,0:T(8,128)(2,1)S(1)} %shard_map.59.after.refs_0_), channel_id=1, source_target_pairs={{0,3},{1,2},{2,1},{3,0},{4,7},{5,6},{6,5},{7,4},{8,11},{9,10},{10,... | collective-permute-start | bytes 393224 | tf_op jit(solution)/shard_map/ppermute | solution.py:231
  44.8 6.9 %collective-permute-start.24 = (bf16[64,1024]{1,0:T(8,128)(2,1)S(1)}, bf16[64,1024]{1,0:T(8,128)(2,1)S(1)}, u32[]{:S(2)}, u32[]{:S(2)}) collective-permute-start(bf16[64,1024]{1,0:T(8,128)(2,1)S(1)} %shard_map.59.after.refs_0_), channel_id=1, source_target_pairs={{0,2},{1,3},{2,0},{3,1},{4,6},{5,7},{6,4},{7,5},{8,10},{9,11},{10,... | collective-permute-start | bytes 393224 | tf_op jit(solution)/shard_map/ppermute | solution.py:231
  46.2 6.2 %collective-permute-start.23 = (bf16[64,1024]{1,0:T(8,128)(2,1)S(1)}, bf16[64,1024]{1,0:T(8,128)(2,1)S(1)}, u32[]{:S(2)}, u32[]{:S(2)}) collective-permute-start(bf16[64,1024]{1,0:T(8,128)(2,1)S(1)} %shard_map.59.after.refs_0_), channel_id=1, source_target_pairs={{0,1},{1,0},{2,3},{3,2},{4,5},{5,4},{6,7},{7,6},{8,9},{9,8},{10,11... | collective-permute-start | bytes 393224 | tf_op jit(solution)/shard_map/ppermute | solution.py:231
  49.6 2.8 %collective-permute-start.22 = (bf16[128,512]{1,0:T(8,128)(2,1)S(1)}, bf16[128,512]{1,0:T(8,128)(2,1)S(1)}, u32[]{:S(2)}, u32[]{:S(2)}) collective-permute-start(bf16[128,512]{1,0:T(8,128)(2,1)S(1)} %get-tuple-element.59), channel_id=1, source_target_pairs={{0,8},{8,0},{1,9},{9,1},{2,10},{10,2},{3,11},{11,3},{4,12},{12,4},... | collective-permute-start | bytes 393224 | tf_op jit(solution)/shard_map/ppermute | solution.py:335

commit v20 on v17

--- a/solution.py
+++ b/solution.py
@@ -66,22 +66,16 @@
     )
 
 
-def first_kernel(
-    weight, local, cot_last, partner, partner_local,
-    own, kept, last, slope_own, slope_partner, down,
-):
+def first_kernel(own, partner, local, partner_local, cot_last, slope_own, slope_partner, down):
     core = lax.axis_index("core")
-    last[...] = cot_last[core]
-    slope_own[...] = slope_of(local[core], weight[...])
+    slope_own[...] = slope_of(local[core], own[...])
     slope_partner[...] = slope_of(partner_local[core], partner[...])
 
     def run(odd, even):
-        cot = layer(last[...], odd[1][...], odd[0][...])[1]
+        cot = layer(cot_last[core], odd[1][...], odd[0][...])[1]
         down[...] = layer(cot, even[1][...], even[0][...])[1]
 
-    by_core(core, run, (weight, slope_own), (partner, slope_partner))
-    own[...] = weight[...]
-    kept[...] = local[...]
+    by_core(core, run, (own, slope_own), (partner, slope_partner))
 
 
 def sum_kernel(*refs):
@@ -97,7 +91,7 @@
 def layers_kernel(
     own, partner, slope_own, slope_partner, arrived, last, own_dh, give_dh, own_cot, give_cot
 ):
-    upstream = jnp.where(lax.axis_index("row") == lax.axis_size("row") - 1, last[...], arrived[...])
+    upstream = jnp.where(lax.axis_index("row") == lax.axis_size("row") - 1, last[lax.axis_index("core")], arrived[...])
 
     def run(odd, even):
         dh, cot = layer(upstream, odd[1][...], odd[0][...])
@@ -266,12 +260,10 @@
     partner_local = lax.ppermute(local, "core", SWAP)
     block = array(rows, width)
     slope = array(rows, width, dtype=F32)
-    own, kept, last, slope_own, slope_partner, down = call(
-        first_kernel,
-        8 * rows * width**2,
-        [array(width, width), array(micro, rows, width), block, slope, slope, block],
-        [VMEM] * 5,
-    )(near_copy(weight), near_copy(local), near_copy(cot_last), partner, partner_local)
+    own, kept, last = near_copy(weight), near_copy(local), near_copy(cot_last)
+    slope_own, slope_partner, down = call(
+        first_kernel, 8 * rows * width**2, [slope, slope, block], [VMEM] * 5
+    )(own, partner, kept, partner_local, last)
     first = down
     for turn in range(1, pairs):
         upstream = lax.ppermute(down, "row", [(r, r - 1) for r in range(1, pairs)])

time: 53.2 us -> 53.1 us (level)
  no operation moved by 1% of the time
where the time goes in v20:
time: 53.1 us; the launch traced here: 52.9 us
  starting transfers between devices  31.6 us (60%)
  waiting for transfers between devices  11.1 us (21%)
  Pallas kernels  8.2 us (15%)
  other arithmetic  1.18 us (2%)
  between operations  0.8 us (2%)
    ppermute x18, starting transfers between devices, send(): lax.ppermute(parts[step], ('near', 'side'), [(i, i ^ step) for i in range...  25.3 us
    ppermute x18, waiting for transfers between devices, send(): lax.ppermute(parts[step], ('near', 'side'), [(i, i ^ step) for i in range...  8.58 us
    ppermute x3, starting transfers between devices, exchange(): got = lax.ppermute(value, 'far', route)  4.2 us
    pallas_call x2, Pallas kernels, inverse(): call(functools.partial(through_kernel if through else inverse_kernel, cou...  4.05 us
    ppermute x1, waiting for transfers between devices, body(): upstream = lax.ppermute(down, 'row', [(r, r - 1) for r in range(1, pairs)])  1.7 us
    pallas_call x1, Pallas kernels, body(): call(update_kernel, 10 * width ** 3, [array(width, width, dtype=F32), arr...  1.63 us
    ppermute x1, starting transfers between devices, body(): upstream = lax.ppermute(down, 'row', [(r, r - 1) for r in range(1, pairs)])  1.29 us
    select_n x2, other arithmetic, near_copy(): return jnp.where(core > 1, jnp.zeros_like(value), value)  1.18 us
  transfers between devices with their start and end apart: 26, of which 10 were waited for; matrix products, arithmetic and copies ran while one was open for 2% of the time, Pallas kernels for 11%

profile of v20, /device:TPU:0, one launch (start us, length us, event | category | flops | bytes accessed | tf_op | source)
XLA Modules:
  0.0 52.9 jit_solution(3681809246414579296)
XLA Ops:
  0.6 0.5 collective-permute-start
  1.1 0.1 collective-permute-start.1
  1.2 0.0 copy-start
  1.2 1.1 %broadcast_select_fusion.own = bf16[512,512]{1,0:T(8,128)(2,1)S(1)} fusion(pred[]{:T(512)S(6)} %gt.2, bf16[1,512,512]{2,1,0:T(8,128)(2,1)} %param.4), kind=kLoop, calls=%fused_computation | loop fusion | flops 262144 | bytes 1048577 | tf_op jit(solution)/shard_map/jit(_where)/select_n | solution.py:257
  2.4 0.0 copy-done
  2.4 0.0 copy-done.1
  2.5 0.8 %collective-permute-done.1.partner_local = bf16[2,128,512]{2,1,0:T(8,128)(2,1)S(1)} collective-permute-done((bf16[2,128,512]{2,1,0:T(8,128)(2,1)}, bf16[2,128,512]{2,1,0:T(8,128)(2,1)S(1)}, u32[]{:S(2)}, u32[]{:S(2)}) %collective-permute-start.1) | collective-permute-done | bytes 262176 | tf_op jit(solution)/shard_map/ppermute | solution.py:260
  3.3 0.0 collective-permute-done.partner
  3.3 0.9 %shard_map.50 = (f32[128,512]{1,0:T(8,128)S(1)}, f32[128,512]{1,0:T(8,128)S(1)}, bf16[128,512]{1,0:T(8,128)(2,1)S(1)}) custom-call(bf16[512,512]{1,0:T(8,128)(2,1)S(1)} %broadcast_select_fusion.own, bf16[512,512]{1,0:T(8,128)(2,1)S(1)} %collective-permute-done.partner, bf16[2,128,512]{2,1,0:T(8,128)(2,1)S(1)} %get-tuple-element.57.local, ...), custom_call_target="tpu_custom_call" | custom-call | flops 268435456 | bytes 1048576 | tf_op jit(solution)/shard_map/pallas_call | solution.py:264
  4.1 1.3 %collective-permute-start.2 = (bf16[128,512]{1,0:T(8,128)(2,1)S(1)}, bf16[128,512]{1,0:T(8,128)(2,1)S(1)}, u32[]{:S(2)}, u32[]{:S(2)}) collective-permute-start(bf16[128,512]{1,0:T(8,128)(2,1)S(1)} %get-tuple-element.31.after), channel_id=1, source_target_pairs={{16,0},{17,1},{18,2},{19,3},{20,4},{21,5},{22,6},{23,7},{24,8},{25... | collective-permute-start | bytes 393224 | tf_op jit(solution)/shard_map/ppermute | solution.py:269
  5.4 0.4 shard_map.52
  5.8 4.0 %collective-permute-start.4 = (bf16[64,640]{1,0:T(8,128)(2,1)S(1)}, bf16[64,640]{1,0:T(8,128)(2,1)S(1)}, u32[]{:S(2)}, u32[]{:S(2)}) collective-permute-start(bf16[64,640]{1,0:T(8,128)(2,1)S(1)} %get-tuple-element.35), channel_id=1, source_target_pairs={{0,3},{1,2},{2,1},{3,0},{4,7},{5,6},{6,5},{7,4},{8,11},{9,10},{10,... | collective-permute-start | bytes 245768 | tf_op jit(solution)/shard_map/ppermute | solution.py:225
  9.8 0.5 %collective-permute-start.5 = (bf16[64,640]{1,0:T(8,128)(2,1)S(1)}, bf16[64,640]{1,0:T(8,128)(2,1)S(1)}, u32[]{:S(2)}, u32[]{:S(2)}) collective-permute-start(bf16[64,640]{1,0:T(8,128)(2,1)S(1)} %get-tuple-element.36), channel_id=1, source_target_pairs={{0,1},{1,0},{2,3},{3,2},{4,5},{5,4},{6,7},{7,6},{8,9},{9,8},{10,11... | collective-permute-start | bytes 245768 | tf_op jit(solution)/shard_map/ppermute | solution.py:225
  10.3 0.1 collective-permute-start.6
  10.4 1.7 %collective-permute-done.2.arrived = bf16[128,512]{1,0:T(8,128)(2,1)S(1)} collective-permute-done((bf16[128,512]{1,0:T(8,128)(2,1)S(1)}, bf16[128,512]{1,0:T(8,128)(2,1)S(1)}, u32[]{:S(2)}, u32[]{:S(2)}) %collective-permute-start.2) | collective-permute-done | bytes 131104 | tf_op jit(solution)/shard_map/ppermute | solution.py:269
  12.1 0.5 %shard_map.51 = (bf16[128,512]{1,0:T(8,128)(2,1)S(1)}, bf16[128,512]{1,0:T(8,128)(2,1)S(1)}, bf16[128,512]{1,0:T(8,128)(2,1)S(1)}, bf16[128,512]{1,0:T(8,128)(2,1)S(1)}) custom-call(bf16[512,512]{1,0:T(8,128)(2,1)S(1)} %broadcast_select_fusion.own, bf16[512,512]{1,0:T(8,128)(2,1)S(1)} %collective-permute-done.partner, ...), custom_call_target="tpu_custom_call" | custom-call | flops 2147483648 | bytes 1048576 | tf_op jit(solution)/shard_map/pallas_call | solution.py:286
  12.7 0.1 collective-permute-start.3
  12.7 0.0 collective-permute-done.4.refs_1_
  12.7 1.5 %collective-permute-done.5.refs_2_ = bf16[64,640]{1,0:T(8,128)(2,1)S(1)} collective-permute-done((bf16[64,640]{1,0:T(8,128)(2,1)S(1)}, bf16[64,640]{1,0:T(8,128)(2,1)S(1)}, u32[]{:S(2)}, u32[]{:S(2)}) %collective-permute-start.5) | collective-permute-done | bytes 81952 | tf_op jit(solution)/shard_map/ppermute | solution.py:225
  14.3 0.5 collective-permute-done.6.refs_3_
  14.8 2.7 %collective-permute-start.13 = (bf16[64,640]{1,0:T(8,128)(2,1)S(1)}, bf16[64,640]{1,0:T(8,128)(2,1)S(1)}, u32[]{:S(2)}, u32[]{:S(2)}) collective-permute-start(bf16[64,640]{1,0:T(8,128)(2,1)S(1)} %shard_map.53.after.left), channel_id=1, source_target_pairs={{0,4},{4,0},{1,5},{5,1},{2,6},{6,2},{3,7},{7,3},{8,12},{12,8},{9,1... | collective-permute-start | bytes 245768 | tf_op jit(solution)/shard_map/ppermute | solution.py:233
  17.4 0.0 collective-permute-done.3.dh_got
  17.4 0.5 %shard_map.54 = (bf16[64,640]{1,0:T(8,128)(2,1)S(1)}, bf16[64,640]{1,0:T(8,128)(2,1)S(1)}, bf16[64,640]{1,0:T(8,128)(2,1)S(1)}, bf16[64,640]{1,0:T(8,128)(2,1)S(...) custom-call(bf16[2,128,512]{2,1,0:T(8,128)(2,1)S(1)} %get-tuple-elem, ...), custom_call_target="tpu_custom_call" | custom-call | flops 268435456 | bytes 1048576 | tf_op jit(solution)/shard_map/pallas_call | solution.py:294
  18.0 1.5 %collective-permute-start.10 = (bf16[64,640]{1,0:T(8,128)(2,1)S(1)}, bf16[64,640]{1,0:T(8,128)(2,1)S(1)}, u32[]{:S(2)}, u32[]{:S(2)}) collective-permute-start(bf16[64,640]{1,0:T(8,128)(2,1)S(1)} %get-tuple-element.43), channel_id=1, source_target_pairs={{0,3},{1,2},{2,1},{3,0},{4,7},{5,6},{6,5},{7,4},{8,11},{9,10},{10,... | collective-permute-start | bytes 245768 | tf_op jit(solution)/shard_map/ppermute | solution.py:225
  19.5 1.3 %collective-permute-start.11 = (bf16[64,640]{1,0:T(8,128)(2,1)S(1)}, bf16[64,640]{1,0:T(8,128)(2,1)S(1)}, u32[]{:S(2)}, u32[]{:S(2)}) collective-permute-start(bf16[64,640]{1,0:T(8,128)(2,1)S(1)} %get-tuple-element.44), channel_id=1, source_target_pairs={{0,1},{1,0},{2,3},{3,2},{4,5},{5,4},{6,7},{7,6},{8,9},{9,8},{10,11... | collective-permute-start | bytes 245768 | tf_op jit(solution)/shard_map/ppermute | solution.py:225
  20.8 0.7 %collective-permute-start.12 = (bf16[64,640]{1,0:T(8,128)(2,1)S(1)}, bf16[64,640]{1,0:T(8,128)(2,1)S(1)}, u32[]{:S(2)}, u32[]{:S(2)}) collective-permute-start(bf16[64,640]{1,0:T(8,128)(2,1)S(1)} %get-tuple-element.45), channel_id=1, source_target_pairs={{0,2},{1,3},{2,0},{3,1},{4,6},{5,7},{6,4},{7,5},{8,10},{9,11},{10,... | collective-permute-start | bytes 245768 | tf_op jit(solution)/shard_map/ppermute | solution.py:225
  21.5 1.4 %collective-permute-start.7 = (bf16[64,1024]{1,0:T(8,128)(2,1)S(1)}, bf16[64,1024]{1,0:T(8,128)(2,1)S(1)}, u32[]{:S(2)}, u32[]{:S(2)}) collective-permute-start(bf16[64,1024]{1,0:T(8,128)(2,1)S(1)} %get-tuple-element.39), channel_id=1, source_target_pairs={{0,3},{1,2},{2,1},{3,0},{4,7},{5,6},{6,5},{7,4},{8,11},{9,10},{10,... | collective-permute-start | bytes 393224 | tf_op jit(solution)/shard_map/ppermute | solution.py:225
  23.0 0.0 collective-permute-done.13.right
  23.0 1.3 %collective-permute-start.8 = (bf16[64,1024]{1,0:T(8,128)(2,1)S(1)}, bf16[64,1024]{1,0:T(8,128)(2,1)S(1)}, u32[]{:S(2)}, u32[]{:S(2)}) collective-permute-start(bf16[64,1024]{1,0:T(8,128)(2,1)S(1)} %get-tuple-element.40), channel_id=1, source_target_pairs={{0,1},{1,0},{2,3},{3,2},{4,5},{5,4},{6,7},{7,6},{8,9},{9,8},{10,11... | collective-permute-start | bytes 393224 | tf_op jit(solution)/shard_map/ppermute | solution.py:225
  24.3 0.0 collective-permute-done.10.refs_1_
  24.3 1.2 %collective-permute-start.9 = (bf16[64,1024]{1,0:T(8,128)(2,1)S(1)}, bf16[64,1024]{1,0:T(8,128)(2,1)S(1)}, u32[]{:S(2)}, u32[]{:S(2)}) collective-permute-start(bf16[64,1024]{1,0:T(8,128)(2,1)S(1)} %get-tuple-element.41), channel_id=1, source_target_pairs={{0,2},{1,3},{2,0},{3,1},{4,6},{5,7},{6,4},{7,5},{8,10},{9,11},{10,... | collective-permute-start | bytes 393224 | tf_op jit(solution)/shard_map/ppermute | solution.py:225
  25.5 0.0 collective-permute-done.11.refs_2_
  25.5 0.7 %collective-permute-done.12.refs_3_ = bf16[64,640]{1,0:T(8,128)(2,1)S(1)} collective-permute-done((bf16[64,640]{1,0:T(8,128)(2,1)S(1)}, bf16[64,640]{1,0:T(8,128)(2,1)S(1)}, u32[]{:S(2)}, u32[]{:S(2)}) %collective-permute-start.12) | collective-permute-done | bytes 81952 | tf_op jit(solution)/shard_map/ppermute | solution.py:225
  26.2 1.2 %collective-permute-start.15 = (bf16[64,640]{1,0:T(8,128)(2,1)S(1)}, bf16[64,640]{1,0:T(8,128)(2,1)S(1)}, u32[]{:S(2)}, u32[]{:S(2)}) collective-permute-start(bf16[64,640]{1,0:T(8,128)(2,1)S(1)} %get-tuple-element.48.left), channel_id=1, source_target_pairs={{0,4},{4,0},{1,5},{5,1},{2,6},{6,2},{3,7},{7,3},{8,12},{12,8},{9,1... | collective-permute-start | bytes 245768 | tf_op jit(solution)/shard_map/ppermute | solution.py:233
  27.4 2.6 %collective-permute-done.7.refs_1_ = bf16[64,1024]{1,0:T(8,128)(2,1)S(1)} collective-permute-done((bf16[64,1024]{1,0:T(8,128)(2,1)S(1)}, bf16[64,1024]{1,0:T(8,128)(2,1)S(1)}, u32[]{:S(2)}, u32[]{:S(2)}) %collective-permute-start.7) | collective-permute-done | bytes 131104 | tf_op jit(solution)/shard_map/ppermute | solution.py:225
  30.0 0.2 collective-permute-done.8.refs_2_
  30.2 2.3 %collective-permute-done.9.refs_3_ = bf16[64,1024]{1,0:T(8,128)(2,1)S(1)} collective-permute-done((bf16[64,1024]{1,0:T(8,128)(2,1)S(1)}, bf16[64,1024]{1,0:T(8,128)(2,1)S(1)}, u32[]{:S(2)}, u32[]{:S(2)}) %collective-permute-start.9) | collective-permute-done | bytes 131104 | tf_op jit(solution)/shard_map/ppermute | solution.py:225
  32.5 0.1 shard_map.57
  32.6 0.4 collective-permute-start.14
  33.0 1.0 %collective-permute-start.19 = (bf16[64,640]{1,0:T(8,128)(2,1)S(1)}, bf16[64,640]{1,0:T(8,128)(2,1)S(1)}, u32[]{:S(2)}, u32[]{:S(2)}) collective-permute-start(bf16[64,640]{1,0:T(8,128)(2,1)S(1)} %get-tuple-element.49.refs_0_), channel_id=1, source_target_pairs={{0,1},{1,0},{2,3},{3,2},{4,5},{5,4},{6,7},{7,6},{8,9},{9,8},{10,11... | collective-permute-start | bytes 245768 | tf_op jit(solution)/shard_map/ppermute | solution.py:225
  34.0 0.0 collective-permute-done.15.right
  34.0 3.0 %collective-permute-start.18 = (bf16[64,640]{1,0:T(8,128)(2,1)S(1)}, bf16[64,640]{1,0:T(8,128)(2,1)S(1)}, u32[]{:S(2)}, u32[]{:S(2)}) collective-permute-start(bf16[64,640]{1,0:T(8,128)(2,1)S(1)} %shard_map.58.refs_0_), channel_id=1, source_target_pairs={{0,3},{1,2},{2,1},{3,0},{4,7},{5,6},{6,5},{7,4},{8,11},{9,10},{10,... | collective-permute-start | bytes 245768 | tf_op jit(solution)/shard_map/ppermute | solution.py:225
  37.0 0.0 collective-permute-start.17
  37.0 1.0 %collective-permute-start.16 = (bf16[64,640]{1,0:T(8,128)(2,1)S(1)}, bf16[64,640]{1,0:T(8,128)(2,1)S(1)}, u32[]{:S(2)}, u32[]{:S(2)}) collective-permute-start(bf16[64,640]{1,0:T(8,128)(2,1)S(1)} %shard_map.58.refs_0_), channel_id=1, source_target_pairs={{0,1},{1,0},{2,3},{3,2},{4,5},{5,4},{6,7},{7,6},{8,9},{9,8},{10,11... | collective-permute-start | bytes 245768 | tf_op jit(solution)/shard_map/ppermute | solution.py:225
  38.0 0.4 collective-permute-done.19.refs_4_.refs_1_
  38.3 4.7 %collective-permute-start.21 = (bf16[64,640]{1,0:T(8,128)(2,1)S(1)}, bf16[64,640]{1,0:T(8,128)(2,1)S(1)}, u32[]{:S(2)}, u32[]{:S(2)}) collective-permute-start(bf16[64,640]{1,0:T(8,128)(2,1)S(1)} %get-tuple-element.49.refs_0_), channel_id=1, source_target_pairs={{0,3},{1,2},{2,1},{3,0},{4,7},{5,6},{6,5},{7,4},{8,11},{9,10},{10,... | collective-permute-start | bytes 245768 | tf_op jit(solution)/shard_map/ppermute | solution.py:225
  43.1 0.0 collective-permute-done.18.refs_3_
  43.1 0.0 collective-permute-start.20
  43.1 0.0 collective-permute-done.17.refs_2_
  43.1 0.0 collective-permute-done.16.refs_1_
  43.1 0.0 collective-permute-done.14.right
  43.2 1.3 %collective-permute-start.25 = (bf16[64,1024]{1,0:T(8,128)(2,1)S(1)}, bf16[64,1024]{1,0:T(8,128)(2,1)S(1)}, u32[]{:S(2)}, u32[]{:S(2)}) collective-permute-start(bf16[64,1024]{1,0:T(8,128)(2,1)S(1)} %shard_map.59.after.refs_0_), channel_id=1, source_target_pairs={{0,3},{1,2},{2,1},{3,0},{4,7},{5,6},{6,5},{7,4},{8,11},{9,10},{10,... | collective-permute-start | bytes 393224 | tf_op jit(solution)/shard_map/ppermute | solution.py:225
  44.5 0.8 %collective-permute-start.24 = (bf16[64,1024]{1,0:T(8,128)(2,1)S(1)}, bf16[64,1024]{1,0:T(8,128)(2,1)S(1)}, u32[]{:S(2)}, u32[]{:S(2)}) collective-permute-start(bf16[64,1024]{1,0:T(8,128)(2,1)S(1)} %shard_map.59.after.refs_0_), channel_id=1, source_target_pairs={{0,2},{1,3},{2,0},{3,1},{4,6},{5,7},{6,4},{7,5},{8,10},{9,11},{10,... | collective-permute-start | bytes 393224 | tf_op jit(solution)/shard_map/ppermute | solution.py:225
  45.3 1.4 %collective-permute-start.23 = (bf16[64,1024]{1,0:T(8,128)(2,1)S(1)}, bf16[64,1024]{1,0:T(8,128)(2,1)S(1)}, u32[]{:S(2)}, u32[]{:S(2)}) collective-permute-start(bf16[64,1024]{1,0:T(8,128)(2,1)S(1)} %shard_map.59.after.refs_0_), channel_id=1, source_target_pairs={{0,1},{1,0},{2,3},{3,2},{4,5},{5,4},{6,7},{7,6},{8,9},{9,8},{10,11... | collective-permute-start | bytes 393224 | tf_op jit(solution)/shard_map/ppermute | solution.py:225
  46.7 2.0 %shard_map.61 = (bf16[512,512]{1,0:T(8,128)(2,1)S(1)}, bf16[128,512]{1,0:T(8,128)(2,1)S(1)}) custom-call(bf16[128,512]{1,0:T(8,128)(2,1)S(1)} %get-tuple-element.50.through, bf16[64,1024]{1,0:T(8,128)(2,1)S(1)} %shard_map.59.after.refs_0_, bf16[64,640]{1,0:T(8,128)(2,1)S(1)} %shard_map.58.refs_0_, bf16[64,640]{1,0:T(8,128)(2,1)S(1)} %collective-permute-done.16.refs_1_, ...), custom_call_target="tpu_custom_call" | custom-call | flops 2684354560 | bytes 1048576 | tf_op jit(solution)/shard_map/pallas_call | solution.py:315
  48.8 0.0 collective-permute-done.21.refs_3_
  48.8 0.1 collective-permute-start.22
  48.9 0.0 collective-permute-done.20.refs_2_
  48.9 2.0 %shard_map.60.act_inv = bf16[512,512]{1,0:T(8,128)(2,1)S(1)} custom-call(bf16[64,1024]{1,0:T(8,128)(2,1)S(1)} %shard_map.59.after.refs_0_, bf16[64,640]{1,0:T(8,128)(2,1)S(1)} %get-tuple-element.49.refs_0_, bf16[64,640]{1,0:T(8,128)(2,1)S(1)} %collective-permute-done.19.refs_4_.refs_1_, bf16[64,640]{1,0:T(8,128)(2,1)S(1)} %collective-permute-done.20.refs_2_, ...), custom_call_target="tpu_custom_call" | custom-call | flops 2684354560 | bytes 1048576 | tf_op jit(solution)/shard_map/pallas_call | solution.py:315
  50.9 0.0 collective-permute-done.25.refs_3_
  50.9 0.4 collective-permute-done.24.refs_2_
  51.3 0.0 collective-permute-done.23.refs_1_
  51.3 0.0 collective-permute-done.22.other_cot
  51.3 1.6 %shard_map.62 = (f32[512,512]{1,0:T(8,128)}, bf16[2,128,512]{2,1,0:T(8,128)(2,1)}) custom-call(bf16[512,512]{1,0:T(8,128)(2,1)S(1)} %shard_map.60.act_inv, bf16[512,512]{1,0:T(8,128)(2,1)S(1)} %get-tuple-element.51.out_inv, bf16[128,512]{1,0:T(8,128)(2,1)S(1)} %get-tuple-element.52.own_cot, bf16[128,512]{1,0:T(8,128)(2,1)S(1)} %collective-permute-done.22.other_cot, ...), custom_call_target="tpu_custom_call" | custom-call | flops 1342177280 | bytes 1048576 | tf_op jit(solution)/shard_map/pallas_call | solution.py:328
  (7 shorter events, 0.2 us)
Async XLA Ops:
  0.6 2.6 %collective-permute-start = (bf16[512,512]{1,0:T(8,128)(2,1)}, bf16[512,512]{1,0:T(8,128)(2,1)S(1)}, u32[]{:S(2)}, u32[]{:S(2)}) collective-permute-start(bf16[512,512]{1,0:T(8,128)(2,1)} %bitcast.6), channel_id=1, source_target_pairs={{0,8},{8,0},{1,9},{9,1},{2,10},{10,2},{3,11},{11,3},{4,12},{12,4},... | collective-permute-start | bytes 1572872 | tf_op jit(solution)/shard_map/ppermute | solution.py:259
  1.1 2.1 %collective-permute-start.1 = (bf16[2,128,512]{2,1,0:T(8,128)(2,1)}, bf16[2,128,512]{2,1,0:T(8,128)(2,1)S(1)}, u32[]{:S(2)}, u32[]{:S(2)}) collective-permute-start(bf16[2,128,512]{2,1,0:T(8,128)(2,1)} %bitcast.7), channel_id=1, source_target_pairs={{0,8},{8,0},{1,9},{9,1},{2,10},{10,2},{3,11},{11,3},{4,12},{12,4},... | collective-permute-start | bytes 786440 | tf_op jit(solution)/shard_map/ppermute | solution.py:260
  1.2 1.1 %copy-start = (bf16[2,128,512]{2,1,0:T(8,128)(2,1)S(1)}, bf16[2,128,512]{2,1,0:T(8,128)(2,1)}, u32[]{:S(2)}) copy-start(bf16[2,128,512]{2,1,0:T(8,128)(2,1)} %param.5) | copy-start | bytes 786436
  1.2 1.2 %copy-start.1 = (bf16[1,2,128,512]{3,2,1,0:T(8,128)(2,1)S(1)}, bf16[1,2,128,512]{3,2,1,0:T(8,128)(2,1)}, u32[]{:S(2)}) copy-start(bf16[1,2,128,512]{3,2,1,0:T(8,128)(2,1)} %param.3) | copy-start | bytes 786436
  4.1 8.0 %collective-permute-start.2 = (bf16[128,512]{1,0:T(8,128)(2,1)S(1)}, bf16[128,512]{1,0:T(8,128)(2,1)S(1)}, u32[]{:S(2)}, u32[]{:S(2)}) collective-permute-start(bf16[128,512]{1,0:T(8,128)(2,1)S(1)} %get-tuple-element.31.after), channel_id=1, source_target_pairs={{16,0},{17,1},{18,2},{19,3},{20,4},{21,5},{22,6},{23,7},{24,8},{25... | collective-permute-start | bytes 393224 | tf_op jit(solution)/shard_map/ppermute | solution.py:269
  5.8 6.9 %collective-permute-start.4 = (bf16[64,640]{1,0:T(8,128)(2,1)S(1)}, bf16[64,640]{1,0:T(8,128)(2,1)S(1)}, u32[]{:S(2)}, u32[]{:S(2)}) collective-permute-start(bf16[64,640]{1,0:T(8,128)(2,1)S(1)} %get-tuple-element.35), channel_id=1, source_target_pairs={{0,3},{1,2},{2,1},{3,0},{4,7},{5,6},{6,5},{7,4},{8,11},{9,10},{10,... | collective-permute-start | bytes 245768 | tf_op jit(solution)/shard_map/ppermute | solution.py:225
  9.8 4.5 %collective-permute-start.5 = (bf16[64,640]{1,0:T(8,128)(2,1)S(1)}, bf16[64,640]{1,0:T(8,128)(2,1)S(1)}, u32[]{:S(2)}, u32[]{:S(2)}) collective-permute-start(bf16[64,640]{1,0:T(8,128)(2,1)S(1)} %get-tuple-element.36), channel_id=1, source_target_pairs={{0,1},{1,0},{2,3},{3,2},{4,5},{5,4},{6,7},{7,6},{8,9},{9,8},{10,11... | collective-permute-start | bytes 245768 | tf_op jit(solution)/shard_map/ppermute | solution.py:225
  10.3 4.4 %collective-permute-start.6 = (bf16[64,640]{1,0:T(8,128)(2,1)S(1)}, bf16[64,640]{1,0:T(8,128)(2,1)S(1)}, u32[]{:S(2)}, u32[]{:S(2)}) collective-permute-start(bf16[64,640]{1,0:T(8,128)(2,1)S(1)} %get-tuple-element.37), channel_id=1, source_target_pairs={{0,2},{1,3},{2,0},{3,1},{4,6},{5,7},{6,4},{7,5},{8,10},{9,11},{10,... | collective-permute-start | bytes 245768 | tf_op jit(solution)/shard_map/ppermute | solution.py:225
  12.7 4.8 %collective-permute-start.3 = (bf16[128,512]{1,0:T(8,128)(2,1)S(1)}, bf16[128,512]{1,0:T(8,128)(2,1)S(1)}, u32[]{:S(2)}, u32[]{:S(2)}) collective-permute-start(bf16[128,512]{1,0:T(8,128)(2,1)S(1)} %get-tuple-element.33), channel_id=1, source_target_pairs={{0,8},{8,0},{1,9},{9,1},{2,10},{10,2},{3,11},{11,3},{4,12},{12,4},... | collective-permute-start | bytes 393224 | tf_op jit(solution)/shard_map/ppermute | solution.py:292
  14.8 8.2 %collective-permute-start.13 = (bf16[64,640]{1,0:T(8,128)(2,1)S(1)}, bf16[64,640]{1,0:T(8,128)(2,1)S(1)}, u32[]{:S(2)}, u32[]{:S(2)}) collective-permute-start(bf16[64,640]{1,0:T(8,128)(2,1)S(1)} %shard_map.53.after.left), channel_id=1, source_target_pairs={{0,4},{4,0},{1,5},{5,1},{2,6},{6,2},{3,7},{7,3},{8,12},{12,8},{9,1... | collective-permute-start | bytes 245768 | tf_op jit(solution)/shard_map/ppermute | solution.py:233
  18.0 6.3 %collective-permute-start.10 = (bf16[64,640]{1,0:T(8,128)(2,1)S(1)}, bf16[64,640]{1,0:T(8,128)(2,1)S(1)}, u32[]{:S(2)}, u32[]{:S(2)}) collective-permute-start(bf16[64,640]{1,0:T(8,128)(2,1)S(1)} %get-tuple-element.43), channel_id=1, source_target_pairs={{0,3},{1,2},{2,1},{3,0},{4,7},{5,6},{6,5},{7,4},{8,11},{9,10},{10,... | collective-permute-start | bytes 245768 | tf_op jit(solution)/shard_map/ppermute | solution.py:225
  19.5 6.1 %collective-permute-start.11 = (bf16[64,640]{1,0:T(8,128)(2,1)S(1)}, bf16[64,640]{1,0:T(8,128)(2,1)S(1)}, u32[]{:S(2)}, u32[]{:S(2)}) collective-permute-start(bf16[64,640]{1,0:T(8,128)(2,1)S(1)} %get-tuple-element.44), channel_id=1, source_target_pairs={{0,1},{1,0},{2,3},{3,2},{4,5},{5,4},{6,7},{7,6},{8,9},{9,8},{10,11... | collective-permute-start | bytes 245768 | tf_op jit(solution)/shard_map/ppermute | solution.py:225
  20.8 5.4 %collective-permute-start.12 = (bf16[64,640]{1,0:T(8,128)(2,1)S(1)}, bf16[64,640]{1,0:T(8,128)(2,1)S(1)}, u32[]{:S(2)}, u32[]{:S(2)}) collective-permute-start(bf16[64,640]{1,0:T(8,128)(2,1)S(1)} %get-tuple-element.45), channel_id=1, source_target_pairs={{0,2},{1,3},{2,0},{3,1},{4,6},{5,7},{6,4},{7,5},{8,10},{9,11},{10,... | collective-permute-start | bytes 245768 | tf_op jit(solution)/shard_map/ppermute | solution.py:225
  21.5 8.4 %collective-permute-start.7 = (bf16[64,1024]{1,0:T(8,128)(2,1)S(1)}, bf16[64,1024]{1,0:T(8,128)(2,1)S(1)}, u32[]{:S(2)}, u32[]{:S(2)}) collective-permute-start(bf16[64,1024]{1,0:T(8,128)(2,1)S(1)} %get-tuple-element.39), channel_id=1, source_target_pairs={{0,3},{1,2},{2,1},{3,0},{4,7},{5,6},{6,5},{7,4},{8,11},{9,10},{10,... | collective-permute-start | bytes 393224 | tf_op jit(solution)/shard_map/ppermute | solution.py:225
  23.0 7.3 %collective-permute-start.8 = (bf16[64,1024]{1,0:T(8,128)(2,1)S(1)}, bf16[64,1024]{1,0:T(8,128)(2,1)S(1)}, u32[]{:S(2)}, u32[]{:S(2)}) collective-permute-start(bf16[64,1024]{1,0:T(8,128)(2,1)S(1)} %get-tuple-element.40), channel_id=1, source_target_pairs={{0,1},{1,0},{2,3},{3,2},{4,5},{5,4},{6,7},{7,6},{8,9},{9,8},{10,11... | collective-permute-start | bytes 393224 | tf_op jit(solution)/shard_map/ppermute | solution.py:225
  24.3 8.2 %collective-permute-start.9 = (bf16[64,1024]{1,0:T(8,128)(2,1)S(1)}, bf16[64,1024]{1,0:T(8,128)(2,1)S(1)}, u32[]{:S(2)}, u32[]{:S(2)}) collective-permute-start(bf16[64,1024]{1,0:T(8,128)(2,1)S(1)} %get-tuple-element.41), channel_id=1, source_target_pairs={{0,2},{1,3},{2,0},{3,1},{4,6},{5,7},{6,4},{7,5},{8,10},{9,11},{10,... | collective-permute-start | bytes 393224 | tf_op jit(solution)/shard_map/ppermute | solution.py:225
  26.2 7.7 %collective-permute-start.15 = (bf16[64,640]{1,0:T(8,128)(2,1)S(1)}, bf16[64,640]{1,0:T(8,128)(2,1)S(1)}, u32[]{:S(2)}, u32[]{:S(2)}) collective-permute-start(bf16[64,640]{1,0:T(8,128)(2,1)S(1)} %get-tuple-element.48.left), channel_id=1, source_target_pairs={{0,4},{4,0},{1,5},{5,1},{2,6},{6,2},{3,7},{7,3},{8,12},{12,8},{9,1... | collective-permute-start | bytes 245768 | tf_op jit(solution)/shard_map/ppermute | solution.py:233
  32.6 10.5 %collective-permute-start.14 = (bf16[64,1024]{1,0:T(8,128)(2,1)S(1)}, bf16[64,1024]{1,0:T(8,128)(2,1)S(1)}, u32[]{:S(2)}, u32[]{:S(2)}) collective-permute-start(bf16[64,1024]{1,0:T(8,128)(2,1)S(1)} %get-tuple-element.47.left), channel_id=1, source_target_pairs={{0,4},{4,0},{1,5},{5,1},{2,6},{6,2},{3,7},{7,3},{8,12},{12,8},{9,1... | collective-permute-start | bytes 393224 | tf_op jit(solution)/shard_map/ppermute | solution.py:233
  33.0 5.3 %collective-permute-start.19 = (bf16[64,640]{1,0:T(8,128)(2,1)S(1)}, bf16[64,640]{1,0:T(8,128)(2,1)S(1)}, u32[]{:S(2)}, u32[]{:S(2)}) collective-permute-start(bf16[64,640]{1,0:T(8,128)(2,1)S(1)} %get-tuple-element.49.refs_0_), channel_id=1, source_target_pairs={{0,1},{1,0},{2,3},{3,2},{4,5},{5,4},{6,7},{7,6},{8,9},{9,8},{10,11... | collective-permute-start | bytes 245768 | tf_op jit(solution)/shard_map/ppermute | solution.py:225
  34.0 9.1 %collective-permute-start.18 = (bf16[64,640]{1,0:T(8,128)(2,1)S(1)}, bf16[64,640]{1,0:T(8,128)(2,1)S(1)}, u32[]{:S(2)}, u32[]{:S(2)}) collective-permute-start(bf16[64,640]{1,0:T(8,128)(2,1)S(1)} %shard_map.58.refs_0_), channel_id=1, source_target_pairs={{0,3},{1,2},{2,1},{3,0},{4,7},{5,6},{6,5},{7,4},{8,11},{9,10},{10,... | collective-permute-start | bytes 245768 | tf_op jit(solution)/shard_map/ppermute | solution.py:225
  37.0 6.1 %collective-permute-start.17 = (bf16[64,640]{1,0:T(8,128)(2,1)S(1)}, bf16[64,640]{1,0:T(8,128)(2,1)S(1)}, u32[]{:S(2)}, u32[]{:S(2)}) collective-permute-start(bf16[64,640]{1,0:T(8,128)(2,1)S(1)} %shard_map.58.refs_0_), channel_id=1, source_target_pairs={{0,2},{1,3},{2,0},{3,1},{4,6},{5,7},{6,4},{7,5},{8,10},{9,11},{10,... | collective-permute-start | bytes 245768 | tf_op jit(solution)/shard_map/ppermute | solution.py:225
  37.0 6.1 %collective-permute-start.16 = (bf16[64,640]{1,0:T(8,128)(2,1)S(1)}, bf16[64,640]{1,0:T(8,128)(2,1)S(1)}, u32[]{:S(2)}, u32[]{:S(2)}) collective-permute-start(bf16[64,640]{1,0:T(8,128)(2,1)S(1)} %shard_map.58.refs_0_), channel_id=1, source_target_pairs={{0,1},{1,0},{2,3},{3,2},{4,5},{5,4},{6,7},{7,6},{8,9},{9,8},{10,11... | collective-permute-start | bytes 245768 | tf_op jit(solution)/shard_map/ppermute | solution.py:225
  38.3 10.4 %collective-permute-start.21 = (bf16[64,640]{1,0:T(8,128)(2,1)S(1)}, bf16[64,640]{1,0:T(8,128)(2,1)S(1)}, u32[]{:S(2)}, u32[]{:S(2)}) collective-permute-start(bf16[64,640]{1,0:T(8,128)(2,1)S(1)} %get-tuple-element.49.refs_0_), channel_id=1, source_target_pairs={{0,3},{1,2},{2,1},{3,0},{4,7},{5,6},{6,5},{7,4},{8,11},{9,10},{10,... | collective-permute-start | bytes 245768 | tf_op jit(solution)/shard_map/ppermute | solution.py:225
  43.1 5.8 %collective-permute-start.20 = (bf16[64,640]{1,0:T(8,128)(2,1)S(1)}, bf16[64,640]{1,0:T(8,128)(2,1)S(1)}, u32[]{:S(2)}, u32[]{:S(2)}) collective-permute-start(bf16[64,640]{1,0:T(8,128)(2,1)S(1)} %get-tuple-element.49.refs_0_), channel_id=1, source_target_pairs={{0,2},{1,3},{2,0},{3,1},{4,6},{5,7},{6,4},{7,5},{8,10},{9,11},{10,... | collective-permute-start | bytes 245768 | tf_op jit(solution)/shard_map/ppermute | solution.py:225
  43.2 7.7 %collective-permute-start.25 = (bf16[64,1024]{1,0:T(8,128)(2,1)S(1)}, bf16[64,1024]{1,0:T(8,128)(2,1)S(1)}, u32[]{:S(2)}, u32[]{:S(2)}) collective-permute-start(bf16[64,1024]{1,0:T(8,128)(2,1)S(1)} %shard_map.59.after.refs_0_), channel_id=1, source_target_pairs={{0,3},{1,2},{2,1},{3,0},{4,7},{5,6},{6,5},{7,4},{8,11},{9,10},{10,... | collective-permute-start | bytes 393224 | tf_op jit(solution)/shard_map/ppermute | solution.py:225
  44.5 6.7 %collective-permute-start.24 = (bf16[64,1024]{1,0:T(8,128)(2,1)S(1)}, bf16[64,1024]{1,0:T(8,128)(2,1)S(1)}, u32[]{:S(2)}, u32[]{:S(2)}) collective-permute-start(bf16[64,1024]{1,0:T(8,128)(2,1)S(1)} %shard_map.59.after.refs_0_), channel_id=1, source_target_pairs={{0,2},{1,3},{2,0},{3,1},{4,6},{5,7},{6,4},{7,5},{8,10},{9,11},{10,... | collective-permute-start | bytes 393224 | tf_op jit(solution)/shard_map/ppermute | solution.py:225
  45.3 6.0 %collective-permute-start.23 = (bf16[64,1024]{1,0:T(8,128)(2,1)S(1)}, bf16[64,1024]{1,0:T(8,128)(2,1)S(1)}, u32[]{:S(2)}, u32[]{:S(2)}) collective-permute-start(bf16[64,1024]{1,0:T(8,128)(2,1)S(1)} %shard_map.59.after.refs_0_), channel_id=1, source_target_pairs={{0,1},{1,0},{2,3},{3,2},{4,5},{5,4},{6,7},{7,6},{8,9},{9,8},{10,11... | collective-permute-start | bytes 393224 | tf_op jit(solution)/shard_map/ppermute | solution.py:225
  48.8 2.5 %collective-permute-start.22 = (bf16[128,512]{1,0:T(8,128)(2,1)S(1)}, bf16[128,512]{1,0:T(8,128)(2,1)S(1)}, u32[]{:S(2)}, u32[]{:S(2)}) collective-permute-start(bf16[128,512]{1,0:T(8,128)(2,1)S(1)} %get-tuple-element.53), channel_id=1, source_target_pairs={{0,8},{8,0},{1,9},{9,1},{2,10},{10,2},{3,11},{11,3},{4,12},{12,4},... | collective-permute-start | bytes 393224 | tf_op jit(solution)/shard_map/ppermute | solution.py:327
